TPU v7x, 32 devices: a whole 2x2x4 slice. The times are simulated.
32 devices in a mesh: group: 2 (over y), expert: 8 (over z, x), dp: 2 (over core).
Axes of the slice: x: 2, y: 2, z: 4, core: 2. Of those that a mesh axis runs over, the one named last changes fastest.
Arguments:
- tokens: bfloat16 [4096, 2048], P(('group', 'expert', 'dp')), parts along dimension 0, may hold values from -6 to 6
- routes: int32 [4096, 8], P(('group', 'expert', 'dp')), parts along dimension 0, may hold values from 0 to 15, as said below
- gate_levels: int32 [4096, 8], P(('group', 'expert', 'dp')), parts along dimension 0, may hold values from 1 to 1024
- latent_grad: bfloat16 [4096, 512], P(('group', 'expert', 'dp')), parts along dimension 0, may hold values from -6 to 6
- down_weight: bfloat16 [2048, 512], P(('expert', 'dp')), may hold values from -0.125 to 0.125
- expert_in: bfloat16 [16, 512, 512], P(('expert', 'dp')), may hold values from -0.25 to 0.25
- expert_out: bfloat16 [16, 512, 512], P(('expert', 'dp')), may hold values from -0.25 to 0.25
Outputs:
- latent_out: bfloat16 [4096, 512], P(('group', 'expert', 'dp')), parts along dimension 0
- grad_tokens: bfloat16 [4096, 2048], P(('group', 'expert', 'dp')), parts along dimension 0
- grad_down: float32 [4096, 512], P(('group', 'expert', 'dp')), parts along dimension 0
- grad_in: bfloat16 [32, 512, 512], P(('group', 'expert', 'dp')), parts along dimension 0
- grad_out: bfloat16 [32, 512, 512], P(('group', 'expert', 'dp')), parts along dimension 0
There are 2 independent parts, one for each index of `group`. A program takes and returns all parts, laid end to end along the dimension named above; an argument that names none is the same for every part. Nothing has to cross between parts.
Inputs may be any that keep to these rules, and one draw needn't show every extreme that they name: `routes`: each row names 8 different experts. Among the 128 rows of one device no expert is named more than 96 times, and some expert is named exactly 96 times by the rows of every device.
All inputs are finite; a program needn't handle non-finite values.
Results may differ from a plain program's by a relative error of at most 0.0076.
Values may be sent and summed in bfloat16 or wider, within the bound.
No kernel may reach another device: no remote copies, remote signals or barrier semaphores. Data moves between devices by JAX's collectives and lax.ppermute only.
A program may use at most 128 MiB of HBM per device.

v0:
```python
import jax
import jax.numpy as jnp
from jax import lax
from jax.sharding import PartitionSpec as P

gate_unit = 1.0 / 1024.0


def slot_table(routes, capacity):
    flat = routes.reshape(-1)
    count = flat.shape[0]
    order = jnp.arange(count, dtype=jnp.int32)
    same = (flat[:, None] == flat[None, :]) & (order[None, :] < order[:, None])
    placed = jnp.sum(jnp.where(same, 1, 0), axis=1).astype(jnp.int32)
    return flat * capacity + placed


def on_device(tokens, routes, gate_levels, latent_grad, down_weight, expert_in, expert_out):
    tok_rows = tokens.shape[0]
    top = routes.shape[1]
    latent_width = down_weight.shape[1]
    n_major = lax.axis_size("expert")
    n_minor = lax.axis_size("dp")
    n_experts = n_major * n_minor
    capacity = 3 * tok_rows * top // (2 * n_experts)
    entries = tok_rows * top
    contract_last = (((1,), (1,)), ((), ()))
    contract_first = (((0,), (0,)), ((), ()))
    full_down = lax.all_gather(down_weight, ("expert", "dp"), axis=0, tiled=True)
    latent = jnp.dot(tokens, full_down, preferred_element_type=jnp.float32)
    latent = latent.astype(jnp.bfloat16)
    dest = slot_table(routes, capacity)
    source = (
        jnp.full((n_experts * capacity,), entries, jnp.int32)
        .at[dest]
        .set(jnp.arange(entries, dtype=jnp.int32))
    )
    token_of = jnp.where(source < entries, source // top, tok_rows)
    gates = gate_levels.astype(jnp.float32) * gate_unit
    zero_row = jnp.zeros((1, latent_width), jnp.bfloat16)
    latent_pad = jnp.concatenate([latent, zero_row], axis=0)
    send_latent = latent_pad[token_of].reshape(n_major, n_minor, capacity, latent_width)
    scaled = (gates[:, :, None] * latent_grad.astype(jnp.float32)[:, None, :]).astype(jnp.bfloat16)
    scaled_pad = jnp.concatenate([scaled.reshape(entries, latent_width), zero_row], axis=0)
    send_grad = scaled_pad[source].reshape(n_major, n_minor, capacity, latent_width)
    arrived = lax.all_to_all(
        lax.all_to_all(send_latent, "expert", split_axis=0, concat_axis=0, tiled=True),
        "dp",
        split_axis=1,
        concat_axis=1,
        tiled=True,
    )
    rows = arrived.reshape(-1, latent_width)
    weight_in = expert_in[0]
    weight_out = expert_out[0]
    before = jnp.dot(rows, weight_in, preferred_element_type=jnp.float32)
    active = jnp.maximum(before, 0.0)
    hidden = (active * active).astype(jnp.bfloat16)
    result = jnp.dot(hidden, weight_out, preferred_element_type=jnp.float32).astype(jnp.bfloat16)
    returned = lax.all_to_all(
        lax.all_to_all(
            result.reshape(n_major, n_minor, capacity, latent_width),
            "expert",
            split_axis=0,
            concat_axis=0,
            tiled=True,
        ),
        "dp",
        split_axis=1,
        concat_axis=1,
        tiled=True,
    )
    picked = returned.reshape(n_experts * capacity, latent_width)[dest].astype(jnp.float32)
    picked = picked.reshape(tok_rows, top, latent_width)
    latent_out = jnp.sum(gates[:, :, None] * picked, axis=1).astype(jnp.bfloat16)
    arrived_grad = lax.all_to_all(
        lax.all_to_all(send_grad, "expert", split_axis=0, concat_axis=0, tiled=True),
        "dp",
        split_axis=1,
        concat_axis=1,
        tiled=True,
    )
    grad_rows = arrived_grad.reshape(-1, latent_width)
    back_hidden = lax.dot_general(
        grad_rows, weight_out, contract_last, preferred_element_type=jnp.float32
    )
    back_pre = (back_hidden * 2.0 * active).astype(jnp.bfloat16)
    grad_out = lax.dot_general(
        hidden, grad_rows, contract_first, preferred_element_type=jnp.float32
    ).astype(jnp.bfloat16)
    grad_in = lax.dot_general(
        rows, back_pre, contract_first, preferred_element_type=jnp.float32
    ).astype(jnp.bfloat16)
    back_rows = lax.dot_general(
        back_pre, weight_in, contract_last, preferred_element_type=jnp.float32
    ).astype(jnp.bfloat16)
    came_back = lax.all_to_all(
        lax.all_to_all(
            back_rows.reshape(n_major, n_minor, capacity, latent_width),
            "expert",
            split_axis=0,
            concat_axis=0,
            tiled=True,
        ),
        "dp",
        split_axis=1,
        concat_axis=1,
        tiled=True,
    )
    gathered_back = came_back.reshape(n_experts * capacity, latent_width)[dest].astype(jnp.float32)
    latent_delta = jnp.sum(gathered_back.reshape(tok_rows, top, latent_width), axis=1).astype(
        jnp.bfloat16
    )
    grad_tokens = lax.dot_general(
        latent_delta, full_down, contract_last, preferred_element_type=jnp.float32
    )
    grad_tokens = grad_tokens.astype(jnp.bfloat16)
    grad_down = lax.psum_scatter(
        lax.dot_general(tokens, latent_delta, contract_first, preferred_element_type=jnp.float32),
        ("expert", "dp"),
        scatter_dimension=0,
        tiled=True,
    )
    return (latent_out, grad_tokens, grad_down, grad_in[None], grad_out[None])


def solution(mesh):
    in_specs = (
        P(("group", "expert", "dp"), None),
        P(("group", "expert", "dp"), None),
        P(("group", "expert", "dp"), None),
        P(("group", "expert", "dp"), None),
        P(("expert", "dp"), None),
        P(("expert", "dp"), None, None),
        P(("expert", "dp"), None, None),
    )
    out_specs = (
        P(("group", "expert", "dp"), None),
        P(("group", "expert", "dp"), None),
        P(("group", "expert", "dp"), None),
        P(("group", "expert", "dp"), None, None),
        P(("group", "expert", "dp"), None, None),
    )
    return jax.shard_map(
        on_device, mesh=mesh, in_specs=in_specs, out_specs=out_specs, check_vma=False
    )
```

profile of v0, /device:TPU:0, one launch (start us, length us, event | category | flops | bytes accessed | tf_op | source)
XLA Modules:
  0.0 289.0 jit_solution(17984936915933106498)
XLA Ops:
  12.4 4.3 %scatter_custom_fusion = s32[1536]{0:T(1024)S(1)} fusion(s32[1024]{0:T(1024)S(1)} %bitcast.58, s32[1024]{0:T(1024)S(1)} %iota.10, s32[]{:T(128)} %constant.17.clone.1), kind=kCustom, calls=%fused_computation.44 | custom fusion | bytes 6148 | tf_op jit(solution)/shard_map/scatter | solution.py:36
  16.8 5.4 %gather_fusion.2 = bf16[1536,512]{1,0:T(8,128)(2,1)} fusion(bf16[1025,512]{1,0:T(8,128)(2,1)S(1)} %concatenate.7, s32[2048]{0:T(1024)S(1)} %pad_clamp_fusion), kind=kCustom, calls=%fused_computation.2 | custom fusion | bytes 3151872 | tf_op jit(solution)/shard_map/gather | solution.py:45
  22.2 7.3 %all-to-all-start.4 = ((bf16[8,2,96,512]{3,2,1,0:T(8,128)(2,1)}), bf16[8,2,96,512]{3,2,1,0:T(8,128)(2,1)S(1)}, u32[]{:S(2)}, u32[]{:S(2)}) async-start(bf16[8,2,96,512]{3,2,1,0:T(8,128)(2,1)} %bitcast.53), calls=%async_computation.4 | async-start | bytes 3145728 | tf_op jit(solution)/shard_map/all_to_all | solution.py:77
  29.5 45.7 %all-to-all-done.4 = bf16[8,2,96,512]{3,2,1,0:T(8,128)(2,1)S(1)} async-done(((bf16[8,2,96,512]{3,2,1,0:T(8,128)(2,1)}), bf16[8,2,96,512]{3,2,1,0:T(8,128)(2,1)S(1)}, u32[]{:S(2)}, u32[]{:S(2)}) %all-to-all-start.4) | async-done | bytes 1572896 | tf_op jit(solution)/shard_map/all_to_all | solution.py:77
  76.5 3.8 %all-to-all-start.5 = ((bf16[8,2,96,512]{3,2,0,1:T(8,128)(2,1)}), bf16[8,2,96,512]{3,2,0,1:T(8,128)(2,1)S(1)}, u32[]{:S(2)}, u32[]{:S(2)}) async-start(bf16[8,2,96,512]{3,2,0,1:T(8,128)(2,1)} %copy.64), calls=%async_computation.5 | async-start | bytes 3145728 | tf_op jit(solution)/shard_map/all_to_all | solution.py:76
  82.4 5.4 %gather_fusion = bf16[1536,512]{1,0:T(8,128)(2,1)} fusion(bf16[129,512]{1,0:T(8,128)(2,1)S(1)} %concatenate.6, s32[2048]{0:T(1024)S(1)} %pad_clamp_fusion.1), kind=kCustom, calls=%fused_computation | custom fusion | bytes 3151872 | tf_op jit(solution)/shard_map/gather | solution.py:42
  87.8 4.3 %all-to-all-start = ((bf16[8,2,96,512]{3,2,1,0:T(8,128)(2,1)}), bf16[8,2,96,512]{3,2,1,0:T(8,128)(2,1)}, u32[]{:S(2)}, u32[]{:S(2)}) async-start(bf16[8,2,96,512]{3,2,1,0:T(8,128)(2,1)} %bitcast.52), calls=%async_computation | async-start | bytes 3145728 | tf_op jit(solution)/shard_map/all_to_all | solution.py:47
  93.4 36.6 %all-to-all-done = bf16[8,2,96,512]{3,2,1,0:T(8,128)(2,1)} async-done(((bf16[8,2,96,512]{3,2,1,0:T(8,128)(2,1)}), bf16[8,2,96,512]{3,2,1,0:T(8,128)(2,1)}, u32[]{:S(2)}, u32[]{:S(2)}) %all-to-all-start) | async-done | bytes 1572896 | tf_op jit(solution)/shard_map/all_to_all | solution.py:47
  131.5 5.0 %all_to_all.40 = bf16[8,2,96,512]{3,2,0,1:T(8,128)(2,1)S(1)} all-to-all(bf16[8,2,96,512]{3,2,0,1:T(8,128)(2,1)S(1)} %copy.59), channel_id=1, replica_groups=mesh['group'=2,'expert'=8,'dp'=2] {'dp'}, dimensions={1} | all-to-all | bytes 3145728 | tf_op jit(solution)/shard_map/all_to_all | solution.py:46
  139.9 2.2 convolution_convert_fusion
  142.1 3.6 %all-to-all-start.6 = ((bf16[8,2,96,512]{3,2,1,0:T(8,128)(2,1)}), bf16[8,2,96,512]{3,2,1,0:T(8,128)(2,1)S(1)}, u32[]{:S(2)}, u32[]{:S(2)}) async-start(bf16[8,2,96,512]{3,2,1,0:T(8,128)(2,1)} %bitcast.57), calls=%async_computation.6 | async-start | bytes 3145728 | tf_op jit(solution)/shard_map/all_to_all | solution.py:98
  145.8 37.4 %all-to-all-done.6 = bf16[8,2,96,512]{3,2,1,0:T(8,128)(2,1)S(1)} async-done(((bf16[8,2,96,512]{3,2,1,0:T(8,128)(2,1)}), bf16[8,2,96,512]{3,2,1,0:T(8,128)(2,1)S(1)}, u32[]{:S(2)}, u32[]{:S(2)}) %all-to-all-start.6) | async-done | bytes 1572896 | tf_op jit(solution)/shard_map/all_to_all | solution.py:98
  183.3 5.0 %all_to_all.41 = bf16[8,2,96,512]{3,2,0,1:T(8,128)(2,1)S(1)} all-to-all(bf16[8,2,96,512]{3,2,0,1:T(8,128)(2,1)S(1)} %copy.66), channel_id=1, replica_groups=mesh['group'=2,'expert'=8,'dp'=2] {'dp'}, dimensions={1} | all-to-all | bytes 3145728 | tf_op jit(solution)/shard_map/all_to_all | solution.py:97
  188.4 4.0 %gather_fusion.3 = bf16[1024,512]{1,0:T(8,128)(2,1)S(1)} fusion(bf16[1536,512]{1,0:T(8,128)(2,1)S(1)} %bitcast.49, s32[1024]{0:T(1024)S(1)} %broadcast_clamp_fusion), kind=kCustom, calls=%fused_computation.3 | custom fusion | bytes 2101248 | tf_op jit(solution)/shard_map/gather | solution.py:110
  193.1 3.7 %convolution_bitcast_fusion = f32[2048,512]{0,1:T(8,128)} fusion(bf16[128,512]{1,0:T(8,128)(2,1)S(1)} %bitcast_reduce_fusion, bf16[128,2048]{1,0:T(8,128)(2,1)} %param.7), kind=kOutput, calls=%fused_computation.11 | convolution fusion | flops 268435456 | bytes 4849664 | tf_op jit(solution)/shard_map/dot_general | solution.py:119
  197.8 4.0 %convolution_convert_fusion.1 = bf16[1536,512]{1,0:T(8,128)(2,1)} fusion(f32[1536,512]{1,0:T(8,128)} %copy-done.1, bf16[1,512,512]{2,1,0:T(8,128)(2,1)S(1)} %copy-done.9), kind=kOutput, calls=%fused_computation.14 | convolution fusion | flops 807665664 | bytes 5242880 | tf_op jit(solution)/shard_map/dot_general | solution.py:59
  201.8 4.6 %all-to-all-start.2 = ((bf16[8,2,96,512]{3,2,1,0:T(8,128)(2,1)}), bf16[8,2,96,512]{3,2,1,0:T(8,128)(2,1)}, u32[]{:S(2)}, u32[]{:S(2)}) async-start(bf16[8,2,96,512]{3,2,1,0:T(8,128)(2,1)} %bitcast.54), calls=%async_computation.2 | async-start | bytes 3145728 | tf_op jit(solution)/shard_map/all_to_all | solution.py:61
  206.5 3.4 %fusion.5 = bf16[1,512,512]{2,1,0:T(8,128)(2,1)} fusion(bf16[1536,512]{1,0:T(8,128)(2,1)S(1)} %bitcast.51, bf16[1536,512]{1,0:T(8,128)(2,1)} %copy-done.5), kind=kOutput, calls=%fused_computation.23 | convolution fusion | flops 805568512 | bytes 3670016 | tf_op jit(solution)/shard_map/dot_general | solution.py:91
  209.9 3.3 %fusion.6 = bf16[1,512,512]{2,1,0:T(8,128)(2,1)} fusion(bf16[1536,512]{1,0:T(8,128)(2,1)} %bitcast.55, f32[1536,512]{1,0:T(8,128)S(1)} %copy-done.2), kind=kOutput, calls=%fused_computation.24 | convolution fusion | flops 807141376 | bytes 5242880 | tf_op jit(solution)/shard_map/dot_general | solution.py:88
  213.2 47.1 %all-to-all-done.2 = bf16[8,2,96,512]{3,2,1,0:T(8,128)(2,1)} async-done(((bf16[8,2,96,512]{3,2,1,0:T(8,128)(2,1)}), bf16[8,2,96,512]{3,2,1,0:T(8,128)(2,1)}, u32[]{:S(2)}, u32[]{:S(2)}) %all-to-all-start.2) | async-done | bytes 1572896 | tf_op jit(solution)/shard_map/all_to_all | solution.py:61
  261.9 5.0 %all_to_all.42 = bf16[8,2,96,512]{3,2,0,1:T(8,128)(2,1)S(1)} all-to-all(bf16[8,2,96,512]{3,2,0,1:T(8,128)(2,1)S(1)} %copy.61), channel_id=1, replica_groups=mesh['group'=2,'expert'=8,'dp'=2] {'dp'}, dimensions={1} | all-to-all | bytes 3145728 | tf_op jit(solution)/shard_map/all_to_all | solution.py:60
  267.0 4.0 %gather_fusion.1 = bf16[1024,512]{1,0:T(8,128)(2,1)S(1)} fusion(bf16[1536,512]{1,0:T(8,128)(2,1)S(1)} %bitcast.48, s32[1024]{0:T(1024)S(1)} %broadcast_clamp_fusion), kind=kCustom, calls=%fused_computation.1 | custom fusion | bytes 2101248 | tf_op jit(solution)/shard_map/gather | solution.py:73
  272.3 3.2 %convolution_convert_fusion.2 = bf16[128,2048]{1,0:T(8,128)(2,1)} fusion(bf16[128,512]{1,0:T(8,128)(2,1)S(1)} %bitcast_reduce_fusion, bf16[2048,512]{1,0:T(8,128)(2,1)} %all-gather.2.cloned.1.call-done), kind=kOutput, calls=%fused_computation.16 | convolution fusion | flops 268697600 | bytes 2752512 | tf_op jit(solution)/shard_map/dot_general | solution.py:114
  275.5 4.9 %reduce-scatter.2.cloned.1.call-done = f32[128,512]{0,1:T(8,128)} async-done(((f32[2048,512]{0,1:T(8,128)}), f32[128,512]{0,1:T(8,128)}) %reduce-scatter.2.cloned.1.call-update) | async-done | bytes 262160 | tf_op jit(solution)/shard_map/reduce_scatter | solution.py:118
  (59 shorter events, 21.5 us)
Async XLA Ops:
  7.2 129.5 %copy-start = (bf16[1,512,512]{2,1,0:T(8,128)(2,1)S(1)}, bf16[1,512,512]{2,1,0:T(8,128)(2,1)}, u32[]{:S(2)}) copy-start(bf16[1,512,512]{2,1,0:T(8,128)(2,1)} %param.12) | copy-start | bytes 1572868
  7.2 73.1 %all-gather.2.cloned.1.call-start = ((), (), s32[]{:S(2)}) async-start(), calls=%async_computation.9 | async-start | bytes 2228224 | tf_op jit(solution)/shard_map/all_gather | solution.py:29
  22.2 53.0 %all-to-all-start.4 = ((bf16[8,2,96,512]{3,2,1,0:T(8,128)(2,1)}), bf16[8,2,96,512]{3,2,1,0:T(8,128)(2,1)S(1)}, u32[]{:S(2)}, u32[]{:S(2)}) async-start(bf16[8,2,96,512]{3,2,1,0:T(8,128)(2,1)} %bitcast.53), calls=%async_computation.4 | async-start | bytes 3145728 | tf_op jit(solution)/shard_map/all_to_all | solution.py:77
  76.5 3.8 %copy-start.7 = (bf16[128,2048]{1,0:T(8,128)(2,1)S(1)}, bf16[128,2048]{1,0:T(8,128)(2,1)}, u32[]{:S(2)}) copy-start(bf16[128,2048]{1,0:T(8,128)(2,1)} %param.7) | copy-start | bytes 1572868
  76.5 11.3 %all-to-all-start.5 = ((bf16[8,2,96,512]{3,2,0,1:T(8,128)(2,1)}), bf16[8,2,96,512]{3,2,0,1:T(8,128)(2,1)S(1)}, u32[]{:S(2)}, u32[]{:S(2)}) async-start(bf16[8,2,96,512]{3,2,0,1:T(8,128)(2,1)} %copy.64), calls=%async_computation.5 | async-start | bytes 3145728 | tf_op jit(solution)/shard_map/all_to_all | solution.py:76
  87.8 42.2 %all-to-all-start = ((bf16[8,2,96,512]{3,2,1,0:T(8,128)(2,1)}), bf16[8,2,96,512]{3,2,1,0:T(8,128)(2,1)}, u32[]{:S(2)}, u32[]{:S(2)}) async-start(bf16[8,2,96,512]{3,2,1,0:T(8,128)(2,1)} %bitcast.52), calls=%async_computation | async-start | bytes 3145728 | tf_op jit(solution)/shard_map/all_to_all | solution.py:47
  136.7 1.2 copy-start.3
  136.7 2.0 copy-start.6
  136.7 2.1 copy-start.8
  137.8 2.1 copy-start.1
  139.9 2.2 copy-start.5
  142.1 41.1 %all-to-all-start.6 = ((bf16[8,2,96,512]{3,2,1,0:T(8,128)(2,1)}), bf16[8,2,96,512]{3,2,1,0:T(8,128)(2,1)S(1)}, u32[]{:S(2)}, u32[]{:S(2)}) async-start(bf16[8,2,96,512]{3,2,1,0:T(8,128)(2,1)} %bitcast.57), calls=%async_computation.6 | async-start | bytes 3145728 | tf_op jit(solution)/shard_map/all_to_all | solution.py:98
  145.7 134.7 %reduce-scatter.2.cloned.1.call-start = ((), (), s32[]{:S(2)}) async-start(), calls=%async_computation.10 | async-start | bytes 4456448 | tf_op jit(solution)/shard_map/reduce_scatter | solution.py:118
  196.8 1.0 copy-start.9
  201.8 4.6 %copy-start.4 = (bf16[8,2,96,512]{3,2,1,0:T(8,128)(2,1)S(1)}, bf16[8,2,96,512]{3,2,1,0:T(8,128)(2,1)}, u32[]{:S(2)}) copy-start(bf16[8,2,96,512]{3,2,1,0:T(8,128)(2,1)} %copy-done.3) | copy-start | bytes 4718596
  201.8 58.5 %all-to-all-start.2 = ((bf16[8,2,96,512]{3,2,1,0:T(8,128)(2,1)}), bf16[8,2,96,512]{3,2,1,0:T(8,128)(2,1)}, u32[]{:S(2)}, u32[]{:S(2)}) async-start(bf16[8,2,96,512]{3,2,1,0:T(8,128)(2,1)} %bitcast.54), calls=%async_computation.2 | async-start | bytes 3145728 | tf_op jit(solution)/shard_map/all_to_all | solution.py:61
  206.5 3.4 %copy-start.2 = (f32[1536,512]{1,0:T(8,128)S(1)}, f32[1536,512]{1,0:T(8,128)}, u32[]{:S(2)}) copy-start(f32[1536,512]{1,0:T(8,128)} %copy-done.1) | copy-start | bytes 9437188
Sparse Core Ops, SparseCore 0:
  10.2 61.6 all-gather.1
  196.9 83.4 reduce-scatter.1
where the time goes:
time: 290 us; the launch traced here: 289 us
  waiting for transfers between devices  172 us (59%)
  local copies, waits for them, and re-layouts  34.5 us (12%)
  matrix products  24 us (8%)
  starting transfers between devices  23.6 us (8%)
  blocking collectives  15 us (5%)
  between operations  14.3 us (5%)
  other arithmetic  5.21 us (2%)
    all_to_all x1, waiting for transfers between devices, on_device(): lax.all_to_all(result.reshape(n_major, n_minor, capacity, latent_width),...  47.1 us
    all_to_all x1, waiting for transfers between devices, on_device(): lax.all_to_all(send_grad, 'expert', split_axis=0, concat_axis=0, tiled=True)  45.7 us
    all_to_all x1, waiting for transfers between devices, on_device(): lax.all_to_all(back_rows.reshape(n_major, n_minor, capacity, latent_width...  37.4 us
    all_to_all x1, waiting for transfers between devices, on_device(): lax.all_to_all(send_latent, 'expert', split_axis=0, concat_axis=0, tiled=...  36.6 us
    all_to_all x1, starting transfers between devices, on_device(): lax.all_to_all(send_grad, 'expert', split_axis=0, concat_axis=0, tiled=True)  7.25 us
  transfers between devices with their start and end apart: 7, of which 5 were waited for; matrix products, arithmetic and copies ran while one was open for 16% of the time, Pallas kernels for 0%

commit v1 on v0

--- a/solution.py
+++ b/solution.py
@@ -4,6 +4,130 @@
 from jax.sharding import PartitionSpec as P
 
 gate_unit = 1.0 / 1024.0
+contract_last = (((1,), (1,)), ((), ()))
+contract_first = (((0,), (0,)), ((), ()))
+plane = ("expert", "dp")
+
+
+def device_pairs(n_line, move):
+    pairs = []
+    for z in range(n_line):
+        for x in range(2):
+            for c in range(2):
+                to_z, to_x, to_c = move(z, x, c)
+                pairs.append(((z * 2 + x) * 2 + c, (to_z * 2 + to_x) * 2 + to_c))
+    return pairs
+
+
+def turn(value, n_line, by):
+    return lax.ppermute(value, plane, device_pairs(n_line, lambda z, x, c: ((z + by) % n_line, x, c)))
+
+
+def swap_x(value, n_line):
+    return lax.ppermute(value, plane, device_pairs(n_line, lambda z, x, c: (z, 1 - x, c)))
+
+
+def swap_core(value, n_line):
+    return lax.ppermute(value, plane, device_pairs(n_line, lambda z, x, c: (z, x, 1 - c)))
+
+
+def spread(rows, n_line):
+    line = jnp.stack([rows] + [turn(rows, n_line, by) for by in range(1, n_line)])
+    sheet = jnp.stack([line, swap_x(line, n_line)])
+    return jnp.stack([sheet, swap_core(sheet, n_line)])
+
+
+def add_up(parts, n_line):
+    wide = jnp.float32
+    half = parts[0].astype(wide) + swap_core(parts[1], n_line).astype(wide)
+    half = half.astype(jnp.bfloat16)
+    line = half[0].astype(wide) + swap_x(half[1], n_line).astype(wide)
+    line = line.astype(jnp.bfloat16)
+    return add_line(line, n_line)
+
+
+def add_line(line, n_line):
+    total = line[0].astype(jnp.float32)
+    for back in range(1, n_line):
+        total = total + turn(line[back], n_line, n_line - back).astype(jnp.float32)
+    return total
+
+
+def all_rows(tokens, routes, gate_levels, latent_grad, down_weight, expert_in, expert_out):
+    tok_rows = tokens.shape[0]
+    width = tokens.shape[1]
+    latent_width = down_weight.shape[1]
+    n_major = lax.axis_size("expert")
+    n_line = n_major // 2
+    n_experts = n_major * 2
+    block = width // n_experts
+    place = lax.axis_index("expert")
+    my_z, my_x, my_c = place // 2, place % 2, lax.axis_index("dp")
+    core, side, back = jnp.meshgrid(jnp.arange(2), jnp.arange(2), jnp.arange(n_line), indexing="ij")
+    order = ((my_z - back) % n_line * 2 + (my_x + side) % 2) * 2 + (my_c + core) % 2
+    order = order.reshape(-1).astype(jnp.int32)
+
+    experts = jnp.arange(n_experts, dtype=jnp.int32)
+    levels = jnp.sum(
+        jnp.where(routes[:, :, None] == experts, gate_levels[:, :, None], 0), axis=1
+    )
+    gates = levels.astype(jnp.float32) * gate_unit
+    all_gates = lax.all_gather(gates.T, plane, axis=0, tiled=False)
+    my_expert = place * 2 + my_c
+    my_gates = lax.dynamic_index_in_dim(all_gates, my_expert, 1, keepdims=False)[order].reshape(-1, 1)
+
+    full_down = spread(down_weight, n_line).reshape(width, latent_width)
+    token_blocks = tokens.reshape(tok_rows, n_experts, block)
+    turned_tokens = jnp.take(token_blocks, order, axis=1).reshape(tok_rows, width)
+    latent = jnp.dot(turned_tokens, full_down, preferred_element_type=jnp.float32)
+    latent = latent.astype(jnp.bfloat16)
+    rows = spread(latent, n_line).reshape(-1, latent_width)
+    cotangent = spread(latent_grad, n_line).reshape(-1, latent_width)
+    scaled = (my_gates * cotangent.astype(jnp.float32)).astype(jnp.bfloat16)
+
+    weight_in = expert_in[0]
+    weight_out = expert_out[0]
+    before = jnp.dot(rows, weight_in, preferred_element_type=jnp.float32)
+    active = jnp.maximum(before, 0.0)
+    hidden = (active * active).astype(jnp.bfloat16)
+    result = jnp.dot(hidden, weight_out, preferred_element_type=jnp.float32).astype(jnp.bfloat16)
+    back_hidden = lax.dot_general(
+        scaled, weight_out, contract_last, preferred_element_type=jnp.float32
+    )
+    back_pre = (back_hidden * 2.0 * active).astype(jnp.bfloat16)
+    grad_out = lax.dot_general(
+        hidden, scaled, contract_first, preferred_element_type=jnp.float32
+    ).astype(jnp.bfloat16)
+    grad_in = lax.dot_general(
+        rows, back_pre, contract_first, preferred_element_type=jnp.float32
+    ).astype(jnp.bfloat16)
+    back_rows = lax.dot_general(
+        back_pre, weight_in, contract_last, preferred_element_type=jnp.float32
+    ).astype(jnp.bfloat16)
+    parts = (2, 2, n_line, tok_rows, latent_width)
+    latent_delta = add_up(back_rows.reshape(parts), n_line).astype(jnp.bfloat16)
+    weighted = (my_gates * result.astype(jnp.float32)).astype(jnp.bfloat16)
+    latent_out = add_up(weighted.reshape(parts), n_line).astype(jnp.bfloat16)
+
+    turned_grad = lax.dot_general(
+        latent_delta, full_down, contract_last, preferred_element_type=jnp.float32
+    ).astype(jnp.bfloat16)
+    undo = jnp.zeros((n_experts,), jnp.int32).at[order].set(experts)
+    grad_tokens = jnp.take(turned_grad.reshape(tok_rows, n_experts, block), undo, axis=1)
+    grad_tokens = grad_tokens.reshape(tok_rows, width)
+
+    kept = turned_tokens.reshape(tok_rows, 2, 2, n_line * block).transpose(1, 2, 0, 3)
+    by_x = jnp.stack([kept[:, 0], swap_x(kept[:, 1], n_line)])
+    by_core = jnp.stack([by_x[:, 0], swap_core(by_x[:, 1], n_line)])
+    near_tokens = by_core.reshape(4 * tok_rows, n_line * block)
+    near_delta = jnp.stack([latent_delta, swap_x(latent_delta, n_line)])
+    near_delta = jnp.stack([near_delta, swap_core(near_delta, n_line)])
+    near_delta = near_delta.reshape(4 * tok_rows, latent_width)
+    partial = lax.dot_general(
+        near_tokens, near_delta, contract_first, preferred_element_type=jnp.float32
+    )
+    grad_down = add_line(partial.astype(jnp.bfloat16).reshape(n_line, block, latent_width), n_line)
+    return (latent_out, grad_tokens, grad_down, grad_in[None], grad_out[None])
 
 
 def slot_table(routes, capacity):
@@ -15,7 +139,7 @@
     return flat * capacity + placed
 
 
-def on_device(tokens, routes, gate_levels, latent_grad, down_weight, expert_in, expert_out):
+def routed_rows(tokens, routes, gate_levels, latent_grad, down_weight, expert_in, expert_out):
     tok_rows = tokens.shape[0]
     top = routes.shape[1]
     latent_width = down_weight.shape[1]
@@ -124,6 +248,13 @@
     return (latent_out, grad_tokens, grad_down, grad_in[None], grad_out[None])
 
 
+def on_device(tokens, routes, *others):
+    n_major = lax.axis_size("expert")
+    n_experts = n_major * lax.axis_size("dp")
+    few = n_experts <= 2 * routes.shape[1] and n_major % 2 == 0 and lax.axis_size("dp") == 2
+    return (all_rows if few else routed_rows)(tokens, routes, *others)
+
+
 def solution(mesh):
     in_specs = (
         P(("group", "expert", "dp"), None),

time: 290 us -> 164 us (0.57)
  waiting for transfers between devices: 172 us -> 57.2 us
  local copies, waits for them, and re-layouts: 34.5 us -> 8.59 us
  other arithmetic: 5.21 us -> 21.9 us
  starting transfers between devices: 23.6 us -> 38.2 us
  between operations: 14.3 us -> 1.14 us
  matrix products: 24 us -> 12.1 us
  blocking collectives: 15 us -> 24.2 us
    all_to_all x5 -> x0, waiting for transfers between devices: 167 us -> none  [the longest x1 47.1 us: on_device(): lax.all_to_all(result.reshape(n_major, n_minor, capacity, latent_width),...]
    ppermute x0 -> x32, waiting for transfers between devices: none -> 57.2 us  [the longest x7 28.2 us: swap_x(): lax.ppermute(value, plane, device_pairs(n_line, lambda z, x, c: (z, 1 - x...]
    ppermute x0 -> x32, starting transfers between devices: none -> 38.2 us  [the longest x18 28.7 us: turn(): lax.ppermute(value, plane, device_pairs(n_line, lambda z, x, c: ((z + by)...]
    all_gather x0 -> x1, blocking collectives: none -> 24.2 us  [all_rows(): all_gates = lax.all_gather(gates.T, plane, axis=0, tiled=False)]
    all_to_all x5 -> x0, starting transfers between devices: 23.6 us -> none  [the longest x1 7.25 us: on_device(): lax.all_to_all(send_grad, 'expert', split_axis=0, concat_axis=0, tiled=True)]
    gather x4 -> x3, local copies, waits for them, and re-layouts: 18.7 us -> 1.86 us  [the longest x1 0.65 us: all_rows(): jnp.take(token_blocks, order, axis=1).reshape(tok_rows, width)]
    all_to_all x3 -> x0, blocking collectives: 15 us -> none  [the longest x1 5 us: on_device(): lax.all_to_all(lax.all_to_all(send_latent, 'expert', split_axis=0, concat...]
    another operation x0 -> x10, other arithmetic: none -> 14.1 us  [the longest x5 8.65 us: spread(): return jnp.stack([sheet, swap_core(sheet, n_line)])]
  transfers between devices with their start and end apart: 7 -> 32, of which waited for: 5 -> 12; matrix products, arithmetic and copies ran while one was open for 16% -> 26% of each run, Pallas kernels for 0% -> 0%
where the time goes in v1:
time: 164 us; the launch traced here: 163 us
  waiting for transfers between devices  57.2 us (35%)
  starting transfers between devices  38.2 us (23%)
  blocking collectives  24.2 us (15%)
  other arithmetic  21.9 us (13%)
  matrix products  12.1 us (7%)
  local copies, waits for them, and re-layouts  8.59 us (5%)
    ppermute x18, starting transfers between devices, turn(): lax.ppermute(value, plane, device_pairs(n_line, lambda z, x, c: ((z + by)...  28.7 us
    ppermute x7, waiting for transfers between devices, swap_x(): lax.ppermute(value, plane, device_pairs(n_line, lambda z, x, c: (z, 1 - x...  28.2 us
    ppermute x18, waiting for transfers between devices, turn(): lax.ppermute(value, plane, device_pairs(n_line, lambda z, x, c: ((z + by)...  27.8 us
    all_gather x1, blocking collectives, all_rows(): all_gates = lax.all_gather(gates.T, plane, axis=0, tiled=False)  24.2 us
    another operation x5, other arithmetic, spread(): return jnp.stack([sheet, swap_core(sheet, n_line)])  8.65 us
    ppermute x7, starting transfers between devices, swap_x(): lax.ppermute(value, plane, device_pairs(n_line, lambda z, x, c: (z, 1 - x...  8.43 us
    convert_element_type x3, other arithmetic, all_rows(): scaled = (my_gates * cotangent.astype(jnp.float32)).astype(jnp.bfloat16)  4.02 us
  transfers between devices with their start and end apart: 32, of which 12 were waited for; matrix products, arithmetic and copies ran while one was open for 26% of the time, Pallas kernels for 0%

profile of v1, /device:TPU:0, one launch (start us, length us, event | category | flops | bytes accessed | tf_op | source)
XLA Modules:
  0.0 163.2 jit_solution(10120264724508805451)
XLA Ops:
  0.6 3.1 %collective-permute-start = (bf16[128,512]{1,0:T(8,128)(2,1)}, bf16[128,512]{1,0:T(8,128)(2,1)S(1)}, u32[]{:S(2)}, u32[]{:S(2)}) collective-permute-start(bf16[128,512]{1,0:T(8,128)(2,1)} %param.13), channel_id=1, source_target_pairs={{0,4},{1,5},{2,6},{3,7},{4,8},{5,9},{6,10},{7,11},{8,12},{9,13},{1... | collective-permute-start | bytes 393224 | tf_op jit(solution)/shard_map/ppermute | solution.py:23
  3.7 2.1 %collective-permute-start.2 = (bf16[128,512]{1,0:T(8,128)(2,1)}, bf16[128,512]{1,0:T(8,128)(2,1)S(1)}, u32[]{:S(2)}, u32[]{:S(2)}) collective-permute-start(bf16[128,512]{1,0:T(8,128)(2,1)} %param.13), channel_id=1, source_target_pairs={{0,12},{1,13},{2,14},{3,15},{4,0},{5,1},{6,2},{7,3},{8,4},{9,5},{1... | collective-permute-start | bytes 393224 | tf_op jit(solution)/shard_map/ppermute | solution.py:23
  8.3 2.2 %collective-permute-start.17 = (bf16[128,512]{1,0:T(8,128)(2,1)}, bf16[128,512]{1,0:T(8,128)(2,1)}, u32[]{:S(2)}, u32[]{:S(2)}) collective-permute-start(bf16[128,512]{1,0:T(8,128)(2,1)} %param.12), channel_id=1, source_target_pairs={{0,12},{1,13},{2,14},{3,15},{4,0},{5,1},{6,2},{7,3},{8,4},{9,5},{1... | collective-permute-start | bytes 393224 | tf_op jit(solution)/shard_map/ppermute | solution.py:23
  10.6 5.7 %collective-permute-start.16 = (bf16[128,512]{1,0:T(8,128)(2,1)}, bf16[128,512]{1,0:T(8,128)(2,1)}, u32[]{:S(2)}, u32[]{:S(2)}) collective-permute-start(bf16[128,512]{1,0:T(8,128)(2,1)} %param.12), channel_id=1, source_target_pairs={{0,8},{1,9},{2,10},{3,11},{4,12},{5,13},{6,14},{7,15},{8,0},{9,1},... | collective-permute-start | bytes 393224 | tf_op jit(solution)/shard_map/ppermute | solution.py:23
  16.3 5.4 %collective-permute-done.1 = bf16[128,512]{1,0:T(8,128)(2,1)S(1)} collective-permute-done((bf16[128,512]{1,0:T(8,128)(2,1)}, bf16[128,512]{1,0:T(8,128)(2,1)S(1)}, u32[]{:S(2)}, u32[]{:S(2)}) %collective-permute-start.1) | collective-permute-done | bytes 131104 | tf_op jit(solution)/shard_map/ppermute | solution.py:23
  22.6 1.8 %collective-permute-start.3 = (bf16[4,128,512]{2,1,0:T(8,128)(2,1)S(1)}, bf16[4,128,512]{2,1,0:T(8,128)(2,1)S(1)}, u32[]{:S(2)}, u32[]{:S(2)}) collective-permute-start(bf16[4,128,512]{2,1,0:T(8,128)(2,1)S(1)} %get-tuple-element.46), channel_id=1, source_target_pairs={{0,2},{1,3},{2,0},{3,1},{4,6},{5,7},{6,4},{7,5},{8,10},{9,11},{10,... | collective-permute-start | bytes 1572872 | tf_op jit(solution)/shard_map/ppermute | solution.py:27
  26.5 9.8 %collective-permute-done.3 = bf16[4,128,512]{2,1,0:T(8,128)(2,1)S(1)} collective-permute-done((bf16[4,128,512]{2,1,0:T(8,128)(2,1)S(1)}, bf16[4,128,512]{2,1,0:T(8,128)(2,1)S(1)}, u32[]{:S(2)}, u32[]{:S(2)}) %collective-permute-start.3) | collective-permute-done | bytes 524320 | tf_op jit(solution)/shard_map/ppermute | solution.py:27
  45.5 1.9 %collective-permute-start.5 = (bf16[128,512]{1,0:T(8,128)(2,1)S(1)}, bf16[128,512]{1,0:T(8,128)(2,1)S(1)}, u32[]{:S(2)}, u32[]{:S(2)}) collective-permute-start(bf16[128,512]{1,0:T(8,128)(2,1)S(1)} %convolution_convert_fusion.5), channel_id=1, source_target_pairs={{0,4},{1,5},{2,6},{3,7},{4,8},{5,9},{6,10},{7,11},{8,12},{9,13},{1... | collective-permute-start | bytes 393224 | tf_op jit(solution)/shard_map/ppermute | solution.py:23
  47.4 4.7 %collective-permute-done.7 = bf16[128,512]{1,0:T(8,128)(2,1)S(1)} collective-permute-done((bf16[128,512]{1,0:T(8,128)(2,1)S(1)}, bf16[128,512]{1,0:T(8,128)(2,1)S(1)}, u32[]{:S(2)}, u32[]{:S(2)}) %collective-permute-start.7) | collective-permute-done | bytes 131104 | tf_op jit(solution)/shard_map/ppermute | solution.py:23
  52.2 5.2 %collective-permute-done.6 = bf16[128,512]{1,0:T(8,128)(2,1)S(1)} collective-permute-done((bf16[128,512]{1,0:T(8,128)(2,1)S(1)}, bf16[128,512]{1,0:T(8,128)(2,1)S(1)}, u32[]{:S(2)}, u32[]{:S(2)}) %collective-permute-start.6) | collective-permute-done | bytes 131104 | tf_op jit(solution)/shard_map/ppermute | solution.py:23
  61.5 24.2 %all-gather = f32[256,128]{1,0:T(8,128)S(1)} all-gather(f32[16,128]{1,0:T(8,128)S(1)} %multiply_bitcast_fusion), channel_id=2, replica_groups=mesh['group'=2,'expert'=8,'dp'=2] {'expert','dp'}, dimensions={0}, use_global_device_ids=true | all-gather | bytes 139264 | tf_op jit(solution)/shard_map/all_gather | solution.py:75
  86.5 2.5 %fusion.49 = (bf16[1,2,4,128,512]{4,3,2,1,0:T(8,128)(2,1)}, bf16[2,4,128,512]{3,2,1,0:T(8,128)(2,1)}) fusion(bf16[1,4,128,512]{3,2,1,0:T(8,128)(2,1)} %bitcast.22, bf16[1,4,128,512]{3,2,1,0:T(8,128)(2,1)S(1)} %get-tuple-element.43), kind=kLoop, calls=%fused_computation.136 | loop fusion | flops 524288 | bytes 3145728 | tf_op jit(solution)/shard_map/stack | solution.py:37
  90.0 1.8 %fusion.21 = (bf16[1,2,128,512]{2,3,1,0:T(8,128)(2,1)}, bf16[2,128,512]{1,2,0:T(8,128)(2,1)}) fusion(bf16[1,2,128,512]{2,3,0,1:T(8,128)(2,1)S(1)} %get-tuple-element.33, bf16[1,2,128,512]{2,3,0,1:T(8,128)(2,1)} %bitcast.61), kind=kLoop, calls=%fused_computation.60 | loop fusion | flops 262144 | bytes 1048576 | tf_op jit(solution)/shard_map/stack;squeeze | solution.py:121
  91.9 1.9 %maximum_convert_fusion = f32[2,2,4,128,512]{4,3,2,1,0:T(8,128)S(1)} fusion(bf16[1,2,4,128,512]{4,3,2,1,0:T(8,128)(2,1)} %bitcast.44, bf16[1,2,4,128,512]{4,3,2,1,0:T(8,128)(2,1)} %get-tuple-element.22), kind=kLoop, calls=%fused_computation.15 | loop fusion | flops 2097152 | bytes 6291456 | tf_op jit(solution)/shard_map/convert_element_type | solution.py:86
  103.6 2.1 %fusion.5 = bf16[1,512,512]{2,1,0:T(8,128)(2,1)} fusion(bf16[2048,512]{1,0:T(8,128)(2,1)S(1)} %fusion, f32[2048,512]{1,0:T(8,128)S(1)} %fusion.18), kind=kOutput, calls=%fused_computation.25 | convolution fusion | flops 1077149696 | bytes 6815744 | tf_op jit(solution)/shard_map/dot_general | solution.py:98
  107.7 2.1 %collective-permute-start.11 = (bf16[4,128,512]{2,1,0:T(8,128)(2,1)S(1)}, bf16[4,128,512]{2,1,0:T(8,128)(2,1)S(1)}, u32[]{:S(2)}, u32[]{:S(2)}) collective-permute-start(bf16[4,128,512]{2,1,0:T(8,128)(2,1)S(1)} %slice_bitcast_fusion.2), channel_id=1, source_target_pairs={{0,2},{1,3},{2,0},{3,1},{4,6},{5,7},{6,4},{7,5},{8,10},{9,11},{10,... | collective-permute-start | bytes 1572872 | tf_op jit(solution)/shard_map/ppermute | solution.py:27
  109.8 2.1 %fusion.4 = bf16[1,512,512]{2,1,0:T(8,128)(2,1)} fusion(bf16[2048,512]{1,0:T(8,128)(2,1)S(1)} %bitcast.152, bf16[2048,512]{1,0:T(8,128)(2,1)S(1)} %multiply_convert_fusion), kind=kOutput, calls=%fused_computation.24 | convolution fusion | flops 1074003968 | bytes 4718592 | tf_op jit(solution)/shard_map/dot_general | solution.py:101
  111.8 10.2 %collective-permute-done.21 = bf16[4,128,512]{2,1,0:T(8,128)(2,1)S(1)} collective-permute-done((bf16[4,128,512]{2,1,0:T(8,128)(2,1)S(1)}, bf16[4,128,512]{2,1,0:T(8,128)(2,1)S(1)}, u32[]{:S(2)}, u32[]{:S(2)}) %collective-permute-start.21) | collective-permute-done | bytes 524320 | tf_op jit(solution)/shard_map/ppermute | solution.py:27
  124.9 7.8 %collective-permute-done.11 = bf16[4,128,512]{2,1,0:T(8,128)(2,1)S(1)} collective-permute-done((bf16[4,128,512]{2,1,0:T(8,128)(2,1)S(1)}, bf16[4,128,512]{2,1,0:T(8,128)(2,1)S(1)}, u32[]{:S(2)}, u32[]{:S(2)}) %collective-permute-start.11) | collective-permute-done | bytes 524320 | tf_op jit(solution)/shard_map/ppermute | solution.py:27
  132.9 1.8 %collective-permute-done.23 = bf16[128,512]{1,0:T(8,128)(2,1)S(1)} collective-permute-done((bf16[128,512]{1,0:T(8,128)(2,1)S(1)}, bf16[128,512]{1,0:T(8,128)(2,1)S(1)}, u32[]{:S(2)}, u32[]{:S(2)}) %collective-permute-start.23) | collective-permute-done | bytes 131104 | tf_op jit(solution)/shard_map/ppermute | solution.py:23
  136.2 2.8 %collective-permute-start.12 = (bf16[128,512]{1,0:T(8,128)(2,1)}, bf16[128,512]{1,0:T(8,128)(2,1)S(1)}, u32[]{:S(2)}, u32[]{:S(2)}) collective-permute-start(bf16[128,512]{1,0:T(8,128)(2,1)} %get-tuple-element.40), channel_id=1, source_target_pairs={{0,12},{1,13},{2,14},{3,15},{4,0},{5,1},{6,2},{7,3},{8,4},{9,5},{1... | collective-permute-start | bytes 393224 | tf_op jit(solution)/shard_map/ppermute | solution.py:23
  145.1 3.0 %collective-permute-start.29 = (bf16[128,512]{1,0:T(8,128)(2,1)S(1)}, bf16[128,512]{1,0:T(8,128)(2,1)S(1)}, u32[]{:S(2)}, u32[]{:S(2)}) collective-permute-start(bf16[128,512]{1,0:T(8,128)(2,1)S(1)} %get-tuple-element.28), channel_id=1, source_target_pairs={{0,12},{1,13},{2,14},{3,15},{4,0},{5,1},{6,2},{7,3},{8,4},{9,5},{1... | collective-permute-start | bytes 393224 | tf_op jit(solution)/shard_map/ppermute | solution.py:23
  153.0 3.4 %collective-permute-done.31 = bf16[128,512]{1,0:T(8,128)(2,1)S(1)} collective-permute-done((bf16[128,512]{1,0:T(8,128)(2,1)S(1)}, bf16[128,512]{1,0:T(8,128)(2,1)S(1)}, u32[]{:S(2)}, u32[]{:S(2)}) %collective-permute-start.31) | collective-permute-done | bytes 131104 | tf_op jit(solution)/shard_map/ppermute | solution.py:23
  156.4 6.1 %collective-permute-done.30 = bf16[128,512]{1,0:T(8,128)(2,1)S(1)} collective-permute-done((bf16[128,512]{1,0:T(8,128)(2,1)S(1)}, bf16[128,512]{1,0:T(8,128)(2,1)S(1)}, u32[]{:S(2)}, u32[]{:S(2)}) %collective-permute-start.30) | collective-permute-done | bytes 131104 | tf_op jit(solution)/shard_map/ppermute | solution.py:23
  (130 shorter events, 48.4 us)
Async XLA Ops:
  0.6 9.9 %collective-permute-start = (bf16[128,512]{1,0:T(8,128)(2,1)}, bf16[128,512]{1,0:T(8,128)(2,1)S(1)}, u32[]{:S(2)}, u32[]{:S(2)}) collective-permute-start(bf16[128,512]{1,0:T(8,128)(2,1)} %param.13), channel_id=1, source_target_pairs={{0,4},{1,5},{2,6},{3,7},{4,8},{5,9},{6,10},{7,11},{8,12},{9,13},{1... | collective-permute-start | bytes 393224 | tf_op jit(solution)/shard_map/ppermute | solution.py:23
  3.7 12.5 %collective-permute-start.2 = (bf16[128,512]{1,0:T(8,128)(2,1)}, bf16[128,512]{1,0:T(8,128)(2,1)S(1)}, u32[]{:S(2)}, u32[]{:S(2)}) collective-permute-start(bf16[128,512]{1,0:T(8,128)(2,1)} %param.13), channel_id=1, source_target_pairs={{0,12},{1,13},{2,14},{3,15},{4,0},{5,1},{6,2},{7,3},{8,4},{9,5},{1... | collective-permute-start | bytes 393224 | tf_op jit(solution)/shard_map/ppermute | solution.py:23
  5.8 15.8 %collective-permute-start.1 = (bf16[128,512]{1,0:T(8,128)(2,1)}, bf16[128,512]{1,0:T(8,128)(2,1)S(1)}, u32[]{:S(2)}, u32[]{:S(2)}) collective-permute-start(bf16[128,512]{1,0:T(8,128)(2,1)} %param.13), channel_id=1, source_target_pairs={{0,8},{1,9},{2,10},{3,11},{4,12},{5,13},{6,14},{7,15},{8,0},{9,1},... | collective-permute-start | bytes 393224 | tf_op jit(solution)/shard_map/ppermute | solution.py:23
  6.8 34.9 %collective-permute-start.15 = (bf16[128,512]{1,0:T(8,128)(2,1)}, bf16[128,512]{1,0:T(8,128)(2,1)S(1)}, u32[]{:S(2)}, u32[]{:S(2)}) collective-permute-start(bf16[128,512]{1,0:T(8,128)(2,1)} %param.12), channel_id=1, source_target_pairs={{0,4},{1,5},{2,6},{3,7},{4,8},{5,9},{6,10},{7,11},{8,12},{9,13},{1... | collective-permute-start | bytes 393224 | tf_op jit(solution)/shard_map/ppermute | solution.py:23
  8.3 33.4 %collective-permute-start.17 = (bf16[128,512]{1,0:T(8,128)(2,1)}, bf16[128,512]{1,0:T(8,128)(2,1)}, u32[]{:S(2)}, u32[]{:S(2)}) collective-permute-start(bf16[128,512]{1,0:T(8,128)(2,1)} %param.12), channel_id=1, source_target_pairs={{0,12},{1,13},{2,14},{3,15},{4,0},{5,1},{6,2},{7,3},{8,4},{9,5},{1... | collective-permute-start | bytes 393224 | tf_op jit(solution)/shard_map/ppermute | solution.py:23
  10.6 31.1 %collective-permute-start.16 = (bf16[128,512]{1,0:T(8,128)(2,1)}, bf16[128,512]{1,0:T(8,128)(2,1)}, u32[]{:S(2)}, u32[]{:S(2)}) collective-permute-start(bf16[128,512]{1,0:T(8,128)(2,1)} %param.12), channel_id=1, source_target_pairs={{0,8},{1,9},{2,10},{3,11},{4,12},{5,13},{6,14},{7,15},{8,0},{9,1},... | collective-permute-start | bytes 393224 | tf_op jit(solution)/shard_map/ppermute | solution.py:23
  22.6 13.7 %collective-permute-start.3 = (bf16[4,128,512]{2,1,0:T(8,128)(2,1)S(1)}, bf16[4,128,512]{2,1,0:T(8,128)(2,1)S(1)}, u32[]{:S(2)}, u32[]{:S(2)}) collective-permute-start(bf16[4,128,512]{2,1,0:T(8,128)(2,1)S(1)} %get-tuple-element.46), channel_id=1, source_target_pairs={{0,2},{1,3},{2,0},{3,1},{4,6},{5,7},{6,4},{7,5},{8,10},{9,11},{10,... | collective-permute-start | bytes 1572872 | tf_op jit(solution)/shard_map/ppermute | solution.py:27
  39.6 50.3 %collective-permute-start.25 = (bf16[2,128,512]{1,2,0:T(8,128)(2,1)}, bf16[2,128,512]{1,2,0:T(8,128)(2,1)}, u32[]{:S(2)}, u32[]{:S(2)}) collective-permute-start(bf16[2,128,512]{1,2,0:T(8,128)(2,1)} %get-tuple-element.34), channel_id=1, source_target_pairs={{0,2},{1,3},{2,0},{3,1},{4,6},{5,7},{6,4},{7,5},{8,10},{9,11},{10,... | collective-permute-start | bytes 786440 | tf_op jit(solution)/shard_map/ppermute | solution.py:27
  42.8 17.2 %collective-permute-start.18 = (bf16[4,128,512]{2,1,0:T(8,128)(2,1)S(1)}, bf16[4,128,512]{2,1,0:T(8,128)(2,1)S(1)}, u32[]{:S(2)}, u32[]{:S(2)}) collective-permute-start(bf16[4,128,512]{2,1,0:T(8,128)(2,1)S(1)} %get-tuple-element.39), channel_id=1, source_target_pairs={{0,2},{1,3},{2,0},{3,1},{4,6},{5,7},{6,4},{7,5},{8,10},{9,11},{10,... | collective-permute-start | bytes 1572872 | tf_op jit(solution)/shard_map/ppermute | solution.py:27
  45.4 12.0 %collective-permute-start.6 = (bf16[128,512]{1,0:T(8,128)(2,1)S(1)}, bf16[128,512]{1,0:T(8,128)(2,1)S(1)}, u32[]{:S(2)}, u32[]{:S(2)}) collective-permute-start(bf16[128,512]{1,0:T(8,128)(2,1)S(1)} %convolution_convert_fusion.5), channel_id=1, source_target_pairs={{0,8},{1,9},{2,10},{3,11},{4,12},{5,13},{6,14},{7,15},{8,0},{9,1},... | collective-permute-start | bytes 393224 | tf_op jit(solution)/shard_map/ppermute | solution.py:23
  45.5 11.9 %collective-permute-start.5 = (bf16[128,512]{1,0:T(8,128)(2,1)S(1)}, bf16[128,512]{1,0:T(8,128)(2,1)S(1)}, u32[]{:S(2)}, u32[]{:S(2)}) collective-permute-start(bf16[128,512]{1,0:T(8,128)(2,1)S(1)} %convolution_convert_fusion.5), channel_id=1, source_target_pairs={{0,4},{1,5},{2,6},{3,7},{4,8},{5,9},{6,10},{7,11},{8,12},{9,13},{1... | collective-permute-start | bytes 393224 | tf_op jit(solution)/shard_map/ppermute | solution.py:23
  58.3 28.2 %collective-permute-start.8 = (bf16[4,128,512]{2,1,0:T(8,128)(2,1)}, bf16[4,128,512]{2,1,0:T(8,128)(2,1)}, u32[]{:S(2)}, u32[]{:S(2)}) collective-permute-start(bf16[4,128,512]{2,1,0:T(8,128)(2,1)} %get-tuple-element.44), channel_id=1, source_target_pairs={{0,2},{1,3},{2,0},{3,1},{4,6},{5,7},{6,4},{7,5},{8,10},{9,11},{10,... | collective-permute-start | bytes 1572872 | tf_op jit(solution)/shard_map/ppermute | solution.py:27
  61.5 30.5 %collective-permute-start.19 = (bf16[2,4,128,512]{3,2,1,0:T(8,128)(2,1)}, bf16[2,4,128,512]{3,2,1,0:T(8,128)(2,1)}, u32[]{:S(2)}, u32[]{:S(2)}) collective-permute-start(bf16[2,4,128,512]{3,2,1,0:T(8,128)(2,1)} %get-tuple-element.23), channel_id=1, source_target_pairs={{0,1},{1,0},{2,3},{3,2},{4,5},{5,4},{6,7},{7,6},{8,9},{9,8},{10,11... | collective-permute-start | bytes 3145736 | tf_op jit(solution)/shard_map/ppermute | solution.py:31
  91.8 51.8 %collective-permute-start.26 = (bf16[2,128,512]{1,2,0:T(8,128)(2,1)}, bf16[2,128,512]{1,2,0:T(8,128)(2,1)}, u32[]{:S(2)}, u32[]{:S(2)}) collective-permute-start(bf16[2,128,512]{1,2,0:T(8,128)(2,1)} %get-tuple-element.32), channel_id=1, source_target_pairs={{0,1},{1,0},{2,3},{3,2},{4,5},{5,4},{6,7},{7,6},{8,9},{9,8},{10,11... | collective-permute-start | bytes 786440 | tf_op jit(solution)/shard_map/ppermute | solution.py:31
  107.3 14.8 %collective-permute-start.21 = (bf16[4,128,512]{2,1,0:T(8,128)(2,1)S(1)}, bf16[4,128,512]{2,1,0:T(8,128)(2,1)S(1)}, u32[]{:S(2)}, u32[]{:S(2)}) collective-permute-start(bf16[4,128,512]{2,1,0:T(8,128)(2,1)S(1)} %slice_bitcast_fusion), channel_id=1, source_target_pairs={{0,2},{1,3},{2,0},{3,1},{4,6},{5,7},{6,4},{7,5},{8,10},{9,11},{10,... | collective-permute-start | bytes 1572872 | tf_op jit(solution)/shard_map/ppermute | solution.py:27
  107.7 25.0 %collective-permute-start.11 = (bf16[4,128,512]{2,1,0:T(8,128)(2,1)S(1)}, bf16[4,128,512]{2,1,0:T(8,128)(2,1)S(1)}, u32[]{:S(2)}, u32[]{:S(2)}) collective-permute-start(bf16[4,128,512]{2,1,0:T(8,128)(2,1)S(1)} %slice_bitcast_fusion.2), channel_id=1, source_target_pairs={{0,2},{1,3},{2,0},{3,1},{4,6},{5,7},{6,4},{7,5},{8,10},{9,11},{10,... | collective-permute-start | bytes 1572872 | tf_op jit(solution)/shard_map/ppermute | solution.py:27
  122.2 10.6 %collective-permute-start.22 = (bf16[128,512]{1,0:T(8,128)(2,1)S(1)}, bf16[128,512]{1,0:T(8,128)(2,1)S(1)}, u32[]{:S(2)}, u32[]{:S(2)}) collective-permute-start(bf16[128,512]{1,0:T(8,128)(2,1)S(1)} %get-tuple-element.35), channel_id=1, source_target_pairs={{0,12},{1,13},{2,14},{3,15},{4,0},{5,1},{6,2},{7,3},{8,4},{9,5},{1... | collective-permute-start | bytes 393224 | tf_op jit(solution)/shard_map/ppermute | solution.py:23
  123.7 9.1 %collective-permute-start.24 = (bf16[128,512]{1,0:T(8,128)(2,1)S(1)}, bf16[128,512]{1,0:T(8,128)(2,1)S(1)}, u32[]{:S(2)}, u32[]{:S(2)}) collective-permute-start(bf16[128,512]{1,0:T(8,128)(2,1)S(1)} %get-tuple-element.36), channel_id=1, source_target_pairs={{0,4},{1,5},{2,6},{3,7},{4,8},{5,9},{6,10},{7,11},{8,12},{9,13},{1... | collective-permute-start | bytes 393224 | tf_op jit(solution)/shard_map/ppermute | solution.py:23
  124.3 10.4 %collective-permute-start.23 = (bf16[128,512]{1,0:T(8,128)(2,1)S(1)}, bf16[128,512]{1,0:T(8,128)(2,1)S(1)}, u32[]{:S(2)}, u32[]{:S(2)}) collective-permute-start(bf16[128,512]{1,0:T(8,128)(2,1)S(1)} %get-tuple-element.37), channel_id=1, source_target_pairs={{0,8},{1,9},{2,10},{3,11},{4,12},{5,13},{6,14},{7,15},{8,0},{9,1},... | collective-permute-start | bytes 393224 | tf_op jit(solution)/shard_map/ppermute | solution.py:23
  136.2 12.6 %collective-permute-start.12 = (bf16[128,512]{1,0:T(8,128)(2,1)}, bf16[128,512]{1,0:T(8,128)(2,1)S(1)}, u32[]{:S(2)}, u32[]{:S(2)}) collective-permute-start(bf16[128,512]{1,0:T(8,128)(2,1)} %get-tuple-element.40), channel_id=1, source_target_pairs={{0,12},{1,13},{2,14},{3,15},{4,0},{5,1},{6,2},{7,3},{8,4},{9,5},{1... | collective-permute-start | bytes 393224 | tf_op jit(solution)/shard_map/ppermute | solution.py:23
  138.9 11.2 %collective-permute-start.14 = (bf16[128,512]{1,0:T(8,128)(2,1)}, bf16[128,512]{1,0:T(8,128)(2,1)}, u32[]{:S(2)}, u32[]{:S(2)}) collective-permute-start(bf16[128,512]{1,0:T(8,128)(2,1)} %get-tuple-element.41), channel_id=1, source_target_pairs={{0,4},{1,5},{2,6},{3,7},{4,8},{5,9},{6,10},{7,11},{8,12},{9,13},{1... | collective-permute-start | bytes 393224 | tf_op jit(solution)/shard_map/ppermute | solution.py:23
  138.9 11.2 %collective-permute-start.13 = (bf16[128,512]{1,0:T(8,128)(2,1)}, bf16[128,512]{1,0:T(8,128)(2,1)}, u32[]{:S(2)}, u32[]{:S(2)}) collective-permute-start(bf16[128,512]{1,0:T(8,128)(2,1)} %get-tuple-element.42), channel_id=1, source_target_pairs={{0,8},{1,9},{2,10},{3,11},{4,12},{5,13},{6,14},{7,15},{8,0},{9,1},... | collective-permute-start | bytes 393224 | tf_op jit(solution)/shard_map/ppermute | solution.py:23
  148.1 8.2 %collective-permute-start.31 = (bf16[128,512]{1,0:T(8,128)(2,1)S(1)}, bf16[128,512]{1,0:T(8,128)(2,1)S(1)}, u32[]{:S(2)}, u32[]{:S(2)}) collective-permute-start(bf16[128,512]{1,0:T(8,128)(2,1)S(1)} %get-tuple-element.29), channel_id=1, source_target_pairs={{0,4},{1,5},{2,6},{3,7},{4,8},{5,9},{6,10},{7,11},{8,12},{9,13},{1... | collective-permute-start | bytes 393224 | tf_op jit(solution)/shard_map/ppermute | solution.py:23
  148.7 13.7 %collective-permute-start.30 = (bf16[128,512]{1,0:T(8,128)(2,1)S(1)}, bf16[128,512]{1,0:T(8,128)(2,1)S(1)}, u32[]{:S(2)}, u32[]{:S(2)}) collective-permute-start(bf16[128,512]{1,0:T(8,128)(2,1)S(1)} %get-tuple-element.30), channel_id=1, source_target_pairs={{0,8},{1,9},{2,10},{3,11},{4,12},{5,13},{6,14},{7,15},{8,0},{9,1},... | collective-permute-start | bytes 393224 | tf_op jit(solution)/shard_map/ppermute | solution.py:23
  (16 other events, 158.1 us)

commit v2 on v0

--- a/solution.py
+++ b/solution.py
@@ -1,9 +1,300 @@
+import functools
+
 import jax
 import jax.numpy as jnp
 from jax import lax
+from jax.experimental import pallas as pl
+from jax.experimental.pallas import tpu as pltpu
 from jax.sharding import PartitionSpec as P
 
 gate_unit = 1.0 / 1024.0
+contract_last = (((1,), (1,)), ((), ()))
+contract_first = (((0,), (0,)), ((), ()))
+plane = ("expert", "dp")
+wide = jnp.float32
+narrow = jnp.bfloat16
+
+
+def device_pairs(n_line, move):
+    pairs = []
+    for z in range(n_line):
+        for x in range(2):
+            for c in range(2):
+                to_z, to_x, to_c = move(z, x, c)
+                pairs.append(((z * 2 + x) * 2 + c, (to_z * 2 + to_x) * 2 + to_c))
+    return pairs
+
+
+def turn(value, n_line, by):
+    return lax.ppermute(value, plane, device_pairs(n_line, lambda z, x, c: ((z + by) % n_line, x, c)))
+
+
+def swap(value, n_line, core, side):
+    return lax.ppermute(value, plane, device_pairs(n_line, lambda z, x, c: (z, x ^ side, c ^ core)))
+
+
+def after(value, *earlier):
+    return lax.optimization_barrier((value,) + earlier)[0]
+
+
+def call(body, outs, name, scratch=(), flops=0, nbytes=0):
+    vmem = pl.BlockSpec(memory_space=pltpu.VMEM)
+
+    def run(place, *operands):
+        return pl.pallas_call(
+            body,
+            out_shape=outs,
+            in_specs=[pl.BlockSpec(memory_space=pltpu.SMEM)] + [vmem] * len(operands),
+            out_specs=[vmem] * len(outs),
+            scratch_shapes=list(scratch),
+            compiler_params=pltpu.CompilerParams(vmem_limit_bytes=40 * 1024 * 1024),
+            cost_estimate=pl.CostEstimate(flops=flops, bytes_accessed=nbytes, transcendentals=0),
+            name=name,
+        )(place, *operands)
+
+    return run
+
+
+def prepare_body(n_line, block, place, tokens, routes, levels, cotangent, *outs):
+    pieces, payload = outs[:4], outs[4]
+    for core in range(2):
+        for side in range(2):
+            owner = (place[1] ^ side) * 2 + (place[2] ^ core)
+            for z in range(n_line):
+                start = pl.multiple_of((z * 4 + owner) * block, block)
+                pieces[core * 2 + side][:, z * block : (z + 1) * block] = tokens[:, pl.ds(start, block)]
+    tok_rows = cotangent.shape[0]
+    gate_rows = payload.shape[0] - tok_rows
+    payload[:tok_rows, :] = cotangent[...]
+    expert = lax.broadcasted_iota(jnp.int32, (gate_rows, tok_rows), 0)
+    total = jnp.zeros((gate_rows, tok_rows), jnp.int32)
+    for k in range(routes.shape[0]):
+        total = total + jnp.where(expert == routes[k : k + 1, :], levels[k : k + 1, :], 0)
+    low = total & 31
+    payload[tok_rows:, :tok_rows] = (total - low).astype(wide).astype(narrow)
+    payload[tok_rows:, tok_rows : 2 * tok_rows] = low.astype(wide).astype(narrow)
+    rest = payload.shape[1] - 2 * tok_rows
+    payload[tok_rows:, 2 * tok_rows :] = jnp.zeros((gate_rows, rest), narrow)
+
+
+def project_body(n_line, place, *refs):
+    pieces, downs = refs[:4], refs[4 : 4 + n_line]
+    keep, send, down = refs[4 + n_line :]
+    block = downs[0].shape[0]
+    for back in range(n_line):
+        z = lax.rem(place[0] + n_line - back, n_line)
+        down[pl.ds(pl.multiple_of(z * block, block), block), :] = downs[back][...]
+    for core, out in ((1, send), (0, keep)):
+        for side in range(2):
+            out[side] = jnp.dot(pieces[core * 2 + side][...], down[...], preferred_element_type=wide)
+
+
+def gate_tile(payload, tok_rows, expert):
+    packed = payload[tok_rows:, :]
+    rows = lax.broadcasted_iota(jnp.int32, (packed.shape[0], 128), 0)
+    pick = jnp.where(rows == expert, 1.0, 0.0).astype(narrow)
+    dot = functools.partial(lax.dot_general, dimension_numbers=contract_first, preferred_element_type=wide)
+    total = dot(packed[:, :tok_rows], pick) + dot(packed[:, tok_rows : 2 * tok_rows], pick)
+    return total * gate_unit
+
+
+def expert_body(count, place, *refs):
+    rows_in, payloads = refs[:count], refs[count : 2 * count]
+    weights = refs[2 * count : 2 * count + 4]
+    outs = refs[2 * count + 4 :]
+    combined, deltas = outs[:count], outs[count : 2 * count]
+    hiddens, scaleds, back_pres = outs[2 * count :]
+    tok_rows, width = rows_in[0].shape
+    for first in range(0, count, 2):
+        pair = (first, first + 1)
+        span = slice(first * tok_rows, (first + 2) * tok_rows)
+        rows = jnp.concatenate([rows_in[i][...] for i in pair], axis=0)
+        cotangent = jnp.concatenate([payloads[i][:tok_rows, :] for i in pair], axis=0).astype(wide)
+        out_sum = jnp.zeros((2 * tok_rows, width), wide)
+        delta_sum = jnp.zeros((2 * tok_rows, width), wide)
+        for e in range(2):
+            weight_in, weight_out = weights[2 * e], weights[2 * e + 1]
+            expert = place[3 + e]
+            gate = jnp.concatenate([gate_tile(payloads[i], tok_rows, expert) for i in pair], axis=0)
+            gate = jnp.concatenate([gate] * (width // 128), axis=1)
+            active = jnp.maximum(jnp.dot(rows, weight_in[...], preferred_element_type=wide), 0.0)
+            hidden = (active * active).astype(narrow)
+            hiddens[e, span, :] = hidden
+            scaled = (gate * cotangent).astype(narrow)
+            scaleds[e, span, :] = scaled
+            back_hidden = lax.dot_general(scaled, weight_out[...], contract_last, preferred_element_type=wide)
+            back_pre = (back_hidden * 2.0 * active).astype(narrow)
+            back_pres[e, span, :] = back_pre
+            result = jnp.dot(hidden, weight_out[...], preferred_element_type=wide).astype(narrow)
+            out_sum = out_sum + gate * result.astype(wide)
+            back_rows = lax.dot_general(back_pre, weight_in[...], contract_last, preferred_element_type=wide)
+            delta_sum = delta_sum + back_rows.astype(narrow).astype(wide)
+        for i in pair:
+            part = slice((i - first) * tok_rows, (i - first + 1) * tok_rows)
+            combined[i][...] = out_sum[part].astype(combined[i].dtype)
+            deltas[i][...] = delta_sum[part].astype(deltas[i].dtype)
+
+
+def weight_grad_body(n_rows, n_sets, place, *refs):
+    rows_in = refs[:n_rows]
+    sets = [refs[n_rows + 3 * i : n_rows + 3 * i + 3] for i in range(n_sets)]
+    keep_in, keep_out, send_in, send_out = refs[n_rows + 3 * n_sets :]
+    dot = functools.partial(lax.dot_general, dimension_numbers=contract_first, preferred_element_type=wide)
+    rows = jnp.concatenate([r[...] for r in rows_in], axis=0)
+    for e, out_in, out_out in ((1, send_in, send_out), (0, keep_in, keep_out)):
+        hidden = jnp.concatenate([s[0][e] for s in sets], axis=0)
+        scaled = jnp.concatenate([s[1][e] for s in sets], axis=0)
+        back_pre = jnp.concatenate([s[2][e] for s in sets], axis=0)
+        out_out[...] = dot(hidden, scaled).astype(out_out.dtype)
+        out_in[...] = dot(rows, back_pre).astype(out_in.dtype)
+
+
+def tail_body(n_line, place, *refs):
+    pieces, deltas, down = refs[:4], refs[4:8], refs[8]
+    blocks, grads = refs[9 : 9 + n_line], refs[9 + n_line :]
+    tokens = jnp.concatenate([p[...] for p in pieces], axis=0)
+    delta = jnp.concatenate([d[...] for d in deltas], axis=0)
+    part = lax.dot_general(tokens, delta, contract_first, preferred_element_type=wide)
+    block = blocks[0].shape[0]
+    for z in range(n_line):
+        for back in range(n_line):
+
+            @pl.when(lax.rem(place[0] + n_line - back, n_line) == z)
+            def _(z=z, back=back):
+                blocks[back][...] = part[z * block : (z + 1) * block].astype(blocks[back].dtype)
+
+    for i in range(4):
+        grads[i][...] = lax.dot_general(
+            deltas[i][...], down[...], contract_last, preferred_element_type=wide
+        ).astype(narrow)
+
+
+def arrange_body(n_line, block, place, *refs):
+    pieces, out = refs[:4], refs[4]
+    for core in range(2):
+        for side in range(2):
+            owner = (place[1] ^ side) * 2 + (place[2] ^ core)
+            for z in range(n_line):
+                start = pl.multiple_of((z * 4 + owner) * block, block)
+                out[:, pl.ds(start, block)] = pieces[core * 2 + side][:, z * block : (z + 1) * block]
+
+
+def all_rows(tokens, routes, gate_levels, latent_grad, down_weight, expert_in, expert_out):
+    tok_rows, width = tokens.shape
+    latent_width = down_weight.shape[1]
+    hidden_width = expert_in.shape[2]
+    n_major = lax.axis_size("expert")
+    n_line = n_major // 2
+    n_experts = n_major * 2
+    block = width // n_experts
+    major = lax.axis_index("expert")
+    my_core = lax.axis_index("dp")
+    place = jnp.stack(
+        [major // 2, major % 2, my_core, major * 2 + my_core, major * 2 + 1 - my_core]
+    ).astype(jnp.int32)
+    shape = jax.ShapeDtypeStruct
+    rows_of = lambda kind: shape((tok_rows, latent_width), kind)
+
+    downs = [down_weight] + [turn(down_weight, n_line, back) for back in range(1, n_line)]
+
+    gate_rows = -(-n_experts // 16) * 16
+    prepare = call(
+        functools.partial(prepare_body, n_line, block),
+        [shape((tok_rows, n_line * block), narrow)] * 4 + [shape((tok_rows + gate_rows, latent_width), narrow)],
+        "prepare",
+        nbytes=3 * tok_rows * width * 2,
+    )
+    *columns, payload = prepare(place, tokens, routes.T, gate_levels.T, latent_grad)
+    near_tokens = [
+        columns[core * 2 + side] if core + side == 0 else swap(columns[core * 2 + side], n_line, core, side)
+        for core in range(2)
+        for side in range(2)
+    ]
+    own = (expert_in[0], expert_out[0])
+    weights = own + tuple(swap(w, n_line, 1, 0) for w in own)
+
+    project = call(
+        functools.partial(project_body, n_line),
+        [shape((2, tok_rows, latent_width), wide)] * 2 + [shape((n_line * block, latent_width), narrow)],
+        "project",
+        flops=2 * 4 * tok_rows * n_line * block * latent_width,
+    )
+    keep, send, down = project(place, *near_tokens, *downs)
+    half = keep + swap(send, n_line, 1, 0)
+    latent = (half[0] + swap(half[1], n_line, 0, 1)).astype(narrow)
+
+    payload = after(payload, downs[-1])
+    payloads = [payload] + [turn(payload, n_line, back) for back in range(1, n_line)]
+    far_payloads = [swap(p, n_line, 0, 1) for p in payloads]
+    rows = [latent] + [turn(latent, n_line, back) for back in range(1, n_line)]
+    far_rows = [swap(r, n_line, 0, 1) for r in rows]
+
+    def experts(count, kind, name):
+        saved = shape((2, count * tok_rows, hidden_width), narrow)
+        return call(
+            functools.partial(expert_body, count),
+            [rows_of(kind)] * (2 * count) + [saved] * 3,
+            name,
+            flops=2 * 2 * 4 * count * tok_rows * latent_width * hidden_width,
+            nbytes=4 * latent_width * hidden_width * 2,
+        )
+
+    outs = experts(n_line, wide, "near_experts")(place, *rows, *payloads, *weights)
+    near_out, near_delta, near_saved = outs[:n_line], outs[n_line : 2 * n_line], outs[2 * n_line :]
+    outs = experts(n_line, narrow, "far_experts")(place, *far_rows, *far_payloads, *weights)
+    far_out, far_delta, far_saved = outs[:n_line], outs[n_line : 2 * n_line], outs[2 * n_line :]
+
+    def return_sums(near, far):
+        total = None
+        for back in [*range(1, n_line), 0]:
+            line = near[back] + swap(far[back], n_line, 0, 1).astype(wide)
+            if back:
+                line = turn(line.astype(narrow), n_line, n_line - back).astype(wide)
+            total = line if total is None else total + line
+        return total.astype(narrow)
+
+    delta = return_sums(near_delta, far_delta)
+    latent_out = return_sums(near_out, far_out)
+
+    weight_grad = call(
+        functools.partial(weight_grad_body, 2 * n_line, 2),
+        [shape((latent_width, hidden_width), wide), shape((hidden_width, latent_width), wide)]
+        + [shape((latent_width, hidden_width), narrow), shape((hidden_width, latent_width), narrow)],
+        "weight_grads",
+        flops=2 * 2 * 2 * 2 * n_line * tok_rows * latent_width * hidden_width,
+    )
+    keep_in, keep_out, send_in, send_out = weight_grad(place, *rows, *far_rows, *near_saved, *far_saved)
+    grad_in = (keep_in + swap(send_in, n_line, 1, 0).astype(wide)).astype(narrow)
+    grad_out = (keep_out + swap(send_out, n_line, 1, 0).astype(wide)).astype(narrow)
+
+    side_delta = swap(delta, n_line, 0, 1)
+    deltas = [delta, side_delta, swap(delta, n_line, 1, 0), swap(side_delta, n_line, 1, 0)]
+    tail = call(
+        functools.partial(tail_body, n_line),
+        [shape((block, latent_width), wide)]
+        + [shape((block, latent_width), narrow)] * (n_line - 1)
+        + [shape((tok_rows, n_line * block), narrow)] * 4,
+        "tail",
+        flops=2 * 2 * 4 * tok_rows * n_line * block * latent_width,
+    )
+    outs = tail(place, *near_tokens, *deltas, down)
+    blocks, grads = outs[:n_line], outs[n_line:]
+    grad_down = blocks[0]
+    for back in range(1, n_line):
+        grad_down = grad_down + turn(blocks[back], n_line, n_line - back).astype(wide)
+    grads = [
+        grads[core * 2 + side] if core + side == 0 else swap(grads[core * 2 + side], n_line, core, side)
+        for core in range(2)
+        for side in range(2)
+    ]
+    arrange = call(
+        functools.partial(arrange_body, n_line, block),
+        [shape((tok_rows, width), narrow)],
+        "arrange",
+        nbytes=2 * tok_rows * width * 2,
+    )
+    (grad_tokens,) = arrange(place, *grads)
+    return (latent_out, grad_tokens, grad_down, grad_in[None], grad_out[None])
 
 
 def slot_table(routes, capacity):
@@ -15,7 +306,7 @@
     return flat * capacity + placed
 
 
-def on_device(tokens, routes, gate_levels, latent_grad, down_weight, expert_in, expert_out):
+def routed_rows(tokens, routes, gate_levels, latent_grad, down_weight, expert_in, expert_out):
     tok_rows = tokens.shape[0]
     top = routes.shape[1]
     latent_width = down_weight.shape[1]
@@ -124,6 +415,13 @@
     return (latent_out, grad_tokens, grad_down, grad_in[None], grad_out[None])
 
 
+def on_device(tokens, routes, *others):
+    n_major = lax.axis_size("expert")
+    n_experts = n_major * lax.axis_size("dp")
+    few = n_experts <= 2 * routes.shape[1] and n_major % 4 == 0 and lax.axis_size("dp") == 2
+    return (all_rows if few else routed_rows)(tokens, routes, *others)
+
+
 def solution(mesh):
     in_specs = (
         P(("group", "expert", "dp"), None),

time: 290 us -> 139 us (0.48)
  waiting for transfers between devices: 172 us -> 57.8 us
  starting transfers between devices: 23.6 us -> 58 us
  local copies, waits for them, and re-layouts: 34.5 us -> 2.66 us
  matrix products: 24 us -> 0 us
  Pallas kernels: 0 us -> 15 us
  blocking collectives: 15 us -> 0 us
  between operations: 14.3 us -> 0.85 us
    all_to_all x5 -> x0, waiting for transfers between devices: 167 us -> none  [the longest x1 47.1 us: on_device(): lax.all_to_all(result.reshape(n_major, n_minor, capacity, latent_width),...]
    ppermute x0 -> x49, starting transfers between devices: none -> 58 us  [the longest x18 31.4 us: turn(): lax.ppermute(value, plane, device_pairs(n_line, lambda z, x, c: ((z + by)...]
    ppermute x0 -> x49, waiting for transfers between devices: none -> 57.8 us  [the longest x18 32.5 us: turn(): lax.ppermute(value, plane, device_pairs(n_line, lambda z, x, c: ((z + by)...]
    dot_general x9 -> x0, matrix products: 24 us -> none  [the longest x1 4 us: on_device(): jnp.dot(hidden, weight_out, preferred_element_type=jnp.float32)]
    all_to_all x5 -> x0, starting transfers between devices: 23.6 us -> none  [the longest x1 7.25 us: on_device(): lax.all_to_all(send_grad, 'expert', split_axis=0, concat_axis=0, tiled=True)]
    gather x4 -> x0, local copies, waits for them, and re-layouts: 18.7 us -> none  [the longest x1 5.41 us: on_device(): scaled_pad[source].reshape(n_major, n_minor, capacity, latent_width)]
    all_to_all x3 -> x0, blocking collectives: 15 us -> none  [the longest x1 5 us: on_device(): lax.all_to_all(lax.all_to_all(send_latent, 'expert', split_axis=0, concat...]
    pallas_call x0 -> x7, Pallas kernels: none -> 15 us  [run(): pl.pallas_call(body, out_shape=outs, in_specs=[pl.BlockSpec(memory_space=...]
  transfers between devices with their start and end apart: 7 -> 49, of which waited for: 5 -> 25; matrix products, arithmetic and copies ran while one was open for 16% -> 2% of each run, Pallas kernels for 0% -> 7%
where the time goes in v2:
time: 139 us; the launch traced here: 138 us
  starting transfers between devices  58 us (42%)
  waiting for transfers between devices  57.8 us (42%)
  Pallas kernels  15 us (11%)
  other arithmetic  3.78 us (3%)
  local copies, waits for them, and re-layouts  2.66 us (2%)
    ppermute x18, waiting for transfers between devices, turn(): lax.ppermute(value, plane, device_pairs(n_line, lambda z, x, c: ((z + by)...  32.5 us
    ppermute x18, starting transfers between devices, turn(): lax.ppermute(value, plane, device_pairs(n_line, lambda z, x, c: ((z + by)...  31.4 us
    ppermute x31, starting transfers between devices, swap(): lax.ppermute(value, plane, device_pairs(n_line, lambda z, x, c: (z, x ^ s...  26.6 us
    ppermute x31, waiting for transfers between devices, swap(): lax.ppermute(value, plane, device_pairs(n_line, lambda z, x, c: (z, x ^ s...  25.3 us
    pallas_call x7, Pallas kernels, run(): pl.pallas_call(body, out_shape=outs, in_specs=[pl.BlockSpec(memory_space=...  15 us
  transfers between devices with their start and end apart: 49, of which 25 were waited for; matrix products, arithmetic and copies ran while one was open for 2% of the time, Pallas kernels for 7%

profile of v2, /device:TPU:0, one launch (start us, length us, event | category | flops | bytes accessed | tf_op | source)
XLA Modules:
  0.0 138.0 jit_solution(16280034871923471359)
XLA Ops:
  4.0 3.0 %collective-permute-start = (bf16[128,512]{1,0:T(8,128)(2,1)S(1)}, bf16[128,512]{1,0:T(8,128)(2,1)S(1)}, u32[]{:S(2)}, u32[]{:S(2)}) collective-permute-start(bf16[128,512]{1,0:T(8,128)(2,1)S(1)} %get-tuple-element.49), channel_id=1, source_target_pairs={{0,2},{1,3},{2,0},{3,1},{4,6},{5,7},{6,4},{7,5},{8,10},{9,11},{10,... | collective-permute-start | bytes 393224 | tf_op jit(solution)/shard_map/ppermute | solution.py:33
  7.2 2.0 %collective-permute-start.3 = (bf16[128,512]{1,0:T(8,128)(2,1)S(1)}, bf16[128,512]{1,0:T(8,128)(2,1)S(1)}, u32[]{:S(2)}, u32[]{:S(2)}) collective-permute-start(bf16[128,512]{1,0:T(8,128)(2,1)S(1)} %copy-done.2), channel_id=1, source_target_pairs={{0,4},{1,5},{2,6},{3,7},{4,8},{5,9},{6,10},{7,11},{8,12},{9,13},{1... | collective-permute-start | bytes 393224 | tf_op jit(solution)/shard_map/ppermute | solution.py:29
  9.2 2.6 %collective-permute-start.4 = (bf16[128,512]{1,0:T(8,128)(2,1)S(1)}, bf16[128,512]{1,0:T(8,128)(2,1)S(1)}, u32[]{:S(2)}, u32[]{:S(2)}) collective-permute-start(bf16[128,512]{1,0:T(8,128)(2,1)S(1)} %copy-done.2), channel_id=1, source_target_pairs={{0,8},{1,9},{2,10},{3,11},{4,12},{5,13},{6,14},{7,15},{8,0},{9,1},... | collective-permute-start | bytes 393224 | tf_op jit(solution)/shard_map/ppermute | solution.py:29
  11.8 3.3 %collective-permute-start.5 = (bf16[128,512]{1,0:T(8,128)(2,1)S(1)}, bf16[128,512]{1,0:T(8,128)(2,1)S(1)}, u32[]{:S(2)}, u32[]{:S(2)}) collective-permute-start(bf16[128,512]{1,0:T(8,128)(2,1)S(1)} %copy-done.2), channel_id=1, source_target_pairs={{0,12},{1,13},{2,14},{3,15},{4,0},{5,1},{6,2},{7,3},{8,4},{9,5},{1... | collective-permute-start | bytes 393224 | tf_op jit(solution)/shard_map/ppermute | solution.py:29
  15.7 5.0 %collective-permute-done.4.refs_6_ = bf16[128,512]{1,0:T(8,128)(2,1)S(1)} collective-permute-done((bf16[128,512]{1,0:T(8,128)(2,1)S(1)}, bf16[128,512]{1,0:T(8,128)(2,1)S(1)}, u32[]{:S(2)}, u32[]{:S(2)}) %collective-permute-start.4) | collective-permute-done | bytes 131104 | tf_op jit(solution)/shard_map/ppermute | solution.py:29
  21.7 3.3 %collective-permute-start.11 = (bf16[144,512]{1,0:T(8,128)(2,1)S(1)}, bf16[144,512]{1,0:T(8,128)(2,1)S(1)}, u32[]{:S(2)}, u32[]{:S(2)}) collective-permute-start(bf16[144,512]{1,0:T(8,128)(2,1)S(1)} %get-tuple-element.55.refs_4_), channel_id=1, source_target_pairs={{0,4},{1,5},{2,6},{3,7},{4,8},{5,9},{6,10},{7,11},{8,12},{9,13},{1... | collective-permute-start | bytes 442376 | tf_op jit(solution)/shard_map/ppermute | solution.py:29
  32.3 5.7 %collective-permute-done.12.refs_6_ = bf16[144,512]{1,0:T(8,128)(2,1)S(1)} collective-permute-done((bf16[144,512]{1,0:T(8,128)(2,1)S(1)}, bf16[144,512]{1,0:T(8,128)(2,1)S(1)}, u32[]{:S(2)}, u32[]{:S(2)}) %collective-permute-start.12) | collective-permute-done | bytes 147488 | tf_op jit(solution)/shard_map/ppermute | solution.py:29
  41.1 3.7 %collective-permute-done.20.refs_4_ = bf16[144,512]{1,0:T(8,128)(2,1)S(1)} collective-permute-done((bf16[144,512]{1,0:T(8,128)(2,1)S(1)}, bf16[144,512]{1,0:T(8,128)(2,1)S(1)}, u32[]{:S(2)}, u32[]{:S(2)}) %collective-permute-start.20) | collective-permute-done | bytes 147488 | tf_op jit(solution)/shard_map/ppermute | solution.py:33
  46.9 3.2 %collective-permute-start.9 = (bf16[128,512]{1,0:T(8,128)(2,1)S(1)}, bf16[128,512]{1,0:T(8,128)(2,1)S(1)}, u32[]{:S(2)}, u32[]{:S(2)}) collective-permute-start(bf16[128,512]{1,0:T(8,128)(2,1)S(1)} %fusion.3.refs_0_), channel_id=1, source_target_pairs={{0,8},{1,9},{2,10},{3,11},{4,12},{5,13},{6,14},{7,15},{8,0},{9,1},... | collective-permute-start | bytes 393224 | tf_op jit(solution)/shard_map/ppermute | solution.py:29
  50.1 4.8 %collective-permute-start.10 = (bf16[128,512]{1,0:T(8,128)(2,1)S(1)}, bf16[128,512]{1,0:T(8,128)(2,1)S(1)}, u32[]{:S(2)}, u32[]{:S(2)}) collective-permute-start(bf16[128,512]{1,0:T(8,128)(2,1)S(1)} %fusion.3.refs_0_), channel_id=1, source_target_pairs={{0,12},{1,13},{2,14},{3,15},{4,0},{5,1},{6,2},{7,3},{8,4},{9,5},{1... | collective-permute-start | bytes 393224 | tf_op jit(solution)/shard_map/ppermute | solution.py:29
  60.3 3.4 %near_experts.1 = (f32[128,512]{1,0:T(8,128)S(1)}, f32[128,512]{1,0:T(8,128)S(1)}, f32[128,512]{1,0:T(8,128)S(1)}, f32[128,512]{1,0:T(8,128)S(1)}, f32[128,512]{...) custom-call(s32[5]{0:T(128)S(1)} %stack.23.place, ...), custom_call_target="tpu_custom_call" | custom-call | flops 2147483648 | bytes 2097152 | tf_op jit(solution)/shard_map/near_experts/pallas_call | solution.py:44
  64.6 2.8 %collective-permute-done.17.refs_1_.refs_5_ = bf16[128,512]{1,0:T(8,128)(2,1)S(1)} collective-permute-done((bf16[128,512]{1,0:T(8,128)(2,1)S(1)}, bf16[128,512]{1,0:T(8,128)(2,1)S(1)}, u32[]{:S(2)}, u32[]{:S(2)}) %collective-permute-start.17) | collective-permute-done | bytes 131104 | tf_op jit(solution)/shard_map/ppermute | solution.py:33
  67.4 2.1 %collective-permute-done.18.refs_2_.refs_6_ = bf16[128,512]{1,0:T(8,128)(2,1)S(1)} collective-permute-done((bf16[128,512]{1,0:T(8,128)(2,1)S(1)}, bf16[128,512]{1,0:T(8,128)(2,1)S(1)}, u32[]{:S(2)}, u32[]{:S(2)}) %collective-permute-start.18) | collective-permute-done | bytes 131104 | tf_op jit(solution)/shard_map/ppermute | solution.py:33
  70.9 3.4 %far_experts.1 = (bf16[128,512]{1,0:T(8,128)(2,1)S(1)}, bf16[128,512]{1,0:T(8,128)(2,1)S(1)}, bf16[128,512]{1,0:T(8,128)(2,1)S(1)}, bf16[128,512]{1,0:T(8,128)(2...) custom-call(s32[5]{0:T(128)S(1)} %stack.23.place, ...), custom_call_target="tpu_custom_call" | custom-call | flops 2147483648 | bytes 2097152 | tf_op jit(solution)/shard_map/far_experts/pallas_call | solution.py:44
  79.6 2.9 %weight_grads.1 = (f32[512,512]{1,0:T(8,128)S(1)}, f32[512,512]{1,0:T(8,128)S(1)}, bf16[512,512]{1,0:T(8,128)(2,1)S(1)}, bf16[512,512]{1,0:T(8,128)(2,1)S(1)}) custom-call(s32[5]{0:T(128)S(1)} %stack.23.place, bf16[128,512]{1,0:T(8,128)(2,1)S(1)} %fusion.3.refs_0_, bf16[128,512]{1,0:T(8,128)(2,1)S(1)} %collective-permute-done.8.refs_1_, ...), custom_call_target="tpu_custom_call" | custom-call | flops 2147483648 | tf_op jit(solution)/shard_map/weight_grads/pallas_call | solution.py:44
  87.6 6.9 %collective-permute-done.35 = bf16[128,512]{1,0:T(8,128)(2,1)S(1)} collective-permute-done((bf16[128,512]{1,0:T(8,128)(2,1)S(1)}, bf16[128,512]{1,0:T(8,128)(2,1)S(1)}, u32[]{:S(2)}, u32[]{:S(2)}) %collective-permute-start.35) | collective-permute-done | bytes 131104 | tf_op jit(solution)/shard_map/ppermute | solution.py:33
  96.0 3.5 %collective-permute-done.31 = bf16[128,512]{1,0:T(8,128)(2,1)S(1)} collective-permute-done((bf16[128,512]{1,0:T(8,128)(2,1)S(1)}, bf16[128,512]{1,0:T(8,128)(2,1)S(1)}, u32[]{:S(2)}, u32[]{:S(2)}) %collective-permute-start.31) | collective-permute-done | bytes 131104 | tf_op jit(solution)/shard_map/ppermute | solution.py:33
  100.3 2.5 %collective-permute-done.36 = bf16[128,512]{1,0:T(8,128)(2,1)S(1)} collective-permute-done((bf16[128,512]{1,0:T(8,128)(2,1)S(1)}, bf16[128,512]{1,0:T(8,128)(2,1)S(1)}, u32[]{:S(2)}, u32[]{:S(2)}) %collective-permute-start.36) | collective-permute-done | bytes 131104 | tf_op jit(solution)/shard_map/ppermute | solution.py:29
  102.9 3.9 %collective-permute-done.34 = bf16[128,512]{1,0:T(8,128)(2,1)S(1)} collective-permute-done((bf16[128,512]{1,0:T(8,128)(2,1)S(1)}, bf16[128,512]{1,0:T(8,128)(2,1)S(1)}, u32[]{:S(2)}, u32[]{:S(2)}) %collective-permute-start.34) | collective-permute-done | bytes 131104 | tf_op jit(solution)/shard_map/ppermute | solution.py:29
  108.6 2.5 %collective-permute-start.25 = (bf16[128,512]{1,0:T(8,128)(2,1)S(1)}, bf16[128,512]{1,0:T(8,128)(2,1)S(1)}, u32[]{:S(2)}, u32[]{:S(2)}) collective-permute-start(bf16[128,512]{1,0:T(8,128)(2,1)S(1)} %add_convert_fusion.9), channel_id=1, source_target_pairs={{0,12},{1,13},{2,14},{3,15},{4,0},{5,1},{6,2},{7,3},{8,4},{9,5},{1... | collective-permute-start | bytes 393224 | tf_op jit(solution)/shard_map/ppermute | solution.py:29
  111.2 5.9 %collective-permute-done.27 = bf16[128,512]{1,0:T(8,128)(2,1)S(1)} collective-permute-done((bf16[128,512]{1,0:T(8,128)(2,1)S(1)}, bf16[128,512]{1,0:T(8,128)(2,1)S(1)}, u32[]{:S(2)}, u32[]{:S(2)}) %collective-permute-start.27) | collective-permute-done | bytes 131104 | tf_op jit(solution)/shard_map/ppermute | solution.py:29
  120.1 2.0 %tail.1 = (f32[128,512]{1,0:T(8,128)S(1)}, bf16[128,512]{1,0:T(8,128)(2,1)S(1)}, bf16[128,512]{1,0:T(8,128)(2,1)S(1)}, bf16[128,512]{1,0:T(8,128)(2,1)S(1)}, bf1...) custom-call(s32[5]{0:T(128)S(1)} %stack.23.place, ...), custom_call_target="tpu_custom_call" | custom-call | flops 536870912 | tf_op jit(solution)/shard_map/tail/pallas_call | solution.py:44
  124.3 2.0 %collective-permute-start.46 = (bf16[128,512]{1,0:T(8,128)(2,1)S(1)}, bf16[128,512]{1,0:T(8,128)(2,1)S(1)}, u32[]{:S(2)}, u32[]{:S(2)}) collective-permute-start(bf16[128,512]{1,0:T(8,128)(2,1)S(1)} %get-tuple-element.80), channel_id=1, source_target_pairs={{0,4},{1,5},{2,6},{3,7},{4,8},{5,9},{6,10},{7,11},{8,12},{9,13},{1... | collective-permute-start | bytes 393224 | tf_op jit(solution)/shard_map/ppermute | solution.py:29
  132.6 4.7 %collective-permute-done.45 = bf16[128,512]{1,0:T(8,128)(2,1)S(1)} collective-permute-done((bf16[128,512]{1,0:T(8,128)(2,1)S(1)}, bf16[128,512]{1,0:T(8,128)(2,1)S(1)}, u32[]{:S(2)}, u32[]{:S(2)}) %collective-permute-start.45) | collective-permute-done | bytes 131104 | tf_op jit(solution)/shard_map/ppermute | solution.py:29
  (110 shorter events, 51.8 us)
Async XLA Ops:
  9.2 11.4 %collective-permute-start.4 = (bf16[128,512]{1,0:T(8,128)(2,1)S(1)}, bf16[128,512]{1,0:T(8,128)(2,1)S(1)}, u32[]{:S(2)}, u32[]{:S(2)}) collective-permute-start(bf16[128,512]{1,0:T(8,128)(2,1)S(1)} %copy-done.2), channel_id=1, source_target_pairs={{0,8},{1,9},{2,10},{3,11},{4,12},{5,13},{6,14},{7,15},{8,0},{9,1},... | collective-permute-start | bytes 393224 | tf_op jit(solution)/shard_map/ppermute | solution.py:29
  25.2 14.9 %collective-permute-start.7 = (f32[128,512]{1,0:T(8,128)S(1)}, f32[128,512]{1,0:T(8,128)S(1)}, u32[]{:S(2)}, u32[]{:S(2)}) collective-permute-start(f32[128,512]{1,0:T(8,128)S(1)} %slice_bitcast_fusion), channel_id=1, source_target_pairs={{0,2},{1,3},{2,0},{3,1},{4,6},{5,7},{6,4},{7,5},{8,10},{9,11},{10,... | collective-permute-start | bytes 786440 | tf_op jit(solution)/shard_map/ppermute | solution.py:33
  26.8 28.2 %collective-permute-start.14 = (bf16[512,512]{1,0:T(8,128)(2,1)S(1)}, bf16[512,512]{1,0:T(8,128)(2,1)S(1)}, u32[]{:S(2)}, u32[]{:S(2)}) collective-permute-start(bf16[512,512]{1,0:T(8,128)(2,1)S(1)} %bitcast.23), channel_id=1, source_target_pairs={{0,1},{1,0},{2,3},{3,2},{4,5},{5,4},{6,7},{7,6},{8,9},{9,8},{10,11... | collective-permute-start | bytes 1572872 | tf_op jit(solution)/shard_map/ppermute | solution.py:33
  26.8 29.4 %collective-permute-start.15 = (bf16[512,512]{1,0:T(8,128)(2,1)S(1)}, bf16[512,512]{1,0:T(8,128)(2,1)S(1)}, u32[]{:S(2)}, u32[]{:S(2)}) collective-permute-start(bf16[512,512]{1,0:T(8,128)(2,1)S(1)} %bitcast.26), channel_id=1, source_target_pairs={{0,1},{1,0},{2,3},{3,2},{4,5},{5,4},{6,7},{7,6},{8,9},{9,8},{10,11... | collective-permute-start | bytes 1572872 | tf_op jit(solution)/shard_map/ppermute | solution.py:33
  27.3 10.8 %collective-permute-start.12 = (bf16[144,512]{1,0:T(8,128)(2,1)S(1)}, bf16[144,512]{1,0:T(8,128)(2,1)S(1)}, u32[]{:S(2)}, u32[]{:S(2)}) collective-permute-start(bf16[144,512]{1,0:T(8,128)(2,1)S(1)} %get-tuple-element.55.refs_4_), channel_id=1, source_target_pairs={{0,8},{1,9},{2,10},{3,11},{4,12},{5,13},{6,14},{7,15},{8,0},{9,1},... | collective-permute-start | bytes 442376 | tf_op jit(solution)/shard_map/ppermute | solution.py:29
  40.1 10.1 %collective-permute-start.22 = (bf16[144,512]{1,0:T(8,128)(2,1)S(1)}, bf16[144,512]{1,0:T(8,128)(2,1)S(1)}, u32[]{:S(2)}, u32[]{:S(2)}) collective-permute-start(bf16[144,512]{1,0:T(8,128)(2,1)S(1)} %collective-permute-done.12.refs_6_), channel_id=1, source_target_pairs={{0,2},{1,3},{2,0},{3,1},{4,6},{5,7},{6,4},{7,5},{8,10},{9,11},{10,... | collective-permute-start | bytes 442376 | tf_op jit(solution)/shard_map/ppermute | solution.py:33
  44.8 12.2 %collective-permute-start.8 = (bf16[128,512]{1,0:T(8,128)(2,1)S(1)}, bf16[128,512]{1,0:T(8,128)(2,1)S(1)}, u32[]{:S(2)}, u32[]{:S(2)}) collective-permute-start(bf16[128,512]{1,0:T(8,128)(2,1)S(1)} %fusion.3.refs_0_), channel_id=1, source_target_pairs={{0,4},{1,5},{2,6},{3,7},{4,8},{5,9},{6,10},{7,11},{8,12},{9,13},{1... | collective-permute-start | bytes 393224 | tf_op jit(solution)/shard_map/ppermute | solution.py:29
  46.9 11.4 %collective-permute-start.9 = (bf16[128,512]{1,0:T(8,128)(2,1)S(1)}, bf16[128,512]{1,0:T(8,128)(2,1)S(1)}, u32[]{:S(2)}, u32[]{:S(2)}) collective-permute-start(bf16[128,512]{1,0:T(8,128)(2,1)S(1)} %fusion.3.refs_0_), channel_id=1, source_target_pairs={{0,8},{1,9},{2,10},{3,11},{4,12},{5,13},{6,14},{7,15},{8,0},{9,1},... | collective-permute-start | bytes 393224 | tf_op jit(solution)/shard_map/ppermute | solution.py:29
  50.1 9.3 %collective-permute-start.10 = (bf16[128,512]{1,0:T(8,128)(2,1)S(1)}, bf16[128,512]{1,0:T(8,128)(2,1)S(1)}, u32[]{:S(2)}, u32[]{:S(2)}) collective-permute-start(bf16[128,512]{1,0:T(8,128)(2,1)S(1)} %fusion.3.refs_0_), channel_id=1, source_target_pairs={{0,12},{1,13},{2,14},{3,15},{4,0},{5,1},{6,2},{7,3},{8,4},{9,5},{1... | collective-permute-start | bytes 393224 | tf_op jit(solution)/shard_map/ppermute | solution.py:29
  57.0 10.4 %collective-permute-start.17 = (bf16[128,512]{1,0:T(8,128)(2,1)S(1)}, bf16[128,512]{1,0:T(8,128)(2,1)S(1)}, u32[]{:S(2)}, u32[]{:S(2)}) collective-permute-start(bf16[128,512]{1,0:T(8,128)(2,1)S(1)} %collective-permute-done.8.refs_1_), channel_id=1, source_target_pairs={{0,2},{1,3},{2,0},{3,1},{4,6},{5,7},{6,4},{7,5},{8,10},{9,11},{10,... | collective-permute-start | bytes 393224 | tf_op jit(solution)/shard_map/ppermute | solution.py:33
  58.3 11.2 %collective-permute-start.18 = (bf16[128,512]{1,0:T(8,128)(2,1)S(1)}, bf16[128,512]{1,0:T(8,128)(2,1)S(1)}, u32[]{:S(2)}, u32[]{:S(2)}) collective-permute-start(bf16[128,512]{1,0:T(8,128)(2,1)S(1)} %collective-permute-done.9.refs_2_), channel_id=1, source_target_pairs={{0,2},{1,3},{2,0},{3,1},{4,6},{5,7},{6,4},{7,5},{8,10},{9,11},{10,... | collective-permute-start | bytes 393224 | tf_op jit(solution)/shard_map/ppermute | solution.py:33
  59.5 11.4 %collective-permute-start.19 = (bf16[128,512]{1,0:T(8,128)(2,1)S(1)}, bf16[128,512]{1,0:T(8,128)(2,1)S(1)}, u32[]{:S(2)}, u32[]{:S(2)}) collective-permute-start(bf16[128,512]{1,0:T(8,128)(2,1)S(1)} %collective-permute-done.10.refs_3_), channel_id=1, source_target_pairs={{0,2},{1,3},{2,0},{3,1},{4,6},{5,7},{6,4},{7,5},{8,10},{9,11},{10,... | collective-permute-start | bytes 393224 | tf_op jit(solution)/shard_map/ppermute | solution.py:33
  74.3 34.3 %collective-permute-start.30 = (bf16[128,512]{1,0:T(8,128)(2,1)S(1)}, bf16[128,512]{1,0:T(8,128)(2,1)S(1)}, u32[]{:S(2)}, u32[]{:S(2)}) collective-permute-start(bf16[128,512]{1,0:T(8,128)(2,1)S(1)} %get-tuple-element.63), channel_id=1, source_target_pairs={{0,2},{1,3},{2,0},{3,1},{4,6},{5,7},{6,4},{7,5},{8,10},{9,11},{10,... | collective-permute-start | bytes 393224 | tf_op jit(solution)/shard_map/ppermute | solution.py:33
  76.4 10.0 %collective-permute-start.26 = (bf16[128,512]{1,0:T(8,128)(2,1)S(1)}, bf16[128,512]{1,0:T(8,128)(2,1)S(1)}, u32[]{:S(2)}, u32[]{:S(2)}) collective-permute-start(bf16[128,512]{1,0:T(8,128)(2,1)S(1)} %get-tuple-element.59), channel_id=1, source_target_pairs={{0,2},{1,3},{2,0},{3,1},{4,6},{5,7},{6,4},{7,5},{8,10},{9,11},{10,... | collective-permute-start | bytes 393224 | tf_op jit(solution)/shard_map/ppermute | solution.py:33
  77.6 22.0 %collective-permute-start.24 = (bf16[128,512]{1,0:T(8,128)(2,1)S(1)}, bf16[128,512]{1,0:T(8,128)(2,1)S(1)}, u32[]{:S(2)}, u32[]{:S(2)}) collective-permute-start(bf16[128,512]{1,0:T(8,128)(2,1)S(1)} %get-tuple-element.57), channel_id=1, source_target_pairs={{0,2},{1,3},{2,0},{3,1},{4,6},{5,7},{6,4},{7,5},{8,10},{9,11},{10,... | collective-permute-start | bytes 393224 | tf_op jit(solution)/shard_map/ppermute | solution.py:33
  78.4 21.8 %collective-permute-start.37 = (bf16[128,512]{1,0:T(8,128)(2,1)S(1)}, bf16[128,512]{1,0:T(8,128)(2,1)S(1)}, u32[]{:S(2)}, u32[]{:S(2)}) collective-permute-start(bf16[128,512]{1,0:T(8,128)(2,1)S(1)} %get-tuple-element.71), channel_id=1, source_target_pairs={{0,2},{1,3},{2,0},{3,1},{4,6},{5,7},{6,4},{7,5},{8,10},{9,11},{10,... | collective-permute-start | bytes 393224 | tf_op jit(solution)/shard_map/ppermute | solution.py:33
  83.6 11.0 %collective-permute-start.35 = (bf16[128,512]{1,0:T(8,128)(2,1)S(1)}, bf16[128,512]{1,0:T(8,128)(2,1)S(1)}, u32[]{:S(2)}, u32[]{:S(2)}) collective-permute-start(bf16[128,512]{1,0:T(8,128)(2,1)S(1)} %get-tuple-element.69), channel_id=1, source_target_pairs={{0,2},{1,3},{2,0},{3,1},{4,6},{5,7},{6,4},{7,5},{8,10},{9,11},{10,... | collective-permute-start | bytes 393224 | tf_op jit(solution)/shard_map/ppermute | solution.py:33
  86.4 9.6 %collective-permute-start.33 = (bf16[128,512]{1,0:T(8,128)(2,1)S(1)}, bf16[128,512]{1,0:T(8,128)(2,1)S(1)}, u32[]{:S(2)}, u32[]{:S(2)}) collective-permute-start(bf16[128,512]{1,0:T(8,128)(2,1)S(1)} %get-tuple-element.67), channel_id=1, source_target_pairs={{0,2},{1,3},{2,0},{3,1},{4,6},{5,7},{6,4},{7,5},{8,10},{9,11},{10,... | collective-permute-start | bytes 393224 | tf_op jit(solution)/shard_map/ppermute | solution.py:33
  100.2 24.1 %collective-permute-start.47 = (bf16[512,512]{1,0:T(8,128)(2,1)S(1)}, bf16[512,512]{1,0:T(8,128)(2,1)S(1)}, u32[]{:S(2)}, u32[]{:S(2)}) collective-permute-start(bf16[512,512]{1,0:T(8,128)(2,1)S(1)} %get-tuple-element.88), channel_id=1, source_target_pairs={{0,1},{1,0},{2,3},{3,2},{4,5},{5,4},{6,7},{7,6},{8,9},{9,8},{10,11... | collective-permute-start | bytes 1572872 | tf_op jit(solution)/shard_map/ppermute | solution.py:33
  106.8 10.4 %collective-permute-start.27 = (bf16[128,512]{1,0:T(8,128)(2,1)S(1)}, bf16[128,512]{1,0:T(8,128)(2,1)S(1)}, u32[]{:S(2)}, u32[]{:S(2)}) collective-permute-start(bf16[128,512]{1,0:T(8,128)(2,1)S(1)} %add_convert_fusion.8), channel_id=1, source_target_pairs={{0,8},{1,9},{2,10},{3,11},{4,12},{5,13},{6,14},{7,15},{8,0},{9,1},... | collective-permute-start | bytes 393224 | tf_op jit(solution)/shard_map/ppermute | solution.py:29
  107.3 9.8 %collective-permute-start.38 = (bf16[128,512]{1,0:T(8,128)(2,1)S(1)}, bf16[128,512]{1,0:T(8,128)(2,1)S(1)}, u32[]{:S(2)}, u32[]{:S(2)}) collective-permute-start(bf16[128,512]{1,0:T(8,128)(2,1)S(1)} %add_convert_fusion.2.refs_4_), channel_id=1, source_target_pairs={{0,2},{1,3},{2,0},{3,1},{4,6},{5,7},{6,4},{7,5},{8,10},{9,11},{10,... | collective-permute-start | bytes 393224 | tf_op jit(solution)/shard_map/ppermute | solution.py:33
  108.6 10.8 %collective-permute-start.25 = (bf16[128,512]{1,0:T(8,128)(2,1)S(1)}, bf16[128,512]{1,0:T(8,128)(2,1)S(1)}, u32[]{:S(2)}, u32[]{:S(2)}) collective-permute-start(bf16[128,512]{1,0:T(8,128)(2,1)S(1)} %add_convert_fusion.9), channel_id=1, source_target_pairs={{0,12},{1,13},{2,14},{3,15},{4,0},{5,1},{6,2},{7,3},{8,4},{9,5},{1... | collective-permute-start | bytes 393224 | tf_op jit(solution)/shard_map/ppermute | solution.py:29
  111.2 16.1 %collective-permute-start.48 = (bf16[512,512]{1,0:T(8,128)(2,1)S(1)}, bf16[512,512]{1,0:T(8,128)(2,1)S(1)}, u32[]{:S(2)}, u32[]{:S(2)}) collective-permute-start(bf16[512,512]{1,0:T(8,128)(2,1)S(1)} %get-tuple-element.90), channel_id=1, source_target_pairs={{0,1},{1,0},{2,3},{3,2},{4,5},{5,4},{6,7},{7,6},{8,9},{9,8},{10,11... | collective-permute-start | bytes 1572872 | tf_op jit(solution)/shard_map/ppermute | solution.py:33
  127.3 9.9 %collective-permute-start.45 = (bf16[128,512]{1,0:T(8,128)(2,1)S(1)}, bf16[128,512]{1,0:T(8,128)(2,1)S(1)}, u32[]{:S(2)}, u32[]{:S(2)}) collective-permute-start(bf16[128,512]{1,0:T(8,128)(2,1)S(1)} %get-tuple-element.79), channel_id=1, source_target_pairs={{0,8},{1,9},{2,10},{3,11},{4,12},{5,13},{6,14},{7,15},{8,0},{9,1},... | collective-permute-start | bytes 393224 | tf_op jit(solution)/shard_map/ppermute | solution.py:29
  (32 other events, 192.5 us)

commit v3 on v2

--- a/solution.py
+++ b/solution.py
@@ -149,9 +149,8 @@
         out_in[...] = dot(rows, back_pre).astype(out_in.dtype)
 
 
-def tail_body(n_line, place, *refs):
-    pieces, deltas, down = refs[:4], refs[4:8], refs[8]
-    blocks, grads = refs[9 : 9 + n_line], refs[9 + n_line :]
+def down_grad_body(n_line, place, *refs):
+    pieces, deltas, blocks = refs[:4], refs[4:8], refs[8:]
     tokens = jnp.concatenate([p[...] for p in pieces], axis=0)
     delta = jnp.concatenate([d[...] for d in deltas], axis=0)
     part = lax.dot_general(tokens, delta, contract_first, preferred_element_type=wide)
@@ -163,9 +162,12 @@
             def _(z=z, back=back):
                 blocks[back][...] = part[z * block : (z + 1) * block].astype(blocks[back].dtype)
 
-    for i in range(4):
-        grads[i][...] = lax.dot_general(
-            deltas[i][...], down[...], contract_last, preferred_element_type=wide
+
+def token_grad_body(place, *refs):
+    deltas, down, grads = refs[:4], refs[4], refs[5:]
+    for delta, grad in zip(deltas, grads):
+        grad[...] = lax.dot_general(
+            delta[...], down[...], contract_last, preferred_element_type=wide
         ).astype(narrow)
 
 
@@ -205,10 +207,9 @@
         nbytes=3 * tok_rows * width * 2,
     )
     *columns, payload = prepare(place, tokens, routes.T, gate_levels.T, latent_grad)
-    near_tokens = [
-        columns[core * 2 + side] if core + side == 0 else swap(columns[core * 2 + side], n_line, core, side)
-        for core in range(2)
-        for side in range(2)
+    near_tokens = columns[:1] + [
+        swap(after(columns[core * 2 + side], downs[1]), n_line, core, side)
+        for core, side in ((0, 1), (1, 0), (1, 1))
     ]
     own = (expert_in[0], expert_out[0])
     weights = own + tuple(swap(w, n_line, 1, 0) for w in own)
@@ -223,11 +224,13 @@
     half = keep + swap(send, n_line, 1, 0)
     latent = (half[0] + swap(half[1], n_line, 0, 1)).astype(narrow)
 
-    payload = after(payload, downs[-1])
-    payloads = [payload] + [turn(payload, n_line, back) for back in range(1, n_line)]
-    far_payloads = [swap(p, n_line, 0, 1) for p in payloads]
+    later_payload = after(payload, half)
+    payloads = [payload] + [turn(later_payload, n_line, back) for back in range(1, n_line)]
     rows = [latent] + [turn(latent, n_line, back) for back in range(1, n_line)]
     far_rows = [swap(r, n_line, 0, 1) for r in rows]
+    far_payloads = [swap(after(payload, near_tokens[1]), n_line, 0, 1)] + [
+        swap(after(p, latent), n_line, 0, 1) for p in payloads[1:]
+    ]
 
     def experts(count, kind, name):
         saved = shape((2, count * tok_rows, hidden_width), narrow)
@@ -240,48 +243,64 @@
         )
 
     outs = experts(n_line, wide, "near_experts")(place, *rows, *payloads, *weights)
-    near_out, near_delta, near_saved = outs[:n_line], outs[n_line : 2 * n_line], outs[2 * n_line :]
-    outs = experts(n_line, narrow, "far_experts")(place, *far_rows, *far_payloads, *weights)
-    far_out, far_delta, far_saved = outs[:n_line], outs[n_line : 2 * n_line], outs[2 * n_line :]
-
-    def return_sums(near, far):
-        total = None
-        for back in [*range(1, n_line), 0]:
-            line = near[back] + swap(far[back], n_line, 0, 1).astype(wide)
+    near_out, near_delta, saved = outs[:n_line], outs[n_line : 2 * n_line], [outs[2 * n_line :]]
+    far_out, far_delta = [], []
+    part = n_line // 2
+    for first in range(0, n_line, part):
+        span = slice(first, first + part)
+        outs = experts(part, narrow, "far_experts")(place, *far_rows[span], *far_payloads[span], *weights)
+        far_out += outs[:part]
+        far_delta += outs[part : 2 * part]
+        saved.append(outs[2 * part :])
+
+    def return_lines(near, far):
+        lines = []
+        for back in range(n_line):
+            line = near[back] + far[back].astype(wide)
             if back:
-                line = turn(line.astype(narrow), n_line, n_line - back).astype(wide)
-            total = line if total is None else total + line
-        return total.astype(narrow)
-
-    delta = return_sums(near_delta, far_delta)
-    latent_out = return_sums(near_out, far_out)
+                line = turn(line.astype(narrow), n_line, n_line - back)
+            lines.append(line)
+        return lines
+
+    far_delta = [swap(d, n_line, 0, 1) for d in far_delta]
+    delta = sum(line.astype(wide) for line in return_lines(near_delta, far_delta)).astype(narrow)
+    far_out = [swap(after(o, far_delta[-1]), n_line, 0, 1) for o in far_out]
+    out_lines = return_lines(near_out, far_out)
 
     weight_grad = call(
-        functools.partial(weight_grad_body, 2 * n_line, 2),
+        functools.partial(weight_grad_body, 2 * n_line, len(saved)),
         [shape((latent_width, hidden_width), wide), shape((hidden_width, latent_width), wide)]
         + [shape((latent_width, hidden_width), narrow), shape((hidden_width, latent_width), narrow)],
         "weight_grads",
         flops=2 * 2 * 2 * 2 * n_line * tok_rows * latent_width * hidden_width,
     )
-    keep_in, keep_out, send_in, send_out = weight_grad(place, *rows, *far_rows, *near_saved, *far_saved)
+    keep_in, keep_out, send_in, send_out = weight_grad(
+        place, *rows, *far_rows, *(value for values in saved for value in values)
+    )
     grad_in = (keep_in + swap(send_in, n_line, 1, 0).astype(wide)).astype(narrow)
     grad_out = (keep_out + swap(send_out, n_line, 1, 0).astype(wide)).astype(narrow)
 
     side_delta = swap(delta, n_line, 0, 1)
     deltas = [delta, side_delta, swap(delta, n_line, 1, 0), swap(side_delta, n_line, 1, 0)]
-    tail = call(
-        functools.partial(tail_body, n_line),
-        [shape((block, latent_width), wide)]
-        + [shape((block, latent_width), narrow)] * (n_line - 1)
-        + [shape((tok_rows, n_line * block), narrow)] * 4,
-        "tail",
-        flops=2 * 2 * 4 * tok_rows * n_line * block * latent_width,
-    )
-    outs = tail(place, *near_tokens, *deltas, down)
-    blocks, grads = outs[:n_line], outs[n_line:]
-    grad_down = blocks[0]
-    for back in range(1, n_line):
-        grad_down = grad_down + turn(blocks[back], n_line, n_line - back).astype(wide)
+    narrow_columns = shape((tok_rows, n_line * block), narrow)
+    down_grad = call(
+        functools.partial(down_grad_body, n_line),
+        [shape((block, latent_width), wide)] + [shape((block, latent_width), narrow)] * (n_line - 1),
+        "down_grad",
+        flops=2 * 4 * tok_rows * n_line * block * latent_width,
+    )
+    blocks = down_grad(place, *near_tokens, *deltas)
+    token_grad = call(
+        token_grad_body,
+        [narrow_columns] * 4,
+        "token_grad",
+        flops=2 * 4 * tok_rows * n_line * block * latent_width,
+    )
+    grads = token_grad(place, *deltas, down)
+    blocks = [blocks[0]] + [turn(blocks[back], n_line, n_line - back) for back in range(1, n_line)]
+    grad_down = sum(value.astype(wide) for value in blocks)
+    out_lines = [after(line, blocks[1]) for line in out_lines]
+    latent_out = sum(line.astype(wide) for line in out_lines).astype(narrow)
     grads = [
         grads[core * 2 + side] if core + side == 0 else swap(grads[core * 2 + side], n_line, core, side)
         for core in range(2)

time: 139 us -> 138 us (level)
  waiting for transfers between devices: 57.8 us -> 51 us
  starting transfers between devices: 58 us -> 61.5 us
    ppermute x18, waiting for transfers between devices: 32.5 us -> 24.4 us  [turn(): lax.ppermute(value, plane, device_pairs(n_line, lambda z, x, c: ((z + by)...]
    ppermute x18, starting transfers between devices: 31.4 us -> 35.4 us  [turn(): lax.ppermute(value, plane, device_pairs(n_line, lambda z, x, c: ((z + by)...]
    pallas_call x7 -> x9, Pallas kernels: 15 us -> 16.2 us  [run(): pl.pallas_call(body, out_shape=outs, in_specs=[pl.BlockSpec(memory_space=...]
  transfers between devices with their start and end apart: 49 -> 49, of which waited for: 25 -> 21; matrix products, arithmetic and copies ran while one was open for 2% -> 3% of each run, Pallas kernels for 7% -> 10%
where the time goes in v3:
time: 138 us; the launch traced here: 136 us
  starting transfers between devices  61.5 us (45%)
  waiting for transfers between devices  51 us (37%)
  Pallas kernels  16.2 us (12%)
  other arithmetic  3.79 us (3%)
  local copies, waits for them, and re-layouts  2.68 us (2%)
    ppermute x18, starting transfers between devices, turn(): lax.ppermute(value, plane, device_pairs(n_line, lambda z, x, c: ((z + by)...  35.4 us
    ppermute x31, waiting for transfers between devices, swap(): lax.ppermute(value, plane, device_pairs(n_line, lambda z, x, c: (z, x ^ s...  26.5 us
    ppermute x31, starting transfers between devices, swap(): lax.ppermute(value, plane, device_pairs(n_line, lambda z, x, c: (z, x ^ s...  26.1 us
    ppermute x18, waiting for transfers between devices, turn(): lax.ppermute(value, plane, device_pairs(n_line, lambda z, x, c: ((z + by)...  24.4 us
    pallas_call x9, Pallas kernels, run(): pl.pallas_call(body, out_shape=outs, in_specs=[pl.BlockSpec(memory_space=...  16.2 us
  transfers between devices with their start and end apart: 49, of which 21 were waited for; matrix products, arithmetic and copies ran while one was open for 3% of the time, Pallas kernels for 10%

profile of v3, /device:TPU:0, one launch (start us, length us, event | category | flops | bytes accessed | tf_op | source)
XLA Modules:
  0.0 136.0 jit_solution(6426941994970368138)
XLA Ops:
  0.6 3.1 %collective-permute-start = (bf16[128,512]{1,0:T(8,128)(2,1)}, bf16[128,512]{1,0:T(8,128)(2,1)S(1)}, u32[]{:S(2)}, u32[]{:S(2)}) collective-permute-start(bf16[128,512]{1,0:T(8,128)(2,1)} %refs_4_.1), channel_id=1, source_target_pairs={{0,4},{1,5},{2,6},{3,7},{4,8},{5,9},{6,10},{7,11},{8,12},{9,13},{1... | collective-permute-start | bytes 393224 | tf_op jit(solution)/shard_map/ppermute | solution.py:29
  3.7 2.6 %collective-permute-start.4 = (bf16[128,512]{1,0:T(8,128)(2,1)}, bf16[128,512]{1,0:T(8,128)(2,1)S(1)}, u32[]{:S(2)}, u32[]{:S(2)}) collective-permute-start(bf16[128,512]{1,0:T(8,128)(2,1)} %refs_4_.1), channel_id=1, source_target_pairs={{0,8},{1,9},{2,10},{3,11},{4,12},{5,13},{6,14},{7,15},{8,0},{9,1},... | collective-permute-start | bytes 393224 | tf_op jit(solution)/shard_map/ppermute | solution.py:29
  13.2 1.9 %collective-permute-done.4.refs_6_ = bf16[128,512]{1,0:T(8,128)(2,1)S(1)} collective-permute-done((bf16[128,512]{1,0:T(8,128)(2,1)}, bf16[128,512]{1,0:T(8,128)(2,1)S(1)}, u32[]{:S(2)}, u32[]{:S(2)}) %collective-permute-start.4) | collective-permute-done | bytes 131104 | tf_op jit(solution)/shard_map/ppermute | solution.py:29
  16.5 1.8 %collective-permute-done.3.refs_3_ = bf16[128,512]{1,0:T(8,128)(2,1)S(1)} collective-permute-done((bf16[128,512]{1,0:T(8,128)(2,1)S(1)}, bf16[128,512]{1,0:T(8,128)(2,1)S(1)}, u32[]{:S(2)}, u32[]{:S(2)}) %collective-permute-start.3) | collective-permute-done | bytes 131104 | tf_op jit(solution)/shard_map/ppermute | solution.py:33
  19.8 1.6 %collective-permute-done.6 = f32[2,128,512]{2,1,0:T(8,128)S(1)} collective-permute-done((f32[2,128,512]{2,1,0:T(8,128)S(1)}, f32[2,128,512]{2,1,0:T(8,128)S(1)}, u32[]{:S(2)}, u32[]{:S(2)}) %collective-permute-start.6) | collective-permute-done | bytes 524320 | tf_op jit(solution)/shard_map/ppermute | solution.py:33
  23.5 4.1 %collective-permute-start.11 = (bf16[144,512]{1,0:T(8,128)(2,1)S(1)}, bf16[144,512]{1,0:T(8,128)(2,1)S(1)}, u32[]{:S(2)}, u32[]{:S(2)}) collective-permute-start(bf16[144,512]{1,0:T(8,128)(2,1)S(1)} %get-tuple-element.78.refs_4_), channel_id=1, source_target_pairs={{0,4},{1,5},{2,6},{3,7},{4,8},{5,9},{6,10},{7,11},{8,12},{9,13},{1... | collective-permute-start | bytes 442376 | tf_op jit(solution)/shard_map/ppermute | solution.py:29
  27.5 1.8 %collective-permute-start.12 = (bf16[144,512]{1,0:T(8,128)(2,1)S(1)}, bf16[144,512]{1,0:T(8,128)(2,1)S(1)}, u32[]{:S(2)}, u32[]{:S(2)}) collective-permute-start(bf16[144,512]{1,0:T(8,128)(2,1)S(1)} %get-tuple-element.78.refs_4_), channel_id=1, source_target_pairs={{0,8},{1,9},{2,10},{3,11},{4,12},{5,13},{6,14},{7,15},{8,0},{9,1},... | collective-permute-start | bytes 442376 | tf_op jit(solution)/shard_map/ppermute | solution.py:29
  30.1 2.2 %collective-permute-start.13 = (bf16[144,512]{1,0:T(8,128)(2,1)S(1)}, bf16[144,512]{1,0:T(8,128)(2,1)S(1)}, u32[]{:S(2)}, u32[]{:S(2)}) collective-permute-start(bf16[144,512]{1,0:T(8,128)(2,1)S(1)} %get-tuple-element.78.refs_4_), channel_id=1, source_target_pairs={{0,12},{1,13},{2,14},{3,15},{4,0},{5,1},{6,2},{7,3},{8,4},{9,5},{1... | collective-permute-start | bytes 442376 | tf_op jit(solution)/shard_map/ppermute | solution.py:29
  32.3 6.0 %collective-permute-done.12.refs_6_ = bf16[144,512]{1,0:T(8,128)(2,1)S(1)} collective-permute-done((bf16[144,512]{1,0:T(8,128)(2,1)S(1)}, bf16[144,512]{1,0:T(8,128)(2,1)S(1)}, u32[]{:S(2)}, u32[]{:S(2)}) %collective-permute-start.12) | collective-permute-done | bytes 147488 | tf_op jit(solution)/shard_map/ppermute | solution.py:29
  39.2 9.2 %collective-permute-start.10 = (bf16[128,512]{1,0:T(8,128)(2,1)S(1)}, bf16[128,512]{1,0:T(8,128)(2,1)S(1)}, u32[]{:S(2)}, u32[]{:S(2)}) collective-permute-start(bf16[128,512]{1,0:T(8,128)(2,1)S(1)} %fusion.3.refs_0_), channel_id=1, source_target_pairs={{0,12},{1,13},{2,14},{3,15},{4,0},{5,1},{6,2},{7,3},{8,4},{9,5},{1... | collective-permute-start | bytes 393224 | tf_op jit(solution)/shard_map/ppermute | solution.py:29
  53.3 3.9 %collective-permute-done.8.refs_1_ = bf16[128,512]{1,0:T(8,128)(2,1)S(1)} collective-permute-done((bf16[128,512]{1,0:T(8,128)(2,1)S(1)}, bf16[128,512]{1,0:T(8,128)(2,1)S(1)}, u32[]{:S(2)}, u32[]{:S(2)}) %collective-permute-start.8) | collective-permute-done | bytes 131104 | tf_op jit(solution)/shard_map/ppermute | solution.py:29
  63.9 2.1 %far_experts.3 = (bf16[128,512]{1,0:T(8,128)(2,1)S(1)}, bf16[128,512]{1,0:T(8,128)(2,1)S(1)}, bf16[128,512]{1,0:T(8,128)(2,1)S(1)}, bf16[128,512]{1,0:T(8,128)(2...) custom-call(s32[5]{0:T(128)S(1)} %stack.23.place, ...), custom_call_target="tpu_custom_call" | custom-call | flops 1073741824 | bytes 2097152 | tf_op jit(solution)/shard_map/far_experts/pallas_call | solution.py:44
  67.3 3.4 %near_experts.1 = (f32[128,512]{1,0:T(8,128)S(1)}, f32[128,512]{1,0:T(8,128)S(1)}, f32[128,512]{1,0:T(8,128)S(1)}, f32[128,512]{1,0:T(8,128)S(1)}, f32[128,512]{...) custom-call(s32[5]{0:T(128)S(1)} %stack.23.place, ...), custom_call_target="tpu_custom_call" | custom-call | flops 2147483648 | bytes 2097152 | tf_op jit(solution)/shard_map/near_experts/pallas_call | solution.py:44
  73.1 2.8 %collective-permute-done.17.refs_1_.refs_5_ = bf16[128,512]{1,0:T(8,128)(2,1)S(1)} collective-permute-done((bf16[128,512]{1,0:T(8,128)(2,1)S(1)}, bf16[128,512]{1,0:T(8,128)(2,1)S(1)}, u32[]{:S(2)}, u32[]{:S(2)}) %collective-permute-start.17) | collective-permute-done | bytes 131104 | tf_op jit(solution)/shard_map/ppermute | solution.py:33
  75.9 2.1 %far_experts.2 = (bf16[128,512]{1,0:T(8,128)(2,1)S(1)}, bf16[128,512]{1,0:T(8,128)(2,1)S(1)}, bf16[128,512]{1,0:T(8,128)(2,1)S(1)}, bf16[128,512]{1,0:T(8,128)(2...) custom-call(s32[5]{0:T(128)S(1)} %stack.23.place, ...), custom_call_target="tpu_custom_call" | custom-call | flops 1073741824 | bytes 2097152 | tf_op jit(solution)/shard_map/far_experts/pallas_call | solution.py:44
  81.5 2.1 %collective-permute-start.30 = (bf16[128,512]{1,0:T(8,128)(2,1)S(1)}, bf16[128,512]{1,0:T(8,128)(2,1)S(1)}, u32[]{:S(2)}, u32[]{:S(2)}) collective-permute-start(bf16[128,512]{1,0:T(8,128)(2,1)S(1)} %add_convert_fusion.8), channel_id=1, source_target_pairs={{0,8},{1,9},{2,10},{3,11},{4,12},{5,13},{6,14},{7,15},{8,0},{9,1},... | collective-permute-start | bytes 393224 | tf_op jit(solution)/shard_map/ppermute | solution.py:29
  83.7 2.4 %collective-permute-start.28 = (bf16[128,512]{1,0:T(8,128)(2,1)S(1)}, bf16[128,512]{1,0:T(8,128)(2,1)S(1)}, u32[]{:S(2)}, u32[]{:S(2)}) collective-permute-start(bf16[128,512]{1,0:T(8,128)(2,1)S(1)} %add_convert_fusion.9), channel_id=1, source_target_pairs={{0,12},{1,13},{2,14},{3,15},{4,0},{5,1},{6,2},{7,3},{8,4},{9,5},{1... | collective-permute-start | bytes 393224 | tf_op jit(solution)/shard_map/ppermute | solution.py:29
  86.0 2.9 %weight_grads.1 = (f32[512,512]{1,0:T(8,128)S(1)}, f32[512,512]{1,0:T(8,128)S(1)}, bf16[512,512]{1,0:T(8,128)(2,1)S(1)}, bf16[512,512]{1,0:T(8,128)(2,1)S(1)}) custom-call(s32[5]{0:T(128)S(1)} %stack.23.place, bf16[128,512]{1,0:T(8,128)(2,1)S(1)} %fusion.3.refs_0_, bf16[128,512]{1,0:T(8,128)(2,1)S(1)} %collective-permute-done.8.refs_1_, ...), custom_call_target="tpu_custom_call" | custom-call | flops 2147483648 | tf_op jit(solution)/shard_map/weight_grads/pallas_call | solution.py:44
  89.5 1.6 %collective-permute-start.40 = (bf16[128,512]{1,0:T(8,128)(2,1)S(1)}, bf16[128,512]{1,0:T(8,128)(2,1)S(1)}, u32[]{:S(2)}, u32[]{:S(2)}) collective-permute-start(bf16[128,512]{1,0:T(8,128)(2,1)S(1)} %get-tuple-element.104), channel_id=1, source_target_pairs={{0,2},{1,3},{2,0},{3,1},{4,6},{5,7},{6,4},{7,5},{8,10},{9,11},{10,... | collective-permute-start | bytes 393224 | tf_op jit(solution)/shard_map/ppermute | solution.py:33
  93.2 7.4 %collective-permute-done.25 = bf16[128,512]{1,0:T(8,128)(2,1)S(1)} collective-permute-done((bf16[128,512]{1,0:T(8,128)(2,1)S(1)}, bf16[128,512]{1,0:T(8,128)(2,1)S(1)}, u32[]{:S(2)}, u32[]{:S(2)}) %collective-permute-start.25) | collective-permute-done | bytes 131104 | tf_op jit(solution)/shard_map/ppermute | solution.py:33
  102.9 3.8 %collective-permute-done.36 = bf16[128,512]{1,0:T(8,128)(2,1)S(1)} collective-permute-done((bf16[128,512]{1,0:T(8,128)(2,1)S(1)}, bf16[128,512]{1,0:T(8,128)(2,1)S(1)}, u32[]{:S(2)}, u32[]{:S(2)}) %collective-permute-start.36) | collective-permute-done | bytes 131104 | tf_op jit(solution)/shard_map/ppermute | solution.py:33
  109.4 2.4 %collective-permute-start.37 = (bf16[128,512]{1,0:T(8,128)(2,1)S(1)}, bf16[128,512]{1,0:T(8,128)(2,1)S(1)}, u32[]{:S(2)}, u32[]{:S(2)}) collective-permute-start(bf16[128,512]{1,0:T(8,128)(2,1)S(1)} %add_convert_fusion.5), channel_id=1, source_target_pairs={{0,12},{1,13},{2,14},{3,15},{4,0},{5,1},{6,2},{7,3},{8,4},{9,5},{1... | collective-permute-start | bytes 393224 | tf_op jit(solution)/shard_map/ppermute | solution.py:29
  119.2 4.2 %collective-permute-done.35 = bf16[128,512]{1,0:T(8,128)(2,1)S(1)} collective-permute-done((bf16[128,512]{1,0:T(8,128)(2,1)S(1)}, bf16[128,512]{1,0:T(8,128)(2,1)S(1)}, u32[]{:S(2)}, u32[]{:S(2)}) %collective-permute-start.35) | collective-permute-done | bytes 131104 | tf_op jit(solution)/shard_map/ppermute | solution.py:29
  126.2 6.9 %collective-permute-done.45 = bf16[128,512]{1,0:T(8,128)(2,1)S(1)} collective-permute-done((bf16[128,512]{1,0:T(8,128)(2,1)S(1)}, bf16[128,512]{1,0:T(8,128)(2,1)S(1)}, u32[]{:S(2)}, u32[]{:S(2)}) %collective-permute-start.45) | collective-permute-done | bytes 131104 | tf_op jit(solution)/shard_map/ppermute | solution.py:29
  (113 shorter events, 53.0 us)
Async XLA Ops:
  0.6 10.4 %collective-permute-start = (bf16[128,512]{1,0:T(8,128)(2,1)}, bf16[128,512]{1,0:T(8,128)(2,1)S(1)}, u32[]{:S(2)}, u32[]{:S(2)}) collective-permute-start(bf16[128,512]{1,0:T(8,128)(2,1)} %refs_4_.1), channel_id=1, source_target_pairs={{0,4},{1,5},{2,6},{3,7},{4,8},{5,9},{6,10},{7,11},{8,12},{9,13},{1... | collective-permute-start | bytes 393224 | tf_op jit(solution)/shard_map/ppermute | solution.py:29
  3.7 11.4 %collective-permute-start.4 = (bf16[128,512]{1,0:T(8,128)(2,1)}, bf16[128,512]{1,0:T(8,128)(2,1)S(1)}, u32[]{:S(2)}, u32[]{:S(2)}) collective-permute-start(bf16[128,512]{1,0:T(8,128)(2,1)} %refs_4_.1), channel_id=1, source_target_pairs={{0,8},{1,9},{2,10},{3,11},{4,12},{5,13},{6,14},{7,15},{8,0},{9,1},... | collective-permute-start | bytes 393224 | tf_op jit(solution)/shard_map/ppermute | solution.py:29
  23.0 25.4 %collective-permute-start.14 = (bf16[512,512]{1,0:T(8,128)(2,1)S(1)}, bf16[512,512]{1,0:T(8,128)(2,1)S(1)}, u32[]{:S(2)}, u32[]{:S(2)}) collective-permute-start(bf16[512,512]{1,0:T(8,128)(2,1)S(1)} %bitcast.23), channel_id=1, source_target_pairs={{0,1},{1,0},{2,3},{3,2},{4,5},{5,4},{6,7},{7,6},{8,9},{9,8},{10,11... | collective-permute-start | bytes 1572872 | tf_op jit(solution)/shard_map/ppermute | solution.py:33
  23.0 26.6 %collective-permute-start.15 = (bf16[512,512]{1,0:T(8,128)(2,1)S(1)}, bf16[512,512]{1,0:T(8,128)(2,1)S(1)}, u32[]{:S(2)}, u32[]{:S(2)}) collective-permute-start(bf16[512,512]{1,0:T(8,128)(2,1)S(1)} %bitcast.27), channel_id=1, source_target_pairs={{0,1},{1,0},{2,3},{3,2},{4,5},{5,4},{6,7},{7,6},{8,9},{9,8},{10,11... | collective-permute-start | bytes 1572872 | tf_op jit(solution)/shard_map/ppermute | solution.py:33
  23.5 26.9 %collective-permute-start.11 = (bf16[144,512]{1,0:T(8,128)(2,1)S(1)}, bf16[144,512]{1,0:T(8,128)(2,1)S(1)}, u32[]{:S(2)}, u32[]{:S(2)}) collective-permute-start(bf16[144,512]{1,0:T(8,128)(2,1)S(1)} %get-tuple-element.78.refs_4_), channel_id=1, source_target_pairs={{0,4},{1,5},{2,6},{3,7},{4,8},{5,9},{6,10},{7,11},{8,12},{9,13},{1... | collective-permute-start | bytes 442376 | tf_op jit(solution)/shard_map/ppermute | solution.py:29
  27.5 10.8 %collective-permute-start.12 = (bf16[144,512]{1,0:T(8,128)(2,1)S(1)}, bf16[144,512]{1,0:T(8,128)(2,1)S(1)}, u32[]{:S(2)}, u32[]{:S(2)}) collective-permute-start(bf16[144,512]{1,0:T(8,128)(2,1)S(1)} %get-tuple-element.78.refs_4_), channel_id=1, source_target_pairs={{0,8},{1,9},{2,10},{3,11},{4,12},{5,13},{6,14},{7,15},{8,0},{9,1},... | collective-permute-start | bytes 442376 | tf_op jit(solution)/shard_map/ppermute | solution.py:29
  38.3 12.7 %collective-permute-start.9 = (bf16[128,512]{1,0:T(8,128)(2,1)S(1)}, bf16[128,512]{1,0:T(8,128)(2,1)S(1)}, u32[]{:S(2)}, u32[]{:S(2)}) collective-permute-start(bf16[128,512]{1,0:T(8,128)(2,1)S(1)} %fusion.3.refs_0_), channel_id=1, source_target_pairs={{0,8},{1,9},{2,10},{3,11},{4,12},{5,13},{6,14},{7,15},{8,0},{9,1},... | collective-permute-start | bytes 393224 | tf_op jit(solution)/shard_map/ppermute | solution.py:29
  39.2 13.1 %collective-permute-start.10 = (bf16[128,512]{1,0:T(8,128)(2,1)S(1)}, bf16[128,512]{1,0:T(8,128)(2,1)S(1)}, u32[]{:S(2)}, u32[]{:S(2)}) collective-permute-start(bf16[128,512]{1,0:T(8,128)(2,1)S(1)} %fusion.3.refs_0_), channel_id=1, source_target_pairs={{0,12},{1,13},{2,14},{3,15},{4,0},{5,1},{6,2},{7,3},{8,4},{9,5},{1... | collective-permute-start | bytes 393224 | tf_op jit(solution)/shard_map/ppermute | solution.py:29
  52.3 11.6 %collective-permute-start.21 = (bf16[128,512]{1,0:T(8,128)(2,1)S(1)}, bf16[128,512]{1,0:T(8,128)(2,1)S(1)}, u32[]{:S(2)}, u32[]{:S(2)}) collective-permute-start(bf16[128,512]{1,0:T(8,128)(2,1)S(1)} %collective-permute-done.10.refs_3_), channel_id=1, source_target_pairs={{0,2},{1,3},{2,0},{3,1},{4,6},{5,7},{6,4},{7,5},{8,10},{9,11},{10,... | collective-permute-start | bytes 393224 | tf_op jit(solution)/shard_map/ppermute | solution.py:33
  57.2 13.6 %collective-permute-start.18 = (bf16[144,512]{1,0:T(8,128)(2,1)S(1)}, bf16[144,512]{1,0:T(8,128)(2,1)S(1)}, u32[]{:S(2)}, u32[]{:S(2)}) collective-permute-start(bf16[144,512]{1,0:T(8,128)(2,1)S(1)} %get-tuple-element.78.refs_4_), channel_id=1, source_target_pairs={{0,2},{1,3},{2,0},{3,1},{4,6},{5,7},{6,4},{7,5},{8,10},{9,11},{10,... | collective-permute-start | bytes 442376 | tf_op jit(solution)/shard_map/ppermute | solution.py:33
  58.5 13.2 %collective-permute-start.16 = (bf16[128,512]{1,0:T(8,128)(2,1)S(1)}, bf16[128,512]{1,0:T(8,128)(2,1)S(1)}, u32[]{:S(2)}, u32[]{:S(2)}) collective-permute-start(bf16[128,512]{1,0:T(8,128)(2,1)S(1)} %fusion.3.refs_0_), channel_id=1, source_target_pairs={{0,2},{1,3},{2,0},{3,1},{4,6},{5,7},{6,4},{7,5},{8,10},{9,11},{10,... | collective-permute-start | bytes 393224 | tf_op jit(solution)/shard_map/ppermute | solution.py:33
  59.2 13.9 %collective-permute-start.19 = (bf16[144,512]{1,0:T(8,128)(2,1)S(1)}, bf16[144,512]{1,0:T(8,128)(2,1)S(1)}, u32[]{:S(2)}, u32[]{:S(2)}) collective-permute-start(bf16[144,512]{1,0:T(8,128)(2,1)S(1)} %collective-permute-done.11.refs_5_), channel_id=1, source_target_pairs={{0,2},{1,3},{2,0},{3,1},{4,6},{5,7},{6,4},{7,5},{8,10},{9,11},{10,... | collective-permute-start | bytes 442376 | tf_op jit(solution)/shard_map/ppermute | solution.py:33
  61.1 14.7 %collective-permute-start.17 = (bf16[128,512]{1,0:T(8,128)(2,1)S(1)}, bf16[128,512]{1,0:T(8,128)(2,1)S(1)}, u32[]{:S(2)}, u32[]{:S(2)}) collective-permute-start(bf16[128,512]{1,0:T(8,128)(2,1)S(1)} %collective-permute-done.8.refs_1_), channel_id=1, source_target_pairs={{0,2},{1,3},{2,0},{3,1},{4,6},{5,7},{6,4},{7,5},{8,10},{9,11},{10,... | collective-permute-start | bytes 393224 | tf_op jit(solution)/shard_map/ppermute | solution.py:33
  66.0 14.0 %collective-permute-start.24 = (bf16[128,512]{1,0:T(8,128)(2,1)S(1)}, bf16[128,512]{1,0:T(8,128)(2,1)S(1)}, u32[]{:S(2)}, u32[]{:S(2)}) collective-permute-start(bf16[128,512]{1,0:T(8,128)(2,1)S(1)} %get-tuple-element.83), channel_id=1, source_target_pairs={{0,2},{1,3},{2,0},{3,1},{4,6},{5,7},{6,4},{7,5},{8,10},{9,11},{10,... | collective-permute-start | bytes 393224 | tf_op jit(solution)/shard_map/ppermute | solution.py:33
  70.8 10.7 %collective-permute-start.29 = (bf16[128,512]{1,0:T(8,128)(2,1)S(1)}, bf16[128,512]{1,0:T(8,128)(2,1)S(1)}, u32[]{:S(2)}, u32[]{:S(2)}) collective-permute-start(bf16[128,512]{1,0:T(8,128)(2,1)S(1)} %get-tuple-element.90), channel_id=1, source_target_pairs={{0,2},{1,3},{2,0},{3,1},{4,6},{5,7},{6,4},{7,5},{8,10},{9,11},{10,... | collective-permute-start | bytes 393224 | tf_op jit(solution)/shard_map/ppermute | solution.py:33
  88.9 24.1 %collective-permute-start.47 = (bf16[512,512]{1,0:T(8,128)(2,1)S(1)}, bf16[512,512]{1,0:T(8,128)(2,1)S(1)}, u32[]{:S(2)}, u32[]{:S(2)}) collective-permute-start(bf16[512,512]{1,0:T(8,128)(2,1)S(1)} %get-tuple-element.124), channel_id=1, source_target_pairs={{0,1},{1,0},{2,3},{3,2},{4,5},{5,4},{6,7},{7,6},{8,9},{9,8},{10,11... | collective-permute-start | bytes 1572872 | tf_op jit(solution)/shard_map/ppermute | solution.py:33
  89.0 27.1 %collective-permute-start.48 = (bf16[512,512]{1,0:T(8,128)(2,1)S(1)}, bf16[512,512]{1,0:T(8,128)(2,1)S(1)}, u32[]{:S(2)}, u32[]{:S(2)}) collective-permute-start(bf16[512,512]{1,0:T(8,128)(2,1)S(1)} %get-tuple-element.126), channel_id=1, source_target_pairs={{0,1},{1,0},{2,3},{3,2},{4,5},{5,4},{6,7},{7,6},{8,9},{9,8},{10,11... | collective-permute-start | bytes 1572872 | tf_op jit(solution)/shard_map/ppermute | solution.py:33
  89.5 12.7 %collective-permute-start.40 = (bf16[128,512]{1,0:T(8,128)(2,1)S(1)}, bf16[128,512]{1,0:T(8,128)(2,1)S(1)}, u32[]{:S(2)}, u32[]{:S(2)}) collective-permute-start(bf16[128,512]{1,0:T(8,128)(2,1)S(1)} %get-tuple-element.104), channel_id=1, source_target_pairs={{0,2},{1,3},{2,0},{3,1},{4,6},{5,7},{6,4},{7,5},{8,10},{9,11},{10,... | collective-permute-start | bytes 393224 | tf_op jit(solution)/shard_map/ppermute | solution.py:33
  91.1 11.7 %collective-permute-start.38 = (bf16[128,512]{1,0:T(8,128)(2,1)S(1)}, bf16[128,512]{1,0:T(8,128)(2,1)S(1)}, u32[]{:S(2)}, u32[]{:S(2)}) collective-permute-start(bf16[128,512]{1,0:T(8,128)(2,1)S(1)} %get-tuple-element.100), channel_id=1, source_target_pairs={{0,2},{1,3},{2,0},{3,1},{4,6},{5,7},{6,4},{7,5},{8,10},{9,11},{10,... | collective-permute-start | bytes 393224 | tf_op jit(solution)/shard_map/ppermute | solution.py:33
  108.1 16.8 %collective-permute-start.39 = (bf16[128,512]{1,0:T(8,128)(2,1)S(1)}, bf16[128,512]{1,0:T(8,128)(2,1)S(1)}, u32[]{:S(2)}, u32[]{:S(2)}) collective-permute-start(bf16[128,512]{1,0:T(8,128)(2,1)S(1)} %add_convert_fusion.4), channel_id=1, source_target_pairs={{0,8},{1,9},{2,10},{3,11},{4,12},{5,13},{6,14},{7,15},{8,0},{9,1},... | collective-permute-start | bytes 393224 | tf_op jit(solution)/shard_map/ppermute | solution.py:29
  109.4 15.5 %collective-permute-start.37 = (bf16[128,512]{1,0:T(8,128)(2,1)S(1)}, bf16[128,512]{1,0:T(8,128)(2,1)S(1)}, u32[]{:S(2)}, u32[]{:S(2)}) collective-permute-start(bf16[128,512]{1,0:T(8,128)(2,1)S(1)} %add_convert_fusion.5), channel_id=1, source_target_pairs={{0,12},{1,13},{2,14},{3,15},{4,0},{5,1},{6,2},{7,3},{8,4},{9,5},{1... | collective-permute-start | bytes 393224 | tf_op jit(solution)/shard_map/ppermute | solution.py:29
  114.9 11.3 %collective-permute-start.46 = (bf16[128,512]{1,0:T(8,128)(2,1)S(1)}, bf16[128,512]{1,0:T(8,128)(2,1)S(1)}, u32[]{:S(2)}, u32[]{:S(2)}) collective-permute-start(bf16[128,512]{1,0:T(8,128)(2,1)S(1)} %get-tuple-element.113), channel_id=1, source_target_pairs={{0,4},{1,5},{2,6},{3,7},{4,8},{5,9},{6,10},{7,11},{8,12},{9,13},{1... | collective-permute-start | bytes 393224 | tf_op jit(solution)/shard_map/ppermute | solution.py:29
  116.1 16.9 %collective-permute-start.45 = (bf16[128,512]{1,0:T(8,128)(2,1)S(1)}, bf16[128,512]{1,0:T(8,128)(2,1)S(1)}, u32[]{:S(2)}, u32[]{:S(2)}) collective-permute-start(bf16[128,512]{1,0:T(8,128)(2,1)S(1)} %get-tuple-element.112), channel_id=1, source_target_pairs={{0,8},{1,9},{2,10},{3,11},{4,12},{5,13},{6,14},{7,15},{8,0},{9,1},... | collective-permute-start | bytes 393224 | tf_op jit(solution)/shard_map/ppermute | solution.py:29
  123.4 11.1 %collective-permute-start.42 = (bf16[128,512]{1,0:T(8,128)(2,1)S(1)}, bf16[128,512]{1,0:T(8,128)(2,1)S(1)}, u32[]{:S(2)}, u32[]{:S(2)}) collective-permute-start(bf16[128,512]{1,0:T(8,128)(2,1)S(1)} %get-tuple-element.108), channel_id=1, source_target_pairs={{0,2},{1,3},{2,0},{3,1},{4,6},{5,7},{6,4},{7,5},{8,10},{9,11},{10,... | collective-permute-start | bytes 393224 | tf_op jit(solution)/shard_map/ppermute | solution.py:33
  (32 other events, 202.6 us)

commit v4 on v3

--- a/solution.py
+++ b/solution.py
@@ -100,22 +100,22 @@
 
 def expert_body(count, place, *refs):
     rows_in, payloads = refs[:count], refs[count : 2 * count]
-    weights = refs[2 * count : 2 * count + 4]
-    outs = refs[2 * count + 4 :]
+    weights = refs[2 * count : 2 * count + 8]
+    outs = refs[2 * count + 8 :]
     combined, deltas = outs[:count], outs[count : 2 * count]
     hiddens, scaleds, back_pres = outs[2 * count :]
     tok_rows, width = rows_in[0].shape
     for first in range(0, count, 2):
-        pair = (first, first + 1)
-        span = slice(first * tok_rows, (first + 2) * tok_rows)
-        rows = jnp.concatenate([rows_in[i][...] for i in pair], axis=0)
-        cotangent = jnp.concatenate([payloads[i][:tok_rows, :] for i in pair], axis=0).astype(wide)
-        out_sum = jnp.zeros((2 * tok_rows, width), wide)
-        delta_sum = jnp.zeros((2 * tok_rows, width), wide)
-        for e in range(2):
+        group = range(first, min(first + 2, count))
+        span = slice(first * tok_rows, (first + len(group)) * tok_rows)
+        stack = lambda values: jnp.concatenate(list(values), axis=0)
+        rows = stack(rows_in[i][...] for i in group)
+        cotangent = stack(payloads[i][:tok_rows, :] for i in group).astype(wide)
+        out_sum = jnp.zeros(rows.shape, wide)
+        delta_sum = jnp.zeros(rows.shape, wide)
+        for e in range(4):
             weight_in, weight_out = weights[2 * e], weights[2 * e + 1]
-            expert = place[3 + e]
-            gate = jnp.concatenate([gate_tile(payloads[i], tok_rows, expert) for i in pair], axis=0)
+            gate = stack(gate_tile(payloads[i], tok_rows, place[3 + e]) for i in group)
             gate = jnp.concatenate([gate] * (width // 128), axis=1)
             active = jnp.maximum(jnp.dot(rows, weight_in[...], preferred_element_type=wide), 0.0)
             hidden = (active * active).astype(narrow)
@@ -129,24 +129,24 @@
             out_sum = out_sum + gate * result.astype(wide)
             back_rows = lax.dot_general(back_pre, weight_in[...], contract_last, preferred_element_type=wide)
             delta_sum = delta_sum + back_rows.astype(narrow).astype(wide)
-        for i in pair:
+        for i in group:
             part = slice((i - first) * tok_rows, (i - first + 1) * tok_rows)
             combined[i][...] = out_sum[part].astype(combined[i].dtype)
             deltas[i][...] = delta_sum[part].astype(deltas[i].dtype)
 
 
-def weight_grad_body(n_rows, n_sets, place, *refs):
+def weight_grad_body(side, n_rows, n_sets, place, *refs):
     rows_in = refs[:n_rows]
     sets = [refs[n_rows + 3 * i : n_rows + 3 * i + 3] for i in range(n_sets)]
-    keep_in, keep_out, send_in, send_out = refs[n_rows + 3 * n_sets :]
+    outs = refs[n_rows + 3 * n_sets :]
     dot = functools.partial(lax.dot_general, dimension_numbers=contract_first, preferred_element_type=wide)
     rows = jnp.concatenate([r[...] for r in rows_in], axis=0)
-    for e, out_in, out_out in ((1, send_in, send_out), (0, keep_in, keep_out)):
-        hidden = jnp.concatenate([s[0][e] for s in sets], axis=0)
-        scaled = jnp.concatenate([s[1][e] for s in sets], axis=0)
-        back_pre = jnp.concatenate([s[2][e] for s in sets], axis=0)
-        out_out[...] = dot(hidden, scaled).astype(out_out.dtype)
-        out_in[...] = dot(rows, back_pre).astype(out_in.dtype)
+    for core in (1, 0):
+        hidden, scaled, back_pre = (
+            jnp.concatenate([values[i][core * 2 + side] for values in sets], axis=0) for i in range(3)
+        )
+        outs[2 * core][...] = dot(rows, back_pre).astype(outs[2 * core].dtype)
+        outs[2 * core + 1][...] = dot(hidden, scaled).astype(outs[2 * core + 1].dtype)
 
 
 def down_grad_body(n_line, place, *refs):
@@ -163,22 +163,17 @@
                 blocks[back][...] = part[z * block : (z + 1) * block].astype(blocks[back].dtype)
 
 
-def token_grad_body(place, *refs):
-    deltas, down, grads = refs[:4], refs[4], refs[5:]
-    for delta, grad in zip(deltas, grads):
-        grad[...] = lax.dot_general(
-            delta[...], down[...], contract_last, preferred_element_type=wide
-        ).astype(narrow)
-
-
-def arrange_body(n_line, block, place, *refs):
-    pieces, out = refs[:4], refs[4]
+def token_grad_body(n_line, block, place, delta, *refs):
+    downs, out = refs[:4], refs[4]
     for core in range(2):
         for side in range(2):
             owner = (place[1] ^ side) * 2 + (place[2] ^ core)
+            part = lax.dot_general(
+                delta[...], downs[core * 2 + side][...], contract_last, preferred_element_type=wide
+            ).astype(narrow)
             for z in range(n_line):
                 start = pl.multiple_of((z * 4 + owner) * block, block)
-                out[:, pl.ds(start, block)] = pieces[core * 2 + side][:, z * block : (z + 1) * block]
+                out[:, pl.ds(start, block)] = part[:, z * block : (z + 1) * block]
 
 
 def all_rows(tokens, routes, gate_levels, latent_grad, down_weight, expert_in, expert_out):
@@ -192,7 +187,8 @@
     major = lax.axis_index("expert")
     my_core = lax.axis_index("dp")
     place = jnp.stack(
-        [major // 2, major % 2, my_core, major * 2 + my_core, major * 2 + 1 - my_core]
+        [major // 2, major % 2, my_core]
+        + [(major ^ side) * 2 + (my_core ^ core) for core in range(2) for side in range(2)]
     ).astype(jnp.int32)
     shape = jax.ShapeDtypeStruct
     rows_of = lambda kind: shape((tok_rows, latent_width), kind)
@@ -207,12 +203,15 @@
         nbytes=3 * tok_rows * width * 2,
     )
     *columns, payload = prepare(place, tokens, routes.T, gate_levels.T, latent_grad)
+    own = [expert_in[0], expert_out[0]]
+    side_in = swap(own[0], n_line, 0, 1)
     near_tokens = columns[:1] + [
-        swap(after(columns[core * 2 + side], downs[1]), n_line, core, side)
+        swap(after(columns[core * 2 + side], side_in), n_line, core, side)
         for core, side in ((0, 1), (1, 0), (1, 1))
     ]
-    own = (expert_in[0], expert_out[0])
-    weights = own + tuple(swap(w, n_line, 1, 0) for w in own)
+    payloads = [payload] + [None] * (n_line - 1)
+    payloads[1] = turn(after(payload, *downs[1:]), n_line, 1)
+    near_tokens[0] = after(near_tokens[0], payloads[1])
 
     project = call(
         functools.partial(project_body, n_line),
@@ -222,98 +221,93 @@
     )
     keep, send, down = project(place, *near_tokens, *downs)
     half = keep + swap(send, n_line, 1, 0)
-    latent = (half[0] + swap(half[1], n_line, 0, 1)).astype(narrow)
-
-    later_payload = after(payload, half)
-    payloads = [payload] + [turn(later_payload, n_line, back) for back in range(1, n_line)]
-    rows = [latent] + [turn(latent, n_line, back) for back in range(1, n_line)]
-    far_rows = [swap(r, n_line, 0, 1) for r in rows]
-    far_payloads = [swap(after(payload, near_tokens[1]), n_line, 0, 1)] + [
-        swap(after(p, latent), n_line, 0, 1) for p in payloads[1:]
-    ]
-
-    def experts(count, kind, name):
-        saved = shape((2, count * tok_rows, hidden_width), narrow)
-        return call(
+    for back in range(2, n_line):
+        payloads[back] = turn(after(payload, half), n_line, back)
+    latent = (half[0] + after(swap(half[1], n_line, 0, 1), *payloads[2:])).astype(narrow)
+    ends = [1, n_line - 1]
+    middle = list(range(2, n_line - 1))
+    groups = [ends, [0], middle]
+    rows = [latent] + [None] * (n_line - 1)
+    for back in ends:
+        rows[back] = turn(latent, n_line, back)
+    end_rows = [rows[back] for back in ends]
+    for back in middle:
+        rows[back] = turn(after(latent, *end_rows), n_line, back)
+
+    side_out = after(swap(after(own[1], latent), n_line, 0, 1), *end_rows)
+    side_down = swap(after(down, side_out), n_line, 0, 1)
+    near = own + [side_in, side_out]
+    all_down = [down, side_down] + [swap(d, n_line, 1, 0) for d in (down, side_down)]
+    weights = near + [swap(w, n_line, 1, 0) for w in near]
+
+    outs_of, deltas_of, saved = [None] * n_line, [None] * n_line, []
+    for group in groups:
+        count = len(group)
+        kind = narrow if group[0] else wide
+        values = call(
             functools.partial(expert_body, count),
-            [rows_of(kind)] * (2 * count) + [saved] * 3,
-            name,
-            flops=2 * 2 * 4 * count * tok_rows * latent_width * hidden_width,
-            nbytes=4 * latent_width * hidden_width * 2,
+            [rows_of(kind)] * (2 * count) + [shape((4, count * tok_rows, hidden_width), narrow)] * 3,
+            "experts",
+            flops=4 * 2 * 4 * count * tok_rows * latent_width * hidden_width,
+            nbytes=8 * latent_width * hidden_width * 2,
+        )(place, *(rows[i] for i in group), *(payloads[i] for i in group), *weights)
+        for i, back in enumerate(group):
+            outs_of[back], deltas_of[back] = values[i], values[count + i]
+        saved.append(list(values[2 * count :]))
+
+    def home(value, back):
+        return turn(value, n_line, n_line - back) if back else value
+
+    delta_lines = [home(value, back) for back, value in enumerate(deltas_of)]
+
+    def weight_grads(side, *earlier):
+        sizes = [(latent_width, hidden_width), (hidden_width, latent_width)]
+        values = call(
+            functools.partial(weight_grad_body, side, n_line, len(groups)),
+            [shape(size, kind) for kind in (wide, narrow) for size in sizes],
+            "weight_grads",
+            flops=2 * 2 * 2 * n_line * tok_rows * latent_width * hidden_width,
+        )(
+            after(place, *earlier),
+            *(rows[i] for group in groups for i in group),
+            *(value for values in saved for value in values),
         )
-
-    outs = experts(n_line, wide, "near_experts")(place, *rows, *payloads, *weights)
-    near_out, near_delta, saved = outs[:n_line], outs[n_line : 2 * n_line], [outs[2 * n_line :]]
-    far_out, far_delta = [], []
-    part = n_line // 2
-    for first in range(0, n_line, part):
-        span = slice(first, first + part)
-        outs = experts(part, narrow, "far_experts")(place, *far_rows[span], *far_payloads[span], *weights)
-        far_out += outs[:part]
-        far_delta += outs[part : 2 * part]
-        saved.append(outs[2 * part :])
-
-    def return_lines(near, far):
-        lines = []
-        for back in range(n_line):
-            line = near[back] + far[back].astype(wide)
-            if back:
-                line = turn(line.astype(narrow), n_line, n_line - back)
-            lines.append(line)
-        return lines
-
-    far_delta = [swap(d, n_line, 0, 1) for d in far_delta]
-    delta = sum(line.astype(wide) for line in return_lines(near_delta, far_delta)).astype(narrow)
-    far_out = [swap(after(o, far_delta[-1]), n_line, 0, 1) for o in far_out]
-    out_lines = return_lines(near_out, far_out)
-
-    weight_grad = call(
-        functools.partial(weight_grad_body, 2 * n_line, len(saved)),
-        [shape((latent_width, hidden_width), wide), shape((hidden_width, latent_width), wide)]
-        + [shape((latent_width, hidden_width), narrow), shape((hidden_width, latent_width), narrow)],
-        "weight_grads",
-        flops=2 * 2 * 2 * 2 * n_line * tok_rows * latent_width * hidden_width,
-    )
-    keep_in, keep_out, send_in, send_out = weight_grad(
-        place, *rows, *far_rows, *(value for values in saved for value in values)
-    )
-    grad_in = (keep_in + swap(send_in, n_line, 1, 0).astype(wide)).astype(narrow)
-    grad_out = (keep_out + swap(send_out, n_line, 1, 0).astype(wide)).astype(narrow)
-
+        return [mine + swap(other, n_line, 1, 0).astype(wide) for mine, other in zip(values[:2], values[2:])]
+
+    far_in, far_out = (
+        value.astype(narrow) for value in weight_grads(1, *(delta_lines[back] for back in ends))
+    )
+    delta_lines = [after(line, far_in, *all_down) for line in delta_lines]
+    delta = sum(line.astype(wide) for line in delta_lines).astype(narrow)
     side_delta = swap(delta, n_line, 0, 1)
+    out_lines = [outs_of[0]] + [None] * (n_line - 1)
+    for back in ends:
+        out_lines[back] = home(after(outs_of[back], delta), back)
+    near_in, near_out = weight_grads(0, *(out_lines[back] for back in ends))
+    far_out = swap(far_out, n_line, 0, 1)
+    grad_out = near_out + far_out.astype(wide)
+    far_in = swap(after(far_in, side_delta), n_line, 0, 1)
+    grad_in = near_in + far_in.astype(wide)
     deltas = [delta, side_delta, swap(delta, n_line, 1, 0), swap(side_delta, n_line, 1, 0)]
-    narrow_columns = shape((tok_rows, n_line * block), narrow)
-    down_grad = call(
+    blocks = call(
         functools.partial(down_grad_body, n_line),
         [shape((block, latent_width), wide)] + [shape((block, latent_width), narrow)] * (n_line - 1),
         "down_grad",
         flops=2 * 4 * tok_rows * n_line * block * latent_width,
-    )
-    blocks = down_grad(place, *near_tokens, *deltas)
-    token_grad = call(
-        token_grad_body,
-        [narrow_columns] * 4,
+    )(place, *near_tokens, *deltas)
+    sent = [after(value, far_out, *(out_lines[back] for back in ends)) for value in blocks]
+    (grad_tokens,) = call(
+        functools.partial(token_grad_body, n_line, block),
+        [shape((tok_rows, width), narrow)],
         "token_grad",
         flops=2 * 4 * tok_rows * n_line * block * latent_width,
-    )
-    grads = token_grad(place, *deltas, down)
-    blocks = [blocks[0]] + [turn(blocks[back], n_line, n_line - back) for back in range(1, n_line)]
-    grad_down = sum(value.astype(wide) for value in blocks)
-    out_lines = [after(line, blocks[1]) for line in out_lines]
+    )(place, after(delta, blocks[1]), *all_down)
+    blocks = [blocks[0]] + [home(sent[back], back) for back in range(1, n_line)]
+    for back in middle:
+        out_lines[back] = home(after(outs_of[back], *(out_lines[end] for end in ends)), back)
+    grad_down = sum(after(value, far_in).astype(wide) for value in blocks)
     latent_out = sum(line.astype(wide) for line in out_lines).astype(narrow)
-    grads = [
-        grads[core * 2 + side] if core + side == 0 else swap(grads[core * 2 + side], n_line, core, side)
-        for core in range(2)
-        for side in range(2)
-    ]
-    arrange = call(
-        functools.partial(arrange_body, n_line, block),
-        [shape((tok_rows, width), narrow)],
-        "arrange",
-        nbytes=2 * tok_rows * width * 2,
-    )
-    (grad_tokens,) = arrange(place, *grads)
-    return (latent_out, grad_tokens, grad_down, grad_in[None], grad_out[None])
+    return (latent_out, grad_tokens, grad_down, grad_in.astype(narrow)[None], grad_out.astype(narrow)[None])
 
 
 def slot_table(routes, capacity):
@@ -437,7 +431,7 @@
 def on_device(tokens, routes, *others):
     n_major = lax.axis_size("expert")
     n_experts = n_major * lax.axis_size("dp")
-    few = n_experts <= 2 * routes.shape[1] and n_major % 4 == 0 and lax.axis_size("dp") == 2
+    few = n_experts <= 2 * routes.shape[1] and n_major % 2 == 0 and n_major >= 6 and lax.axis_size("dp") == 2
     return (all_rows if few else routed_rows)(tokens, routes, *others)
 
 

time: 138 us -> 120 us (0.87)
  starting transfers between devices: 61.5 us -> 47.6 us
  waiting for transfers between devices: 51 us -> 46.7 us
    ppermute x31 -> x23, waiting for transfers between devices: 26.5 us -> 10.2 us  [swap(): lax.ppermute(value, plane, device_pairs(n_line, lambda z, x, c: (z, x ^ s...]
    ppermute x18, waiting for transfers between devices: 24.4 us -> 36.4 us  [turn(): lax.ppermute(value, plane, device_pairs(n_line, lambda z, x, c: ((z + by)...]
    ppermute x31 -> x23, starting transfers between devices: 26.1 us -> 14.8 us  [swap(): lax.ppermute(value, plane, device_pairs(n_line, lambda z, x, c: (z, x ^ s...]
    ppermute x18, starting transfers between devices: 35.4 us -> 32.8 us  [turn(): lax.ppermute(value, plane, device_pairs(n_line, lambda z, x, c: ((z + by)...]
  transfers between devices with their start and end apart: 49 -> 41, of which waited for: 21 -> 18; matrix products, arithmetic and copies ran while one was open for 3% -> 3% of each run, Pallas kernels for 10% -> 14%
where the time goes in v4:
time: 120 us; the launch traced here: 119 us
  starting transfers between devices  47.6 us (40%)
  waiting for transfers between devices  46.7 us (39%)
  Pallas kernels  17.5 us (15%)
  other arithmetic  4.02 us (3%)
  local copies, waits for them, and re-layouts  2.68 us (2%)
    ppermute x18, waiting for transfers between devices, turn(): lax.ppermute(value, plane, device_pairs(n_line, lambda z, x, c: ((z + by)...  36.4 us
    ppermute x18, starting transfers between devices, turn(): lax.ppermute(value, plane, device_pairs(n_line, lambda z, x, c: ((z + by)...  32.8 us
    pallas_call x9, Pallas kernels, run(): pl.pallas_call(body, out_shape=outs, in_specs=[pl.BlockSpec(memory_space=...  17.5 us
    ppermute x23, starting transfers between devices, swap(): lax.ppermute(value, plane, device_pairs(n_line, lambda z, x, c: (z, x ^ s...  14.8 us
    ppermute x23, waiting for transfers between devices, swap(): lax.ppermute(value, plane, device_pairs(n_line, lambda z, x, c: (z, x ^ s...  10.2 us
    unnamed x14, local copies, waits for them, and re-layouts  2.58 us
  transfers between devices with their start and end apart: 41, of which 18 were waited for; matrix products, arithmetic and copies ran while one was open for 3% of the time, Pallas kernels for 14%

profile of v4, /device:TPU:0, one launch (start us, length us, event | category | flops | bytes accessed | tf_op | source)
XLA Modules:
  0.0 119.4 jit_solution(1304984368453486360)
XLA Ops:
  0.6 3.0 %collective-permute-start.4 = (bf16[512,512]{1,0:T(8,128)(2,1)}, bf16[512,512]{1,0:T(8,128)(2,1)S(1)}, u32[]{:S(2)}, u32[]{:S(2)}) collective-permute-start(bf16[512,512]{1,0:T(8,128)(2,1)} %bitcast.23), channel_id=1, source_target_pairs={{0,2},{1,3},{2,0},{3,1},{4,6},{5,7},{6,4},{7,5},{8,10},{9,11},{10,... | collective-permute-start | bytes 1572872 | tf_op jit(solution)/shard_map/ppermute | solution.py:33
  5.2 2.6 %collective-permute-start.1 = (bf16[128,512]{1,0:T(8,128)(2,1)}, bf16[128,512]{1,0:T(8,128)(2,1)S(1)}, u32[]{:S(2)}, u32[]{:S(2)}) collective-permute-start(bf16[128,512]{1,0:T(8,128)(2,1)} %refs_4_.1), channel_id=1, source_target_pairs={{0,8},{1,9},{2,10},{3,11},{4,12},{5,13},{6,14},{7,15},{8,0},{9,1},... | collective-permute-start | bytes 393224 | tf_op jit(solution)/shard_map/ppermute | solution.py:29
  12.5 3.9 %collective-permute-done.1.refs_6_ = bf16[128,512]{1,0:T(8,128)(2,1)S(1)} collective-permute-done((bf16[128,512]{1,0:T(8,128)(2,1)}, bf16[128,512]{1,0:T(8,128)(2,1)S(1)}, u32[]{:S(2)}, u32[]{:S(2)}) %collective-permute-start.1) | collective-permute-done | bytes 131104 | tf_op jit(solution)/shard_map/ppermute | solution.py:29
  16.4 3.3 %collective-permute-start.3 = (bf16[144,512]{1,0:T(8,128)(2,1)S(1)}, bf16[144,512]{1,0:T(8,128)(2,1)S(1)}, u32[]{:S(2)}, u32[]{:S(2)}) collective-permute-start(bf16[144,512]{1,0:T(8,128)(2,1)S(1)} %get-tuple-element.83.refs_1_), channel_id=1, source_target_pairs={{0,4},{1,5},{2,6},{3,7},{4,8},{5,9},{6,10},{7,11},{8,12},{9,13},{1... | collective-permute-start | bytes 442376 | tf_op jit(solution)/shard_map/ppermute | solution.py:29
  21.8 2.1 %collective-permute-done.3.refs_2_ = bf16[144,512]{1,0:T(8,128)(2,1)S(1)} collective-permute-done((bf16[144,512]{1,0:T(8,128)(2,1)S(1)}, bf16[144,512]{1,0:T(8,128)(2,1)S(1)}, u32[]{:S(2)}, u32[]{:S(2)}) %collective-permute-start.3) | collective-permute-done | bytes 147488 | tf_op jit(solution)/shard_map/ppermute | solution.py:29
  23.9 2.2 %collective-permute-done.5.refs_1_ = bf16[128,512]{1,0:T(8,128)(2,1)S(1)} collective-permute-done((bf16[128,512]{1,0:T(8,128)(2,1)S(1)}, bf16[128,512]{1,0:T(8,128)(2,1)S(1)}, u32[]{:S(2)}, u32[]{:S(2)}) %collective-permute-start.5) | collective-permute-done | bytes 131104 | tf_op jit(solution)/shard_map/ppermute | solution.py:33
  33.5 7.1 %collective-permute-done.10.refs_1_ = bf16[144,512]{1,0:T(8,128)(2,1)S(1)} collective-permute-done((bf16[144,512]{1,0:T(8,128)(2,1)S(1)}, bf16[144,512]{1,0:T(8,128)(2,1)S(1)}, u32[]{:S(2)}, u32[]{:S(2)}) %collective-permute-start.10) | collective-permute-done | bytes 147488 | tf_op jit(solution)/shard_map/ppermute | solution.py:29
  42.5 3.3 %collective-permute-start.13 = (bf16[128,512]{1,0:T(8,128)(2,1)S(1)}, bf16[128,512]{1,0:T(8,128)(2,1)S(1)}, u32[]{:S(2)}, u32[]{:S(2)}) collective-permute-start(bf16[128,512]{1,0:T(8,128)(2,1)S(1)} %fusion.3.refs_0_.refs_2_), channel_id=1, source_target_pairs={{0,4},{1,5},{2,6},{3,7},{4,8},{5,9},{6,10},{7,11},{8,12},{9,13},{1... | collective-permute-start | bytes 393224 | tf_op jit(solution)/shard_map/ppermute | solution.py:29
  46.9 3.7 %collective-permute-done.13.refs_0_ = bf16[128,512]{1,0:T(8,128)(2,1)S(1)} collective-permute-done((bf16[128,512]{1,0:T(8,128)(2,1)S(1)}, bf16[128,512]{1,0:T(8,128)(2,1)S(1)}, u32[]{:S(2)}, u32[]{:S(2)}) %collective-permute-start.13) | collective-permute-done | bytes 131104 | tf_op jit(solution)/shard_map/ppermute | solution.py:29
  52.1 2.3 %collective-permute-done.12.refs_5_.refs_7_ = bf16[512,512]{1,0:T(8,128)(2,1)S(1)} collective-permute-done((bf16[512,512]{1,0:T(8,128)(2,1)S(1)}, bf16[512,512]{1,0:T(8,128)(2,1)S(1)}, u32[]{:S(2)}, u32[]{:S(2)}) %collective-permute-start.12) | collective-permute-done | bytes 524320 | tf_op jit(solution)/shard_map/ppermute | solution.py:33
  54.4 2.7 %collective-permute-start.21 = (bf16[128,512]{1,0:T(8,128)(2,1)S(1)}, bf16[128,512]{1,0:T(8,128)(2,1)S(1)}, u32[]{:S(2)}, u32[]{:S(2)}) collective-permute-start(bf16[128,512]{1,0:T(8,128)(2,1)S(1)} %fusion.3.refs_0_.refs_2_), channel_id=1, source_target_pairs={{0,8},{1,9},{2,10},{3,11},{4,12},{5,13},{6,14},{7,15},{8,0},{9,1},... | collective-permute-start | bytes 393224 | tf_op jit(solution)/shard_map/ppermute | solution.py:29
  58.7 3.4 %experts.4 = (bf16[128,512]{1,0:T(8,128)(2,1)S(1)}, bf16[128,512]{1,0:T(8,128)(2,1)S(1)}, bf16[128,512]{1,0:T(8,128)(2,1)S(1)}, bf16[128,512]{1,0:T(8,128)(2,1)S...) custom-call(s32[7]{0:T(128)S(1)} %stack.31.place, ...), custom_call_target="tpu_custom_call" | custom-call | flops 2147483648 | bytes 4194304 | tf_op jit(solution)/shard_map/experts/pallas_call | solution.py:44
  63.5 2.5 %collective-permute-start.19 = (bf16[128,512]{1,0:T(8,128)(2,1)S(1)}, bf16[128,512]{1,0:T(8,128)(2,1)S(1)}, u32[]{:S(2)}, u32[]{:S(2)}) collective-permute-start(bf16[128,512]{1,0:T(8,128)(2,1)S(1)} %get-tuple-element.90), channel_id=1, source_target_pairs={{0,12},{1,13},{2,14},{3,15},{4,0},{5,1},{6,2},{7,3},{8,4},{9,5},{1... | collective-permute-start | bytes 393224 | tf_op jit(solution)/shard_map/ppermute | solution.py:29
  66.0 2.7 %experts.3 = (f32[128,512]{1,0:T(8,128)S(1)}, f32[128,512]{1,0:T(8,128)S(1)}, bf16[4,128,512]{2,1,0:T(8,128)(2,1)S(1)}, bf16[4,128,512]{2,1,0:T(8,128)(2,1)S(1)}, bf16[4,128,512]{2,1,0:T(8,128)(2,1)S(1)}) custom-call(s32[7]{0:T(128)S(1)} %stack.31.place, bf16[128,512]{1,0:T(8,128)(2,1)S(1)} %fusion.3.refs_0_.refs_2_, ...), custom_call_target="tpu_custom_call" | custom-call | flops 1073741824 | bytes 4194304 | tf_op jit(solution)/shard_map/experts/pallas_call | solution.py:44
  68.7 2.7 %experts.5 = (bf16[128,512]{1,0:T(8,128)(2,1)S(1)}, bf16[128,512]{1,0:T(8,128)(2,1)S(1)}, bf16[4,128,512]{2,1,0:T(8,128)(2,1)S(1)}, bf16[4,128,512]{2,1,0:T(8,128)(2,1)S(1)}, bf16[4,128,512]{2,1,0:T(8,128)(2,1)S(1)}) custom-call(s32[7]{0:T(128)S(1)} %stack.31.place, bf16[128,512]{1,0:T(8,128)(2,1)S(1)} %collective-permute-done.21.refs_0_.refs_3_, ...), custom_call_target="tpu_custom_call" | custom-call | flops 1073741824 | bytes 4194304 | tf_op jit(solution)/shard_map/experts/pallas_call | solution.py:44
  76.9 6.8 %collective-permute-done.26 = bf16[128,512]{1,0:T(8,128)(2,1)S(1)} collective-permute-done((bf16[128,512]{1,0:T(8,128)(2,1)S(1)}, bf16[128,512]{1,0:T(8,128)(2,1)S(1)}, u32[]{:S(2)}, u32[]{:S(2)}) %collective-permute-start.26) | collective-permute-done | bytes 131104 | tf_op jit(solution)/shard_map/ppermute | solution.py:29
  84.9 3.8 %collective-permute-start.27 = (bf16[128,512]{1,0:T(8,128)(2,1)S(1)}, bf16[128,512]{1,0:T(8,128)(2,1)S(1)}, u32[]{:S(2)}, u32[]{:S(2)}) collective-permute-start(bf16[128,512]{1,0:T(8,128)(2,1)S(1)} %get-tuple-element.112), channel_id=1, source_target_pairs={{0,12},{1,13},{2,14},{3,15},{4,0},{5,1},{6,2},{7,3},{8,4},{9,5},{1... | collective-permute-start | bytes 393224 | tf_op jit(solution)/shard_map/ppermute | solution.py:29
  89.9 3.1 %collective-permute-done.28 = bf16[128,512]{1,0:T(8,128)(2,1)S(1)} collective-permute-done((bf16[128,512]{1,0:T(8,128)(2,1)S(1)}, bf16[128,512]{1,0:T(8,128)(2,1)S(1)}, u32[]{:S(2)}, u32[]{:S(2)}) %collective-permute-start.28) | collective-permute-done | bytes 131104 | tf_op jit(solution)/shard_map/ppermute | solution.py:29
  95.5 2.2 %collective-permute-start.29 = (bf16[128,512]{1,0:T(8,128)(2,1)S(1)}, bf16[128,512]{1,0:T(8,128)(2,1)S(1)}, u32[]{:S(2)}, u32[]{:S(2)}) collective-permute-start(bf16[128,512]{1,0:T(8,128)(2,1)S(1)} %get-tuple-element.116), channel_id=1, source_target_pairs={{0,8},{1,9},{2,10},{3,11},{4,12},{5,13},{6,14},{7,15},{8,0},{9,1},... | collective-permute-start | bytes 393224 | tf_op jit(solution)/shard_map/ppermute | solution.py:29
  99.4 2.2 %token_grad.1 = bf16[128,2048]{1,0:T(8,128)(2,1)} custom-call(s32[7]{0:T(128)S(1)} %stack.31.place, bf16[128,512]{1,0:T(8,128)(2,1)S(1)} %add_convert_fusion.5.refs_4_.delta, bf16[512,512]{1,0:T(8,128)(2,1)S(1)} %get-tuple-element.106.refs_0_, bf16[512,512]{1,0:T(8,128)(2,1)S(1)} %collective-permute-done.23.refs_1_, ...), custom_call_target="tpu_custom_call" | custom-call | flops 268435456 | tf_op jit(solution)/shard_map/token_grad/pallas_call | solution.py:44
  101.6 3.2 %collective-permute-done.29 = bf16[128,512]{1,0:T(8,128)(2,1)S(1)} collective-permute-done((bf16[128,512]{1,0:T(8,128)(2,1)S(1)}, bf16[128,512]{1,0:T(8,128)(2,1)S(1)}, u32[]{:S(2)}, u32[]{:S(2)}) %collective-permute-start.29) | collective-permute-done | bytes 131104 | tf_op jit(solution)/shard_map/ppermute | solution.py:29
  105.6 3.2 %collective-permute-start.37 = (bf16[128,512]{1,0:T(8,128)(2,1)S(1)}, bf16[128,512]{1,0:T(8,128)(2,1)S(1)}, u32[]{:S(2)}, u32[]{:S(2)}) collective-permute-start(bf16[128,512]{1,0:T(8,128)(2,1)S(1)} %get-tuple-element.127), channel_id=1, source_target_pairs={{0,8},{1,9},{2,10},{3,11},{4,12},{5,13},{6,14},{7,15},{8,0},{9,1},... | collective-permute-start | bytes 393224 | tf_op jit(solution)/shard_map/ppermute | solution.py:29
  110.4 2.8 %collective-permute-done.33 = bf16[512,512]{1,0:T(8,128)(2,1)S(1)} collective-permute-done((bf16[512,512]{1,0:T(8,128)(2,1)S(1)}, bf16[512,512]{1,0:T(8,128)(2,1)S(1)}, u32[]{:S(2)}, u32[]{:S(2)}) %collective-permute-start.33) | collective-permute-done | bytes 524320 | tf_op jit(solution)/shard_map/ppermute | solution.py:33
  114.2 4.4 %collective-permute-done.37 = bf16[128,512]{1,0:T(8,128)(2,1)S(1)} collective-permute-done((bf16[128,512]{1,0:T(8,128)(2,1)S(1)}, bf16[128,512]{1,0:T(8,128)(2,1)S(1)}, u32[]{:S(2)}, u32[]{:S(2)}) %collective-permute-start.37) | collective-permute-done | bytes 131104 | tf_op jit(solution)/shard_map/ppermute | solution.py:29
  (92 shorter events, 39.5 us)
Async XLA Ops:
  0.6 19.1 %collective-permute-start.4 = (bf16[512,512]{1,0:T(8,128)(2,1)}, bf16[512,512]{1,0:T(8,128)(2,1)S(1)}, u32[]{:S(2)}, u32[]{:S(2)}) collective-permute-start(bf16[512,512]{1,0:T(8,128)(2,1)} %bitcast.23), channel_id=1, source_target_pairs={{0,2},{1,3},{2,0},{3,1},{4,6},{5,7},{6,4},{7,5},{8,10},{9,11},{10,... | collective-permute-start | bytes 1572872 | tf_op jit(solution)/shard_map/ppermute | solution.py:33
  3.6 8.9 %collective-permute-start = (bf16[128,512]{1,0:T(8,128)(2,1)}, bf16[128,512]{1,0:T(8,128)(2,1)S(1)}, u32[]{:S(2)}, u32[]{:S(2)}) collective-permute-start(bf16[128,512]{1,0:T(8,128)(2,1)} %refs_4_.1), channel_id=1, source_target_pairs={{0,4},{1,5},{2,6},{3,7},{4,8},{5,9},{6,10},{7,11},{8,12},{9,13},{1... | collective-permute-start | bytes 393224 | tf_op jit(solution)/shard_map/ppermute | solution.py:29
  5.2 11.2 %collective-permute-start.1 = (bf16[128,512]{1,0:T(8,128)(2,1)}, bf16[128,512]{1,0:T(8,128)(2,1)S(1)}, u32[]{:S(2)}, u32[]{:S(2)}) collective-permute-start(bf16[128,512]{1,0:T(8,128)(2,1)} %refs_4_.1), channel_id=1, source_target_pairs={{0,8},{1,9},{2,10},{3,11},{4,12},{5,13},{6,14},{7,15},{8,0},{9,1},... | collective-permute-start | bytes 393224 | tf_op jit(solution)/shard_map/ppermute | solution.py:29
  7.8 8.6 %collective-permute-start.2 = (bf16[128,512]{1,0:T(8,128)(2,1)}, bf16[128,512]{1,0:T(8,128)(2,1)S(1)}, u32[]{:S(2)}, u32[]{:S(2)}) collective-permute-start(bf16[128,512]{1,0:T(8,128)(2,1)} %refs_4_.1), channel_id=1, source_target_pairs={{0,12},{1,13},{2,14},{3,15},{4,0},{5,1},{6,2},{7,3},{8,4},{9,5},{1... | collective-permute-start | bytes 393224 | tf_op jit(solution)/shard_map/ppermute | solution.py:29
  30.2 10.7 %collective-permute-start.9 = (f32[128,512]{1,0:T(8,128)S(1)}, f32[128,512]{1,0:T(8,128)S(1)}, u32[]{:S(2)}, u32[]{:S(2)}) collective-permute-start(f32[128,512]{1,0:T(8,128)S(1)} %slice_bitcast_fusion), channel_id=1, source_target_pairs={{0,2},{1,3},{2,0},{3,1},{4,6},{5,7},{6,4},{7,5},{8,10},{9,11},{10,... | collective-permute-start | bytes 786440 | tf_op jit(solution)/shard_map/ppermute | solution.py:33
  30.8 9.7 %collective-permute-start.10 = (bf16[144,512]{1,0:T(8,128)(2,1)S(1)}, bf16[144,512]{1,0:T(8,128)(2,1)S(1)}, u32[]{:S(2)}, u32[]{:S(2)}) collective-permute-start(bf16[144,512]{1,0:T(8,128)(2,1)S(1)} %get-tuple-element.83.refs_1_), channel_id=1, source_target_pairs={{0,8},{1,9},{2,10},{3,11},{4,12},{5,13},{6,14},{7,15},{8,0},{9,1},... | collective-permute-start | bytes 442376 | tf_op jit(solution)/shard_map/ppermute | solution.py:29
  32.3 8.6 %collective-permute-start.11 = (bf16[144,512]{1,0:T(8,128)(2,1)S(1)}, bf16[144,512]{1,0:T(8,128)(2,1)S(1)}, u32[]{:S(2)}, u32[]{:S(2)}) collective-permute-start(bf16[144,512]{1,0:T(8,128)(2,1)S(1)} %get-tuple-element.83.refs_1_), channel_id=1, source_target_pairs={{0,12},{1,13},{2,14},{3,15},{4,0},{5,1},{6,2},{7,3},{8,4},{9,5},{1... | collective-permute-start | bytes 442376 | tf_op jit(solution)/shard_map/ppermute | solution.py:29
  41.0 13.4 %collective-permute-start.12 = (bf16[512,512]{1,0:T(8,128)(2,1)S(1)}, bf16[512,512]{1,0:T(8,128)(2,1)S(1)}, u32[]{:S(2)}, u32[]{:S(2)}) collective-permute-start(bf16[512,512]{1,0:T(8,128)(2,1)S(1)} %bitcast.28), channel_id=1, source_target_pairs={{0,2},{1,3},{2,0},{3,1},{4,6},{5,7},{6,4},{7,5},{8,10},{9,11},{10,... | collective-permute-start | bytes 1572872 | tf_op jit(solution)/shard_map/ppermute | solution.py:33
  46.4 10.7 %collective-permute-start.15 = (bf16[512,512]{1,0:T(8,128)(2,1)S(1)}, bf16[512,512]{1,0:T(8,128)(2,1)S(1)}, u32[]{:S(2)}, u32[]{:S(2)}) collective-permute-start(bf16[512,512]{1,0:T(8,128)(2,1)S(1)} %bitcast.24), channel_id=1, source_target_pairs={{0,1},{1,0},{2,3},{3,2},{4,5},{5,4},{6,7},{7,6},{8,9},{9,8},{10,11... | collective-permute-start | bytes 1572872 | tf_op jit(solution)/shard_map/ppermute | solution.py:33
  46.4 12.3 %collective-permute-start.16 = (bf16[512,512]{1,0:T(8,128)(2,1)S(1)}, bf16[512,512]{1,0:T(8,128)(2,1)S(1)}, u32[]{:S(2)}, u32[]{:S(2)}) collective-permute-start(bf16[512,512]{1,0:T(8,128)(2,1)S(1)} %bitcast.29), channel_id=1, source_target_pairs={{0,1},{1,0},{2,3},{3,2},{4,5},{5,4},{6,7},{7,6},{8,9},{9,8},{10,11... | collective-permute-start | bytes 1572872 | tf_op jit(solution)/shard_map/ppermute | solution.py:33
  54.4 14.2 %collective-permute-start.21 = (bf16[128,512]{1,0:T(8,128)(2,1)S(1)}, bf16[128,512]{1,0:T(8,128)(2,1)S(1)}, u32[]{:S(2)}, u32[]{:S(2)}) collective-permute-start(bf16[128,512]{1,0:T(8,128)(2,1)S(1)} %fusion.3.refs_0_.refs_2_), channel_id=1, source_target_pairs={{0,8},{1,9},{2,10},{3,11},{4,12},{5,13},{6,14},{7,15},{8,0},{9,1},... | collective-permute-start | bytes 393224 | tf_op jit(solution)/shard_map/ppermute | solution.py:29
  57.2 16.9 %collective-permute-start.23 = (bf16[512,512]{1,0:T(8,128)(2,1)S(1)}, bf16[512,512]{1,0:T(8,128)(2,1)S(1)}, u32[]{:S(2)}, u32[]{:S(2)}) collective-permute-start(bf16[512,512]{1,0:T(8,128)(2,1)S(1)} %get-tuple-element.106.refs_0_), channel_id=1, source_target_pairs={{0,2},{1,3},{2,0},{3,1},{4,6},{5,7},{6,4},{7,5},{8,10},{9,11},{10,... | collective-permute-start | bytes 1572872 | tf_op jit(solution)/shard_map/ppermute | solution.py:33
  62.1 9.3 %collective-permute-start.20 = (bf16[128,512]{1,0:T(8,128)(2,1)S(1)}, bf16[128,512]{1,0:T(8,128)(2,1)S(1)}, u32[]{:S(2)}, u32[]{:S(2)}) collective-permute-start(bf16[128,512]{1,0:T(8,128)(2,1)S(1)} %get-tuple-element.91), channel_id=1, source_target_pairs={{0,4},{1,5},{2,6},{3,7},{4,8},{5,9},{6,10},{7,11},{8,12},{9,13},{1... | collective-permute-start | bytes 393224 | tf_op jit(solution)/shard_map/ppermute | solution.py:29
  74.1 14.6 %collective-permute-start.34 = (bf16[512,512]{1,0:T(8,128)(2,1)S(1)}, bf16[512,512]{1,0:T(8,128)(2,1)S(1)}, u32[]{:S(2)}, u32[]{:S(2)}) collective-permute-start(bf16[512,512]{1,0:T(8,128)(2,1)S(1)} %get-tuple-element.123), channel_id=1, source_target_pairs={{0,1},{1,0},{2,3},{3,2},{4,5},{5,4},{6,7},{7,6},{8,9},{9,8},{10,11... | collective-permute-start | bytes 1572872 | tf_op jit(solution)/shard_map/ppermute | solution.py:33
  74.5 9.2 %collective-permute-start.26 = (bf16[128,512]{1,0:T(8,128)(2,1)S(1)}, bf16[128,512]{1,0:T(8,128)(2,1)S(1)}, u32[]{:S(2)}, u32[]{:S(2)}) collective-permute-start(bf16[128,512]{1,0:T(8,128)(2,1)S(1)} %get-tuple-element.109), channel_id=1, source_target_pairs={{0,8},{1,9},{2,10},{3,11},{4,12},{5,13},{6,14},{7,15},{8,0},{9,1},... | collective-permute-start | bytes 393224 | tf_op jit(solution)/shard_map/ppermute | solution.py:29
  83.8 11.7 %collective-permute-start.30 = (bf16[128,512]{1,0:T(8,128)(2,1)S(1)}, bf16[128,512]{1,0:T(8,128)(2,1)S(1)}, u32[]{:S(2)}, u32[]{:S(2)}) collective-permute-start(bf16[128,512]{1,0:T(8,128)(2,1)S(1)} %add_convert_fusion.5.refs_4_.delta), channel_id=1, source_target_pairs={{0,2},{1,3},{2,0},{3,1},{4,6},{5,7},{6,4},{7,5},{8,10},{9,11},{10,... | collective-permute-start | bytes 393224 | tf_op jit(solution)/shard_map/ppermute | solution.py:33
  88.9 16.7 %collective-permute-start.35 = (bf16[512,512]{1,0:T(8,128)(2,1)S(1)}, bf16[512,512]{1,0:T(8,128)(2,1)S(1)}, u32[]{:S(2)}, u32[]{:S(2)}) collective-permute-start(bf16[512,512]{1,0:T(8,128)(2,1)S(1)} %add_convert_fusion.2), channel_id=1, source_target_pairs={{0,2},{1,3},{2,0},{3,1},{4,6},{5,7},{6,4},{7,5},{8,10},{9,11},{10,... | collective-permute-start | bytes 1572872 | tf_op jit(solution)/shard_map/ppermute | solution.py:33
  94.9 13.9 %collective-permute-start.40 = (bf16[512,512]{1,0:T(8,128)(2,1)S(1)}, bf16[512,512]{1,0:T(8,128)(2,1)S(1)}, u32[]{:S(2)}, u32[]{:S(2)}) collective-permute-start(bf16[512,512]{1,0:T(8,128)(2,1)S(1)} %get-tuple-element.136), channel_id=1, source_target_pairs={{0,1},{1,0},{2,3},{3,2},{4,5},{5,4},{6,7},{7,6},{8,9},{9,8},{10,11... | collective-permute-start | bytes 1572872 | tf_op jit(solution)/shard_map/ppermute | solution.py:33
  95.5 9.3 %collective-permute-start.29 = (bf16[128,512]{1,0:T(8,128)(2,1)S(1)}, bf16[128,512]{1,0:T(8,128)(2,1)S(1)}, u32[]{:S(2)}, u32[]{:S(2)}) collective-permute-start(bf16[128,512]{1,0:T(8,128)(2,1)S(1)} %get-tuple-element.116), channel_id=1, source_target_pairs={{0,8},{1,9},{2,10},{3,11},{4,12},{5,13},{6,14},{7,15},{8,0},{9,1},... | collective-permute-start | bytes 393224 | tf_op jit(solution)/shard_map/ppermute | solution.py:29
  97.7 15.5 %collective-permute-start.33 = (bf16[512,512]{1,0:T(8,128)(2,1)S(1)}, bf16[512,512]{1,0:T(8,128)(2,1)S(1)}, u32[]{:S(2)}, u32[]{:S(2)}) collective-permute-start(bf16[512,512]{1,0:T(8,128)(2,1)S(1)} %add_convert_fusion.3), channel_id=1, source_target_pairs={{0,2},{1,3},{2,0},{3,1},{4,6},{5,7},{6,4},{7,5},{8,10},{9,11},{10,... | collective-permute-start | bytes 1572872 | tf_op jit(solution)/shard_map/ppermute | solution.py:33
  98.2 15.0 %collective-permute-start.39 = (bf16[512,512]{1,0:T(8,128)(2,1)S(1)}, bf16[512,512]{1,0:T(8,128)(2,1)S(1)}, u32[]{:S(2)}, u32[]{:S(2)}) collective-permute-start(bf16[512,512]{1,0:T(8,128)(2,1)S(1)} %get-tuple-element.134), channel_id=1, source_target_pairs={{0,1},{1,0},{2,3},{3,2},{4,5},{5,4},{6,7},{7,6},{8,9},{9,8},{10,11... | collective-permute-start | bytes 1572872 | tf_op jit(solution)/shard_map/ppermute | solution.py:33
  105.6 8.6 %collective-permute-start.38 = (bf16[128,512]{1,0:T(8,128)(2,1)S(1)}, bf16[128,512]{1,0:T(8,128)(2,1)S(1)}, u32[]{:S(2)}, u32[]{:S(2)}) collective-permute-start(bf16[128,512]{1,0:T(8,128)(2,1)S(1)} %get-tuple-element.130), channel_id=1, source_target_pairs={{0,4},{1,5},{2,6},{3,7},{4,8},{5,9},{6,10},{7,11},{8,12},{9,13},{1... | collective-permute-start | bytes 393224 | tf_op jit(solution)/shard_map/ppermute | solution.py:29
  105.6 13.0 %collective-permute-start.37 = (bf16[128,512]{1,0:T(8,128)(2,1)S(1)}, bf16[128,512]{1,0:T(8,128)(2,1)S(1)}, u32[]{:S(2)}, u32[]{:S(2)}) collective-permute-start(bf16[128,512]{1,0:T(8,128)(2,1)S(1)} %get-tuple-element.127), channel_id=1, source_target_pairs={{0,8},{1,9},{2,10},{3,11},{4,12},{5,13},{6,14},{7,15},{8,0},{9,1},... | collective-permute-start | bytes 393224 | tf_op jit(solution)/shard_map/ppermute | solution.py:29
  108.8 9.8 %collective-permute-start.36 = (bf16[128,512]{1,0:T(8,128)(2,1)S(1)}, bf16[128,512]{1,0:T(8,128)(2,1)S(1)}, u32[]{:S(2)}, u32[]{:S(2)}) collective-permute-start(bf16[128,512]{1,0:T(8,128)(2,1)S(1)} %get-tuple-element.124), channel_id=1, source_target_pairs={{0,12},{1,13},{2,14},{3,15},{4,0},{5,1},{6,2},{7,3},{8,4},{9,5},{1... | collective-permute-start | bytes 393224 | tf_op jit(solution)/shard_map/ppermute | solution.py:29
  (24 other events, 138.0 us)

commit v5 on v4

--- a/solution.py
+++ b/solution.py
@@ -37,32 +37,47 @@
     return lax.optimization_barrier((value,) + earlier)[0]
 
 
-def call(body, outs, name, scratch=(), flops=0, nbytes=0):
+def call(body, outs, name, scratch=(), outside=0):
     vmem = pl.BlockSpec(memory_space=pltpu.VMEM)
+    anywhere = pl.BlockSpec(memory_space=pl.ANY)
 
     def run(place, *operands):
         return pl.pallas_call(
             body,
             out_shape=outs,
-            in_specs=[pl.BlockSpec(memory_space=pltpu.SMEM)] + [vmem] * len(operands),
+            in_specs=[pl.BlockSpec(memory_space=pltpu.SMEM)]
+            + [anywhere] * outside
+            + [vmem] * (len(operands) - outside),
             out_specs=[vmem] * len(outs),
             scratch_shapes=list(scratch),
             compiler_params=pltpu.CompilerParams(vmem_limit_bytes=40 * 1024 * 1024),
-            cost_estimate=pl.CostEstimate(flops=flops, bytes_accessed=nbytes, transcendentals=0),
+            cost_estimate=pl.CostEstimate(flops=0, bytes_accessed=0, transcendentals=0),
             name=name,
         )(place, *operands)
 
     return run
 
 
-def prepare_body(n_line, block, place, tokens, routes, levels, cotangent, *outs):
-    pieces, payload = outs[:4], outs[4]
+def columns_body(n_line, block, place, tokens, *refs):
+    own, other, across, sems = refs
+    pieces = (own, across.at[0], other, across.at[1])
+    copies = []
     for core in range(2):
         for side in range(2):
             owner = (place[1] ^ side) * 2 + (place[2] ^ core)
             for z in range(n_line):
                 start = pl.multiple_of((z * 4 + owner) * block, block)
-                pieces[core * 2 + side][:, z * block : (z + 1) * block] = tokens[:, pl.ds(start, block)]
+                piece = pieces[core * 2 + side].at[:, pl.ds(z * block, block)]
+                copies.append(
+                    pltpu.make_async_copy(tokens.at[:, pl.ds(start, block)], piece, sems.at[len(copies)])
+                )
+    for copy in copies:
+        copy.start()
+    for copy in copies:
+        copy.wait()
+
+
+def payload_body(place, routes, levels, cotangent, payload):
     tok_rows = cotangent.shape[0]
     gate_rows = payload.shape[0] - tok_rows
     payload[:tok_rows, :] = cotangent[...]
@@ -145,8 +160,16 @@
         hidden, scaled, back_pre = (
             jnp.concatenate([values[i][core * 2 + side] for values in sets], axis=0) for i in range(3)
         )
-        outs[2 * core][...] = dot(rows, back_pre).astype(outs[2 * core].dtype)
-        outs[2 * core + 1][...] = dot(hidden, scaled).astype(outs[2 * core + 1].dtype)
+        outs[core][0] = dot(rows, back_pre).astype(outs[core].dtype)
+        outs[core][1] = dot(hidden, scaled).astype(outs[core].dtype)
+
+
+def order_body(n_line, place, *refs):
+    pieces, out = refs[:n_line], refs[n_line]
+    tok_rows = pieces[0].shape[0]
+    for back in range(n_line):
+        z = lax.rem(place[0] + n_line - back, n_line)
+        out[pl.ds(pl.multiple_of(z * tok_rows, tok_rows), tok_rows), :] = pieces[back][...].astype(out.dtype)
 
 
 def down_grad_body(n_line, place, *refs):
@@ -196,34 +219,32 @@
     downs = [down_weight] + [turn(down_weight, n_line, back) for back in range(1, n_line)]
 
     gate_rows = -(-n_experts // 16) * 16
-    prepare = call(
-        functools.partial(prepare_body, n_line, block),
-        [shape((tok_rows, n_line * block), narrow)] * 4 + [shape((tok_rows + gate_rows, latent_width), narrow)],
-        "prepare",
-        nbytes=3 * tok_rows * width * 2,
-    )
-    *columns, payload = prepare(place, tokens, routes.T, gate_levels.T, latent_grad)
+    columns = call(
+        functools.partial(columns_body, n_line, block),
+        [shape((tok_rows, n_line * block), narrow)] * 2 + [shape((2, tok_rows, n_line * block), narrow)],
+        "columns",
+        scratch=[pltpu.SemaphoreType.DMA((4 * n_line,))],
+        outside=1,
+    )(place, tokens)
+    (payload,) = call(payload_body, [shape((tok_rows + gate_rows, latent_width), narrow)], "payload")(
+        place, routes.T, gate_levels.T, latent_grad
+    )
     own = [expert_in[0], expert_out[0]]
     side_in = swap(own[0], n_line, 0, 1)
-    near_tokens = columns[:1] + [
-        swap(after(columns[core * 2 + side], side_in), n_line, core, side)
-        for core, side in ((0, 1), (1, 0), (1, 1))
-    ]
-    payloads = [payload] + [None] * (n_line - 1)
-    payloads[1] = turn(after(payload, *downs[1:]), n_line, 1)
-    near_tokens[0] = after(near_tokens[0], payloads[1])
+    across = swap(columns[2], n_line, 0, 1)
+    near_tokens = [columns[0], across[0], swap(after(columns[1], across), n_line, 1, 0), swap(across[1], n_line, 1, 0)]
+    payloads = [payload, turn(after(payload, *downs[1:]), n_line, 1)]
 
     project = call(
         functools.partial(project_body, n_line),
         [shape((2, tok_rows, latent_width), wide)] * 2 + [shape((n_line * block, latent_width), narrow)],
         "project",
-        flops=2 * 4 * tok_rows * n_line * block * latent_width,
-    )
-    keep, send, down = project(place, *near_tokens, *downs)
-    half = keep + swap(send, n_line, 1, 0)
-    for back in range(2, n_line):
-        payloads[back] = turn(after(payload, half), n_line, back)
-    latent = (half[0] + after(swap(half[1], n_line, 0, 1), *payloads[2:])).astype(narrow)
+    )
+    keep, send, down = project(after(place, side_in), *near_tokens, *downs)
+    half = keep + after(swap(send, n_line, 1, 0), payloads[1])
+    payloads += [turn(after(payload, half), n_line, back) for back in range(2, n_line)]
+    core_in = [swap(after(w, half), n_line, 1, 0) for w in (own[0], side_in)]
+    latent = (half[0] + after(swap(half[1], n_line, 0, 1), *core_in, *payloads[2:])).astype(narrow)
     ends = [1, n_line - 1]
     middle = list(range(2, n_line - 1))
     groups = [ends, [0], middle]
@@ -234,22 +255,24 @@
     for back in middle:
         rows[back] = turn(after(latent, *end_rows), n_line, back)
 
-    side_out = after(swap(after(own[1], latent), n_line, 0, 1), *end_rows)
+    side_out = swap(after(own[1], latent), n_line, 0, 1)
+    core_out = [swap(after(own[1], latent), n_line, 1, 0), swap(after(side_out, *end_rows), n_line, 1, 0)]
+    weights = [own[0], own[1], side_in, side_out, core_in[0], core_out[0], core_in[1], core_out[1]]
     side_down = swap(after(down, side_out), n_line, 0, 1)
-    near = own + [side_in, side_out]
     all_down = [down, side_down] + [swap(d, n_line, 1, 0) for d in (down, side_down)]
-    weights = near + [swap(w, n_line, 1, 0) for w in near]
 
     outs_of, deltas_of, saved = [None] * n_line, [None] * n_line, []
     for group in groups:
         count = len(group)
         kind = narrow if group[0] else wide
+        if group == middle:
+            rows[group[0]] = after(rows[group[0]], deltas_of[0])
+        if not group[0]:
+            rows[0] = after(latent, deltas_of[1])
         values = call(
             functools.partial(expert_body, count),
             [rows_of(kind)] * (2 * count) + [shape((4, count * tok_rows, hidden_width), narrow)] * 3,
             "experts",
-            flops=4 * 2 * 4 * count * tok_rows * latent_width * hidden_width,
-            nbytes=8 * latent_width * hidden_width * 2,
         )(place, *(rows[i] for i in group), *(payloads[i] for i in group), *weights)
         for i, back in enumerate(group):
             outs_of[back], deltas_of[back] = values[i], values[count + i]
@@ -261,53 +284,56 @@
     delta_lines = [home(value, back) for back, value in enumerate(deltas_of)]
 
     def weight_grads(side, *earlier):
-        sizes = [(latent_width, hidden_width), (hidden_width, latent_width)]
-        values = call(
+        mine, other = call(
             functools.partial(weight_grad_body, side, n_line, len(groups)),
-            [shape(size, kind) for kind in (wide, narrow) for size in sizes],
+            [shape((2, latent_width, hidden_width), kind) for kind in (wide, narrow)],
             "weight_grads",
-            flops=2 * 2 * 2 * n_line * tok_rows * latent_width * hidden_width,
         )(
             after(place, *earlier),
             *(rows[i] for group in groups for i in group),
             *(value for values in saved for value in values),
         )
-        return [mine + swap(other, n_line, 1, 0).astype(wide) for mine, other in zip(values[:2], values[2:])]
-
-    far_in, far_out = (
-        value.astype(narrow) for value in weight_grads(1, *(delta_lines[back] for back in ends))
-    )
-    delta_lines = [after(line, far_in, *all_down) for line in delta_lines]
+        return mine, swap(other, n_line, 1, 0)
+
+    (sums,) = call(
+        functools.partial(order_body, n_line),
+        [shape((n_line * tok_rows, latent_width), narrow)],
+        "order",
+    )(place, *outs_of)
+    first_lines = [delta_lines[back] for back in ends]
+    mine, other = weight_grads(1, side_down, sums, *first_lines)
+    near_mine, near_other = weight_grads(0, mine)
+    far_sums = [(mine[i] + other[i].astype(wide)).astype(narrow) for i in range(2)]
+    delta_lines = [after(line, near_mine, *far_sums) for line in delta_lines]
     delta = sum(line.astype(wide) for line in delta_lines).astype(narrow)
     side_delta = swap(delta, n_line, 0, 1)
-    out_lines = [outs_of[0]] + [None] * (n_line - 1)
-    for back in ends:
-        out_lines[back] = home(after(outs_of[back], delta), back)
-    near_in, near_out = weight_grads(0, *(out_lines[back] for back in ends))
-    far_out = swap(far_out, n_line, 0, 1)
-    grad_out = near_out + far_out.astype(wide)
-    far_in = swap(after(far_in, side_delta), n_line, 0, 1)
-    grad_in = near_in + far_in.astype(wide)
+    latent_out = lax.psum_scatter(
+        sums,
+        plane,
+        scatter_dimension=0,
+        axis_index_groups=[[z * 4 + i for z in range(n_line)] for i in range(4)],
+        tiled=True,
+    )
+    far_in = swap(after(far_sums[0], delta), n_line, 0, 1)
     deltas = [delta, side_delta, swap(delta, n_line, 1, 0), swap(side_delta, n_line, 1, 0)]
     blocks = call(
         functools.partial(down_grad_body, n_line),
         [shape((block, latent_width), wide)] + [shape((block, latent_width), narrow)] * (n_line - 1),
         "down_grad",
-        flops=2 * 4 * tok_rows * n_line * block * latent_width,
-    )(place, *near_tokens, *deltas)
-    sent = [after(value, far_out, *(out_lines[back] for back in ends)) for value in blocks]
+    )(after(place, near_other, *all_down[2:]), *near_tokens, *deltas)
+    far_out = swap(after(far_sums[1], far_in, blocks[1]), n_line, 0, 1)
+    grad_in, grad_out = (
+        (near_mine[i] + near_other[i].astype(wide) + far.astype(wide)).astype(narrow)
+        for i, far in enumerate((far_in, far_out))
+    )
     (grad_tokens,) = call(
         functools.partial(token_grad_body, n_line, block),
         [shape((tok_rows, width), narrow)],
         "token_grad",
-        flops=2 * 4 * tok_rows * n_line * block * latent_width,
-    )(place, after(delta, blocks[1]), *all_down)
-    blocks = [blocks[0]] + [home(sent[back], back) for back in range(1, n_line)]
-    for back in middle:
-        out_lines[back] = home(after(outs_of[back], *(out_lines[end] for end in ends)), back)
-    grad_down = sum(after(value, far_in).astype(wide) for value in blocks)
-    latent_out = sum(line.astype(wide) for line in out_lines).astype(narrow)
-    return (latent_out, grad_tokens, grad_down, grad_in.astype(narrow)[None], grad_out.astype(narrow)[None])
+    )(place, after(delta, blocks[1], far_in, latent_out), *all_down)
+    blocks = [blocks[0]] + [home(blocks[back], back) for back in range(1, n_line)]
+    grad_down = sum(after(value, grad_tokens).astype(wide) for value in blocks)
+    return (latent_out, grad_tokens, grad_down, grad_in[None], grad_out[None])
 
 
 def slot_table(routes, capacity):

time: 120 us -> 168 us (1.40)
  local copies, waits for them, and re-layouts: 2.68 us -> 27.1 us
  between operations: 0.82 us -> 14.4 us
  waiting for transfers between devices: 46.7 us -> 55.8 us
  starting transfers between devices: 47.6 us -> 39.3 us
  Pallas kernels: 17.5 us -> 21.9 us
  other arithmetic: 4.02 us -> 8.17 us
    unnamed x14 -> x106, local copies, waits for them, and re-layouts: 2.58 us -> 27 us
    ppermute x23 -> x21, waiting for transfers between devices: 10.2 us -> 28.9 us  [swap(): lax.ppermute(value, plane, device_pairs(n_line, lambda z, x, c: (z, x ^ s...]
    ppermute x18 -> x15, waiting for transfers between devices: 36.4 us -> 26.8 us  [turn(): lax.ppermute(value, plane, device_pairs(n_line, lambda z, x, c: ((z + by)...]
    ppermute x18 -> x15, starting transfers between devices: 32.8 us -> 27.2 us  [turn(): lax.ppermute(value, plane, device_pairs(n_line, lambda z, x, c: ((z + by)...]
    pallas_call x9 -> x11, Pallas kernels: 17.5 us -> 21.9 us  [run(): pl.pallas_call(body, out_shape=outs, in_specs=[pl.BlockSpec(memory_space=...]
    ppermute x23 -> x21, starting transfers between devices: 14.8 us -> 12 us  [swap(): lax.ppermute(value, plane, device_pairs(n_line, lambda z, x, c: (z, x ^ s...]
    convert_element_type x4 -> x2, other arithmetic: 1.09 us -> 2.83 us  [the longest x1 2.79 us: all_rows(): (mine[i] + other[i].astype(wide)).astype(narrow)]
  transfers between devices with their start and end apart: 41 -> 37, of which waited for: 18 -> 12; matrix products, arithmetic and copies ran while one was open for 3% -> 3% of each run, Pallas kernels for 14% -> 11%
where the time goes in v5:
time: 168 us; the launch traced here: 167 us
  waiting for transfers between devices  55.8 us (33%)
  starting transfers between devices  39.3 us (23%)
  local copies, waits for them, and re-layouts  27.1 us (16%)
  Pallas kernels  21.9 us (13%)
  between operations  14.4 us (9%)
  other arithmetic  8.17 us (5%)
    ppermute x21, waiting for transfers between devices, swap(): lax.ppermute(value, plane, device_pairs(n_line, lambda z, x, c: (z, x ^ s...  28.9 us
    ppermute x15, starting transfers between devices, turn(): lax.ppermute(value, plane, device_pairs(n_line, lambda z, x, c: ((z + by)...  27.2 us
    unnamed x106, local copies, waits for them, and re-layouts  27 us
    ppermute x15, waiting for transfers between devices, turn(): lax.ppermute(value, plane, device_pairs(n_line, lambda z, x, c: ((z + by)...  26.8 us
    pallas_call x11, Pallas kernels, run(): pl.pallas_call(body, out_shape=outs, in_specs=[pl.BlockSpec(memory_space=...  21.9 us
    ppermute x21, starting transfers between devices, swap(): lax.ppermute(value, plane, device_pairs(n_line, lambda z, x, c: (z, x ^ s...  12 us
  transfers between devices with their start and end apart: 37, of which 12 were waited for; matrix products, arithmetic and copies ran while one was open for 3% of the time, Pallas kernels for 11%

profile of v5, /device:TPU:0, one launch (start us, length us, event | category | flops | bytes accessed | tf_op | source)
XLA Modules:
  0.0 166.7 jit_solution(3839873566358892605)
XLA Ops:
  7.2 3.0 %collective-permute-start = (bf16[512,512]{1,0:T(8,128)(2,1)}, bf16[512,512]{1,0:T(8,128)(2,1)S(1)}, u32[]{:S(2)}, u32[]{:S(2)}) collective-permute-start(bf16[512,512]{1,0:T(8,128)(2,1)} %bitcast.43), channel_id=1, source_target_pairs={{0,2},{1,3},{2,0},{3,1},{4,6},{5,7},{6,4},{7,5},{8,10},{9,11},{10,... | collective-permute-start | bytes 1572872 | tf_op jit(solution)/shard_map/ppermute | solution.py:33
  12.4 2.1 %collective-permute-start.4 = (bf16[128,512]{1,0:T(8,128)(2,1)}, bf16[128,512]{1,0:T(8,128)(2,1)S(1)}, u32[]{:S(2)}, u32[]{:S(2)}) collective-permute-start(bf16[128,512]{1,0:T(8,128)(2,1)} %refs_4_.1), channel_id=1, source_target_pairs={{0,4},{1,5},{2,6},{3,7},{4,8},{5,9},{6,10},{7,11},{8,12},{9,13},{1... | collective-permute-start | bytes 393224 | tf_op jit(solution)/shard_map/ppermute | solution.py:29
  14.4 2.6 %collective-permute-start.5 = (bf16[128,512]{1,0:T(8,128)(2,1)}, bf16[128,512]{1,0:T(8,128)(2,1)S(1)}, u32[]{:S(2)}, u32[]{:S(2)}) collective-permute-start(bf16[128,512]{1,0:T(8,128)(2,1)} %refs_4_.1), channel_id=1, source_target_pairs={{0,8},{1,9},{2,10},{3,11},{4,12},{5,13},{6,14},{7,15},{8,0},{9,1},... | collective-permute-start | bytes 393224 | tf_op jit(solution)/shard_map/ppermute | solution.py:29
  18.4 9.6 %collective-permute-done.1 = bf16[2,128,512]{2,1,0:T(8,128)(2,1)S(1)} collective-permute-done((bf16[2,128,512]{2,1,0:T(8,128)(2,1)S(1)}, bf16[2,128,512]{2,1,0:T(8,128)(2,1)S(1)}, u32[]{:S(2)}, u32[]{:S(2)}) %collective-permute-start.1) | collective-permute-done | bytes 262176 | tf_op jit(solution)/shard_map/ppermute | solution.py:33
  32.9 1.9 %collective-permute-start.8 = (bf16[144,512]{1,0:T(8,128)(2,1)S(1)}, bf16[144,512]{1,0:T(8,128)(2,1)S(1)}, u32[]{:S(2)}, u32[]{:S(2)}) collective-permute-start(bf16[144,512]{1,0:T(8,128)(2,1)S(1)} %payload.1.refs_1_), channel_id=1, source_target_pairs={{0,4},{1,5},{2,6},{3,7},{4,8},{5,9},{6,10},{7,11},{8,12},{9,13},{1... | collective-permute-start | bytes 442376 | tf_op jit(solution)/shard_map/ppermute | solution.py:29
  34.8 6.2 %collective-permute-done.8.refs_2_ = bf16[144,512]{1,0:T(8,128)(2,1)S(1)} collective-permute-done((bf16[144,512]{1,0:T(8,128)(2,1)S(1)}, bf16[144,512]{1,0:T(8,128)(2,1)S(1)}, u32[]{:S(2)}, u32[]{:S(2)}) %collective-permute-start.8) | collective-permute-done | bytes 147488 | tf_op jit(solution)/shard_map/ppermute | solution.py:29
  45.3 6.8 %collective-permute-done.12.refs_1_ = bf16[144,512]{1,0:T(8,128)(2,1)S(1)} collective-permute-done((bf16[144,512]{1,0:T(8,128)(2,1)S(1)}, bf16[144,512]{1,0:T(8,128)(2,1)S(1)}, u32[]{:S(2)}, u32[]{:S(2)}) %collective-permute-start.12) | collective-permute-done | bytes 147488 | tf_op jit(solution)/shard_map/ppermute | solution.py:29
  53.0 3.4 %collective-permute-start.14 = (bf16[128,512]{1,0:T(8,128)(2,1)S(1)}, bf16[128,512]{1,0:T(8,128)(2,1)S(1)}, u32[]{:S(2)}, u32[]{:S(2)}) collective-permute-start(bf16[128,512]{1,0:T(8,128)(2,1)S(1)} %fusion.7.refs_0_.refs_2_), channel_id=1, source_target_pairs={{0,4},{1,5},{2,6},{3,7},{4,8},{5,9},{6,10},{7,11},{8,12},{9,13},{1... | collective-permute-start | bytes 393224 | tf_op jit(solution)/shard_map/ppermute | solution.py:29
  56.4 1.9 %collective-permute-start.15 = (bf16[128,512]{1,0:T(8,128)(2,1)S(1)}, bf16[128,512]{1,0:T(8,128)(2,1)S(1)}, u32[]{:S(2)}, u32[]{:S(2)}) collective-permute-start(bf16[128,512]{1,0:T(8,128)(2,1)S(1)} %fusion.7.refs_0_.refs_2_), channel_id=1, source_target_pairs={{0,12},{1,13},{2,14},{3,15},{4,0},{5,1},{6,2},{7,3},{8,4},{9,5},{1... | collective-permute-start | bytes 393224 | tf_op jit(solution)/shard_map/ppermute | solution.py:29
  58.3 4.3 %collective-permute-done.14.refs_0_ = bf16[128,512]{1,0:T(8,128)(2,1)S(1)} collective-permute-done((bf16[128,512]{1,0:T(8,128)(2,1)S(1)}, bf16[128,512]{1,0:T(8,128)(2,1)S(1)}, u32[]{:S(2)}, u32[]{:S(2)}) %collective-permute-start.14) | collective-permute-done | bytes 131104 | tf_op jit(solution)/shard_map/ppermute | solution.py:29
  64.1 1.9 %collective-permute-done.16.refs_7_.refs_5_ = bf16[512,512]{1,0:T(8,128)(2,1)S(1)} collective-permute-done((bf16[512,512]{1,0:T(8,128)(2,1)S(1)}, bf16[512,512]{1,0:T(8,128)(2,1)S(1)}, u32[]{:S(2)}, u32[]{:S(2)}) %collective-permute-start.16) | collective-permute-done | bytes 524320 | tf_op jit(solution)/shard_map/ppermute | solution.py:33
  66.5 2.7 %collective-permute-start.19 = (bf16[128,512]{1,0:T(8,128)(2,1)S(1)}, bf16[128,512]{1,0:T(8,128)(2,1)S(1)}, u32[]{:S(2)}, u32[]{:S(2)}) collective-permute-start(bf16[128,512]{1,0:T(8,128)(2,1)S(1)} %fusion.7.refs_0_.refs_2_), channel_id=1, source_target_pairs={{0,8},{1,9},{2,10},{3,11},{4,12},{5,13},{6,14},{7,15},{8,0},{9,1},... | collective-permute-start | bytes 393224 | tf_op jit(solution)/shard_map/ppermute | solution.py:29
  69.2 4.0 %experts.3 = (bf16[128,512]{1,0:T(8,128)(2,1)S(1)}, bf16[128,512]{1,0:T(8,128)(2,1)S(1)}, bf16[128,512]{1,0:T(8,128)(2,1)}, bf16[128,512]{1,0:T(8,128)(2,1)}, bf...) custom-call(s32[7]{0:T(128)S(1)} %stack.31.place, ...), custom_call_target="tpu_custom_call" | custom-call | tf_op jit(solution)/shard_map/experts/pallas_call | solution.py:45
  73.2 4.3 %collective-permute-start.21 = (bf16[128,512]{1,0:T(8,128)(2,1)}, bf16[128,512]{1,0:T(8,128)(2,1)}, u32[]{:S(2)}, u32[]{:S(2)}) collective-permute-start(bf16[128,512]{1,0:T(8,128)(2,1)} %get-tuple-element.79), channel_id=1, source_target_pairs={{0,12},{1,13},{2,14},{3,15},{4,0},{5,1},{6,2},{7,3},{8,4},{9,5},{1... | collective-permute-start | bytes 393224 | tf_op jit(solution)/shard_map/ppermute | solution.py:29
  77.5 2.6 %experts.4 = (f32[128,512]{1,0:T(8,128)S(1)}, f32[128,512]{1,0:T(8,128)S(1)}, bf16[4,128,512]{2,1,0:T(8,128)(2,1)S(1)}, bf16[4,128,512]{2,1,0:T(8,128)(2,1)S(1)}, bf16[4,128,512]{2,1,0:T(8,128)(2,1)S(1)}) custom-call(s32[7]{0:T(128)S(1)} %stack.31.place, bf16[128,512]{1,0:T(8,128)(2,1)S(1)} %fusion.7.refs_0_.refs_2_, bf16[144,512]{1,0:T(8,128)(2,1)S(1)} %payload.1.refs_1_, ...), custom_call_target="tpu_custom_call" | custom-call | tf_op jit(solution)/shard_map/experts/pallas_call | solution.py:45
  82.5 2.6 %experts.5 = (bf16[128,512]{1,0:T(8,128)(2,1)S(1)}, bf16[128,512]{1,0:T(8,128)(2,1)S(1)}, bf16[4,128,512]{2,1,0:T(8,128)(2,1)S(1)}, bf16[4,128,512]{2,1,0:T(8,128)(2,1)S(1)}, bf16[4,128,512]{2,1,0:T(8,128)(2,1)S(1)}) custom-call(s32[7]{0:T(128)S(1)} %stack.31.place, bf16[128,512]{1,0:T(8,128)(2,1)S(1)} %collective-permute-done.19.refs_0_.refs_3_, ...), custom_call_target="tpu_custom_call" | custom-call | tf_op jit(solution)/shard_map/experts/pallas_call | solution.py:45
  98.0 2.4 %weight_grads.2 = (f32[2,512,512]{2,1,0:T(8,128)S(1)}, bf16[2,512,512]{2,1,0:T(8,128)(2,1)}) custom-call(s32[7]{0:T(128)S(1)} %stack.31.place, bf16[128,512]{1,0:T(8,128)(2,1)S(1)} %collective-permute-done.14.refs_0_, bf16[128,512]{1,0:T(8,128)(2,1)S(1)} %collective-permute-done.15.refs_1_, bf16[128,512]{1,0:T(8,128)(2,1)S(1)} %fusion.7.refs_0_.refs_2_, ...), custom_call_target="tpu_custom_call" | custom-call | tf_op jit(solution)/shard_map/weight_grads/pallas_call | solution.py:45
  112.6 2.8 %fusion.3 = (bf16[512,512]{1,0:T(8,128)(2,1)}, bf16[512,512]{1,0:T(8,128)(2,1)S(1)}) fusion(f32[2,512,512]{2,1,0:T(8,128)S(1)} %copy-done.8, bf16[2,512,512]{2,1,0:T(8,128)(2,1)} %collective-permute-done.23), kind=kLoop, calls=%fused_computation.7 | loop fusion | flops 1572864 | bytes 4194304 | tf_op jit(solution)/shard_map/convert_element_type | solution.py:306
  118.6 15.1 %collective-permute-done.28.refs_5_ = bf16[128,512]{1,0:T(8,128)(2,1)S(1)} collective-permute-done((bf16[128,512]{1,0:T(8,128)(2,1)S(1)}, bf16[128,512]{1,0:T(8,128)(2,1)S(1)}, u32[]{:S(2)}, u32[]{:S(2)}) %collective-permute-start.28) | collective-permute-done | bytes 131104 | tf_op jit(solution)/shard_map/ppermute | solution.py:33
  135.0 1.9 %down_grad.1 = (f32[128,512]{1,0:T(8,128)S(1)}, bf16[128,512]{1,0:T(8,128)(2,1)}, bf16[128,512]{1,0:T(8,128)(2,1)}, bf16[128,512]{1,0:T(8,128)(2,1)}) custom-call(s32[7]{0:T(128)S(1)} %stack.31.place, bf16[128,512]{1,0:T(8,128)(2,1)S(1)} %copy-done.37, bf16[128,512]{1,0:T(8,128)(2,1)S(1)} %copy-done.32, bf16[128,512]{1,0:T(8,128)(2,1)S(1)} %copy-done.39, ...), custom_call_target="tpu_custom_call" | custom-call | tf_op jit(solution)/shard_map/down_grad/pallas_call | solution.py:45
  139.3 2.9 %collective-permute-start.32 = (bf16[128,512]{1,0:T(8,128)(2,1)}, bf16[128,512]{1,0:T(8,128)(2,1)}, u32[]{:S(2)}, u32[]{:S(2)}) collective-permute-start(bf16[128,512]{1,0:T(8,128)(2,1)} %get-tuple-element.112), channel_id=1, source_target_pairs={{0,12},{1,13},{2,14},{3,15},{4,0},{5,1},{6,2},{7,3},{8,4},{9,5},{1... | collective-permute-start | bytes 393224 | tf_op jit(solution)/shard_map/ppermute | solution.py:29
  144.6 3.1 %token_grad.1 = bf16[128,2048]{1,0:T(8,128)(2,1)} custom-call(s32[7]{0:T(128)S(1)} %stack.31.place, bf16[128,512]{1,0:T(8,128)(2,1)S(1)} %add_convert_fusion.2.refs_4_.delta, bf16[512,512]{1,0:T(8,128)(2,1)} %get-tuple-element.89.refs_0_, bf16[512,512]{1,0:T(8,128)(2,1)} %collective-permute-done.20.refs_1_, ...), custom_call_target="tpu_custom_call" | custom-call | tf_op jit(solution)/shard_map/token_grad/pallas_call | solution.py:45
  147.8 7.8 %collective-permute-done.33 = bf16[128,512]{1,0:T(8,128)(2,1)} collective-permute-done((bf16[128,512]{1,0:T(8,128)(2,1)}, bf16[128,512]{1,0:T(8,128)(2,1)}, u32[]{:S(2)}, u32[]{:S(2)}) %collective-permute-start.33) | collective-permute-done | bytes 131104 | tf_op jit(solution)/shard_map/ppermute | solution.py:29
  157.4 2.4 %fusion.5 = (bf16[1,512,512]{2,1,0:T(8,128)(2,1)}, bf16[1,512,512]{2,1,0:T(8,128)(2,1)}) fusion(bf16[512,512]{1,0:T(8,128)(2,1)} %collective-permute-done.35, f32[2,512,512]{2,1,0:T(8,128)S(1)} %copy-done.6, bf16[2,512,512]{2,1,0:T(8,128)(2,1)S(1)} %copy-done.50, bf16[512,512]{1,0:T(8,128)(2,1)S(1)} %copy-done.52), kind=kLoop, calls=%fused_computation.9 | loop fusion | flops 2621440 | bytes 5242880 | tf_op jit(solution)/shard_map/broadcast_in_dim | solution.py:336
  (177 shorter events, 54.0 us)
Async XLA Ops:
  7.2 136.4 %reduce-scatter.2.cloned.1.call-start = ((), (), s32[]{:S(2)}) async-start(), calls=%async_computation.1 | async-start | bytes 655360 | tf_op jit(solution)/shard_map/reduce_scatter | solution.py:310
  7.2 20.8 %collective-permute-start = (bf16[512,512]{1,0:T(8,128)(2,1)}, bf16[512,512]{1,0:T(8,128)(2,1)S(1)}, u32[]{:S(2)}, u32[]{:S(2)}) collective-permute-start(bf16[512,512]{1,0:T(8,128)(2,1)} %bitcast.43), channel_id=1, source_target_pairs={{0,2},{1,3},{2,0},{3,1},{4,6},{5,7},{6,4},{7,5},{8,10},{9,11},{10,... | collective-permute-start | bytes 1572872 | tf_op jit(solution)/shard_map/ppermute | solution.py:33
  12.3 15.7 %collective-permute-start.1 = (bf16[2,128,512]{2,1,0:T(8,128)(2,1)S(1)}, bf16[2,128,512]{2,1,0:T(8,128)(2,1)S(1)}, u32[]{:S(2)}, u32[]{:S(2)}) collective-permute-start(bf16[2,128,512]{2,1,0:T(8,128)(2,1)S(1)} %get-tuple-element.66), channel_id=1, source_target_pairs={{0,2},{1,3},{2,0},{3,1},{4,6},{5,7},{6,4},{7,5},{8,10},{9,11},{10,... | collective-permute-start | bytes 786440 | tf_op jit(solution)/shard_map/ppermute | solution.py:33
  12.4 16.2 %collective-permute-start.4 = (bf16[128,512]{1,0:T(8,128)(2,1)}, bf16[128,512]{1,0:T(8,128)(2,1)S(1)}, u32[]{:S(2)}, u32[]{:S(2)}) collective-permute-start(bf16[128,512]{1,0:T(8,128)(2,1)} %refs_4_.1), channel_id=1, source_target_pairs={{0,4},{1,5},{2,6},{3,7},{4,8},{5,9},{6,10},{7,11},{8,12},{9,13},{1... | collective-permute-start | bytes 393224 | tf_op jit(solution)/shard_map/ppermute | solution.py:29
  14.4 14.2 %collective-permute-start.5 = (bf16[128,512]{1,0:T(8,128)(2,1)}, bf16[128,512]{1,0:T(8,128)(2,1)S(1)}, u32[]{:S(2)}, u32[]{:S(2)}) collective-permute-start(bf16[128,512]{1,0:T(8,128)(2,1)} %refs_4_.1), channel_id=1, source_target_pairs={{0,8},{1,9},{2,10},{3,11},{4,12},{5,13},{6,14},{7,15},{8,0},{9,1},... | collective-permute-start | bytes 393224 | tf_op jit(solution)/shard_map/ppermute | solution.py:29
  17.0 11.6 %collective-permute-start.6 = (bf16[128,512]{1,0:T(8,128)(2,1)}, bf16[128,512]{1,0:T(8,128)(2,1)S(1)}, u32[]{:S(2)}, u32[]{:S(2)}) collective-permute-start(bf16[128,512]{1,0:T(8,128)(2,1)} %refs_4_.1), channel_id=1, source_target_pairs={{0,12},{1,13},{2,14},{3,15},{4,0},{5,1},{6,2},{7,3},{8,4},{9,5},{1... | collective-permute-start | bytes 393224 | tf_op jit(solution)/shard_map/ppermute | solution.py:29
  41.0 11.3 %collective-permute-start.11 = (bf16[512,512]{1,0:T(8,128)(2,1)S(1)}, bf16[512,512]{1,0:T(8,128)(2,1)S(1)}, u32[]{:S(2)}, u32[]{:S(2)}) collective-permute-start(bf16[512,512]{1,0:T(8,128)(2,1)S(1)} %collective-permute-done.refs_6_.refs_4_), channel_id=1, source_target_pairs={{0,1},{1,0},{2,3},{3,2},{4,5},{5,4},{6,7},{7,6},{8,9},{9,8},{10,11... | collective-permute-start | bytes 1572872 | tf_op jit(solution)/shard_map/ppermute | solution.py:33
  41.1 11.2 %collective-permute-start.10 = (bf16[512,512]{1,0:T(8,128)(2,1)S(1)}, bf16[512,512]{1,0:T(8,128)(2,1)S(1)}, u32[]{:S(2)}, u32[]{:S(2)}) collective-permute-start(bf16[512,512]{1,0:T(8,128)(2,1)S(1)} %bitcast.44), channel_id=1, source_target_pairs={{0,1},{1,0},{2,3},{3,2},{4,5},{5,4},{6,7},{7,6},{8,9},{9,8},{10,11... | collective-permute-start | bytes 1572872 | tf_op jit(solution)/shard_map/ppermute | solution.py:33
  52.4 13.6 %collective-permute-start.16 = (bf16[512,512]{1,0:T(8,128)(2,1)S(1)}, bf16[512,512]{1,0:T(8,128)(2,1)S(1)}, u32[]{:S(2)}, u32[]{:S(2)}) collective-permute-start(bf16[512,512]{1,0:T(8,128)(2,1)S(1)} %bitcast.48), channel_id=1, source_target_pairs={{0,2},{1,3},{2,0},{3,1},{4,6},{5,7},{6,4},{7,5},{8,10},{9,11},{10,... | collective-permute-start | bytes 1572872 | tf_op jit(solution)/shard_map/ppermute | solution.py:33
  66.0 23.6 %collective-permute-start.20 = (bf16[512,512]{1,0:T(8,128)(2,1)}, bf16[512,512]{1,0:T(8,128)(2,1)}, u32[]{:S(2)}, u32[]{:S(2)}) collective-permute-start(bf16[512,512]{1,0:T(8,128)(2,1)} %get-tuple-element.89.refs_0_), channel_id=1, source_target_pairs={{0,2},{1,3},{2,0},{3,1},{4,6},{5,7},{6,4},{7,5},{8,10},{9,11},{10,... | collective-permute-start | bytes 1572872 | tf_op jit(solution)/shard_map/ppermute | solution.py:33
  66.5 16.0 %collective-permute-start.19 = (bf16[128,512]{1,0:T(8,128)(2,1)S(1)}, bf16[128,512]{1,0:T(8,128)(2,1)S(1)}, u32[]{:S(2)}, u32[]{:S(2)}) collective-permute-start(bf16[128,512]{1,0:T(8,128)(2,1)S(1)} %fusion.7.refs_0_.refs_2_), channel_id=1, source_target_pairs={{0,8},{1,9},{2,10},{3,11},{4,12},{5,13},{6,14},{7,15},{8,0},{9,1},... | collective-permute-start | bytes 393224 | tf_op jit(solution)/shard_map/ppermute | solution.py:29
  73.2 16.4 %collective-permute-start.21 = (bf16[128,512]{1,0:T(8,128)(2,1)}, bf16[128,512]{1,0:T(8,128)(2,1)}, u32[]{:S(2)}, u32[]{:S(2)}) collective-permute-start(bf16[128,512]{1,0:T(8,128)(2,1)} %get-tuple-element.79), channel_id=1, source_target_pairs={{0,12},{1,13},{2,14},{3,15},{4,0},{5,1},{6,2},{7,3},{8,4},{9,5},{1... | collective-permute-start | bytes 393224 | tf_op jit(solution)/shard_map/ppermute | solution.py:29
  77.4 12.2 %collective-permute-start.22 = (bf16[128,512]{1,0:T(8,128)(2,1)}, bf16[128,512]{1,0:T(8,128)(2,1)}, u32[]{:S(2)}, u32[]{:S(2)}) collective-permute-start(bf16[128,512]{1,0:T(8,128)(2,1)} %get-tuple-element.90), channel_id=1, source_target_pairs={{0,4},{1,5},{2,6},{3,7},{4,8},{5,9},{6,10},{7,11},{8,12},{9,13},{1... | collective-permute-start | bytes 393224 | tf_op jit(solution)/shard_map/ppermute | solution.py:29
  101.7 10.9 %collective-permute-start.23 = (bf16[2,512,512]{2,1,0:T(8,128)(2,1)}, bf16[2,512,512]{2,1,0:T(8,128)(2,1)}, u32[]{:S(2)}, u32[]{:S(2)}) collective-permute-start(bf16[2,512,512]{2,1,0:T(8,128)(2,1)} %get-tuple-element.104), channel_id=1, source_target_pairs={{0,1},{1,0},{2,3},{3,2},{4,5},{5,4},{6,7},{7,6},{8,9},{9,8},{10,11... | collective-permute-start | bytes 3145736 | tf_op jit(solution)/shard_map/ppermute | solution.py:33
  101.7 16.8 %collective-permute-start.26 = (bf16[512,512]{1,0:T(8,128)(2,1)}, bf16[512,512]{1,0:T(8,128)(2,1)}, u32[]{:S(2)}, u32[]{:S(2)}) collective-permute-start(bf16[512,512]{1,0:T(8,128)(2,1)} %get-tuple-element.89.refs_0_), channel_id=1, source_target_pairs={{0,1},{1,0},{2,3},{3,2},{4,5},{5,4},{6,7},{7,6},{8,9},{9,8},{10,11... | collective-permute-start | bytes 1572872 | tf_op jit(solution)/shard_map/ppermute | solution.py:33
  102.3 13.2 %collective-permute-start.24 = (bf16[128,512]{1,0:T(8,128)(2,1)}, bf16[128,512]{1,0:T(8,128)(2,1)S(1)}, u32[]{:S(2)}, u32[]{:S(2)}) collective-permute-start(bf16[128,512]{1,0:T(8,128)(2,1)} %copy-done.48), channel_id=1, source_target_pairs={{0,8},{1,9},{2,10},{3,11},{4,12},{5,13},{6,14},{7,15},{8,0},{9,1},... | collective-permute-start | bytes 393224 | tf_op jit(solution)/shard_map/ppermute | solution.py:29
  103.0 30.7 %collective-permute-start.27 = (bf16[512,512]{1,0:T(8,128)(2,1)}, bf16[512,512]{1,0:T(8,128)(2,1)S(1)}, u32[]{:S(2)}, u32[]{:S(2)}) collective-permute-start(bf16[512,512]{1,0:T(8,128)(2,1)} %collective-permute-done.20.refs_1_), channel_id=1, source_target_pairs={{0,1},{1,0},{2,3},{3,2},{4,5},{5,4},{6,7},{7,6},{8,9},{9,8},{10,11... | collective-permute-start | bytes 1572872 | tf_op jit(solution)/shard_map/ppermute | solution.py:33
  112.1 21.6 %collective-permute-start.25 = (bf16[2,512,512]{2,1,0:T(8,128)(2,1)S(1)}, bf16[2,512,512]{2,1,0:T(8,128)(2,1)S(1)}, u32[]{:S(2)}, u32[]{:S(2)}) collective-permute-start(bf16[2,512,512]{2,1,0:T(8,128)(2,1)S(1)} %get-tuple-element.110), channel_id=1, source_target_pairs={{0,1},{1,0},{2,3},{3,2},{4,5},{5,4},{6,7},{7,6},{8,9},{9,8},{10,11... | collective-permute-start | bytes 3145736 | tf_op jit(solution)/shard_map/ppermute | solution.py:33
  116.5 20.5 %collective-permute-start.31 = (bf16[512,512]{1,0:T(8,128)(2,1)S(1)}, bf16[512,512]{1,0:T(8,128)(2,1)S(1)}, u32[]{:S(2)}, u32[]{:S(2)}) collective-permute-start(bf16[512,512]{1,0:T(8,128)(2,1)S(1)} %get-tuple-element.113), channel_id=1, source_target_pairs={{0,2},{1,3},{2,0},{3,1},{4,6},{5,7},{6,4},{7,5},{8,10},{9,11},{10,... | collective-permute-start | bytes 1572872 | tf_op jit(solution)/shard_map/ppermute | solution.py:33
  118.0 15.7 %collective-permute-start.28 = (bf16[128,512]{1,0:T(8,128)(2,1)S(1)}, bf16[128,512]{1,0:T(8,128)(2,1)S(1)}, u32[]{:S(2)}, u32[]{:S(2)}) collective-permute-start(bf16[128,512]{1,0:T(8,128)(2,1)S(1)} %add_convert_fusion.2.refs_4_.delta), channel_id=1, source_target_pairs={{0,2},{1,3},{2,0},{3,1},{4,6},{5,7},{6,4},{7,5},{8,10},{9,11},{10,... | collective-permute-start | bytes 393224 | tf_op jit(solution)/shard_map/ppermute | solution.py:33
  118.6 15.1 %collective-permute-start.29 = (bf16[128,512]{1,0:T(8,128)(2,1)S(1)}, bf16[128,512]{1,0:T(8,128)(2,1)S(1)}, u32[]{:S(2)}, u32[]{:S(2)}) collective-permute-start(bf16[128,512]{1,0:T(8,128)(2,1)S(1)} %add_convert_fusion.2.refs_4_.delta), channel_id=1, source_target_pairs={{0,1},{1,0},{2,3},{3,2},{4,5},{5,4},{6,7},{7,6},{8,9},{9,8},{10,11... | collective-permute-start | bytes 393224 | tf_op jit(solution)/shard_map/ppermute | solution.py:33
  137.8 19.6 %collective-permute-start.35 = (bf16[512,512]{1,0:T(8,128)(2,1)}, bf16[512,512]{1,0:T(8,128)(2,1)}, u32[]{:S(2)}, u32[]{:S(2)}) collective-permute-start(bf16[512,512]{1,0:T(8,128)(2,1)} %get-tuple-element.122), channel_id=1, source_target_pairs={{0,2},{1,3},{2,0},{3,1},{4,6},{5,7},{6,4},{7,5},{8,10},{9,11},{10,... | collective-permute-start | bytes 1572872 | tf_op jit(solution)/shard_map/ppermute | solution.py:33
  142.2 13.4 %collective-permute-start.33 = (bf16[128,512]{1,0:T(8,128)(2,1)}, bf16[128,512]{1,0:T(8,128)(2,1)}, u32[]{:S(2)}, u32[]{:S(2)}) collective-permute-start(bf16[128,512]{1,0:T(8,128)(2,1)} %get-tuple-element.118), channel_id=1, source_target_pairs={{0,8},{1,9},{2,10},{3,11},{4,12},{5,13},{6,14},{7,15},{8,0},{9,1},... | collective-permute-start | bytes 393224 | tf_op jit(solution)/shard_map/ppermute | solution.py:29
  143.6 12.0 %collective-permute-start.34 = (bf16[128,512]{1,0:T(8,128)(2,1)}, bf16[128,512]{1,0:T(8,128)(2,1)}, u32[]{:S(2)}, u32[]{:S(2)}) collective-permute-start(bf16[128,512]{1,0:T(8,128)(2,1)} %get-tuple-element.120), channel_id=1, source_target_pairs={{0,4},{1,5},{2,6},{3,7},{4,8},{5,9},{6,10},{7,11},{8,12},{9,13},{1... | collective-permute-start | bytes 393224 | tf_op jit(solution)/shard_map/ppermute | solution.py:29
  (66 other events, 495.1 us)
Sparse Core Ops, SparseCore 0:
  102.4 22.0 reduce-scatter.1

commit v6 on v5

--- a/solution.py
+++ b/solution.py
@@ -115,8 +115,9 @@
 
 def expert_body(count, place, *refs):
     rows_in, payloads = refs[:count], refs[count : 2 * count]
-    weights = refs[2 * count : 2 * count + 8]
-    outs = refs[2 * count + 8 :]
+    own, core, *sides = refs[2 * count : 2 * count + 6]
+    weights = (own.at[0], own.at[1], sides[0], sides[1], core.at[0], core.at[1], sides[2], sides[3])
+    outs = refs[2 * count + 6 :]
     combined, deltas = outs[:count], outs[count : 2 * count]
     hiddens, scaleds, back_pres = outs[2 * count :]
     tok_rows, width = rows_in[0].shape
@@ -150,32 +151,30 @@
             deltas[i][...] = delta_sum[part].astype(deltas[i].dtype)
 
 
-def weight_grad_body(side, n_rows, n_sets, place, *refs):
+def weight_grad_body(n_rows, n_sets, place, *refs):
     rows_in = refs[:n_rows]
     sets = [refs[n_rows + 3 * i : n_rows + 3 * i + 3] for i in range(n_sets)]
-    outs = refs[n_rows + 3 * n_sets :]
+    near, far, other = refs[n_rows + 3 * n_sets :]
     dot = functools.partial(lax.dot_general, dimension_numbers=contract_first, preferred_element_type=wide)
     rows = jnp.concatenate([r[...] for r in rows_in], axis=0)
     for core in (1, 0):
-        hidden, scaled, back_pre = (
-            jnp.concatenate([values[i][core * 2 + side] for values in sets], axis=0) for i in range(3)
-        )
-        outs[core][0] = dot(rows, back_pre).astype(outs[core].dtype)
-        outs[core][1] = dot(hidden, scaled).astype(outs[core].dtype)
-
-
-def order_body(n_line, place, *refs):
-    pieces, out = refs[:n_line], refs[n_line]
-    tok_rows = pieces[0].shape[0]
-    for back in range(n_line):
-        z = lax.rem(place[0] + n_line - back, n_line)
-        out[pl.ds(pl.multiple_of(z * tok_rows, tok_rows), tok_rows), :] = pieces[back][...].astype(out.dtype)
+        for side in (1, 0):
+            hidden, scaled, back_pre = (
+                jnp.concatenate([values[i][core * 2 + side] for values in sets], axis=0) for i in range(3)
+            )
+            grad_in, grad_out = dot(rows, back_pre), dot(hidden, scaled)
+            if core:
+                other[2 * side] = grad_in.astype(narrow)
+                other[2 * side + 1] = grad_out.astype(narrow)
+            else:
+                own = far if side else near
+                own[0], own[1] = grad_in, grad_out
 
 
 def down_grad_body(n_line, place, *refs):
-    pieces, deltas, blocks = refs[:4], refs[4:8], refs[8:]
+    pieces, deltas, core_deltas, blocks = refs[:4], refs[4:6], refs[6], refs[7:]
     tokens = jnp.concatenate([p[...] for p in pieces], axis=0)
-    delta = jnp.concatenate([d[...] for d in deltas], axis=0)
+    delta = jnp.concatenate([d[...] for d in deltas] + [core_deltas[0], core_deltas[1]], axis=0)
     part = lax.dot_general(tokens, delta, contract_first, preferred_element_type=wide)
     block = blocks[0].shape[0]
     for z in range(n_line):
@@ -186,17 +185,21 @@
                 blocks[back][...] = part[z * block : (z + 1) * block].astype(blocks[back].dtype)
 
 
-def token_grad_body(n_line, block, place, delta, *refs):
-    downs, out = refs[:4], refs[4]
-    for core in range(2):
+def token_grad_body(place, delta, core_deltas, down, side_down, own, other):
+    for rows, out in ((core_deltas[0], other), (delta[...], own)):
+        for side, weight in enumerate((down, side_down)):
+            out[side] = lax.dot_general(
+                rows, weight[...], contract_last, preferred_element_type=wide
+            ).astype(narrow)
+
+
+def arrange_body(n_line, block, place, own, other, out):
+    for core, pieces in enumerate((own, other)):
         for side in range(2):
             owner = (place[1] ^ side) * 2 + (place[2] ^ core)
-            part = lax.dot_general(
-                delta[...], downs[core * 2 + side][...], contract_last, preferred_element_type=wide
-            ).astype(narrow)
             for z in range(n_line):
                 start = pl.multiple_of((z * 4 + owner) * block, block)
-                out[:, pl.ds(start, block)] = part[:, z * block : (z + 1) * block]
+                out[:, pl.ds(start, block)] = pieces[side, :, z * block : (z + 1) * block]
 
 
 def all_rows(tokens, routes, gate_levels, latent_grad, down_weight, expert_in, expert_out):
@@ -229,46 +232,40 @@
     (payload,) = call(payload_body, [shape((tok_rows + gate_rows, latent_width), narrow)], "payload")(
         place, routes.T, gate_levels.T, latent_grad
     )
-    own = [expert_in[0], expert_out[0]]
-    side_in = swap(own[0], n_line, 0, 1)
     across = swap(columns[2], n_line, 0, 1)
     near_tokens = [columns[0], across[0], swap(after(columns[1], across), n_line, 1, 0), swap(across[1], n_line, 1, 0)]
-    payloads = [payload, turn(after(payload, *downs[1:]), n_line, 1)]
+    side_in = swap(after(expert_in[0], across, near_tokens[2]), n_line, 0, 1)
 
     project = call(
         functools.partial(project_body, n_line),
         [shape((2, tok_rows, latent_width), wide)] * 2 + [shape((n_line * block, latent_width), narrow)],
         "project",
     )
-    keep, send, down = project(after(place, side_in), *near_tokens, *downs)
-    half = keep + after(swap(send, n_line, 1, 0), payloads[1])
-    payloads += [turn(after(payload, half), n_line, back) for back in range(2, n_line)]
-    core_in = [swap(after(w, half), n_line, 1, 0) for w in (own[0], side_in)]
-    latent = (half[0] + after(swap(half[1], n_line, 0, 1), *core_in, *payloads[2:])).astype(narrow)
+    keep, send, down = project(place, *near_tokens, *downs)
+    half = keep + after(swap(send, n_line, 1, 0), side_in)
+    payloads = [payload] + [turn(after(payload, half), n_line, back) for back in range(1, n_line)]
+    own = jnp.concatenate([expert_in, expert_out])
+    core_own = swap(after(own, half), n_line, 1, 0)
+    latent = (half[0] + after(swap(half[1], n_line, 0, 1), core_own, *payloads[1:])).astype(narrow)
     ends = [1, n_line - 1]
     middle = list(range(2, n_line - 1))
-    groups = [ends, [0], middle]
-    rows = [latent] + [None] * (n_line - 1)
-    for back in ends:
-        rows[back] = turn(latent, n_line, back)
-    end_rows = [rows[back] for back in ends]
-    for back in middle:
-        rows[back] = turn(after(latent, *end_rows), n_line, back)
-
-    side_out = swap(after(own[1], latent), n_line, 0, 1)
-    core_out = [swap(after(own[1], latent), n_line, 1, 0), swap(after(side_out, *end_rows), n_line, 1, 0)]
-    weights = [own[0], own[1], side_in, side_out, core_in[0], core_out[0], core_in[1], core_out[1]]
+    groups = [ends, middle, [0]]
+    rows = [latent] + [turn(latent, n_line, back) for back in range(1, n_line)]
+
+    side_out = swap(after(expert_out[0], latent), n_line, 0, 1)
+    far_in = swap(after(side_in, latent), n_line, 1, 0)
+    far_out = swap(after(side_out, *rows[1:]), n_line, 1, 0)
+    weights = [own, core_own, side_in, side_out, far_in, far_out]
     side_down = swap(after(down, side_out), n_line, 0, 1)
-    all_down = [down, side_down] + [swap(d, n_line, 1, 0) for d in (down, side_down)]
 
     outs_of, deltas_of, saved = [None] * n_line, [None] * n_line, []
     for group in groups:
         count = len(group)
         kind = narrow if group[0] else wide
         if group == middle:
-            rows[group[0]] = after(rows[group[0]], deltas_of[0])
+            rows[group[0]] = after(rows[group[0]], deltas_of[1])
         if not group[0]:
-            rows[0] = after(latent, deltas_of[1])
+            rows[0] = after(latent, deltas_of[middle[0]])
         values = call(
             functools.partial(expert_body, count),
             [rows_of(kind)] * (2 * count) + [shape((4, count * tok_rows, hidden_width), narrow)] * 3,
@@ -283,57 +280,40 @@
 
     delta_lines = [home(value, back) for back, value in enumerate(deltas_of)]
 
-    def weight_grads(side, *earlier):
-        mine, other = call(
-            functools.partial(weight_grad_body, side, n_line, len(groups)),
-            [shape((2, latent_width, hidden_width), kind) for kind in (wide, narrow)],
-            "weight_grads",
-        )(
-            after(place, *earlier),
-            *(rows[i] for group in groups for i in group),
-            *(value for values in saved for value in values),
-        )
-        return mine, swap(other, n_line, 1, 0)
-
-    (sums,) = call(
-        functools.partial(order_body, n_line),
-        [shape((n_line * tok_rows, latent_width), narrow)],
-        "order",
-    )(place, *outs_of)
-    first_lines = [delta_lines[back] for back in ends]
-    mine, other = weight_grads(1, side_down, sums, *first_lines)
-    near_mine, near_other = weight_grads(0, mine)
-    far_sums = [(mine[i] + other[i].astype(wide)).astype(narrow) for i in range(2)]
-    delta_lines = [after(line, near_mine, *far_sums) for line in delta_lines]
+    pair = (2, latent_width, hidden_width)
+    near, far, other = call(
+        functools.partial(weight_grad_body, n_line, len(groups)),
+        [shape(pair, wide)] * 2 + [shape((4, latent_width, hidden_width), narrow)],
+        "weight_grads",
+    )(
+        after(place, side_down),
+        *(rows[i] for group in groups for i in group),
+        *(value for values in saved for value in values),
+    )
+    delta_lines = [after(line, near) for line in delta_lines]
     delta = sum(line.astype(wide) for line in delta_lines).astype(narrow)
     side_delta = swap(delta, n_line, 0, 1)
-    latent_out = lax.psum_scatter(
-        sums,
-        plane,
-        scatter_dimension=0,
-        axis_index_groups=[[z * 4 + i for z in range(n_line)] for i in range(4)],
-        tiled=True,
-    )
-    far_in = swap(after(far_sums[0], delta), n_line, 0, 1)
-    deltas = [delta, side_delta, swap(delta, n_line, 1, 0), swap(side_delta, n_line, 1, 0)]
+    out_lines = [outs_of[0]] + [home(after(outs_of[back], delta), back) for back in range(1, n_line)]
+    latent_out = sum(line.astype(wide) for line in out_lines).astype(narrow)
+    other = swap(after(other, delta), n_line, 1, 0)
+    far = swap((far + other[2:].astype(wide)).astype(narrow), n_line, 0, 1)
+    core_deltas = swap(jnp.stack([delta, after(side_delta, out_lines[1], out_lines[-1])]), n_line, 1, 0)
     blocks = call(
         functools.partial(down_grad_body, n_line),
         [shape((block, latent_width), wide)] + [shape((block, latent_width), narrow)] * (n_line - 1),
         "down_grad",
-    )(after(place, near_other, *all_down[2:]), *near_tokens, *deltas)
-    far_out = swap(after(far_sums[1], far_in, blocks[1]), n_line, 0, 1)
-    grad_in, grad_out = (
-        (near_mine[i] + near_other[i].astype(wide) + far.astype(wide)).astype(narrow)
-        for i, far in enumerate((far_in, far_out))
+    )(after(place, *out_lines[1:]), *near_tokens, delta, side_delta, core_deltas)
+    weight_grad = (near + other[:2].astype(wide) + far.astype(wide)).astype(narrow)
+    both = [shape((2, tok_rows, n_line * block), narrow)] * 2
+    own_grads, core_grads = call(token_grad_body, both, "token_grad")(
+        place, after(delta, blocks[1]), core_deltas, down, side_down
     )
     (grad_tokens,) = call(
-        functools.partial(token_grad_body, n_line, block),
-        [shape((tok_rows, width), narrow)],
-        "token_grad",
-    )(place, after(delta, blocks[1], far_in, latent_out), *all_down)
+        functools.partial(arrange_body, n_line, block), [shape((tok_rows, width), narrow)], "arrange"
+    )(place, own_grads, swap(core_grads, n_line, 1, 0))
     blocks = [blocks[0]] + [home(blocks[back], back) for back in range(1, n_line)]
-    grad_down = sum(after(value, grad_tokens).astype(wide) for value in blocks)
-    return (latent_out, grad_tokens, grad_down, grad_in[None], grad_out[None])
+    grad_down = sum(value.astype(wide) for value in blocks)
+    return (latent_out, grad_tokens, grad_down, weight_grad[:1], weight_grad[1:])
 
 
 def slot_table(routes, capacity):

time: 168 us -> 143 us (0.85)
  local copies, waits for them, and re-layouts: 27.1 us -> 3.2 us
  waiting for transfers between devices: 55.8 us -> 79.3 us
  between operations: 14.4 us -> 0.92 us
  other arithmetic: 8.17 us -> 2.55 us
  Pallas kernels: 21.9 us -> 18.2 us
    unnamed x106 -> x15, local copies, waits for them, and re-layouts: 27 us -> 2.01 us
    ppermute x15 -> x18, waiting for transfers between devices: 26.8 us -> 48.3 us  [turn(): lax.ppermute(value, plane, device_pairs(n_line, lambda z, x, c: ((z + by)...]
    pallas_call x11 -> x10, Pallas kernels: 21.9 us -> 18.2 us  [run(): pl.pallas_call(body, out_shape=outs, in_specs=[pl.BlockSpec(memory_space=...]
    broadcast_in_dim x1 -> x0, other arithmetic: 2.44 us -> none  [all_rows(): return (latent_out, grad_tokens, grad_down, grad_in[None], grad_out[None])]
    ppermute x21 -> x16, waiting for transfers between devices: 28.9 us -> 31 us  [swap(): lax.ppermute(value, plane, device_pairs(n_line, lambda z, x, c: (z, x ^ s...]
    ppermute x21 -> x16, starting transfers between devices: 12 us -> 11.4 us  [swap(): lax.ppermute(value, plane, device_pairs(n_line, lambda z, x, c: (z, x ^ s...]
    ppermute x15 -> x18, starting transfers between devices: 27.2 us -> 27.1 us  [turn(): lax.ppermute(value, plane, device_pairs(n_line, lambda z, x, c: ((z + by)...]
  transfers between devices with their start and end apart: 37 -> 34, of which waited for: 12 -> 17; matrix products, arithmetic and copies ran while one was open for 3% -> 1% of each run, Pallas kernels for 11% -> 12%
where the time goes in v6:
time: 143 us
  waiting for transfers between devices  79.3 us (55%)
  starting transfers between devices  38.6 us (27%)
  Pallas kernels  18.2 us (13%)
  local copies, waits for them, and re-layouts  3.2 us (2%)
  other arithmetic  2.55 us (2%)
    ppermute x18, waiting for transfers between devices, turn(): lax.ppermute(value, plane, device_pairs(n_line, lambda z, x, c: ((z + by)...  48.3 us
    ppermute x16, waiting for transfers between devices, swap(): lax.ppermute(value, plane, device_pairs(n_line, lambda z, x, c: (z, x ^ s...  31 us
    ppermute x18, starting transfers between devices, turn(): lax.ppermute(value, plane, device_pairs(n_line, lambda z, x, c: ((z + by)...  27.1 us
    pallas_call x10, Pallas kernels, run(): pl.pallas_call(body, out_shape=outs, in_specs=[pl.BlockSpec(memory_space=...  18.2 us
    ppermute x16, starting transfers between devices, swap(): lax.ppermute(value, plane, device_pairs(n_line, lambda z, x, c: (z, x ^ s...  11.4 us
  transfers between devices with their start and end apart: 34, of which 17 were waited for; matrix products, arithmetic and copies ran while one was open for 1% of the time, Pallas kernels for 12%

profile of v6, /device:TPU:0, one launch (start us, length us, event | category | flops | bytes accessed | tf_op | source)
XLA Modules:
  0.0 142.7 jit_solution(7667778092086307179)
XLA Ops:
  2.7 3.0 %collective-permute-start = (bf16[2,128,512]{2,1,0:T(8,128)(2,1)S(1)}, bf16[2,128,512]{2,1,0:T(8,128)(2,1)S(1)}, u32[]{:S(2)}, u32[]{:S(2)}) collective-permute-start(bf16[2,128,512]{2,1,0:T(8,128)(2,1)S(1)} %get-tuple-element.62), channel_id=1, source_target_pairs={{0,2},{1,3},{2,0},{3,1},{4,6},{5,7},{6,4},{7,5},{8,10},{9,11},{10,... | collective-permute-start | bytes 786440 | tf_op jit(solution)/shard_map/ppermute | solution.py:33
  5.7 2.6 %collective-permute-start.4 = (bf16[128,512]{1,0:T(8,128)(2,1)}, bf16[128,512]{1,0:T(8,128)(2,1)S(1)}, u32[]{:S(2)}, u32[]{:S(2)}) collective-permute-start(bf16[128,512]{1,0:T(8,128)(2,1)} %refs_4_.1), channel_id=1, source_target_pairs={{0,8},{1,9},{2,10},{3,11},{4,12},{5,13},{6,14},{7,15},{8,0},{9,1},... | collective-permute-start | bytes 393224 | tf_op jit(solution)/shard_map/ppermute | solution.py:29
  15.1 3.5 %collective-permute-done.4.refs_6_ = bf16[128,512]{1,0:T(8,128)(2,1)S(1)} collective-permute-done((bf16[128,512]{1,0:T(8,128)(2,1)}, bf16[128,512]{1,0:T(8,128)(2,1)S(1)}, u32[]{:S(2)}, u32[]{:S(2)}) %collective-permute-start.4) | collective-permute-done | bytes 131104 | tf_op jit(solution)/shard_map/ppermute | solution.py:29
  21.1 6.5 %collective-permute-done.7.refs_6_.refs_4_ = bf16[512,512]{1,0:T(8,128)(2,1)S(1)} collective-permute-done((bf16[512,512]{1,0:T(8,128)(2,1)}, bf16[512,512]{1,0:T(8,128)(2,1)S(1)}, u32[]{:S(2)}, u32[]{:S(2)}) %collective-permute-start.7) | collective-permute-done | bytes 524320 | tf_op jit(solution)/shard_map/ppermute | solution.py:33
  30.1 3.7 %collective-permute-start.12 = (bf16[144,512]{1,0:T(8,128)(2,1)S(1)}, bf16[144,512]{1,0:T(8,128)(2,1)S(1)}, u32[]{:S(2)}, u32[]{:S(2)}) collective-permute-start(bf16[144,512]{1,0:T(8,128)(2,1)S(1)} %payload.1.refs_1_), channel_id=1, source_target_pairs={{0,12},{1,13},{2,14},{3,15},{4,0},{5,1},{6,2},{7,3},{8,4},{9,5},{1... | collective-permute-start | bytes 442376 | tf_op jit(solution)/shard_map/ppermute | solution.py:29
  34.8 3.3 %collective-permute-done.12.refs_3_ = bf16[144,512]{1,0:T(8,128)(2,1)S(1)} collective-permute-done((bf16[144,512]{1,0:T(8,128)(2,1)S(1)}, bf16[144,512]{1,0:T(8,128)(2,1)S(1)}, u32[]{:S(2)}, u32[]{:S(2)}) %collective-permute-start.12) | collective-permute-done | bytes 147488 | tf_op jit(solution)/shard_map/ppermute | solution.py:29
  38.0 8.6 %collective-permute-done.11.refs_1_ = bf16[144,512]{1,0:T(8,128)(2,1)S(1)} collective-permute-done((bf16[144,512]{1,0:T(8,128)(2,1)S(1)}, bf16[144,512]{1,0:T(8,128)(2,1)S(1)}, u32[]{:S(2)}, u32[]{:S(2)}) %collective-permute-start.11) | collective-permute-done | bytes 147488 | tf_op jit(solution)/shard_map/ppermute | solution.py:29
  49.3 2.7 %collective-permute-start.13 = (bf16[128,512]{1,0:T(8,128)(2,1)S(1)}, bf16[128,512]{1,0:T(8,128)(2,1)S(1)}, u32[]{:S(2)}, u32[]{:S(2)}) collective-permute-start(bf16[128,512]{1,0:T(8,128)(2,1)S(1)} %fusion.1.refs_0_.refs_3_), channel_id=1, source_target_pairs={{0,8},{1,9},{2,10},{3,11},{4,12},{5,13},{6,14},{7,15},{8,0},{9,1},... | collective-permute-start | bytes 393224 | tf_op jit(solution)/shard_map/ppermute | solution.py:29
  52.1 2.5 %collective-permute-done.15.refs_1_ = bf16[128,512]{1,0:T(8,128)(2,1)S(1)} collective-permute-done((bf16[128,512]{1,0:T(8,128)(2,1)S(1)}, bf16[128,512]{1,0:T(8,128)(2,1)S(1)}, u32[]{:S(2)}, u32[]{:S(2)}) %collective-permute-start.15) | collective-permute-done | bytes 131104 | tf_op jit(solution)/shard_map/ppermute | solution.py:29
  54.6 3.5 %collective-permute-done.14.refs_0_ = bf16[128,512]{1,0:T(8,128)(2,1)S(1)} collective-permute-done((bf16[128,512]{1,0:T(8,128)(2,1)S(1)}, bf16[128,512]{1,0:T(8,128)(2,1)S(1)}, u32[]{:S(2)}, u32[]{:S(2)}) %collective-permute-start.14) | collective-permute-done | bytes 131104 | tf_op jit(solution)/shard_map/ppermute | solution.py:29
  58.1 3.2 %collective-permute-done.13.refs_0_.refs_2_ = bf16[128,512]{1,0:T(8,128)(2,1)S(1)} collective-permute-done((bf16[128,512]{1,0:T(8,128)(2,1)S(1)}, bf16[128,512]{1,0:T(8,128)(2,1)S(1)}, u32[]{:S(2)}, u32[]{:S(2)}) %collective-permute-start.13) | collective-permute-done | bytes 131104 | tf_op jit(solution)/shard_map/ppermute | solution.py:29
  63.2 3.4 %experts.3 = (bf16[128,512]{1,0:T(8,128)(2,1)S(1)}, bf16[128,512]{1,0:T(8,128)(2,1)S(1)}, bf16[128,512]{1,0:T(8,128)(2,1)S(1)}, bf16[128,512]{1,0:T(8,128)(2,1)S...) custom-call(s32[7]{0:T(128)S(1)} %stack.40.place, ...), custom_call_target="tpu_custom_call" | custom-call | tf_op jit(solution)/shard_map/experts/pallas_call | solution.py:45
  66.7 2.7 %experts.4 = (bf16[128,512]{1,0:T(8,128)(2,1)S(1)}, bf16[128,512]{1,0:T(8,128)(2,1)S(1)}, bf16[4,128,512]{2,1,0:T(8,128)(2,1)S(1)}, bf16[4,128,512]{2,1,0:T(8,128)(2,1)S(1)}, bf16[4,128,512]{2,1,0:T(8,128)(2,1)S(1)}) custom-call(s32[7]{0:T(128)S(1)} %stack.40.place, bf16[128,512]{1,0:T(8,128)(2,1)S(1)} %collective-permute-done.13.refs_0_.refs_2_, ...), custom_call_target="tpu_custom_call" | custom-call | tf_op jit(solution)/shard_map/experts/pallas_call | solution.py:45
  71.2 2.5 %collective-permute-start.20 = (bf16[128,512]{1,0:T(8,128)(2,1)S(1)}, bf16[128,512]{1,0:T(8,128)(2,1)S(1)}, u32[]{:S(2)}, u32[]{:S(2)}) collective-permute-start(bf16[128,512]{1,0:T(8,128)(2,1)S(1)} %get-tuple-element.75), channel_id=1, source_target_pairs={{0,12},{1,13},{2,14},{3,15},{4,0},{5,1},{6,2},{7,3},{8,4},{9,5},{1... | collective-permute-start | bytes 393224 | tf_op jit(solution)/shard_map/ppermute | solution.py:29
  75.6 2.7 %experts.5 = (f32[128,512]{1,0:T(8,128)S(1)}, f32[128,512]{1,0:T(8,128)S(1)}, bf16[4,128,512]{2,1,0:T(8,128)(2,1)S(1)}, bf16[4,128,512]{2,1,0:T(8,128)(2,1)S(1)}, bf16[4,128,512]{2,1,0:T(8,128)(2,1)S(1)}) custom-call(s32[7]{0:T(128)S(1)} %stack.40.place, bf16[128,512]{1,0:T(8,128)(2,1)S(1)} %fusion.1.refs_0_.refs_3_, bf16[144,512]{1,0:T(8,128)(2,1)S(1)} %payload.1.refs_1_, ...), custom_call_target="tpu_custom_call" | custom-call | tf_op jit(solution)/shard_map/experts/pallas_call | solution.py:45
  78.3 2.9 %weight_grads.1 = (f32[2,512,512]{2,1,0:T(8,128)S(1)}, f32[2,512,512]{2,1,0:T(8,128)S(1)}, bf16[4,512,512]{2,1,0:T(8,128)(2,1)S(1)}) custom-call(s32[7]{0:T(128)S(1)} %stack.40.place, bf16[128,512]{1,0:T(8,128)(2,1)S(1)} %collective-permute-done.14.refs_0_, bf16[128,512]{1,0:T(8,128)(2,1)S(1)} %collective-permute-done.15.refs_1_, ...), custom_call_target="tpu_custom_call" | custom-call | tf_op jit(solution)/shard_map/weight_grads/pallas_call | solution.py:45
  81.4 4.1 %collective-permute-done.32 = bf16[4,512,512]{2,1,0:T(8,128)(2,1)S(1)} collective-permute-done((bf16[4,512,512]{2,1,0:T(8,128)(2,1)S(1)}, bf16[4,512,512]{2,1,0:T(8,128)(2,1)S(1)}, u32[]{:S(2)}, u32[]{:S(2)}) %collective-permute-start.32) | collective-permute-done | bytes 2097184 | tf_op jit(solution)/shard_map/ppermute | solution.py:33
  87.5 2.6 %collective-permute-start.23 = (bf16[128,512]{1,0:T(8,128)(2,1)S(1)}, bf16[128,512]{1,0:T(8,128)(2,1)S(1)}, u32[]{:S(2)}, u32[]{:S(2)}) collective-permute-start(bf16[128,512]{1,0:T(8,128)(2,1)S(1)} %get-tuple-element.100), channel_id=1, source_target_pairs={{0,12},{1,13},{2,14},{3,15},{4,0},{5,1},{6,2},{7,3},{8,4},{9,5},{1... | collective-permute-start | bytes 393224 | tf_op jit(solution)/shard_map/ppermute | solution.py:29
  90.6 3.4 %collective-permute-done.23 = bf16[128,512]{1,0:T(8,128)(2,1)S(1)} collective-permute-done((bf16[128,512]{1,0:T(8,128)(2,1)S(1)}, bf16[128,512]{1,0:T(8,128)(2,1)S(1)}, u32[]{:S(2)}, u32[]{:S(2)}) %collective-permute-start.23) | collective-permute-done | bytes 131104 | tf_op jit(solution)/shard_map/ppermute | solution.py:29
  94.0 2.9 %collective-permute-done.25 = bf16[128,512]{1,0:T(8,128)(2,1)S(1)} collective-permute-done((bf16[128,512]{1,0:T(8,128)(2,1)S(1)}, bf16[128,512]{1,0:T(8,128)(2,1)S(1)}, u32[]{:S(2)}, u32[]{:S(2)}) %collective-permute-start.25) | collective-permute-done | bytes 131104 | tf_op jit(solution)/shard_map/ppermute | solution.py:29
  96.9 17.2 %collective-permute-done.26.refs_5_ = bf16[128,512]{1,0:T(8,128)(2,1)S(1)} collective-permute-done((bf16[128,512]{1,0:T(8,128)(2,1)S(1)}, bf16[128,512]{1,0:T(8,128)(2,1)S(1)}, u32[]{:S(2)}, u32[]{:S(2)}) %collective-permute-start.26) | collective-permute-done | bytes 131104 | tf_op jit(solution)/shard_map/ppermute | solution.py:33
  115.6 8.2 %collective-permute-done.24 = bf16[128,512]{1,0:T(8,128)(2,1)S(1)} collective-permute-done((bf16[128,512]{1,0:T(8,128)(2,1)S(1)}, bf16[128,512]{1,0:T(8,128)(2,1)S(1)}, u32[]{:S(2)}, u32[]{:S(2)}) %collective-permute-start.24) | collective-permute-done | bytes 131104 | tf_op jit(solution)/shard_map/ppermute | solution.py:29
  125.0 2.3 %collective-permute-start.29 = (bf16[128,512]{1,0:T(8,128)(2,1)S(1)}, bf16[128,512]{1,0:T(8,128)(2,1)S(1)}, u32[]{:S(2)}, u32[]{:S(2)}) collective-permute-start(bf16[128,512]{1,0:T(8,128)(2,1)S(1)} %get-tuple-element.107), channel_id=1, source_target_pairs={{0,12},{1,13},{2,14},{3,15},{4,0},{5,1},{6,2},{7,3},{8,4},{9,5},{1... | collective-permute-start | bytes 393224 | tf_op jit(solution)/shard_map/ppermute | solution.py:29
  130.1 8.9 %collective-permute-done.30 = bf16[128,512]{1,0:T(8,128)(2,1)S(1)} collective-permute-done((bf16[128,512]{1,0:T(8,128)(2,1)S(1)}, bf16[128,512]{1,0:T(8,128)(2,1)S(1)}, u32[]{:S(2)}, u32[]{:S(2)}) %collective-permute-start.30) | collective-permute-done | bytes 131104 | tf_op jit(solution)/shard_map/ppermute | solution.py:29
  (82 shorter events, 35.0 us)
Async XLA Ops:
  2.7 9.4 %collective-permute-start = (bf16[2,128,512]{2,1,0:T(8,128)(2,1)S(1)}, bf16[2,128,512]{2,1,0:T(8,128)(2,1)S(1)}, u32[]{:S(2)}, u32[]{:S(2)}) collective-permute-start(bf16[2,128,512]{2,1,0:T(8,128)(2,1)S(1)} %get-tuple-element.62), channel_id=1, source_target_pairs={{0,2},{1,3},{2,0},{3,1},{4,6},{5,7},{6,4},{7,5},{8,10},{9,11},{10,... | collective-permute-start | bytes 786440 | tf_op jit(solution)/shard_map/ppermute | solution.py:33
  5.7 12.8 %collective-permute-start.4 = (bf16[128,512]{1,0:T(8,128)(2,1)}, bf16[128,512]{1,0:T(8,128)(2,1)S(1)}, u32[]{:S(2)}, u32[]{:S(2)}) collective-permute-start(bf16[128,512]{1,0:T(8,128)(2,1)} %refs_4_.1), channel_id=1, source_target_pairs={{0,8},{1,9},{2,10},{3,11},{4,12},{5,13},{6,14},{7,15},{8,0},{9,1},... | collective-permute-start | bytes 393224 | tf_op jit(solution)/shard_map/ppermute | solution.py:29
  8.3 10.3 %collective-permute-start.3 = (bf16[128,512]{1,0:T(8,128)(2,1)}, bf16[128,512]{1,0:T(8,128)(2,1)S(1)}, u32[]{:S(2)}, u32[]{:S(2)}) collective-permute-start(bf16[128,512]{1,0:T(8,128)(2,1)} %refs_4_.1), channel_id=1, source_target_pairs={{0,4},{1,5},{2,6},{3,7},{4,8},{5,9},{6,10},{7,11},{8,12},{9,13},{1... | collective-permute-start | bytes 393224 | tf_op jit(solution)/shard_map/ppermute | solution.py:29
  13.5 14.2 %collective-permute-start.7 = (bf16[512,512]{1,0:T(8,128)(2,1)}, bf16[512,512]{1,0:T(8,128)(2,1)S(1)}, u32[]{:S(2)}, u32[]{:S(2)}) collective-permute-start(bf16[512,512]{1,0:T(8,128)(2,1)} %bitcast.29), channel_id=1, source_target_pairs={{0,2},{1,3},{2,0},{3,1},{4,6},{5,7},{6,4},{7,5},{8,10},{9,11},{10,... | collective-permute-start | bytes 1572872 | tf_op jit(solution)/shard_map/ppermute | solution.py:33
  27.7 18.9 %collective-permute-start.9 = (bf16[2,512,512]{2,1,0:T(8,128)(2,1)S(1)}, bf16[2,512,512]{2,1,0:T(8,128)(2,1)S(1)}, u32[]{:S(2)}, u32[]{:S(2)}) collective-permute-start(bf16[2,512,512]{2,1,0:T(8,128)(2,1)S(1)} %constant_dynamic-update-slice_fusion.refs_4_.refs_2_), channel_id=1, source_target_pairs={{0,1},{1,0},{2,3},{3,2},{4,5},{5,4},{6,7},{7,6},{8,9},{9,8},{10,11... | collective-permute-start | bytes 3145736 | tf_op jit(solution)/shard_map/ppermute | solution.py:33
  27.8 18.8 %collective-permute-start.8 = (f32[128,512]{1,0:T(8,128)S(1)}, f32[128,512]{1,0:T(8,128)S(1)}, u32[]{:S(2)}, u32[]{:S(2)}) collective-permute-start(f32[128,512]{1,0:T(8,128)S(1)} %slice_bitcast_fusion), channel_id=1, source_target_pairs={{0,2},{1,3},{2,0},{3,1},{4,6},{5,7},{6,4},{7,5},{8,10},{9,11},{10,... | collective-permute-start | bytes 786440 | tf_op jit(solution)/shard_map/ppermute | solution.py:33
  33.8 12.9 %collective-permute-start.11 = (bf16[144,512]{1,0:T(8,128)(2,1)S(1)}, bf16[144,512]{1,0:T(8,128)(2,1)S(1)}, u32[]{:S(2)}, u32[]{:S(2)}) collective-permute-start(bf16[144,512]{1,0:T(8,128)(2,1)S(1)} %payload.1.refs_1_), channel_id=1, source_target_pairs={{0,8},{1,9},{2,10},{3,11},{4,12},{5,13},{6,14},{7,15},{8,0},{9,1},... | collective-permute-start | bytes 442376 | tf_op jit(solution)/shard_map/ppermute | solution.py:29
  33.8 12.9 %collective-permute-start.10 = (bf16[144,512]{1,0:T(8,128)(2,1)S(1)}, bf16[144,512]{1,0:T(8,128)(2,1)S(1)}, u32[]{:S(2)}, u32[]{:S(2)}) collective-permute-start(bf16[144,512]{1,0:T(8,128)(2,1)S(1)} %payload.1.refs_1_), channel_id=1, source_target_pairs={{0,4},{1,5},{2,6},{3,7},{4,8},{5,9},{6,10},{7,11},{8,12},{9,13},{1... | collective-permute-start | bytes 442376 | tf_op jit(solution)/shard_map/ppermute | solution.py:29
  46.7 14.6 %collective-permute-start.16 = (bf16[512,512]{1,0:T(8,128)(2,1)S(1)}, bf16[512,512]{1,0:T(8,128)(2,1)S(1)}, u32[]{:S(2)}, u32[]{:S(2)}) collective-permute-start(bf16[512,512]{1,0:T(8,128)(2,1)S(1)} %bitcast.30), channel_id=1, source_target_pairs={{0,2},{1,3},{2,0},{3,1},{4,6},{5,7},{6,4},{7,5},{8,10},{9,11},{10,... | collective-permute-start | bytes 1572872 | tf_op jit(solution)/shard_map/ppermute | solution.py:33
  48.6 9.5 %collective-permute-start.14 = (bf16[128,512]{1,0:T(8,128)(2,1)S(1)}, bf16[128,512]{1,0:T(8,128)(2,1)S(1)}, u32[]{:S(2)}, u32[]{:S(2)}) collective-permute-start(bf16[128,512]{1,0:T(8,128)(2,1)S(1)} %fusion.1.refs_0_.refs_3_), channel_id=1, source_target_pairs={{0,4},{1,5},{2,6},{3,7},{4,8},{5,9},{6,10},{7,11},{8,12},{9,13},{1... | collective-permute-start | bytes 393224 | tf_op jit(solution)/shard_map/ppermute | solution.py:29
  49.3 12.0 %collective-permute-start.13 = (bf16[128,512]{1,0:T(8,128)(2,1)S(1)}, bf16[128,512]{1,0:T(8,128)(2,1)S(1)}, u32[]{:S(2)}, u32[]{:S(2)}) collective-permute-start(bf16[128,512]{1,0:T(8,128)(2,1)S(1)} %fusion.1.refs_0_.refs_3_), channel_id=1, source_target_pairs={{0,8},{1,9},{2,10},{3,11},{4,12},{5,13},{6,14},{7,15},{8,0},{9,1},... | collective-permute-start | bytes 393224 | tf_op jit(solution)/shard_map/ppermute | solution.py:29
  52.1 10.7 %collective-permute-start.17 = (bf16[512,512]{1,0:T(8,128)(2,1)S(1)}, bf16[512,512]{1,0:T(8,128)(2,1)S(1)}, u32[]{:S(2)}, u32[]{:S(2)}) collective-permute-start(bf16[512,512]{1,0:T(8,128)(2,1)S(1)} %collective-permute-done.7.refs_6_.refs_4_), channel_id=1, source_target_pairs={{0,1},{1,0},{2,3},{3,2},{4,5},{5,4},{6,7},{7,6},{8,9},{9,8},{10,11... | collective-permute-start | bytes 1572872 | tf_op jit(solution)/shard_map/ppermute | solution.py:33
  61.3 14.3 %collective-permute-start.19 = (bf16[512,512]{1,0:T(8,128)(2,1)S(1)}, bf16[512,512]{1,0:T(8,128)(2,1)S(1)}, u32[]{:S(2)}, u32[]{:S(2)}) collective-permute-start(bf16[512,512]{1,0:T(8,128)(2,1)S(1)} %get-tuple-element.83.down), channel_id=1, source_target_pairs={{0,2},{1,3},{2,0},{3,1},{4,6},{5,7},{6,4},{7,5},{8,10},{9,11},{10,... | collective-permute-start | bytes 1572872 | tf_op jit(solution)/shard_map/ppermute | solution.py:33
  66.6 14.6 %collective-permute-start.22 = (bf16[128,512]{1,0:T(8,128)(2,1)S(1)}, bf16[128,512]{1,0:T(8,128)(2,1)S(1)}, u32[]{:S(2)}, u32[]{:S(2)}) collective-permute-start(bf16[128,512]{1,0:T(8,128)(2,1)S(1)} %get-tuple-element.98), channel_id=1, source_target_pairs={{0,4},{1,5},{2,6},{3,7},{4,8},{5,9},{6,10},{7,11},{8,12},{9,13},{1... | collective-permute-start | bytes 393224 | tf_op jit(solution)/shard_map/ppermute | solution.py:29
  69.4 11.9 %collective-permute-start.21 = (bf16[128,512]{1,0:T(8,128)(2,1)S(1)}, bf16[128,512]{1,0:T(8,128)(2,1)S(1)}, u32[]{:S(2)}, u32[]{:S(2)}) collective-permute-start(bf16[128,512]{1,0:T(8,128)(2,1)S(1)} %get-tuple-element.77), channel_id=1, source_target_pairs={{0,8},{1,9},{2,10},{3,11},{4,12},{5,13},{6,14},{7,15},{8,0},{9,1},... | collective-permute-start | bytes 393224 | tf_op jit(solution)/shard_map/ppermute | solution.py:29
  71.2 10.1 %collective-permute-start.20 = (bf16[128,512]{1,0:T(8,128)(2,1)S(1)}, bf16[128,512]{1,0:T(8,128)(2,1)S(1)}, u32[]{:S(2)}, u32[]{:S(2)}) collective-permute-start(bf16[128,512]{1,0:T(8,128)(2,1)S(1)} %get-tuple-element.75), channel_id=1, source_target_pairs={{0,12},{1,13},{2,14},{3,15},{4,0},{5,1},{6,2},{7,3},{8,4},{9,5},{1... | collective-permute-start | bytes 393224 | tf_op jit(solution)/shard_map/ppermute | solution.py:29
  86.0 55.2 %collective-permute-start.33 = (bf16[2,512,512]{2,1,0:T(8,128)(2,1)S(1)}, bf16[2,512,512]{2,1,0:T(8,128)(2,1)S(1)}, u32[]{:S(2)}, u32[]{:S(2)}) collective-permute-start(bf16[2,512,512]{2,1,0:T(8,128)(2,1)S(1)} %add_convert_fusion.1), channel_id=1, source_target_pairs={{0,2},{1,3},{2,0},{3,1},{4,6},{5,7},{6,4},{7,5},{8,10},{9,11},{10,... | collective-permute-start | bytes 3145736 | tf_op jit(solution)/shard_map/ppermute | solution.py:33
  90.1 24.0 %collective-permute-start.26 = (bf16[128,512]{1,0:T(8,128)(2,1)S(1)}, bf16[128,512]{1,0:T(8,128)(2,1)S(1)}, u32[]{:S(2)}, u32[]{:S(2)}) collective-permute-start(bf16[128,512]{1,0:T(8,128)(2,1)S(1)} %add_convert_fusion.3.refs_4_.delta), channel_id=1, source_target_pairs={{0,2},{1,3},{2,0},{3,1},{4,6},{5,7},{6,4},{7,5},{8,10},{9,11},{10,... | collective-permute-start | bytes 393224 | tf_op jit(solution)/shard_map/ppermute | solution.py:33
  114.1 9.7 %collective-permute-start.27 = (bf16[2,128,512]{2,1,0:T(8,128)(2,1)S(1)}, bf16[2,128,512]{2,1,0:T(8,128)(2,1)S(1)}, u32[]{:S(2)}, u32[]{:S(2)}) collective-permute-start(bf16[2,128,512]{2,1,0:T(8,128)(2,1)S(1)} %pad_maximum_fusion), channel_id=1, source_target_pairs={{0,1},{1,0},{2,3},{3,2},{4,5},{5,4},{6,7},{7,6},{8,9},{9,8},{10,11... | collective-permute-start | bytes 786440 | tf_op jit(solution)/shard_map/ppermute | solution.py:33
  114.2 9.6 %collective-permute-start.24 = (bf16[128,512]{1,0:T(8,128)(2,1)S(1)}, bf16[128,512]{1,0:T(8,128)(2,1)S(1)}, u32[]{:S(2)}, u32[]{:S(2)}) collective-permute-start(bf16[128,512]{1,0:T(8,128)(2,1)S(1)} %get-tuple-element.102), channel_id=1, source_target_pairs={{0,8},{1,9},{2,10},{3,11},{4,12},{5,13},{6,14},{7,15},{8,0},{9,1},... | collective-permute-start | bytes 393224 | tf_op jit(solution)/shard_map/ppermute | solution.py:29
  125.0 14.0 %collective-permute-start.29 = (bf16[128,512]{1,0:T(8,128)(2,1)S(1)}, bf16[128,512]{1,0:T(8,128)(2,1)S(1)}, u32[]{:S(2)}, u32[]{:S(2)}) collective-permute-start(bf16[128,512]{1,0:T(8,128)(2,1)S(1)} %get-tuple-element.107), channel_id=1, source_target_pairs={{0,12},{1,13},{2,14},{3,15},{4,0},{5,1},{6,2},{7,3},{8,4},{9,5},{1... | collective-permute-start | bytes 393224 | tf_op jit(solution)/shard_map/ppermute | solution.py:29
  127.3 11.6 %collective-permute-start.30 = (bf16[128,512]{1,0:T(8,128)(2,1)S(1)}, bf16[128,512]{1,0:T(8,128)(2,1)S(1)}, u32[]{:S(2)}, u32[]{:S(2)}) collective-permute-start(bf16[128,512]{1,0:T(8,128)(2,1)S(1)} %get-tuple-element.112), channel_id=1, source_target_pairs={{0,8},{1,9},{2,10},{3,11},{4,12},{5,13},{6,14},{7,15},{8,0},{9,1},... | collective-permute-start | bytes 393224 | tf_op jit(solution)/shard_map/ppermute | solution.py:29
  127.3 11.6 %collective-permute-start.31 = (bf16[128,512]{1,0:T(8,128)(2,1)S(1)}, bf16[128,512]{1,0:T(8,128)(2,1)S(1)}, u32[]{:S(2)}, u32[]{:S(2)}) collective-permute-start(bf16[128,512]{1,0:T(8,128)(2,1)S(1)} %get-tuple-element.113), channel_id=1, source_target_pairs={{0,4},{1,5},{2,6},{3,7},{4,8},{5,9},{6,10},{7,11},{8,12},{9,13},{1... | collective-permute-start | bytes 393224 | tf_op jit(solution)/shard_map/ppermute | solution.py:29
  129.3 10.4 %collective-permute-start.28 = (bf16[2,128,512]{2,1,0:T(8,128)(2,1)S(1)}, bf16[2,128,512]{2,1,0:T(8,128)(2,1)S(1)}, u32[]{:S(2)}, u32[]{:S(2)}) collective-permute-start(bf16[2,128,512]{2,1,0:T(8,128)(2,1)S(1)} %get-tuple-element.110), channel_id=1, source_target_pairs={{0,1},{1,0},{2,3},{3,2},{4,5},{5,4},{6,7},{7,6},{8,9},{9,8},{10,11... | collective-permute-start | bytes 786440 | tf_op jit(solution)/shard_map/ppermute | solution.py:33
  (17 other events, 124.9 us)

commit v7 on v6

--- a/solution.py
+++ b/solution.py
@@ -115,9 +115,9 @@
 
 def expert_body(count, place, *refs):
     rows_in, payloads = refs[:count], refs[count : 2 * count]
-    own, core, *sides = refs[2 * count : 2 * count + 6]
-    weights = (own.at[0], own.at[1], sides[0], sides[1], core.at[0], core.at[1], sides[2], sides[3])
-    outs = refs[2 * count + 6 :]
+    own, core, side_out, core_out = refs[2 * count : 2 * count + 4]
+    weights = (own.at[0], own.at[1], own.at[2], side_out, core.at[0], core.at[1], core.at[2], core_out)
+    outs = refs[2 * count + 4 :]
     combined, deltas = outs[:count], outs[count : 2 * count]
     hiddens, scaleds, back_pres = outs[2 * count :]
     tok_rows, width = rows_in[0].shape
@@ -232,19 +232,19 @@
     (payload,) = call(payload_body, [shape((tok_rows + gate_rows, latent_width), narrow)], "payload")(
         place, routes.T, gate_levels.T, latent_grad
     )
+    side_in = swap(expert_in[0], n_line, 0, 1)
     across = swap(columns[2], n_line, 0, 1)
     near_tokens = [columns[0], across[0], swap(after(columns[1], across), n_line, 1, 0), swap(across[1], n_line, 1, 0)]
-    side_in = swap(after(expert_in[0], across, near_tokens[2]), n_line, 0, 1)
 
     project = call(
         functools.partial(project_body, n_line),
         [shape((2, tok_rows, latent_width), wide)] * 2 + [shape((n_line * block, latent_width), narrow)],
         "project",
     )
-    keep, send, down = project(place, *near_tokens, *downs)
-    half = keep + after(swap(send, n_line, 1, 0), side_in)
-    payloads = [payload] + [turn(after(payload, half), n_line, back) for back in range(1, n_line)]
-    own = jnp.concatenate([expert_in, expert_out])
+    keep, send, down = project(after(place, side_in), *near_tokens, *downs)
+    half = keep + swap(send, n_line, 1, 0)
+    payloads = [payload] + [turn(after(payload, *downs[1:]), n_line, back) for back in range(1, n_line)]
+    own = jnp.concatenate([expert_in, expert_out, side_in[None]])
     core_own = swap(after(own, half), n_line, 1, 0)
     latent = (half[0] + after(swap(half[1], n_line, 0, 1), core_own, *payloads[1:])).astype(narrow)
     ends = [1, n_line - 1]
@@ -253,9 +253,8 @@
     rows = [latent] + [turn(latent, n_line, back) for back in range(1, n_line)]
 
     side_out = swap(after(expert_out[0], latent), n_line, 0, 1)
-    far_in = swap(after(side_in, latent), n_line, 1, 0)
-    far_out = swap(after(side_out, *rows[1:]), n_line, 1, 0)
-    weights = [own, core_own, side_in, side_out, far_in, far_out]
+    core_out = swap(after(side_out, *rows[1:]), n_line, 1, 0)
+    weights = [own, core_own, side_out, core_out]
     side_down = swap(after(down, side_out), n_line, 0, 1)
 
     outs_of, deltas_of, saved = [None] * n_line, [None] * n_line, []
@@ -293,11 +292,11 @@
     delta_lines = [after(line, near) for line in delta_lines]
     delta = sum(line.astype(wide) for line in delta_lines).astype(narrow)
     side_delta = swap(delta, n_line, 0, 1)
-    out_lines = [outs_of[0]] + [home(after(outs_of[back], delta), back) for back in range(1, n_line)]
+    out_lines = [outs_of[0]] + [home(outs_of[back], back) for back in range(1, n_line)]
     latent_out = sum(line.astype(wide) for line in out_lines).astype(narrow)
     other = swap(after(other, delta), n_line, 1, 0)
-    far = swap((far + other[2:].astype(wide)).astype(narrow), n_line, 0, 1)
-    core_deltas = swap(jnp.stack([delta, after(side_delta, out_lines[1], out_lines[-1])]), n_line, 1, 0)
+    far = swap((far + after(other[2:], side_delta, out_lines[1]).astype(wide)).astype(narrow), n_line, 0, 1)
+    core_deltas = swap(jnp.stack([delta, side_delta]), n_line, 1, 0)
     blocks = call(
         functools.partial(down_grad_body, n_line),
         [shape((block, latent_width), wide)] + [shape((block, latent_width), narrow)] * (n_line - 1),

time: 143 us -> 121 us (0.85)
  waiting for transfers between devices: 79.3 us -> 55.3 us
  starting transfers between devices: 38.6 us -> 40.1 us
    ppermute x16 -> x15, waiting for transfers between devices: 31 us -> 15.6 us  [swap(): lax.ppermute(value, plane, device_pairs(n_line, lambda z, x, c: (z, x ^ s...]
    ppermute x18, waiting for transfers between devices: 48.3 us -> 39.7 us  [turn(): lax.ppermute(value, plane, device_pairs(n_line, lambda z, x, c: ((z + by)...]
    ppermute x16 -> x15, starting transfers between devices: 11.4 us -> 11.7 us  [swap(): lax.ppermute(value, plane, device_pairs(n_line, lambda z, x, c: (z, x ^ s...]
  transfers between devices with their start and end apart: 34 -> 33, of which waited for: 17 -> 16; matrix products, arithmetic and copies ran while one was open for 1% -> 2% of each run, Pallas kernels for 12% -> 14%
where the time goes in v7:
time: 121 us; the launch traced here: 120 us
  waiting for transfers between devices  55.3 us (46%)
  starting transfers between devices  40.1 us (33%)
  Pallas kernels  18.2 us (15%)
  local copies, waits for them, and re-layouts  3.19 us (3%)
  other arithmetic  2.72 us (2%)
    ppermute x18, waiting for transfers between devices, turn(): lax.ppermute(value, plane, device_pairs(n_line, lambda z, x, c: ((z + by)...  39.7 us
    ppermute x18, starting transfers between devices, turn(): lax.ppermute(value, plane, device_pairs(n_line, lambda z, x, c: ((z + by)...  28.4 us
    pallas_call x10, Pallas kernels, run(): pl.pallas_call(body, out_shape=outs, in_specs=[pl.BlockSpec(memory_space=...  18.2 us
    ppermute x15, waiting for transfers between devices, swap(): lax.ppermute(value, plane, device_pairs(n_line, lambda z, x, c: (z, x ^ s...  15.6 us
    ppermute x15, starting transfers between devices, swap(): lax.ppermute(value, plane, device_pairs(n_line, lambda z, x, c: (z, x ^ s...  11.7 us
  transfers between devices with their start and end apart: 33, of which 16 were waited for; matrix products, arithmetic and copies ran while one was open for 2% of the time, Pallas kernels for 14%

profile of v7, /device:TPU:0, one launch (start us, length us, event | category | flops | bytes accessed | tf_op | source)
XLA Modules:
  0.0 120.4 jit_solution(5014553876391117706)
XLA Ops:
  0.6 3.0 %collective-permute-start = (bf16[512,512]{1,0:T(8,128)(2,1)}, bf16[512,512]{1,0:T(8,128)(2,1)S(1)}, u32[]{:S(2)}, u32[]{:S(2)}) collective-permute-start(bf16[512,512]{1,0:T(8,128)(2,1)} %bitcast.30), channel_id=1, source_target_pairs={{0,2},{1,3},{2,0},{3,1},{4,6},{5,7},{6,4},{7,5},{8,10},{9,11},{10,... | collective-permute-start | bytes 1572872 | tf_op jit(solution)/shard_map/ppermute | solution.py:33
  5.8 3.1 %collective-permute-start.5 = (bf16[128,512]{1,0:T(8,128)(2,1)}, bf16[128,512]{1,0:T(8,128)(2,1)S(1)}, u32[]{:S(2)}, u32[]{:S(2)}) collective-permute-start(bf16[128,512]{1,0:T(8,128)(2,1)} %refs_4_.1), channel_id=1, source_target_pairs={{0,8},{1,9},{2,10},{3,11},{4,12},{5,13},{6,14},{7,15},{8,0},{9,1},... | collective-permute-start | bytes 393224 | tf_op jit(solution)/shard_map/ppermute | solution.py:29
  10.4 2.2 %collective-permute-start.6 = (bf16[128,512]{1,0:T(8,128)(2,1)}, bf16[128,512]{1,0:T(8,128)(2,1)S(1)}, u32[]{:S(2)}, u32[]{:S(2)}) collective-permute-start(bf16[128,512]{1,0:T(8,128)(2,1)} %refs_4_.1), channel_id=1, source_target_pairs={{0,12},{1,13},{2,14},{3,15},{4,0},{5,1},{6,2},{7,3},{8,4},{9,5},{1... | collective-permute-start | bytes 393224 | tf_op jit(solution)/shard_map/ppermute | solution.py:29
  12.7 8.7 %collective-permute-done.1 = bf16[2,128,512]{2,1,0:T(8,128)(2,1)S(1)} collective-permute-done((bf16[2,128,512]{2,1,0:T(8,128)(2,1)S(1)}, bf16[2,128,512]{2,1,0:T(8,128)(2,1)S(1)}, u32[]{:S(2)}, u32[]{:S(2)}) %collective-permute-start.1) | collective-permute-done | bytes 262176 | tf_op jit(solution)/shard_map/ppermute | solution.py:33
  29.8 3.7 %collective-permute-start.12 = (bf16[144,512]{1,0:T(8,128)(2,1)S(1)}, bf16[144,512]{1,0:T(8,128)(2,1)S(1)}, u32[]{:S(2)}, u32[]{:S(2)}) collective-permute-start(bf16[144,512]{1,0:T(8,128)(2,1)S(1)} %payload.1.refs_1_), channel_id=1, source_target_pairs={{0,12},{1,13},{2,14},{3,15},{4,0},{5,1},{6,2},{7,3},{8,4},{9,5},{1... | collective-permute-start | bytes 442376 | tf_op jit(solution)/shard_map/ppermute | solution.py:29
  34.5 3.3 %collective-permute-done.12.refs_3_ = bf16[144,512]{1,0:T(8,128)(2,1)S(1)} collective-permute-done((bf16[144,512]{1,0:T(8,128)(2,1)S(1)}, bf16[144,512]{1,0:T(8,128)(2,1)S(1)}, u32[]{:S(2)}, u32[]{:S(2)}) %collective-permute-start.12) | collective-permute-done | bytes 147488 | tf_op jit(solution)/shard_map/ppermute | solution.py:29
  37.8 8.2 %collective-permute-done.11.refs_1_ = bf16[144,512]{1,0:T(8,128)(2,1)S(1)} collective-permute-done((bf16[144,512]{1,0:T(8,128)(2,1)S(1)}, bf16[144,512]{1,0:T(8,128)(2,1)S(1)}, u32[]{:S(2)}, u32[]{:S(2)}) %collective-permute-start.11) | collective-permute-done | bytes 147488 | tf_op jit(solution)/shard_map/ppermute | solution.py:29
  48.7 2.8 %collective-permute-start.13 = (bf16[128,512]{1,0:T(8,128)(2,1)S(1)}, bf16[128,512]{1,0:T(8,128)(2,1)S(1)}, u32[]{:S(2)}, u32[]{:S(2)}) collective-permute-start(bf16[128,512]{1,0:T(8,128)(2,1)S(1)} %fusion.1.refs_0_.refs_3_), channel_id=1, source_target_pairs={{0,8},{1,9},{2,10},{3,11},{4,12},{5,13},{6,14},{7,15},{8,0},{9,1},... | collective-permute-start | bytes 393224 | tf_op jit(solution)/shard_map/ppermute | solution.py:29
  51.4 2.6 %collective-permute-done.15.refs_1_ = bf16[128,512]{1,0:T(8,128)(2,1)S(1)} collective-permute-done((bf16[128,512]{1,0:T(8,128)(2,1)S(1)}, bf16[128,512]{1,0:T(8,128)(2,1)S(1)}, u32[]{:S(2)}, u32[]{:S(2)}) %collective-permute-start.15) | collective-permute-done | bytes 131104 | tf_op jit(solution)/shard_map/ppermute | solution.py:29
  54.1 3.3 %collective-permute-done.14.refs_0_ = bf16[128,512]{1,0:T(8,128)(2,1)S(1)} collective-permute-done((bf16[128,512]{1,0:T(8,128)(2,1)S(1)}, bf16[128,512]{1,0:T(8,128)(2,1)S(1)}, u32[]{:S(2)}, u32[]{:S(2)}) %collective-permute-start.14) | collective-permute-done | bytes 131104 | tf_op jit(solution)/shard_map/ppermute | solution.py:29
  57.4 3.1 %collective-permute-done.13.refs_0_.refs_2_ = bf16[128,512]{1,0:T(8,128)(2,1)S(1)} collective-permute-done((bf16[128,512]{1,0:T(8,128)(2,1)S(1)}, bf16[128,512]{1,0:T(8,128)(2,1)S(1)}, u32[]{:S(2)}, u32[]{:S(2)}) %collective-permute-start.13) | collective-permute-done | bytes 131104 | tf_op jit(solution)/shard_map/ppermute | solution.py:29
  62.4 3.4 %experts.3 = (bf16[128,512]{1,0:T(8,128)(2,1)S(1)}, bf16[128,512]{1,0:T(8,128)(2,1)S(1)}, bf16[128,512]{1,0:T(8,128)(2,1)S(1)}, bf16[128,512]{1,0:T(8,128)(2,1)S...) custom-call(s32[7]{0:T(128)S(1)} %stack.40.place, ...), custom_call_target="tpu_custom_call" | custom-call | tf_op jit(solution)/shard_map/experts/pallas_call | solution.py:45
  65.9 2.7 %experts.4 = (bf16[128,512]{1,0:T(8,128)(2,1)S(1)}, bf16[128,512]{1,0:T(8,128)(2,1)S(1)}, bf16[4,128,512]{2,1,0:T(8,128)(2,1)S(1)}, bf16[4,128,512]{2,1,0:T(8,128)(2,1)S(1)}, bf16[4,128,512]{2,1,0:T(8,128)(2,1)S(1)}) custom-call(s32[7]{0:T(128)S(1)} %stack.40.place, bf16[128,512]{1,0:T(8,128)(2,1)S(1)} %collective-permute-done.13.refs_0_.refs_2_, ...), custom_call_target="tpu_custom_call" | custom-call | tf_op jit(solution)/shard_map/experts/pallas_call | solution.py:45
  68.6 1.9 %collective-permute-start.23 = (bf16[128,512]{1,0:T(8,128)(2,1)S(1)}, bf16[128,512]{1,0:T(8,128)(2,1)S(1)}, u32[]{:S(2)}, u32[]{:S(2)}) collective-permute-start(bf16[128,512]{1,0:T(8,128)(2,1)S(1)} %get-tuple-element.70), channel_id=1, source_target_pairs={{0,8},{1,9},{2,10},{3,11},{4,12},{5,13},{6,14},{7,15},{8,0},{9,1},... | collective-permute-start | bytes 393224 | tf_op jit(solution)/shard_map/ppermute | solution.py:29
  70.5 2.5 %collective-permute-start.22 = (bf16[128,512]{1,0:T(8,128)(2,1)S(1)}, bf16[128,512]{1,0:T(8,128)(2,1)S(1)}, u32[]{:S(2)}, u32[]{:S(2)}) collective-permute-start(bf16[128,512]{1,0:T(8,128)(2,1)S(1)} %get-tuple-element.68), channel_id=1, source_target_pairs={{0,12},{1,13},{2,14},{3,15},{4,0},{5,1},{6,2},{7,3},{8,4},{9,5},{1... | collective-permute-start | bytes 393224 | tf_op jit(solution)/shard_map/ppermute | solution.py:29
  73.0 1.9 %collective-permute-done.21.side_down = bf16[512,512]{1,0:T(8,128)(2,1)S(1)} collective-permute-done((bf16[512,512]{1,0:T(8,128)(2,1)S(1)}, bf16[512,512]{1,0:T(8,128)(2,1)S(1)}, u32[]{:S(2)}, u32[]{:S(2)}) %collective-permute-start.21) | collective-permute-done | bytes 524320 | tf_op jit(solution)/shard_map/ppermute | solution.py:33
  74.9 2.7 %experts.5 = (f32[128,512]{1,0:T(8,128)S(1)}, f32[128,512]{1,0:T(8,128)S(1)}, bf16[4,128,512]{2,1,0:T(8,128)(2,1)S(1)}, bf16[4,128,512]{2,1,0:T(8,128)(2,1)S(1)}, bf16[4,128,512]{2,1,0:T(8,128)(2,1)S(1)}) custom-call(s32[7]{0:T(128)S(1)} %stack.40.place, bf16[128,512]{1,0:T(8,128)(2,1)S(1)} %fusion.1.refs_0_.refs_3_, bf16[144,512]{1,0:T(8,128)(2,1)S(1)} %payload.1.refs_1_, ...), custom_call_target="tpu_custom_call" | custom-call | tf_op jit(solution)/shard_map/experts/pallas_call | solution.py:45
  77.6 2.9 %weight_grads.1 = (f32[2,512,512]{2,1,0:T(8,128)S(1)}, f32[2,512,512]{2,1,0:T(8,128)S(1)}, bf16[4,512,512]{2,1,0:T(8,128)(2,1)S(1)}) custom-call(s32[7]{0:T(128)S(1)} %stack.40.place, bf16[128,512]{1,0:T(8,128)(2,1)S(1)} %collective-permute-done.14.refs_0_, bf16[128,512]{1,0:T(8,128)(2,1)S(1)} %collective-permute-done.15.refs_1_, ...), custom_call_target="tpu_custom_call" | custom-call | tf_op jit(solution)/shard_map/weight_grads/pallas_call | solution.py:45
  80.7 2.9 %collective-permute-start.18 = (bf16[128,512]{1,0:T(8,128)(2,1)S(1)}, bf16[128,512]{1,0:T(8,128)(2,1)S(1)}, u32[]{:S(2)}, u32[]{:S(2)}) collective-permute-start(bf16[128,512]{1,0:T(8,128)(2,1)S(1)} %get-tuple-element.73), channel_id=1, source_target_pairs={{0,12},{1,13},{2,14},{3,15},{4,0},{5,1},{6,2},{7,3},{8,4},{9,5},{1... | collective-permute-start | bytes 393224 | tf_op jit(solution)/shard_map/ppermute | solution.py:29
  86.7 2.2 %collective-permute-done.25.refs_5_ = bf16[128,512]{1,0:T(8,128)(2,1)S(1)} collective-permute-done((bf16[128,512]{1,0:T(8,128)(2,1)S(1)}, bf16[128,512]{1,0:T(8,128)(2,1)S(1)}, u32[]{:S(2)}, u32[]{:S(2)}) %collective-permute-start.25) | collective-permute-done | bytes 131104 | tf_op jit(solution)/shard_map/ppermute | solution.py:33
  91.0 2.6 %collective-permute-start.19 = (bf16[128,512]{1,0:T(8,128)(2,1)S(1)}, bf16[128,512]{1,0:T(8,128)(2,1)S(1)}, u32[]{:S(2)}, u32[]{:S(2)}) collective-permute-start(bf16[128,512]{1,0:T(8,128)(2,1)S(1)} %get-tuple-element.74), channel_id=1, source_target_pairs={{0,8},{1,9},{2,10},{3,11},{4,12},{5,13},{6,14},{7,15},{8,0},{9,1},... | collective-permute-start | bytes 393224 | tf_op jit(solution)/shard_map/ppermute | solution.py:29
  93.7 5.6 %collective-permute-done.20 = bf16[128,512]{1,0:T(8,128)(2,1)S(1)} collective-permute-done((bf16[128,512]{1,0:T(8,128)(2,1)S(1)}, bf16[128,512]{1,0:T(8,128)(2,1)S(1)}, u32[]{:S(2)}, u32[]{:S(2)}) %collective-permute-start.20) | collective-permute-done | bytes 131104 | tf_op jit(solution)/shard_map/ppermute | solution.py:29
  99.2 4.2 %collective-permute-done.19 = bf16[128,512]{1,0:T(8,128)(2,1)S(1)} collective-permute-done((bf16[128,512]{1,0:T(8,128)(2,1)S(1)}, bf16[128,512]{1,0:T(8,128)(2,1)S(1)}, u32[]{:S(2)}, u32[]{:S(2)}) %collective-permute-start.19) | collective-permute-done | bytes 131104 | tf_op jit(solution)/shard_map/ppermute | solution.py:29
  108.8 7.8 %collective-permute-done.29 = bf16[128,512]{1,0:T(8,128)(2,1)S(1)} collective-permute-done((bf16[128,512]{1,0:T(8,128)(2,1)S(1)}, bf16[128,512]{1,0:T(8,128)(2,1)S(1)}, u32[]{:S(2)}, u32[]{:S(2)}) %collective-permute-start.29) | collective-permute-done | bytes 131104 | tf_op jit(solution)/shard_map/ppermute | solution.py:29
  (80 shorter events, 32.3 us)
Async XLA Ops:
  0.6 20.8 %collective-permute-start = (bf16[512,512]{1,0:T(8,128)(2,1)}, bf16[512,512]{1,0:T(8,128)(2,1)S(1)}, u32[]{:S(2)}, u32[]{:S(2)}) collective-permute-start(bf16[512,512]{1,0:T(8,128)(2,1)} %bitcast.30), channel_id=1, source_target_pairs={{0,2},{1,3},{2,0},{3,1},{4,6},{5,7},{6,4},{7,5},{8,10},{9,11},{10,... | collective-permute-start | bytes 1572872 | tf_op jit(solution)/shard_map/ppermute | solution.py:33
  5.7 15.7 %collective-permute-start.1 = (bf16[2,128,512]{2,1,0:T(8,128)(2,1)S(1)}, bf16[2,128,512]{2,1,0:T(8,128)(2,1)S(1)}, u32[]{:S(2)}, u32[]{:S(2)}) collective-permute-start(bf16[2,128,512]{2,1,0:T(8,128)(2,1)S(1)} %get-tuple-element.58), channel_id=1, source_target_pairs={{0,2},{1,3},{2,0},{3,1},{4,6},{5,7},{6,4},{7,5},{8,10},{9,11},{10,... | collective-permute-start | bytes 786440 | tf_op jit(solution)/shard_map/ppermute | solution.py:33
  5.8 16.2 %collective-permute-start.5 = (bf16[128,512]{1,0:T(8,128)(2,1)}, bf16[128,512]{1,0:T(8,128)(2,1)S(1)}, u32[]{:S(2)}, u32[]{:S(2)}) collective-permute-start(bf16[128,512]{1,0:T(8,128)(2,1)} %refs_4_.1), channel_id=1, source_target_pairs={{0,8},{1,9},{2,10},{3,11},{4,12},{5,13},{6,14},{7,15},{8,0},{9,1},... | collective-permute-start | bytes 393224 | tf_op jit(solution)/shard_map/ppermute | solution.py:29
  8.9 13.2 %collective-permute-start.4 = (bf16[128,512]{1,0:T(8,128)(2,1)}, bf16[128,512]{1,0:T(8,128)(2,1)S(1)}, u32[]{:S(2)}, u32[]{:S(2)}) collective-permute-start(bf16[128,512]{1,0:T(8,128)(2,1)} %refs_4_.1), channel_id=1, source_target_pairs={{0,4},{1,5},{2,6},{3,7},{4,8},{5,9},{6,10},{7,11},{8,12},{9,13},{1... | collective-permute-start | bytes 393224 | tf_op jit(solution)/shard_map/ppermute | solution.py:29
  10.4 11.6 %collective-permute-start.6 = (bf16[128,512]{1,0:T(8,128)(2,1)}, bf16[128,512]{1,0:T(8,128)(2,1)S(1)}, u32[]{:S(2)}, u32[]{:S(2)}) collective-permute-start(bf16[128,512]{1,0:T(8,128)(2,1)} %refs_4_.1), channel_id=1, source_target_pairs={{0,12},{1,13},{2,14},{3,15},{4,0},{5,1},{6,2},{7,3},{8,4},{9,5},{1... | collective-permute-start | bytes 393224 | tf_op jit(solution)/shard_map/ppermute | solution.py:29
  27.0 19.0 %collective-permute-start.9 = (bf16[3,512,512]{2,1,0:T(8,128)(2,1)S(1)}, bf16[3,512,512]{2,1,0:T(8,128)(2,1)S(1)}, u32[]{:S(2)}, u32[]{:S(2)}) collective-permute-start(bf16[3,512,512]{2,1,0:T(8,128)(2,1)S(1)} %pad_maximum_fusion.refs_4_.refs_2_), channel_id=1, source_target_pairs={{0,1},{1,0},{2,3},{3,2},{4,5},{5,4},{6,7},{7,6},{8,9},{9,8},{10,11... | collective-permute-start | bytes 4718600 | tf_op jit(solution)/shard_map/ppermute | solution.py:33
  27.4 18.6 %collective-permute-start.8 = (f32[128,512]{1,0:T(8,128)S(1)}, f32[128,512]{1,0:T(8,128)S(1)}, u32[]{:S(2)}, u32[]{:S(2)}) collective-permute-start(f32[128,512]{1,0:T(8,128)S(1)} %slice_bitcast_fusion), channel_id=1, source_target_pairs={{0,2},{1,3},{2,0},{3,1},{4,6},{5,7},{6,4},{7,5},{8,10},{9,11},{10,... | collective-permute-start | bytes 786440 | tf_op jit(solution)/shard_map/ppermute | solution.py:33
  33.5 12.5 %collective-permute-start.11 = (bf16[144,512]{1,0:T(8,128)(2,1)S(1)}, bf16[144,512]{1,0:T(8,128)(2,1)S(1)}, u32[]{:S(2)}, u32[]{:S(2)}) collective-permute-start(bf16[144,512]{1,0:T(8,128)(2,1)S(1)} %payload.1.refs_1_), channel_id=1, source_target_pairs={{0,8},{1,9},{2,10},{3,11},{4,12},{5,13},{6,14},{7,15},{8,0},{9,1},... | collective-permute-start | bytes 442376 | tf_op jit(solution)/shard_map/ppermute | solution.py:29
  33.5 12.5 %collective-permute-start.10 = (bf16[144,512]{1,0:T(8,128)(2,1)S(1)}, bf16[144,512]{1,0:T(8,128)(2,1)S(1)}, u32[]{:S(2)}, u32[]{:S(2)}) collective-permute-start(bf16[144,512]{1,0:T(8,128)(2,1)S(1)} %payload.1.refs_1_), channel_id=1, source_target_pairs={{0,4},{1,5},{2,6},{3,7},{4,8},{5,9},{6,10},{7,11},{8,12},{9,13},{1... | collective-permute-start | bytes 442376 | tf_op jit(solution)/shard_map/ppermute | solution.py:29
  46.0 14.5 %collective-permute-start.16 = (bf16[512,512]{1,0:T(8,128)(2,1)S(1)}, bf16[512,512]{1,0:T(8,128)(2,1)S(1)}, u32[]{:S(2)}, u32[]{:S(2)}) collective-permute-start(bf16[512,512]{1,0:T(8,128)(2,1)S(1)} %bitcast.31), channel_id=1, source_target_pairs={{0,2},{1,3},{2,0},{3,1},{4,6},{5,7},{6,4},{7,5},{8,10},{9,11},{10,... | collective-permute-start | bytes 1572872 | tf_op jit(solution)/shard_map/ppermute | solution.py:33
  48.0 9.4 %collective-permute-start.14 = (bf16[128,512]{1,0:T(8,128)(2,1)S(1)}, bf16[128,512]{1,0:T(8,128)(2,1)S(1)}, u32[]{:S(2)}, u32[]{:S(2)}) collective-permute-start(bf16[128,512]{1,0:T(8,128)(2,1)S(1)} %fusion.1.refs_0_.refs_3_), channel_id=1, source_target_pairs={{0,4},{1,5},{2,6},{3,7},{4,8},{5,9},{6,10},{7,11},{8,12},{9,13},{1... | collective-permute-start | bytes 393224 | tf_op jit(solution)/shard_map/ppermute | solution.py:29
  48.7 11.9 %collective-permute-start.13 = (bf16[128,512]{1,0:T(8,128)(2,1)S(1)}, bf16[128,512]{1,0:T(8,128)(2,1)S(1)}, u32[]{:S(2)}, u32[]{:S(2)}) collective-permute-start(bf16[128,512]{1,0:T(8,128)(2,1)S(1)} %fusion.1.refs_0_.refs_3_), channel_id=1, source_target_pairs={{0,8},{1,9},{2,10},{3,11},{4,12},{5,13},{6,14},{7,15},{8,0},{9,1},... | collective-permute-start | bytes 393224 | tf_op jit(solution)/shard_map/ppermute | solution.py:29
  60.5 14.3 %collective-permute-start.21 = (bf16[512,512]{1,0:T(8,128)(2,1)S(1)}, bf16[512,512]{1,0:T(8,128)(2,1)S(1)}, u32[]{:S(2)}, u32[]{:S(2)}) collective-permute-start(bf16[512,512]{1,0:T(8,128)(2,1)S(1)} %get-tuple-element.78.down), channel_id=1, source_target_pairs={{0,2},{1,3},{2,0},{3,1},{4,6},{5,7},{6,4},{7,5},{8,10},{9,11},{10,... | collective-permute-start | bytes 1572872 | tf_op jit(solution)/shard_map/ppermute | solution.py:33
  65.9 14.6 %collective-permute-start.24 = (bf16[128,512]{1,0:T(8,128)(2,1)S(1)}, bf16[128,512]{1,0:T(8,128)(2,1)S(1)}, u32[]{:S(2)}, u32[]{:S(2)}) collective-permute-start(bf16[128,512]{1,0:T(8,128)(2,1)S(1)} %get-tuple-element.93), channel_id=1, source_target_pairs={{0,4},{1,5},{2,6},{3,7},{4,8},{5,9},{6,10},{7,11},{8,12},{9,13},{1... | collective-permute-start | bytes 393224 | tf_op jit(solution)/shard_map/ppermute | solution.py:29
  68.6 11.9 %collective-permute-start.23 = (bf16[128,512]{1,0:T(8,128)(2,1)S(1)}, bf16[128,512]{1,0:T(8,128)(2,1)S(1)}, u32[]{:S(2)}, u32[]{:S(2)}) collective-permute-start(bf16[128,512]{1,0:T(8,128)(2,1)S(1)} %get-tuple-element.70), channel_id=1, source_target_pairs={{0,8},{1,9},{2,10},{3,11},{4,12},{5,13},{6,14},{7,15},{8,0},{9,1},... | collective-permute-start | bytes 393224 | tf_op jit(solution)/shard_map/ppermute | solution.py:29
  70.5 10.0 %collective-permute-start.22 = (bf16[128,512]{1,0:T(8,128)(2,1)S(1)}, bf16[128,512]{1,0:T(8,128)(2,1)S(1)}, u32[]{:S(2)}, u32[]{:S(2)}) collective-permute-start(bf16[128,512]{1,0:T(8,128)(2,1)S(1)} %get-tuple-element.68), channel_id=1, source_target_pairs={{0,12},{1,13},{2,14},{3,15},{4,0},{5,1},{6,2},{7,3},{8,4},{9,5},{1... | collective-permute-start | bytes 393224 | tf_op jit(solution)/shard_map/ppermute | solution.py:29
  89.3 29.6 %collective-permute-start.32 = (bf16[2,512,512]{2,1,0:T(8,128)(2,1)S(1)}, bf16[2,512,512]{2,1,0:T(8,128)(2,1)S(1)}, u32[]{:S(2)}, u32[]{:S(2)}) collective-permute-start(bf16[2,512,512]{2,1,0:T(8,128)(2,1)S(1)} %add_convert_fusion.1), channel_id=1, source_target_pairs={{0,2},{1,3},{2,0},{3,1},{4,6},{5,7},{6,4},{7,5},{8,10},{9,11},{10,... | collective-permute-start | bytes 3145736 | tf_op jit(solution)/shard_map/ppermute | solution.py:33
  90.9 12.5 %collective-permute-start.26 = (bf16[2,128,512]{2,1,0:T(8,128)(2,1)S(1)}, bf16[2,128,512]{2,1,0:T(8,128)(2,1)S(1)}, u32[]{:S(2)}, u32[]{:S(2)}) collective-permute-start(bf16[2,128,512]{2,1,0:T(8,128)(2,1)S(1)} %pad_maximum_fusion.1), channel_id=1, source_target_pairs={{0,1},{1,0},{2,3},{3,2},{4,5},{5,4},{6,7},{7,6},{8,9},{9,8},{10,11... | collective-permute-start | bytes 786440 | tf_op jit(solution)/shard_map/ppermute | solution.py:33
  91.0 8.2 %collective-permute-start.20 = (bf16[128,512]{1,0:T(8,128)(2,1)S(1)}, bf16[128,512]{1,0:T(8,128)(2,1)S(1)}, u32[]{:S(2)}, u32[]{:S(2)}) collective-permute-start(bf16[128,512]{1,0:T(8,128)(2,1)S(1)} %get-tuple-element.75), channel_id=1, source_target_pairs={{0,4},{1,5},{2,6},{3,7},{4,8},{5,9},{6,10},{7,11},{8,12},{9,13},{1... | collective-permute-start | bytes 393224 | tf_op jit(solution)/shard_map/ppermute | solution.py:29
  91.0 12.4 %collective-permute-start.19 = (bf16[128,512]{1,0:T(8,128)(2,1)S(1)}, bf16[128,512]{1,0:T(8,128)(2,1)S(1)}, u32[]{:S(2)}, u32[]{:S(2)}) collective-permute-start(bf16[128,512]{1,0:T(8,128)(2,1)S(1)} %get-tuple-element.74), channel_id=1, source_target_pairs={{0,8},{1,9},{2,10},{3,11},{4,12},{5,13},{6,14},{7,15},{8,0},{9,1},... | collective-permute-start | bytes 393224 | tf_op jit(solution)/shard_map/ppermute | solution.py:29
  104.6 12.0 %collective-permute-start.28 = (bf16[128,512]{1,0:T(8,128)(2,1)S(1)}, bf16[128,512]{1,0:T(8,128)(2,1)S(1)}, u32[]{:S(2)}, u32[]{:S(2)}) collective-permute-start(bf16[128,512]{1,0:T(8,128)(2,1)S(1)} %get-tuple-element.96), channel_id=1, source_target_pairs={{0,12},{1,13},{2,14},{3,15},{4,0},{5,1},{6,2},{7,3},{8,4},{9,5},{1... | collective-permute-start | bytes 393224 | tf_op jit(solution)/shard_map/ppermute | solution.py:29
  105.4 11.2 %collective-permute-start.29 = (bf16[128,512]{1,0:T(8,128)(2,1)S(1)}, bf16[128,512]{1,0:T(8,128)(2,1)S(1)}, u32[]{:S(2)}, u32[]{:S(2)}) collective-permute-start(bf16[128,512]{1,0:T(8,128)(2,1)S(1)} %get-tuple-element.101), channel_id=1, source_target_pairs={{0,8},{1,9},{2,10},{3,11},{4,12},{5,13},{6,14},{7,15},{8,0},{9,1},... | collective-permute-start | bytes 393224 | tf_op jit(solution)/shard_map/ppermute | solution.py:29
  105.4 11.2 %collective-permute-start.30 = (bf16[128,512]{1,0:T(8,128)(2,1)S(1)}, bf16[128,512]{1,0:T(8,128)(2,1)S(1)}, u32[]{:S(2)}, u32[]{:S(2)}) collective-permute-start(bf16[128,512]{1,0:T(8,128)(2,1)S(1)} %get-tuple-element.102), channel_id=1, source_target_pairs={{0,4},{1,5},{2,6},{3,7},{4,8},{5,9},{6,10},{7,11},{8,12},{9,13},{1... | collective-permute-start | bytes 393224 | tf_op jit(solution)/shard_map/ppermute | solution.py:29
  108.0 9.4 %collective-permute-start.27 = (bf16[2,128,512]{2,1,0:T(8,128)(2,1)S(1)}, bf16[2,128,512]{2,1,0:T(8,128)(2,1)S(1)}, u32[]{:S(2)}, u32[]{:S(2)}) collective-permute-start(bf16[2,128,512]{2,1,0:T(8,128)(2,1)S(1)} %get-tuple-element.99), channel_id=1, source_target_pairs={{0,1},{1,0},{2,3},{3,2},{4,5},{5,4},{6,7},{7,6},{8,9},{9,8},{10,11... | collective-permute-start | bytes 786440 | tf_op jit(solution)/shard_map/ppermute | solution.py:33
  (16 other events, 92.8 us)

commit v8 on v6

--- a/solution.py
+++ b/solution.py
@@ -118,8 +118,7 @@
     own, core, *sides = refs[2 * count : 2 * count + 6]
     weights = (own.at[0], own.at[1], sides[0], sides[1], core.at[0], core.at[1], sides[2], sides[3])
     outs = refs[2 * count + 6 :]
-    combined, deltas = outs[:count], outs[count : 2 * count]
-    hiddens, scaleds, back_pres = outs[2 * count :]
+    *sums, hiddens, scaleds, back_pres = outs
     tok_rows, width = rows_in[0].shape
     for first in range(0, count, 2):
         group = range(first, min(first + 2, count))
@@ -147,8 +146,10 @@
             delta_sum = delta_sum + back_rows.astype(narrow).astype(wide)
         for i in group:
             part = slice((i - first) * tok_rows, (i - first + 1) * tok_rows)
-            combined[i][...] = out_sum[part].astype(combined[i].dtype)
-            deltas[i][...] = delta_sum[part].astype(deltas[i].dtype)
+            out = sums.pop(0)
+            delta_out, sum_out = (out, sums.pop(0)) if len(out.shape) == 2 else (out.at[0], out.at[1])
+            delta_out[...] = delta_sum[part].astype(out.dtype)
+            sum_out[...] = out_sum[part].astype(out.dtype)
 
 
 def weight_grad_body(n_rows, n_sets, place, *refs):
@@ -185,21 +186,14 @@
                 blocks[back][...] = part[z * block : (z + 1) * block].astype(blocks[back].dtype)
 
 
-def token_grad_body(place, delta, core_deltas, down, side_down, own, other):
-    for rows, out in ((core_deltas[0], other), (delta[...], own)):
-        for side, weight in enumerate((down, side_down)):
-            out[side] = lax.dot_general(
-                rows, weight[...], contract_last, preferred_element_type=wide
-            ).astype(narrow)
-
-
-def arrange_body(n_line, block, place, own, other, out):
-    for core, pieces in enumerate((own, other)):
-        for side in range(2):
-            owner = (place[1] ^ side) * 2 + (place[2] ^ core)
-            for z in range(n_line):
-                start = pl.multiple_of((z * 4 + owner) * block, block)
-                out[:, pl.ds(start, block)] = pieces[side, :, z * block : (z + 1) * block]
+def token_grad_body(n_line, block, place, delta, downs, core_downs, out):
+    for i, weight in enumerate((downs.at[0], downs.at[1], core_downs.at[0], core_downs.at[1])):
+        owner = (place[1] ^ (i % 2)) * 2 + (place[2] ^ (i // 2))
+        part = lax.dot_general(delta[...], weight[...], contract_last, preferred_element_type=wide)
+        part = part.astype(narrow)
+        for z in range(n_line):
+            start = pl.multiple_of((z * 4 + owner) * block, block)
+            out[:, pl.ds(start, block)] = part[:, z * block : (z + 1) * block]
 
 
 def all_rows(tokens, routes, gate_levels, latent_grad, down_weight, expert_in, expert_out):
@@ -232,9 +226,11 @@
     (payload,) = call(payload_body, [shape((tok_rows + gate_rows, latent_width), narrow)], "payload")(
         place, routes.T, gate_levels.T, latent_grad
     )
+    own = jnp.concatenate([expert_in, expert_out])
+    core_own = swap(own, n_line, 1, 0)
     across = swap(columns[2], n_line, 0, 1)
-    near_tokens = [columns[0], across[0], swap(after(columns[1], across), n_line, 1, 0), swap(across[1], n_line, 1, 0)]
-    side_in = swap(after(expert_in[0], across, near_tokens[2]), n_line, 0, 1)
+    near_tokens = [columns[0], across[0], swap(after(columns[1], across, core_own), n_line, 1, 0), swap(across[1], n_line, 1, 0)]
+    side_in = swap(after(expert_in[0], near_tokens[2]), n_line, 0, 1)
 
     project = call(
         functools.partial(project_body, n_line),
@@ -242,43 +238,46 @@
         "project",
     )
     keep, send, down = project(place, *near_tokens, *downs)
-    half = keep + after(swap(send, n_line, 1, 0), side_in)
-    payloads = [payload] + [turn(after(payload, half), n_line, back) for back in range(1, n_line)]
-    own = jnp.concatenate([expert_in, expert_out])
-    core_own = swap(after(own, half), n_line, 1, 0)
-    latent = (half[0] + after(swap(half[1], n_line, 0, 1), core_own, *payloads[1:])).astype(narrow)
-    ends = [1, n_line - 1]
+    half = keep + swap(send, n_line, 1, 0)
+    payloads = [payload] + [turn(after(payload, *downs[1:]), n_line, back) for back in range(1, n_line)]
+    crossed = swap(half[1].astype(narrow), n_line, 0, 1).astype(wide)
+    latent = (half[0] + after(crossed, side_in, *payloads[1:])).astype(narrow)
     middle = list(range(2, n_line - 1))
-    groups = [ends, middle, [0]]
+    groups = [[1] + middle, [n_line - 1, 0]]
     rows = [latent] + [turn(latent, n_line, back) for back in range(1, n_line)]
 
     side_out = swap(after(expert_out[0], latent), n_line, 0, 1)
-    far_in = swap(after(side_in, latent), n_line, 1, 0)
-    far_out = swap(after(side_out, *rows[1:]), n_line, 1, 0)
-    weights = [own, core_own, side_in, side_out, far_in, far_out]
+    core_in = swap(after(side_in, latent), n_line, 1, 0)
+    core_out = swap(after(side_out, *rows[1:]), n_line, 1, 0)
+    weights = [own, core_own, side_in, side_out, core_in, core_out]
     side_down = swap(after(down, side_out), n_line, 0, 1)
-
-    outs_of, deltas_of, saved = [None] * n_line, [None] * n_line, []
+    both_down = jnp.stack([down, side_down])
+    core_down = swap(both_down, n_line, 1, 0)
+
+    sums, saved = [None] * n_line, []
+    done = latent
     for group in groups:
         count = len(group)
-        kind = narrow if group[0] else wide
-        if group == middle:
-            rows[group[0]] = after(rows[group[0]], deltas_of[1])
-        if not group[0]:
-            rows[0] = after(latent, deltas_of[middle[0]])
+        outs = []
+        for back in group:
+            kind = narrow if back else wide
+            outs += [rows_of(kind)] * 2 if back in middle else [shape((2, tok_rows, latent_width), kind)]
         values = call(
             functools.partial(expert_body, count),
-            [rows_of(kind)] * (2 * count) + [shape((4, count * tok_rows, hidden_width), narrow)] * 3,
+            outs + [shape((4, count * tok_rows, hidden_width), narrow)] * 3,
             "experts",
-        )(place, *(rows[i] for i in group), *(payloads[i] for i in group), *weights)
-        for i, back in enumerate(group):
-            outs_of[back], deltas_of[back] = values[i], values[count + i]
-        saved.append(list(values[2 * count :]))
-
-    def home(value, back):
-        return turn(value, n_line, n_line - back) if back else value
-
-    delta_lines = [home(value, back) for back, value in enumerate(deltas_of)]
+        )(after(place, done), *(rows[i] for i in group), *(payloads[i] for i in group), *weights)
+        done, saved = values[0], saved + [list(values[-3:])]
+        values = list(values[:-3])
+        for back in group:
+            sums[back] = [values.pop(0) for _ in range(2 if back in middle else 1)]
+
+    lines = [
+        [turn(value, n_line, n_line - back) if back else value for value in values]
+        for back, values in enumerate(sums)
+    ]
+    delta_lines = [values[0] if len(values) == 2 else values[0][0] for values in lines]
+    out_lines = [values[1] if len(values) == 2 else values[0][1] for values in lines]
 
     pair = (2, latent_width, hidden_width)
     near, far, other = call(
@@ -286,32 +285,28 @@
         [shape(pair, wide)] * 2 + [shape((4, latent_width, hidden_width), narrow)],
         "weight_grads",
     )(
-        after(place, side_down),
+        after(place, delta_lines[1]),
         *(rows[i] for group in groups for i in group),
         *(value for values in saved for value in values),
     )
-    delta_lines = [after(line, near) for line in delta_lines]
+    delta_lines = [after(line, near, both_down) for line in delta_lines]
     delta = sum(line.astype(wide) for line in delta_lines).astype(narrow)
     side_delta = swap(delta, n_line, 0, 1)
-    out_lines = [outs_of[0]] + [home(after(outs_of[back], delta), back) for back in range(1, n_line)]
     latent_out = sum(line.astype(wide) for line in out_lines).astype(narrow)
     other = swap(after(other, delta), n_line, 1, 0)
-    far = swap((far + other[2:].astype(wide)).astype(narrow), n_line, 0, 1)
-    core_deltas = swap(jnp.stack([delta, after(side_delta, out_lines[1], out_lines[-1])]), n_line, 1, 0)
+    far = (far + other[2:].astype(wide)).astype(narrow)
+    far = swap(after(far, side_delta, *(out_lines[back] for back in middle)), n_line, 0, 1)
+    core_deltas = swap(jnp.stack([delta, after(side_delta, *(out_lines[back] for back in middle))]), n_line, 1, 0)
     blocks = call(
         functools.partial(down_grad_body, n_line),
         [shape((block, latent_width), wide)] + [shape((block, latent_width), narrow)] * (n_line - 1),
         "down_grad",
-    )(after(place, *out_lines[1:]), *near_tokens, delta, side_delta, core_deltas)
+    )(after(place, *(out_lines[back] for back in middle)), *near_tokens, delta, side_delta, core_deltas)
     weight_grad = (near + other[:2].astype(wide) + far.astype(wide)).astype(narrow)
-    both = [shape((2, tok_rows, n_line * block), narrow)] * 2
-    own_grads, core_grads = call(token_grad_body, both, "token_grad")(
-        place, after(delta, blocks[1]), core_deltas, down, side_down
-    )
     (grad_tokens,) = call(
-        functools.partial(arrange_body, n_line, block), [shape((tok_rows, width), narrow)], "arrange"
-    )(place, own_grads, swap(core_grads, n_line, 1, 0))
-    blocks = [blocks[0]] + [home(blocks[back], back) for back in range(1, n_line)]
+        functools.partial(token_grad_body, n_line, block), [shape((tok_rows, width), narrow)], "token_grad"
+    )(place, after(delta, blocks[1]), both_down, core_down)
+    blocks = [blocks[0]] + [turn(blocks[back], n_line, n_line - back) for back in range(1, n_line)]
     grad_down = sum(value.astype(wide) for value in blocks)
     return (latent_out, grad_tokens, grad_down, weight_grad[:1], weight_grad[1:])
 

time: 143 us -> 116 us (0.81)
  waiting for transfers between devices: 79.3 us -> 56.4 us
  Pallas kernels: 18.2 us -> 15.5 us
    ppermute x16, waiting for transfers between devices: 31 us -> 19.3 us  [swap(): lax.ppermute(value, plane, device_pairs(n_line, lambda z, x, c: (z, x ^ s...]
    ppermute x18 -> x16, waiting for transfers between devices: 48.3 us -> 37.1 us  [turn(): lax.ppermute(value, plane, device_pairs(n_line, lambda z, x, c: ((z + by)...]
    pallas_call x10 -> x8, Pallas kernels: 18.2 us -> 15.5 us  [run(): pl.pallas_call(body, out_shape=outs, in_specs=[pl.BlockSpec(memory_space=...]
    ppermute x18 -> x16, starting transfers between devices: 27.1 us -> 26.4 us  [turn(): lax.ppermute(value, plane, device_pairs(n_line, lambda z, x, c: ((z + by)...]
  transfers between devices with their start and end apart: 34 -> 32, of which waited for: 17 -> 17; matrix products, arithmetic and copies ran while one was open for 1% -> 2% of each run, Pallas kernels for 12% -> 12%
where the time goes in v8:
time: 116 us
  waiting for transfers between devices  56.4 us (49%)
  starting transfers between devices  37.2 us (32%)
  Pallas kernels  15.5 us (13%)
  local copies, waits for them, and re-layouts  3.47 us (3%)
  other arithmetic  2.66 us (2%)
    ppermute x16, waiting for transfers between devices, turn(): lax.ppermute(value, plane, device_pairs(n_line, lambda z, x, c: ((z + by)...  37.1 us
    ppermute x16, starting transfers between devices, turn(): lax.ppermute(value, plane, device_pairs(n_line, lambda z, x, c: ((z + by)...  26.4 us
    ppermute x16, waiting for transfers between devices, swap(): lax.ppermute(value, plane, device_pairs(n_line, lambda z, x, c: (z, x ^ s...  19.3 us
    pallas_call x8, Pallas kernels, run(): pl.pallas_call(body, out_shape=outs, in_specs=[pl.BlockSpec(memory_space=...  15.5 us
    ppermute x16, starting transfers between devices, swap(): lax.ppermute(value, plane, device_pairs(n_line, lambda z, x, c: (z, x ^ s...  10.8 us
  transfers between devices with their start and end apart: 32, of which 17 were waited for; matrix products, arithmetic and copies ran while one was open for 2% of the time, Pallas kernels for 12%

profile of v8, /device:TPU:0, one launch (start us, length us, event | category | flops | bytes accessed | tf_op | source)
XLA Modules:
  0.0 116.2 jit_solution(12571792476278373537)
XLA Ops:
  4.4 2.6 %collective-permute-start = (bf16[2,128,512]{2,1,0:T(8,128)(2,1)S(1)}, bf16[2,128,512]{2,1,0:T(8,128)(2,1)S(1)}, u32[]{:S(2)}, u32[]{:S(2)}) collective-permute-start(bf16[2,128,512]{2,1,0:T(8,128)(2,1)S(1)} %get-tuple-element.50), channel_id=1, source_target_pairs={{0,2},{1,3},{2,0},{3,1},{4,6},{5,7},{6,4},{7,5},{8,10},{9,11},{10,... | collective-permute-start | bytes 786440 | tf_op jit(solution)/shard_map/ppermute | solution.py:33
  8.6 2.6 %collective-permute-start.5 = (bf16[128,512]{1,0:T(8,128)(2,1)S(1)}, bf16[128,512]{1,0:T(8,128)(2,1)S(1)}, u32[]{:S(2)}, u32[]{:S(2)}) collective-permute-start(bf16[128,512]{1,0:T(8,128)(2,1)S(1)} %copy-done.2), channel_id=1, source_target_pairs={{0,8},{1,9},{2,10},{3,11},{4,12},{5,13},{6,14},{7,15},{8,0},{9,1},... | collective-permute-start | bytes 393224 | tf_op jit(solution)/shard_map/ppermute | solution.py:29
  15.3 4.9 %collective-permute-done.5.refs_6_ = bf16[128,512]{1,0:T(8,128)(2,1)S(1)} collective-permute-done((bf16[128,512]{1,0:T(8,128)(2,1)S(1)}, bf16[128,512]{1,0:T(8,128)(2,1)S(1)}, u32[]{:S(2)}, u32[]{:S(2)}) %collective-permute-start.5) | collective-permute-done | bytes 131104 | tf_op jit(solution)/shard_map/ppermute | solution.py:29
  22.5 3.3 %collective-permute-start.10 = (bf16[144,512]{1,0:T(8,128)(2,1)S(1)}, bf16[144,512]{1,0:T(8,128)(2,1)S(1)}, u32[]{:S(2)}, u32[]{:S(2)}) collective-permute-start(bf16[144,512]{1,0:T(8,128)(2,1)S(1)} %payload.1.refs_3_), channel_id=1, source_target_pairs={{0,4},{1,5},{2,6},{3,7},{4,8},{5,9},{6,10},{7,11},{8,12},{9,13},{1... | collective-permute-start | bytes 442376 | tf_op jit(solution)/shard_map/ppermute | solution.py:29
  25.8 1.6 %collective-permute-start.11 = (bf16[144,512]{1,0:T(8,128)(2,1)S(1)}, bf16[144,512]{1,0:T(8,128)(2,1)S(1)}, u32[]{:S(2)}, u32[]{:S(2)}) collective-permute-start(bf16[144,512]{1,0:T(8,128)(2,1)S(1)} %payload.1.refs_3_), channel_id=1, source_target_pairs={{0,8},{1,9},{2,10},{3,11},{4,12},{5,13},{6,14},{7,15},{8,0},{9,1},... | collective-permute-start | bytes 442376 | tf_op jit(solution)/shard_map/ppermute | solution.py:29
  30.0 8.5 %collective-permute-done.8 = bf16[128,512]{1,0:T(8,128)(2,1)S(1)} collective-permute-done((bf16[128,512]{1,0:T(8,128)(2,1)S(1)}, bf16[128,512]{1,0:T(8,128)(2,1)S(1)}, u32[]{:S(2)}, u32[]{:S(2)}) %collective-permute-start.8) | collective-permute-done | bytes 131104 | tf_op jit(solution)/shard_map/ppermute | solution.py:33
  39.2 3.5 %collective-permute-start.13 = (bf16[128,512]{1,0:T(8,128)(2,1)S(1)}, bf16[128,512]{1,0:T(8,128)(2,1)S(1)}, u32[]{:S(2)}, u32[]{:S(2)}) collective-permute-start(bf16[128,512]{1,0:T(8,128)(2,1)S(1)} %fusion.1.refs_1_.refs_3_), channel_id=1, source_target_pairs={{0,4},{1,5},{2,6},{3,7},{4,8},{5,9},{6,10},{7,11},{8,12},{9,13},{1... | collective-permute-start | bytes 393224 | tf_op jit(solution)/shard_map/ppermute | solution.py:29
  45.1 2.7 %collective-permute-done.13.refs_0_ = bf16[128,512]{1,0:T(8,128)(2,1)S(1)} collective-permute-done((bf16[128,512]{1,0:T(8,128)(2,1)S(1)}, bf16[128,512]{1,0:T(8,128)(2,1)S(1)}, u32[]{:S(2)}, u32[]{:S(2)}) %collective-permute-start.13) | collective-permute-done | bytes 131104 | tf_op jit(solution)/shard_map/ppermute | solution.py:29
  47.9 4.4 %collective-permute-done.14.refs_1_ = bf16[128,512]{1,0:T(8,128)(2,1)S(1)} collective-permute-done((bf16[128,512]{1,0:T(8,128)(2,1)S(1)}, bf16[128,512]{1,0:T(8,128)(2,1)S(1)}, u32[]{:S(2)}, u32[]{:S(2)}) %collective-permute-start.14) | collective-permute-done | bytes 131104 | tf_op jit(solution)/shard_map/ppermute | solution.py:29
  54.2 3.4 %experts.2 = (bf16[2,128,512]{2,1,0:T(8,128)(2,1)S(1)}, bf16[128,512]{1,0:T(8,128)(2,1)S(1)}, bf16[128,512]{1,0:T(8,128)(2,1)S(1)}, bf16[4,256,512]{2,1,0:T(8,12...) custom-call(s32[7]{0:T(128)S(1)} %stack.49.place, ...), custom_call_target="tpu_custom_call" | custom-call | tf_op jit(solution)/shard_map/experts/pallas_call | solution.py:45
  57.6 4.7 %collective-permute-start.19 = (bf16[2,128,512]{2,1,0:T(8,128)(2,1)S(1)}, bf16[2,128,512]{2,1,0:T(8,128)(2,1)S(1)}, u32[]{:S(2)}, u32[]{:S(2)}) collective-permute-start(bf16[2,128,512]{2,1,0:T(8,128)(2,1)S(1)} %get-tuple-element.62), channel_id=1, source_target_pairs={{0,12},{1,13},{2,14},{3,15},{4,0},{5,1},{6,2},{7,3},{8,4},{9,5},{1... | collective-permute-start | bytes 786440 | tf_op jit(solution)/shard_map/ppermute | solution.py:29
  62.3 3.4 %experts.3 = (bf16[2,128,512]{2,1,0:T(8,128)(2,1)S(1)}, f32[2,128,512]{2,1,0:T(8,128)S(1)}, bf16[4,256,512]{2,1,0:T(8,128)(2,1)S(1)}, bf16[4,256,512]{2,1,0:T(8,128)(2,1)S(1)}, bf16[4,256,512]{2,1,0:T(8,128)(2,1)S(1)}) custom-call(s32[7]{0:T(128)S(1)} %stack.49.place, bf16[128,512]{1,0:T(8,128)(2,1)S(1)} %collective-permute-done.17.refs_0_.refs_2_, ...), custom_call_target="tpu_custom_call" | custom-call | tf_op jit(solution)/shard_map/experts/pallas_call | solution.py:45
  66.8 2.2 %collective-permute-done.19 = bf16[2,128,512]{2,1,0:T(8,128)(2,1)S(1)} collective-permute-done((bf16[2,128,512]{2,1,0:T(8,128)(2,1)S(1)}, bf16[2,128,512]{2,1,0:T(8,128)(2,1)S(1)}, u32[]{:S(2)}, u32[]{:S(2)}) %collective-permute-start.19) | collective-permute-done | bytes 262176 | tf_op jit(solution)/shard_map/ppermute | solution.py:29
  69.0 2.9 %weight_grads.1 = (f32[2,512,512]{2,1,0:T(8,128)S(1)}, f32[2,512,512]{2,1,0:T(8,128)S(1)}, bf16[4,512,512]{2,1,0:T(8,128)(2,1)S(1)}) custom-call(s32[7]{0:T(128)S(1)} %stack.49.place, bf16[128,512]{1,0:T(8,128)(2,1)S(1)} %collective-permute-done.13.refs_0_, bf16[128,512]{1,0:T(8,128)(2,1)S(1)} %collective-permute-done.14.refs_1_, ...), custom_call_target="tpu_custom_call" | custom-call | tf_op jit(solution)/shard_map/weight_grads/pallas_call | solution.py:45
  71.9 4.8 %collective-permute-done.21 = bf16[2,128,512]{2,1,0:T(8,128)(2,1)S(1)} collective-permute-done((bf16[2,128,512]{2,1,0:T(8,128)(2,1)S(1)}, bf16[2,128,512]{2,1,0:T(8,128)(2,1)S(1)}, u32[]{:S(2)}, u32[]{:S(2)}) %collective-permute-start.21) | collective-permute-done | bytes 262176 | tf_op jit(solution)/shard_map/ppermute | solution.py:29
  76.8 3.6 %collective-permute-done.23 = bf16[128,512]{1,0:T(8,128)(2,1)S(1)} collective-permute-done((bf16[128,512]{1,0:T(8,128)(2,1)S(1)}, bf16[128,512]{1,0:T(8,128)(2,1)S(1)}, u32[]{:S(2)}, u32[]{:S(2)}) %collective-permute-start.23) | collective-permute-done | bytes 131104 | tf_op jit(solution)/shard_map/ppermute | solution.py:29
  82.1 2.6 %collective-permute-done.30 = bf16[4,512,512]{2,1,0:T(8,128)(2,1)S(1)} collective-permute-done((bf16[4,512,512]{2,1,0:T(8,128)(2,1)S(1)}, bf16[4,512,512]{2,1,0:T(8,128)(2,1)S(1)}, u32[]{:S(2)}, u32[]{:S(2)}) %collective-permute-start.30) | collective-permute-done | bytes 2097184 | tf_op jit(solution)/shard_map/ppermute | solution.py:33
  85.0 5.2 %collective-permute-done.20 = bf16[128,512]{1,0:T(8,128)(2,1)S(1)} collective-permute-done((bf16[128,512]{1,0:T(8,128)(2,1)S(1)}, bf16[128,512]{1,0:T(8,128)(2,1)S(1)}, u32[]{:S(2)}, u32[]{:S(2)}) %collective-permute-start.20) | collective-permute-done | bytes 131104 | tf_op jit(solution)/shard_map/ppermute | solution.py:29
  94.2 1.7 %collective-permute-start.28 = (bf16[128,512]{1,0:T(8,128)(2,1)S(1)}, bf16[128,512]{1,0:T(8,128)(2,1)S(1)}, u32[]{:S(2)}, u32[]{:S(2)}) collective-permute-start(bf16[128,512]{1,0:T(8,128)(2,1)S(1)} %get-tuple-element.87), channel_id=1, source_target_pairs={{0,8},{1,9},{2,10},{3,11},{4,12},{5,13},{6,14},{7,15},{8,0},{9,1},... | collective-permute-start | bytes 393224 | tf_op jit(solution)/shard_map/ppermute | solution.py:29
  95.9 2.1 %collective-permute-start.27 = (bf16[128,512]{1,0:T(8,128)(2,1)S(1)}, bf16[128,512]{1,0:T(8,128)(2,1)S(1)}, u32[]{:S(2)}, u32[]{:S(2)}) collective-permute-start(bf16[128,512]{1,0:T(8,128)(2,1)S(1)} %get-tuple-element.84), channel_id=1, source_target_pairs={{0,12},{1,13},{2,14},{3,15},{4,0},{5,1},{6,2},{7,3},{8,4},{9,5},{1... | collective-permute-start | bytes 393224 | tf_op jit(solution)/shard_map/ppermute | solution.py:29
  98.7 3.7 %collective-permute-done.29 = bf16[128,512]{1,0:T(8,128)(2,1)S(1)} collective-permute-done((bf16[128,512]{1,0:T(8,128)(2,1)S(1)}, bf16[128,512]{1,0:T(8,128)(2,1)S(1)}, u32[]{:S(2)}, u32[]{:S(2)}) %collective-permute-start.29) | collective-permute-done | bytes 131104 | tf_op jit(solution)/shard_map/ppermute | solution.py:29
  102.4 4.7 %collective-permute-done.28 = bf16[128,512]{1,0:T(8,128)(2,1)S(1)} collective-permute-done((bf16[128,512]{1,0:T(8,128)(2,1)S(1)}, bf16[128,512]{1,0:T(8,128)(2,1)S(1)}, u32[]{:S(2)}, u32[]{:S(2)}) %collective-permute-start.28) | collective-permute-done | bytes 131104 | tf_op jit(solution)/shard_map/ppermute | solution.py:29
  107.9 2.2 %token_grad.1 = bf16[128,2048]{1,0:T(8,128)(2,1)} custom-call(s32[7]{0:T(128)S(1)} %stack.49.place, bf16[128,512]{1,0:T(8,128)(2,1)S(1)} %add_convert_fusion.2.refs_4_.delta, bf16[2,512,512]{2,1,0:T(8,128)(2,1)S(1)} %pad_maximum_fusion.downs, bf16[2,512,512]{2,1,0:T(8,128)(2,1)S(1)} %collective-permute-done.26.core_downs), custom_call_target="tpu_custom_call" | custom-call | tf_op jit(solution)/shard_map/token_grad/pallas_call | solution.py:45
  110.1 4.6 %collective-permute-done.31 = bf16[2,512,512]{2,1,0:T(8,128)(2,1)S(1)} collective-permute-done((bf16[2,512,512]{2,1,0:T(8,128)(2,1)S(1)}, bf16[2,512,512]{2,1,0:T(8,128)(2,1)S(1)}, u32[]{:S(2)}, u32[]{:S(2)}) %collective-permute-start.31) | collective-permute-done | bytes 1048608 | tf_op jit(solution)/shard_map/ppermute | solution.py:33
  (81 shorter events, 29.2 us)
Async XLA Ops:
  2.9 11.1 %collective-permute-start.1 = (bf16[2,512,512]{2,1,0:T(8,128)(2,1)S(1)}, bf16[2,512,512]{2,1,0:T(8,128)(2,1)S(1)}, u32[]{:S(2)}, u32[]{:S(2)}) collective-permute-start(bf16[2,512,512]{2,1,0:T(8,128)(2,1)S(1)} %constant_dynamic-update-slice_fusion.refs_4_), channel_id=1, source_target_pairs={{0,1},{1,0},{2,3},{3,2},{4,5},{5,4},{6,7},{7,6},{8,9},{9,8},{10,11... | collective-permute-start | bytes 3145736 | tf_op jit(solution)/shard_map/ppermute | solution.py:33
  4.4 9.5 %collective-permute-start = (bf16[2,128,512]{2,1,0:T(8,128)(2,1)S(1)}, bf16[2,128,512]{2,1,0:T(8,128)(2,1)S(1)}, u32[]{:S(2)}, u32[]{:S(2)}) collective-permute-start(bf16[2,128,512]{2,1,0:T(8,128)(2,1)S(1)} %get-tuple-element.50), channel_id=1, source_target_pairs={{0,2},{1,3},{2,0},{3,1},{4,6},{5,7},{6,4},{7,5},{8,10},{9,11},{10,... | collective-permute-start | bytes 786440 | tf_op jit(solution)/shard_map/ppermute | solution.py:33
  8.6 11.6 %collective-permute-start.5 = (bf16[128,512]{1,0:T(8,128)(2,1)S(1)}, bf16[128,512]{1,0:T(8,128)(2,1)S(1)}, u32[]{:S(2)}, u32[]{:S(2)}) collective-permute-start(bf16[128,512]{1,0:T(8,128)(2,1)S(1)} %copy-done.2), channel_id=1, source_target_pairs={{0,8},{1,9},{2,10},{3,11},{4,12},{5,13},{6,14},{7,15},{8,0},{9,1},... | collective-permute-start | bytes 393224 | tf_op jit(solution)/shard_map/ppermute | solution.py:29
  11.2 9.0 %collective-permute-start.6 = (bf16[128,512]{1,0:T(8,128)(2,1)S(1)}, bf16[128,512]{1,0:T(8,128)(2,1)S(1)}, u32[]{:S(2)}, u32[]{:S(2)}) collective-permute-start(bf16[128,512]{1,0:T(8,128)(2,1)S(1)} %copy-done.2), channel_id=1, source_target_pairs={{0,12},{1,13},{2,14},{3,15},{4,0},{5,1},{6,2},{7,3},{8,4},{9,5},{1... | collective-permute-start | bytes 393224 | tf_op jit(solution)/shard_map/ppermute | solution.py:29
  21.4 17.2 %collective-permute-start.9 = (bf16[512,512]{1,0:T(8,128)(2,1)S(1)}, bf16[512,512]{1,0:T(8,128)(2,1)S(1)}, u32[]{:S(2)}, u32[]{:S(2)}) collective-permute-start(bf16[512,512]{1,0:T(8,128)(2,1)S(1)} %bitcast.47), channel_id=1, source_target_pairs={{0,2},{1,3},{2,0},{3,1},{4,6},{5,7},{6,4},{7,5},{8,10},{9,11},{10,... | collective-permute-start | bytes 1572872 | tf_op jit(solution)/shard_map/ppermute | solution.py:33
  22.5 16.0 %collective-permute-start.10 = (bf16[144,512]{1,0:T(8,128)(2,1)S(1)}, bf16[144,512]{1,0:T(8,128)(2,1)S(1)}, u32[]{:S(2)}, u32[]{:S(2)}) collective-permute-start(bf16[144,512]{1,0:T(8,128)(2,1)S(1)} %payload.1.refs_3_), channel_id=1, source_target_pairs={{0,4},{1,5},{2,6},{3,7},{4,8},{5,9},{6,10},{7,11},{8,12},{9,13},{1... | collective-permute-start | bytes 442376 | tf_op jit(solution)/shard_map/ppermute | solution.py:29
  25.8 12.7 %collective-permute-start.11 = (bf16[144,512]{1,0:T(8,128)(2,1)S(1)}, bf16[144,512]{1,0:T(8,128)(2,1)S(1)}, u32[]{:S(2)}, u32[]{:S(2)}) collective-permute-start(bf16[144,512]{1,0:T(8,128)(2,1)S(1)} %payload.1.refs_3_), channel_id=1, source_target_pairs={{0,8},{1,9},{2,10},{3,11},{4,12},{5,13},{6,14},{7,15},{8,0},{9,1},... | collective-permute-start | bytes 442376 | tf_op jit(solution)/shard_map/ppermute | solution.py:29
  27.5 11.1 %collective-permute-start.12 = (bf16[144,512]{1,0:T(8,128)(2,1)S(1)}, bf16[144,512]{1,0:T(8,128)(2,1)S(1)}, u32[]{:S(2)}, u32[]{:S(2)}) collective-permute-start(bf16[144,512]{1,0:T(8,128)(2,1)S(1)} %payload.1.refs_3_), channel_id=1, source_target_pairs={{0,12},{1,13},{2,14},{3,15},{4,0},{5,1},{6,2},{7,3},{8,4},{9,5},{1... | collective-permute-start | bytes 442376 | tf_op jit(solution)/shard_map/ppermute | solution.py:29
  28.4 10.1 %collective-permute-start.8 = (bf16[128,512]{1,0:T(8,128)(2,1)S(1)}, bf16[128,512]{1,0:T(8,128)(2,1)S(1)}, u32[]{:S(2)}, u32[]{:S(2)}) collective-permute-start(bf16[128,512]{1,0:T(8,128)(2,1)S(1)} %fusion.3), channel_id=1, source_target_pairs={{0,2},{1,3},{2,0},{3,1},{4,6},{5,7},{6,4},{7,5},{8,10},{9,11},{10,... | collective-permute-start | bytes 393224 | tf_op jit(solution)/shard_map/ppermute | solution.py:33
  38.6 13.7 %collective-permute-start.15 = (bf16[512,512]{1,0:T(8,128)(2,1)S(1)}, bf16[512,512]{1,0:T(8,128)(2,1)S(1)}, u32[]{:S(2)}, u32[]{:S(2)}) collective-permute-start(bf16[512,512]{1,0:T(8,128)(2,1)S(1)} %bitcast.48), channel_id=1, source_target_pairs={{0,2},{1,3},{2,0},{3,1},{4,6},{5,7},{6,4},{7,5},{8,10},{9,11},{10,... | collective-permute-start | bytes 1572872 | tf_op jit(solution)/shard_map/ppermute | solution.py:33
  39.2 8.6 %collective-permute-start.13 = (bf16[128,512]{1,0:T(8,128)(2,1)S(1)}, bf16[128,512]{1,0:T(8,128)(2,1)S(1)}, u32[]{:S(2)}, u32[]{:S(2)}) collective-permute-start(bf16[128,512]{1,0:T(8,128)(2,1)S(1)} %fusion.1.refs_1_.refs_3_), channel_id=1, source_target_pairs={{0,4},{1,5},{2,6},{3,7},{4,8},{5,9},{6,10},{7,11},{8,12},{9,13},{1... | collective-permute-start | bytes 393224 | tf_op jit(solution)/shard_map/ppermute | solution.py:29
  42.8 9.5 %collective-permute-start.14 = (bf16[128,512]{1,0:T(8,128)(2,1)S(1)}, bf16[128,512]{1,0:T(8,128)(2,1)S(1)}, u32[]{:S(2)}, u32[]{:S(2)}) collective-permute-start(bf16[128,512]{1,0:T(8,128)(2,1)S(1)} %fusion.1.refs_1_.refs_3_), channel_id=1, source_target_pairs={{0,8},{1,9},{2,10},{3,11},{4,12},{5,13},{6,14},{7,15},{8,0},{9,1},... | collective-permute-start | bytes 393224 | tf_op jit(solution)/shard_map/ppermute | solution.py:29
  45.1 8.8 %collective-permute-start.16 = (bf16[512,512]{1,0:T(8,128)(2,1)S(1)}, bf16[512,512]{1,0:T(8,128)(2,1)S(1)}, u32[]{:S(2)}, u32[]{:S(2)}) collective-permute-start(bf16[512,512]{1,0:T(8,128)(2,1)S(1)} %collective-permute-done.9.refs_6_), channel_id=1, source_target_pairs={{0,1},{1,0},{2,3},{3,2},{4,5},{5,4},{6,7},{7,6},{8,9},{9,8},{10,11... | collective-permute-start | bytes 1572872 | tf_op jit(solution)/shard_map/ppermute | solution.py:33
  52.3 14.3 %collective-permute-start.22 = (bf16[512,512]{1,0:T(8,128)(2,1)S(1)}, bf16[512,512]{1,0:T(8,128)(2,1)S(1)}, u32[]{:S(2)}, u32[]{:S(2)}) collective-permute-start(bf16[512,512]{1,0:T(8,128)(2,1)S(1)} %get-tuple-element.76), channel_id=1, source_target_pairs={{0,2},{1,3},{2,0},{3,1},{4,6},{5,7},{6,4},{7,5},{8,10},{9,11},{10,... | collective-permute-start | bytes 1572872 | tf_op jit(solution)/shard_map/ppermute | solution.py:33
  57.6 11.4 %collective-permute-start.19 = (bf16[2,128,512]{2,1,0:T(8,128)(2,1)S(1)}, bf16[2,128,512]{2,1,0:T(8,128)(2,1)S(1)}, u32[]{:S(2)}, u32[]{:S(2)}) collective-permute-start(bf16[2,128,512]{2,1,0:T(8,128)(2,1)S(1)} %get-tuple-element.62), channel_id=1, source_target_pairs={{0,12},{1,13},{2,14},{3,15},{4,0},{5,1},{6,2},{7,3},{8,4},{9,5},{1... | collective-permute-start | bytes 786440 | tf_op jit(solution)/shard_map/ppermute | solution.py:29
  65.7 11.1 %collective-permute-start.21 = (bf16[2,128,512]{2,1,0:T(8,128)(2,1)S(1)}, bf16[2,128,512]{2,1,0:T(8,128)(2,1)S(1)}, u32[]{:S(2)}, u32[]{:S(2)}) collective-permute-start(bf16[2,128,512]{2,1,0:T(8,128)(2,1)S(1)} %get-tuple-element.66), channel_id=1, source_target_pairs={{0,4},{1,5},{2,6},{3,7},{4,8},{5,9},{6,10},{7,11},{8,12},{9,13},{1... | collective-permute-start | bytes 786440 | tf_op jit(solution)/shard_map/ppermute | solution.py:29
  65.7 14.6 %collective-permute-start.23 = (bf16[128,512]{1,0:T(8,128)(2,1)S(1)}, bf16[128,512]{1,0:T(8,128)(2,1)S(1)}, u32[]{:S(2)}, u32[]{:S(2)}) collective-permute-start(bf16[128,512]{1,0:T(8,128)(2,1)S(1)} %get-tuple-element.79), channel_id=1, source_target_pairs={{0,8},{1,9},{2,10},{3,11},{4,12},{5,13},{6,14},{7,15},{8,0},{9,1},... | collective-permute-start | bytes 393224 | tf_op jit(solution)/shard_map/ppermute | solution.py:29
  80.5 27.4 %collective-permute-start.26 = (bf16[2,512,512]{2,1,0:T(8,128)(2,1)S(1)}, bf16[2,512,512]{2,1,0:T(8,128)(2,1)S(1)}, u32[]{:S(2)}, u32[]{:S(2)}) collective-permute-start(bf16[2,512,512]{2,1,0:T(8,128)(2,1)S(1)} %pad_maximum_fusion.downs), channel_id=1, source_target_pairs={{0,1},{1,0},{2,3},{3,2},{4,5},{5,4},{6,7},{7,6},{8,9},{9,8},{10,11... | collective-permute-start | bytes 3145736 | tf_op jit(solution)/shard_map/ppermute | solution.py:33
  81.0 9.2 %collective-permute-start.20 = (bf16[128,512]{1,0:T(8,128)(2,1)S(1)}, bf16[128,512]{1,0:T(8,128)(2,1)S(1)}, u32[]{:S(2)}, u32[]{:S(2)}) collective-permute-start(bf16[128,512]{1,0:T(8,128)(2,1)S(1)} %get-tuple-element.65), channel_id=1, source_target_pairs={{0,8},{1,9},{2,10},{3,11},{4,12},{5,13},{6,14},{7,15},{8,0},{9,1},... | collective-permute-start | bytes 393224 | tf_op jit(solution)/shard_map/ppermute | solution.py:29
  81.0 9.2 %collective-permute-start.24 = (bf16[128,512]{1,0:T(8,128)(2,1)S(1)}, bf16[128,512]{1,0:T(8,128)(2,1)S(1)}, u32[]{:S(2)}, u32[]{:S(2)}) collective-permute-start(bf16[128,512]{1,0:T(8,128)(2,1)S(1)} %add_convert_fusion.2.refs_4_.delta), channel_id=1, source_target_pairs={{0,2},{1,3},{2,0},{3,1},{4,6},{5,7},{6,4},{7,5},{8,10},{9,11},{10,... | collective-permute-start | bytes 393224 | tf_op jit(solution)/shard_map/ppermute | solution.py:33
  90.2 24.5 %collective-permute-start.31 = (bf16[2,512,512]{2,1,0:T(8,128)(2,1)S(1)}, bf16[2,512,512]{2,1,0:T(8,128)(2,1)S(1)}, u32[]{:S(2)}, u32[]{:S(2)}) collective-permute-start(bf16[2,512,512]{2,1,0:T(8,128)(2,1)S(1)} %add_convert_fusion.1), channel_id=1, source_target_pairs={{0,2},{1,3},{2,0},{3,1},{4,6},{5,7},{6,4},{7,5},{8,10},{9,11},{10,... | collective-permute-start | bytes 3145736 | tf_op jit(solution)/shard_map/ppermute | solution.py:33
  94.1 8.3 %collective-permute-start.29 = (bf16[128,512]{1,0:T(8,128)(2,1)S(1)}, bf16[128,512]{1,0:T(8,128)(2,1)S(1)}, u32[]{:S(2)}, u32[]{:S(2)}) collective-permute-start(bf16[128,512]{1,0:T(8,128)(2,1)S(1)} %get-tuple-element.88), channel_id=1, source_target_pairs={{0,4},{1,5},{2,6},{3,7},{4,8},{5,9},{6,10},{7,11},{8,12},{9,13},{1... | collective-permute-start | bytes 393224 | tf_op jit(solution)/shard_map/ppermute | solution.py:29
  94.2 12.9 %collective-permute-start.28 = (bf16[128,512]{1,0:T(8,128)(2,1)S(1)}, bf16[128,512]{1,0:T(8,128)(2,1)S(1)}, u32[]{:S(2)}, u32[]{:S(2)}) collective-permute-start(bf16[128,512]{1,0:T(8,128)(2,1)S(1)} %get-tuple-element.87), channel_id=1, source_target_pairs={{0,8},{1,9},{2,10},{3,11},{4,12},{5,13},{6,14},{7,15},{8,0},{9,1},... | collective-permute-start | bytes 393224 | tf_op jit(solution)/shard_map/ppermute | solution.py:29
  95.9 11.2 %collective-permute-start.27 = (bf16[128,512]{1,0:T(8,128)(2,1)S(1)}, bf16[128,512]{1,0:T(8,128)(2,1)S(1)}, u32[]{:S(2)}, u32[]{:S(2)}) collective-permute-start(bf16[128,512]{1,0:T(8,128)(2,1)S(1)} %get-tuple-element.84), channel_id=1, source_target_pairs={{0,12},{1,13},{2,14},{3,15},{4,0},{5,1},{6,2},{7,3},{8,4},{9,5},{1... | collective-permute-start | bytes 393224 | tf_op jit(solution)/shard_map/ppermute | solution.py:29
  (15 other events, 155.7 us)

commit v9 on v8

--- a/solution.py
+++ b/solution.py
@@ -58,10 +58,12 @@
     return run
 
 
-def columns_body(n_line, block, place, tokens, *refs):
-    own, other, across, sems = refs
+def columns_body(n_line, block, place, tokens, expert_in, expert_out, *refs):
+    own, other, across, weights, sems = refs
     pieces = (own, across.at[0], other, across.at[1])
     copies = []
+    for i, weight in enumerate((expert_in, expert_out)):
+        copies.append(pltpu.make_async_copy(weight, weights.at[pl.ds(i, 1)], sems.at[i]))
     for core in range(2):
         for side in range(2):
             owner = (place[1] ^ side) * 2 + (place[2] ^ core)
@@ -93,7 +95,8 @@
 
 
 def project_body(n_line, place, *refs):
-    pieces, downs = refs[:4], refs[4 : 4 + n_line]
+    own, across, core, core_across, *downs = refs[: 4 + n_line]
+    pieces = (own, across.at[0], core, core_across)
     keep, send, down = refs[4 + n_line :]
     block = downs[0].shape[0]
     for back in range(n_line):
@@ -147,9 +150,9 @@
         for i in group:
             part = slice((i - first) * tok_rows, (i - first + 1) * tok_rows)
             out = sums.pop(0)
-            delta_out, sum_out = (out, sums.pop(0)) if len(out.shape) == 2 else (out.at[0], out.at[1])
-            delta_out[...] = delta_sum[part].astype(out.dtype)
-            sum_out[...] = out_sum[part].astype(out.dtype)
+            out[...] = delta_sum[part].astype(out.dtype)
+            out = sums.pop(0)
+            out[...] = out_sum[part].astype(out.dtype)
 
 
 def weight_grad_body(n_rows, n_sets, place, *refs):
@@ -173,8 +176,9 @@
 
 
 def down_grad_body(n_line, place, *refs):
-    pieces, deltas, core_deltas, blocks = refs[:4], refs[4:6], refs[6], refs[7:]
-    tokens = jnp.concatenate([p[...] for p in pieces], axis=0)
+    own, across, core, core_across, *deltas, core_deltas = refs[:7]
+    blocks = refs[7:]
+    tokens = jnp.concatenate([own[...], across[0], core[...], core_across[...]], axis=0)
     delta = jnp.concatenate([d[...] for d in deltas] + [core_deltas[0], core_deltas[1]], axis=0)
     part = lax.dot_general(tokens, delta, contract_first, preferred_element_type=wide)
     block = blocks[0].shape[0]
@@ -218,26 +222,27 @@
     gate_rows = -(-n_experts // 16) * 16
     columns = call(
         functools.partial(columns_body, n_line, block),
-        [shape((tok_rows, n_line * block), narrow)] * 2 + [shape((2, tok_rows, n_line * block), narrow)],
+        [shape((tok_rows, n_line * block), narrow)] * 2
+        + [shape((2, tok_rows, n_line * block), narrow), shape((2, latent_width, hidden_width), narrow)],
         "columns",
-        scratch=[pltpu.SemaphoreType.DMA((4 * n_line,))],
-        outside=1,
-    )(place, tokens)
+        scratch=[pltpu.SemaphoreType.DMA((4 * n_line + 2,))],
+        outside=3,
+    )(place, tokens, expert_in, expert_out)
     (payload,) = call(payload_body, [shape((tok_rows + gate_rows, latent_width), narrow)], "payload")(
         place, routes.T, gate_levels.T, latent_grad
     )
-    own = jnp.concatenate([expert_in, expert_out])
+    own = columns[3]
     core_own = swap(own, n_line, 1, 0)
     across = swap(columns[2], n_line, 0, 1)
-    near_tokens = [columns[0], across[0], swap(after(columns[1], across, core_own), n_line, 1, 0), swap(across[1], n_line, 1, 0)]
-    side_in = swap(after(expert_in[0], near_tokens[2]), n_line, 0, 1)
+    core_tokens = [swap(after(columns[1], across, core_own), n_line, 1, 0), swap(across[1], n_line, 1, 0)]
+    side_in = swap(after(expert_in[0], across), n_line, 0, 1)
 
     project = call(
         functools.partial(project_body, n_line),
         [shape((2, tok_rows, latent_width), wide)] * 2 + [shape((n_line * block, latent_width), narrow)],
         "project",
     )
-    keep, send, down = project(place, *near_tokens, *downs)
+    keep, send, down = project(after(place, payload), columns[0], across, *core_tokens, *downs)
     half = keep + swap(send, n_line, 1, 0)
     payloads = [payload] + [turn(after(payload, *downs[1:]), n_line, back) for back in range(1, n_line)]
     crossed = swap(half[1].astype(narrow), n_line, 0, 1).astype(wide)
@@ -250,34 +255,27 @@
     core_in = swap(after(side_in, latent), n_line, 1, 0)
     core_out = swap(after(side_out, *rows[1:]), n_line, 1, 0)
     weights = [own, core_own, side_in, side_out, core_in, core_out]
-    side_down = swap(after(down, side_out), n_line, 0, 1)
+    side_down = swap(after(down, *rows[1:]), n_line, 0, 1)
+
     both_down = jnp.stack([down, side_down])
-    core_down = swap(both_down, n_line, 1, 0)
-
-    sums, saved = [None] * n_line, []
+    deltas_of, outs_of, saved = [None] * n_line, [None] * n_line, []
     done = latent
     for group in groups:
         count = len(group)
-        outs = []
-        for back in group:
-            kind = narrow if back else wide
-            outs += [rows_of(kind)] * 2 if back in middle else [shape((2, tok_rows, latent_width), kind)]
+        outs = [rows_of(narrow if back else wide) for back in group for _ in range(2)]
         values = call(
             functools.partial(expert_body, count),
             outs + [shape((4, count * tok_rows, hidden_width), narrow)] * 3,
             "experts",
         )(after(place, done), *(rows[i] for i in group), *(payloads[i] for i in group), *weights)
         done, saved = values[0], saved + [list(values[-3:])]
-        values = list(values[:-3])
-        for back in group:
-            sums[back] = [values.pop(0) for _ in range(2 if back in middle else 1)]
-
-    lines = [
-        [turn(value, n_line, n_line - back) if back else value for value in values]
-        for back, values in enumerate(sums)
-    ]
-    delta_lines = [values[0] if len(values) == 2 else values[0][0] for values in lines]
-    out_lines = [values[1] if len(values) == 2 else values[0][1] for values in lines]
+        for i, back in enumerate(group):
+            deltas_of[back], outs_of[back] = values[2 * i], values[2 * i + 1]
+
+    def home(value, back):
+        return turn(value, n_line, n_line - back) if back else value
+
+    delta_lines = [home(value, back) for back, value in enumerate(deltas_of)]
 
     pair = (2, latent_width, hidden_width)
     near, far, other = call(
@@ -292,22 +290,27 @@
     delta_lines = [after(line, near, both_down) for line in delta_lines]
     delta = sum(line.astype(wide) for line in delta_lines).astype(narrow)
     side_delta = swap(delta, n_line, 0, 1)
-    latent_out = sum(line.astype(wide) for line in out_lines).astype(narrow)
+    first_out = home(outs_of[1], 1)
     other = swap(after(other, delta), n_line, 1, 0)
     far = (far + other[2:].astype(wide)).astype(narrow)
-    far = swap(after(far, side_delta, *(out_lines[back] for back in middle)), n_line, 0, 1)
-    core_deltas = swap(jnp.stack([delta, after(side_delta, *(out_lines[back] for back in middle))]), n_line, 1, 0)
+    sent = far
+    far = swap(after(far, side_delta), n_line, 0, 1)
+    core_deltas = swap(jnp.stack([delta, after(side_delta, first_out, sent)]), n_line, 1, 0)
     blocks = call(
         functools.partial(down_grad_body, n_line),
         [shape((block, latent_width), wide)] + [shape((block, latent_width), narrow)] * (n_line - 1),
         "down_grad",
-    )(after(place, *(out_lines[back] for back in middle)), *near_tokens, delta, side_delta, core_deltas)
-    weight_grad = (near + other[:2].astype(wide) + far.astype(wide)).astype(narrow)
+    )(place, columns[0], across, *core_tokens, delta, side_delta, core_deltas)
+    core_down = swap(after(both_down, blocks[1]), n_line, 1, 0)
     (grad_tokens,) = call(
         functools.partial(token_grad_body, n_line, block), [shape((tok_rows, width), narrow)], "token_grad"
     )(place, after(delta, blocks[1]), both_down, core_down)
     blocks = [blocks[0]] + [turn(blocks[back], n_line, n_line - back) for back in range(1, n_line)]
+    first_block = blocks[1]
+    out_lines = [outs_of[0], first_out] + [home(after(outs_of[back], first_block), back) for back in range(2, n_line)]
+    latent_out = sum(line.astype(wide) for line in out_lines).astype(narrow)
     grad_down = sum(value.astype(wide) for value in blocks)
+    weight_grad = (near + other[:2].astype(wide) + after(far, grad_tokens).astype(wide)).astype(narrow)
     return (latent_out, grad_tokens, grad_down, weight_grad[:1], weight_grad[1:])
 
 

time: 116 us -> 118 us (1.017)
  waiting for transfers between devices: 56.4 us -> 44 us
  starting transfers between devices: 37.2 us -> 47.9 us
  local copies, waits for them, and re-layouts: 3.47 us -> 6.56 us
    ppermute x16 -> x18, starting transfers between devices: 26.4 us -> 36.6 us  [turn(): lax.ppermute(value, plane, device_pairs(n_line, lambda z, x, c: ((z + by)...]
    ppermute x16 -> x18, waiting for transfers between devices: 37.1 us -> 28.5 us  [turn(): lax.ppermute(value, plane, device_pairs(n_line, lambda z, x, c: ((z + by)...]
    unnamed x15 -> x18, local copies, waits for them, and re-layouts: 1.2 us -> 5.42 us
    ppermute x16, waiting for transfers between devices: 19.3 us -> 15.6 us  [swap(): lax.ppermute(value, plane, device_pairs(n_line, lambda z, x, c: (z, x ^ s...]
  transfers between devices with their start and end apart: 32 -> 34, of which waited for: 17 -> 16; matrix products, arithmetic and copies ran while one was open for 2% -> 2% of each run, Pallas kernels for 12% -> 11%
where the time goes in v9:
time: 118 us
  starting transfers between devices  47.9 us (41%)
  waiting for transfers between devices  44 us (37%)
  Pallas kernels  15.7 us (13%)
  local copies, waits for them, and re-layouts  6.56 us (6%)
  other arithmetic  2.66 us (2%)
    ppermute x18, starting transfers between devices, turn(): lax.ppermute(value, plane, device_pairs(n_line, lambda z, x, c: ((z + by)...  36.6 us
    ppermute x18, waiting for transfers between devices, turn(): lax.ppermute(value, plane, device_pairs(n_line, lambda z, x, c: ((z + by)...  28.5 us
    pallas_call x8, Pallas kernels, run(): pl.pallas_call(body, out_shape=outs, in_specs=[pl.BlockSpec(memory_space=...  15.7 us
    ppermute x16, waiting for transfers between devices, swap(): lax.ppermute(value, plane, device_pairs(n_line, lambda z, x, c: (z, x ^ s...  15.6 us
    ppermute x16, starting transfers between devices, swap(): lax.ppermute(value, plane, device_pairs(n_line, lambda z, x, c: (z, x ^ s...  11.3 us
    unnamed x18, local copies, waits for them, and re-layouts  5.42 us
  transfers between devices with their start and end apart: 34, of which 16 were waited for; matrix products, arithmetic and copies ran while one was open for 2% of the time, Pallas kernels for 11%

profile of v9, /device:TPU:0, one launch (start us, length us, event | category | flops | bytes accessed | tf_op | source)
XLA Modules:
  0.0 117.8 jit_solution(14977862914308573101)
XLA Ops:
  5.4 2.6 %collective-permute-start = (bf16[2,128,512]{2,1,0:T(8,128)(2,1)S(1)}, bf16[2,128,512]{2,1,0:T(8,128)(2,1)S(1)}, u32[]{:S(2)}, u32[]{:S(2)}) collective-permute-start(bf16[2,128,512]{2,1,0:T(8,128)(2,1)S(1)} %get-tuple-element.59), channel_id=1, source_target_pairs={{0,2},{1,3},{2,0},{3,1},{4,6},{5,7},{6,4},{7,5},{8,10},{9,11},{10,... | collective-permute-start | bytes 786440 | tf_op jit(solution)/shard_map/ppermute | solution.py:33
  7.9 1.6 %collective-permute-start.4 = (bf16[128,512]{1,0:T(8,128)(2,1)}, bf16[128,512]{1,0:T(8,128)(2,1)S(1)}, u32[]{:S(2)}, u32[]{:S(2)}) collective-permute-start(bf16[128,512]{1,0:T(8,128)(2,1)} %refs_4_.1), channel_id=1, source_target_pairs={{0,4},{1,5},{2,6},{3,7},{4,8},{5,9},{6,10},{7,11},{8,12},{9,13},{1... | collective-permute-start | bytes 393224 | tf_op jit(solution)/shard_map/ppermute | solution.py:29
  9.5 2.6 %collective-permute-start.5 = (bf16[128,512]{1,0:T(8,128)(2,1)}, bf16[128,512]{1,0:T(8,128)(2,1)S(1)}, u32[]{:S(2)}, u32[]{:S(2)}) collective-permute-start(bf16[128,512]{1,0:T(8,128)(2,1)} %refs_4_.1), channel_id=1, source_target_pairs={{0,8},{1,9},{2,10},{3,11},{4,12},{5,13},{6,14},{7,15},{8,0},{9,1},... | collective-permute-start | bytes 393224 | tf_op jit(solution)/shard_map/ppermute | solution.py:29
  18.3 3.0 %collective-permute-done.5.refs_6_ = bf16[128,512]{1,0:T(8,128)(2,1)S(1)} collective-permute-done((bf16[128,512]{1,0:T(8,128)(2,1)}, bf16[128,512]{1,0:T(8,128)(2,1)S(1)}, u32[]{:S(2)}, u32[]{:S(2)}) %collective-permute-start.5) | collective-permute-done | bytes 131104 | tf_op jit(solution)/shard_map/ppermute | solution.py:29
  23.0 3.3 %collective-permute-start.10 = (bf16[144,512]{1,0:T(8,128)(2,1)S(1)}, bf16[144,512]{1,0:T(8,128)(2,1)S(1)}, u32[]{:S(2)}, u32[]{:S(2)}) collective-permute-start(bf16[144,512]{1,0:T(8,128)(2,1)S(1)} %payload.1.refs_3_), channel_id=1, source_target_pairs={{0,4},{1,5},{2,6},{3,7},{4,8},{5,9},{6,10},{7,11},{8,12},{9,13},{1... | collective-permute-start | bytes 442376 | tf_op jit(solution)/shard_map/ppermute | solution.py:29
  26.3 1.6 %collective-permute-start.11 = (bf16[144,512]{1,0:T(8,128)(2,1)S(1)}, bf16[144,512]{1,0:T(8,128)(2,1)S(1)}, u32[]{:S(2)}, u32[]{:S(2)}) collective-permute-start(bf16[144,512]{1,0:T(8,128)(2,1)S(1)} %payload.1.refs_3_), channel_id=1, source_target_pairs={{0,8},{1,9},{2,10},{3,11},{4,12},{5,13},{6,14},{7,15},{8,0},{9,1},... | collective-permute-start | bytes 442376 | tf_op jit(solution)/shard_map/ppermute | solution.py:29
  30.3 9.2 %collective-permute-done.8 = bf16[128,512]{1,0:T(8,128)(2,1)S(1)} collective-permute-done((bf16[128,512]{1,0:T(8,128)(2,1)S(1)}, bf16[128,512]{1,0:T(8,128)(2,1)S(1)}, u32[]{:S(2)}, u32[]{:S(2)}) %collective-permute-start.8) | collective-permute-done | bytes 131104 | tf_op jit(solution)/shard_map/ppermute | solution.py:33
  40.3 3.3 %collective-permute-start.13 = (bf16[128,512]{1,0:T(8,128)(2,1)S(1)}, bf16[128,512]{1,0:T(8,128)(2,1)S(1)}, u32[]{:S(2)}, u32[]{:S(2)}) collective-permute-start(bf16[128,512]{1,0:T(8,128)(2,1)S(1)} %fusion.1.refs_1_.refs_3_), channel_id=1, source_target_pairs={{0,4},{1,5},{2,6},{3,7},{4,8},{5,9},{6,10},{7,11},{8,12},{9,13},{1... | collective-permute-start | bytes 393224 | tf_op jit(solution)/shard_map/ppermute | solution.py:29
  43.6 1.6 %collective-permute-start.14 = (bf16[128,512]{1,0:T(8,128)(2,1)S(1)}, bf16[128,512]{1,0:T(8,128)(2,1)S(1)}, u32[]{:S(2)}, u32[]{:S(2)}) collective-permute-start(bf16[128,512]{1,0:T(8,128)(2,1)S(1)} %fusion.1.refs_1_.refs_3_), channel_id=1, source_target_pairs={{0,8},{1,9},{2,10},{3,11},{4,12},{5,13},{6,14},{7,15},{8,0},{9,1},... | collective-permute-start | bytes 393224 | tf_op jit(solution)/shard_map/ppermute | solution.py:29
  45.9 3.2 %collective-permute-done.13.refs_0_ = bf16[128,512]{1,0:T(8,128)(2,1)S(1)} collective-permute-done((bf16[128,512]{1,0:T(8,128)(2,1)S(1)}, bf16[128,512]{1,0:T(8,128)(2,1)S(1)}, u32[]{:S(2)}, u32[]{:S(2)}) %collective-permute-start.13) | collective-permute-done | bytes 131104 | tf_op jit(solution)/shard_map/ppermute | solution.py:29
  49.1 4.3 %collective-permute-done.14.refs_1_ = bf16[128,512]{1,0:T(8,128)(2,1)S(1)} collective-permute-done((bf16[128,512]{1,0:T(8,128)(2,1)S(1)}, bf16[128,512]{1,0:T(8,128)(2,1)S(1)}, u32[]{:S(2)}, u32[]{:S(2)}) %collective-permute-start.14) | collective-permute-done | bytes 131104 | tf_op jit(solution)/shard_map/ppermute | solution.py:29
  55.3 3.4 %experts.2 = (bf16[128,512]{1,0:T(8,128)(2,1)S(1)}, bf16[128,512]{1,0:T(8,128)(2,1)S(1)}, bf16[128,512]{1,0:T(8,128)(2,1)S(1)}, bf16[128,512]{1,0:T(8,128)(2,1)S...) custom-call(s32[7]{0:T(128)S(1)} %stack.49.place, ...), custom_call_target="tpu_custom_call" | custom-call | tf_op jit(solution)/shard_map/experts/pallas_call | solution.py:45
  58.7 4.2 %collective-permute-start.20 = (bf16[128,512]{1,0:T(8,128)(2,1)S(1)}, bf16[128,512]{1,0:T(8,128)(2,1)S(1)}, u32[]{:S(2)}, u32[]{:S(2)}) collective-permute-start(bf16[128,512]{1,0:T(8,128)(2,1)S(1)} %get-tuple-element.72), channel_id=1, source_target_pairs={{0,12},{1,13},{2,14},{3,15},{4,0},{5,1},{6,2},{7,3},{8,4},{9,5},{1... | collective-permute-start | bytes 393224 | tf_op jit(solution)/shard_map/ppermute | solution.py:29
  63.0 3.4 %experts.3 = (bf16[128,512]{1,0:T(8,128)(2,1)S(1)}, bf16[128,512]{1,0:T(8,128)(2,1)S(1)}, f32[128,512]{1,0:T(8,128)S(1)}, f32[128,512]{1,0:T(8,128)S(1)}, bf16[4...) custom-call(s32[7]{0:T(128)S(1)} %stack.49.place, ...), custom_call_target="tpu_custom_call" | custom-call | tf_op jit(solution)/shard_map/experts/pallas_call | solution.py:45
  67.9 2.9 %weight_grads.1 = (f32[2,512,512]{2,1,0:T(8,128)S(1)}, f32[2,512,512]{2,1,0:T(8,128)S(1)}, bf16[4,512,512]{2,1,0:T(8,128)(2,1)S(1)}) custom-call(s32[7]{0:T(128)S(1)} %stack.49.place, bf16[128,512]{1,0:T(8,128)(2,1)S(1)} %collective-permute-done.13.refs_0_, bf16[128,512]{1,0:T(8,128)(2,1)S(1)} %collective-permute-done.14.refs_1_, ...), custom_call_target="tpu_custom_call" | custom-call | tf_op jit(solution)/shard_map/weight_grads/pallas_call | solution.py:45
  70.8 3.9 %collective-permute-done.23 = bf16[128,512]{1,0:T(8,128)(2,1)S(1)} collective-permute-done((bf16[128,512]{1,0:T(8,128)(2,1)S(1)}, bf16[128,512]{1,0:T(8,128)(2,1)S(1)}, u32[]{:S(2)}, u32[]{:S(2)}) %collective-permute-start.23) | collective-permute-done | bytes 131104 | tf_op jit(solution)/shard_map/ppermute | solution.py:29
  74.7 3.6 %collective-permute-done.22 = bf16[128,512]{1,0:T(8,128)(2,1)S(1)} collective-permute-done((bf16[128,512]{1,0:T(8,128)(2,1)S(1)}, bf16[128,512]{1,0:T(8,128)(2,1)S(1)}, u32[]{:S(2)}, u32[]{:S(2)}) %collective-permute-start.22) | collective-permute-done | bytes 131104 | tf_op jit(solution)/shard_map/ppermute | solution.py:29
  80.4 2.1 %collective-permute-done.25 = bf16[4,512,512]{2,1,0:T(8,128)(2,1)S(1)} collective-permute-done((bf16[4,512,512]{2,1,0:T(8,128)(2,1)S(1)}, bf16[4,512,512]{2,1,0:T(8,128)(2,1)S(1)}, u32[]{:S(2)}, u32[]{:S(2)}) %collective-permute-start.25) | collective-permute-done | bytes 2097184 | tf_op jit(solution)/shard_map/ppermute | solution.py:33
  89.1 2.1 %collective-permute-start.27 = (bf16[128,512]{1,0:T(8,128)(2,1)S(1)}, bf16[128,512]{1,0:T(8,128)(2,1)S(1)}, u32[]{:S(2)}, u32[]{:S(2)}) collective-permute-start(bf16[128,512]{1,0:T(8,128)(2,1)S(1)} %get-tuple-element.98), channel_id=1, source_target_pairs={{0,12},{1,13},{2,14},{3,15},{4,0},{5,1},{6,2},{7,3},{8,4},{9,5},{1... | collective-permute-start | bytes 393224 | tf_op jit(solution)/shard_map/ppermute | solution.py:29
  91.9 3.2 %collective-permute-done.27 = bf16[128,512]{1,0:T(8,128)(2,1)S(1)} collective-permute-done((bf16[128,512]{1,0:T(8,128)(2,1)S(1)}, bf16[128,512]{1,0:T(8,128)(2,1)S(1)}, u32[]{:S(2)}, u32[]{:S(2)}) %collective-permute-start.27) | collective-permute-done | bytes 131104 | tf_op jit(solution)/shard_map/ppermute | solution.py:29
  95.1 11.5 %collective-permute-start.29 = (bf16[128,512]{1,0:T(8,128)(2,1)S(1)}, bf16[128,512]{1,0:T(8,128)(2,1)S(1)}, u32[]{:S(2)}, u32[]{:S(2)}) collective-permute-start(bf16[128,512]{1,0:T(8,128)(2,1)S(1)} %get-tuple-element.101), channel_id=1, source_target_pairs={{0,4},{1,5},{2,6},{3,7},{4,8},{5,9},{6,10},{7,11},{8,12},{9,13},{1... | collective-permute-start | bytes 393224 | tf_op jit(solution)/shard_map/ppermute | solution.py:29
  106.6 2.2 %collective-permute-done.31 = bf16[128,512]{1,0:T(8,128)(2,1)S(1)} collective-permute-done((bf16[128,512]{1,0:T(8,128)(2,1)S(1)}, bf16[128,512]{1,0:T(8,128)(2,1)S(1)}, u32[]{:S(2)}, u32[]{:S(2)}) %collective-permute-start.31) | collective-permute-done | bytes 131104 | tf_op jit(solution)/shard_map/ppermute | solution.py:29
  109.6 3.7 %collective-permute-done.28 = bf16[128,512]{1,0:T(8,128)(2,1)S(1)} collective-permute-done((bf16[128,512]{1,0:T(8,128)(2,1)S(1)}, bf16[128,512]{1,0:T(8,128)(2,1)S(1)}, u32[]{:S(2)}, u32[]{:S(2)}) %collective-permute-start.28) | collective-permute-done | bytes 131104 | tf_op jit(solution)/shard_map/ppermute | solution.py:29
  114.1 2.2 %token_grad.1 = bf16[128,2048]{1,0:T(8,128)(2,1)} custom-call(s32[7]{0:T(128)S(1)} %stack.49.place, bf16[128,512]{1,0:T(8,128)(2,1)S(1)} %add_convert_fusion.3.refs_4_.delta, bf16[2,512,512]{2,1,0:T(8,128)(2,1)S(1)} %pad_maximum_fusion.downs, bf16[2,512,512]{2,1,0:T(8,128)(2,1)S(1)} %collective-permute-done.30.core_downs), custom_call_target="tpu_custom_call" | custom-call | tf_op jit(solution)/shard_map/token_grad/pallas_call | solution.py:45
  (84 shorter events, 32.1 us)
Async XLA Ops:
  4.9 10.1 %collective-permute-start.1 = (bf16[2,512,512]{2,1,0:T(8,128)(2,1)S(1)}, bf16[2,512,512]{2,1,0:T(8,128)(2,1)S(1)}, u32[]{:S(2)}, u32[]{:S(2)}) collective-permute-start(bf16[2,512,512]{2,1,0:T(8,128)(2,1)S(1)} %get-tuple-element.61.refs_4_), channel_id=1, source_target_pairs={{0,1},{1,0},{2,3},{3,2},{4,5},{5,4},{6,7},{7,6},{8,9},{9,8},{10,11... | collective-permute-start | bytes 3145736 | tf_op jit(solution)/shard_map/ppermute | solution.py:33
  5.4 9.5 %collective-permute-start = (bf16[2,128,512]{2,1,0:T(8,128)(2,1)S(1)}, bf16[2,128,512]{2,1,0:T(8,128)(2,1)S(1)}, u32[]{:S(2)}, u32[]{:S(2)}) collective-permute-start(bf16[2,128,512]{2,1,0:T(8,128)(2,1)S(1)} %get-tuple-element.59), channel_id=1, source_target_pairs={{0,2},{1,3},{2,0},{3,1},{4,6},{5,7},{6,4},{7,5},{8,10},{9,11},{10,... | collective-permute-start | bytes 786440 | tf_op jit(solution)/shard_map/ppermute | solution.py:33
  7.9 10.4 %collective-permute-start.4 = (bf16[128,512]{1,0:T(8,128)(2,1)}, bf16[128,512]{1,0:T(8,128)(2,1)S(1)}, u32[]{:S(2)}, u32[]{:S(2)}) collective-permute-start(bf16[128,512]{1,0:T(8,128)(2,1)} %refs_4_.1), channel_id=1, source_target_pairs={{0,4},{1,5},{2,6},{3,7},{4,8},{5,9},{6,10},{7,11},{8,12},{9,13},{1... | collective-permute-start | bytes 393224 | tf_op jit(solution)/shard_map/ppermute | solution.py:29
  9.5 11.8 %collective-permute-start.5 = (bf16[128,512]{1,0:T(8,128)(2,1)}, bf16[128,512]{1,0:T(8,128)(2,1)S(1)}, u32[]{:S(2)}, u32[]{:S(2)}) collective-permute-start(bf16[128,512]{1,0:T(8,128)(2,1)} %refs_4_.1), channel_id=1, source_target_pairs={{0,8},{1,9},{2,10},{3,11},{4,12},{5,13},{6,14},{7,15},{8,0},{9,1},... | collective-permute-start | bytes 393224 | tf_op jit(solution)/shard_map/ppermute | solution.py:29
  12.1 9.2 %collective-permute-start.6 = (bf16[128,512]{1,0:T(8,128)(2,1)}, bf16[128,512]{1,0:T(8,128)(2,1)S(1)}, u32[]{:S(2)}, u32[]{:S(2)}) collective-permute-start(bf16[128,512]{1,0:T(8,128)(2,1)} %refs_4_.1), channel_id=1, source_target_pairs={{0,12},{1,13},{2,14},{3,15},{4,0},{5,1},{6,2},{7,3},{8,4},{9,5},{1... | collective-permute-start | bytes 393224 | tf_op jit(solution)/shard_map/ppermute | solution.py:29
  22.4 17.2 %collective-permute-start.9 = (bf16[512,512]{1,0:T(8,128)(2,1)S(1)}, bf16[512,512]{1,0:T(8,128)(2,1)S(1)}, u32[]{:S(2)}, u32[]{:S(2)}) collective-permute-start(bf16[512,512]{1,0:T(8,128)(2,1)S(1)} %bitcast.26), channel_id=1, source_target_pairs={{0,2},{1,3},{2,0},{3,1},{4,6},{5,7},{6,4},{7,5},{8,10},{9,11},{10,... | collective-permute-start | bytes 1572872 | tf_op jit(solution)/shard_map/ppermute | solution.py:33
  23.0 16.6 %collective-permute-start.10 = (bf16[144,512]{1,0:T(8,128)(2,1)S(1)}, bf16[144,512]{1,0:T(8,128)(2,1)S(1)}, u32[]{:S(2)}, u32[]{:S(2)}) collective-permute-start(bf16[144,512]{1,0:T(8,128)(2,1)S(1)} %payload.1.refs_3_), channel_id=1, source_target_pairs={{0,4},{1,5},{2,6},{3,7},{4,8},{5,9},{6,10},{7,11},{8,12},{9,13},{1... | collective-permute-start | bytes 442376 | tf_op jit(solution)/shard_map/ppermute | solution.py:29
  26.3 13.3 %collective-permute-start.11 = (bf16[144,512]{1,0:T(8,128)(2,1)S(1)}, bf16[144,512]{1,0:T(8,128)(2,1)S(1)}, u32[]{:S(2)}, u32[]{:S(2)}) collective-permute-start(bf16[144,512]{1,0:T(8,128)(2,1)S(1)} %payload.1.refs_3_), channel_id=1, source_target_pairs={{0,8},{1,9},{2,10},{3,11},{4,12},{5,13},{6,14},{7,15},{8,0},{9,1},... | collective-permute-start | bytes 442376 | tf_op jit(solution)/shard_map/ppermute | solution.py:29
  27.9 11.7 %collective-permute-start.12 = (bf16[144,512]{1,0:T(8,128)(2,1)S(1)}, bf16[144,512]{1,0:T(8,128)(2,1)S(1)}, u32[]{:S(2)}, u32[]{:S(2)}) collective-permute-start(bf16[144,512]{1,0:T(8,128)(2,1)S(1)} %payload.1.refs_3_), channel_id=1, source_target_pairs={{0,12},{1,13},{2,14},{3,15},{4,0},{5,1},{6,2},{7,3},{8,4},{9,5},{1... | collective-permute-start | bytes 442376 | tf_op jit(solution)/shard_map/ppermute | solution.py:29
  28.8 10.8 %collective-permute-start.8 = (bf16[128,512]{1,0:T(8,128)(2,1)S(1)}, bf16[128,512]{1,0:T(8,128)(2,1)S(1)}, u32[]{:S(2)}, u32[]{:S(2)}) collective-permute-start(bf16[128,512]{1,0:T(8,128)(2,1)S(1)} %fusion.2), channel_id=1, source_target_pairs={{0,2},{1,3},{2,0},{3,1},{4,6},{5,7},{6,4},{7,5},{8,10},{9,11},{10,... | collective-permute-start | bytes 393224 | tf_op jit(solution)/shard_map/ppermute | solution.py:33
  39.7 13.7 %collective-permute-start.15 = (bf16[512,512]{1,0:T(8,128)(2,1)S(1)}, bf16[512,512]{1,0:T(8,128)(2,1)S(1)}, u32[]{:S(2)}, u32[]{:S(2)}) collective-permute-start(bf16[512,512]{1,0:T(8,128)(2,1)S(1)} %bitcast.27), channel_id=1, source_target_pairs={{0,2},{1,3},{2,0},{3,1},{4,6},{5,7},{6,4},{7,5},{8,10},{9,11},{10,... | collective-permute-start | bytes 1572872 | tf_op jit(solution)/shard_map/ppermute | solution.py:33
  40.3 8.8 %collective-permute-start.13 = (bf16[128,512]{1,0:T(8,128)(2,1)S(1)}, bf16[128,512]{1,0:T(8,128)(2,1)S(1)}, u32[]{:S(2)}, u32[]{:S(2)}) collective-permute-start(bf16[128,512]{1,0:T(8,128)(2,1)S(1)} %fusion.1.refs_1_.refs_3_), channel_id=1, source_target_pairs={{0,4},{1,5},{2,6},{3,7},{4,8},{5,9},{6,10},{7,11},{8,12},{9,13},{1... | collective-permute-start | bytes 393224 | tf_op jit(solution)/shard_map/ppermute | solution.py:29
  43.6 9.8 %collective-permute-start.14 = (bf16[128,512]{1,0:T(8,128)(2,1)S(1)}, bf16[128,512]{1,0:T(8,128)(2,1)S(1)}, u32[]{:S(2)}, u32[]{:S(2)}) collective-permute-start(bf16[128,512]{1,0:T(8,128)(2,1)S(1)} %fusion.1.refs_1_.refs_3_), channel_id=1, source_target_pairs={{0,8},{1,9},{2,10},{3,11},{4,12},{5,13},{6,14},{7,15},{8,0},{9,1},... | collective-permute-start | bytes 393224 | tf_op jit(solution)/shard_map/ppermute | solution.py:29
  45.2 8.2 %collective-permute-start.17 = (bf16[128,512]{1,0:T(8,128)(2,1)S(1)}, bf16[128,512]{1,0:T(8,128)(2,1)S(1)}, u32[]{:S(2)}, u32[]{:S(2)}) collective-permute-start(bf16[128,512]{1,0:T(8,128)(2,1)S(1)} %fusion.1.refs_1_.refs_3_), channel_id=1, source_target_pairs={{0,12},{1,13},{2,14},{3,15},{4,0},{5,1},{6,2},{7,3},{8,4},{9,5},{1... | collective-permute-start | bytes 393224 | tf_op jit(solution)/shard_map/ppermute | solution.py:29
  45.9 9.0 %collective-permute-start.16 = (bf16[512,512]{1,0:T(8,128)(2,1)S(1)}, bf16[512,512]{1,0:T(8,128)(2,1)S(1)}, u32[]{:S(2)}, u32[]{:S(2)}) collective-permute-start(bf16[512,512]{1,0:T(8,128)(2,1)S(1)} %collective-permute-done.9.refs_6_), channel_id=1, source_target_pairs={{0,1},{1,0},{2,3},{3,2},{4,5},{5,4},{6,7},{7,6},{8,9},{9,8},{10,11... | collective-permute-start | bytes 1572872 | tf_op jit(solution)/shard_map/ppermute | solution.py:33
  53.4 14.3 %collective-permute-start.21 = (bf16[512,512]{1,0:T(8,128)(2,1)S(1)}, bf16[512,512]{1,0:T(8,128)(2,1)S(1)}, u32[]{:S(2)}, u32[]{:S(2)}) collective-permute-start(bf16[512,512]{1,0:T(8,128)(2,1)S(1)} %get-tuple-element.87), channel_id=1, source_target_pairs={{0,2},{1,3},{2,0},{3,1},{4,6},{5,7},{6,4},{7,5},{8,10},{9,11},{10,... | collective-permute-start | bytes 1572872 | tf_op jit(solution)/shard_map/ppermute | solution.py:33
  58.7 9.1 %collective-permute-start.20 = (bf16[128,512]{1,0:T(8,128)(2,1)S(1)}, bf16[128,512]{1,0:T(8,128)(2,1)S(1)}, u32[]{:S(2)}, u32[]{:S(2)}) collective-permute-start(bf16[128,512]{1,0:T(8,128)(2,1)S(1)} %get-tuple-element.72), channel_id=1, source_target_pairs={{0,12},{1,13},{2,14},{3,15},{4,0},{5,1},{6,2},{7,3},{8,4},{9,5},{1... | collective-permute-start | bytes 393224 | tf_op jit(solution)/shard_map/ppermute | solution.py:29
  66.4 8.3 %collective-permute-start.23 = (bf16[128,512]{1,0:T(8,128)(2,1)S(1)}, bf16[128,512]{1,0:T(8,128)(2,1)S(1)}, u32[]{:S(2)}, u32[]{:S(2)}) collective-permute-start(bf16[128,512]{1,0:T(8,128)(2,1)S(1)} %get-tuple-element.92), channel_id=1, source_target_pairs={{0,4},{1,5},{2,6},{3,7},{4,8},{5,9},{6,10},{7,11},{8,12},{9,13},{1... | collective-permute-start | bytes 393224 | tf_op jit(solution)/shard_map/ppermute | solution.py:29
  66.5 11.8 %collective-permute-start.22 = (bf16[128,512]{1,0:T(8,128)(2,1)S(1)}, bf16[128,512]{1,0:T(8,128)(2,1)S(1)}, u32[]{:S(2)}, u32[]{:S(2)}) collective-permute-start(bf16[128,512]{1,0:T(8,128)(2,1)S(1)} %get-tuple-element.90), channel_id=1, source_target_pairs={{0,8},{1,9},{2,10},{3,11},{4,12},{5,13},{6,14},{7,15},{8,0},{9,1},... | collective-permute-start | bytes 393224 | tf_op jit(solution)/shard_map/ppermute | solution.py:29
  87.4 26.7 %collective-permute-start.30 = (bf16[2,512,512]{2,1,0:T(8,128)(2,1)S(1)}, bf16[2,512,512]{2,1,0:T(8,128)(2,1)S(1)}, u32[]{:S(2)}, u32[]{:S(2)}) collective-permute-start(bf16[2,512,512]{2,1,0:T(8,128)(2,1)S(1)} %pad_maximum_fusion.downs), channel_id=1, source_target_pairs={{0,1},{1,0},{2,3},{3,2},{4,5},{5,4},{6,7},{7,6},{8,9},{9,8},{10,11... | collective-permute-start | bytes 3145736 | tf_op jit(solution)/shard_map/ppermute | solution.py:33
  87.6 28.7 %collective-permute-start.33 = (bf16[2,512,512]{2,1,0:T(8,128)(2,1)S(1)}, bf16[2,512,512]{2,1,0:T(8,128)(2,1)S(1)}, u32[]{:S(2)}, u32[]{:S(2)}) collective-permute-start(bf16[2,512,512]{2,1,0:T(8,128)(2,1)S(1)} %add_convert_fusion.1), channel_id=1, source_target_pairs={{0,2},{1,3},{2,0},{3,1},{4,6},{5,7},{6,4},{7,5},{8,10},{9,11},{10,... | collective-permute-start | bytes 3145736 | tf_op jit(solution)/shard_map/ppermute | solution.py:33
  91.2 15.5 %collective-permute-start.32 = (bf16[128,512]{1,0:T(8,128)(2,1)S(1)}, bf16[128,512]{1,0:T(8,128)(2,1)S(1)}, u32[]{:S(2)}, u32[]{:S(2)}) collective-permute-start(bf16[128,512]{1,0:T(8,128)(2,1)S(1)} %get-tuple-element.106), channel_id=1, source_target_pairs={{0,4},{1,5},{2,6},{3,7},{4,8},{5,9},{6,10},{7,11},{8,12},{9,13},{1... | collective-permute-start | bytes 393224 | tf_op jit(solution)/shard_map/ppermute | solution.py:29
  91.2 17.7 %collective-permute-start.31 = (bf16[128,512]{1,0:T(8,128)(2,1)S(1)}, bf16[128,512]{1,0:T(8,128)(2,1)S(1)}, u32[]{:S(2)}, u32[]{:S(2)}) collective-permute-start(bf16[128,512]{1,0:T(8,128)(2,1)S(1)} %get-tuple-element.105), channel_id=1, source_target_pairs={{0,8},{1,9},{2,10},{3,11},{4,12},{5,13},{6,14},{7,15},{8,0},{9,1},... | collective-permute-start | bytes 393224 | tf_op jit(solution)/shard_map/ppermute | solution.py:29
  95.1 14.6 %collective-permute-start.29 = (bf16[128,512]{1,0:T(8,128)(2,1)S(1)}, bf16[128,512]{1,0:T(8,128)(2,1)S(1)}, u32[]{:S(2)}, u32[]{:S(2)}) collective-permute-start(bf16[128,512]{1,0:T(8,128)(2,1)S(1)} %get-tuple-element.101), channel_id=1, source_target_pairs={{0,4},{1,5},{2,6},{3,7},{4,8},{5,9},{6,10},{7,11},{8,12},{9,13},{1... | collective-permute-start | bytes 393224 | tf_op jit(solution)/shard_map/ppermute | solution.py:29
  (19 other events, 113.8 us)

commit v10 on v9

--- a/solution.py
+++ b/solution.py
@@ -39,14 +39,14 @@
 
 def call(body, outs, name, scratch=(), outside=0):
     vmem = pl.BlockSpec(memory_space=pltpu.VMEM)
-    anywhere = pl.BlockSpec(memory_space=pl.ANY)
+    outer = pl.BlockSpec(memory_space=pltpu.HBM)
 
     def run(place, *operands):
         return pl.pallas_call(
             body,
             out_shape=outs,
             in_specs=[pl.BlockSpec(memory_space=pltpu.SMEM)]
-            + [anywhere] * outside
+            + [outer] * outside
             + [vmem] * (len(operands) - outside),
             out_specs=[vmem] * len(outs),
             scratch_shapes=list(scratch),
@@ -177,17 +177,20 @@
 
 def down_grad_body(n_line, place, *refs):
     own, across, core, core_across, *deltas, core_deltas = refs[:7]
-    blocks = refs[7:]
+    riders, blocks = refs[7:-n_line], refs[-n_line:]
     tokens = jnp.concatenate([own[...], across[0], core[...], core_across[...]], axis=0)
     delta = jnp.concatenate([d[...] for d in deltas] + [core_deltas[0], core_deltas[1]], axis=0)
     part = lax.dot_general(tokens, delta, contract_first, preferred_element_type=wide)
     block = blocks[0].shape[0]
+    targets = [out if len(out.shape) == 2 else out.at[0] for out in blocks]
+    for rider, out in zip(riders, [out for out in blocks if len(out.shape) == 3]):
+        out[1] = rider[...]
     for z in range(n_line):
         for back in range(n_line):
 
             @pl.when(lax.rem(place[0] + n_line - back, n_line) == z)
             def _(z=z, back=back):
-                blocks[back][...] = part[z * block : (z + 1) * block].astype(blocks[back].dtype)
+                targets[back][...] = part[z * block : (z + 1) * block].astype(targets[back].dtype)
 
 
 def token_grad_body(n_line, block, place, delta, downs, core_downs, out):
@@ -247,8 +250,8 @@
     payloads = [payload] + [turn(after(payload, *downs[1:]), n_line, back) for back in range(1, n_line)]
     crossed = swap(half[1].astype(narrow), n_line, 0, 1).astype(wide)
     latent = (half[0] + after(crossed, side_in, *payloads[1:])).astype(narrow)
-    middle = list(range(2, n_line - 1))
-    groups = [[1] + middle, [n_line - 1, 0]]
+    groups = [[*range(1, n_line), 0]]
+    riding = range(2, n_line)
     rows = [latent] + [turn(latent, n_line, back) for back in range(1, n_line)]
 
     side_out = swap(after(expert_out[0], latent), n_line, 0, 1)
@@ -290,27 +293,30 @@
     delta_lines = [after(line, near, both_down) for line in delta_lines]
     delta = sum(line.astype(wide) for line in delta_lines).astype(narrow)
     side_delta = swap(delta, n_line, 0, 1)
-    first_out = home(outs_of[1], 1)
+    out_lines = [outs_of[0]] + [home(outs_of[back], back) if back not in riding else None for back in range(1, n_line)]
     other = swap(after(other, delta), n_line, 1, 0)
-    far = (far + other[2:].astype(wide)).astype(narrow)
+    far = (far + after(other, out_lines[1])[2:].astype(wide)).astype(narrow)
     sent = far
     far = swap(after(far, side_delta), n_line, 0, 1)
-    core_deltas = swap(jnp.stack([delta, after(side_delta, first_out, sent)]), n_line, 1, 0)
+    core_deltas = swap(jnp.stack([delta, after(side_delta, sent)]), n_line, 1, 0)
     blocks = call(
         functools.partial(down_grad_body, n_line),
-        [shape((block, latent_width), wide)] + [shape((block, latent_width), narrow)] * (n_line - 1),
+        [
+            shape((2, block, latent_width) if back in riding else (block, latent_width), narrow if back else wide)
+            for back in range(n_line)
+        ],
         "down_grad",
-    )(place, columns[0], across, *core_tokens, delta, side_delta, core_deltas)
+    )(place, columns[0], across, *core_tokens, delta, side_delta, core_deltas, *(outs_of[back] for back in riding))
     core_down = swap(after(both_down, blocks[1]), n_line, 1, 0)
     (grad_tokens,) = call(
         functools.partial(token_grad_body, n_line, block), [shape((tok_rows, width), narrow)], "token_grad"
     )(place, after(delta, blocks[1]), both_down, core_down)
     blocks = [blocks[0]] + [turn(blocks[back], n_line, n_line - back) for back in range(1, n_line)]
-    first_block = blocks[1]
-    out_lines = [outs_of[0], first_out] + [home(after(outs_of[back], first_block), back) for back in range(2, n_line)]
+    grad_down = sum((value[0] if back in riding else value).astype(wide) for back, value in enumerate(blocks))
+    out_lines = [blocks[back][1] if back in riding else line for back, line in enumerate(out_lines)]
+    out_lines[0] = after(out_lines[0], grad_tokens)
     latent_out = sum(line.astype(wide) for line in out_lines).astype(narrow)
-    grad_down = sum(value.astype(wide) for value in blocks)
-    weight_grad = (near + other[:2].astype(wide) + after(far, grad_tokens).astype(wide)).astype(narrow)
+    weight_grad = (near + other[:2].astype(wide) + far.astype(wide)).astype(narrow)
     return (latent_out, grad_tokens, grad_down, weight_grad[:1], weight_grad[1:])
 
 

time: 118 us -> 114 us (0.966)
  starting transfers between devices: 47.9 us -> 37.6 us
  waiting for transfers between devices: 44 us -> 52 us
    ppermute x16, waiting for transfers between devices: 15.6 us -> 31.6 us  [swap(): lax.ppermute(value, plane, device_pairs(n_line, lambda z, x, c: (z, x ^ s...]
    ppermute x18 -> x16, starting transfers between devices: 36.6 us -> 26.2 us  [turn(): lax.ppermute(value, plane, device_pairs(n_line, lambda z, x, c: ((z + by)...]
    ppermute x18 -> x16, waiting for transfers between devices: 28.5 us -> 20.5 us  [turn(): lax.ppermute(value, plane, device_pairs(n_line, lambda z, x, c: ((z + by)...]
    pallas_call x8 -> x7, Pallas kernels: 15.7 us -> 15 us  [run(): pl.pallas_call(body, out_shape=outs, in_specs=[pl.BlockSpec(memory_space=...]
  transfers between devices with their start and end apart: 34 -> 32, of which waited for: 16 -> 13; matrix products, arithmetic and copies ran while one was open for 2% -> 2% of each run, Pallas kernels for 11% -> 11%
where the time goes in v10:
time: 114 us
  waiting for transfers between devices  52 us (46%)
  starting transfers between devices  37.6 us (33%)
  Pallas kernels  15 us (13%)
  local copies, waits for them, and re-layouts  6.56 us (6%)
  other arithmetic  2.05 us (2%)
    ppermute x16, waiting for transfers between devices, swap(): lax.ppermute(value, plane, device_pairs(n_line, lambda z, x, c: (z, x ^ s...  31.6 us
    ppermute x16, starting transfers between devices, turn(): lax.ppermute(value, plane, device_pairs(n_line, lambda z, x, c: ((z + by)...  26.2 us
    ppermute x16, waiting for transfers between devices, turn(): lax.ppermute(value, plane, device_pairs(n_line, lambda z, x, c: ((z + by)...  20.5 us
    pallas_call x7, Pallas kernels, run(): pl.pallas_call(body, out_shape=outs, in_specs=[pl.BlockSpec(memory_space=...  15 us
    ppermute x16, starting transfers between devices, swap(): lax.ppermute(value, plane, device_pairs(n_line, lambda z, x, c: (z, x ^ s...  11.4 us
    unnamed x18, local copies, waits for them, and re-layouts  5.42 us
  transfers between devices with their start and end apart: 32, of which 13 were waited for; matrix products, arithmetic and copies ran while one was open for 2% of the time, Pallas kernels for 11%

profile of v10, /device:TPU:0, one launch (start us, length us, event | category | flops | bytes accessed | tf_op | source)
XLA Modules:
  0.0 114.2 jit_solution(5367647726620811699)
XLA Ops:
  5.4 2.6 %collective-permute-start = (bf16[2,128,512]{2,1,0:T(8,128)(2,1)S(1)}, bf16[2,128,512]{2,1,0:T(8,128)(2,1)S(1)}, u32[]{:S(2)}, u32[]{:S(2)}) collective-permute-start(bf16[2,128,512]{2,1,0:T(8,128)(2,1)S(1)} %get-tuple-element.54), channel_id=1, source_target_pairs={{0,2},{1,3},{2,0},{3,1},{4,6},{5,7},{6,4},{7,5},{8,10},{9,11},{10,... | collective-permute-start | bytes 786440 | tf_op jit(solution)/shard_map/ppermute | solution.py:33
  7.9 1.6 %collective-permute-start.4 = (bf16[128,512]{1,0:T(8,128)(2,1)}, bf16[128,512]{1,0:T(8,128)(2,1)S(1)}, u32[]{:S(2)}, u32[]{:S(2)}) collective-permute-start(bf16[128,512]{1,0:T(8,128)(2,1)} %refs_4_.1), channel_id=1, source_target_pairs={{0,4},{1,5},{2,6},{3,7},{4,8},{5,9},{6,10},{7,11},{8,12},{9,13},{1... | collective-permute-start | bytes 393224 | tf_op jit(solution)/shard_map/ppermute | solution.py:29
  9.5 2.6 %collective-permute-start.5 = (bf16[128,512]{1,0:T(8,128)(2,1)}, bf16[128,512]{1,0:T(8,128)(2,1)S(1)}, u32[]{:S(2)}, u32[]{:S(2)}) collective-permute-start(bf16[128,512]{1,0:T(8,128)(2,1)} %refs_4_.1), channel_id=1, source_target_pairs={{0,8},{1,9},{2,10},{3,11},{4,12},{5,13},{6,14},{7,15},{8,0},{9,1},... | collective-permute-start | bytes 393224 | tf_op jit(solution)/shard_map/ppermute | solution.py:29
  18.3 3.0 %collective-permute-done.5.refs_6_ = bf16[128,512]{1,0:T(8,128)(2,1)S(1)} collective-permute-done((bf16[128,512]{1,0:T(8,128)(2,1)}, bf16[128,512]{1,0:T(8,128)(2,1)S(1)}, u32[]{:S(2)}, u32[]{:S(2)}) %collective-permute-start.5) | collective-permute-done | bytes 131104 | tf_op jit(solution)/shard_map/ppermute | solution.py:29
  23.0 3.3 %collective-permute-start.10 = (bf16[144,512]{1,0:T(8,128)(2,1)S(1)}, bf16[144,512]{1,0:T(8,128)(2,1)S(1)}, u32[]{:S(2)}, u32[]{:S(2)}) collective-permute-start(bf16[144,512]{1,0:T(8,128)(2,1)S(1)} %payload.1.refs_7_), channel_id=1, source_target_pairs={{0,4},{1,5},{2,6},{3,7},{4,8},{5,9},{6,10},{7,11},{8,12},{9,13},{1... | collective-permute-start | bytes 442376 | tf_op jit(solution)/shard_map/ppermute | solution.py:29
  26.3 1.6 %collective-permute-start.11 = (bf16[144,512]{1,0:T(8,128)(2,1)S(1)}, bf16[144,512]{1,0:T(8,128)(2,1)S(1)}, u32[]{:S(2)}, u32[]{:S(2)}) collective-permute-start(bf16[144,512]{1,0:T(8,128)(2,1)S(1)} %payload.1.refs_7_), channel_id=1, source_target_pairs={{0,8},{1,9},{2,10},{3,11},{4,12},{5,13},{6,14},{7,15},{8,0},{9,1},... | collective-permute-start | bytes 442376 | tf_op jit(solution)/shard_map/ppermute | solution.py:29
  28.8 1.6 %collective-permute-start.8 = (bf16[128,512]{1,0:T(8,128)(2,1)S(1)}, bf16[128,512]{1,0:T(8,128)(2,1)S(1)}, u32[]{:S(2)}, u32[]{:S(2)}) collective-permute-start(bf16[128,512]{1,0:T(8,128)(2,1)S(1)} %fusion.3), channel_id=1, source_target_pairs={{0,2},{1,3},{2,0},{3,1},{4,6},{5,7},{6,4},{7,5},{8,10},{9,11},{10,... | collective-permute-start | bytes 393224 | tf_op jit(solution)/shard_map/ppermute | solution.py:33
  30.3 9.2 %collective-permute-done.8 = bf16[128,512]{1,0:T(8,128)(2,1)S(1)} collective-permute-done((bf16[128,512]{1,0:T(8,128)(2,1)S(1)}, bf16[128,512]{1,0:T(8,128)(2,1)S(1)}, u32[]{:S(2)}, u32[]{:S(2)}) %collective-permute-start.8) | collective-permute-done | bytes 131104 | tf_op jit(solution)/shard_map/ppermute | solution.py:33
  40.3 3.3 %collective-permute-start.13 = (bf16[128,512]{1,0:T(8,128)(2,1)S(1)}, bf16[128,512]{1,0:T(8,128)(2,1)S(1)}, u32[]{:S(2)}, u32[]{:S(2)}) collective-permute-start(bf16[128,512]{1,0:T(8,128)(2,1)S(1)} %fusion.1.refs_3_), channel_id=1, source_target_pairs={{0,4},{1,5},{2,6},{3,7},{4,8},{5,9},{6,10},{7,11},{8,12},{9,13},{1... | collective-permute-start | bytes 393224 | tf_op jit(solution)/shard_map/ppermute | solution.py:29
  43.6 1.6 %collective-permute-start.14 = (bf16[128,512]{1,0:T(8,128)(2,1)S(1)}, bf16[128,512]{1,0:T(8,128)(2,1)S(1)}, u32[]{:S(2)}, u32[]{:S(2)}) collective-permute-start(bf16[128,512]{1,0:T(8,128)(2,1)S(1)} %fusion.1.refs_3_), channel_id=1, source_target_pairs={{0,8},{1,9},{2,10},{3,11},{4,12},{5,13},{6,14},{7,15},{8,0},{9,1},... | collective-permute-start | bytes 393224 | tf_op jit(solution)/shard_map/ppermute | solution.py:29
  45.9 3.2 %collective-permute-done.13.refs_0_ = bf16[128,512]{1,0:T(8,128)(2,1)S(1)} collective-permute-done((bf16[128,512]{1,0:T(8,128)(2,1)S(1)}, bf16[128,512]{1,0:T(8,128)(2,1)S(1)}, u32[]{:S(2)}, u32[]{:S(2)}) %collective-permute-start.13) | collective-permute-done | bytes 131104 | tf_op jit(solution)/shard_map/ppermute | solution.py:29
  49.1 4.3 %collective-permute-done.14.refs_1_ = bf16[128,512]{1,0:T(8,128)(2,1)S(1)} collective-permute-done((bf16[128,512]{1,0:T(8,128)(2,1)S(1)}, bf16[128,512]{1,0:T(8,128)(2,1)S(1)}, u32[]{:S(2)}, u32[]{:S(2)}) %collective-permute-start.14) | collective-permute-done | bytes 131104 | tf_op jit(solution)/shard_map/ppermute | solution.py:29
  53.4 1.5 %collective-permute-start.20 = (bf16[512,512]{1,0:T(8,128)(2,1)S(1)}, bf16[512,512]{1,0:T(8,128)(2,1)S(1)}, u32[]{:S(2)}, u32[]{:S(2)}) collective-permute-start(bf16[512,512]{1,0:T(8,128)(2,1)S(1)} %get-tuple-element.76), channel_id=1, source_target_pairs={{0,2},{1,3},{2,0},{3,1},{4,6},{5,7},{6,4},{7,5},{8,10},{9,11},{10,... | collective-permute-start | bytes 1572872 | tf_op jit(solution)/shard_map/ppermute | solution.py:33
  55.3 6.1 %experts.1 = (bf16[128,512]{1,0:T(8,128)(2,1)S(1)}, bf16[128,512]{1,0:T(8,128)(2,1)S(1)}, bf16[128,512]{1,0:T(8,128)(2,1)S(1)}, bf16[128,512]{1,0:T(8,128)(2,1)S...) custom-call(s32[7]{0:T(128)S(1)} %stack.49.place, ...), custom_call_target="tpu_custom_call" | custom-call | tf_op jit(solution)/shard_map/experts/pallas_call | solution.py:45
  61.5 3.3 %collective-permute-start.22 = (bf16[128,512]{1,0:T(8,128)(2,1)S(1)}, bf16[128,512]{1,0:T(8,128)(2,1)S(1)}, u32[]{:S(2)}, u32[]{:S(2)}) collective-permute-start(bf16[128,512]{1,0:T(8,128)(2,1)S(1)} %get-tuple-element.81), channel_id=1, source_target_pairs={{0,4},{1,5},{2,6},{3,7},{4,8},{5,9},{6,10},{7,11},{8,12},{9,13},{1... | collective-permute-start | bytes 393224 | tf_op jit(solution)/shard_map/ppermute | solution.py:29
  67.9 4.4 %collective-permute-done.19 = bf16[128,512]{1,0:T(8,128)(2,1)S(1)} collective-permute-done((bf16[128,512]{1,0:T(8,128)(2,1)S(1)}, bf16[128,512]{1,0:T(8,128)(2,1)S(1)}, u32[]{:S(2)}, u32[]{:S(2)}) %collective-permute-start.19) | collective-permute-done | bytes 131104 | tf_op jit(solution)/shard_map/ppermute | solution.py:29
  72.3 2.9 %weight_grads.1 = (f32[2,512,512]{2,1,0:T(8,128)S(1)}, f32[2,512,512]{2,1,0:T(8,128)S(1)}, bf16[4,512,512]{2,1,0:T(8,128)(2,1)S(1)}) custom-call(s32[7]{0:T(128)S(1)} %stack.49.place, bf16[128,512]{1,0:T(8,128)(2,1)S(1)} %collective-permute-done.13.refs_0_, bf16[128,512]{1,0:T(8,128)(2,1)S(1)} %collective-permute-done.14.refs_1_, ...), custom_call_target="tpu_custom_call" | custom-call | tf_op jit(solution)/shard_map/weight_grads/pallas_call | solution.py:45
  75.2 2.7 %collective-permute-done.21 = bf16[128,512]{1,0:T(8,128)(2,1)S(1)} collective-permute-done((bf16[128,512]{1,0:T(8,128)(2,1)S(1)}, bf16[128,512]{1,0:T(8,128)(2,1)S(1)}, u32[]{:S(2)}, u32[]{:S(2)}) %collective-permute-start.21) | collective-permute-done | bytes 131104 | tf_op jit(solution)/shard_map/ppermute | solution.py:29
  78.1 1.5 %collective-permute-start.25 = (bf16[128,512]{1,0:T(8,128)(2,1)S(1)}, bf16[128,512]{1,0:T(8,128)(2,1)S(1)}, u32[]{:S(2)}, u32[]{:S(2)}) collective-permute-start(bf16[128,512]{1,0:T(8,128)(2,1)S(1)} %get-tuple-element.86), channel_id=1, source_target_pairs={{0,12},{1,13},{2,14},{3,15},{4,0},{5,1},{6,2},{7,3},{8,4},{9,5},{1... | collective-permute-start | bytes 393224 | tf_op jit(solution)/shard_map/ppermute | solution.py:29
  81.1 2.9 %collective-permute-done.25 = bf16[128,512]{1,0:T(8,128)(2,1)S(1)} collective-permute-done((bf16[128,512]{1,0:T(8,128)(2,1)S(1)}, bf16[128,512]{1,0:T(8,128)(2,1)S(1)}, u32[]{:S(2)}, u32[]{:S(2)}) %collective-permute-start.25) | collective-permute-done | bytes 131104 | tf_op jit(solution)/shard_map/ppermute | solution.py:29
  86.8 1.5 %collective-permute-done.26.refs_6_ = bf16[2,128,512]{2,1,0:T(8,128)(2,1)S(1)} collective-permute-done((bf16[2,128,512]{2,1,0:T(8,128)(2,1)S(1)}, bf16[2,128,512]{2,1,0:T(8,128)(2,1)S(1)}, u32[]{:S(2)}, u32[]{:S(2)}) %collective-permute-start.26) | collective-permute-done | bytes 262176 | tf_op jit(solution)/shard_map/ppermute | solution.py:33
  89.7 2.6 %collective-permute-start.30 = (bf16[128,512]{1,0:T(8,128)(2,1)S(1)}, bf16[128,512]{1,0:T(8,128)(2,1)S(1)}, u32[]{:S(2)}, u32[]{:S(2)}) collective-permute-start(bf16[128,512]{1,0:T(8,128)(2,1)S(1)} %get-tuple-element.91), channel_id=1, source_target_pairs={{0,12},{1,13},{2,14},{3,15},{4,0},{5,1},{6,2},{7,3},{8,4},{9,5},{1... | collective-permute-start | bytes 393224 | tf_op jit(solution)/shard_map/ppermute | solution.py:29
  92.8 16.8 %collective-permute-done.31 = bf16[2,512,512]{2,1,0:T(8,128)(2,1)S(1)} collective-permute-done((bf16[2,512,512]{2,1,0:T(8,128)(2,1)S(1)}, bf16[2,512,512]{2,1,0:T(8,128)(2,1)S(1)}, u32[]{:S(2)}, u32[]{:S(2)}) %collective-permute-start.31) | collective-permute-done | bytes 1048608 | tf_op jit(solution)/shard_map/ppermute | solution.py:33
  111.1 2.2 %token_grad.1 = bf16[128,2048]{1,0:T(8,128)(2,1)} custom-call(s32[7]{0:T(128)S(1)} %stack.49.place, bf16[128,512]{1,0:T(8,128)(2,1)S(1)} %add_convert_fusion.2.refs_4_.delta, bf16[2,512,512]{2,1,0:T(8,128)(2,1)S(1)} %pad_maximum_fusion.downs, bf16[2,512,512]{2,1,0:T(8,128)(2,1)S(1)} %collective-permute-done.27.core_downs), custom_call_target="tpu_custom_call" | custom-call | tf_op jit(solution)/shard_map/token_grad/pallas_call | solution.py:45
  (78 shorter events, 27.1 us)
Async XLA Ops:
  4.9 10.1 %collective-permute-start.1 = (bf16[2,512,512]{2,1,0:T(8,128)(2,1)S(1)}, bf16[2,512,512]{2,1,0:T(8,128)(2,1)S(1)}, u32[]{:S(2)}, u32[]{:S(2)}) collective-permute-start(bf16[2,512,512]{2,1,0:T(8,128)(2,1)S(1)} %get-tuple-element.56.refs_8_), channel_id=1, source_target_pairs={{0,1},{1,0},{2,3},{3,2},{4,5},{5,4},{6,7},{7,6},{8,9},{9,8},{10,11... | collective-permute-start | bytes 3145736 | tf_op jit(solution)/shard_map/ppermute | solution.py:33
  5.4 9.5 %collective-permute-start = (bf16[2,128,512]{2,1,0:T(8,128)(2,1)S(1)}, bf16[2,128,512]{2,1,0:T(8,128)(2,1)S(1)}, u32[]{:S(2)}, u32[]{:S(2)}) collective-permute-start(bf16[2,128,512]{2,1,0:T(8,128)(2,1)S(1)} %get-tuple-element.54), channel_id=1, source_target_pairs={{0,2},{1,3},{2,0},{3,1},{4,6},{5,7},{6,4},{7,5},{8,10},{9,11},{10,... | collective-permute-start | bytes 786440 | tf_op jit(solution)/shard_map/ppermute | solution.py:33
  7.9 10.4 %collective-permute-start.4 = (bf16[128,512]{1,0:T(8,128)(2,1)}, bf16[128,512]{1,0:T(8,128)(2,1)S(1)}, u32[]{:S(2)}, u32[]{:S(2)}) collective-permute-start(bf16[128,512]{1,0:T(8,128)(2,1)} %refs_4_.1), channel_id=1, source_target_pairs={{0,4},{1,5},{2,6},{3,7},{4,8},{5,9},{6,10},{7,11},{8,12},{9,13},{1... | collective-permute-start | bytes 393224 | tf_op jit(solution)/shard_map/ppermute | solution.py:29
  9.5 11.8 %collective-permute-start.5 = (bf16[128,512]{1,0:T(8,128)(2,1)}, bf16[128,512]{1,0:T(8,128)(2,1)S(1)}, u32[]{:S(2)}, u32[]{:S(2)}) collective-permute-start(bf16[128,512]{1,0:T(8,128)(2,1)} %refs_4_.1), channel_id=1, source_target_pairs={{0,8},{1,9},{2,10},{3,11},{4,12},{5,13},{6,14},{7,15},{8,0},{9,1},... | collective-permute-start | bytes 393224 | tf_op jit(solution)/shard_map/ppermute | solution.py:29
  12.1 9.2 %collective-permute-start.6 = (bf16[128,512]{1,0:T(8,128)(2,1)}, bf16[128,512]{1,0:T(8,128)(2,1)S(1)}, u32[]{:S(2)}, u32[]{:S(2)}) collective-permute-start(bf16[128,512]{1,0:T(8,128)(2,1)} %refs_4_.1), channel_id=1, source_target_pairs={{0,12},{1,13},{2,14},{3,15},{4,0},{5,1},{6,2},{7,3},{8,4},{9,5},{1... | collective-permute-start | bytes 393224 | tf_op jit(solution)/shard_map/ppermute | solution.py:29
  22.4 17.2 %collective-permute-start.9 = (bf16[512,512]{1,0:T(8,128)(2,1)S(1)}, bf16[512,512]{1,0:T(8,128)(2,1)S(1)}, u32[]{:S(2)}, u32[]{:S(2)}) collective-permute-start(bf16[512,512]{1,0:T(8,128)(2,1)S(1)} %bitcast.46), channel_id=1, source_target_pairs={{0,2},{1,3},{2,0},{3,1},{4,6},{5,7},{6,4},{7,5},{8,10},{9,11},{10,... | collective-permute-start | bytes 1572872 | tf_op jit(solution)/shard_map/ppermute | solution.py:33
  23.0 16.6 %collective-permute-start.10 = (bf16[144,512]{1,0:T(8,128)(2,1)S(1)}, bf16[144,512]{1,0:T(8,128)(2,1)S(1)}, u32[]{:S(2)}, u32[]{:S(2)}) collective-permute-start(bf16[144,512]{1,0:T(8,128)(2,1)S(1)} %payload.1.refs_7_), channel_id=1, source_target_pairs={{0,4},{1,5},{2,6},{3,7},{4,8},{5,9},{6,10},{7,11},{8,12},{9,13},{1... | collective-permute-start | bytes 442376 | tf_op jit(solution)/shard_map/ppermute | solution.py:29
  26.3 13.3 %collective-permute-start.11 = (bf16[144,512]{1,0:T(8,128)(2,1)S(1)}, bf16[144,512]{1,0:T(8,128)(2,1)S(1)}, u32[]{:S(2)}, u32[]{:S(2)}) collective-permute-start(bf16[144,512]{1,0:T(8,128)(2,1)S(1)} %payload.1.refs_7_), channel_id=1, source_target_pairs={{0,8},{1,9},{2,10},{3,11},{4,12},{5,13},{6,14},{7,15},{8,0},{9,1},... | collective-permute-start | bytes 442376 | tf_op jit(solution)/shard_map/ppermute | solution.py:29
  27.9 11.7 %collective-permute-start.12 = (bf16[144,512]{1,0:T(8,128)(2,1)S(1)}, bf16[144,512]{1,0:T(8,128)(2,1)S(1)}, u32[]{:S(2)}, u32[]{:S(2)}) collective-permute-start(bf16[144,512]{1,0:T(8,128)(2,1)S(1)} %payload.1.refs_7_), channel_id=1, source_target_pairs={{0,12},{1,13},{2,14},{3,15},{4,0},{5,1},{6,2},{7,3},{8,4},{9,5},{1... | collective-permute-start | bytes 442376 | tf_op jit(solution)/shard_map/ppermute | solution.py:29
  28.8 10.8 %collective-permute-start.8 = (bf16[128,512]{1,0:T(8,128)(2,1)S(1)}, bf16[128,512]{1,0:T(8,128)(2,1)S(1)}, u32[]{:S(2)}, u32[]{:S(2)}) collective-permute-start(bf16[128,512]{1,0:T(8,128)(2,1)S(1)} %fusion.3), channel_id=1, source_target_pairs={{0,2},{1,3},{2,0},{3,1},{4,6},{5,7},{6,4},{7,5},{8,10},{9,11},{10,... | collective-permute-start | bytes 393224 | tf_op jit(solution)/shard_map/ppermute | solution.py:33
  39.7 13.7 %collective-permute-start.16 = (bf16[512,512]{1,0:T(8,128)(2,1)S(1)}, bf16[512,512]{1,0:T(8,128)(2,1)S(1)}, u32[]{:S(2)}, u32[]{:S(2)}) collective-permute-start(bf16[512,512]{1,0:T(8,128)(2,1)S(1)} %bitcast.47), channel_id=1, source_target_pairs={{0,2},{1,3},{2,0},{3,1},{4,6},{5,7},{6,4},{7,5},{8,10},{9,11},{10,... | collective-permute-start | bytes 1572872 | tf_op jit(solution)/shard_map/ppermute | solution.py:33
  40.3 8.8 %collective-permute-start.13 = (bf16[128,512]{1,0:T(8,128)(2,1)S(1)}, bf16[128,512]{1,0:T(8,128)(2,1)S(1)}, u32[]{:S(2)}, u32[]{:S(2)}) collective-permute-start(bf16[128,512]{1,0:T(8,128)(2,1)S(1)} %fusion.1.refs_3_), channel_id=1, source_target_pairs={{0,4},{1,5},{2,6},{3,7},{4,8},{5,9},{6,10},{7,11},{8,12},{9,13},{1... | collective-permute-start | bytes 393224 | tf_op jit(solution)/shard_map/ppermute | solution.py:29
  43.6 9.8 %collective-permute-start.14 = (bf16[128,512]{1,0:T(8,128)(2,1)S(1)}, bf16[128,512]{1,0:T(8,128)(2,1)S(1)}, u32[]{:S(2)}, u32[]{:S(2)}) collective-permute-start(bf16[128,512]{1,0:T(8,128)(2,1)S(1)} %fusion.1.refs_3_), channel_id=1, source_target_pairs={{0,8},{1,9},{2,10},{3,11},{4,12},{5,13},{6,14},{7,15},{8,0},{9,1},... | collective-permute-start | bytes 393224 | tf_op jit(solution)/shard_map/ppermute | solution.py:29
  45.2 8.2 %collective-permute-start.15 = (bf16[128,512]{1,0:T(8,128)(2,1)S(1)}, bf16[128,512]{1,0:T(8,128)(2,1)S(1)}, u32[]{:S(2)}, u32[]{:S(2)}) collective-permute-start(bf16[128,512]{1,0:T(8,128)(2,1)S(1)} %fusion.1.refs_3_), channel_id=1, source_target_pairs={{0,12},{1,13},{2,14},{3,15},{4,0},{5,1},{6,2},{7,3},{8,4},{9,5},{1... | collective-permute-start | bytes 393224 | tf_op jit(solution)/shard_map/ppermute | solution.py:29
  45.9 9.0 %collective-permute-start.17 = (bf16[512,512]{1,0:T(8,128)(2,1)S(1)}, bf16[512,512]{1,0:T(8,128)(2,1)S(1)}, u32[]{:S(2)}, u32[]{:S(2)}) collective-permute-start(bf16[512,512]{1,0:T(8,128)(2,1)S(1)} %collective-permute-done.9.refs_10_), channel_id=1, source_target_pairs={{0,1},{1,0},{2,3},{3,2},{4,5},{5,4},{6,7},{7,6},{8,9},{9,8},{10,11... | collective-permute-start | bytes 1572872 | tf_op jit(solution)/shard_map/ppermute | solution.py:33
  53.4 14.3 %collective-permute-start.20 = (bf16[512,512]{1,0:T(8,128)(2,1)S(1)}, bf16[512,512]{1,0:T(8,128)(2,1)S(1)}, u32[]{:S(2)}, u32[]{:S(2)}) collective-permute-start(bf16[512,512]{1,0:T(8,128)(2,1)S(1)} %get-tuple-element.76), channel_id=1, source_target_pairs={{0,2},{1,3},{2,0},{3,1},{4,6},{5,7},{6,4},{7,5},{8,10},{9,11},{10,... | collective-permute-start | bytes 1572872 | tf_op jit(solution)/shard_map/ppermute | solution.py:33
  61.5 13.8 %collective-permute-start.22 = (bf16[128,512]{1,0:T(8,128)(2,1)S(1)}, bf16[128,512]{1,0:T(8,128)(2,1)S(1)}, u32[]{:S(2)}, u32[]{:S(2)}) collective-permute-start(bf16[128,512]{1,0:T(8,128)(2,1)S(1)} %get-tuple-element.81), channel_id=1, source_target_pairs={{0,4},{1,5},{2,6},{3,7},{4,8},{5,9},{6,10},{7,11},{8,12},{9,13},{1... | collective-permute-start | bytes 393224 | tf_op jit(solution)/shard_map/ppermute | solution.py:29
  64.8 7.6 %collective-permute-start.19 = (bf16[128,512]{1,0:T(8,128)(2,1)S(1)}, bf16[128,512]{1,0:T(8,128)(2,1)S(1)}, u32[]{:S(2)}, u32[]{:S(2)}) collective-permute-start(bf16[128,512]{1,0:T(8,128)(2,1)S(1)} %get-tuple-element.69), channel_id=1, source_target_pairs={{0,12},{1,13},{2,14},{3,15},{4,0},{5,1},{6,2},{7,3},{8,4},{9,5},{1... | collective-permute-start | bytes 393224 | tf_op jit(solution)/shard_map/ppermute | solution.py:29
  65.7 12.2 %collective-permute-start.21 = (bf16[128,512]{1,0:T(8,128)(2,1)S(1)}, bf16[128,512]{1,0:T(8,128)(2,1)S(1)}, u32[]{:S(2)}, u32[]{:S(2)}) collective-permute-start(bf16[128,512]{1,0:T(8,128)(2,1)S(1)} %get-tuple-element.79), channel_id=1, source_target_pairs={{0,8},{1,9},{2,10},{3,11},{4,12},{5,13},{6,14},{7,15},{8,0},{9,1},... | collective-permute-start | bytes 393224 | tf_op jit(solution)/shard_map/ppermute | solution.py:29
  85.2 24.4 %collective-permute-start.31 = (bf16[2,512,512]{2,1,0:T(8,128)(2,1)S(1)}, bf16[2,512,512]{2,1,0:T(8,128)(2,1)S(1)}, u32[]{:S(2)}, u32[]{:S(2)}) collective-permute-start(bf16[2,512,512]{2,1,0:T(8,128)(2,1)S(1)} %add_convert_fusion.1), channel_id=1, source_target_pairs={{0,2},{1,3},{2,0},{3,1},{4,6},{5,7},{6,4},{7,5},{8,10},{9,11},{10,... | collective-permute-start | bytes 3145736 | tf_op jit(solution)/shard_map/ppermute | solution.py:33
  89.5 21.6 %collective-permute-start.27 = (bf16[2,512,512]{2,1,0:T(8,128)(2,1)S(1)}, bf16[2,512,512]{2,1,0:T(8,128)(2,1)S(1)}, u32[]{:S(2)}, u32[]{:S(2)}) collective-permute-start(bf16[2,512,512]{2,1,0:T(8,128)(2,1)S(1)} %pad_maximum_fusion.downs), channel_id=1, source_target_pairs={{0,1},{1,0},{2,3},{3,2},{4,5},{5,4},{6,7},{7,6},{8,9},{9,8},{10,11... | collective-permute-start | bytes 3145736 | tf_op jit(solution)/shard_map/ppermute | solution.py:33
  89.7 23.6 %collective-permute-start.30 = (bf16[128,512]{1,0:T(8,128)(2,1)S(1)}, bf16[128,512]{1,0:T(8,128)(2,1)S(1)}, u32[]{:S(2)}, u32[]{:S(2)}) collective-permute-start(bf16[128,512]{1,0:T(8,128)(2,1)S(1)} %get-tuple-element.91), channel_id=1, source_target_pairs={{0,12},{1,13},{2,14},{3,15},{4,0},{5,1},{6,2},{7,3},{8,4},{9,5},{1... | collective-permute-start | bytes 393224 | tf_op jit(solution)/shard_map/ppermute | solution.py:29
  92.2 21.0 %collective-permute-start.29 = (bf16[2,128,512]{2,1,0:T(8,128)(2,1)S(1)}, bf16[2,128,512]{2,1,0:T(8,128)(2,1)S(1)}, u32[]{:S(2)}, u32[]{:S(2)}) collective-permute-start(bf16[2,128,512]{2,1,0:T(8,128)(2,1)S(1)} %get-tuple-element.96), channel_id=1, source_target_pairs={{0,4},{1,5},{2,6},{3,7},{4,8},{5,9},{6,10},{7,11},{8,12},{9,13},{1... | collective-permute-start | bytes 786440 | tf_op jit(solution)/shard_map/ppermute | solution.py:29
  92.2 21.0 %collective-permute-start.28 = (bf16[2,128,512]{2,1,0:T(8,128)(2,1)S(1)}, bf16[2,128,512]{2,1,0:T(8,128)(2,1)S(1)}, u32[]{:S(2)}, u32[]{:S(2)}) collective-permute-start(bf16[2,128,512]{2,1,0:T(8,128)(2,1)S(1)} %get-tuple-element.95), channel_id=1, source_target_pairs={{0,8},{1,9},{2,10},{3,11},{4,12},{5,13},{6,14},{7,15},{8,0},{9,1},... | collective-permute-start | bytes 786440 | tf_op jit(solution)/shard_map/ppermute | solution.py:29
  (17 other events, 102.9 us)

commit v11 on v10

--- a/solution.py
+++ b/solution.py
@@ -58,12 +58,10 @@
     return run
 
 
-def columns_body(n_line, block, place, tokens, expert_in, expert_out, *refs):
-    own, other, across, weights, sems = refs
+def columns_body(n_line, block, place, tokens, *refs):
+    own, other, across, sems = refs
     pieces = (own, across.at[0], other, across.at[1])
     copies = []
-    for i, weight in enumerate((expert_in, expert_out)):
-        copies.append(pltpu.make_async_copy(weight, weights.at[pl.ds(i, 1)], sems.at[i]))
     for core in range(2):
         for side in range(2):
             owner = (place[1] ^ side) * 2 + (place[2] ^ core)
@@ -77,6 +75,45 @@
         copy.start()
     for copy in copies:
         copy.wait()
+
+
+def stack_body(place, first, second, out):
+    out[0], out[1] = first[...], second[...]
+
+
+def add_body(place, *refs):
+    total = refs[0][...].astype(wide)
+    for value in refs[1:-1]:
+        total = total + value[...].astype(wide)
+    refs[-1][...] = total.astype(refs[-1].dtype)
+
+
+def half_body(place, keep, arrived, mine, other):
+    mine[...] = keep[0] + arrived[0]
+    other[...] = (keep[1] + arrived[1]).astype(narrow)
+
+
+def far_body(place, far, arrived, out):
+    out[...] = (far[...] + arrived[2:].astype(wide)).astype(narrow)
+
+
+def near_body(place, near, arrived, far, grad_in, grad_out):
+    for i, out in enumerate((grad_in, grad_out)):
+        out[0] = (near[i] + arrived[i].astype(wide) + far[i].astype(wide)).astype(narrow)
+
+
+def last_body(riding, place, *refs):
+    n_line = (len(refs) - 2 + len(riding)) // 2
+    blocks, pieces, grad_down, combined = refs[:n_line], list(refs[n_line:-2]), refs[-2], refs[-1]
+    total = blocks[0][...]
+    out_total = pieces.pop(0)[...]
+    for back in range(1, n_line):
+        block = blocks[back].at[0] if back in riding else blocks[back]
+        piece = blocks[back].at[1] if back in riding else pieces.pop(0)
+        total = total + block[...].astype(wide)
+        out_total = out_total + piece[...].astype(wide)
+    grad_down[...] = total
+    combined[...] = out_total.astype(narrow)
 
 
 def payload_body(place, routes, levels, cotangent, payload):
@@ -226,15 +263,18 @@
     columns = call(
         functools.partial(columns_body, n_line, block),
         [shape((tok_rows, n_line * block), narrow)] * 2
-        + [shape((2, tok_rows, n_line * block), narrow), shape((2, latent_width, hidden_width), narrow)],
+        + [shape((2, tok_rows, n_line * block), narrow)],
         "columns",
-        scratch=[pltpu.SemaphoreType.DMA((4 * n_line + 2,))],
-        outside=3,
-    )(place, tokens, expert_in, expert_out)
+        scratch=[pltpu.SemaphoreType.DMA((4 * n_line,))],
+        outside=1,
+    )(place, tokens)
+    stack = lambda first, second, *earlier: call(
+        stack_body, [shape((2,) + first.shape, narrow)], "stack"
+    )(after(place, *earlier) if earlier else place, first, second)[0]
     (payload,) = call(payload_body, [shape((tok_rows + gate_rows, latent_width), narrow)], "payload")(
         place, routes.T, gate_levels.T, latent_grad
     )
-    own = columns[3]
+    own = stack(expert_in[0], expert_out[0], downs[1])
     core_own = swap(own, n_line, 1, 0)
     across = swap(columns[2], n_line, 0, 1)
     core_tokens = [swap(after(columns[1], across, core_own), n_line, 1, 0), swap(across[1], n_line, 1, 0)]
@@ -246,10 +286,14 @@
         "project",
     )
     keep, send, down = project(after(place, payload), columns[0], across, *core_tokens, *downs)
-    half = keep + swap(send, n_line, 1, 0)
+    half, cross = call(half_body, [rows_of(wide), rows_of(narrow)], "half")(
+        place, keep, swap(send, n_line, 1, 0)
+    )
     payloads = [payload] + [turn(after(payload, *downs[1:]), n_line, back) for back in range(1, n_line)]
-    crossed = swap(half[1].astype(narrow), n_line, 0, 1).astype(wide)
-    latent = (half[0] + after(crossed, side_in, *payloads[1:])).astype(narrow)
+    crossed = swap(cross, n_line, 0, 1)
+    (latent,) = call(add_body, [rows_of(narrow)], "latent")(
+        place, half, after(crossed, side_in, *payloads[1:])
+    )
     groups = [[*range(1, n_line), 0]]
     riding = range(2, n_line)
     rows = [latent] + [turn(latent, n_line, back) for back in range(1, n_line)]
@@ -260,7 +304,7 @@
     weights = [own, core_own, side_in, side_out, core_in, core_out]
     side_down = swap(after(down, *rows[1:]), n_line, 0, 1)
 
-    both_down = jnp.stack([down, side_down])
+    both_down = stack(down, side_down)
     deltas_of, outs_of, saved = [None] * n_line, [None] * n_line, []
     done = latent
     for group in groups:
@@ -291,14 +335,14 @@
         *(value for values in saved for value in values),
     )
     delta_lines = [after(line, near, both_down) for line in delta_lines]
-    delta = sum(line.astype(wide) for line in delta_lines).astype(narrow)
+    (delta,) = call(add_body, [rows_of(narrow)], "latent_delta")(place, *delta_lines)
     side_delta = swap(delta, n_line, 0, 1)
     out_lines = [outs_of[0]] + [home(outs_of[back], back) if back not in riding else None for back in range(1, n_line)]
     other = swap(after(other, delta), n_line, 1, 0)
-    far = (far + after(other, out_lines[1])[2:].astype(wide)).astype(narrow)
+    (far,) = call(far_body, [shape(pair, narrow)], "far_grads")(place, far, after(other, out_lines[1]))
     sent = far
     far = swap(after(far, side_delta), n_line, 0, 1)
-    core_deltas = swap(jnp.stack([delta, after(side_delta, sent)]), n_line, 1, 0)
+    core_deltas = swap(stack(delta, side_delta, sent), n_line, 1, 0)
     blocks = call(
         functools.partial(down_grad_body, n_line),
         [
@@ -312,12 +356,13 @@
         functools.partial(token_grad_body, n_line, block), [shape((tok_rows, width), narrow)], "token_grad"
     )(place, after(delta, blocks[1]), both_down, core_down)
     blocks = [blocks[0]] + [turn(blocks[back], n_line, n_line - back) for back in range(1, n_line)]
-    grad_down = sum((value[0] if back in riding else value).astype(wide) for back, value in enumerate(blocks))
-    out_lines = [blocks[back][1] if back in riding else line for back, line in enumerate(out_lines)]
-    out_lines[0] = after(out_lines[0], grad_tokens)
-    latent_out = sum(line.astype(wide) for line in out_lines).astype(narrow)
-    weight_grad = (near + other[:2].astype(wide) + far.astype(wide)).astype(narrow)
-    return (latent_out, grad_tokens, grad_down, weight_grad[:1], weight_grad[1:])
+    grad_down, latent_out = call(
+        functools.partial(last_body, riding), [shape((block, latent_width), wide), rows_of(narrow)], "last_sums"
+    )(after(place, grad_tokens), *blocks, *(line for line in out_lines if line is not None))
+    grad_in, grad_out = call(
+        near_body, [shape(expert_in.shape, narrow), shape(expert_out.shape, narrow)], "near_grads"
+    )(after(place, grad_down), near, other, far)
+    return (latent_out, grad_tokens, grad_down, grad_in, grad_out)
 
 
 def slot_table(routes, capacity):

time: 114 us -> 120 us (1.053)
  Pallas kernels: 15 us -> 22.2 us
  waiting for transfers between devices: 52 us -> 56.6 us
  local copies, waits for them, and re-layouts: 6.56 us -> 2.53 us
  other arithmetic: 2.05 us -> 0 us
    ppermute x16, waiting for transfers between devices: 20.5 us -> 46.2 us  [turn(): lax.ppermute(value, plane, device_pairs(n_line, lambda z, x, c: ((z + by)...]
    ppermute x16, waiting for transfers between devices: 31.6 us -> 10.4 us  [swap(): lax.ppermute(value, plane, device_pairs(n_line, lambda z, x, c: (z, x ^ s...]
    pallas_call x7 -> x16, Pallas kernels: 15 us -> 22.2 us  [run(): pl.pallas_call(body, out_shape=outs, in_specs=[pl.BlockSpec(memory_space=...]
    unnamed x18, local copies, waits for them, and re-layouts: 5.42 us -> 2.43 us
  transfers between devices with their start and end apart: 32 -> 32, of which waited for: 13 -> 18; matrix products, arithmetic and copies ran while one was open for 2% -> 0% of each run, Pallas kernels for 11% -> 13%
where the time goes in v11:
time: 120 us
  waiting for transfers between devices  56.6 us (47%)
  starting transfers between devices  37.3 us (31%)
  Pallas kernels  22.2 us (18%)
  local copies, waits for them, and re-layouts  2.53 us (2%)
    ppermute x16, waiting for transfers between devices, turn(): lax.ppermute(value, plane, device_pairs(n_line, lambda z, x, c: ((z + by)...  46.2 us
    ppermute x16, starting transfers between devices, turn(): lax.ppermute(value, plane, device_pairs(n_line, lambda z, x, c: ((z + by)...  25.6 us
    pallas_call x16, Pallas kernels, run(): pl.pallas_call(body, out_shape=outs, in_specs=[pl.BlockSpec(memory_space=...  22.2 us
    ppermute x16, starting transfers between devices, swap(): lax.ppermute(value, plane, device_pairs(n_line, lambda z, x, c: (z, x ^ s...  11.7 us
    ppermute x16, waiting for transfers between devices, swap(): lax.ppermute(value, plane, device_pairs(n_line, lambda z, x, c: (z, x ^ s...  10.4 us
    unnamed x18, local copies, waits for them, and re-layouts  2.43 us
  transfers between devices with their start and end apart: 32, of which 18 were waited for; matrix products, arithmetic and copies ran while one was open for 0% of the time, Pallas kernels for 13%

profile of v11, /device:TPU:0, one launch (start us, length us, event | category | flops | bytes accessed | tf_op | source)
XLA Modules:
  0.0 119.5 jit_solution(6241985319142433445)
XLA Ops:
  0.7 3.1 %collective-permute-start.1 = (bf16[128,512]{1,0:T(8,128)(2,1)}, bf16[128,512]{1,0:T(8,128)(2,1)S(1)}, u32[]{:S(2)}, u32[]{:S(2)}) collective-permute-start(bf16[128,512]{1,0:T(8,128)(2,1)} %refs_4_.1), channel_id=1, source_target_pairs={{0,4},{1,5},{2,6},{3,7},{4,8},{5,9},{6,10},{7,11},{8,12},{9,13},{1... | collective-permute-start | bytes 393224 | tf_op jit(solution)/shard_map/ppermute | solution.py:29
  3.8 5.6 %collective-permute-done.1.refs_5_ = bf16[128,512]{1,0:T(8,128)(2,1)S(1)} collective-permute-done((bf16[128,512]{1,0:T(8,128)(2,1)}, bf16[128,512]{1,0:T(8,128)(2,1)S(1)}, u32[]{:S(2)}, u32[]{:S(2)}) %collective-permute-start.1) | collective-permute-done | bytes 131104 | tf_op jit(solution)/shard_map/ppermute | solution.py:29
  17.1 4.8 %collective-permute-done.refs_1_ = bf16[2,128,512]{2,1,0:T(8,128)(2,1)S(1)} collective-permute-done((bf16[2,128,512]{2,1,0:T(8,128)(2,1)S(1)}, bf16[2,128,512]{2,1,0:T(8,128)(2,1)S(1)}, u32[]{:S(2)}, u32[]{:S(2)}) %collective-permute-start) | collective-permute-done | bytes 262176 | tf_op jit(solution)/shard_map/ppermute | solution.py:33
  26.5 1.9 %collective-permute-start.10 = (bf16[144,512]{1,0:T(8,128)(2,1)S(1)}, bf16[144,512]{1,0:T(8,128)(2,1)S(1)}, u32[]{:S(2)}, u32[]{:S(2)}) collective-permute-start(bf16[144,512]{1,0:T(8,128)(2,1)S(1)} %payload.1.refs_7_), channel_id=1, source_target_pairs={{0,4},{1,5},{2,6},{3,7},{4,8},{5,9},{6,10},{7,11},{8,12},{9,13},{1... | collective-permute-start | bytes 442376 | tf_op jit(solution)/shard_map/ppermute | solution.py:29
  28.3 2.4 %collective-permute-start.11 = (bf16[144,512]{1,0:T(8,128)(2,1)S(1)}, bf16[144,512]{1,0:T(8,128)(2,1)S(1)}, u32[]{:S(2)}, u32[]{:S(2)}) collective-permute-start(bf16[144,512]{1,0:T(8,128)(2,1)S(1)} %payload.1.refs_7_), channel_id=1, source_target_pairs={{0,8},{1,9},{2,10},{3,11},{4,12},{5,13},{6,14},{7,15},{8,0},{9,1},... | collective-permute-start | bytes 442376 | tf_op jit(solution)/shard_map/ppermute | solution.py:29
  31.4 1.6 %collective-permute-start.8 = (bf16[128,512]{1,0:T(8,128)(2,1)S(1)}, bf16[128,512]{1,0:T(8,128)(2,1)S(1)}, u32[]{:S(2)}, u32[]{:S(2)}) collective-permute-start(bf16[128,512]{1,0:T(8,128)(2,1)S(1)} %get-tuple-element.68), channel_id=1, source_target_pairs={{0,2},{1,3},{2,0},{3,1},{4,6},{5,7},{6,4},{7,5},{8,10},{9,11},{10,... | collective-permute-start | bytes 393224 | tf_op jit(solution)/shard_map/ppermute | solution.py:33
  32.9 2.1 %collective-permute-done.10.refs_4_ = bf16[144,512]{1,0:T(8,128)(2,1)S(1)} collective-permute-done((bf16[144,512]{1,0:T(8,128)(2,1)S(1)}, bf16[144,512]{1,0:T(8,128)(2,1)S(1)}, u32[]{:S(2)}, u32[]{:S(2)}) %collective-permute-start.10) | collective-permute-done | bytes 147488 | tf_op jit(solution)/shard_map/ppermute | solution.py:29
  35.0 5.8 %collective-permute-done.11.refs_5_ = bf16[144,512]{1,0:T(8,128)(2,1)S(1)} collective-permute-done((bf16[144,512]{1,0:T(8,128)(2,1)S(1)}, bf16[144,512]{1,0:T(8,128)(2,1)S(1)}, u32[]{:S(2)}, u32[]{:S(2)}) %collective-permute-start.11) | collective-permute-done | bytes 147488 | tf_op jit(solution)/shard_map/ppermute | solution.py:29
  43.9 2.6 %collective-permute-start.13 = (bf16[128,512]{1,0:T(8,128)(2,1)S(1)}, bf16[128,512]{1,0:T(8,128)(2,1)S(1)}, u32[]{:S(2)}, u32[]{:S(2)}) collective-permute-start(bf16[128,512]{1,0:T(8,128)(2,1)S(1)} %latent.1.refs_3_), channel_id=1, source_target_pairs={{0,4},{1,5},{2,6},{3,7},{4,8},{5,9},{6,10},{7,11},{8,12},{9,13},{1... | collective-permute-start | bytes 393224 | tf_op jit(solution)/shard_map/ppermute | solution.py:29
  46.6 1.9 %collective-permute-start.14 = (bf16[128,512]{1,0:T(8,128)(2,1)S(1)}, bf16[128,512]{1,0:T(8,128)(2,1)S(1)}, u32[]{:S(2)}, u32[]{:S(2)}) collective-permute-start(bf16[128,512]{1,0:T(8,128)(2,1)S(1)} %latent.1.refs_3_), channel_id=1, source_target_pairs={{0,8},{1,9},{2,10},{3,11},{4,12},{5,13},{6,14},{7,15},{8,0},{9,1},... | collective-permute-start | bytes 393224 | tf_op jit(solution)/shard_map/ppermute | solution.py:29
  48.9 3.5 %collective-permute-done.13.refs_0_ = bf16[128,512]{1,0:T(8,128)(2,1)S(1)} collective-permute-done((bf16[128,512]{1,0:T(8,128)(2,1)S(1)}, bf16[128,512]{1,0:T(8,128)(2,1)S(1)}, u32[]{:S(2)}, u32[]{:S(2)}) %collective-permute-start.13) | collective-permute-done | bytes 131104 | tf_op jit(solution)/shard_map/ppermute | solution.py:29
  52.4 4.3 %collective-permute-done.14.refs_1_ = bf16[128,512]{1,0:T(8,128)(2,1)S(1)} collective-permute-done((bf16[128,512]{1,0:T(8,128)(2,1)S(1)}, bf16[128,512]{1,0:T(8,128)(2,1)S(1)}, u32[]{:S(2)}, u32[]{:S(2)}) %collective-permute-start.14) | collective-permute-done | bytes 131104 | tf_op jit(solution)/shard_map/ppermute | solution.py:29
  56.7 1.6 %collective-permute-start.20 = (bf16[512,512]{1,0:T(8,128)(2,1)S(1)}, bf16[512,512]{1,0:T(8,128)(2,1)S(1)}, u32[]{:S(2)}, u32[]{:S(2)}) collective-permute-start(bf16[512,512]{1,0:T(8,128)(2,1)S(1)} %get-tuple-element.84.first), channel_id=1, source_target_pairs={{0,2},{1,3},{2,0},{3,1},{4,6},{5,7},{6,4},{7,5},{8,10},{9,11},{10,... | collective-permute-start | bytes 1572872 | tf_op jit(solution)/shard_map/ppermute | solution.py:33
  58.6 6.1 %experts.1 = (bf16[128,512]{1,0:T(8,128)(2,1)S(1)}, bf16[128,512]{1,0:T(8,128)(2,1)S(1)}, bf16[128,512]{1,0:T(8,128)(2,1)S(1)}, bf16[128,512]{1,0:T(8,128)(2,1)S...) custom-call(s32[7]{0:T(128)S(1)} %stack.34.place, ...), custom_call_target="tpu_custom_call" | custom-call | tf_op jit(solution)/shard_map/experts/pallas_call | solution.py:45
  64.8 4.2 %collective-permute-start.19 = (bf16[128,512]{1,0:T(8,128)(2,1)S(1)}, bf16[128,512]{1,0:T(8,128)(2,1)S(1)}, u32[]{:S(2)}, u32[]{:S(2)}) collective-permute-start(bf16[128,512]{1,0:T(8,128)(2,1)S(1)} %get-tuple-element.77), channel_id=1, source_target_pairs={{0,12},{1,13},{2,14},{3,15},{4,0},{5,1},{6,2},{7,3},{8,4},{9,5},{1... | collective-permute-start | bytes 393224 | tf_op jit(solution)/shard_map/ppermute | solution.py:29
  72.9 2.9 %weight_grads.1 = (f32[2,512,512]{2,1,0:T(8,128)S(1)}, f32[2,512,512]{2,1,0:T(8,128)S(1)}, bf16[4,512,512]{2,1,0:T(8,128)(2,1)S(1)}) custom-call(s32[7]{0:T(128)S(1)} %stack.34.place, bf16[128,512]{1,0:T(8,128)(2,1)S(1)} %collective-permute-done.13.refs_0_, bf16[128,512]{1,0:T(8,128)(2,1)S(1)} %collective-permute-done.14.refs_1_, ...), custom_call_target="tpu_custom_call" | custom-call | tf_op jit(solution)/shard_map/weight_grads/pallas_call | solution.py:45
  75.8 5.6 %collective-permute-done.21.refs_2_ = bf16[128,512]{1,0:T(8,128)(2,1)S(1)} collective-permute-done((bf16[128,512]{1,0:T(8,128)(2,1)S(1)}, bf16[128,512]{1,0:T(8,128)(2,1)S(1)}, u32[]{:S(2)}, u32[]{:S(2)}) %collective-permute-start.21) | collective-permute-done | bytes 131104 | tf_op jit(solution)/shard_map/ppermute | solution.py:29
  83.8 4.2 %collective-permute-done.25.refs_5_ = bf16[128,512]{1,0:T(8,128)(2,1)S(1)} collective-permute-done((bf16[128,512]{1,0:T(8,128)(2,1)S(1)}, bf16[128,512]{1,0:T(8,128)(2,1)S(1)}, u32[]{:S(2)}, u32[]{:S(2)}) %collective-permute-start.25) | collective-permute-done | bytes 131104 | tf_op jit(solution)/shard_map/ppermute | solution.py:29
  93.9 2.0 %collective-permute-start.29 = (bf16[2,128,512]{2,1,0:T(8,128)(2,1)S(1)}, bf16[2,128,512]{2,1,0:T(8,128)(2,1)S(1)}, u32[]{:S(2)}, u32[]{:S(2)}) collective-permute-start(bf16[2,128,512]{2,1,0:T(8,128)(2,1)S(1)} %get-tuple-element.104), channel_id=1, source_target_pairs={{0,8},{1,9},{2,10},{3,11},{4,12},{5,13},{6,14},{7,15},{8,0},{9,1},... | collective-permute-start | bytes 786440 | tf_op jit(solution)/shard_map/ppermute | solution.py:29
  96.5 3.1 %collective-permute-start.28 = (bf16[128,512]{1,0:T(8,128)(2,1)S(1)}, bf16[128,512]{1,0:T(8,128)(2,1)S(1)}, u32[]{:S(2)}, u32[]{:S(2)}) collective-permute-start(bf16[128,512]{1,0:T(8,128)(2,1)S(1)} %get-tuple-element.99), channel_id=1, source_target_pairs={{0,12},{1,13},{2,14},{3,15},{4,0},{5,1},{6,2},{7,3},{8,4},{9,5},{1... | collective-permute-start | bytes 393224 | tf_op jit(solution)/shard_map/ppermute | solution.py:29
  99.7 2.2 %token_grad.1 = bf16[128,2048]{1,0:T(8,128)(2,1)} custom-call(s32[7]{0:T(128)S(1)} %stack.34.place, bf16[128,512]{1,0:T(8,128)(2,1)S(1)} %latent_delta.1.first.refs_4_.delta, bf16[2,512,512]{2,1,0:T(8,128)(2,1)S(1)} %stack.36.downs, bf16[2,512,512]{2,1,0:T(8,128)(2,1)S(1)} %collective-permute-done.27.core_downs), custom_call_target="tpu_custom_call" | custom-call | tf_op jit(solution)/shard_map/token_grad/pallas_call | solution.py:45
  101.9 8.3 %collective-permute-done.28.refs_1_ = bf16[128,512]{1,0:T(8,128)(2,1)S(1)} collective-permute-done((bf16[128,512]{1,0:T(8,128)(2,1)S(1)}, bf16[128,512]{1,0:T(8,128)(2,1)S(1)}, u32[]{:S(2)}, u32[]{:S(2)}) %collective-permute-start.28) | collective-permute-done | bytes 131104 | tf_op jit(solution)/shard_map/ppermute | solution.py:29
  110.2 5.0 %collective-permute-done.29.refs_2_ = bf16[2,128,512]{2,1,0:T(8,128)(2,1)S(1)} collective-permute-done((bf16[2,128,512]{2,1,0:T(8,128)(2,1)S(1)}, bf16[2,128,512]{2,1,0:T(8,128)(2,1)S(1)}, u32[]{:S(2)}, u32[]{:S(2)}) %collective-permute-start.29) | collective-permute-done | bytes 262176 | tf_op jit(solution)/shard_map/ppermute | solution.py:29
  117.8 1.7 %near_grads.1 = (bf16[1,512,512]{2,1,0:T(8,128)(2,1)}, bf16[1,512,512]{2,1,0:T(8,128)(2,1)}) custom-call(s32[7]{0:T(128)S(1)} %stack.34.place, f32[2,512,512]{2,1,0:T(8,128)S(1)} %get-tuple-element.82.near, bf16[4,512,512]{2,1,0:T(8,128)(2,1)S(1)} %collective-permute-done.24.arrived, bf16[2,512,512]{2,1,0:T(8,128)(2,1)S(1)} %collective-permute-done.31.far), custom_call_target="tpu_custom_call" | custom-call | tf_op jit(solution)/shard_map/near_grads/pallas_call | solution.py:45
  (76 shorter events, 32.1 us)
Async XLA Ops:
  0.7 8.8 %collective-permute-start.1 = (bf16[128,512]{1,0:T(8,128)(2,1)}, bf16[128,512]{1,0:T(8,128)(2,1)S(1)}, u32[]{:S(2)}, u32[]{:S(2)}) collective-permute-start(bf16[128,512]{1,0:T(8,128)(2,1)} %refs_4_.1), channel_id=1, source_target_pairs={{0,4},{1,5},{2,6},{3,7},{4,8},{5,9},{6,10},{7,11},{8,12},{9,13},{1... | collective-permute-start | bytes 393224 | tf_op jit(solution)/shard_map/ppermute | solution.py:29
  12.2 9.8 %collective-permute-start.2 = (bf16[2,512,512]{2,1,0:T(8,128)(2,1)S(1)}, bf16[2,512,512]{2,1,0:T(8,128)(2,1)S(1)}, u32[]{:S(2)}, u32[]{:S(2)}) collective-permute-start(bf16[2,512,512]{2,1,0:T(8,128)(2,1)S(1)} %stack.35.refs_8_), channel_id=1, source_target_pairs={{0,1},{1,0},{2,3},{3,2},{4,5},{5,4},{6,7},{7,6},{8,9},{9,8},{10,11... | collective-permute-start | bytes 3145736 | tf_op jit(solution)/shard_map/ppermute | solution.py:33
  13.5 8.5 %collective-permute-start = (bf16[2,128,512]{2,1,0:T(8,128)(2,1)S(1)}, bf16[2,128,512]{2,1,0:T(8,128)(2,1)S(1)}, u32[]{:S(2)}, u32[]{:S(2)}) collective-permute-start(bf16[2,128,512]{2,1,0:T(8,128)(2,1)S(1)} %get-tuple-element.61), channel_id=1, source_target_pairs={{0,2},{1,3},{2,0},{3,1},{4,6},{5,7},{6,4},{7,5},{8,10},{9,11},{10,... | collective-permute-start | bytes 786440 | tf_op jit(solution)/shard_map/ppermute | solution.py:33
  15.0 8.3 %collective-permute-start.5 = (bf16[128,512]{1,0:T(8,128)(2,1)S(1)}, bf16[128,512]{1,0:T(8,128)(2,1)S(1)}, u32[]{:S(2)}, u32[]{:S(2)}) collective-permute-start(bf16[128,512]{1,0:T(8,128)(2,1)S(1)} %copy-done.5), channel_id=1, source_target_pairs={{0,8},{1,9},{2,10},{3,11},{4,12},{5,13},{6,14},{7,15},{8,0},{9,1},... | collective-permute-start | bytes 393224 | tf_op jit(solution)/shard_map/ppermute | solution.py:29
  15.8 7.8 %collective-permute-start.6 = (bf16[128,512]{1,0:T(8,128)(2,1)S(1)}, bf16[128,512]{1,0:T(8,128)(2,1)S(1)}, u32[]{:S(2)}, u32[]{:S(2)}) collective-permute-start(bf16[128,512]{1,0:T(8,128)(2,1)S(1)} %copy-done.5), channel_id=1, source_target_pairs={{0,12},{1,13},{2,14},{3,15},{4,0},{5,1},{6,2},{7,3},{8,4},{9,5},{1... | collective-permute-start | bytes 393224 | tf_op jit(solution)/shard_map/ppermute | solution.py:29
  25.0 15.8 %collective-permute-start.9 = (bf16[512,512]{1,0:T(8,128)(2,1)S(1)}, bf16[512,512]{1,0:T(8,128)(2,1)S(1)}, u32[]{:S(2)}, u32[]{:S(2)}) collective-permute-start(bf16[512,512]{1,0:T(8,128)(2,1)S(1)} %bitcast.14), channel_id=1, source_target_pairs={{0,2},{1,3},{2,0},{3,1},{4,6},{5,7},{6,4},{7,5},{8,10},{9,11},{10,... | collective-permute-start | bytes 1572872 | tf_op jit(solution)/shard_map/ppermute | solution.py:33
  26.5 8.6 %collective-permute-start.10 = (bf16[144,512]{1,0:T(8,128)(2,1)S(1)}, bf16[144,512]{1,0:T(8,128)(2,1)S(1)}, u32[]{:S(2)}, u32[]{:S(2)}) collective-permute-start(bf16[144,512]{1,0:T(8,128)(2,1)S(1)} %payload.1.refs_7_), channel_id=1, source_target_pairs={{0,4},{1,5},{2,6},{3,7},{4,8},{5,9},{6,10},{7,11},{8,12},{9,13},{1... | collective-permute-start | bytes 442376 | tf_op jit(solution)/shard_map/ppermute | solution.py:29
  28.3 12.5 %collective-permute-start.11 = (bf16[144,512]{1,0:T(8,128)(2,1)S(1)}, bf16[144,512]{1,0:T(8,128)(2,1)S(1)}, u32[]{:S(2)}, u32[]{:S(2)}) collective-permute-start(bf16[144,512]{1,0:T(8,128)(2,1)S(1)} %payload.1.refs_7_), channel_id=1, source_target_pairs={{0,8},{1,9},{2,10},{3,11},{4,12},{5,13},{6,14},{7,15},{8,0},{9,1},... | collective-permute-start | bytes 442376 | tf_op jit(solution)/shard_map/ppermute | solution.py:29
  30.8 10.0 %collective-permute-start.12 = (bf16[144,512]{1,0:T(8,128)(2,1)S(1)}, bf16[144,512]{1,0:T(8,128)(2,1)S(1)}, u32[]{:S(2)}, u32[]{:S(2)}) collective-permute-start(bf16[144,512]{1,0:T(8,128)(2,1)S(1)} %payload.1.refs_7_), channel_id=1, source_target_pairs={{0,12},{1,13},{2,14},{3,15},{4,0},{5,1},{6,2},{7,3},{8,4},{9,5},{1... | collective-permute-start | bytes 442376 | tf_op jit(solution)/shard_map/ppermute | solution.py:29
  31.4 10.5 %collective-permute-start.8 = (bf16[128,512]{1,0:T(8,128)(2,1)S(1)}, bf16[128,512]{1,0:T(8,128)(2,1)S(1)}, u32[]{:S(2)}, u32[]{:S(2)}) collective-permute-start(bf16[128,512]{1,0:T(8,128)(2,1)S(1)} %get-tuple-element.68), channel_id=1, source_target_pairs={{0,2},{1,3},{2,0},{3,1},{4,6},{5,7},{6,4},{7,5},{8,10},{9,11},{10,... | collective-permute-start | bytes 393224 | tf_op jit(solution)/shard_map/ppermute | solution.py:33
  42.4 14.3 %collective-permute-start.16 = (bf16[512,512]{1,0:T(8,128)(2,1)S(1)}, bf16[512,512]{1,0:T(8,128)(2,1)S(1)}, u32[]{:S(2)}, u32[]{:S(2)}) collective-permute-start(bf16[512,512]{1,0:T(8,128)(2,1)S(1)} %bitcast.16), channel_id=1, source_target_pairs={{0,2},{1,3},{2,0},{3,1},{4,6},{5,7},{6,4},{7,5},{8,10},{9,11},{10,... | collective-permute-start | bytes 1572872 | tf_op jit(solution)/shard_map/ppermute | solution.py:33
  43.9 8.5 %collective-permute-start.13 = (bf16[128,512]{1,0:T(8,128)(2,1)S(1)}, bf16[128,512]{1,0:T(8,128)(2,1)S(1)}, u32[]{:S(2)}, u32[]{:S(2)}) collective-permute-start(bf16[128,512]{1,0:T(8,128)(2,1)S(1)} %latent.1.refs_3_), channel_id=1, source_target_pairs={{0,4},{1,5},{2,6},{3,7},{4,8},{5,9},{6,10},{7,11},{8,12},{9,13},{1... | collective-permute-start | bytes 393224 | tf_op jit(solution)/shard_map/ppermute | solution.py:29
  46.6 10.1 %collective-permute-start.14 = (bf16[128,512]{1,0:T(8,128)(2,1)S(1)}, bf16[128,512]{1,0:T(8,128)(2,1)S(1)}, u32[]{:S(2)}, u32[]{:S(2)}) collective-permute-start(bf16[128,512]{1,0:T(8,128)(2,1)S(1)} %latent.1.refs_3_), channel_id=1, source_target_pairs={{0,8},{1,9},{2,10},{3,11},{4,12},{5,13},{6,14},{7,15},{8,0},{9,1},... | collective-permute-start | bytes 393224 | tf_op jit(solution)/shard_map/ppermute | solution.py:29
  48.5 8.2 %collective-permute-start.15 = (bf16[128,512]{1,0:T(8,128)(2,1)S(1)}, bf16[128,512]{1,0:T(8,128)(2,1)S(1)}, u32[]{:S(2)}, u32[]{:S(2)}) collective-permute-start(bf16[128,512]{1,0:T(8,128)(2,1)S(1)} %latent.1.refs_3_), channel_id=1, source_target_pairs={{0,12},{1,13},{2,14},{3,15},{4,0},{5,1},{6,2},{7,3},{8,4},{9,5},{1... | collective-permute-start | bytes 393224 | tf_op jit(solution)/shard_map/ppermute | solution.py:29
  48.9 9.4 %collective-permute-start.17 = (bf16[512,512]{1,0:T(8,128)(2,1)S(1)}, bf16[512,512]{1,0:T(8,128)(2,1)S(1)}, u32[]{:S(2)}, u32[]{:S(2)}) collective-permute-start(bf16[512,512]{1,0:T(8,128)(2,1)S(1)} %collective-permute-done.9.refs_10_), channel_id=1, source_target_pairs={{0,1},{1,0},{2,3},{3,2},{4,5},{5,4},{6,7},{7,6},{8,9},{9,8},{10,11... | collective-permute-start | bytes 1572872 | tf_op jit(solution)/shard_map/ppermute | solution.py:33
  56.7 14.3 %collective-permute-start.20 = (bf16[512,512]{1,0:T(8,128)(2,1)S(1)}, bf16[512,512]{1,0:T(8,128)(2,1)S(1)}, u32[]{:S(2)}, u32[]{:S(2)}) collective-permute-start(bf16[512,512]{1,0:T(8,128)(2,1)S(1)} %get-tuple-element.84.first), channel_id=1, source_target_pairs={{0,2},{1,3},{2,0},{3,1},{4,6},{5,7},{6,4},{7,5},{8,10},{9,11},{10,... | collective-permute-start | bytes 1572872 | tf_op jit(solution)/shard_map/ppermute | solution.py:33
  64.8 8.2 %collective-permute-start.19 = (bf16[128,512]{1,0:T(8,128)(2,1)S(1)}, bf16[128,512]{1,0:T(8,128)(2,1)S(1)}, u32[]{:S(2)}, u32[]{:S(2)}) collective-permute-start(bf16[128,512]{1,0:T(8,128)(2,1)S(1)} %get-tuple-element.77), channel_id=1, source_target_pairs={{0,12},{1,13},{2,14},{3,15},{4,0},{5,1},{6,2},{7,3},{8,4},{9,5},{1... | collective-permute-start | bytes 393224 | tf_op jit(solution)/shard_map/ppermute | solution.py:29
  69.0 12.5 %collective-permute-start.21 = (bf16[128,512]{1,0:T(8,128)(2,1)S(1)}, bf16[128,512]{1,0:T(8,128)(2,1)S(1)}, u32[]{:S(2)}, u32[]{:S(2)}) collective-permute-start(bf16[128,512]{1,0:T(8,128)(2,1)S(1)} %get-tuple-element.87), channel_id=1, source_target_pairs={{0,8},{1,9},{2,10},{3,11},{4,12},{5,13},{6,14},{7,15},{8,0},{9,1},... | collective-permute-start | bytes 393224 | tf_op jit(solution)/shard_map/ppermute | solution.py:29
  69.5 11.9 %collective-permute-start.22 = (bf16[128,512]{1,0:T(8,128)(2,1)S(1)}, bf16[128,512]{1,0:T(8,128)(2,1)S(1)}, u32[]{:S(2)}, u32[]{:S(2)}) collective-permute-start(bf16[128,512]{1,0:T(8,128)(2,1)S(1)} %get-tuple-element.89), channel_id=1, source_target_pairs={{0,4},{1,5},{2,6},{3,7},{4,8},{5,9},{6,10},{7,11},{8,12},{9,13},{1... | collective-permute-start | bytes 393224 | tf_op jit(solution)/shard_map/ppermute | solution.py:29
  92.1 7.5 %collective-permute-start.27 = (bf16[2,512,512]{2,1,0:T(8,128)(2,1)S(1)}, bf16[2,512,512]{2,1,0:T(8,128)(2,1)S(1)}, u32[]{:S(2)}, u32[]{:S(2)}) collective-permute-start(bf16[2,512,512]{2,1,0:T(8,128)(2,1)S(1)} %stack.36.downs), channel_id=1, source_target_pairs={{0,1},{1,0},{2,3},{3,2},{4,5},{5,4},{6,7},{7,6},{8,9},{9,8},{10,11... | collective-permute-start | bytes 3145736 | tf_op jit(solution)/shard_map/ppermute | solution.py:33
  92.3 25.4 %collective-permute-start.31 = (bf16[2,512,512]{2,1,0:T(8,128)(2,1)S(1)}, bf16[2,512,512]{2,1,0:T(8,128)(2,1)S(1)}, u32[]{:S(2)}, u32[]{:S(2)}) collective-permute-start(bf16[2,512,512]{2,1,0:T(8,128)(2,1)S(1)} %far_grads.1), channel_id=1, source_target_pairs={{0,2},{1,3},{2,0},{3,1},{4,6},{5,7},{6,4},{7,5},{8,10},{9,11},{10,... | collective-permute-start | bytes 3145736 | tf_op jit(solution)/shard_map/ppermute | solution.py:33
  93.9 21.3 %collective-permute-start.29 = (bf16[2,128,512]{2,1,0:T(8,128)(2,1)S(1)}, bf16[2,128,512]{2,1,0:T(8,128)(2,1)S(1)}, u32[]{:S(2)}, u32[]{:S(2)}) collective-permute-start(bf16[2,128,512]{2,1,0:T(8,128)(2,1)S(1)} %get-tuple-element.104), channel_id=1, source_target_pairs={{0,8},{1,9},{2,10},{3,11},{4,12},{5,13},{6,14},{7,15},{8,0},{9,1},... | collective-permute-start | bytes 786440 | tf_op jit(solution)/shard_map/ppermute | solution.py:29
  95.9 19.3 %collective-permute-start.30 = (bf16[2,128,512]{2,1,0:T(8,128)(2,1)S(1)}, bf16[2,128,512]{2,1,0:T(8,128)(2,1)S(1)}, u32[]{:S(2)}, u32[]{:S(2)}) collective-permute-start(bf16[2,128,512]{2,1,0:T(8,128)(2,1)S(1)} %get-tuple-element.105), channel_id=1, source_target_pairs={{0,4},{1,5},{2,6},{3,7},{4,8},{5,9},{6,10},{7,11},{8,12},{9,13},{1... | collective-permute-start | bytes 786440 | tf_op jit(solution)/shard_map/ppermute | solution.py:29
  96.5 13.6 %collective-permute-start.28 = (bf16[128,512]{1,0:T(8,128)(2,1)S(1)}, bf16[128,512]{1,0:T(8,128)(2,1)S(1)}, u32[]{:S(2)}, u32[]{:S(2)}) collective-permute-start(bf16[128,512]{1,0:T(8,128)(2,1)S(1)} %get-tuple-element.99), channel_id=1, source_target_pairs={{0,12},{1,13},{2,14},{3,15},{4,0},{5,1},{6,2},{7,3},{8,4},{9,5},{1... | collective-permute-start | bytes 393224 | tf_op jit(solution)/shard_map/ppermute | solution.py:29
  (17 other events, 135.9 us)

commit v12 on v11

--- a/solution.py
+++ b/solution.py
@@ -58,10 +58,12 @@
     return run
 
 
-def columns_body(n_line, block, place, tokens, *refs):
-    own, other, across, sems = refs
+def columns_body(n_line, block, place, tokens, expert_in, expert_out, *refs):
+    own, other, across, weights, sems = refs
     pieces = (own, across.at[0], other, across.at[1])
     copies = []
+    for i, weight in enumerate((expert_in, expert_out)):
+        copies.append(pltpu.make_async_copy(weight, weights.at[pl.ds(i, 1)], sems.at[i]))
     for core in range(2):
         for side in range(2):
             owner = (place[1] ^ side) * 2 + (place[2] ^ core)
@@ -93,13 +95,14 @@
     other[...] = (keep[1] + arrived[1]).astype(narrow)
 
 
-def far_body(place, far, arrived, out):
-    out[...] = (far[...] + arrived[2:].astype(wide)).astype(narrow)
-
-
-def near_body(place, near, arrived, far, grad_in, grad_out):
+def core_sum_body(place, near, far, arrived, near_out, far_out):
+    far_out[...] = (far[...] + arrived[2:].astype(wide)).astype(narrow)
+    near_out[...] = near[...] + arrived[:2].astype(wide)
+
+
+def near_body(place, near, far, grad_in, grad_out):
     for i, out in enumerate((grad_in, grad_out)):
-        out[0] = (near[i] + arrived[i].astype(wide) + far[i].astype(wide)).astype(narrow)
+        out[0] = (near[i] + far[i].astype(wide)).astype(narrow)
 
 
 def last_body(riding, place, *refs):
@@ -263,18 +266,18 @@
     columns = call(
         functools.partial(columns_body, n_line, block),
         [shape((tok_rows, n_line * block), narrow)] * 2
-        + [shape((2, tok_rows, n_line * block), narrow)],
+        + [shape((2, tok_rows, n_line * block), narrow), shape((2, latent_width, hidden_width), narrow)],
         "columns",
-        scratch=[pltpu.SemaphoreType.DMA((4 * n_line,))],
-        outside=1,
-    )(place, tokens)
+        scratch=[pltpu.SemaphoreType.DMA((4 * n_line + 2,))],
+        outside=3,
+    )(place, *(pltpu.with_memory_space_constraint(value, pltpu.HBM) for value in (tokens, expert_in, expert_out)))
     stack = lambda first, second, *earlier: call(
         stack_body, [shape((2,) + first.shape, narrow)], "stack"
     )(after(place, *earlier) if earlier else place, first, second)[0]
     (payload,) = call(payload_body, [shape((tok_rows + gate_rows, latent_width), narrow)], "payload")(
         place, routes.T, gate_levels.T, latent_grad
     )
-    own = stack(expert_in[0], expert_out[0], downs[1])
+    own = columns[3]
     core_own = swap(own, n_line, 1, 0)
     across = swap(columns[2], n_line, 0, 1)
     core_tokens = [swap(after(columns[1], across, core_own), n_line, 1, 0), swap(across[1], n_line, 1, 0)]
@@ -334,12 +337,18 @@
         *(rows[i] for group in groups for i in group),
         *(value for values in saved for value in values),
     )
+    core_down = swap(after(both_down, near), n_line, 1, 0)
     delta_lines = [after(line, near, both_down) for line in delta_lines]
     (delta,) = call(add_body, [rows_of(narrow)], "latent_delta")(place, *delta_lines)
     side_delta = swap(delta, n_line, 0, 1)
+    (grad_tokens,) = call(
+        functools.partial(token_grad_body, n_line, block), [shape((tok_rows, width), narrow)], "token_grad"
+    )(place, delta, both_down, core_down)
     out_lines = [outs_of[0]] + [home(outs_of[back], back) if back not in riding else None for back in range(1, n_line)]
     other = swap(after(other, delta), n_line, 1, 0)
-    (far,) = call(far_body, [shape(pair, narrow)], "far_grads")(place, far, after(other, out_lines[1]))
+    near, far = call(core_sum_body, [shape(pair, wide), shape(pair, narrow)], "core_sums")(
+        after(place, grad_tokens), near, far, after(other, out_lines[1])
+    )
     sent = far
     far = swap(after(far, side_delta), n_line, 0, 1)
     core_deltas = swap(stack(delta, side_delta, sent), n_line, 1, 0)
@@ -351,17 +360,13 @@
         ],
         "down_grad",
     )(place, columns[0], across, *core_tokens, delta, side_delta, core_deltas, *(outs_of[back] for back in riding))
-    core_down = swap(after(both_down, blocks[1]), n_line, 1, 0)
-    (grad_tokens,) = call(
-        functools.partial(token_grad_body, n_line, block), [shape((tok_rows, width), narrow)], "token_grad"
-    )(place, after(delta, blocks[1]), both_down, core_down)
     blocks = [blocks[0]] + [turn(blocks[back], n_line, n_line - back) for back in range(1, n_line)]
     grad_down, latent_out = call(
         functools.partial(last_body, riding), [shape((block, latent_width), wide), rows_of(narrow)], "last_sums"
-    )(after(place, grad_tokens), *blocks, *(line for line in out_lines if line is not None))
+    )(place, *blocks, *(line for line in out_lines if line is not None))
     grad_in, grad_out = call(
         near_body, [shape(expert_in.shape, narrow), shape(expert_out.shape, narrow)], "near_grads"
-    )(after(place, grad_down), near, other, far)
+    )(place, near, far)
     return (latent_out, grad_tokens, grad_down, grad_in, grad_out)
 
 

time: 120 us -> 115 us (0.958)
  waiting for transfers between devices: 56.6 us -> 50.3 us
  starting transfers between devices: 37.3 us -> 38.9 us
    ppermute x16, waiting for transfers between devices: 46.2 us -> 40.5 us  [turn(): lax.ppermute(value, plane, device_pairs(n_line, lambda z, x, c: ((z + by)...]
    ppermute x16, starting transfers between devices: 25.6 us -> 27.4 us  [turn(): lax.ppermute(value, plane, device_pairs(n_line, lambda z, x, c: ((z + by)...]
    pallas_call x16 -> x15, Pallas kernels: 22.2 us -> 22.7 us  [run(): pl.pallas_call(body, out_shape=outs, in_specs=[pl.BlockSpec(memory_space=...]
    unnamed x18 -> x12, local copies, waits for them, and re-layouts: 2.43 us -> 2.29 us
  transfers between devices with their start and end apart: 32 -> 32, of which waited for: 18 -> 15; matrix products, arithmetic and copies ran while one was open for 0% -> 0% of each run, Pallas kernels for 13% -> 15%
where the time goes in v12:
time: 115 us
  waiting for transfers between devices  50.3 us (44%)
  starting transfers between devices  38.9 us (34%)
  Pallas kernels  22.7 us (20%)
  local copies, waits for them, and re-layouts  2.39 us (2%)
    ppermute x16, waiting for transfers between devices, turn(): lax.ppermute(value, plane, device_pairs(n_line, lambda z, x, c: ((z + by)...  40.5 us
    ppermute x16, starting transfers between devices, turn(): lax.ppermute(value, plane, device_pairs(n_line, lambda z, x, c: ((z + by)...  27.4 us
    pallas_call x15, Pallas kernels, run(): pl.pallas_call(body, out_shape=outs, in_specs=[pl.BlockSpec(memory_space=...  22.7 us
    ppermute x16, starting transfers between devices, swap(): lax.ppermute(value, plane, device_pairs(n_line, lambda z, x, c: (z, x ^ s...  11.5 us
    ppermute x16, waiting for transfers between devices, swap(): lax.ppermute(value, plane, device_pairs(n_line, lambda z, x, c: (z, x ^ s...  9.73 us
  transfers between devices with their start and end apart: 32, of which 15 were waited for; matrix products, arithmetic and copies ran while one was open for 0% of the time, Pallas kernels for 15%

profile of v12, /device:TPU:0, one launch (start us, length us, event | category | flops | bytes accessed | tf_op | source)
XLA Modules:
  0.0 115.2 jit_solution(8761986619909379735)
XLA Ops:
  0.8 2.0 %columns.1 = (bf16[128,512]{1,0:T(8,128)(2,1)S(1)}, bf16[128,512]{1,0:T(8,128)(2,1)S(1)}, bf16[2,128,512]{2,1,0:T(8,128)(2,1)S(1)}, bf16[2,512,512]{2,1,0:T(8,128)(2,1)S(1)}) custom-call(s32[7]{0:T(128)S(1)} %stack.33.place, bf16[128,2048]{1,0:T(8,128)(2,1)} %tokens.1, bf16[1,512,512]{2,1,0:T(8,128)(2,1)} %expert_in.1, bf16[1,512,512]{2,1,0:T(8,128)(2,1)} %expert_out.1), custom_call_target="tpu_custom_call" | custom-call | tf_op jit(solution)/shard_map/columns/pallas_call | solution.py:45
  3.3 2.6 %collective-permute-start = (bf16[2,128,512]{2,1,0:T(8,128)(2,1)S(1)}, bf16[2,128,512]{2,1,0:T(8,128)(2,1)S(1)}, u32[]{:S(2)}, u32[]{:S(2)}) collective-permute-start(bf16[2,128,512]{2,1,0:T(8,128)(2,1)S(1)} %get-tuple-element.60), channel_id=1, source_target_pairs={{0,2},{1,3},{2,0},{3,1},{4,6},{5,7},{6,4},{7,5},{8,10},{9,11},{10,... | collective-permute-start | bytes 786440 | tf_op jit(solution)/shard_map/ppermute | solution.py:33
  5.8 1.6 %collective-permute-start.4 = (bf16[128,512]{1,0:T(8,128)(2,1)}, bf16[128,512]{1,0:T(8,128)(2,1)S(1)}, u32[]{:S(2)}, u32[]{:S(2)}) collective-permute-start(bf16[128,512]{1,0:T(8,128)(2,1)} %refs_4_.1), channel_id=1, source_target_pairs={{0,4},{1,5},{2,6},{3,7},{4,8},{5,9},{6,10},{7,11},{8,12},{9,13},{1... | collective-permute-start | bytes 393224 | tf_op jit(solution)/shard_map/ppermute | solution.py:29
  7.4 2.6 %collective-permute-start.5 = (bf16[128,512]{1,0:T(8,128)(2,1)}, bf16[128,512]{1,0:T(8,128)(2,1)S(1)}, u32[]{:S(2)}, u32[]{:S(2)}) collective-permute-start(bf16[128,512]{1,0:T(8,128)(2,1)} %refs_4_.1), channel_id=1, source_target_pairs={{0,8},{1,9},{2,10},{3,11},{4,12},{5,13},{6,14},{7,15},{8,0},{9,1},... | collective-permute-start | bytes 393224 | tf_op jit(solution)/shard_map/ppermute | solution.py:29
  16.2 3.0 %collective-permute-done.5.refs_6_ = bf16[128,512]{1,0:T(8,128)(2,1)S(1)} collective-permute-done((bf16[128,512]{1,0:T(8,128)(2,1)}, bf16[128,512]{1,0:T(8,128)(2,1)S(1)}, u32[]{:S(2)}, u32[]{:S(2)}) %collective-permute-start.5) | collective-permute-done | bytes 131104 | tf_op jit(solution)/shard_map/ppermute | solution.py:29
  20.9 3.3 %collective-permute-start.10 = (bf16[144,512]{1,0:T(8,128)(2,1)S(1)}, bf16[144,512]{1,0:T(8,128)(2,1)S(1)}, u32[]{:S(2)}, u32[]{:S(2)}) collective-permute-start(bf16[144,512]{1,0:T(8,128)(2,1)S(1)} %payload.1.refs_7_), channel_id=1, source_target_pairs={{0,4},{1,5},{2,6},{3,7},{4,8},{5,9},{6,10},{7,11},{8,12},{9,13},{1... | collective-permute-start | bytes 442376 | tf_op jit(solution)/shard_map/ppermute | solution.py:29
  24.2 1.6 %collective-permute-start.11 = (bf16[144,512]{1,0:T(8,128)(2,1)S(1)}, bf16[144,512]{1,0:T(8,128)(2,1)S(1)}, u32[]{:S(2)}, u32[]{:S(2)}) collective-permute-start(bf16[144,512]{1,0:T(8,128)(2,1)S(1)} %payload.1.refs_7_), channel_id=1, source_target_pairs={{0,8},{1,9},{2,10},{3,11},{4,12},{5,13},{6,14},{7,15},{8,0},{9,1},... | collective-permute-start | bytes 442376 | tf_op jit(solution)/shard_map/ppermute | solution.py:29
  30.0 5.9 %collective-permute-done.11.refs_5_ = bf16[144,512]{1,0:T(8,128)(2,1)S(1)} collective-permute-done((bf16[144,512]{1,0:T(8,128)(2,1)S(1)}, bf16[144,512]{1,0:T(8,128)(2,1)S(1)}, u32[]{:S(2)}, u32[]{:S(2)}) %collective-permute-start.11) | collective-permute-done | bytes 147488 | tf_op jit(solution)/shard_map/ppermute | solution.py:29
  35.8 1.6 %collective-permute-done.8.refs_1_ = bf16[128,512]{1,0:T(8,128)(2,1)S(1)} collective-permute-done((bf16[128,512]{1,0:T(8,128)(2,1)S(1)}, bf16[128,512]{1,0:T(8,128)(2,1)S(1)}, u32[]{:S(2)}, u32[]{:S(2)}) %collective-permute-start.8) | collective-permute-done | bytes 131104 | tf_op jit(solution)/shard_map/ppermute | solution.py:33
  38.6 3.3 %collective-permute-start.13 = (bf16[128,512]{1,0:T(8,128)(2,1)S(1)}, bf16[128,512]{1,0:T(8,128)(2,1)S(1)}, u32[]{:S(2)}, u32[]{:S(2)}) collective-permute-start(bf16[128,512]{1,0:T(8,128)(2,1)S(1)} %latent.1.refs_3_), channel_id=1, source_target_pairs={{0,4},{1,5},{2,6},{3,7},{4,8},{5,9},{6,10},{7,11},{8,12},{9,13},{1... | collective-permute-start | bytes 393224 | tf_op jit(solution)/shard_map/ppermute | solution.py:29
  41.9 1.6 %collective-permute-start.14 = (bf16[128,512]{1,0:T(8,128)(2,1)S(1)}, bf16[128,512]{1,0:T(8,128)(2,1)S(1)}, u32[]{:S(2)}, u32[]{:S(2)}) collective-permute-start(bf16[128,512]{1,0:T(8,128)(2,1)S(1)} %latent.1.refs_3_), channel_id=1, source_target_pairs={{0,8},{1,9},{2,10},{3,11},{4,12},{5,13},{6,14},{7,15},{8,0},{9,1},... | collective-permute-start | bytes 393224 | tf_op jit(solution)/shard_map/ppermute | solution.py:29
  44.3 3.2 %collective-permute-done.13.refs_0_ = bf16[128,512]{1,0:T(8,128)(2,1)S(1)} collective-permute-done((bf16[128,512]{1,0:T(8,128)(2,1)S(1)}, bf16[128,512]{1,0:T(8,128)(2,1)S(1)}, u32[]{:S(2)}, u32[]{:S(2)}) %collective-permute-start.13) | collective-permute-done | bytes 131104 | tf_op jit(solution)/shard_map/ppermute | solution.py:29
  47.5 4.3 %collective-permute-done.14.refs_1_ = bf16[128,512]{1,0:T(8,128)(2,1)S(1)} collective-permute-done((bf16[128,512]{1,0:T(8,128)(2,1)S(1)}, bf16[128,512]{1,0:T(8,128)(2,1)S(1)}, u32[]{:S(2)}, u32[]{:S(2)}) %collective-permute-start.14) | collective-permute-done | bytes 131104 | tf_op jit(solution)/shard_map/ppermute | solution.py:29
  53.7 6.1 %experts.1 = (bf16[128,512]{1,0:T(8,128)(2,1)S(1)}, bf16[128,512]{1,0:T(8,128)(2,1)S(1)}, bf16[128,512]{1,0:T(8,128)(2,1)S(1)}, bf16[128,512]{1,0:T(8,128)(2,1)S...) custom-call(s32[7]{0:T(128)S(1)} %stack.33.place, ...), custom_call_target="tpu_custom_call" | custom-call | tf_op jit(solution)/shard_map/experts/pallas_call | solution.py:45
  59.8 4.2 %collective-permute-start.19 = (bf16[128,512]{1,0:T(8,128)(2,1)S(1)}, bf16[128,512]{1,0:T(8,128)(2,1)S(1)}, u32[]{:S(2)}, u32[]{:S(2)}) collective-permute-start(bf16[128,512]{1,0:T(8,128)(2,1)S(1)} %get-tuple-element.77), channel_id=1, source_target_pairs={{0,12},{1,13},{2,14},{3,15},{4,0},{5,1},{6,2},{7,3},{8,4},{9,5},{1... | collective-permute-start | bytes 393224 | tf_op jit(solution)/shard_map/ppermute | solution.py:29
  68.0 2.9 %weight_grads.1 = (f32[2,512,512]{2,1,0:T(8,128)S(1)}, f32[2,512,512]{2,1,0:T(8,128)S(1)}, bf16[4,512,512]{2,1,0:T(8,128)(2,1)S(1)}) custom-call(s32[7]{0:T(128)S(1)} %stack.33.place, bf16[128,512]{1,0:T(8,128)(2,1)S(1)} %collective-permute-done.13.refs_0_, bf16[128,512]{1,0:T(8,128)(2,1)S(1)} %collective-permute-done.14.refs_1_, ...), custom_call_target="tpu_custom_call" | custom-call | tf_op jit(solution)/shard_map/weight_grads/pallas_call | solution.py:45
  70.9 5.6 %collective-permute-done.21.refs_2_ = bf16[128,512]{1,0:T(8,128)(2,1)S(1)} collective-permute-done((bf16[128,512]{1,0:T(8,128)(2,1)S(1)}, bf16[128,512]{1,0:T(8,128)(2,1)S(1)}, u32[]{:S(2)}, u32[]{:S(2)}) %collective-permute-start.21) | collective-permute-done | bytes 131104 | tf_op jit(solution)/shard_map/ppermute | solution.py:29
  79.5 3.4 %collective-permute-done.24.core_downs = bf16[2,512,512]{2,1,0:T(8,128)(2,1)S(1)} collective-permute-done((bf16[2,512,512]{2,1,0:T(8,128)(2,1)S(1)}, bf16[2,512,512]{2,1,0:T(8,128)(2,1)S(1)}, u32[]{:S(2)}, u32[]{:S(2)}) %collective-permute-start.24) | collective-permute-done | bytes 1048608 | tf_op jit(solution)/shard_map/ppermute | solution.py:33
  82.8 2.2 %token_grad.1 = bf16[128,2048]{1,0:T(8,128)(2,1)} custom-call(s32[7]{0:T(128)S(1)} %stack.33.place, bf16[128,512]{1,0:T(8,128)(2,1)S(1)} %latent_delta.1.delta.first.refs_4_, bf16[2,512,512]{2,1,0:T(8,128)(2,1)S(1)} %stack.34.downs, bf16[2,512,512]{2,1,0:T(8,128)(2,1)S(1)} %collective-permute-done.24.core_downs), custom_call_target="tpu_custom_call" | custom-call | tf_op jit(solution)/shard_map/token_grad/pallas_call | solution.py:45
  85.9 1.6 %collective-permute-start.31 = (bf16[2,512,512]{2,1,0:T(8,128)(2,1)S(1)}, bf16[2,512,512]{2,1,0:T(8,128)(2,1)S(1)}, u32[]{:S(2)}, u32[]{:S(2)}) collective-permute-start(bf16[2,512,512]{2,1,0:T(8,128)(2,1)S(1)} %get-tuple-element.110), channel_id=1, source_target_pairs={{0,2},{1,3},{2,0},{3,1},{4,6},{5,7},{6,4},{7,5},{8,10},{9,11},{10,... | collective-permute-start | bytes 3145736 | tf_op jit(solution)/shard_map/ppermute | solution.py:33
  92.5 3.7 %collective-permute-start.28 = (bf16[128,512]{1,0:T(8,128)(2,1)S(1)}, bf16[128,512]{1,0:T(8,128)(2,1)S(1)}, u32[]{:S(2)}, u32[]{:S(2)}) collective-permute-start(bf16[128,512]{1,0:T(8,128)(2,1)S(1)} %get-tuple-element.103), channel_id=1, source_target_pairs={{0,12},{1,13},{2,14},{3,15},{4,0},{5,1},{6,2},{7,3},{8,4},{9,5},{1... | collective-permute-start | bytes 393224 | tf_op jit(solution)/shard_map/ppermute | solution.py:29
  96.2 10.6 %collective-permute-done.28.refs_1_ = bf16[128,512]{1,0:T(8,128)(2,1)S(1)} collective-permute-done((bf16[128,512]{1,0:T(8,128)(2,1)S(1)}, bf16[128,512]{1,0:T(8,128)(2,1)S(1)}, u32[]{:S(2)}, u32[]{:S(2)}) %collective-permute-start.28) | collective-permute-done | bytes 131104 | tf_op jit(solution)/shard_map/ppermute | solution.py:29
  106.7 5.5 %collective-permute-done.29.refs_2_ = bf16[2,128,512]{2,1,0:T(8,128)(2,1)S(1)} collective-permute-done((bf16[2,128,512]{2,1,0:T(8,128)(2,1)S(1)}, bf16[2,128,512]{2,1,0:T(8,128)(2,1)S(1)}, u32[]{:S(2)}, u32[]{:S(2)}) %collective-permute-start.29) | collective-permute-done | bytes 262176 | tf_op jit(solution)/shard_map/ppermute | solution.py:29
  113.5 1.6 %near_grads.1 = (bf16[1,512,512]{2,1,0:T(8,128)(2,1)}, bf16[1,512,512]{2,1,0:T(8,128)(2,1)}) custom-call(s32[7]{0:T(128)S(1)} %stack.33.place, f32[2,512,512]{2,1,0:T(8,128)S(1)} %get-tuple-element.109.near, bf16[2,512,512]{2,1,0:T(8,128)(2,1)S(1)} %collective-permute-done.31.far), custom_call_target="tpu_custom_call" | custom-call | tf_op jit(solution)/shard_map/near_grads/pallas_call | solution.py:45
  (69 shorter events, 30.6 us)
Async XLA Ops:
  2.7 10.1 %collective-permute-start.1 = (bf16[2,512,512]{2,1,0:T(8,128)(2,1)S(1)}, bf16[2,512,512]{2,1,0:T(8,128)(2,1)S(1)}, u32[]{:S(2)}, u32[]{:S(2)}) collective-permute-start(bf16[2,512,512]{2,1,0:T(8,128)(2,1)S(1)} %get-tuple-element.62.refs_8_), channel_id=1, source_target_pairs={{0,1},{1,0},{2,3},{3,2},{4,5},{5,4},{6,7},{7,6},{8,9},{9,8},{10,11... | collective-permute-start | bytes 3145736 | tf_op jit(solution)/shard_map/ppermute | solution.py:33
  3.3 9.5 %collective-permute-start = (bf16[2,128,512]{2,1,0:T(8,128)(2,1)S(1)}, bf16[2,128,512]{2,1,0:T(8,128)(2,1)S(1)}, u32[]{:S(2)}, u32[]{:S(2)}) collective-permute-start(bf16[2,128,512]{2,1,0:T(8,128)(2,1)S(1)} %get-tuple-element.60), channel_id=1, source_target_pairs={{0,2},{1,3},{2,0},{3,1},{4,6},{5,7},{6,4},{7,5},{8,10},{9,11},{10,... | collective-permute-start | bytes 786440 | tf_op jit(solution)/shard_map/ppermute | solution.py:33
  5.8 10.3 %collective-permute-start.4 = (bf16[128,512]{1,0:T(8,128)(2,1)}, bf16[128,512]{1,0:T(8,128)(2,1)S(1)}, u32[]{:S(2)}, u32[]{:S(2)}) collective-permute-start(bf16[128,512]{1,0:T(8,128)(2,1)} %refs_4_.1), channel_id=1, source_target_pairs={{0,4},{1,5},{2,6},{3,7},{4,8},{5,9},{6,10},{7,11},{8,12},{9,13},{1... | collective-permute-start | bytes 393224 | tf_op jit(solution)/shard_map/ppermute | solution.py:29
  7.4 11.8 %collective-permute-start.5 = (bf16[128,512]{1,0:T(8,128)(2,1)}, bf16[128,512]{1,0:T(8,128)(2,1)S(1)}, u32[]{:S(2)}, u32[]{:S(2)}) collective-permute-start(bf16[128,512]{1,0:T(8,128)(2,1)} %refs_4_.1), channel_id=1, source_target_pairs={{0,8},{1,9},{2,10},{3,11},{4,12},{5,13},{6,14},{7,15},{8,0},{9,1},... | collective-permute-start | bytes 393224 | tf_op jit(solution)/shard_map/ppermute | solution.py:29
  10.0 9.2 %collective-permute-start.6 = (bf16[128,512]{1,0:T(8,128)(2,1)}, bf16[128,512]{1,0:T(8,128)(2,1)S(1)}, u32[]{:S(2)}, u32[]{:S(2)}) collective-permute-start(bf16[128,512]{1,0:T(8,128)(2,1)} %refs_4_.1), channel_id=1, source_target_pairs={{0,12},{1,13},{2,14},{3,15},{4,0},{5,1},{6,2},{7,3},{8,4},{9,5},{1... | collective-permute-start | bytes 393224 | tf_op jit(solution)/shard_map/ppermute | solution.py:29
  20.3 15.5 %collective-permute-start.9 = (bf16[512,512]{1,0:T(8,128)(2,1)S(1)}, bf16[512,512]{1,0:T(8,128)(2,1)S(1)}, u32[]{:S(2)}, u32[]{:S(2)}) collective-permute-start(bf16[512,512]{1,0:T(8,128)(2,1)S(1)} %bitcast.15), channel_id=1, source_target_pairs={{0,2},{1,3},{2,0},{3,1},{4,6},{5,7},{6,4},{7,5},{8,10},{9,11},{10,... | collective-permute-start | bytes 1572872 | tf_op jit(solution)/shard_map/ppermute | solution.py:33
  20.9 9.1 %collective-permute-start.10 = (bf16[144,512]{1,0:T(8,128)(2,1)S(1)}, bf16[144,512]{1,0:T(8,128)(2,1)S(1)}, u32[]{:S(2)}, u32[]{:S(2)}) collective-permute-start(bf16[144,512]{1,0:T(8,128)(2,1)S(1)} %payload.1.refs_7_), channel_id=1, source_target_pairs={{0,4},{1,5},{2,6},{3,7},{4,8},{5,9},{6,10},{7,11},{8,12},{9,13},{1... | collective-permute-start | bytes 442376 | tf_op jit(solution)/shard_map/ppermute | solution.py:29
  24.2 11.7 %collective-permute-start.11 = (bf16[144,512]{1,0:T(8,128)(2,1)S(1)}, bf16[144,512]{1,0:T(8,128)(2,1)S(1)}, u32[]{:S(2)}, u32[]{:S(2)}) collective-permute-start(bf16[144,512]{1,0:T(8,128)(2,1)S(1)} %payload.1.refs_7_), channel_id=1, source_target_pairs={{0,8},{1,9},{2,10},{3,11},{4,12},{5,13},{6,14},{7,15},{8,0},{9,1},... | collective-permute-start | bytes 442376 | tf_op jit(solution)/shard_map/ppermute | solution.py:29
  25.8 10.0 %collective-permute-start.12 = (bf16[144,512]{1,0:T(8,128)(2,1)S(1)}, bf16[144,512]{1,0:T(8,128)(2,1)S(1)}, u32[]{:S(2)}, u32[]{:S(2)}) collective-permute-start(bf16[144,512]{1,0:T(8,128)(2,1)S(1)} %payload.1.refs_7_), channel_id=1, source_target_pairs={{0,12},{1,13},{2,14},{3,15},{4,0},{5,1},{6,2},{7,3},{8,4},{9,5},{1... | collective-permute-start | bytes 442376 | tf_op jit(solution)/shard_map/ppermute | solution.py:29
  27.2 10.3 %collective-permute-start.8 = (bf16[128,512]{1,0:T(8,128)(2,1)S(1)}, bf16[128,512]{1,0:T(8,128)(2,1)S(1)}, u32[]{:S(2)}, u32[]{:S(2)}) collective-permute-start(bf16[128,512]{1,0:T(8,128)(2,1)S(1)} %get-tuple-element.68), channel_id=1, source_target_pairs={{0,2},{1,3},{2,0},{3,1},{4,6},{5,7},{6,4},{7,5},{8,10},{9,11},{10,... | collective-permute-start | bytes 393224 | tf_op jit(solution)/shard_map/ppermute | solution.py:33
  38.0 13.7 %collective-permute-start.16 = (bf16[512,512]{1,0:T(8,128)(2,1)S(1)}, bf16[512,512]{1,0:T(8,128)(2,1)S(1)}, u32[]{:S(2)}, u32[]{:S(2)}) collective-permute-start(bf16[512,512]{1,0:T(8,128)(2,1)S(1)} %bitcast.16), channel_id=1, source_target_pairs={{0,2},{1,3},{2,0},{3,1},{4,6},{5,7},{6,4},{7,5},{8,10},{9,11},{10,... | collective-permute-start | bytes 1572872 | tf_op jit(solution)/shard_map/ppermute | solution.py:33
  38.6 8.8 %collective-permute-start.13 = (bf16[128,512]{1,0:T(8,128)(2,1)S(1)}, bf16[128,512]{1,0:T(8,128)(2,1)S(1)}, u32[]{:S(2)}, u32[]{:S(2)}) collective-permute-start(bf16[128,512]{1,0:T(8,128)(2,1)S(1)} %latent.1.refs_3_), channel_id=1, source_target_pairs={{0,4},{1,5},{2,6},{3,7},{4,8},{5,9},{6,10},{7,11},{8,12},{9,13},{1... | collective-permute-start | bytes 393224 | tf_op jit(solution)/shard_map/ppermute | solution.py:29
  41.9 9.8 %collective-permute-start.14 = (bf16[128,512]{1,0:T(8,128)(2,1)S(1)}, bf16[128,512]{1,0:T(8,128)(2,1)S(1)}, u32[]{:S(2)}, u32[]{:S(2)}) collective-permute-start(bf16[128,512]{1,0:T(8,128)(2,1)S(1)} %latent.1.refs_3_), channel_id=1, source_target_pairs={{0,8},{1,9},{2,10},{3,11},{4,12},{5,13},{6,14},{7,15},{8,0},{9,1},... | collective-permute-start | bytes 393224 | tf_op jit(solution)/shard_map/ppermute | solution.py:29
  43.6 8.2 %collective-permute-start.15 = (bf16[128,512]{1,0:T(8,128)(2,1)S(1)}, bf16[128,512]{1,0:T(8,128)(2,1)S(1)}, u32[]{:S(2)}, u32[]{:S(2)}) collective-permute-start(bf16[128,512]{1,0:T(8,128)(2,1)S(1)} %latent.1.refs_3_), channel_id=1, source_target_pairs={{0,12},{1,13},{2,14},{3,15},{4,0},{5,1},{6,2},{7,3},{8,4},{9,5},{1... | collective-permute-start | bytes 393224 | tf_op jit(solution)/shard_map/ppermute | solution.py:29
  44.3 9.0 %collective-permute-start.17 = (bf16[512,512]{1,0:T(8,128)(2,1)S(1)}, bf16[512,512]{1,0:T(8,128)(2,1)S(1)}, u32[]{:S(2)}, u32[]{:S(2)}) collective-permute-start(bf16[512,512]{1,0:T(8,128)(2,1)S(1)} %collective-permute-done.9.refs_10_), channel_id=1, source_target_pairs={{0,1},{1,0},{2,3},{3,2},{4,5},{5,4},{6,7},{7,6},{8,9},{9,8},{10,11... | collective-permute-start | bytes 1572872 | tf_op jit(solution)/shard_map/ppermute | solution.py:33
  51.8 14.3 %collective-permute-start.20 = (bf16[512,512]{1,0:T(8,128)(2,1)S(1)}, bf16[512,512]{1,0:T(8,128)(2,1)S(1)}, u32[]{:S(2)}, u32[]{:S(2)}) collective-permute-start(bf16[512,512]{1,0:T(8,128)(2,1)S(1)} %get-tuple-element.84.first), channel_id=1, source_target_pairs={{0,2},{1,3},{2,0},{3,1},{4,6},{5,7},{6,4},{7,5},{8,10},{9,11},{10,... | collective-permute-start | bytes 1572872 | tf_op jit(solution)/shard_map/ppermute | solution.py:33
  59.8 8.2 %collective-permute-start.19 = (bf16[128,512]{1,0:T(8,128)(2,1)S(1)}, bf16[128,512]{1,0:T(8,128)(2,1)S(1)}, u32[]{:S(2)}, u32[]{:S(2)}) collective-permute-start(bf16[128,512]{1,0:T(8,128)(2,1)S(1)} %get-tuple-element.77), channel_id=1, source_target_pairs={{0,12},{1,13},{2,14},{3,15},{4,0},{5,1},{6,2},{7,3},{8,4},{9,5},{1... | collective-permute-start | bytes 393224 | tf_op jit(solution)/shard_map/ppermute | solution.py:29
  64.0 12.5 %collective-permute-start.21 = (bf16[128,512]{1,0:T(8,128)(2,1)S(1)}, bf16[128,512]{1,0:T(8,128)(2,1)S(1)}, u32[]{:S(2)}, u32[]{:S(2)}) collective-permute-start(bf16[128,512]{1,0:T(8,128)(2,1)S(1)} %get-tuple-element.87), channel_id=1, source_target_pairs={{0,8},{1,9},{2,10},{3,11},{4,12},{5,13},{6,14},{7,15},{8,0},{9,1},... | collective-permute-start | bytes 393224 | tf_op jit(solution)/shard_map/ppermute | solution.py:29
  64.6 11.9 %collective-permute-start.22 = (bf16[128,512]{1,0:T(8,128)(2,1)S(1)}, bf16[128,512]{1,0:T(8,128)(2,1)S(1)}, u32[]{:S(2)}, u32[]{:S(2)}) collective-permute-start(bf16[128,512]{1,0:T(8,128)(2,1)S(1)} %get-tuple-element.89), channel_id=1, source_target_pairs={{0,4},{1,5},{2,6},{3,7},{4,8},{5,9},{6,10},{7,11},{8,12},{9,13},{1... | collective-permute-start | bytes 393224 | tf_op jit(solution)/shard_map/ppermute | solution.py:29
  77.1 7.9 %collective-permute-start.25 = (bf16[4,512,512]{2,1,0:T(8,128)(2,1)S(1)}, bf16[4,512,512]{2,1,0:T(8,128)(2,1)S(1)}, u32[]{:S(2)}, u32[]{:S(2)}) collective-permute-start(bf16[4,512,512]{2,1,0:T(8,128)(2,1)S(1)} %get-tuple-element.95), channel_id=1, source_target_pairs={{0,1},{1,0},{2,3},{3,2},{4,5},{5,4},{6,7},{7,6},{8,9},{9,8},{10,11... | collective-permute-start | bytes 6291464 | tf_op jit(solution)/shard_map/ppermute | solution.py:33
  85.9 27.6 %collective-permute-start.31 = (bf16[2,512,512]{2,1,0:T(8,128)(2,1)S(1)}, bf16[2,512,512]{2,1,0:T(8,128)(2,1)S(1)}, u32[]{:S(2)}, u32[]{:S(2)}) collective-permute-start(bf16[2,512,512]{2,1,0:T(8,128)(2,1)S(1)} %get-tuple-element.110), channel_id=1, source_target_pairs={{0,2},{1,3},{2,0},{3,1},{4,6},{5,7},{6,4},{7,5},{8,10},{9,11},{10,... | collective-permute-start | bytes 3145736 | tf_op jit(solution)/shard_map/ppermute | solution.py:33
  90.9 21.3 %collective-permute-start.29 = (bf16[2,128,512]{2,1,0:T(8,128)(2,1)S(1)}, bf16[2,128,512]{2,1,0:T(8,128)(2,1)S(1)}, u32[]{:S(2)}, u32[]{:S(2)}) collective-permute-start(bf16[2,128,512]{2,1,0:T(8,128)(2,1)S(1)} %get-tuple-element.104), channel_id=1, source_target_pairs={{0,8},{1,9},{2,10},{3,11},{4,12},{5,13},{6,14},{7,15},{8,0},{9,1},... | collective-permute-start | bytes 786440 | tf_op jit(solution)/shard_map/ppermute | solution.py:29
  92.3 19.9 %collective-permute-start.30 = (bf16[2,128,512]{2,1,0:T(8,128)(2,1)S(1)}, bf16[2,128,512]{2,1,0:T(8,128)(2,1)S(1)}, u32[]{:S(2)}, u32[]{:S(2)}) collective-permute-start(bf16[2,128,512]{2,1,0:T(8,128)(2,1)S(1)} %get-tuple-element.105), channel_id=1, source_target_pairs={{0,4},{1,5},{2,6},{3,7},{4,8},{5,9},{6,10},{7,11},{8,12},{9,13},{1... | collective-permute-start | bytes 786440 | tf_op jit(solution)/shard_map/ppermute | solution.py:29
  92.5 14.2 %collective-permute-start.28 = (bf16[128,512]{1,0:T(8,128)(2,1)S(1)}, bf16[128,512]{1,0:T(8,128)(2,1)S(1)}, u32[]{:S(2)}, u32[]{:S(2)}) collective-permute-start(bf16[128,512]{1,0:T(8,128)(2,1)S(1)} %get-tuple-element.103), channel_id=1, source_target_pairs={{0,12},{1,13},{2,14},{3,15},{4,0},{5,1},{6,2},{7,3},{8,4},{9,5},{1... | collective-permute-start | bytes 393224 | tf_op jit(solution)/shard_map/ppermute | solution.py:29
  (14 other events, 121.1 us)

commit v13 on v12

--- a/solution.py
+++ b/solution.py
@@ -303,7 +303,7 @@
 
     side_out = swap(after(expert_out[0], latent), n_line, 0, 1)
     core_in = swap(after(side_in, latent), n_line, 1, 0)
-    core_out = swap(after(side_out, *rows[1:]), n_line, 1, 0)
+    core_out = swap(after(side_out, rows[1]), n_line, 1, 0)
     weights = [own, core_own, side_in, side_out, core_in, core_out]
     side_down = swap(after(down, *rows[1:]), n_line, 0, 1)
 
@@ -337,17 +337,13 @@
         *(rows[i] for group in groups for i in group),
         *(value for values in saved for value in values),
     )
-    core_down = swap(after(both_down, near), n_line, 1, 0)
     delta_lines = [after(line, near, both_down) for line in delta_lines]
     (delta,) = call(add_body, [rows_of(narrow)], "latent_delta")(place, *delta_lines)
     side_delta = swap(delta, n_line, 0, 1)
-    (grad_tokens,) = call(
-        functools.partial(token_grad_body, n_line, block), [shape((tok_rows, width), narrow)], "token_grad"
-    )(place, delta, both_down, core_down)
     out_lines = [outs_of[0]] + [home(outs_of[back], back) if back not in riding else None for back in range(1, n_line)]
     other = swap(after(other, delta), n_line, 1, 0)
     near, far = call(core_sum_body, [shape(pair, wide), shape(pair, narrow)], "core_sums")(
-        after(place, grad_tokens), near, far, after(other, out_lines[1])
+        place, near, far, after(other, out_lines[1])
     )
     sent = far
     far = swap(after(far, side_delta), n_line, 0, 1)
@@ -360,10 +356,14 @@
         ],
         "down_grad",
     )(place, columns[0], across, *core_tokens, delta, side_delta, core_deltas, *(outs_of[back] for back in riding))
+    core_down = swap(after(both_down, blocks[1]), n_line, 1, 0)
+    (grad_tokens,) = call(
+        functools.partial(token_grad_body, n_line, block), [shape((tok_rows, width), narrow)], "token_grad"
+    )(place, after(delta, blocks[1]), both_down, core_down)
     blocks = [blocks[0]] + [turn(blocks[back], n_line, n_line - back) for back in range(1, n_line)]
     grad_down, latent_out = call(
         functools.partial(last_body, riding), [shape((block, latent_width), wide), rows_of(narrow)], "last_sums"
-    )(place, *blocks, *(line for line in out_lines if line is not None))
+    )(after(place, grad_tokens), *blocks, *(line for line in out_lines if line is not None))
     grad_in, grad_out = call(
         near_body, [shape(expert_in.shape, narrow), shape(expert_out.shape, narrow)], "near_grads"
     )(place, near, far)

time: 115 us -> 115 us (level)
  waiting for transfers between devices: 50.3 us -> 51.6 us
  starting transfers between devices: 38.9 us -> 37.6 us
    ppermute x16, waiting for transfers between devices: 9.73 us -> 26.5 us  [swap(): lax.ppermute(value, plane, device_pairs(n_line, lambda z, x, c: (z, x ^ s...]
    ppermute x16, waiting for transfers between devices: 40.5 us -> 25.1 us  [turn(): lax.ppermute(value, plane, device_pairs(n_line, lambda z, x, c: ((z + by)...]
    ppermute x16, starting transfers between devices: 11.5 us -> 9.53 us  [swap(): lax.ppermute(value, plane, device_pairs(n_line, lambda z, x, c: (z, x ^ s...]
  transfers between devices with their start and end apart: 32 -> 32, of which waited for: 15 -> 15; matrix products, arithmetic and copies ran while one was open for 0% -> 0% of each run, Pallas kernels for 15% -> 14%
where the time goes in v13:
time: 115 us
  waiting for transfers between devices  51.6 us (45%)
  starting transfers between devices  37.6 us (33%)
  Pallas kernels  22.7 us (20%)
  local copies, waits for them, and re-layouts  2.39 us (2%)
    ppermute x16, starting transfers between devices, turn(): lax.ppermute(value, plane, device_pairs(n_line, lambda z, x, c: ((z + by)...  28.1 us
    ppermute x16, waiting for transfers between devices, swap(): lax.ppermute(value, plane, device_pairs(n_line, lambda z, x, c: (z, x ^ s...  26.5 us
    ppermute x16, waiting for transfers between devices, turn(): lax.ppermute(value, plane, device_pairs(n_line, lambda z, x, c: ((z + by)...  25.1 us
    pallas_call x15, Pallas kernels, run(): pl.pallas_call(body, out_shape=outs, in_specs=[pl.BlockSpec(memory_space=...  22.7 us
    ppermute x16, starting transfers between devices, swap(): lax.ppermute(value, plane, device_pairs(n_line, lambda z, x, c: (z, x ^ s...  9.53 us
  transfers between devices with their start and end apart: 32, of which 15 were waited for; matrix products, arithmetic and copies ran while one was open for 0% of the time, Pallas kernels for 14%

profile of v13, /device:TPU:0, one launch (start us, length us, event | category | flops | bytes accessed | tf_op | source)
XLA Modules:
  0.0 115.2 jit_solution(16236262220006203816)
XLA Ops:
  0.8 2.0 %columns.1 = (bf16[128,512]{1,0:T(8,128)(2,1)S(1)}, bf16[128,512]{1,0:T(8,128)(2,1)S(1)}, bf16[2,128,512]{2,1,0:T(8,128)(2,1)S(1)}, bf16[2,512,512]{2,1,0:T(8,128)(2,1)S(1)}) custom-call(s32[7]{0:T(128)S(1)} %stack.33.place, bf16[128,2048]{1,0:T(8,128)(2,1)} %tokens.1, bf16[1,512,512]{2,1,0:T(8,128)(2,1)} %expert_in.1, bf16[1,512,512]{2,1,0:T(8,128)(2,1)} %expert_out.1), custom_call_target="tpu_custom_call" | custom-call | tf_op jit(solution)/shard_map/columns/pallas_call | solution.py:45
  3.3 2.6 %collective-permute-start = (bf16[2,128,512]{2,1,0:T(8,128)(2,1)S(1)}, bf16[2,128,512]{2,1,0:T(8,128)(2,1)S(1)}, u32[]{:S(2)}, u32[]{:S(2)}) collective-permute-start(bf16[2,128,512]{2,1,0:T(8,128)(2,1)S(1)} %get-tuple-element.62), channel_id=1, source_target_pairs={{0,2},{1,3},{2,0},{3,1},{4,6},{5,7},{6,4},{7,5},{8,10},{9,11},{10,... | collective-permute-start | bytes 786440 | tf_op jit(solution)/shard_map/ppermute | solution.py:33
  5.8 1.6 %collective-permute-start.4 = (bf16[128,512]{1,0:T(8,128)(2,1)}, bf16[128,512]{1,0:T(8,128)(2,1)S(1)}, u32[]{:S(2)}, u32[]{:S(2)}) collective-permute-start(bf16[128,512]{1,0:T(8,128)(2,1)} %refs_4_.1), channel_id=1, source_target_pairs={{0,4},{1,5},{2,6},{3,7},{4,8},{5,9},{6,10},{7,11},{8,12},{9,13},{1... | collective-permute-start | bytes 393224 | tf_op jit(solution)/shard_map/ppermute | solution.py:29
  7.4 2.6 %collective-permute-start.5 = (bf16[128,512]{1,0:T(8,128)(2,1)}, bf16[128,512]{1,0:T(8,128)(2,1)S(1)}, u32[]{:S(2)}, u32[]{:S(2)}) collective-permute-start(bf16[128,512]{1,0:T(8,128)(2,1)} %refs_4_.1), channel_id=1, source_target_pairs={{0,8},{1,9},{2,10},{3,11},{4,12},{5,13},{6,14},{7,15},{8,0},{9,1},... | collective-permute-start | bytes 393224 | tf_op jit(solution)/shard_map/ppermute | solution.py:29
  16.2 3.0 %collective-permute-done.5.refs_6_ = bf16[128,512]{1,0:T(8,128)(2,1)S(1)} collective-permute-done((bf16[128,512]{1,0:T(8,128)(2,1)}, bf16[128,512]{1,0:T(8,128)(2,1)S(1)}, u32[]{:S(2)}, u32[]{:S(2)}) %collective-permute-start.5) | collective-permute-done | bytes 131104 | tf_op jit(solution)/shard_map/ppermute | solution.py:29
  20.9 3.3 %collective-permute-start.10 = (bf16[144,512]{1,0:T(8,128)(2,1)S(1)}, bf16[144,512]{1,0:T(8,128)(2,1)S(1)}, u32[]{:S(2)}, u32[]{:S(2)}) collective-permute-start(bf16[144,512]{1,0:T(8,128)(2,1)S(1)} %payload.1.refs_7_), channel_id=1, source_target_pairs={{0,4},{1,5},{2,6},{3,7},{4,8},{5,9},{6,10},{7,11},{8,12},{9,13},{1... | collective-permute-start | bytes 442376 | tf_op jit(solution)/shard_map/ppermute | solution.py:29
  24.2 1.6 %collective-permute-start.11 = (bf16[144,512]{1,0:T(8,128)(2,1)S(1)}, bf16[144,512]{1,0:T(8,128)(2,1)S(1)}, u32[]{:S(2)}, u32[]{:S(2)}) collective-permute-start(bf16[144,512]{1,0:T(8,128)(2,1)S(1)} %payload.1.refs_7_), channel_id=1, source_target_pairs={{0,8},{1,9},{2,10},{3,11},{4,12},{5,13},{6,14},{7,15},{8,0},{9,1},... | collective-permute-start | bytes 442376 | tf_op jit(solution)/shard_map/ppermute | solution.py:29
  27.2 1.6 %collective-permute-start.8 = (bf16[128,512]{1,0:T(8,128)(2,1)S(1)}, bf16[128,512]{1,0:T(8,128)(2,1)S(1)}, u32[]{:S(2)}, u32[]{:S(2)}) collective-permute-start(bf16[128,512]{1,0:T(8,128)(2,1)S(1)} %get-tuple-element.69), channel_id=1, source_target_pairs={{0,2},{1,3},{2,0},{3,1},{4,6},{5,7},{6,4},{7,5},{8,10},{9,11},{10,... | collective-permute-start | bytes 393224 | tf_op jit(solution)/shard_map/ppermute | solution.py:33
  30.0 5.9 %collective-permute-done.11.refs_5_ = bf16[144,512]{1,0:T(8,128)(2,1)S(1)} collective-permute-done((bf16[144,512]{1,0:T(8,128)(2,1)S(1)}, bf16[144,512]{1,0:T(8,128)(2,1)S(1)}, u32[]{:S(2)}, u32[]{:S(2)}) %collective-permute-start.11) | collective-permute-done | bytes 147488 | tf_op jit(solution)/shard_map/ppermute | solution.py:29
  35.8 1.6 %collective-permute-done.8.refs_1_ = bf16[128,512]{1,0:T(8,128)(2,1)S(1)} collective-permute-done((bf16[128,512]{1,0:T(8,128)(2,1)S(1)}, bf16[128,512]{1,0:T(8,128)(2,1)S(1)}, u32[]{:S(2)}, u32[]{:S(2)}) %collective-permute-start.8) | collective-permute-done | bytes 131104 | tf_op jit(solution)/shard_map/ppermute | solution.py:33
  38.6 3.3 %collective-permute-start.13 = (bf16[128,512]{1,0:T(8,128)(2,1)S(1)}, bf16[128,512]{1,0:T(8,128)(2,1)S(1)}, u32[]{:S(2)}, u32[]{:S(2)}) collective-permute-start(bf16[128,512]{1,0:T(8,128)(2,1)S(1)} %latent.1.refs_3_), channel_id=1, source_target_pairs={{0,4},{1,5},{2,6},{3,7},{4,8},{5,9},{6,10},{7,11},{8,12},{9,13},{1... | collective-permute-start | bytes 393224 | tf_op jit(solution)/shard_map/ppermute | solution.py:29
  41.9 1.6 %collective-permute-start.14 = (bf16[128,512]{1,0:T(8,128)(2,1)S(1)}, bf16[128,512]{1,0:T(8,128)(2,1)S(1)}, u32[]{:S(2)}, u32[]{:S(2)}) collective-permute-start(bf16[128,512]{1,0:T(8,128)(2,1)S(1)} %latent.1.refs_3_), channel_id=1, source_target_pairs={{0,8},{1,9},{2,10},{3,11},{4,12},{5,13},{6,14},{7,15},{8,0},{9,1},... | collective-permute-start | bytes 393224 | tf_op jit(solution)/shard_map/ppermute | solution.py:29
  44.3 3.2 %collective-permute-done.13.refs_0_ = bf16[128,512]{1,0:T(8,128)(2,1)S(1)} collective-permute-done((bf16[128,512]{1,0:T(8,128)(2,1)S(1)}, bf16[128,512]{1,0:T(8,128)(2,1)S(1)}, u32[]{:S(2)}, u32[]{:S(2)}) %collective-permute-start.13) | collective-permute-done | bytes 131104 | tf_op jit(solution)/shard_map/ppermute | solution.py:29
  47.5 4.1 %collective-permute-done.16.refs_11_ = bf16[512,512]{1,0:T(8,128)(2,1)S(1)} collective-permute-done((bf16[512,512]{1,0:T(8,128)(2,1)S(1)}, bf16[512,512]{1,0:T(8,128)(2,1)S(1)}, u32[]{:S(2)}, u32[]{:S(2)}) %collective-permute-start.16) | collective-permute-done | bytes 524320 | tf_op jit(solution)/shard_map/ppermute | solution.py:33
  53.5 6.1 %experts.1 = (bf16[128,512]{1,0:T(8,128)(2,1)S(1)}, bf16[128,512]{1,0:T(8,128)(2,1)S(1)}, bf16[128,512]{1,0:T(8,128)(2,1)S(1)}, bf16[128,512]{1,0:T(8,128)(2,1)S...) custom-call(s32[7]{0:T(128)S(1)} %stack.33.place, ...), custom_call_target="tpu_custom_call" | custom-call | tf_op jit(solution)/shard_map/experts/pallas_call | solution.py:45
  59.6 4.4 %collective-permute-start.19 = (bf16[128,512]{1,0:T(8,128)(2,1)S(1)}, bf16[128,512]{1,0:T(8,128)(2,1)S(1)}, u32[]{:S(2)}, u32[]{:S(2)}) collective-permute-start(bf16[128,512]{1,0:T(8,128)(2,1)S(1)} %get-tuple-element.78), channel_id=1, source_target_pairs={{0,12},{1,13},{2,14},{3,15},{4,0},{5,1},{6,2},{7,3},{8,4},{9,5},{1... | collective-permute-start | bytes 393224 | tf_op jit(solution)/shard_map/ppermute | solution.py:29
  68.0 2.9 %weight_grads.1 = (f32[2,512,512]{2,1,0:T(8,128)S(1)}, f32[2,512,512]{2,1,0:T(8,128)S(1)}, bf16[4,512,512]{2,1,0:T(8,128)(2,1)S(1)}) custom-call(s32[7]{0:T(128)S(1)} %stack.33.place, bf16[128,512]{1,0:T(8,128)(2,1)S(1)} %collective-permute-done.13.refs_0_, bf16[128,512]{1,0:T(8,128)(2,1)S(1)} %collective-permute-done.14.refs_1_, ...), custom_call_target="tpu_custom_call" | custom-call | tf_op jit(solution)/shard_map/weight_grads/pallas_call | solution.py:45
  70.9 5.4 %collective-permute-done.21.refs_2_ = bf16[128,512]{1,0:T(8,128)(2,1)S(1)} collective-permute-done((bf16[128,512]{1,0:T(8,128)(2,1)S(1)}, bf16[128,512]{1,0:T(8,128)(2,1)S(1)}, u32[]{:S(2)}, u32[]{:S(2)}) %collective-permute-start.21) | collective-permute-done | bytes 131104 | tf_op jit(solution)/shard_map/ppermute | solution.py:29
  78.3 4.7 %collective-permute-done.25.refs_5_ = bf16[128,512]{1,0:T(8,128)(2,1)S(1)} collective-permute-done((bf16[128,512]{1,0:T(8,128)(2,1)S(1)}, bf16[128,512]{1,0:T(8,128)(2,1)S(1)}, u32[]{:S(2)}, u32[]{:S(2)}) %collective-permute-start.25) | collective-permute-done | bytes 131104 | tf_op jit(solution)/shard_map/ppermute | solution.py:29
  87.4 1.8 %collective-permute-start.29 = (bf16[2,128,512]{2,1,0:T(8,128)(2,1)S(1)}, bf16[2,128,512]{2,1,0:T(8,128)(2,1)S(1)}, u32[]{:S(2)}, u32[]{:S(2)}) collective-permute-start(bf16[2,128,512]{2,1,0:T(8,128)(2,1)S(1)} %get-tuple-element.106), channel_id=1, source_target_pairs={{0,8},{1,9},{2,10},{3,11},{4,12},{5,13},{6,14},{7,15},{8,0},{9,1},... | collective-permute-start | bytes 786440 | tf_op jit(solution)/shard_map/ppermute | solution.py:29
  90.4 2.6 %collective-permute-start.28 = (bf16[128,512]{1,0:T(8,128)(2,1)S(1)}, bf16[128,512]{1,0:T(8,128)(2,1)S(1)}, u32[]{:S(2)}, u32[]{:S(2)}) collective-permute-start(bf16[128,512]{1,0:T(8,128)(2,1)S(1)} %get-tuple-element.101), channel_id=1, source_target_pairs={{0,12},{1,13},{2,14},{3,15},{4,0},{5,1},{6,2},{7,3},{8,4},{9,5},{1... | collective-permute-start | bytes 393224 | tf_op jit(solution)/shard_map/ppermute | solution.py:29
  93.0 17.1 %collective-permute-done.31.far = bf16[2,512,512]{2,1,0:T(8,128)(2,1)S(1)} collective-permute-done((bf16[2,512,512]{2,1,0:T(8,128)(2,1)S(1)}, bf16[2,512,512]{2,1,0:T(8,128)(2,1)S(1)}, u32[]{:S(2)}, u32[]{:S(2)}) %collective-permute-start.31) | collective-permute-done | bytes 1048608 | tf_op jit(solution)/shard_map/ppermute | solution.py:33
  110.0 1.6 %near_grads.1 = (bf16[1,512,512]{2,1,0:T(8,128)(2,1)}, bf16[1,512,512]{2,1,0:T(8,128)(2,1)}) custom-call(s32[7]{0:T(128)S(1)} %stack.33.place, f32[2,512,512]{2,1,0:T(8,128)S(1)} %get-tuple-element.111.near, bf16[2,512,512]{2,1,0:T(8,128)(2,1)S(1)} %collective-permute-done.31.far), custom_call_target="tpu_custom_call" | custom-call | tf_op jit(solution)/shard_map/near_grads/pallas_call | solution.py:45
  111.7 2.2 %token_grad.1 = bf16[128,2048]{1,0:T(8,128)(2,1)} custom-call(s32[7]{0:T(128)S(1)} %stack.33.place, bf16[128,512]{1,0:T(8,128)(2,1)S(1)} %latent_delta.1.first.refs_4_.delta, bf16[2,512,512]{2,1,0:T(8,128)(2,1)S(1)} %stack.34.downs, bf16[2,512,512]{2,1,0:T(8,128)(2,1)S(1)} %collective-permute-done.27.core_downs), custom_call_target="tpu_custom_call" | custom-call | tf_op jit(solution)/shard_map/token_grad/pallas_call | solution.py:45
  (69 shorter events, 27.7 us)
Async XLA Ops:
  2.7 10.1 %collective-permute-start.1 = (bf16[2,512,512]{2,1,0:T(8,128)(2,1)S(1)}, bf16[2,512,512]{2,1,0:T(8,128)(2,1)S(1)}, u32[]{:S(2)}, u32[]{:S(2)}) collective-permute-start(bf16[2,512,512]{2,1,0:T(8,128)(2,1)S(1)} %get-tuple-element.64.refs_8_), channel_id=1, source_target_pairs={{0,1},{1,0},{2,3},{3,2},{4,5},{5,4},{6,7},{7,6},{8,9},{9,8},{10,11... | collective-permute-start | bytes 3145736 | tf_op jit(solution)/shard_map/ppermute | solution.py:33
  3.3 9.5 %collective-permute-start = (bf16[2,128,512]{2,1,0:T(8,128)(2,1)S(1)}, bf16[2,128,512]{2,1,0:T(8,128)(2,1)S(1)}, u32[]{:S(2)}, u32[]{:S(2)}) collective-permute-start(bf16[2,128,512]{2,1,0:T(8,128)(2,1)S(1)} %get-tuple-element.62), channel_id=1, source_target_pairs={{0,2},{1,3},{2,0},{3,1},{4,6},{5,7},{6,4},{7,5},{8,10},{9,11},{10,... | collective-permute-start | bytes 786440 | tf_op jit(solution)/shard_map/ppermute | solution.py:33
  5.8 10.3 %collective-permute-start.4 = (bf16[128,512]{1,0:T(8,128)(2,1)}, bf16[128,512]{1,0:T(8,128)(2,1)S(1)}, u32[]{:S(2)}, u32[]{:S(2)}) collective-permute-start(bf16[128,512]{1,0:T(8,128)(2,1)} %refs_4_.1), channel_id=1, source_target_pairs={{0,4},{1,5},{2,6},{3,7},{4,8},{5,9},{6,10},{7,11},{8,12},{9,13},{1... | collective-permute-start | bytes 393224 | tf_op jit(solution)/shard_map/ppermute | solution.py:29
  7.4 11.8 %collective-permute-start.5 = (bf16[128,512]{1,0:T(8,128)(2,1)}, bf16[128,512]{1,0:T(8,128)(2,1)S(1)}, u32[]{:S(2)}, u32[]{:S(2)}) collective-permute-start(bf16[128,512]{1,0:T(8,128)(2,1)} %refs_4_.1), channel_id=1, source_target_pairs={{0,8},{1,9},{2,10},{3,11},{4,12},{5,13},{6,14},{7,15},{8,0},{9,1},... | collective-permute-start | bytes 393224 | tf_op jit(solution)/shard_map/ppermute | solution.py:29
  10.0 9.2 %collective-permute-start.6 = (bf16[128,512]{1,0:T(8,128)(2,1)}, bf16[128,512]{1,0:T(8,128)(2,1)S(1)}, u32[]{:S(2)}, u32[]{:S(2)}) collective-permute-start(bf16[128,512]{1,0:T(8,128)(2,1)} %refs_4_.1), channel_id=1, source_target_pairs={{0,12},{1,13},{2,14},{3,15},{4,0},{5,1},{6,2},{7,3},{8,4},{9,5},{1... | collective-permute-start | bytes 393224 | tf_op jit(solution)/shard_map/ppermute | solution.py:29
  20.3 15.5 %collective-permute-start.9 = (bf16[512,512]{1,0:T(8,128)(2,1)S(1)}, bf16[512,512]{1,0:T(8,128)(2,1)S(1)}, u32[]{:S(2)}, u32[]{:S(2)}) collective-permute-start(bf16[512,512]{1,0:T(8,128)(2,1)S(1)} %bitcast.15), channel_id=1, source_target_pairs={{0,2},{1,3},{2,0},{3,1},{4,6},{5,7},{6,4},{7,5},{8,10},{9,11},{10,... | collective-permute-start | bytes 1572872 | tf_op jit(solution)/shard_map/ppermute | solution.py:33
  20.9 9.1 %collective-permute-start.10 = (bf16[144,512]{1,0:T(8,128)(2,1)S(1)}, bf16[144,512]{1,0:T(8,128)(2,1)S(1)}, u32[]{:S(2)}, u32[]{:S(2)}) collective-permute-start(bf16[144,512]{1,0:T(8,128)(2,1)S(1)} %payload.1.refs_7_), channel_id=1, source_target_pairs={{0,4},{1,5},{2,6},{3,7},{4,8},{5,9},{6,10},{7,11},{8,12},{9,13},{1... | collective-permute-start | bytes 442376 | tf_op jit(solution)/shard_map/ppermute | solution.py:29
  24.2 11.7 %collective-permute-start.11 = (bf16[144,512]{1,0:T(8,128)(2,1)S(1)}, bf16[144,512]{1,0:T(8,128)(2,1)S(1)}, u32[]{:S(2)}, u32[]{:S(2)}) collective-permute-start(bf16[144,512]{1,0:T(8,128)(2,1)S(1)} %payload.1.refs_7_), channel_id=1, source_target_pairs={{0,8},{1,9},{2,10},{3,11},{4,12},{5,13},{6,14},{7,15},{8,0},{9,1},... | collective-permute-start | bytes 442376 | tf_op jit(solution)/shard_map/ppermute | solution.py:29
  25.8 10.0 %collective-permute-start.12 = (bf16[144,512]{1,0:T(8,128)(2,1)S(1)}, bf16[144,512]{1,0:T(8,128)(2,1)S(1)}, u32[]{:S(2)}, u32[]{:S(2)}) collective-permute-start(bf16[144,512]{1,0:T(8,128)(2,1)S(1)} %payload.1.refs_7_), channel_id=1, source_target_pairs={{0,12},{1,13},{2,14},{3,15},{4,0},{5,1},{6,2},{7,3},{8,4},{9,5},{1... | collective-permute-start | bytes 442376 | tf_op jit(solution)/shard_map/ppermute | solution.py:29
  27.2 10.3 %collective-permute-start.8 = (bf16[128,512]{1,0:T(8,128)(2,1)S(1)}, bf16[128,512]{1,0:T(8,128)(2,1)S(1)}, u32[]{:S(2)}, u32[]{:S(2)}) collective-permute-start(bf16[128,512]{1,0:T(8,128)(2,1)S(1)} %get-tuple-element.69), channel_id=1, source_target_pairs={{0,2},{1,3},{2,0},{3,1},{4,6},{5,7},{6,4},{7,5},{8,10},{9,11},{10,... | collective-permute-start | bytes 393224 | tf_op jit(solution)/shard_map/ppermute | solution.py:33
  38.0 13.5 %collective-permute-start.16 = (bf16[512,512]{1,0:T(8,128)(2,1)S(1)}, bf16[512,512]{1,0:T(8,128)(2,1)S(1)}, u32[]{:S(2)}, u32[]{:S(2)}) collective-permute-start(bf16[512,512]{1,0:T(8,128)(2,1)S(1)} %bitcast.16), channel_id=1, source_target_pairs={{0,2},{1,3},{2,0},{3,1},{4,6},{5,7},{6,4},{7,5},{8,10},{9,11},{10,... | collective-permute-start | bytes 1572872 | tf_op jit(solution)/shard_map/ppermute | solution.py:33
  38.6 8.8 %collective-permute-start.13 = (bf16[128,512]{1,0:T(8,128)(2,1)S(1)}, bf16[128,512]{1,0:T(8,128)(2,1)S(1)}, u32[]{:S(2)}, u32[]{:S(2)}) collective-permute-start(bf16[128,512]{1,0:T(8,128)(2,1)S(1)} %latent.1.refs_3_), channel_id=1, source_target_pairs={{0,4},{1,5},{2,6},{3,7},{4,8},{5,9},{6,10},{7,11},{8,12},{9,13},{1... | collective-permute-start | bytes 393224 | tf_op jit(solution)/shard_map/ppermute | solution.py:29
  41.9 9.8 %collective-permute-start.14 = (bf16[128,512]{1,0:T(8,128)(2,1)S(1)}, bf16[128,512]{1,0:T(8,128)(2,1)S(1)}, u32[]{:S(2)}, u32[]{:S(2)}) collective-permute-start(bf16[128,512]{1,0:T(8,128)(2,1)S(1)} %latent.1.refs_3_), channel_id=1, source_target_pairs={{0,8},{1,9},{2,10},{3,11},{4,12},{5,13},{6,14},{7,15},{8,0},{9,1},... | collective-permute-start | bytes 393224 | tf_op jit(solution)/shard_map/ppermute | solution.py:29
  43.6 8.2 %collective-permute-start.15 = (bf16[128,512]{1,0:T(8,128)(2,1)S(1)}, bf16[128,512]{1,0:T(8,128)(2,1)S(1)}, u32[]{:S(2)}, u32[]{:S(2)}) collective-permute-start(bf16[128,512]{1,0:T(8,128)(2,1)S(1)} %latent.1.refs_3_), channel_id=1, source_target_pairs={{0,12},{1,13},{2,14},{3,15},{4,0},{5,1},{6,2},{7,3},{8,4},{9,5},{1... | collective-permute-start | bytes 393224 | tf_op jit(solution)/shard_map/ppermute | solution.py:29
  44.3 9.0 %collective-permute-start.17 = (bf16[512,512]{1,0:T(8,128)(2,1)S(1)}, bf16[512,512]{1,0:T(8,128)(2,1)S(1)}, u32[]{:S(2)}, u32[]{:S(2)}) collective-permute-start(bf16[512,512]{1,0:T(8,128)(2,1)S(1)} %collective-permute-done.9.refs_10_), channel_id=1, source_target_pairs={{0,1},{1,0},{2,3},{3,2},{4,5},{5,4},{6,7},{7,6},{8,9},{9,8},{10,11... | collective-permute-start | bytes 1572872 | tf_op jit(solution)/shard_map/ppermute | solution.py:33
  51.8 14.2 %collective-permute-start.20 = (bf16[512,512]{1,0:T(8,128)(2,1)S(1)}, bf16[512,512]{1,0:T(8,128)(2,1)S(1)}, u32[]{:S(2)}, u32[]{:S(2)}) collective-permute-start(bf16[512,512]{1,0:T(8,128)(2,1)S(1)} %get-tuple-element.85.first), channel_id=1, source_target_pairs={{0,2},{1,3},{2,0},{3,1},{4,6},{5,7},{6,4},{7,5},{8,10},{9,11},{10,... | collective-permute-start | bytes 1572872 | tf_op jit(solution)/shard_map/ppermute | solution.py:33
  59.6 8.3 %collective-permute-start.19 = (bf16[128,512]{1,0:T(8,128)(2,1)S(1)}, bf16[128,512]{1,0:T(8,128)(2,1)S(1)}, u32[]{:S(2)}, u32[]{:S(2)}) collective-permute-start(bf16[128,512]{1,0:T(8,128)(2,1)S(1)} %get-tuple-element.78), channel_id=1, source_target_pairs={{0,12},{1,13},{2,14},{3,15},{4,0},{5,1},{6,2},{7,3},{8,4},{9,5},{1... | collective-permute-start | bytes 393224 | tf_op jit(solution)/shard_map/ppermute | solution.py:29
  64.0 12.3 %collective-permute-start.21 = (bf16[128,512]{1,0:T(8,128)(2,1)S(1)}, bf16[128,512]{1,0:T(8,128)(2,1)S(1)}, u32[]{:S(2)}, u32[]{:S(2)}) collective-permute-start(bf16[128,512]{1,0:T(8,128)(2,1)S(1)} %get-tuple-element.88), channel_id=1, source_target_pairs={{0,8},{1,9},{2,10},{3,11},{4,12},{5,13},{6,14},{7,15},{8,0},{9,1},... | collective-permute-start | bytes 393224 | tf_op jit(solution)/shard_map/ppermute | solution.py:29
  64.4 11.9 %collective-permute-start.22 = (bf16[128,512]{1,0:T(8,128)(2,1)S(1)}, bf16[128,512]{1,0:T(8,128)(2,1)S(1)}, u32[]{:S(2)}, u32[]{:S(2)}) collective-permute-start(bf16[128,512]{1,0:T(8,128)(2,1)S(1)} %get-tuple-element.90), channel_id=1, source_target_pairs={{0,4},{1,5},{2,6},{3,7},{4,8},{5,9},{6,10},{7,11},{8,12},{9,13},{1... | collective-permute-start | bytes 393224 | tf_op jit(solution)/shard_map/ppermute | solution.py:29
  84.5 25.6 %collective-permute-start.31 = (bf16[2,512,512]{2,1,0:T(8,128)(2,1)S(1)}, bf16[2,512,512]{2,1,0:T(8,128)(2,1)S(1)}, u32[]{:S(2)}, u32[]{:S(2)}) collective-permute-start(bf16[2,512,512]{2,1,0:T(8,128)(2,1)S(1)} %get-tuple-element.112), channel_id=1, source_target_pairs={{0,2},{1,3},{2,0},{3,1},{4,6},{5,7},{6,4},{7,5},{8,10},{9,11},{10,... | collective-permute-start | bytes 3145736 | tf_op jit(solution)/shard_map/ppermute | solution.py:33
  87.2 24.5 %collective-permute-start.27 = (bf16[2,512,512]{2,1,0:T(8,128)(2,1)S(1)}, bf16[2,512,512]{2,1,0:T(8,128)(2,1)S(1)}, u32[]{:S(2)}, u32[]{:S(2)}) collective-permute-start(bf16[2,512,512]{2,1,0:T(8,128)(2,1)S(1)} %stack.34.downs), channel_id=1, source_target_pairs={{0,1},{1,0},{2,3},{3,2},{4,5},{5,4},{6,7},{7,6},{8,9},{9,8},{10,11... | collective-permute-start | bytes 3145736 | tf_op jit(solution)/shard_map/ppermute | solution.py:33
  87.4 26.5 %collective-permute-start.29 = (bf16[2,128,512]{2,1,0:T(8,128)(2,1)S(1)}, bf16[2,128,512]{2,1,0:T(8,128)(2,1)S(1)}, u32[]{:S(2)}, u32[]{:S(2)}) collective-permute-start(bf16[2,128,512]{2,1,0:T(8,128)(2,1)S(1)} %get-tuple-element.106), channel_id=1, source_target_pairs={{0,8},{1,9},{2,10},{3,11},{4,12},{5,13},{6,14},{7,15},{8,0},{9,1},... | collective-permute-start | bytes 786440 | tf_op jit(solution)/shard_map/ppermute | solution.py:29
  89.2 24.7 %collective-permute-start.30 = (bf16[2,128,512]{2,1,0:T(8,128)(2,1)S(1)}, bf16[2,128,512]{2,1,0:T(8,128)(2,1)S(1)}, u32[]{:S(2)}, u32[]{:S(2)}) collective-permute-start(bf16[2,128,512]{2,1,0:T(8,128)(2,1)S(1)} %get-tuple-element.107), channel_id=1, source_target_pairs={{0,4},{1,5},{2,6},{3,7},{4,8},{5,9},{6,10},{7,11},{8,12},{9,13},{1... | collective-permute-start | bytes 786440 | tf_op jit(solution)/shard_map/ppermute | solution.py:29
  90.4 23.5 %collective-permute-start.28 = (bf16[128,512]{1,0:T(8,128)(2,1)S(1)}, bf16[128,512]{1,0:T(8,128)(2,1)S(1)}, u32[]{:S(2)}, u32[]{:S(2)}) collective-permute-start(bf16[128,512]{1,0:T(8,128)(2,1)S(1)} %get-tuple-element.101), channel_id=1, source_target_pairs={{0,12},{1,13},{2,14},{3,15},{4,0},{5,1},{6,2},{7,3},{8,4},{9,5},{1... | collective-permute-start | bytes 393224 | tf_op jit(solution)/shard_map/ppermute | solution.py:29
  (14 other events, 118.4 us)

commit v14 on v13

--- a/solution.py
+++ b/solution.py
@@ -37,7 +37,7 @@
     return lax.optimization_barrier((value,) + earlier)[0]
 
 
-def call(body, outs, name, scratch=(), outside=0):
+def call(body, outs, name, scratch=(), outside=0, flops=0):
     vmem = pl.BlockSpec(memory_space=pltpu.VMEM)
     outer = pl.BlockSpec(memory_space=pltpu.HBM)
 
@@ -51,7 +51,7 @@
             out_specs=[vmem] * len(outs),
             scratch_shapes=list(scratch),
             compiler_params=pltpu.CompilerParams(vmem_limit_bytes=40 * 1024 * 1024),
-            cost_estimate=pl.CostEstimate(flops=0, bytes_accessed=0, transcendentals=0),
+            cost_estimate=pl.CostEstimate(flops=flops, bytes_accessed=0, transcendentals=0),
             name=name,
         )(place, *operands)
 
@@ -95,19 +95,26 @@
     other[...] = (keep[1] + arrived[1]).astype(narrow)
 
 
-def core_sum_body(place, near, far, arrived, near_out, far_out):
-    far_out[...] = (far[...] + arrived[2:].astype(wide)).astype(narrow)
-    near_out[...] = near[...] + arrived[:2].astype(wide)
-
-
-def near_body(place, near, far, grad_in, grad_out):
-    for i, out in enumerate((grad_in, grad_out)):
-        out[0] = (near[i] + far[i].astype(wide)).astype(narrow)
-
-
-def last_body(riding, place, *refs):
-    n_line = (len(refs) - 2 + len(riding)) // 2
-    blocks, pieces, grad_down, combined = refs[:n_line], list(refs[n_line:-2]), refs[-2], refs[-1]
+def far_body(place, far, arrived, first, rest):
+    split, width = first.shape[0], far.shape[1]
+    total = [far[i] + arrived[i].astype(wide) for i in range(2)]
+    first[...] = total[0][:split].astype(narrow)
+    rest[: width - split] = total[0][split:].astype(narrow)
+    rest[width - split :] = total[1].astype(narrow)
+
+
+def pack_body(place, grads, down, side_down, out):
+    out[:2] = grads[...]
+    out[2], out[3] = down[...], side_down[...]
+
+
+def last_body(riding, n_line, place, near, others, first, rest, *refs):
+    blocks, pieces = refs[:n_line], list(refs[n_line:-4])
+    grad_down, combined, *grads = refs[-4:]
+    split = grads[0].shape[1] - first.shape[0]
+    far = (jnp.concatenate([first[...], rest[:split]], axis=0), rest[split:])
+    for i, out in enumerate(grads):
+        out[0] = (near[i] + others[i].astype(wide) + far[i].astype(wide)).astype(narrow)
     total = blocks[0][...]
     out_total = pieces.pop(0)[...]
     for back in range(1, n_line):
@@ -198,7 +205,7 @@
 def weight_grad_body(n_rows, n_sets, place, *refs):
     rows_in = refs[:n_rows]
     sets = [refs[n_rows + 3 * i : n_rows + 3 * i + 3] for i in range(n_sets)]
-    near, far, other = refs[n_rows + 3 * n_sets :]
+    near, far, near_other, far_other = refs[n_rows + 3 * n_sets :]
     dot = functools.partial(lax.dot_general, dimension_numbers=contract_first, preferred_element_type=wide)
     rows = jnp.concatenate([r[...] for r in rows_in], axis=0)
     for core in (1, 0):
@@ -207,12 +214,8 @@
                 jnp.concatenate([values[i][core * 2 + side] for values in sets], axis=0) for i in range(3)
             )
             grad_in, grad_out = dot(rows, back_pre), dot(hidden, scaled)
-            if core:
-                other[2 * side] = grad_in.astype(narrow)
-                other[2 * side + 1] = grad_out.astype(narrow)
-            else:
-                own = far if side else near
-                own[0], own[1] = grad_in, grad_out
+            out = ((near, far), (near_other, far_other))[core][side]
+            out[0], out[1] = grad_in.astype(out.dtype), grad_out.astype(out.dtype)
 
 
 def down_grad_body(n_line, place, *refs):
@@ -233,8 +236,8 @@
                 targets[back][...] = part[z * block : (z + 1) * block].astype(targets[back].dtype)
 
 
-def token_grad_body(n_line, block, place, delta, downs, core_downs, out):
-    for i, weight in enumerate((downs.at[0], downs.at[1], core_downs.at[0], core_downs.at[1])):
+def token_grad_body(n_line, block, place, delta, held, arrived, out):
+    for i, weight in enumerate((held.at[2], held.at[3], arrived.at[2], arrived.at[3])):
         owner = (place[1] ^ (i % 2)) * 2 + (place[2] ^ (i // 2))
         part = lax.dot_general(delta[...], weight[...], contract_last, preferred_element_type=wide)
         part = part.astype(narrow)
@@ -298,16 +301,15 @@
         place, half, after(crossed, side_in, *payloads[1:])
     )
     groups = [[*range(1, n_line), 0]]
-    riding = range(2, n_line)
+    riding = (1, n_line - 1)
     rows = [latent] + [turn(latent, n_line, back) for back in range(1, n_line)]
 
     side_out = swap(after(expert_out[0], latent), n_line, 0, 1)
     core_in = swap(after(side_in, latent), n_line, 1, 0)
-    core_out = swap(after(side_out, rows[1]), n_line, 1, 0)
+    core_out = swap(after(side_out, *rows[1:]), n_line, 1, 0)
     weights = [own, core_own, side_in, side_out, core_in, core_out]
     side_down = swap(after(down, *rows[1:]), n_line, 0, 1)
 
-    both_down = stack(down, side_down)
     deltas_of, outs_of, saved = [None] * n_line, [None] * n_line, []
     done = latent
     for group in groups:
@@ -328,26 +330,31 @@
     delta_lines = [home(value, back) for back, value in enumerate(deltas_of)]
 
     pair = (2, latent_width, hidden_width)
-    near, far, other = call(
+    near, far, near_other, far_other = call(
         functools.partial(weight_grad_body, n_line, len(groups)),
-        [shape(pair, wide)] * 2 + [shape((4, latent_width, hidden_width), narrow)],
+        [shape(pair, wide)] * 2 + [shape(pair, narrow)] * 2,
         "weight_grads",
+        flops=2 * 8 * n_line * tok_rows * latent_width * hidden_width,
     )(
-        after(place, delta_lines[1]),
+        place,
         *(rows[i] for group in groups for i in group),
         *(value for values in saved for value in values),
     )
-    delta_lines = [after(line, near, both_down) for line in delta_lines]
+    far_other = swap(after(far_other, side_down), n_line, 1, 0)
+    quarter = latent_width // 2
+    far_first, far_rest = call(
+        far_body, [shape((rows, hidden_width), narrow) for rows in (quarter, 2 * latent_width - quarter)], "far_grads"
+    )(place, far, far_other)
+    far_first = swap(far_first, n_line, 0, 1)
+    delta_lines = [after(line, near) for line in delta_lines]
     (delta,) = call(add_body, [rows_of(narrow)], "latent_delta")(place, *delta_lines)
     side_delta = swap(delta, n_line, 0, 1)
     out_lines = [outs_of[0]] + [home(outs_of[back], back) if back not in riding else None for back in range(1, n_line)]
-    other = swap(after(other, delta), n_line, 1, 0)
-    near, far = call(core_sum_body, [shape(pair, wide), shape(pair, narrow)], "core_sums")(
-        place, near, far, after(other, out_lines[1])
-    )
-    sent = far
-    far = swap(after(far, side_delta), n_line, 0, 1)
-    core_deltas = swap(stack(delta, side_delta, sent), n_line, 1, 0)
+    far_rest = swap(after(far_rest, side_delta), n_line, 0, 1)
+    (others,) = call(pack_body, [shape((4, latent_width, hidden_width), narrow)], "pack")(
+        after(place, delta), near_other, down, side_down
+    )
+    core_deltas = swap(stack(delta, side_delta, others, far_first, *(out_lines[back] for back in range(1, n_line) if back not in riding)), n_line, 1, 0)
     blocks = call(
         functools.partial(down_grad_body, n_line),
         [
@@ -356,17 +363,17 @@
         ],
         "down_grad",
     )(place, columns[0], across, *core_tokens, delta, side_delta, core_deltas, *(outs_of[back] for back in riding))
-    core_down = swap(after(both_down, blocks[1]), n_line, 1, 0)
+    others = [others, swap(after(others, blocks[1]), n_line, 1, 0)]
     (grad_tokens,) = call(
         functools.partial(token_grad_body, n_line, block), [shape((tok_rows, width), narrow)], "token_grad"
-    )(place, after(delta, blocks[1]), both_down, core_down)
+    )(place, after(delta, blocks[1]), *others)
     blocks = [blocks[0]] + [turn(blocks[back], n_line, n_line - back) for back in range(1, n_line)]
-    grad_down, latent_out = call(
-        functools.partial(last_body, riding), [shape((block, latent_width), wide), rows_of(narrow)], "last_sums"
-    )(after(place, grad_tokens), *blocks, *(line for line in out_lines if line is not None))
-    grad_in, grad_out = call(
-        near_body, [shape(expert_in.shape, narrow), shape(expert_out.shape, narrow)], "near_grads"
-    )(place, near, far)
+    grad_down, latent_out, grad_in, grad_out = call(
+        functools.partial(last_body, riding, n_line),
+        [shape((block, latent_width), wide), rows_of(narrow)]
+        + [shape(value.shape, narrow) for value in (expert_in, expert_out)],
+        "last_sums",
+    )(after(place, grad_tokens), near, others[1], far_first, far_rest, *blocks, *(line for line in out_lines if line is not None))
     return (latent_out, grad_tokens, grad_down, grad_in, grad_out)
 
 

time: 115 us -> 118 us (1.026)
  starting transfers between devices: 37.6 us -> 39.9 us
  waiting for transfers between devices: 51.6 us -> 53.3 us
    ppermute x16, waiting for transfers between devices: 25.1 us -> 42.3 us  [turn(): lax.ppermute(value, plane, device_pairs(n_line, lambda z, x, c: ((z + by)...]
    ppermute x16 -> x17, waiting for transfers between devices: 26.5 us -> 11.1 us  [swap(): lax.ppermute(value, plane, device_pairs(n_line, lambda z, x, c: (z, x ^ s...]
    ppermute x16 -> x17, starting transfers between devices: 9.53 us -> 12.9 us  [swap(): lax.ppermute(value, plane, device_pairs(n_line, lambda z, x, c: (z, x ^ s...]
    pallas_call x15 -> x14, Pallas kernels: 22.7 us -> 21.6 us  [run(): pl.pallas_call(body, out_shape=outs, in_specs=[pl.BlockSpec(memory_space=...]
  transfers between devices with their start and end apart: 32 -> 33, of which waited for: 15 -> 13; matrix products, arithmetic and copies ran while one was open for 0% -> 0% of each run, Pallas kernels for 14% -> 12%
where the time goes in v14:
time: 118 us
  waiting for transfers between devices  53.3 us (45%)
  starting transfers between devices  39.9 us (34%)
  Pallas kernels  21.6 us (18%)
  local copies, waits for them, and re-layouts  2.39 us (2%)
    ppermute x16, waiting for transfers between devices, turn(): lax.ppermute(value, plane, device_pairs(n_line, lambda z, x, c: ((z + by)...  42.3 us
    ppermute x16, starting transfers between devices, turn(): lax.ppermute(value, plane, device_pairs(n_line, lambda z, x, c: ((z + by)...  27 us
    pallas_call x14, Pallas kernels, run(): pl.pallas_call(body, out_shape=outs, in_specs=[pl.BlockSpec(memory_space=...  21.6 us
    ppermute x17, starting transfers between devices, swap(): lax.ppermute(value, plane, device_pairs(n_line, lambda z, x, c: (z, x ^ s...  12.9 us
    ppermute x17, waiting for transfers between devices, swap(): lax.ppermute(value, plane, device_pairs(n_line, lambda z, x, c: (z, x ^ s...  11.1 us
  transfers between devices with their start and end apart: 33, of which 13 were waited for; matrix products, arithmetic and copies ran while one was open for 0% of the time, Pallas kernels for 12%

profile of v14, /device:TPU:0, one launch (start us, length us, event | category | flops | bytes accessed | tf_op | source)
XLA Modules:
  0.0 118.1 jit_solution(7765617653637785261)
XLA Ops:
  0.8 2.0 %columns.1 = (bf16[128,512]{1,0:T(8,128)(2,1)S(1)}, bf16[128,512]{1,0:T(8,128)(2,1)S(1)}, bf16[2,128,512]{2,1,0:T(8,128)(2,1)S(1)}, bf16[2,512,512]{2,1,0:T(8,128)(2,1)S(1)}) custom-call(s32[7]{0:T(128)S(1)} %stack.32.place, bf16[128,2048]{1,0:T(8,128)(2,1)} %tokens.1, bf16[1,512,512]{2,1,0:T(8,128)(2,1)} %expert_in.1, bf16[1,512,512]{2,1,0:T(8,128)(2,1)} %expert_out.1), custom_call_target="tpu_custom_call" | custom-call | tf_op jit(solution)/shard_map/columns/pallas_call | solution.py:45
  3.3 2.6 %collective-permute-start = (bf16[2,128,512]{2,1,0:T(8,128)(2,1)S(1)}, bf16[2,128,512]{2,1,0:T(8,128)(2,1)S(1)}, u32[]{:S(2)}, u32[]{:S(2)}) collective-permute-start(bf16[2,128,512]{2,1,0:T(8,128)(2,1)S(1)} %get-tuple-element.62), channel_id=1, source_target_pairs={{0,2},{1,3},{2,0},{3,1},{4,6},{5,7},{6,4},{7,5},{8,10},{9,11},{10,... | collective-permute-start | bytes 786440 | tf_op jit(solution)/shard_map/ppermute | solution.py:33
  5.8 1.6 %collective-permute-start.4 = (bf16[128,512]{1,0:T(8,128)(2,1)}, bf16[128,512]{1,0:T(8,128)(2,1)S(1)}, u32[]{:S(2)}, u32[]{:S(2)}) collective-permute-start(bf16[128,512]{1,0:T(8,128)(2,1)} %refs_4_.1), channel_id=1, source_target_pairs={{0,4},{1,5},{2,6},{3,7},{4,8},{5,9},{6,10},{7,11},{8,12},{9,13},{1... | collective-permute-start | bytes 393224 | tf_op jit(solution)/shard_map/ppermute | solution.py:29
  7.4 2.6 %collective-permute-start.5 = (bf16[128,512]{1,0:T(8,128)(2,1)}, bf16[128,512]{1,0:T(8,128)(2,1)S(1)}, u32[]{:S(2)}, u32[]{:S(2)}) collective-permute-start(bf16[128,512]{1,0:T(8,128)(2,1)} %refs_4_.1), channel_id=1, source_target_pairs={{0,8},{1,9},{2,10},{3,11},{4,12},{5,13},{6,14},{7,15},{8,0},{9,1},... | collective-permute-start | bytes 393224 | tf_op jit(solution)/shard_map/ppermute | solution.py:29
  16.2 3.0 %collective-permute-done.5.refs_6_ = bf16[128,512]{1,0:T(8,128)(2,1)S(1)} collective-permute-done((bf16[128,512]{1,0:T(8,128)(2,1)}, bf16[128,512]{1,0:T(8,128)(2,1)S(1)}, u32[]{:S(2)}, u32[]{:S(2)}) %collective-permute-start.5) | collective-permute-done | bytes 131104 | tf_op jit(solution)/shard_map/ppermute | solution.py:29
  20.9 3.3 %collective-permute-start.10 = (bf16[144,512]{1,0:T(8,128)(2,1)S(1)}, bf16[144,512]{1,0:T(8,128)(2,1)S(1)}, u32[]{:S(2)}, u32[]{:S(2)}) collective-permute-start(bf16[144,512]{1,0:T(8,128)(2,1)S(1)} %payload.1.refs_7_), channel_id=1, source_target_pairs={{0,4},{1,5},{2,6},{3,7},{4,8},{5,9},{6,10},{7,11},{8,12},{9,13},{1... | collective-permute-start | bytes 442376 | tf_op jit(solution)/shard_map/ppermute | solution.py:29
  24.2 1.6 %collective-permute-start.11 = (bf16[144,512]{1,0:T(8,128)(2,1)S(1)}, bf16[144,512]{1,0:T(8,128)(2,1)S(1)}, u32[]{:S(2)}, u32[]{:S(2)}) collective-permute-start(bf16[144,512]{1,0:T(8,128)(2,1)S(1)} %payload.1.refs_7_), channel_id=1, source_target_pairs={{0,8},{1,9},{2,10},{3,11},{4,12},{5,13},{6,14},{7,15},{8,0},{9,1},... | collective-permute-start | bytes 442376 | tf_op jit(solution)/shard_map/ppermute | solution.py:29
  30.0 5.9 %collective-permute-done.11.refs_5_ = bf16[144,512]{1,0:T(8,128)(2,1)S(1)} collective-permute-done((bf16[144,512]{1,0:T(8,128)(2,1)S(1)}, bf16[144,512]{1,0:T(8,128)(2,1)S(1)}, u32[]{:S(2)}, u32[]{:S(2)}) %collective-permute-start.11) | collective-permute-done | bytes 147488 | tf_op jit(solution)/shard_map/ppermute | solution.py:29
  35.9 1.6 %collective-permute-done.8.refs_1_ = bf16[128,512]{1,0:T(8,128)(2,1)S(1)} collective-permute-done((bf16[128,512]{1,0:T(8,128)(2,1)S(1)}, bf16[128,512]{1,0:T(8,128)(2,1)S(1)}, u32[]{:S(2)}, u32[]{:S(2)}) %collective-permute-start.8) | collective-permute-done | bytes 131104 | tf_op jit(solution)/shard_map/ppermute | solution.py:33
  38.6 3.3 %collective-permute-start.13 = (bf16[128,512]{1,0:T(8,128)(2,1)S(1)}, bf16[128,512]{1,0:T(8,128)(2,1)S(1)}, u32[]{:S(2)}, u32[]{:S(2)}) collective-permute-start(bf16[128,512]{1,0:T(8,128)(2,1)S(1)} %latent.1.refs_3_), channel_id=1, source_target_pairs={{0,4},{1,5},{2,6},{3,7},{4,8},{5,9},{6,10},{7,11},{8,12},{9,13},{1... | collective-permute-start | bytes 393224 | tf_op jit(solution)/shard_map/ppermute | solution.py:29
  41.9 1.6 %collective-permute-start.14 = (bf16[128,512]{1,0:T(8,128)(2,1)S(1)}, bf16[128,512]{1,0:T(8,128)(2,1)S(1)}, u32[]{:S(2)}, u32[]{:S(2)}) collective-permute-start(bf16[128,512]{1,0:T(8,128)(2,1)S(1)} %latent.1.refs_3_), channel_id=1, source_target_pairs={{0,8},{1,9},{2,10},{3,11},{4,12},{5,13},{6,14},{7,15},{8,0},{9,1},... | collective-permute-start | bytes 393224 | tf_op jit(solution)/shard_map/ppermute | solution.py:29
  44.3 3.2 %collective-permute-done.13.refs_0_ = bf16[128,512]{1,0:T(8,128)(2,1)S(1)} collective-permute-done((bf16[128,512]{1,0:T(8,128)(2,1)S(1)}, bf16[128,512]{1,0:T(8,128)(2,1)S(1)}, u32[]{:S(2)}, u32[]{:S(2)}) %collective-permute-start.13) | collective-permute-done | bytes 131104 | tf_op jit(solution)/shard_map/ppermute | solution.py:29
  47.5 4.3 %collective-permute-done.14.refs_1_ = bf16[128,512]{1,0:T(8,128)(2,1)S(1)} collective-permute-done((bf16[128,512]{1,0:T(8,128)(2,1)S(1)}, bf16[128,512]{1,0:T(8,128)(2,1)S(1)}, u32[]{:S(2)}, u32[]{:S(2)}) %collective-permute-start.14) | collective-permute-done | bytes 131104 | tf_op jit(solution)/shard_map/ppermute | solution.py:29
  53.7 6.1 %experts.1 = (bf16[128,512]{1,0:T(8,128)(2,1)S(1)}, bf16[128,512]{1,0:T(8,128)(2,1)S(1)}, bf16[128,512]{1,0:T(8,128)(2,1)S(1)}, bf16[128,512]{1,0:T(8,128)(2,1)S...) custom-call(s32[7]{0:T(128)S(1)} %stack.32.place, ...), custom_call_target="tpu_custom_call" | custom-call | tf_op jit(solution)/shard_map/experts/pallas_call | solution.py:45
  59.8 2.9 %weight_grads.1 = (f32[2,512,512]{2,1,0:T(8,128)S(1)}, f32[2,512,512]{2,1,0:T(8,128)S(1)}, bf16[2,512,512]{2,1,0:T(8,128)(2,1)S(1)}, bf16[2,512,512]{2,1,0:T(8,128)(2,1)S(1)}) custom-call(s32[7]{0:T(128)S(1)} %stack.32.place, bf16[128,512]{1,0:T(8,128)(2,1)S(1)} %collective-permute-done.13.refs_0_, bf16[128,512]{1,0:T(8,128)(2,1)S(1)} %collective-permute-done.14.refs_1_, ...), custom_call_target="tpu_custom_call" | custom-call | flops 2147483648 | tf_op jit(solution)/shard_map/weight_grads/pallas_call | solution.py:45
  62.7 3.4 %collective-permute-done.23.side_down = bf16[512,512]{1,0:T(8,128)(2,1)S(1)} collective-permute-done((bf16[512,512]{1,0:T(8,128)(2,1)S(1)}, bf16[512,512]{1,0:T(8,128)(2,1)S(1)}, u32[]{:S(2)}, u32[]{:S(2)}) %collective-permute-start.23) | collective-permute-done | bytes 524320 | tf_op jit(solution)/shard_map/ppermute | solution.py:33
  66.1 4.2 %collective-permute-start.19 = (bf16[128,512]{1,0:T(8,128)(2,1)S(1)}, bf16[128,512]{1,0:T(8,128)(2,1)S(1)}, u32[]{:S(2)}, u32[]{:S(2)}) collective-permute-start(bf16[128,512]{1,0:T(8,128)(2,1)S(1)} %get-tuple-element.83), channel_id=1, source_target_pairs={{0,12},{1,13},{2,14},{3,15},{4,0},{5,1},{6,2},{7,3},{8,4},{9,5},{1... | collective-permute-start | bytes 393224 | tf_op jit(solution)/shard_map/ppermute | solution.py:29
  73.1 2.2 %collective-permute-start.26 = (bf16[128,512]{1,0:T(8,128)(2,1)S(1)}, bf16[128,512]{1,0:T(8,128)(2,1)S(1)}, u32[]{:S(2)}, u32[]{:S(2)}) collective-permute-start(bf16[128,512]{1,0:T(8,128)(2,1)S(1)} %get-tuple-element.97), channel_id=1, source_target_pairs={{0,8},{1,9},{2,10},{3,11},{4,12},{5,13},{6,14},{7,15},{8,0},{9,1},... | collective-permute-start | bytes 393224 | tf_op jit(solution)/shard_map/ppermute | solution.py:29
  75.3 11.0 %collective-permute-done.20.refs_2_ = bf16[128,512]{1,0:T(8,128)(2,1)S(1)} collective-permute-done((bf16[128,512]{1,0:T(8,128)(2,1)S(1)}, bf16[128,512]{1,0:T(8,128)(2,1)S(1)}, u32[]{:S(2)}, u32[]{:S(2)}) %collective-permute-start.20) | collective-permute-done | bytes 131104 | tf_op jit(solution)/shard_map/ppermute | solution.py:29
  89.2 2.8 %collective-permute-done.22.second.refs_5_ = bf16[128,512]{1,0:T(8,128)(2,1)S(1)} collective-permute-done((bf16[128,512]{1,0:T(8,128)(2,1)S(1)}, bf16[128,512]{1,0:T(8,128)(2,1)S(1)}, u32[]{:S(2)}, u32[]{:S(2)}) %collective-permute-start.22) | collective-permute-done | bytes 131104 | tf_op jit(solution)/shard_map/ppermute | solution.py:33
  97.0 2.0 %collective-permute-start.32 = (bf16[2,128,512]{2,1,0:T(8,128)(2,1)S(1)}, bf16[2,128,512]{2,1,0:T(8,128)(2,1)S(1)}, u32[]{:S(2)}, u32[]{:S(2)}) collective-permute-start(bf16[2,128,512]{2,1,0:T(8,128)(2,1)S(1)} %get-tuple-element.109), channel_id=1, source_target_pairs={{0,4},{1,5},{2,6},{3,7},{4,8},{5,9},{6,10},{7,11},{8,12},{9,13},{1... | collective-permute-start | bytes 786440 | tf_op jit(solution)/shard_map/ppermute | solution.py:29
  100.4 2.2 %token_grad.1 = bf16[128,2048]{1,0:T(8,128)(2,1)} custom-call(s32[7]{0:T(128)S(1)} %stack.32.place, bf16[128,512]{1,0:T(8,128)(2,1)S(1)} %latent_delta.1.first.refs_4_.delta, bf16[4,512,512]{2,1,0:T(8,128)(2,1)S(1)} %pack.1.held, bf16[4,512,512]{2,1,0:T(8,128)(2,1)S(1)} %collective-permute-done.28.arrived.others), custom_call_target="tpu_custom_call" | custom-call | tf_op jit(solution)/shard_map/token_grad/pallas_call | solution.py:45
  102.6 13.6 %collective-permute-done.31.refs_2_ = bf16[128,512]{1,0:T(8,128)(2,1)S(1)} collective-permute-done((bf16[128,512]{1,0:T(8,128)(2,1)S(1)}, bf16[128,512]{1,0:T(8,128)(2,1)S(1)}, u32[]{:S(2)}, u32[]{:S(2)}) %collective-permute-start.31) | collective-permute-done | bytes 131104 | tf_op jit(solution)/shard_map/ppermute | solution.py:29
  116.2 1.9 %last_sums.1 = (f32[128,512]{1,0:T(8,128)}, bf16[128,512]{1,0:T(8,128)(2,1)}, bf16[1,512,512]{2,1,0:T(8,128)(2,1)}, bf16[1,512,512]{2,1,0:T(8,128)(2,1)}) custom-call(s32[7]{0:T(128)S(1)} %stack.32.place, f32[2,512,512]{2,1,0:T(8,128)S(1)} %get-tuple-element.81.near, bf16[4,512,512]{2,1,0:T(8,128)(2,1)S(1)} %collective-permute-done.28.arrived.others, ...), custom_call_target="tpu_custom_call" | custom-call | tf_op jit(solution)/shard_map/last_sums/pallas_call | solution.py:45
  (70 shorter events, 28.5 us)
Async XLA Ops:
  2.7 10.1 %collective-permute-start.1 = (bf16[2,512,512]{2,1,0:T(8,128)(2,1)S(1)}, bf16[2,512,512]{2,1,0:T(8,128)(2,1)S(1)}, u32[]{:S(2)}, u32[]{:S(2)}) collective-permute-start(bf16[2,512,512]{2,1,0:T(8,128)(2,1)S(1)} %get-tuple-element.64.refs_8_), channel_id=1, source_target_pairs={{0,1},{1,0},{2,3},{3,2},{4,5},{5,4},{6,7},{7,6},{8,9},{9,8},{10,11... | collective-permute-start | bytes 3145736 | tf_op jit(solution)/shard_map/ppermute | solution.py:33
  3.3 9.5 %collective-permute-start = (bf16[2,128,512]{2,1,0:T(8,128)(2,1)S(1)}, bf16[2,128,512]{2,1,0:T(8,128)(2,1)S(1)}, u32[]{:S(2)}, u32[]{:S(2)}) collective-permute-start(bf16[2,128,512]{2,1,0:T(8,128)(2,1)S(1)} %get-tuple-element.62), channel_id=1, source_target_pairs={{0,2},{1,3},{2,0},{3,1},{4,6},{5,7},{6,4},{7,5},{8,10},{9,11},{10,... | collective-permute-start | bytes 786440 | tf_op jit(solution)/shard_map/ppermute | solution.py:33
  5.8 10.3 %collective-permute-start.4 = (bf16[128,512]{1,0:T(8,128)(2,1)}, bf16[128,512]{1,0:T(8,128)(2,1)S(1)}, u32[]{:S(2)}, u32[]{:S(2)}) collective-permute-start(bf16[128,512]{1,0:T(8,128)(2,1)} %refs_4_.1), channel_id=1, source_target_pairs={{0,4},{1,5},{2,6},{3,7},{4,8},{5,9},{6,10},{7,11},{8,12},{9,13},{1... | collective-permute-start | bytes 393224 | tf_op jit(solution)/shard_map/ppermute | solution.py:29
  7.4 11.8 %collective-permute-start.5 = (bf16[128,512]{1,0:T(8,128)(2,1)}, bf16[128,512]{1,0:T(8,128)(2,1)S(1)}, u32[]{:S(2)}, u32[]{:S(2)}) collective-permute-start(bf16[128,512]{1,0:T(8,128)(2,1)} %refs_4_.1), channel_id=1, source_target_pairs={{0,8},{1,9},{2,10},{3,11},{4,12},{5,13},{6,14},{7,15},{8,0},{9,1},... | collective-permute-start | bytes 393224 | tf_op jit(solution)/shard_map/ppermute | solution.py:29
  10.0 9.2 %collective-permute-start.6 = (bf16[128,512]{1,0:T(8,128)(2,1)}, bf16[128,512]{1,0:T(8,128)(2,1)S(1)}, u32[]{:S(2)}, u32[]{:S(2)}) collective-permute-start(bf16[128,512]{1,0:T(8,128)(2,1)} %refs_4_.1), channel_id=1, source_target_pairs={{0,12},{1,13},{2,14},{3,15},{4,0},{5,1},{6,2},{7,3},{8,4},{9,5},{1... | collective-permute-start | bytes 393224 | tf_op jit(solution)/shard_map/ppermute | solution.py:29
  20.3 15.5 %collective-permute-start.9 = (bf16[512,512]{1,0:T(8,128)(2,1)S(1)}, bf16[512,512]{1,0:T(8,128)(2,1)S(1)}, u32[]{:S(2)}, u32[]{:S(2)}) collective-permute-start(bf16[512,512]{1,0:T(8,128)(2,1)S(1)} %bitcast.15), channel_id=1, source_target_pairs={{0,2},{1,3},{2,0},{3,1},{4,6},{5,7},{6,4},{7,5},{8,10},{9,11},{10,... | collective-permute-start | bytes 1572872 | tf_op jit(solution)/shard_map/ppermute | solution.py:33
  20.9 9.1 %collective-permute-start.10 = (bf16[144,512]{1,0:T(8,128)(2,1)S(1)}, bf16[144,512]{1,0:T(8,128)(2,1)S(1)}, u32[]{:S(2)}, u32[]{:S(2)}) collective-permute-start(bf16[144,512]{1,0:T(8,128)(2,1)S(1)} %payload.1.refs_7_), channel_id=1, source_target_pairs={{0,4},{1,5},{2,6},{3,7},{4,8},{5,9},{6,10},{7,11},{8,12},{9,13},{1... | collective-permute-start | bytes 442376 | tf_op jit(solution)/shard_map/ppermute | solution.py:29
  24.2 11.7 %collective-permute-start.11 = (bf16[144,512]{1,0:T(8,128)(2,1)S(1)}, bf16[144,512]{1,0:T(8,128)(2,1)S(1)}, u32[]{:S(2)}, u32[]{:S(2)}) collective-permute-start(bf16[144,512]{1,0:T(8,128)(2,1)S(1)} %payload.1.refs_7_), channel_id=1, source_target_pairs={{0,8},{1,9},{2,10},{3,11},{4,12},{5,13},{6,14},{7,15},{8,0},{9,1},... | collective-permute-start | bytes 442376 | tf_op jit(solution)/shard_map/ppermute | solution.py:29
  25.8 10.0 %collective-permute-start.12 = (bf16[144,512]{1,0:T(8,128)(2,1)S(1)}, bf16[144,512]{1,0:T(8,128)(2,1)S(1)}, u32[]{:S(2)}, u32[]{:S(2)}) collective-permute-start(bf16[144,512]{1,0:T(8,128)(2,1)S(1)} %payload.1.refs_7_), channel_id=1, source_target_pairs={{0,12},{1,13},{2,14},{3,15},{4,0},{5,1},{6,2},{7,3},{8,4},{9,5},{1... | collective-permute-start | bytes 442376 | tf_op jit(solution)/shard_map/ppermute | solution.py:29
  27.2 10.3 %collective-permute-start.8 = (bf16[128,512]{1,0:T(8,128)(2,1)S(1)}, bf16[128,512]{1,0:T(8,128)(2,1)S(1)}, u32[]{:S(2)}, u32[]{:S(2)}) collective-permute-start(bf16[128,512]{1,0:T(8,128)(2,1)S(1)} %get-tuple-element.69), channel_id=1, source_target_pairs={{0,2},{1,3},{2,0},{3,1},{4,6},{5,7},{6,4},{7,5},{8,10},{9,11},{10,... | collective-permute-start | bytes 393224 | tf_op jit(solution)/shard_map/ppermute | solution.py:33
  38.0 13.7 %collective-permute-start.16 = (bf16[512,512]{1,0:T(8,128)(2,1)S(1)}, bf16[512,512]{1,0:T(8,128)(2,1)S(1)}, u32[]{:S(2)}, u32[]{:S(2)}) collective-permute-start(bf16[512,512]{1,0:T(8,128)(2,1)S(1)} %bitcast.16), channel_id=1, source_target_pairs={{0,2},{1,3},{2,0},{3,1},{4,6},{5,7},{6,4},{7,5},{8,10},{9,11},{10,... | collective-permute-start | bytes 1572872 | tf_op jit(solution)/shard_map/ppermute | solution.py:33
  38.6 8.8 %collective-permute-start.13 = (bf16[128,512]{1,0:T(8,128)(2,1)S(1)}, bf16[128,512]{1,0:T(8,128)(2,1)S(1)}, u32[]{:S(2)}, u32[]{:S(2)}) collective-permute-start(bf16[128,512]{1,0:T(8,128)(2,1)S(1)} %latent.1.refs_3_), channel_id=1, source_target_pairs={{0,4},{1,5},{2,6},{3,7},{4,8},{5,9},{6,10},{7,11},{8,12},{9,13},{1... | collective-permute-start | bytes 393224 | tf_op jit(solution)/shard_map/ppermute | solution.py:29
  41.9 9.8 %collective-permute-start.14 = (bf16[128,512]{1,0:T(8,128)(2,1)S(1)}, bf16[128,512]{1,0:T(8,128)(2,1)S(1)}, u32[]{:S(2)}, u32[]{:S(2)}) collective-permute-start(bf16[128,512]{1,0:T(8,128)(2,1)S(1)} %latent.1.refs_3_), channel_id=1, source_target_pairs={{0,8},{1,9},{2,10},{3,11},{4,12},{5,13},{6,14},{7,15},{8,0},{9,1},... | collective-permute-start | bytes 393224 | tf_op jit(solution)/shard_map/ppermute | solution.py:29
  44.3 9.0 %collective-permute-start.17 = (bf16[512,512]{1,0:T(8,128)(2,1)S(1)}, bf16[512,512]{1,0:T(8,128)(2,1)S(1)}, u32[]{:S(2)}, u32[]{:S(2)}) collective-permute-start(bf16[512,512]{1,0:T(8,128)(2,1)S(1)} %collective-permute-done.9.refs_10_), channel_id=1, source_target_pairs={{0,1},{1,0},{2,3},{3,2},{4,5},{5,4},{6,7},{7,6},{8,9},{9,8},{10,11... | collective-permute-start | bytes 1572872 | tf_op jit(solution)/shard_map/ppermute | solution.py:33
  51.8 14.3 %collective-permute-start.23 = (bf16[512,512]{1,0:T(8,128)(2,1)S(1)}, bf16[512,512]{1,0:T(8,128)(2,1)S(1)}, u32[]{:S(2)}, u32[]{:S(2)}) collective-permute-start(bf16[512,512]{1,0:T(8,128)(2,1)S(1)} %get-tuple-element.92.down), channel_id=1, source_target_pairs={{0,2},{1,3},{2,0},{3,1},{4,6},{5,7},{6,4},{7,5},{8,10},{9,11},{10,... | collective-permute-start | bytes 1572872 | tf_op jit(solution)/shard_map/ppermute | solution.py:33
  66.1 9.2 %collective-permute-start.19 = (bf16[128,512]{1,0:T(8,128)(2,1)S(1)}, bf16[128,512]{1,0:T(8,128)(2,1)S(1)}, u32[]{:S(2)}, u32[]{:S(2)}) collective-permute-start(bf16[128,512]{1,0:T(8,128)(2,1)S(1)} %get-tuple-element.83), channel_id=1, source_target_pairs={{0,12},{1,13},{2,14},{3,15},{4,0},{5,1},{6,2},{7,3},{8,4},{9,5},{1... | collective-permute-start | bytes 393224 | tf_op jit(solution)/shard_map/ppermute | solution.py:29
  70.3 16.0 %collective-permute-start.20 = (bf16[128,512]{1,0:T(8,128)(2,1)S(1)}, bf16[128,512]{1,0:T(8,128)(2,1)S(1)}, u32[]{:S(2)}, u32[]{:S(2)}) collective-permute-start(bf16[128,512]{1,0:T(8,128)(2,1)S(1)} %get-tuple-element.85), channel_id=1, source_target_pairs={{0,8},{1,9},{2,10},{3,11},{4,12},{5,13},{6,14},{7,15},{8,0},{9,1},... | collective-permute-start | bytes 393224 | tf_op jit(solution)/shard_map/ppermute | solution.py:29
  70.8 15.5 %collective-permute-start.21 = (bf16[128,512]{1,0:T(8,128)(2,1)S(1)}, bf16[128,512]{1,0:T(8,128)(2,1)S(1)}, u32[]{:S(2)}, u32[]{:S(2)}) collective-permute-start(bf16[128,512]{1,0:T(8,128)(2,1)S(1)} %get-tuple-element.87), channel_id=1, source_target_pairs={{0,4},{1,5},{2,6},{3,7},{4,8},{5,9},{6,10},{7,11},{8,12},{9,13},{1... | collective-permute-start | bytes 393224 | tf_op jit(solution)/shard_map/ppermute | solution.py:29
  71.6 17.6 %collective-permute-start.25 = (bf16[256,512]{1,0:T(8,128)(2,1)S(1)}, bf16[256,512]{1,0:T(8,128)(2,1)S(1)}, u32[]{:S(2)}, u32[]{:S(2)}) collective-permute-start(bf16[256,512]{1,0:T(8,128)(2,1)S(1)} %get-tuple-element.96), channel_id=1, source_target_pairs={{0,2},{1,3},{2,0},{3,1},{4,6},{5,7},{6,4},{7,5},{8,10},{9,11},{10,... | collective-permute-start | bytes 786440 | tf_op jit(solution)/shard_map/ppermute | solution.py:33
  73.1 16.1 %collective-permute-start.26 = (bf16[128,512]{1,0:T(8,128)(2,1)S(1)}, bf16[128,512]{1,0:T(8,128)(2,1)S(1)}, u32[]{:S(2)}, u32[]{:S(2)}) collective-permute-start(bf16[128,512]{1,0:T(8,128)(2,1)S(1)} %get-tuple-element.97), channel_id=1, source_target_pairs={{0,8},{1,9},{2,10},{3,11},{4,12},{5,13},{6,14},{7,15},{8,0},{9,1},... | collective-permute-start | bytes 393224 | tf_op jit(solution)/shard_map/ppermute | solution.py:29
  95.5 20.6 %collective-permute-start.29 = (bf16[768,512]{1,0:T(8,128)(2,1)S(1)}, bf16[768,512]{1,0:T(8,128)(2,1)S(1)}, u32[]{:S(2)}, u32[]{:S(2)}) collective-permute-start(bf16[768,512]{1,0:T(8,128)(2,1)S(1)} %get-tuple-element.106), channel_id=1, source_target_pairs={{0,2},{1,3},{2,0},{3,1},{4,6},{5,7},{6,4},{7,5},{8,10},{9,11},{10,... | collective-permute-start | bytes 2359304 | tf_op jit(solution)/shard_map/ppermute | solution.py:33
  97.0 19.1 %collective-permute-start.30 = (bf16[2,128,512]{2,1,0:T(8,128)(2,1)S(1)}, bf16[2,128,512]{2,1,0:T(8,128)(2,1)S(1)}, u32[]{:S(2)}, u32[]{:S(2)}) collective-permute-start(bf16[2,128,512]{2,1,0:T(8,128)(2,1)S(1)} %get-tuple-element.101), channel_id=1, source_target_pairs={{0,12},{1,13},{2,14},{3,15},{4,0},{5,1},{6,2},{7,3},{8,4},{9,5},{1... | collective-permute-start | bytes 786440 | tf_op jit(solution)/shard_map/ppermute | solution.py:29
  97.0 19.1 %collective-permute-start.32 = (bf16[2,128,512]{2,1,0:T(8,128)(2,1)S(1)}, bf16[2,128,512]{2,1,0:T(8,128)(2,1)S(1)}, u32[]{:S(2)}, u32[]{:S(2)}) collective-permute-start(bf16[2,128,512]{2,1,0:T(8,128)(2,1)S(1)} %get-tuple-element.109), channel_id=1, source_target_pairs={{0,4},{1,5},{2,6},{3,7},{4,8},{5,9},{6,10},{7,11},{8,12},{9,13},{1... | collective-permute-start | bytes 786440 | tf_op jit(solution)/shard_map/ppermute | solution.py:29
  99.1 17.1 %collective-permute-start.31 = (bf16[128,512]{1,0:T(8,128)(2,1)S(1)}, bf16[128,512]{1,0:T(8,128)(2,1)S(1)}, u32[]{:S(2)}, u32[]{:S(2)}) collective-permute-start(bf16[128,512]{1,0:T(8,128)(2,1)S(1)} %get-tuple-element.108), channel_id=1, source_target_pairs={{0,8},{1,9},{2,10},{3,11},{4,12},{5,13},{6,14},{7,15},{8,0},{9,1},... | collective-permute-start | bytes 393224 | tf_op jit(solution)/shard_map/ppermute | solution.py:29
  (15 other events, 123.4 us)

commit v15 on v14

--- a/solution.py
+++ b/solution.py
@@ -308,7 +308,7 @@
     core_in = swap(after(side_in, latent), n_line, 1, 0)
     core_out = swap(after(side_out, *rows[1:]), n_line, 1, 0)
     weights = [own, core_own, side_in, side_out, core_in, core_out]
-    side_down = swap(after(down, *rows[1:]), n_line, 0, 1)
+    side_down = swap(after(down, rows[1]), n_line, 0, 1)
 
     deltas_of, outs_of, saved = [None] * n_line, [None] * n_line, []
     done = latent
@@ -340,16 +340,16 @@
         *(rows[i] for group in groups for i in group),
         *(value for values in saved for value in values),
     )
-    far_other = swap(after(far_other, side_down), n_line, 1, 0)
-    quarter = latent_width // 2
+    far_other = swap(far_other, n_line, 1, 0)
+    ahead = latent_width // 2
     far_first, far_rest = call(
-        far_body, [shape((rows, hidden_width), narrow) for rows in (quarter, 2 * latent_width - quarter)], "far_grads"
+        far_body, [shape((rows, hidden_width), narrow) for rows in (ahead, 2 * latent_width - ahead)], "far_grads"
     )(place, far, far_other)
     far_first = swap(far_first, n_line, 0, 1)
-    delta_lines = [after(line, near) for line in delta_lines]
+    delta_lines = [after(line, near, far_rest) for line in delta_lines]
     (delta,) = call(add_body, [rows_of(narrow)], "latent_delta")(place, *delta_lines)
     side_delta = swap(delta, n_line, 0, 1)
-    out_lines = [outs_of[0]] + [home(outs_of[back], back) if back not in riding else None for back in range(1, n_line)]
+    out_lines = [outs_of[0]] + [home(after(outs_of[back], delta), back) if back not in riding else None for back in range(1, n_line)]
     far_rest = swap(after(far_rest, side_delta), n_line, 0, 1)
     (others,) = call(pack_body, [shape((4, latent_width, hidden_width), narrow)], "pack")(
         after(place, delta), near_other, down, side_down

time: 118 us -> 115 us (0.975)
  waiting for transfers between devices: 53.3 us -> 49.2 us
    ppermute x17, waiting for transfers between devices: 11.1 us -> 7.61 us  [swap(): lax.ppermute(value, plane, device_pairs(n_line, lambda z, x, c: (z, x ^ s...]
    ppermute x16, starting transfers between devices: 27 us -> 29.8 us  [turn(): lax.ppermute(value, plane, device_pairs(n_line, lambda z, x, c: ((z + by)...]
    ppermute x17, starting transfers between devices: 12.9 us -> 10.9 us  [swap(): lax.ppermute(value, plane, device_pairs(n_line, lambda z, x, c: (z, x ^ s...]
  transfers between devices with their start and end apart: 33 -> 33, of which waited for: 13 -> 14; matrix products, arithmetic and copies ran while one was open for 0% -> 0% of each run, Pallas kernels for 12% -> 5%
where the time goes in v15:
time: 115 us
  waiting for transfers between devices  49.2 us (43%)
  starting transfers between devices  40.7 us (35%)
  Pallas kernels  21.6 us (19%)
  local copies, waits for them, and re-layouts  2.39 us (2%)
    ppermute x16, waiting for transfers between devices, turn(): lax.ppermute(value, plane, device_pairs(n_line, lambda z, x, c: ((z + by)...  41.6 us
    ppermute x16, starting transfers between devices, turn(): lax.ppermute(value, plane, device_pairs(n_line, lambda z, x, c: ((z + by)...  29.8 us
    pallas_call x14, Pallas kernels, run(): pl.pallas_call(body, out_shape=outs, in_specs=[pl.BlockSpec(memory_space=...  21.6 us
    ppermute x17, starting transfers between devices, swap(): lax.ppermute(value, plane, device_pairs(n_line, lambda z, x, c: (z, x ^ s...  10.9 us
    ppermute x17, waiting for transfers between devices, swap(): lax.ppermute(value, plane, device_pairs(n_line, lambda z, x, c: (z, x ^ s...  7.61 us
  transfers between devices with their start and end apart: 33, of which 14 were waited for; matrix products, arithmetic and copies ran while one was open for 0% of the time, Pallas kernels for 5%

profile of v15, /device:TPU:0, one launch (start us, length us, event | category | flops | bytes accessed | tf_op | source)
XLA Modules:
  0.0 114.8 jit_solution(13425576497218835935)
XLA Ops:
  0.8 2.0 %columns.1 = (bf16[128,512]{1,0:T(8,128)(2,1)S(1)}, bf16[128,512]{1,0:T(8,128)(2,1)S(1)}, bf16[2,128,512]{2,1,0:T(8,128)(2,1)S(1)}, bf16[2,512,512]{2,1,0:T(8,128)(2,1)S(1)}) custom-call(s32[7]{0:T(128)S(1)} %stack.32.place, bf16[128,2048]{1,0:T(8,128)(2,1)} %tokens.1, bf16[1,512,512]{2,1,0:T(8,128)(2,1)} %expert_in.1, bf16[1,512,512]{2,1,0:T(8,128)(2,1)} %expert_out.1), custom_call_target="tpu_custom_call" | custom-call | tf_op jit(solution)/shard_map/columns/pallas_call | solution.py:45
  3.3 2.6 %collective-permute-start = (bf16[2,128,512]{2,1,0:T(8,128)(2,1)S(1)}, bf16[2,128,512]{2,1,0:T(8,128)(2,1)S(1)}, u32[]{:S(2)}, u32[]{:S(2)}) collective-permute-start(bf16[2,128,512]{2,1,0:T(8,128)(2,1)S(1)} %get-tuple-element.62), channel_id=1, source_target_pairs={{0,2},{1,3},{2,0},{3,1},{4,6},{5,7},{6,4},{7,5},{8,10},{9,11},{10,... | collective-permute-start | bytes 786440 | tf_op jit(solution)/shard_map/ppermute | solution.py:33
  5.8 1.6 %collective-permute-start.4 = (bf16[128,512]{1,0:T(8,128)(2,1)}, bf16[128,512]{1,0:T(8,128)(2,1)S(1)}, u32[]{:S(2)}, u32[]{:S(2)}) collective-permute-start(bf16[128,512]{1,0:T(8,128)(2,1)} %refs_4_.1), channel_id=1, source_target_pairs={{0,4},{1,5},{2,6},{3,7},{4,8},{5,9},{6,10},{7,11},{8,12},{9,13},{1... | collective-permute-start | bytes 393224 | tf_op jit(solution)/shard_map/ppermute | solution.py:29
  7.4 2.6 %collective-permute-start.5 = (bf16[128,512]{1,0:T(8,128)(2,1)}, bf16[128,512]{1,0:T(8,128)(2,1)S(1)}, u32[]{:S(2)}, u32[]{:S(2)}) collective-permute-start(bf16[128,512]{1,0:T(8,128)(2,1)} %refs_4_.1), channel_id=1, source_target_pairs={{0,8},{1,9},{2,10},{3,11},{4,12},{5,13},{6,14},{7,15},{8,0},{9,1},... | collective-permute-start | bytes 393224 | tf_op jit(solution)/shard_map/ppermute | solution.py:29
  16.2 3.0 %collective-permute-done.5.refs_6_ = bf16[128,512]{1,0:T(8,128)(2,1)S(1)} collective-permute-done((bf16[128,512]{1,0:T(8,128)(2,1)}, bf16[128,512]{1,0:T(8,128)(2,1)S(1)}, u32[]{:S(2)}, u32[]{:S(2)}) %collective-permute-start.5) | collective-permute-done | bytes 131104 | tf_op jit(solution)/shard_map/ppermute | solution.py:29
  20.9 3.3 %collective-permute-start.10 = (bf16[144,512]{1,0:T(8,128)(2,1)S(1)}, bf16[144,512]{1,0:T(8,128)(2,1)S(1)}, u32[]{:S(2)}, u32[]{:S(2)}) collective-permute-start(bf16[144,512]{1,0:T(8,128)(2,1)S(1)} %payload.1.refs_7_), channel_id=1, source_target_pairs={{0,4},{1,5},{2,6},{3,7},{4,8},{5,9},{6,10},{7,11},{8,12},{9,13},{1... | collective-permute-start | bytes 442376 | tf_op jit(solution)/shard_map/ppermute | solution.py:29
  24.2 1.6 %collective-permute-start.11 = (bf16[144,512]{1,0:T(8,128)(2,1)S(1)}, bf16[144,512]{1,0:T(8,128)(2,1)S(1)}, u32[]{:S(2)}, u32[]{:S(2)}) collective-permute-start(bf16[144,512]{1,0:T(8,128)(2,1)S(1)} %payload.1.refs_7_), channel_id=1, source_target_pairs={{0,8},{1,9},{2,10},{3,11},{4,12},{5,13},{6,14},{7,15},{8,0},{9,1},... | collective-permute-start | bytes 442376 | tf_op jit(solution)/shard_map/ppermute | solution.py:29
  30.0 5.9 %collective-permute-done.11.refs_5_ = bf16[144,512]{1,0:T(8,128)(2,1)S(1)} collective-permute-done((bf16[144,512]{1,0:T(8,128)(2,1)S(1)}, bf16[144,512]{1,0:T(8,128)(2,1)S(1)}, u32[]{:S(2)}, u32[]{:S(2)}) %collective-permute-start.11) | collective-permute-done | bytes 147488 | tf_op jit(solution)/shard_map/ppermute | solution.py:29
  35.8 1.6 %collective-permute-done.8.refs_1_ = bf16[128,512]{1,0:T(8,128)(2,1)S(1)} collective-permute-done((bf16[128,512]{1,0:T(8,128)(2,1)S(1)}, bf16[128,512]{1,0:T(8,128)(2,1)S(1)}, u32[]{:S(2)}, u32[]{:S(2)}) %collective-permute-start.8) | collective-permute-done | bytes 131104 | tf_op jit(solution)/shard_map/ppermute | solution.py:33
  38.6 3.3 %collective-permute-start.13 = (bf16[128,512]{1,0:T(8,128)(2,1)S(1)}, bf16[128,512]{1,0:T(8,128)(2,1)S(1)}, u32[]{:S(2)}, u32[]{:S(2)}) collective-permute-start(bf16[128,512]{1,0:T(8,128)(2,1)S(1)} %latent.1.refs_3_), channel_id=1, source_target_pairs={{0,4},{1,5},{2,6},{3,7},{4,8},{5,9},{6,10},{7,11},{8,12},{9,13},{1... | collective-permute-start | bytes 393224 | tf_op jit(solution)/shard_map/ppermute | solution.py:29
  41.9 1.6 %collective-permute-start.14 = (bf16[128,512]{1,0:T(8,128)(2,1)S(1)}, bf16[128,512]{1,0:T(8,128)(2,1)S(1)}, u32[]{:S(2)}, u32[]{:S(2)}) collective-permute-start(bf16[128,512]{1,0:T(8,128)(2,1)S(1)} %latent.1.refs_3_), channel_id=1, source_target_pairs={{0,8},{1,9},{2,10},{3,11},{4,12},{5,13},{6,14},{7,15},{8,0},{9,1},... | collective-permute-start | bytes 393224 | tf_op jit(solution)/shard_map/ppermute | solution.py:29
  44.3 3.2 %collective-permute-done.13.refs_0_ = bf16[128,512]{1,0:T(8,128)(2,1)S(1)} collective-permute-done((bf16[128,512]{1,0:T(8,128)(2,1)S(1)}, bf16[128,512]{1,0:T(8,128)(2,1)S(1)}, u32[]{:S(2)}, u32[]{:S(2)}) %collective-permute-start.13) | collective-permute-done | bytes 131104 | tf_op jit(solution)/shard_map/ppermute | solution.py:29
  47.5 4.3 %collective-permute-done.14.refs_1_ = bf16[128,512]{1,0:T(8,128)(2,1)S(1)} collective-permute-done((bf16[128,512]{1,0:T(8,128)(2,1)S(1)}, bf16[128,512]{1,0:T(8,128)(2,1)S(1)}, u32[]{:S(2)}, u32[]{:S(2)}) %collective-permute-start.14) | collective-permute-done | bytes 131104 | tf_op jit(solution)/shard_map/ppermute | solution.py:29
  51.8 1.9 %collective-permute-done.18.refs_13_ = bf16[512,512]{1,0:T(8,128)(2,1)S(1)} collective-permute-done((bf16[512,512]{1,0:T(8,128)(2,1)S(1)}, bf16[512,512]{1,0:T(8,128)(2,1)S(1)}, u32[]{:S(2)}, u32[]{:S(2)}) %collective-permute-start.18) | collective-permute-done | bytes 524320 | tf_op jit(solution)/shard_map/ppermute | solution.py:33
  53.7 6.1 %experts.1 = (bf16[128,512]{1,0:T(8,128)(2,1)S(1)}, bf16[128,512]{1,0:T(8,128)(2,1)S(1)}, bf16[128,512]{1,0:T(8,128)(2,1)S(1)}, bf16[128,512]{1,0:T(8,128)(2,1)S...) custom-call(s32[7]{0:T(128)S(1)} %stack.32.place, ...), custom_call_target="tpu_custom_call" | custom-call | tf_op jit(solution)/shard_map/experts/pallas_call | solution.py:45
  59.8 2.9 %weight_grads.1 = (f32[2,512,512]{2,1,0:T(8,128)S(1)}, f32[2,512,512]{2,1,0:T(8,128)S(1)}, bf16[2,512,512]{2,1,0:T(8,128)(2,1)S(1)}, bf16[2,512,512]{2,1,0:T(8,128)(2,1)S(1)}) custom-call(s32[7]{0:T(128)S(1)} %stack.32.place, bf16[128,512]{1,0:T(8,128)(2,1)S(1)} %collective-permute-done.13.refs_0_, bf16[128,512]{1,0:T(8,128)(2,1)S(1)} %collective-permute-done.14.refs_1_, ...), custom_call_target="tpu_custom_call" | custom-call | flops 2147483648 | tf_op jit(solution)/shard_map/weight_grads/pallas_call | solution.py:45
  64.4 3.2 %collective-permute-start.22 = (bf16[128,512]{1,0:T(8,128)(2,1)S(1)}, bf16[128,512]{1,0:T(8,128)(2,1)S(1)}, u32[]{:S(2)}, u32[]{:S(2)}) collective-permute-start(bf16[128,512]{1,0:T(8,128)(2,1)S(1)} %get-tuple-element.90), channel_id=1, source_target_pairs={{0,4},{1,5},{2,6},{3,7},{4,8},{5,9},{6,10},{7,11},{8,12},{9,13},{1... | collective-permute-start | bytes 393224 | tf_op jit(solution)/shard_map/ppermute | solution.py:29
  72.8 5.1 %collective-permute-done.21.refs_2_ = bf16[128,512]{1,0:T(8,128)(2,1)S(1)} collective-permute-done((bf16[128,512]{1,0:T(8,128)(2,1)S(1)}, bf16[128,512]{1,0:T(8,128)(2,1)S(1)}, u32[]{:S(2)}, u32[]{:S(2)}) %collective-permute-start.21) | collective-permute-done | bytes 131104 | tf_op jit(solution)/shard_map/ppermute | solution.py:29
  78.5 2.3 %collective-permute-start.26 = (bf16[128,512]{1,0:T(8,128)(2,1)S(1)}, bf16[128,512]{1,0:T(8,128)(2,1)S(1)}, u32[]{:S(2)}, u32[]{:S(2)}) collective-permute-start(bf16[128,512]{1,0:T(8,128)(2,1)S(1)} %get-tuple-element.98), channel_id=1, source_target_pairs={{0,8},{1,9},{2,10},{3,11},{4,12},{5,13},{6,14},{7,15},{8,0},{9,1},... | collective-permute-start | bytes 393224 | tf_op jit(solution)/shard_map/ppermute | solution.py:29
  82.2 2.5 %collective-permute-done.26.refs_5_ = bf16[128,512]{1,0:T(8,128)(2,1)S(1)} collective-permute-done((bf16[128,512]{1,0:T(8,128)(2,1)S(1)}, bf16[128,512]{1,0:T(8,128)(2,1)S(1)}, u32[]{:S(2)}, u32[]{:S(2)}) %collective-permute-start.26) | collective-permute-done | bytes 131104 | tf_op jit(solution)/shard_map/ppermute | solution.py:29
  90.6 4.5 %collective-permute-start.30 = (bf16[2,128,512]{2,1,0:T(8,128)(2,1)S(1)}, bf16[2,128,512]{2,1,0:T(8,128)(2,1)S(1)}, u32[]{:S(2)}, u32[]{:S(2)}) collective-permute-start(bf16[2,128,512]{2,1,0:T(8,128)(2,1)S(1)} %get-tuple-element.102), channel_id=1, source_target_pairs={{0,12},{1,13},{2,14},{3,15},{4,0},{5,1},{6,2},{7,3},{8,4},{9,5},{1... | collective-permute-start | bytes 786440 | tf_op jit(solution)/shard_map/ppermute | solution.py:29
  95.7 2.2 %token_grad.1 = bf16[128,2048]{1,0:T(8,128)(2,1)} custom-call(s32[7]{0:T(128)S(1)} %stack.32.place, bf16[128,512]{1,0:T(8,128)(2,1)S(1)} %latent_delta.1.first.refs_4_.delta, bf16[4,512,512]{2,1,0:T(8,128)(2,1)S(1)} %pack.1.held, bf16[4,512,512]{2,1,0:T(8,128)(2,1)S(1)} %collective-permute-done.28.arrived.others), custom_call_target="tpu_custom_call" | custom-call | tf_op jit(solution)/shard_map/token_grad/pallas_call | solution.py:45
  97.9 14.9 %collective-permute-done.31.refs_2_ = bf16[128,512]{1,0:T(8,128)(2,1)S(1)} collective-permute-done((bf16[128,512]{1,0:T(8,128)(2,1)S(1)}, bf16[128,512]{1,0:T(8,128)(2,1)S(1)}, u32[]{:S(2)}, u32[]{:S(2)}) %collective-permute-start.31) | collective-permute-done | bytes 131104 | tf_op jit(solution)/shard_map/ppermute | solution.py:29
  112.9 1.9 %last_sums.1 = (f32[128,512]{1,0:T(8,128)}, bf16[128,512]{1,0:T(8,128)(2,1)}, bf16[1,512,512]{2,1,0:T(8,128)(2,1)}, bf16[1,512,512]{2,1,0:T(8,128)(2,1)}) custom-call(s32[7]{0:T(128)S(1)} %stack.32.place, f32[2,512,512]{2,1,0:T(8,128)S(1)} %get-tuple-element.81.near, bf16[4,512,512]{2,1,0:T(8,128)(2,1)S(1)} %collective-permute-done.28.arrived.others, ...), custom_call_target="tpu_custom_call" | custom-call | tf_op jit(solution)/shard_map/last_sums/pallas_call | solution.py:45
  (70 shorter events, 29.8 us)
Async XLA Ops:
  2.7 10.1 %collective-permute-start.1 = (bf16[2,512,512]{2,1,0:T(8,128)(2,1)S(1)}, bf16[2,512,512]{2,1,0:T(8,128)(2,1)S(1)}, u32[]{:S(2)}, u32[]{:S(2)}) collective-permute-start(bf16[2,512,512]{2,1,0:T(8,128)(2,1)S(1)} %get-tuple-element.64.refs_8_), channel_id=1, source_target_pairs={{0,1},{1,0},{2,3},{3,2},{4,5},{5,4},{6,7},{7,6},{8,9},{9,8},{10,11... | collective-permute-start | bytes 3145736 | tf_op jit(solution)/shard_map/ppermute | solution.py:33
  3.3 9.5 %collective-permute-start = (bf16[2,128,512]{2,1,0:T(8,128)(2,1)S(1)}, bf16[2,128,512]{2,1,0:T(8,128)(2,1)S(1)}, u32[]{:S(2)}, u32[]{:S(2)}) collective-permute-start(bf16[2,128,512]{2,1,0:T(8,128)(2,1)S(1)} %get-tuple-element.62), channel_id=1, source_target_pairs={{0,2},{1,3},{2,0},{3,1},{4,6},{5,7},{6,4},{7,5},{8,10},{9,11},{10,... | collective-permute-start | bytes 786440 | tf_op jit(solution)/shard_map/ppermute | solution.py:33
  5.8 10.3 %collective-permute-start.4 = (bf16[128,512]{1,0:T(8,128)(2,1)}, bf16[128,512]{1,0:T(8,128)(2,1)S(1)}, u32[]{:S(2)}, u32[]{:S(2)}) collective-permute-start(bf16[128,512]{1,0:T(8,128)(2,1)} %refs_4_.1), channel_id=1, source_target_pairs={{0,4},{1,5},{2,6},{3,7},{4,8},{5,9},{6,10},{7,11},{8,12},{9,13},{1... | collective-permute-start | bytes 393224 | tf_op jit(solution)/shard_map/ppermute | solution.py:29
  7.4 11.8 %collective-permute-start.5 = (bf16[128,512]{1,0:T(8,128)(2,1)}, bf16[128,512]{1,0:T(8,128)(2,1)S(1)}, u32[]{:S(2)}, u32[]{:S(2)}) collective-permute-start(bf16[128,512]{1,0:T(8,128)(2,1)} %refs_4_.1), channel_id=1, source_target_pairs={{0,8},{1,9},{2,10},{3,11},{4,12},{5,13},{6,14},{7,15},{8,0},{9,1},... | collective-permute-start | bytes 393224 | tf_op jit(solution)/shard_map/ppermute | solution.py:29
  10.0 9.2 %collective-permute-start.6 = (bf16[128,512]{1,0:T(8,128)(2,1)}, bf16[128,512]{1,0:T(8,128)(2,1)S(1)}, u32[]{:S(2)}, u32[]{:S(2)}) collective-permute-start(bf16[128,512]{1,0:T(8,128)(2,1)} %refs_4_.1), channel_id=1, source_target_pairs={{0,12},{1,13},{2,14},{3,15},{4,0},{5,1},{6,2},{7,3},{8,4},{9,5},{1... | collective-permute-start | bytes 393224 | tf_op jit(solution)/shard_map/ppermute | solution.py:29
  20.3 15.5 %collective-permute-start.9 = (bf16[512,512]{1,0:T(8,128)(2,1)S(1)}, bf16[512,512]{1,0:T(8,128)(2,1)S(1)}, u32[]{:S(2)}, u32[]{:S(2)}) collective-permute-start(bf16[512,512]{1,0:T(8,128)(2,1)S(1)} %bitcast.15), channel_id=1, source_target_pairs={{0,2},{1,3},{2,0},{3,1},{4,6},{5,7},{6,4},{7,5},{8,10},{9,11},{10,... | collective-permute-start | bytes 1572872 | tf_op jit(solution)/shard_map/ppermute | solution.py:33
  20.9 9.1 %collective-permute-start.10 = (bf16[144,512]{1,0:T(8,128)(2,1)S(1)}, bf16[144,512]{1,0:T(8,128)(2,1)S(1)}, u32[]{:S(2)}, u32[]{:S(2)}) collective-permute-start(bf16[144,512]{1,0:T(8,128)(2,1)S(1)} %payload.1.refs_7_), channel_id=1, source_target_pairs={{0,4},{1,5},{2,6},{3,7},{4,8},{5,9},{6,10},{7,11},{8,12},{9,13},{1... | collective-permute-start | bytes 442376 | tf_op jit(solution)/shard_map/ppermute | solution.py:29
  24.2 11.7 %collective-permute-start.11 = (bf16[144,512]{1,0:T(8,128)(2,1)S(1)}, bf16[144,512]{1,0:T(8,128)(2,1)S(1)}, u32[]{:S(2)}, u32[]{:S(2)}) collective-permute-start(bf16[144,512]{1,0:T(8,128)(2,1)S(1)} %payload.1.refs_7_), channel_id=1, source_target_pairs={{0,8},{1,9},{2,10},{3,11},{4,12},{5,13},{6,14},{7,15},{8,0},{9,1},... | collective-permute-start | bytes 442376 | tf_op jit(solution)/shard_map/ppermute | solution.py:29
  25.8 10.0 %collective-permute-start.12 = (bf16[144,512]{1,0:T(8,128)(2,1)S(1)}, bf16[144,512]{1,0:T(8,128)(2,1)S(1)}, u32[]{:S(2)}, u32[]{:S(2)}) collective-permute-start(bf16[144,512]{1,0:T(8,128)(2,1)S(1)} %payload.1.refs_7_), channel_id=1, source_target_pairs={{0,12},{1,13},{2,14},{3,15},{4,0},{5,1},{6,2},{7,3},{8,4},{9,5},{1... | collective-permute-start | bytes 442376 | tf_op jit(solution)/shard_map/ppermute | solution.py:29
  27.2 10.3 %collective-permute-start.8 = (bf16[128,512]{1,0:T(8,128)(2,1)S(1)}, bf16[128,512]{1,0:T(8,128)(2,1)S(1)}, u32[]{:S(2)}, u32[]{:S(2)}) collective-permute-start(bf16[128,512]{1,0:T(8,128)(2,1)S(1)} %get-tuple-element.69), channel_id=1, source_target_pairs={{0,2},{1,3},{2,0},{3,1},{4,6},{5,7},{6,4},{7,5},{8,10},{9,11},{10,... | collective-permute-start | bytes 393224 | tf_op jit(solution)/shard_map/ppermute | solution.py:33
  38.0 13.7 %collective-permute-start.16 = (bf16[512,512]{1,0:T(8,128)(2,1)S(1)}, bf16[512,512]{1,0:T(8,128)(2,1)S(1)}, u32[]{:S(2)}, u32[]{:S(2)}) collective-permute-start(bf16[512,512]{1,0:T(8,128)(2,1)S(1)} %bitcast.16), channel_id=1, source_target_pairs={{0,2},{1,3},{2,0},{3,1},{4,6},{5,7},{6,4},{7,5},{8,10},{9,11},{10,... | collective-permute-start | bytes 1572872 | tf_op jit(solution)/shard_map/ppermute | solution.py:33
  38.6 8.8 %collective-permute-start.13 = (bf16[128,512]{1,0:T(8,128)(2,1)S(1)}, bf16[128,512]{1,0:T(8,128)(2,1)S(1)}, u32[]{:S(2)}, u32[]{:S(2)}) collective-permute-start(bf16[128,512]{1,0:T(8,128)(2,1)S(1)} %latent.1.refs_3_), channel_id=1, source_target_pairs={{0,4},{1,5},{2,6},{3,7},{4,8},{5,9},{6,10},{7,11},{8,12},{9,13},{1... | collective-permute-start | bytes 393224 | tf_op jit(solution)/shard_map/ppermute | solution.py:29
  41.9 9.8 %collective-permute-start.14 = (bf16[128,512]{1,0:T(8,128)(2,1)S(1)}, bf16[128,512]{1,0:T(8,128)(2,1)S(1)}, u32[]{:S(2)}, u32[]{:S(2)}) collective-permute-start(bf16[128,512]{1,0:T(8,128)(2,1)S(1)} %latent.1.refs_3_), channel_id=1, source_target_pairs={{0,8},{1,9},{2,10},{3,11},{4,12},{5,13},{6,14},{7,15},{8,0},{9,1},... | collective-permute-start | bytes 393224 | tf_op jit(solution)/shard_map/ppermute | solution.py:29
  43.5 8.2 %collective-permute-start.15 = (bf16[128,512]{1,0:T(8,128)(2,1)S(1)}, bf16[128,512]{1,0:T(8,128)(2,1)S(1)}, u32[]{:S(2)}, u32[]{:S(2)}) collective-permute-start(bf16[128,512]{1,0:T(8,128)(2,1)S(1)} %latent.1.refs_3_), channel_id=1, source_target_pairs={{0,12},{1,13},{2,14},{3,15},{4,0},{5,1},{6,2},{7,3},{8,4},{9,5},{1... | collective-permute-start | bytes 393224 | tf_op jit(solution)/shard_map/ppermute | solution.py:29
  44.3 7.5 %collective-permute-start.17 = (bf16[512,512]{1,0:T(8,128)(2,1)S(1)}, bf16[512,512]{1,0:T(8,128)(2,1)S(1)}, u32[]{:S(2)}, u32[]{:S(2)}) collective-permute-start(bf16[512,512]{1,0:T(8,128)(2,1)S(1)} %collective-permute-done.9.refs_10_), channel_id=1, source_target_pairs={{0,1},{1,0},{2,3},{3,2},{4,5},{5,4},{6,7},{7,6},{8,9},{9,8},{10,11... | collective-permute-start | bytes 1572872 | tf_op jit(solution)/shard_map/ppermute | solution.py:33
  62.9 18.6 %collective-permute-start.24 = (bf16[512,512]{1,0:T(8,128)(2,1)S(1)}, bf16[512,512]{1,0:T(8,128)(2,1)S(1)}, u32[]{:S(2)}, u32[]{:S(2)}) collective-permute-start(bf16[512,512]{1,0:T(8,128)(2,1)S(1)} %get-tuple-element.95.down), channel_id=1, source_target_pairs={{0,2},{1,3},{2,0},{3,1},{4,6},{5,7},{6,4},{7,5},{8,10},{9,11},{10,... | collective-permute-start | bytes 1572872 | tf_op jit(solution)/shard_map/ppermute | solution.py:33
  64.4 8.4 %collective-permute-start.22 = (bf16[128,512]{1,0:T(8,128)(2,1)S(1)}, bf16[128,512]{1,0:T(8,128)(2,1)S(1)}, u32[]{:S(2)}, u32[]{:S(2)}) collective-permute-start(bf16[128,512]{1,0:T(8,128)(2,1)S(1)} %get-tuple-element.90), channel_id=1, source_target_pairs={{0,4},{1,5},{2,6},{3,7},{4,8},{5,9},{6,10},{7,11},{8,12},{9,13},{1... | collective-permute-start | bytes 393224 | tf_op jit(solution)/shard_map/ppermute | solution.py:29
  67.7 10.2 %collective-permute-start.21 = (bf16[128,512]{1,0:T(8,128)(2,1)S(1)}, bf16[128,512]{1,0:T(8,128)(2,1)S(1)}, u32[]{:S(2)}, u32[]{:S(2)}) collective-permute-start(bf16[128,512]{1,0:T(8,128)(2,1)S(1)} %get-tuple-element.88), channel_id=1, source_target_pairs={{0,8},{1,9},{2,10},{3,11},{4,12},{5,13},{6,14},{7,15},{8,0},{9,1},... | collective-permute-start | bytes 393224 | tf_op jit(solution)/shard_map/ppermute | solution.py:29
  69.0 8.9 %collective-permute-start.20 = (bf16[128,512]{1,0:T(8,128)(2,1)S(1)}, bf16[128,512]{1,0:T(8,128)(2,1)S(1)}, u32[]{:S(2)}, u32[]{:S(2)}) collective-permute-start(bf16[128,512]{1,0:T(8,128)(2,1)S(1)} %get-tuple-element.86), channel_id=1, source_target_pairs={{0,12},{1,13},{2,14},{3,15},{4,0},{5,1},{6,2},{7,3},{8,4},{9,5},{1... | collective-permute-start | bytes 393224 | tf_op jit(solution)/shard_map/ppermute | solution.py:29
  70.8 14.0 %collective-permute-start.25 = (bf16[256,512]{1,0:T(8,128)(2,1)S(1)}, bf16[256,512]{1,0:T(8,128)(2,1)S(1)}, u32[]{:S(2)}, u32[]{:S(2)}) collective-permute-start(bf16[256,512]{1,0:T(8,128)(2,1)S(1)} %get-tuple-element.96), channel_id=1, source_target_pairs={{0,2},{1,3},{2,0},{3,1},{4,6},{5,7},{6,4},{7,5},{8,10},{9,11},{10,... | collective-permute-start | bytes 786440 | tf_op jit(solution)/shard_map/ppermute | solution.py:33
  89.5 23.3 %collective-permute-start.29 = (bf16[768,512]{1,0:T(8,128)(2,1)S(1)}, bf16[768,512]{1,0:T(8,128)(2,1)S(1)}, u32[]{:S(2)}, u32[]{:S(2)}) collective-permute-start(bf16[768,512]{1,0:T(8,128)(2,1)S(1)} %get-tuple-element.106), channel_id=1, source_target_pairs={{0,2},{1,3},{2,0},{3,1},{4,6},{5,7},{6,4},{7,5},{8,10},{9,11},{10,... | collective-permute-start | bytes 2359304 | tf_op jit(solution)/shard_map/ppermute | solution.py:33
  90.6 22.2 %collective-permute-start.30 = (bf16[2,128,512]{2,1,0:T(8,128)(2,1)S(1)}, bf16[2,128,512]{2,1,0:T(8,128)(2,1)S(1)}, u32[]{:S(2)}, u32[]{:S(2)}) collective-permute-start(bf16[2,128,512]{2,1,0:T(8,128)(2,1)S(1)} %get-tuple-element.102), channel_id=1, source_target_pairs={{0,12},{1,13},{2,14},{3,15},{4,0},{5,1},{6,2},{7,3},{8,4},{9,5},{1... | collective-permute-start | bytes 786440 | tf_op jit(solution)/shard_map/ppermute | solution.py:29
  95.1 17.7 %collective-permute-start.32 = (bf16[2,128,512]{2,1,0:T(8,128)(2,1)S(1)}, bf16[2,128,512]{2,1,0:T(8,128)(2,1)S(1)}, u32[]{:S(2)}, u32[]{:S(2)}) collective-permute-start(bf16[2,128,512]{2,1,0:T(8,128)(2,1)S(1)} %get-tuple-element.109), channel_id=1, source_target_pairs={{0,4},{1,5},{2,6},{3,7},{4,8},{5,9},{6,10},{7,11},{8,12},{9,13},{1... | collective-permute-start | bytes 786440 | tf_op jit(solution)/shard_map/ppermute | solution.py:29
  95.2 17.7 %collective-permute-start.31 = (bf16[128,512]{1,0:T(8,128)(2,1)S(1)}, bf16[128,512]{1,0:T(8,128)(2,1)S(1)}, u32[]{:S(2)}, u32[]{:S(2)}) collective-permute-start(bf16[128,512]{1,0:T(8,128)(2,1)S(1)} %get-tuple-element.108), channel_id=1, source_target_pairs={{0,8},{1,9},{2,10},{3,11},{4,12},{5,13},{6,14},{7,15},{8,0},{9,1},... | collective-permute-start | bytes 393224 | tf_op jit(solution)/shard_map/ppermute | solution.py:29
  (15 other events, 125.6 us)

commit v16 on v15

--- a/solution.py
+++ b/solution.py
@@ -26,7 +26,7 @@
 
 
 def turn(value, n_line, by):
-    return lax.ppermute(value, plane, device_pairs(n_line, lambda z, x, c: ((z + by) % n_line, x, c)))
+    return lax.ppermute(value, plane, device_pairs(n_line, lambda z, x, c: (z ^ by, x, c)))
 
 
 def swap(value, n_line, core, side):
@@ -147,7 +147,7 @@
     keep, send, down = refs[4 + n_line :]
     block = downs[0].shape[0]
     for back in range(n_line):
-        z = lax.rem(place[0] + n_line - back, n_line)
+        z = place[0] ^ back
         down[pl.ds(pl.multiple_of(z * block, block), block), :] = downs[back][...]
     for core, out in ((1, send), (0, keep)):
         for side in range(2):
@@ -231,7 +231,7 @@
     for z in range(n_line):
         for back in range(n_line):
 
-            @pl.when(lax.rem(place[0] + n_line - back, n_line) == z)
+            @pl.when((place[0] ^ back) == z)
             def _(z=z, back=back):
                 targets[back][...] = part[z * block : (z + 1) * block].astype(targets[back].dtype)
 
@@ -325,7 +325,7 @@
             deltas_of[back], outs_of[back] = values[2 * i], values[2 * i + 1]
 
     def home(value, back):
-        return turn(value, n_line, n_line - back) if back else value
+        return turn(value, n_line, back) if back else value
 
     delta_lines = [home(value, back) for back, value in enumerate(deltas_of)]
 
@@ -367,7 +367,7 @@
     (grad_tokens,) = call(
         functools.partial(token_grad_body, n_line, block), [shape((tok_rows, width), narrow)], "token_grad"
     )(place, after(delta, blocks[1]), *others)
-    blocks = [blocks[0]] + [turn(blocks[back], n_line, n_line - back) for back in range(1, n_line)]
+    blocks = [blocks[0]] + [turn(blocks[back], n_line, back) for back in range(1, n_line)]
     grad_down, latent_out, grad_in, grad_out = call(
         functools.partial(last_body, riding, n_line),
         [shape((block, latent_width), wide), rows_of(narrow)]
@@ -498,7 +498,7 @@
 def on_device(tokens, routes, *others):
     n_major = lax.axis_size("expert")
     n_experts = n_major * lax.axis_size("dp")
-    few = n_experts <= 2 * routes.shape[1] and n_major % 2 == 0 and n_major >= 6 and lax.axis_size("dp") == 2
+    few = n_experts <= 2 * routes.shape[1] and n_major >= 8 and n_major & (n_major - 1) == 0 and lax.axis_size("dp") == 2
     return (all_rows if few else routed_rows)(tokens, routes, *others)
 
 

time: 115 us -> 120 us (1.043)
  waiting for transfers between devices: 49.2 us -> 60.5 us
  starting transfers between devices: 40.7 us -> 34.1 us
    ppermute x16, waiting for transfers between devices: 41.6 us -> 54.3 us  [turn(): lax.ppermute(value, plane, device_pairs(n_line, lambda z, x, c: (z ^ by,...]
    ppermute x16, starting transfers between devices: 29.8 us -> 22.3 us  [turn(): lax.ppermute(value, plane, device_pairs(n_line, lambda z, x, c: (z ^ by,...]
    ppermute x17, waiting for transfers between devices: 7.61 us -> 6.2 us  [swap(): lax.ppermute(value, plane, device_pairs(n_line, lambda z, x, c: (z, x ^ s...]
  transfers between devices with their start and end apart: 33 -> 33, of which waited for: 14 -> 13; matrix products, arithmetic and copies ran while one was open for 0% -> 0% of each run, Pallas kernels for 5% -> 4%
where the time goes in v16:
time: 120 us; the launch traced here: 119 us
  waiting for transfers between devices  60.5 us (50%)
  starting transfers between devices  34.1 us (28%)
  Pallas kernels  21.6 us (18%)
  local copies, waits for them, and re-layouts  2.39 us (2%)
    ppermute x16, waiting for transfers between devices, turn(): lax.ppermute(value, plane, device_pairs(n_line, lambda z, x, c: (z ^ by,...  54.3 us
    ppermute x16, starting transfers between devices, turn(): lax.ppermute(value, plane, device_pairs(n_line, lambda z, x, c: (z ^ by,...  22.3 us
    pallas_call x14, Pallas kernels, run(): pl.pallas_call(body, out_shape=outs, in_specs=[pl.BlockSpec(memory_space=...  21.6 us
    ppermute x17, starting transfers between devices, swap(): lax.ppermute(value, plane, device_pairs(n_line, lambda z, x, c: (z, x ^ s...  11.8 us
    ppermute x17, waiting for transfers between devices, swap(): lax.ppermute(value, plane, device_pairs(n_line, lambda z, x, c: (z, x ^ s...  6.2 us
  transfers between devices with their start and end apart: 33, of which 13 were waited for; matrix products, arithmetic and copies ran while one was open for 0% of the time, Pallas kernels for 4%

profile of v16, /device:TPU:0, one launch (start us, length us, event | category | flops | bytes accessed | tf_op | source)
XLA Modules:
  0.0 119.4 jit_solution(1796566676834555025)
XLA Ops:
  0.8 2.0 %columns.1 = (bf16[128,512]{1,0:T(8,128)(2,1)S(1)}, bf16[128,512]{1,0:T(8,128)(2,1)S(1)}, bf16[2,128,512]{2,1,0:T(8,128)(2,1)S(1)}, bf16[2,512,512]{2,1,0:T(8,128)(2,1)S(1)}) custom-call(s32[7]{0:T(128)S(1)} %stack.32.place, bf16[128,2048]{1,0:T(8,128)(2,1)} %tokens.1, bf16[1,512,512]{2,1,0:T(8,128)(2,1)} %expert_in.1, bf16[1,512,512]{2,1,0:T(8,128)(2,1)} %expert_out.1), custom_call_target="tpu_custom_call" | custom-call | tf_op jit(solution)/shard_map/columns/pallas_call | solution.py:45
  3.3 2.6 %collective-permute-start = (bf16[2,128,512]{2,1,0:T(8,128)(2,1)S(1)}, bf16[2,128,512]{2,1,0:T(8,128)(2,1)S(1)}, u32[]{:S(2)}, u32[]{:S(2)}) collective-permute-start(bf16[2,128,512]{2,1,0:T(8,128)(2,1)S(1)} %get-tuple-element.62), channel_id=1, source_target_pairs={{0,2},{1,3},{2,0},{3,1},{4,6},{5,7},{6,4},{7,5},{8,10},{9,11},{10,... | collective-permute-start | bytes 786440 | tf_op jit(solution)/shard_map/ppermute | solution.py:33
  5.8 1.6 %collective-permute-start.4 = (bf16[128,512]{1,0:T(8,128)(2,1)}, bf16[128,512]{1,0:T(8,128)(2,1)S(1)}, u32[]{:S(2)}, u32[]{:S(2)}) collective-permute-start(bf16[128,512]{1,0:T(8,128)(2,1)} %refs_4_.1), channel_id=1, source_target_pairs={{0,4},{1,5},{2,6},{3,7},{4,0},{5,1},{6,2},{7,3},{8,12},{9,13},{10,... | collective-permute-start | bytes 393224 | tf_op jit(solution)/shard_map/ppermute | solution.py:29
  7.4 2.6 %collective-permute-start.5 = (bf16[128,512]{1,0:T(8,128)(2,1)}, bf16[128,512]{1,0:T(8,128)(2,1)S(1)}, u32[]{:S(2)}, u32[]{:S(2)}) collective-permute-start(bf16[128,512]{1,0:T(8,128)(2,1)} %refs_4_.1), channel_id=1, source_target_pairs={{0,8},{1,9},{2,10},{3,11},{4,12},{5,13},{6,14},{7,15},{8,0},{9,1},... | collective-permute-start | bytes 393224 | tf_op jit(solution)/shard_map/ppermute | solution.py:29
  10.2 2.5 %collective-permute-done.refs_1_ = bf16[2,128,512]{2,1,0:T(8,128)(2,1)S(1)} collective-permute-done((bf16[2,128,512]{2,1,0:T(8,128)(2,1)S(1)}, bf16[2,128,512]{2,1,0:T(8,128)(2,1)S(1)}, u32[]{:S(2)}, u32[]{:S(2)}) %collective-permute-start) | collective-permute-done | bytes 262176 | tf_op jit(solution)/shard_map/ppermute | solution.py:33
  16.2 4.3 %collective-permute-done.5.refs_6_ = bf16[128,512]{1,0:T(8,128)(2,1)S(1)} collective-permute-done((bf16[128,512]{1,0:T(8,128)(2,1)}, bf16[128,512]{1,0:T(8,128)(2,1)S(1)}, u32[]{:S(2)}, u32[]{:S(2)}) %collective-permute-start.5) | collective-permute-done | bytes 131104 | tf_op jit(solution)/shard_map/ppermute | solution.py:29
  22.2 2.3 %collective-permute-start.10 = (bf16[144,512]{1,0:T(8,128)(2,1)S(1)}, bf16[144,512]{1,0:T(8,128)(2,1)S(1)}, u32[]{:S(2)}, u32[]{:S(2)}) collective-permute-start(bf16[144,512]{1,0:T(8,128)(2,1)S(1)} %payload.1.refs_7_), channel_id=1, source_target_pairs={{0,4},{1,5},{2,6},{3,7},{4,0},{5,1},{6,2},{7,3},{8,12},{9,13},{10,... | collective-permute-start | bytes 442376 | tf_op jit(solution)/shard_map/ppermute | solution.py:29
  27.6 1.6 %collective-permute-start.8 = (bf16[128,512]{1,0:T(8,128)(2,1)S(1)}, bf16[128,512]{1,0:T(8,128)(2,1)S(1)}, u32[]{:S(2)}, u32[]{:S(2)}) collective-permute-start(bf16[128,512]{1,0:T(8,128)(2,1)S(1)} %get-tuple-element.69), channel_id=1, source_target_pairs={{0,2},{1,3},{2,0},{3,1},{4,6},{5,7},{6,4},{7,5},{8,10},{9,11},{10,... | collective-permute-start | bytes 393224 | tf_op jit(solution)/shard_map/ppermute | solution.py:33
  29.2 1.9 %collective-permute-done.10.refs_4_ = bf16[144,512]{1,0:T(8,128)(2,1)S(1)} collective-permute-done((bf16[144,512]{1,0:T(8,128)(2,1)S(1)}, bf16[144,512]{1,0:T(8,128)(2,1)S(1)}, u32[]{:S(2)}, u32[]{:S(2)}) %collective-permute-start.10) | collective-permute-done | bytes 147488 | tf_op jit(solution)/shard_map/ppermute | solution.py:29
  31.1 7.4 %collective-permute-done.11.refs_5_ = bf16[144,512]{1,0:T(8,128)(2,1)S(1)} collective-permute-done((bf16[144,512]{1,0:T(8,128)(2,1)S(1)}, bf16[144,512]{1,0:T(8,128)(2,1)S(1)}, u32[]{:S(2)}, u32[]{:S(2)}) %collective-permute-start.11) | collective-permute-done | bytes 147488 | tf_op jit(solution)/shard_map/ppermute | solution.py:29
  40.7 2.7 %collective-permute-start.13 = (bf16[128,512]{1,0:T(8,128)(2,1)S(1)}, bf16[128,512]{1,0:T(8,128)(2,1)S(1)}, u32[]{:S(2)}, u32[]{:S(2)}) collective-permute-start(bf16[128,512]{1,0:T(8,128)(2,1)S(1)} %latent.1.refs_3_), channel_id=1, source_target_pairs={{0,4},{1,5},{2,6},{3,7},{4,0},{5,1},{6,2},{7,3},{8,12},{9,13},{10,... | collective-permute-start | bytes 393224 | tf_op jit(solution)/shard_map/ppermute | solution.py:29
  45.8 1.8 %collective-permute-done.13.refs_0_ = bf16[128,512]{1,0:T(8,128)(2,1)S(1)} collective-permute-done((bf16[128,512]{1,0:T(8,128)(2,1)S(1)}, bf16[128,512]{1,0:T(8,128)(2,1)S(1)}, u32[]{:S(2)}, u32[]{:S(2)}) %collective-permute-start.13) | collective-permute-done | bytes 131104 | tf_op jit(solution)/shard_map/ppermute | solution.py:29
  47.6 7.6 %collective-permute-done.14.refs_1_ = bf16[128,512]{1,0:T(8,128)(2,1)S(1)} collective-permute-done((bf16[128,512]{1,0:T(8,128)(2,1)S(1)}, bf16[128,512]{1,0:T(8,128)(2,1)S(1)}, u32[]{:S(2)}, u32[]{:S(2)}) %collective-permute-start.14) | collective-permute-done | bytes 131104 | tf_op jit(solution)/shard_map/ppermute | solution.py:29
  55.2 1.9 %collective-permute-done.18.refs_13_ = bf16[512,512]{1,0:T(8,128)(2,1)S(1)} collective-permute-done((bf16[512,512]{1,0:T(8,128)(2,1)S(1)}, bf16[512,512]{1,0:T(8,128)(2,1)S(1)}, u32[]{:S(2)}, u32[]{:S(2)}) %collective-permute-start.18) | collective-permute-done | bytes 524320 | tf_op jit(solution)/shard_map/ppermute | solution.py:33
  57.1 6.1 %experts.1 = (bf16[128,512]{1,0:T(8,128)(2,1)S(1)}, bf16[128,512]{1,0:T(8,128)(2,1)S(1)}, bf16[128,512]{1,0:T(8,128)(2,1)S(1)}, bf16[128,512]{1,0:T(8,128)(2,1)S...) custom-call(s32[7]{0:T(128)S(1)} %stack.32.place, ...), custom_call_target="tpu_custom_call" | custom-call | tf_op jit(solution)/shard_map/experts/pallas_call | solution.py:45
  63.2 2.9 %weight_grads.1 = (f32[2,512,512]{2,1,0:T(8,128)S(1)}, f32[2,512,512]{2,1,0:T(8,128)S(1)}, bf16[2,512,512]{2,1,0:T(8,128)(2,1)S(1)}, bf16[2,512,512]{2,1,0:T(8,128)(2,1)S(1)}) custom-call(s32[7]{0:T(128)S(1)} %stack.32.place, bf16[128,512]{1,0:T(8,128)(2,1)S(1)} %collective-permute-done.13.refs_0_, bf16[128,512]{1,0:T(8,128)(2,1)S(1)} %collective-permute-done.14.refs_1_, ...), custom_call_target="tpu_custom_call" | custom-call | flops 2147483648 | tf_op jit(solution)/shard_map/weight_grads/pallas_call | solution.py:45
  67.4 1.9 %collective-permute-start.22 = (bf16[128,512]{1,0:T(8,128)(2,1)S(1)}, bf16[128,512]{1,0:T(8,128)(2,1)S(1)}, u32[]{:S(2)}, u32[]{:S(2)}) collective-permute-start(bf16[128,512]{1,0:T(8,128)(2,1)S(1)} %get-tuple-element.90), channel_id=1, source_target_pairs={{0,12},{1,13},{2,14},{3,15},{4,8},{5,9},{6,10},{7,11},{8,4},{9,5},... | collective-permute-start | bytes 393224 | tf_op jit(solution)/shard_map/ppermute | solution.py:29
  73.6 2.1 %collective-permute-done.22.refs_3_ = bf16[128,512]{1,0:T(8,128)(2,1)S(1)} collective-permute-done((bf16[128,512]{1,0:T(8,128)(2,1)S(1)}, bf16[128,512]{1,0:T(8,128)(2,1)S(1)}, u32[]{:S(2)}, u32[]{:S(2)}) %collective-permute-start.22) | collective-permute-done | bytes 131104 | tf_op jit(solution)/shard_map/ppermute | solution.py:29
  75.7 7.1 %collective-permute-done.21.refs_2_ = bf16[128,512]{1,0:T(8,128)(2,1)S(1)} collective-permute-done((bf16[128,512]{1,0:T(8,128)(2,1)S(1)}, bf16[128,512]{1,0:T(8,128)(2,1)S(1)}, u32[]{:S(2)}, u32[]{:S(2)}) %collective-permute-start.21) | collective-permute-done | bytes 131104 | tf_op jit(solution)/shard_map/ppermute | solution.py:29
  85.2 7.0 %collective-permute-done.26.refs_5_ = bf16[128,512]{1,0:T(8,128)(2,1)S(1)} collective-permute-done((bf16[128,512]{1,0:T(8,128)(2,1)S(1)}, bf16[128,512]{1,0:T(8,128)(2,1)S(1)}, u32[]{:S(2)}, u32[]{:S(2)}) %collective-permute-start.26) | collective-permute-done | bytes 131104 | tf_op jit(solution)/shard_map/ppermute | solution.py:29
  98.0 2.2 %collective-permute-start.31 = (bf16[128,512]{1,0:T(8,128)(2,1)S(1)}, bf16[128,512]{1,0:T(8,128)(2,1)S(1)}, u32[]{:S(2)}, u32[]{:S(2)}) collective-permute-start(bf16[128,512]{1,0:T(8,128)(2,1)S(1)} %get-tuple-element.108), channel_id=1, source_target_pairs={{0,8},{1,9},{2,10},{3,11},{4,12},{5,13},{6,14},{7,15},{8,0},{9,1},... | collective-permute-start | bytes 393224 | tf_op jit(solution)/shard_map/ppermute | solution.py:29
  100.2 2.2 %token_grad.1 = bf16[128,2048]{1,0:T(8,128)(2,1)} custom-call(s32[7]{0:T(128)S(1)} %stack.32.place, bf16[128,512]{1,0:T(8,128)(2,1)S(1)} %latent_delta.1.first.refs_4_.delta, bf16[4,512,512]{2,1,0:T(8,128)(2,1)S(1)} %pack.1.held, bf16[4,512,512]{2,1,0:T(8,128)(2,1)S(1)} %collective-permute-done.28.arrived.others), custom_call_target="tpu_custom_call" | custom-call | tf_op jit(solution)/shard_map/token_grad/pallas_call | solution.py:45
  102.4 15.0 %collective-permute-done.31.refs_2_ = bf16[128,512]{1,0:T(8,128)(2,1)S(1)} collective-permute-done((bf16[128,512]{1,0:T(8,128)(2,1)S(1)}, bf16[128,512]{1,0:T(8,128)(2,1)S(1)}, u32[]{:S(2)}, u32[]{:S(2)}) %collective-permute-start.31) | collective-permute-done | bytes 131104 | tf_op jit(solution)/shard_map/ppermute | solution.py:29
  117.4 1.9 %last_sums.1 = (f32[128,512]{1,0:T(8,128)}, bf16[128,512]{1,0:T(8,128)(2,1)}, bf16[1,512,512]{2,1,0:T(8,128)(2,1)}, bf16[1,512,512]{2,1,0:T(8,128)(2,1)}) custom-call(s32[7]{0:T(128)S(1)} %stack.32.place, f32[2,512,512]{2,1,0:T(8,128)S(1)} %get-tuple-element.81.near, bf16[4,512,512]{2,1,0:T(8,128)(2,1)S(1)} %collective-permute-done.28.arrived.others, ...), custom_call_target="tpu_custom_call" | custom-call | tf_op jit(solution)/shard_map/last_sums/pallas_call | solution.py:45
  (70 shorter events, 27.3 us)
Async XLA Ops:
  2.7 10.1 %collective-permute-start.1 = (bf16[2,512,512]{2,1,0:T(8,128)(2,1)S(1)}, bf16[2,512,512]{2,1,0:T(8,128)(2,1)S(1)}, u32[]{:S(2)}, u32[]{:S(2)}) collective-permute-start(bf16[2,512,512]{2,1,0:T(8,128)(2,1)S(1)} %get-tuple-element.64.refs_8_), channel_id=1, source_target_pairs={{0,1},{1,0},{2,3},{3,2},{4,5},{5,4},{6,7},{7,6},{8,9},{9,8},{10,11... | collective-permute-start | bytes 3145736 | tf_op jit(solution)/shard_map/ppermute | solution.py:33
  3.3 9.5 %collective-permute-start = (bf16[2,128,512]{2,1,0:T(8,128)(2,1)S(1)}, bf16[2,128,512]{2,1,0:T(8,128)(2,1)S(1)}, u32[]{:S(2)}, u32[]{:S(2)}) collective-permute-start(bf16[2,128,512]{2,1,0:T(8,128)(2,1)S(1)} %get-tuple-element.62), channel_id=1, source_target_pairs={{0,2},{1,3},{2,0},{3,1},{4,6},{5,7},{6,4},{7,5},{8,10},{9,11},{10,... | collective-permute-start | bytes 786440 | tf_op jit(solution)/shard_map/ppermute | solution.py:33
  5.8 10.3 %collective-permute-start.4 = (bf16[128,512]{1,0:T(8,128)(2,1)}, bf16[128,512]{1,0:T(8,128)(2,1)S(1)}, u32[]{:S(2)}, u32[]{:S(2)}) collective-permute-start(bf16[128,512]{1,0:T(8,128)(2,1)} %refs_4_.1), channel_id=1, source_target_pairs={{0,4},{1,5},{2,6},{3,7},{4,0},{5,1},{6,2},{7,3},{8,12},{9,13},{10,... | collective-permute-start | bytes 393224 | tf_op jit(solution)/shard_map/ppermute | solution.py:29
  7.4 13.1 %collective-permute-start.5 = (bf16[128,512]{1,0:T(8,128)(2,1)}, bf16[128,512]{1,0:T(8,128)(2,1)S(1)}, u32[]{:S(2)}, u32[]{:S(2)}) collective-permute-start(bf16[128,512]{1,0:T(8,128)(2,1)} %refs_4_.1), channel_id=1, source_target_pairs={{0,8},{1,9},{2,10},{3,11},{4,12},{5,13},{6,14},{7,15},{8,0},{9,1},... | collective-permute-start | bytes 393224 | tf_op jit(solution)/shard_map/ppermute | solution.py:29
  10.0 10.5 %collective-permute-start.6 = (bf16[128,512]{1,0:T(8,128)(2,1)}, bf16[128,512]{1,0:T(8,128)(2,1)S(1)}, u32[]{:S(2)}, u32[]{:S(2)}) collective-permute-start(bf16[128,512]{1,0:T(8,128)(2,1)} %refs_4_.1), channel_id=1, source_target_pairs={{0,12},{1,13},{2,14},{3,15},{4,8},{5,9},{6,10},{7,11},{8,4},{9,5},... | collective-permute-start | bytes 393224 | tf_op jit(solution)/shard_map/ppermute | solution.py:29
  21.6 16.9 %collective-permute-start.9 = (bf16[512,512]{1,0:T(8,128)(2,1)S(1)}, bf16[512,512]{1,0:T(8,128)(2,1)S(1)}, u32[]{:S(2)}, u32[]{:S(2)}) collective-permute-start(bf16[512,512]{1,0:T(8,128)(2,1)S(1)} %bitcast.15), channel_id=1, source_target_pairs={{0,2},{1,3},{2,0},{3,1},{4,6},{5,7},{6,4},{7,5},{8,10},{9,11},{10,... | collective-permute-start | bytes 1572872 | tf_op jit(solution)/shard_map/ppermute | solution.py:33
  22.2 8.9 %collective-permute-start.10 = (bf16[144,512]{1,0:T(8,128)(2,1)S(1)}, bf16[144,512]{1,0:T(8,128)(2,1)S(1)}, u32[]{:S(2)}, u32[]{:S(2)}) collective-permute-start(bf16[144,512]{1,0:T(8,128)(2,1)S(1)} %payload.1.refs_7_), channel_id=1, source_target_pairs={{0,4},{1,5},{2,6},{3,7},{4,0},{5,1},{6,2},{7,3},{8,12},{9,13},{10,... | collective-permute-start | bytes 442376 | tf_op jit(solution)/shard_map/ppermute | solution.py:29
  24.6 13.9 %collective-permute-start.11 = (bf16[144,512]{1,0:T(8,128)(2,1)S(1)}, bf16[144,512]{1,0:T(8,128)(2,1)S(1)}, u32[]{:S(2)}, u32[]{:S(2)}) collective-permute-start(bf16[144,512]{1,0:T(8,128)(2,1)S(1)} %payload.1.refs_7_), channel_id=1, source_target_pairs={{0,8},{1,9},{2,10},{3,11},{4,12},{5,13},{6,14},{7,15},{8,0},{9,1},... | collective-permute-start | bytes 442376 | tf_op jit(solution)/shard_map/ppermute | solution.py:29
  25.6 13.0 %collective-permute-start.12 = (bf16[144,512]{1,0:T(8,128)(2,1)S(1)}, bf16[144,512]{1,0:T(8,128)(2,1)S(1)}, u32[]{:S(2)}, u32[]{:S(2)}) collective-permute-start(bf16[144,512]{1,0:T(8,128)(2,1)S(1)} %payload.1.refs_7_), channel_id=1, source_target_pairs={{0,12},{1,13},{2,14},{3,15},{4,8},{5,9},{6,10},{7,11},{8,4},{9,5},... | collective-permute-start | bytes 442376 | tf_op jit(solution)/shard_map/ppermute | solution.py:29
  27.6 11.1 %collective-permute-start.8 = (bf16[128,512]{1,0:T(8,128)(2,1)S(1)}, bf16[128,512]{1,0:T(8,128)(2,1)S(1)}, u32[]{:S(2)}, u32[]{:S(2)}) collective-permute-start(bf16[128,512]{1,0:T(8,128)(2,1)S(1)} %get-tuple-element.69), channel_id=1, source_target_pairs={{0,2},{1,3},{2,0},{3,1},{4,6},{5,7},{6,4},{7,5},{8,10},{9,11},{10,... | collective-permute-start | bytes 393224 | tf_op jit(solution)/shard_map/ppermute | solution.py:33
  39.4 15.9 %collective-permute-start.16 = (bf16[512,512]{1,0:T(8,128)(2,1)S(1)}, bf16[512,512]{1,0:T(8,128)(2,1)S(1)}, u32[]{:S(2)}, u32[]{:S(2)}) collective-permute-start(bf16[512,512]{1,0:T(8,128)(2,1)S(1)} %bitcast.16), channel_id=1, source_target_pairs={{0,2},{1,3},{2,0},{3,1},{4,6},{5,7},{6,4},{7,5},{8,10},{9,11},{10,... | collective-permute-start | bytes 1572872 | tf_op jit(solution)/shard_map/ppermute | solution.py:33
  43.3 11.9 %collective-permute-start.14 = (bf16[128,512]{1,0:T(8,128)(2,1)S(1)}, bf16[128,512]{1,0:T(8,128)(2,1)S(1)}, u32[]{:S(2)}, u32[]{:S(2)}) collective-permute-start(bf16[128,512]{1,0:T(8,128)(2,1)S(1)} %latent.1.refs_3_), channel_id=1, source_target_pairs={{0,8},{1,9},{2,10},{3,11},{4,12},{5,13},{6,14},{7,15},{8,0},{9,1},... | collective-permute-start | bytes 393224 | tf_op jit(solution)/shard_map/ppermute | solution.py:29
  44.3 10.9 %collective-permute-start.15 = (bf16[128,512]{1,0:T(8,128)(2,1)S(1)}, bf16[128,512]{1,0:T(8,128)(2,1)S(1)}, u32[]{:S(2)}, u32[]{:S(2)}) collective-permute-start(bf16[128,512]{1,0:T(8,128)(2,1)S(1)} %latent.1.refs_3_), channel_id=1, source_target_pairs={{0,12},{1,13},{2,14},{3,15},{4,8},{5,9},{6,10},{7,11},{8,4},{9,5},... | collective-permute-start | bytes 393224 | tf_op jit(solution)/shard_map/ppermute | solution.py:29
  45.8 9.4 %collective-permute-start.17 = (bf16[512,512]{1,0:T(8,128)(2,1)S(1)}, bf16[512,512]{1,0:T(8,128)(2,1)S(1)}, u32[]{:S(2)}, u32[]{:S(2)}) collective-permute-start(bf16[512,512]{1,0:T(8,128)(2,1)S(1)} %collective-permute-done.9.refs_10_), channel_id=1, source_target_pairs={{0,1},{1,0},{2,3},{3,2},{4,5},{5,4},{6,7},{7,6},{8,9},{9,8},{10,11... | collective-permute-start | bytes 1572872 | tf_op jit(solution)/shard_map/ppermute | solution.py:33
  66.4 18.1 %collective-permute-start.24 = (bf16[512,512]{1,0:T(8,128)(2,1)S(1)}, bf16[512,512]{1,0:T(8,128)(2,1)S(1)}, u32[]{:S(2)}, u32[]{:S(2)}) collective-permute-start(bf16[512,512]{1,0:T(8,128)(2,1)S(1)} %get-tuple-element.95.down), channel_id=1, source_target_pairs={{0,2},{1,3},{2,0},{3,1},{4,6},{5,7},{6,4},{7,5},{8,10},{9,11},{10,... | collective-permute-start | bytes 1572872 | tf_op jit(solution)/shard_map/ppermute | solution.py:33
  69.4 13.4 %collective-permute-start.21 = (bf16[128,512]{1,0:T(8,128)(2,1)S(1)}, bf16[128,512]{1,0:T(8,128)(2,1)S(1)}, u32[]{:S(2)}, u32[]{:S(2)}) collective-permute-start(bf16[128,512]{1,0:T(8,128)(2,1)S(1)} %get-tuple-element.88), channel_id=1, source_target_pairs={{0,8},{1,9},{2,10},{3,11},{4,12},{5,13},{6,14},{7,15},{8,0},{9,1},... | collective-permute-start | bytes 393224 | tf_op jit(solution)/shard_map/ppermute | solution.py:29
  70.9 11.9 %collective-permute-start.20 = (bf16[128,512]{1,0:T(8,128)(2,1)S(1)}, bf16[128,512]{1,0:T(8,128)(2,1)S(1)}, u32[]{:S(2)}, u32[]{:S(2)}) collective-permute-start(bf16[128,512]{1,0:T(8,128)(2,1)S(1)} %get-tuple-element.86), channel_id=1, source_target_pairs={{0,4},{1,5},{2,6},{3,7},{4,0},{5,1},{6,2},{7,3},{8,12},{9,13},{10,... | collective-permute-start | bytes 393224 | tf_op jit(solution)/shard_map/ppermute | solution.py:29
  72.6 19.6 %collective-permute-start.25 = (bf16[256,512]{1,0:T(8,128)(2,1)S(1)}, bf16[256,512]{1,0:T(8,128)(2,1)S(1)}, u32[]{:S(2)}, u32[]{:S(2)}) collective-permute-start(bf16[256,512]{1,0:T(8,128)(2,1)S(1)} %get-tuple-element.96), channel_id=1, source_target_pairs={{0,2},{1,3},{2,0},{3,1},{4,6},{5,7},{6,4},{7,5},{8,10},{9,11},{10,... | collective-permute-start | bytes 786440 | tf_op jit(solution)/shard_map/ppermute | solution.py:33
  83.4 8.8 %collective-permute-start.26 = (bf16[128,512]{1,0:T(8,128)(2,1)S(1)}, bf16[128,512]{1,0:T(8,128)(2,1)S(1)}, u32[]{:S(2)}, u32[]{:S(2)}) collective-permute-start(bf16[128,512]{1,0:T(8,128)(2,1)S(1)} %get-tuple-element.98), channel_id=1, source_target_pairs={{0,8},{1,9},{2,10},{3,11},{4,12},{5,13},{6,14},{7,15},{8,0},{9,1},... | collective-permute-start | bytes 393224 | tf_op jit(solution)/shard_map/ppermute | solution.py:29
  83.4 8.7 %collective-permute-start.23 = (bf16[128,512]{1,0:T(8,128)(2,1)S(1)}, bf16[128,512]{1,0:T(8,128)(2,1)S(1)}, u32[]{:S(2)}, u32[]{:S(2)}) collective-permute-start(bf16[128,512]{1,0:T(8,128)(2,1)S(1)} %latent_delta.1.first.refs_4_.delta), channel_id=1, source_target_pairs={{0,2},{1,3},{2,0},{3,1},{4,6},{5,7},{6,4},{7,5},{8,10},{9,11},{10,... | collective-permute-start | bytes 393224 | tf_op jit(solution)/shard_map/ppermute | solution.py:33
  95.7 21.7 %collective-permute-start.29 = (bf16[768,512]{1,0:T(8,128)(2,1)S(1)}, bf16[768,512]{1,0:T(8,128)(2,1)S(1)}, u32[]{:S(2)}, u32[]{:S(2)}) collective-permute-start(bf16[768,512]{1,0:T(8,128)(2,1)S(1)} %get-tuple-element.106), channel_id=1, source_target_pairs={{0,2},{1,3},{2,0},{3,1},{4,6},{5,7},{6,4},{7,5},{8,10},{9,11},{10,... | collective-permute-start | bytes 2359304 | tf_op jit(solution)/shard_map/ppermute | solution.py:33
  96.7 20.7 %collective-permute-start.30 = (bf16[2,128,512]{2,1,0:T(8,128)(2,1)S(1)}, bf16[2,128,512]{2,1,0:T(8,128)(2,1)S(1)}, u32[]{:S(2)}, u32[]{:S(2)}) collective-permute-start(bf16[2,128,512]{2,1,0:T(8,128)(2,1)S(1)} %get-tuple-element.102), channel_id=1, source_target_pairs={{0,4},{1,5},{2,6},{3,7},{4,0},{5,1},{6,2},{7,3},{8,12},{9,13},{10,... | collective-permute-start | bytes 786440 | tf_op jit(solution)/shard_map/ppermute | solution.py:29
  96.7 20.7 %collective-permute-start.32 = (bf16[2,128,512]{2,1,0:T(8,128)(2,1)S(1)}, bf16[2,128,512]{2,1,0:T(8,128)(2,1)S(1)}, u32[]{:S(2)}, u32[]{:S(2)}) collective-permute-start(bf16[2,128,512]{2,1,0:T(8,128)(2,1)S(1)} %get-tuple-element.109), channel_id=1, source_target_pairs={{0,12},{1,13},{2,14},{3,15},{4,8},{5,9},{6,10},{7,11},{8,4},{9,5},... | collective-permute-start | bytes 786440 | tf_op jit(solution)/shard_map/ppermute | solution.py:29
  98.0 19.4 %collective-permute-start.31 = (bf16[128,512]{1,0:T(8,128)(2,1)S(1)}, bf16[128,512]{1,0:T(8,128)(2,1)S(1)}, u32[]{:S(2)}, u32[]{:S(2)}) collective-permute-start(bf16[128,512]{1,0:T(8,128)(2,1)S(1)} %get-tuple-element.108), channel_id=1, source_target_pairs={{0,8},{1,9},{2,10},{3,11},{4,12},{5,13},{6,14},{7,15},{8,0},{9,1},... | collective-permute-start | bytes 393224 | tf_op jit(solution)/shard_map/ppermute | solution.py:29
  (15 other events, 131.7 us)

commit v17 on v15

--- a/solution.py
+++ b/solution.py
@@ -170,8 +170,8 @@
     outs = refs[2 * count + 6 :]
     *sums, hiddens, scaleds, back_pres = outs
     tok_rows, width = rows_in[0].shape
-    for first in range(0, count, 2):
-        group = range(first, min(first + 2, count))
+    for first in range(0, count, 4):
+        group = range(first, min(first + 4, count))
         span = slice(first * tok_rows, (first + len(group)) * tok_rows)
         stack = lambda values: jnp.concatenate(list(values), axis=0)
         rows = stack(rows_in[i][...] for i in group)

time: 115 us -> 115 us (level)
  no operation moved by 1% of the time
where the time goes in v17:
time: 115 us
  waiting for transfers between devices  49.2 us (43%)
  starting transfers between devices  40.7 us (35%)
  Pallas kernels  21.4 us (19%)
  local copies, waits for them, and re-layouts  2.39 us (2%)
    ppermute x16, waiting for transfers between devices, turn(): lax.ppermute(value, plane, device_pairs(n_line, lambda z, x, c: ((z + by)...  41.6 us
    ppermute x16, starting transfers between devices, turn(): lax.ppermute(value, plane, device_pairs(n_line, lambda z, x, c: ((z + by)...  29.8 us
    pallas_call x14, Pallas kernels, run(): pl.pallas_call(body, out_shape=outs, in_specs=[pl.BlockSpec(memory_space=...  21.4 us
    ppermute x17, starting transfers between devices, swap(): lax.ppermute(value, plane, device_pairs(n_line, lambda z, x, c: (z, x ^ s...  10.9 us
    ppermute x17, waiting for transfers between devices, swap(): lax.ppermute(value, plane, device_pairs(n_line, lambda z, x, c: (z, x ^ s...  7.61 us
  transfers between devices with their start and end apart: 33, of which 14 were waited for; matrix products, arithmetic and copies ran while one was open for 0% of the time, Pallas kernels for 5%

profile of v17, /device:TPU:0, one launch (start us, length us, event | category | flops | bytes accessed | tf_op | source)
XLA Modules:
  0.0 114.6 jit_solution(11634166972623588165)
XLA Ops:
  0.8 2.0 %columns.1 = (bf16[128,512]{1,0:T(8,128)(2,1)S(1)}, bf16[128,512]{1,0:T(8,128)(2,1)S(1)}, bf16[2,128,512]{2,1,0:T(8,128)(2,1)S(1)}, bf16[2,512,512]{2,1,0:T(8,128)(2,1)S(1)}) custom-call(s32[7]{0:T(128)S(1)} %stack.32.place, bf16[128,2048]{1,0:T(8,128)(2,1)} %tokens.1, bf16[1,512,512]{2,1,0:T(8,128)(2,1)} %expert_in.1, bf16[1,512,512]{2,1,0:T(8,128)(2,1)} %expert_out.1), custom_call_target="tpu_custom_call" | custom-call | tf_op jit(solution)/shard_map/columns/pallas_call | solution.py:45
  3.3 2.6 %collective-permute-start = (bf16[2,128,512]{2,1,0:T(8,128)(2,1)S(1)}, bf16[2,128,512]{2,1,0:T(8,128)(2,1)S(1)}, u32[]{:S(2)}, u32[]{:S(2)}) collective-permute-start(bf16[2,128,512]{2,1,0:T(8,128)(2,1)S(1)} %get-tuple-element.62), channel_id=1, source_target_pairs={{0,2},{1,3},{2,0},{3,1},{4,6},{5,7},{6,4},{7,5},{8,10},{9,11},{10,... | collective-permute-start | bytes 786440 | tf_op jit(solution)/shard_map/ppermute | solution.py:33
  5.8 1.6 %collective-permute-start.4 = (bf16[128,512]{1,0:T(8,128)(2,1)}, bf16[128,512]{1,0:T(8,128)(2,1)S(1)}, u32[]{:S(2)}, u32[]{:S(2)}) collective-permute-start(bf16[128,512]{1,0:T(8,128)(2,1)} %refs_4_.1), channel_id=1, source_target_pairs={{0,4},{1,5},{2,6},{3,7},{4,8},{5,9},{6,10},{7,11},{8,12},{9,13},{1... | collective-permute-start | bytes 393224 | tf_op jit(solution)/shard_map/ppermute | solution.py:29
  7.4 2.6 %collective-permute-start.5 = (bf16[128,512]{1,0:T(8,128)(2,1)}, bf16[128,512]{1,0:T(8,128)(2,1)S(1)}, u32[]{:S(2)}, u32[]{:S(2)}) collective-permute-start(bf16[128,512]{1,0:T(8,128)(2,1)} %refs_4_.1), channel_id=1, source_target_pairs={{0,8},{1,9},{2,10},{3,11},{4,12},{5,13},{6,14},{7,15},{8,0},{9,1},... | collective-permute-start | bytes 393224 | tf_op jit(solution)/shard_map/ppermute | solution.py:29
  16.2 3.0 %collective-permute-done.5.refs_6_ = bf16[128,512]{1,0:T(8,128)(2,1)S(1)} collective-permute-done((bf16[128,512]{1,0:T(8,128)(2,1)}, bf16[128,512]{1,0:T(8,128)(2,1)S(1)}, u32[]{:S(2)}, u32[]{:S(2)}) %collective-permute-start.5) | collective-permute-done | bytes 131104 | tf_op jit(solution)/shard_map/ppermute | solution.py:29
  20.9 3.3 %collective-permute-start.10 = (bf16[144,512]{1,0:T(8,128)(2,1)S(1)}, bf16[144,512]{1,0:T(8,128)(2,1)S(1)}, u32[]{:S(2)}, u32[]{:S(2)}) collective-permute-start(bf16[144,512]{1,0:T(8,128)(2,1)S(1)} %payload.1.refs_7_), channel_id=1, source_target_pairs={{0,4},{1,5},{2,6},{3,7},{4,8},{5,9},{6,10},{7,11},{8,12},{9,13},{1... | collective-permute-start | bytes 442376 | tf_op jit(solution)/shard_map/ppermute | solution.py:29
  24.2 1.6 %collective-permute-start.11 = (bf16[144,512]{1,0:T(8,128)(2,1)S(1)}, bf16[144,512]{1,0:T(8,128)(2,1)S(1)}, u32[]{:S(2)}, u32[]{:S(2)}) collective-permute-start(bf16[144,512]{1,0:T(8,128)(2,1)S(1)} %payload.1.refs_7_), channel_id=1, source_target_pairs={{0,8},{1,9},{2,10},{3,11},{4,12},{5,13},{6,14},{7,15},{8,0},{9,1},... | collective-permute-start | bytes 442376 | tf_op jit(solution)/shard_map/ppermute | solution.py:29
  30.0 5.9 %collective-permute-done.11.refs_5_ = bf16[144,512]{1,0:T(8,128)(2,1)S(1)} collective-permute-done((bf16[144,512]{1,0:T(8,128)(2,1)S(1)}, bf16[144,512]{1,0:T(8,128)(2,1)S(1)}, u32[]{:S(2)}, u32[]{:S(2)}) %collective-permute-start.11) | collective-permute-done | bytes 147488 | tf_op jit(solution)/shard_map/ppermute | solution.py:29
  35.8 1.6 %collective-permute-done.8.refs_1_ = bf16[128,512]{1,0:T(8,128)(2,1)S(1)} collective-permute-done((bf16[128,512]{1,0:T(8,128)(2,1)S(1)}, bf16[128,512]{1,0:T(8,128)(2,1)S(1)}, u32[]{:S(2)}, u32[]{:S(2)}) %collective-permute-start.8) | collective-permute-done | bytes 131104 | tf_op jit(solution)/shard_map/ppermute | solution.py:33
  38.6 3.3 %collective-permute-start.13 = (bf16[128,512]{1,0:T(8,128)(2,1)S(1)}, bf16[128,512]{1,0:T(8,128)(2,1)S(1)}, u32[]{:S(2)}, u32[]{:S(2)}) collective-permute-start(bf16[128,512]{1,0:T(8,128)(2,1)S(1)} %latent.1.refs_3_), channel_id=1, source_target_pairs={{0,4},{1,5},{2,6},{3,7},{4,8},{5,9},{6,10},{7,11},{8,12},{9,13},{1... | collective-permute-start | bytes 393224 | tf_op jit(solution)/shard_map/ppermute | solution.py:29
  41.9 1.6 %collective-permute-start.14 = (bf16[128,512]{1,0:T(8,128)(2,1)S(1)}, bf16[128,512]{1,0:T(8,128)(2,1)S(1)}, u32[]{:S(2)}, u32[]{:S(2)}) collective-permute-start(bf16[128,512]{1,0:T(8,128)(2,1)S(1)} %latent.1.refs_3_), channel_id=1, source_target_pairs={{0,8},{1,9},{2,10},{3,11},{4,12},{5,13},{6,14},{7,15},{8,0},{9,1},... | collective-permute-start | bytes 393224 | tf_op jit(solution)/shard_map/ppermute | solution.py:29
  44.3 3.2 %collective-permute-done.13.refs_0_ = bf16[128,512]{1,0:T(8,128)(2,1)S(1)} collective-permute-done((bf16[128,512]{1,0:T(8,128)(2,1)S(1)}, bf16[128,512]{1,0:T(8,128)(2,1)S(1)}, u32[]{:S(2)}, u32[]{:S(2)}) %collective-permute-start.13) | collective-permute-done | bytes 131104 | tf_op jit(solution)/shard_map/ppermute | solution.py:29
  47.5 4.3 %collective-permute-done.14.refs_1_ = bf16[128,512]{1,0:T(8,128)(2,1)S(1)} collective-permute-done((bf16[128,512]{1,0:T(8,128)(2,1)S(1)}, bf16[128,512]{1,0:T(8,128)(2,1)S(1)}, u32[]{:S(2)}, u32[]{:S(2)}) %collective-permute-start.14) | collective-permute-done | bytes 131104 | tf_op jit(solution)/shard_map/ppermute | solution.py:29
  51.8 1.9 %collective-permute-done.18.refs_13_ = bf16[512,512]{1,0:T(8,128)(2,1)S(1)} collective-permute-done((bf16[512,512]{1,0:T(8,128)(2,1)S(1)}, bf16[512,512]{1,0:T(8,128)(2,1)S(1)}, u32[]{:S(2)}, u32[]{:S(2)}) %collective-permute-start.18) | collective-permute-done | bytes 524320 | tf_op jit(solution)/shard_map/ppermute | solution.py:33
  53.7 5.9 %experts.1 = (bf16[128,512]{1,0:T(8,128)(2,1)S(1)}, bf16[128,512]{1,0:T(8,128)(2,1)S(1)}, bf16[128,512]{1,0:T(8,128)(2,1)S(1)}, bf16[128,512]{1,0:T(8,128)(2,1)S...) custom-call(s32[7]{0:T(128)S(1)} %stack.32.place, ...), custom_call_target="tpu_custom_call" | custom-call | tf_op jit(solution)/shard_map/experts/pallas_call | solution.py:45
  59.6 2.9 %weight_grads.1 = (f32[2,512,512]{2,1,0:T(8,128)S(1)}, f32[2,512,512]{2,1,0:T(8,128)S(1)}, bf16[2,512,512]{2,1,0:T(8,128)(2,1)S(1)}, bf16[2,512,512]{2,1,0:T(8,128)(2,1)S(1)}) custom-call(s32[7]{0:T(128)S(1)} %stack.32.place, bf16[128,512]{1,0:T(8,128)(2,1)S(1)} %collective-permute-done.13.refs_0_, bf16[128,512]{1,0:T(8,128)(2,1)S(1)} %collective-permute-done.14.refs_1_, ...), custom_call_target="tpu_custom_call" | custom-call | flops 2147483648 | tf_op jit(solution)/shard_map/weight_grads/pallas_call | solution.py:45
  64.3 3.2 %collective-permute-start.22 = (bf16[128,512]{1,0:T(8,128)(2,1)S(1)}, bf16[128,512]{1,0:T(8,128)(2,1)S(1)}, u32[]{:S(2)}, u32[]{:S(2)}) collective-permute-start(bf16[128,512]{1,0:T(8,128)(2,1)S(1)} %get-tuple-element.90), channel_id=1, source_target_pairs={{0,4},{1,5},{2,6},{3,7},{4,8},{5,9},{6,10},{7,11},{8,12},{9,13},{1... | collective-permute-start | bytes 393224 | tf_op jit(solution)/shard_map/ppermute | solution.py:29
  72.6 5.1 %collective-permute-done.21.refs_2_ = bf16[128,512]{1,0:T(8,128)(2,1)S(1)} collective-permute-done((bf16[128,512]{1,0:T(8,128)(2,1)S(1)}, bf16[128,512]{1,0:T(8,128)(2,1)S(1)}, u32[]{:S(2)}, u32[]{:S(2)}) %collective-permute-start.21) | collective-permute-done | bytes 131104 | tf_op jit(solution)/shard_map/ppermute | solution.py:29
  78.3 2.3 %collective-permute-start.26 = (bf16[128,512]{1,0:T(8,128)(2,1)S(1)}, bf16[128,512]{1,0:T(8,128)(2,1)S(1)}, u32[]{:S(2)}, u32[]{:S(2)}) collective-permute-start(bf16[128,512]{1,0:T(8,128)(2,1)S(1)} %get-tuple-element.98), channel_id=1, source_target_pairs={{0,8},{1,9},{2,10},{3,11},{4,12},{5,13},{6,14},{7,15},{8,0},{9,1},... | collective-permute-start | bytes 393224 | tf_op jit(solution)/shard_map/ppermute | solution.py:29
  82.0 2.6 %collective-permute-done.26.refs_5_ = bf16[128,512]{1,0:T(8,128)(2,1)S(1)} collective-permute-done((bf16[128,512]{1,0:T(8,128)(2,1)S(1)}, bf16[128,512]{1,0:T(8,128)(2,1)S(1)}, u32[]{:S(2)}, u32[]{:S(2)}) %collective-permute-start.26) | collective-permute-done | bytes 131104 | tf_op jit(solution)/shard_map/ppermute | solution.py:29
  90.5 4.5 %collective-permute-start.30 = (bf16[2,128,512]{2,1,0:T(8,128)(2,1)S(1)}, bf16[2,128,512]{2,1,0:T(8,128)(2,1)S(1)}, u32[]{:S(2)}, u32[]{:S(2)}) collective-permute-start(bf16[2,128,512]{2,1,0:T(8,128)(2,1)S(1)} %get-tuple-element.102), channel_id=1, source_target_pairs={{0,12},{1,13},{2,14},{3,15},{4,0},{5,1},{6,2},{7,3},{8,4},{9,5},{1... | collective-permute-start | bytes 786440 | tf_op jit(solution)/shard_map/ppermute | solution.py:29
  95.5 2.2 %token_grad.1 = bf16[128,2048]{1,0:T(8,128)(2,1)} custom-call(s32[7]{0:T(128)S(1)} %stack.32.place, bf16[128,512]{1,0:T(8,128)(2,1)S(1)} %latent_delta.1.first.refs_4_.delta, bf16[4,512,512]{2,1,0:T(8,128)(2,1)S(1)} %pack.1.held, bf16[4,512,512]{2,1,0:T(8,128)(2,1)S(1)} %collective-permute-done.28.arrived.others), custom_call_target="tpu_custom_call" | custom-call | tf_op jit(solution)/shard_map/token_grad/pallas_call | solution.py:45
  97.7 14.9 %collective-permute-done.31.refs_2_ = bf16[128,512]{1,0:T(8,128)(2,1)S(1)} collective-permute-done((bf16[128,512]{1,0:T(8,128)(2,1)S(1)}, bf16[128,512]{1,0:T(8,128)(2,1)S(1)}, u32[]{:S(2)}, u32[]{:S(2)}) %collective-permute-start.31) | collective-permute-done | bytes 131104 | tf_op jit(solution)/shard_map/ppermute | solution.py:29
  112.7 1.9 %last_sums.1 = (f32[128,512]{1,0:T(8,128)}, bf16[128,512]{1,0:T(8,128)(2,1)}, bf16[1,512,512]{2,1,0:T(8,128)(2,1)}, bf16[1,512,512]{2,1,0:T(8,128)(2,1)}) custom-call(s32[7]{0:T(128)S(1)} %stack.32.place, f32[2,512,512]{2,1,0:T(8,128)S(1)} %get-tuple-element.81.near, bf16[4,512,512]{2,1,0:T(8,128)(2,1)S(1)} %collective-permute-done.28.arrived.others, ...), custom_call_target="tpu_custom_call" | custom-call | tf_op jit(solution)/shard_map/last_sums/pallas_call | solution.py:45
  (70 shorter events, 29.8 us)
Async XLA Ops:
  2.7 10.1 %collective-permute-start.1 = (bf16[2,512,512]{2,1,0:T(8,128)(2,1)S(1)}, bf16[2,512,512]{2,1,0:T(8,128)(2,1)S(1)}, u32[]{:S(2)}, u32[]{:S(2)}) collective-permute-start(bf16[2,512,512]{2,1,0:T(8,128)(2,1)S(1)} %get-tuple-element.64.refs_8_), channel_id=1, source_target_pairs={{0,1},{1,0},{2,3},{3,2},{4,5},{5,4},{6,7},{7,6},{8,9},{9,8},{10,11... | collective-permute-start | bytes 3145736 | tf_op jit(solution)/shard_map/ppermute | solution.py:33
  3.3 9.5 %collective-permute-start = (bf16[2,128,512]{2,1,0:T(8,128)(2,1)S(1)}, bf16[2,128,512]{2,1,0:T(8,128)(2,1)S(1)}, u32[]{:S(2)}, u32[]{:S(2)}) collective-permute-start(bf16[2,128,512]{2,1,0:T(8,128)(2,1)S(1)} %get-tuple-element.62), channel_id=1, source_target_pairs={{0,2},{1,3},{2,0},{3,1},{4,6},{5,7},{6,4},{7,5},{8,10},{9,11},{10,... | collective-permute-start | bytes 786440 | tf_op jit(solution)/shard_map/ppermute | solution.py:33
  5.8 10.3 %collective-permute-start.4 = (bf16[128,512]{1,0:T(8,128)(2,1)}, bf16[128,512]{1,0:T(8,128)(2,1)S(1)}, u32[]{:S(2)}, u32[]{:S(2)}) collective-permute-start(bf16[128,512]{1,0:T(8,128)(2,1)} %refs_4_.1), channel_id=1, source_target_pairs={{0,4},{1,5},{2,6},{3,7},{4,8},{5,9},{6,10},{7,11},{8,12},{9,13},{1... | collective-permute-start | bytes 393224 | tf_op jit(solution)/shard_map/ppermute | solution.py:29
  7.4 11.8 %collective-permute-start.5 = (bf16[128,512]{1,0:T(8,128)(2,1)}, bf16[128,512]{1,0:T(8,128)(2,1)S(1)}, u32[]{:S(2)}, u32[]{:S(2)}) collective-permute-start(bf16[128,512]{1,0:T(8,128)(2,1)} %refs_4_.1), channel_id=1, source_target_pairs={{0,8},{1,9},{2,10},{3,11},{4,12},{5,13},{6,14},{7,15},{8,0},{9,1},... | collective-permute-start | bytes 393224 | tf_op jit(solution)/shard_map/ppermute | solution.py:29
  10.0 9.2 %collective-permute-start.6 = (bf16[128,512]{1,0:T(8,128)(2,1)}, bf16[128,512]{1,0:T(8,128)(2,1)S(1)}, u32[]{:S(2)}, u32[]{:S(2)}) collective-permute-start(bf16[128,512]{1,0:T(8,128)(2,1)} %refs_4_.1), channel_id=1, source_target_pairs={{0,12},{1,13},{2,14},{3,15},{4,0},{5,1},{6,2},{7,3},{8,4},{9,5},{1... | collective-permute-start | bytes 393224 | tf_op jit(solution)/shard_map/ppermute | solution.py:29
  20.3 15.5 %collective-permute-start.9 = (bf16[512,512]{1,0:T(8,128)(2,1)S(1)}, bf16[512,512]{1,0:T(8,128)(2,1)S(1)}, u32[]{:S(2)}, u32[]{:S(2)}) collective-permute-start(bf16[512,512]{1,0:T(8,128)(2,1)S(1)} %bitcast.15), channel_id=1, source_target_pairs={{0,2},{1,3},{2,0},{3,1},{4,6},{5,7},{6,4},{7,5},{8,10},{9,11},{10,... | collective-permute-start | bytes 1572872 | tf_op jit(solution)/shard_map/ppermute | solution.py:33
  20.9 9.1 %collective-permute-start.10 = (bf16[144,512]{1,0:T(8,128)(2,1)S(1)}, bf16[144,512]{1,0:T(8,128)(2,1)S(1)}, u32[]{:S(2)}, u32[]{:S(2)}) collective-permute-start(bf16[144,512]{1,0:T(8,128)(2,1)S(1)} %payload.1.refs_7_), channel_id=1, source_target_pairs={{0,4},{1,5},{2,6},{3,7},{4,8},{5,9},{6,10},{7,11},{8,12},{9,13},{1... | collective-permute-start | bytes 442376 | tf_op jit(solution)/shard_map/ppermute | solution.py:29
  24.2 11.7 %collective-permute-start.11 = (bf16[144,512]{1,0:T(8,128)(2,1)S(1)}, bf16[144,512]{1,0:T(8,128)(2,1)S(1)}, u32[]{:S(2)}, u32[]{:S(2)}) collective-permute-start(bf16[144,512]{1,0:T(8,128)(2,1)S(1)} %payload.1.refs_7_), channel_id=1, source_target_pairs={{0,8},{1,9},{2,10},{3,11},{4,12},{5,13},{6,14},{7,15},{8,0},{9,1},... | collective-permute-start | bytes 442376 | tf_op jit(solution)/shard_map/ppermute | solution.py:29
  25.8 10.0 %collective-permute-start.12 = (bf16[144,512]{1,0:T(8,128)(2,1)S(1)}, bf16[144,512]{1,0:T(8,128)(2,1)S(1)}, u32[]{:S(2)}, u32[]{:S(2)}) collective-permute-start(bf16[144,512]{1,0:T(8,128)(2,1)S(1)} %payload.1.refs_7_), channel_id=1, source_target_pairs={{0,12},{1,13},{2,14},{3,15},{4,0},{5,1},{6,2},{7,3},{8,4},{9,5},{1... | collective-permute-start | bytes 442376 | tf_op jit(solution)/shard_map/ppermute | solution.py:29
  27.2 10.3 %collective-permute-start.8 = (bf16[128,512]{1,0:T(8,128)(2,1)S(1)}, bf16[128,512]{1,0:T(8,128)(2,1)S(1)}, u32[]{:S(2)}, u32[]{:S(2)}) collective-permute-start(bf16[128,512]{1,0:T(8,128)(2,1)S(1)} %get-tuple-element.69), channel_id=1, source_target_pairs={{0,2},{1,3},{2,0},{3,1},{4,6},{5,7},{6,4},{7,5},{8,10},{9,11},{10,... | collective-permute-start | bytes 393224 | tf_op jit(solution)/shard_map/ppermute | solution.py:33
  38.0 13.7 %collective-permute-start.16 = (bf16[512,512]{1,0:T(8,128)(2,1)S(1)}, bf16[512,512]{1,0:T(8,128)(2,1)S(1)}, u32[]{:S(2)}, u32[]{:S(2)}) collective-permute-start(bf16[512,512]{1,0:T(8,128)(2,1)S(1)} %bitcast.16), channel_id=1, source_target_pairs={{0,2},{1,3},{2,0},{3,1},{4,6},{5,7},{6,4},{7,5},{8,10},{9,11},{10,... | collective-permute-start | bytes 1572872 | tf_op jit(solution)/shard_map/ppermute | solution.py:33
  38.6 8.8 %collective-permute-start.13 = (bf16[128,512]{1,0:T(8,128)(2,1)S(1)}, bf16[128,512]{1,0:T(8,128)(2,1)S(1)}, u32[]{:S(2)}, u32[]{:S(2)}) collective-permute-start(bf16[128,512]{1,0:T(8,128)(2,1)S(1)} %latent.1.refs_3_), channel_id=1, source_target_pairs={{0,4},{1,5},{2,6},{3,7},{4,8},{5,9},{6,10},{7,11},{8,12},{9,13},{1... | collective-permute-start | bytes 393224 | tf_op jit(solution)/shard_map/ppermute | solution.py:29
  41.9 9.8 %collective-permute-start.14 = (bf16[128,512]{1,0:T(8,128)(2,1)S(1)}, bf16[128,512]{1,0:T(8,128)(2,1)S(1)}, u32[]{:S(2)}, u32[]{:S(2)}) collective-permute-start(bf16[128,512]{1,0:T(8,128)(2,1)S(1)} %latent.1.refs_3_), channel_id=1, source_target_pairs={{0,8},{1,9},{2,10},{3,11},{4,12},{5,13},{6,14},{7,15},{8,0},{9,1},... | collective-permute-start | bytes 393224 | tf_op jit(solution)/shard_map/ppermute | solution.py:29
  43.5 8.2 %collective-permute-start.15 = (bf16[128,512]{1,0:T(8,128)(2,1)S(1)}, bf16[128,512]{1,0:T(8,128)(2,1)S(1)}, u32[]{:S(2)}, u32[]{:S(2)}) collective-permute-start(bf16[128,512]{1,0:T(8,128)(2,1)S(1)} %latent.1.refs_3_), channel_id=1, source_target_pairs={{0,12},{1,13},{2,14},{3,15},{4,0},{5,1},{6,2},{7,3},{8,4},{9,5},{1... | collective-permute-start | bytes 393224 | tf_op jit(solution)/shard_map/ppermute | solution.py:29
  44.3 7.5 %collective-permute-start.17 = (bf16[512,512]{1,0:T(8,128)(2,1)S(1)}, bf16[512,512]{1,0:T(8,128)(2,1)S(1)}, u32[]{:S(2)}, u32[]{:S(2)}) collective-permute-start(bf16[512,512]{1,0:T(8,128)(2,1)S(1)} %collective-permute-done.9.refs_10_), channel_id=1, source_target_pairs={{0,1},{1,0},{2,3},{3,2},{4,5},{5,4},{6,7},{7,6},{8,9},{9,8},{10,11... | collective-permute-start | bytes 1572872 | tf_op jit(solution)/shard_map/ppermute | solution.py:33
  62.8 18.6 %collective-permute-start.24 = (bf16[512,512]{1,0:T(8,128)(2,1)S(1)}, bf16[512,512]{1,0:T(8,128)(2,1)S(1)}, u32[]{:S(2)}, u32[]{:S(2)}) collective-permute-start(bf16[512,512]{1,0:T(8,128)(2,1)S(1)} %get-tuple-element.95.down), channel_id=1, source_target_pairs={{0,2},{1,3},{2,0},{3,1},{4,6},{5,7},{6,4},{7,5},{8,10},{9,11},{10,... | collective-permute-start | bytes 1572872 | tf_op jit(solution)/shard_map/ppermute | solution.py:33
  64.3 8.4 %collective-permute-start.22 = (bf16[128,512]{1,0:T(8,128)(2,1)S(1)}, bf16[128,512]{1,0:T(8,128)(2,1)S(1)}, u32[]{:S(2)}, u32[]{:S(2)}) collective-permute-start(bf16[128,512]{1,0:T(8,128)(2,1)S(1)} %get-tuple-element.90), channel_id=1, source_target_pairs={{0,4},{1,5},{2,6},{3,7},{4,8},{5,9},{6,10},{7,11},{8,12},{9,13},{1... | collective-permute-start | bytes 393224 | tf_op jit(solution)/shard_map/ppermute | solution.py:29
  67.5 10.2 %collective-permute-start.21 = (bf16[128,512]{1,0:T(8,128)(2,1)S(1)}, bf16[128,512]{1,0:T(8,128)(2,1)S(1)}, u32[]{:S(2)}, u32[]{:S(2)}) collective-permute-start(bf16[128,512]{1,0:T(8,128)(2,1)S(1)} %get-tuple-element.88), channel_id=1, source_target_pairs={{0,8},{1,9},{2,10},{3,11},{4,12},{5,13},{6,14},{7,15},{8,0},{9,1},... | collective-permute-start | bytes 393224 | tf_op jit(solution)/shard_map/ppermute | solution.py:29
  68.8 8.9 %collective-permute-start.20 = (bf16[128,512]{1,0:T(8,128)(2,1)S(1)}, bf16[128,512]{1,0:T(8,128)(2,1)S(1)}, u32[]{:S(2)}, u32[]{:S(2)}) collective-permute-start(bf16[128,512]{1,0:T(8,128)(2,1)S(1)} %get-tuple-element.86), channel_id=1, source_target_pairs={{0,12},{1,13},{2,14},{3,15},{4,0},{5,1},{6,2},{7,3},{8,4},{9,5},{1... | collective-permute-start | bytes 393224 | tf_op jit(solution)/shard_map/ppermute | solution.py:29
  70.6 14.0 %collective-permute-start.25 = (bf16[256,512]{1,0:T(8,128)(2,1)S(1)}, bf16[256,512]{1,0:T(8,128)(2,1)S(1)}, u32[]{:S(2)}, u32[]{:S(2)}) collective-permute-start(bf16[256,512]{1,0:T(8,128)(2,1)S(1)} %get-tuple-element.96), channel_id=1, source_target_pairs={{0,2},{1,3},{2,0},{3,1},{4,6},{5,7},{6,4},{7,5},{8,10},{9,11},{10,... | collective-permute-start | bytes 786440 | tf_op jit(solution)/shard_map/ppermute | solution.py:33
  89.3 23.3 %collective-permute-start.29 = (bf16[768,512]{1,0:T(8,128)(2,1)S(1)}, bf16[768,512]{1,0:T(8,128)(2,1)S(1)}, u32[]{:S(2)}, u32[]{:S(2)}) collective-permute-start(bf16[768,512]{1,0:T(8,128)(2,1)S(1)} %get-tuple-element.106), channel_id=1, source_target_pairs={{0,2},{1,3},{2,0},{3,1},{4,6},{5,7},{6,4},{7,5},{8,10},{9,11},{10,... | collective-permute-start | bytes 2359304 | tf_op jit(solution)/shard_map/ppermute | solution.py:33
  90.5 22.2 %collective-permute-start.30 = (bf16[2,128,512]{2,1,0:T(8,128)(2,1)S(1)}, bf16[2,128,512]{2,1,0:T(8,128)(2,1)S(1)}, u32[]{:S(2)}, u32[]{:S(2)}) collective-permute-start(bf16[2,128,512]{2,1,0:T(8,128)(2,1)S(1)} %get-tuple-element.102), channel_id=1, source_target_pairs={{0,12},{1,13},{2,14},{3,15},{4,0},{5,1},{6,2},{7,3},{8,4},{9,5},{1... | collective-permute-start | bytes 786440 | tf_op jit(solution)/shard_map/ppermute | solution.py:29
  95.0 17.7 %collective-permute-start.32 = (bf16[2,128,512]{2,1,0:T(8,128)(2,1)S(1)}, bf16[2,128,512]{2,1,0:T(8,128)(2,1)S(1)}, u32[]{:S(2)}, u32[]{:S(2)}) collective-permute-start(bf16[2,128,512]{2,1,0:T(8,128)(2,1)S(1)} %get-tuple-element.109), channel_id=1, source_target_pairs={{0,4},{1,5},{2,6},{3,7},{4,8},{5,9},{6,10},{7,11},{8,12},{9,13},{1... | collective-permute-start | bytes 786440 | tf_op jit(solution)/shard_map/ppermute | solution.py:29
  95.0 17.7 %collective-permute-start.31 = (bf16[128,512]{1,0:T(8,128)(2,1)S(1)}, bf16[128,512]{1,0:T(8,128)(2,1)S(1)}, u32[]{:S(2)}, u32[]{:S(2)}) collective-permute-start(bf16[128,512]{1,0:T(8,128)(2,1)S(1)} %get-tuple-element.108), channel_id=1, source_target_pairs={{0,8},{1,9},{2,10},{3,11},{4,12},{5,13},{6,14},{7,15},{8,0},{9,1},... | collective-permute-start | bytes 393224 | tf_op jit(solution)/shard_map/ppermute | solution.py:29
  (15 other events, 125.6 us)

commit v18 on v17

--- a/solution.py
+++ b/solution.py
@@ -202,20 +202,18 @@
             out[...] = out_sum[part].astype(out.dtype)
 
 
-def weight_grad_body(n_rows, n_sets, place, *refs):
+def weight_grad_body(side, n_rows, n_sets, place, *refs):
     rows_in = refs[:n_rows]
     sets = [refs[n_rows + 3 * i : n_rows + 3 * i + 3] for i in range(n_sets)]
-    near, far, near_other, far_other = refs[n_rows + 3 * n_sets :]
+    outs = refs[n_rows + 3 * n_sets :]
     dot = functools.partial(lax.dot_general, dimension_numbers=contract_first, preferred_element_type=wide)
     rows = jnp.concatenate([r[...] for r in rows_in], axis=0)
-    for core in (1, 0):
-        for side in (1, 0):
-            hidden, scaled, back_pre = (
-                jnp.concatenate([values[i][core * 2 + side] for values in sets], axis=0) for i in range(3)
-            )
-            grad_in, grad_out = dot(rows, back_pre), dot(hidden, scaled)
-            out = ((near, far), (near_other, far_other))[core][side]
-            out[0], out[1] = grad_in.astype(out.dtype), grad_out.astype(out.dtype)
+    for core, out in enumerate(outs):
+        hidden, scaled, back_pre = (
+            jnp.concatenate([values[i][core * 2 + side] for values in sets], axis=0) for i in range(3)
+        )
+        out[0] = dot(rows, back_pre).astype(out.dtype)
+        out[1] = dot(hidden, scaled).astype(out.dtype)
 
 
 def down_grad_body(n_line, place, *refs):
@@ -330,27 +328,32 @@
     delta_lines = [home(value, back) for back, value in enumerate(deltas_of)]
 
     pair = (2, latent_width, hidden_width)
-    near, far, near_other, far_other = call(
-        functools.partial(weight_grad_body, n_line, len(groups)),
-        [shape(pair, wide)] * 2 + [shape(pair, narrow)] * 2,
-        "weight_grads",
-        flops=2 * 8 * n_line * tok_rows * latent_width * hidden_width,
-    )(
-        place,
-        *(rows[i] for group in groups for i in group),
-        *(value for values in saved for value in values),
-    )
+
+    def weight_grads(side, *earlier):
+        return call(
+            functools.partial(weight_grad_body, side, n_line, len(groups)),
+            [shape(pair, wide), shape(pair, narrow)],
+            "weight_grads",
+            flops=2 * 4 * n_line * tok_rows * latent_width * hidden_width,
+        )(
+            after(place, *earlier),
+            *(rows[i] for group in groups for i in group),
+            *(value for values in saved for value in values),
+        )
+
+    far, far_other = weight_grads(1)
     far_other = swap(far_other, n_line, 1, 0)
     ahead = latent_width // 2
     far_first, far_rest = call(
         far_body, [shape((rows, hidden_width), narrow) for rows in (ahead, 2 * latent_width - ahead)], "far_grads"
     )(place, far, far_other)
     far_first = swap(far_first, n_line, 0, 1)
-    delta_lines = [after(line, near, far_rest) for line in delta_lines]
+    delta_lines = [after(line, far_rest) for line in delta_lines]
     (delta,) = call(add_body, [rows_of(narrow)], "latent_delta")(place, *delta_lines)
     side_delta = swap(delta, n_line, 0, 1)
     out_lines = [outs_of[0]] + [home(after(outs_of[back], delta), back) if back not in riding else None for back in range(1, n_line)]
     far_rest = swap(after(far_rest, side_delta), n_line, 0, 1)
+    near, near_other = weight_grads(0, delta)
     (others,) = call(pack_body, [shape((4, latent_width, hidden_width), narrow)], "pack")(
         after(place, delta), near_other, down, side_down
     )

time: 115 us -> 114 us (level)
  waiting for transfers between devices: 49.2 us -> 47.4 us
    ppermute x16, waiting for transfers between devices: 41.6 us -> 39.8 us  [turn(): lax.ppermute(value, plane, device_pairs(n_line, lambda z, x, c: ((z + by)...]
    pallas_call x14 -> x15, Pallas kernels: 21.4 us -> 22.2 us  [run(): pl.pallas_call(body, out_shape=outs, in_specs=[pl.BlockSpec(memory_space=...]
  transfers between devices with their start and end apart: 33 -> 33, of which waited for: 14 -> 14; matrix products, arithmetic and copies ran while one was open for 0% -> 0% of each run, Pallas kernels for 5% -> 6%
where the time goes in v18:
time: 114 us
  waiting for transfers between devices  47.4 us (42%)
  starting transfers between devices  40.7 us (36%)
  Pallas kernels  22.2 us (19%)
  local copies, waits for them, and re-layouts  2.39 us (2%)
    ppermute x16, waiting for transfers between devices, turn(): lax.ppermute(value, plane, device_pairs(n_line, lambda z, x, c: ((z + by)...  39.8 us
    ppermute x16, starting transfers between devices, turn(): lax.ppermute(value, plane, device_pairs(n_line, lambda z, x, c: ((z + by)...  29.8 us
    pallas_call x15, Pallas kernels, run(): pl.pallas_call(body, out_shape=outs, in_specs=[pl.BlockSpec(memory_space=...  22.2 us
    ppermute x17, starting transfers between devices, swap(): lax.ppermute(value, plane, device_pairs(n_line, lambda z, x, c: (z, x ^ s...  10.9 us
    ppermute x17, waiting for transfers between devices, swap(): lax.ppermute(value, plane, device_pairs(n_line, lambda z, x, c: (z, x ^ s...  7.61 us
    unnamed x12, local copies, waits for them, and re-layouts  2.29 us
  transfers between devices with their start and end apart: 33, of which 14 were waited for; matrix products, arithmetic and copies ran while one was open for 0% of the time, Pallas kernels for 6%

profile of v18, /device:TPU:0, one launch (start us, length us, event | category | flops | bytes accessed | tf_op | source)
XLA Modules:
  0.0 113.5 jit_solution(11830089145640376752)
XLA Ops:
  0.8 2.0 %columns.1 = (bf16[128,512]{1,0:T(8,128)(2,1)S(1)}, bf16[128,512]{1,0:T(8,128)(2,1)S(1)}, bf16[2,128,512]{2,1,0:T(8,128)(2,1)S(1)}, bf16[2,512,512]{2,1,0:T(8,128)(2,1)S(1)}) custom-call(s32[7]{0:T(128)S(1)} %stack.32.place, bf16[128,2048]{1,0:T(8,128)(2,1)} %tokens.1, bf16[1,512,512]{2,1,0:T(8,128)(2,1)} %expert_in.1, bf16[1,512,512]{2,1,0:T(8,128)(2,1)} %expert_out.1), custom_call_target="tpu_custom_call" | custom-call | tf_op jit(solution)/shard_map/columns/pallas_call | solution.py:45
  3.3 2.6 %collective-permute-start = (bf16[2,128,512]{2,1,0:T(8,128)(2,1)S(1)}, bf16[2,128,512]{2,1,0:T(8,128)(2,1)S(1)}, u32[]{:S(2)}, u32[]{:S(2)}) collective-permute-start(bf16[2,128,512]{2,1,0:T(8,128)(2,1)S(1)} %get-tuple-element.62), channel_id=1, source_target_pairs={{0,2},{1,3},{2,0},{3,1},{4,6},{5,7},{6,4},{7,5},{8,10},{9,11},{10,... | collective-permute-start | bytes 786440 | tf_op jit(solution)/shard_map/ppermute | solution.py:33
  5.8 1.6 %collective-permute-start.4 = (bf16[128,512]{1,0:T(8,128)(2,1)}, bf16[128,512]{1,0:T(8,128)(2,1)S(1)}, u32[]{:S(2)}, u32[]{:S(2)}) collective-permute-start(bf16[128,512]{1,0:T(8,128)(2,1)} %refs_4_.1), channel_id=1, source_target_pairs={{0,4},{1,5},{2,6},{3,7},{4,8},{5,9},{6,10},{7,11},{8,12},{9,13},{1... | collective-permute-start | bytes 393224 | tf_op jit(solution)/shard_map/ppermute | solution.py:29
  7.4 2.6 %collective-permute-start.5 = (bf16[128,512]{1,0:T(8,128)(2,1)}, bf16[128,512]{1,0:T(8,128)(2,1)S(1)}, u32[]{:S(2)}, u32[]{:S(2)}) collective-permute-start(bf16[128,512]{1,0:T(8,128)(2,1)} %refs_4_.1), channel_id=1, source_target_pairs={{0,8},{1,9},{2,10},{3,11},{4,12},{5,13},{6,14},{7,15},{8,0},{9,1},... | collective-permute-start | bytes 393224 | tf_op jit(solution)/shard_map/ppermute | solution.py:29
  16.2 3.0 %collective-permute-done.5.refs_6_ = bf16[128,512]{1,0:T(8,128)(2,1)S(1)} collective-permute-done((bf16[128,512]{1,0:T(8,128)(2,1)}, bf16[128,512]{1,0:T(8,128)(2,1)S(1)}, u32[]{:S(2)}, u32[]{:S(2)}) %collective-permute-start.5) | collective-permute-done | bytes 131104 | tf_op jit(solution)/shard_map/ppermute | solution.py:29
  20.9 3.3 %collective-permute-start.10 = (bf16[144,512]{1,0:T(8,128)(2,1)S(1)}, bf16[144,512]{1,0:T(8,128)(2,1)S(1)}, u32[]{:S(2)}, u32[]{:S(2)}) collective-permute-start(bf16[144,512]{1,0:T(8,128)(2,1)S(1)} %payload.1.refs_7_), channel_id=1, source_target_pairs={{0,4},{1,5},{2,6},{3,7},{4,8},{5,9},{6,10},{7,11},{8,12},{9,13},{1... | collective-permute-start | bytes 442376 | tf_op jit(solution)/shard_map/ppermute | solution.py:29
  24.2 1.6 %collective-permute-start.11 = (bf16[144,512]{1,0:T(8,128)(2,1)S(1)}, bf16[144,512]{1,0:T(8,128)(2,1)S(1)}, u32[]{:S(2)}, u32[]{:S(2)}) collective-permute-start(bf16[144,512]{1,0:T(8,128)(2,1)S(1)} %payload.1.refs_7_), channel_id=1, source_target_pairs={{0,8},{1,9},{2,10},{3,11},{4,12},{5,13},{6,14},{7,15},{8,0},{9,1},... | collective-permute-start | bytes 442376 | tf_op jit(solution)/shard_map/ppermute | solution.py:29
  30.0 5.9 %collective-permute-done.11.refs_5_ = bf16[144,512]{1,0:T(8,128)(2,1)S(1)} collective-permute-done((bf16[144,512]{1,0:T(8,128)(2,1)S(1)}, bf16[144,512]{1,0:T(8,128)(2,1)S(1)}, u32[]{:S(2)}, u32[]{:S(2)}) %collective-permute-start.11) | collective-permute-done | bytes 147488 | tf_op jit(solution)/shard_map/ppermute | solution.py:29
  35.8 1.6 %collective-permute-done.8.refs_1_ = bf16[128,512]{1,0:T(8,128)(2,1)S(1)} collective-permute-done((bf16[128,512]{1,0:T(8,128)(2,1)S(1)}, bf16[128,512]{1,0:T(8,128)(2,1)S(1)}, u32[]{:S(2)}, u32[]{:S(2)}) %collective-permute-start.8) | collective-permute-done | bytes 131104 | tf_op jit(solution)/shard_map/ppermute | solution.py:33
  38.6 3.3 %collective-permute-start.13 = (bf16[128,512]{1,0:T(8,128)(2,1)S(1)}, bf16[128,512]{1,0:T(8,128)(2,1)S(1)}, u32[]{:S(2)}, u32[]{:S(2)}) collective-permute-start(bf16[128,512]{1,0:T(8,128)(2,1)S(1)} %latent.1.refs_3_), channel_id=1, source_target_pairs={{0,4},{1,5},{2,6},{3,7},{4,8},{5,9},{6,10},{7,11},{8,12},{9,13},{1... | collective-permute-start | bytes 393224 | tf_op jit(solution)/shard_map/ppermute | solution.py:29
  41.9 1.6 %collective-permute-start.14 = (bf16[128,512]{1,0:T(8,128)(2,1)S(1)}, bf16[128,512]{1,0:T(8,128)(2,1)S(1)}, u32[]{:S(2)}, u32[]{:S(2)}) collective-permute-start(bf16[128,512]{1,0:T(8,128)(2,1)S(1)} %latent.1.refs_3_), channel_id=1, source_target_pairs={{0,8},{1,9},{2,10},{3,11},{4,12},{5,13},{6,14},{7,15},{8,0},{9,1},... | collective-permute-start | bytes 393224 | tf_op jit(solution)/shard_map/ppermute | solution.py:29
  44.3 3.2 %collective-permute-done.13.refs_0_ = bf16[128,512]{1,0:T(8,128)(2,1)S(1)} collective-permute-done((bf16[128,512]{1,0:T(8,128)(2,1)S(1)}, bf16[128,512]{1,0:T(8,128)(2,1)S(1)}, u32[]{:S(2)}, u32[]{:S(2)}) %collective-permute-start.13) | collective-permute-done | bytes 131104 | tf_op jit(solution)/shard_map/ppermute | solution.py:29
  47.5 4.3 %collective-permute-done.14.refs_1_ = bf16[128,512]{1,0:T(8,128)(2,1)S(1)} collective-permute-done((bf16[128,512]{1,0:T(8,128)(2,1)S(1)}, bf16[128,512]{1,0:T(8,128)(2,1)S(1)}, u32[]{:S(2)}, u32[]{:S(2)}) %collective-permute-start.14) | collective-permute-done | bytes 131104 | tf_op jit(solution)/shard_map/ppermute | solution.py:29
  51.8 1.9 %collective-permute-done.18.refs_13_ = bf16[512,512]{1,0:T(8,128)(2,1)S(1)} collective-permute-done((bf16[512,512]{1,0:T(8,128)(2,1)S(1)}, bf16[512,512]{1,0:T(8,128)(2,1)S(1)}, u32[]{:S(2)}, u32[]{:S(2)}) %collective-permute-start.18) | collective-permute-done | bytes 524320 | tf_op jit(solution)/shard_map/ppermute | solution.py:33
  53.7 5.9 %experts.1 = (bf16[128,512]{1,0:T(8,128)(2,1)S(1)}, bf16[128,512]{1,0:T(8,128)(2,1)S(1)}, bf16[128,512]{1,0:T(8,128)(2,1)S(1)}, bf16[128,512]{1,0:T(8,128)(2,1)S...) custom-call(s32[7]{0:T(128)S(1)} %stack.32.place, ...), custom_call_target="tpu_custom_call" | custom-call | tf_op jit(solution)/shard_map/experts/pallas_call | solution.py:45
  59.6 1.8 %weight_grads.2 = (f32[2,512,512]{2,1,0:T(8,128)S(1)}, bf16[2,512,512]{2,1,0:T(8,128)(2,1)S(1)}) custom-call(s32[7]{0:T(128)S(1)} %stack.32.place, bf16[128,512]{1,0:T(8,128)(2,1)S(1)} %collective-permute-done.13.refs_0_, bf16[128,512]{1,0:T(8,128)(2,1)S(1)} %collective-permute-done.14.refs_1_, bf16[128,512]{1,0:T(8,128)(2,1)S(1)} %collective-permute-done.15.refs_2_, ...), custom_call_target="tpu_custom_call" | custom-call | flops 1073741824 | tf_op jit(solution)/shard_map/weight_grads/pallas_call | solution.py:45
  63.2 3.2 %collective-permute-start.22 = (bf16[128,512]{1,0:T(8,128)(2,1)S(1)}, bf16[128,512]{1,0:T(8,128)(2,1)S(1)}, u32[]{:S(2)}, u32[]{:S(2)}) collective-permute-start(bf16[128,512]{1,0:T(8,128)(2,1)S(1)} %get-tuple-element.89), channel_id=1, source_target_pairs={{0,4},{1,5},{2,6},{3,7},{4,8},{5,9},{6,10},{7,11},{8,12},{9,13},{1... | collective-permute-start | bytes 393224 | tf_op jit(solution)/shard_map/ppermute | solution.py:29
  71.5 5.1 %collective-permute-done.21.refs_2_ = bf16[128,512]{1,0:T(8,128)(2,1)S(1)} collective-permute-done((bf16[128,512]{1,0:T(8,128)(2,1)S(1)}, bf16[128,512]{1,0:T(8,128)(2,1)S(1)}, u32[]{:S(2)}, u32[]{:S(2)}) %collective-permute-start.21) | collective-permute-done | bytes 131104 | tf_op jit(solution)/shard_map/ppermute | solution.py:29
  77.2 2.3 %collective-permute-start.26 = (bf16[128,512]{1,0:T(8,128)(2,1)S(1)}, bf16[128,512]{1,0:T(8,128)(2,1)S(1)}, u32[]{:S(2)}, u32[]{:S(2)}) collective-permute-start(bf16[128,512]{1,0:T(8,128)(2,1)S(1)} %get-tuple-element.97), channel_id=1, source_target_pairs={{0,8},{1,9},{2,10},{3,11},{4,12},{5,13},{6,14},{7,15},{8,0},{9,1},... | collective-permute-start | bytes 393224 | tf_op jit(solution)/shard_map/ppermute | solution.py:29
  80.3 1.8 %weight_grads.3 = (f32[2,512,512]{2,1,0:T(8,128)S(1)}, bf16[2,512,512]{2,1,0:T(8,128)(2,1)S(1)}) custom-call(s32[7]{0:T(128)S(1)} %stack.32.place, bf16[128,512]{1,0:T(8,128)(2,1)S(1)} %collective-permute-done.13.refs_0_, bf16[128,512]{1,0:T(8,128)(2,1)S(1)} %collective-permute-done.14.refs_1_, bf16[128,512]{1,0:T(8,128)(2,1)S(1)} %collective-permute-done.15.refs_2_, ...), custom_call_target="tpu_custom_call" | custom-call | flops 1073741824 | tf_op jit(solution)/shard_map/weight_grads/pallas_call | solution.py:45
  89.4 4.5 %collective-permute-start.30 = (bf16[2,128,512]{2,1,0:T(8,128)(2,1)S(1)}, bf16[2,128,512]{2,1,0:T(8,128)(2,1)S(1)}, u32[]{:S(2)}, u32[]{:S(2)}) collective-permute-start(bf16[2,128,512]{2,1,0:T(8,128)(2,1)S(1)} %get-tuple-element.101), channel_id=1, source_target_pairs={{0,12},{1,13},{2,14},{3,15},{4,0},{5,1},{6,2},{7,3},{8,4},{9,5},{1... | collective-permute-start | bytes 786440 | tf_op jit(solution)/shard_map/ppermute | solution.py:29
  94.5 2.2 %token_grad.1 = bf16[128,2048]{1,0:T(8,128)(2,1)} custom-call(s32[7]{0:T(128)S(1)} %stack.32.place, bf16[128,512]{1,0:T(8,128)(2,1)S(1)} %latent_delta.1.first.refs_4_.delta, bf16[4,512,512]{2,1,0:T(8,128)(2,1)S(1)} %pack.1.held, bf16[4,512,512]{2,1,0:T(8,128)(2,1)S(1)} %collective-permute-done.28.arrived.others), custom_call_target="tpu_custom_call" | custom-call | tf_op jit(solution)/shard_map/token_grad/pallas_call | solution.py:45
  96.6 14.9 %collective-permute-done.31.refs_2_ = bf16[128,512]{1,0:T(8,128)(2,1)S(1)} collective-permute-done((bf16[128,512]{1,0:T(8,128)(2,1)S(1)}, bf16[128,512]{1,0:T(8,128)(2,1)S(1)}, u32[]{:S(2)}, u32[]{:S(2)}) %collective-permute-start.31) | collective-permute-done | bytes 131104 | tf_op jit(solution)/shard_map/ppermute | solution.py:29
  111.6 1.9 %last_sums.1 = (f32[128,512]{1,0:T(8,128)}, bf16[128,512]{1,0:T(8,128)(2,1)}, bf16[1,512,512]{2,1,0:T(8,128)(2,1)}, bf16[1,512,512]{2,1,0:T(8,128)(2,1)}) custom-call(s32[7]{0:T(128)S(1)} %stack.32.place, f32[2,512,512]{2,1,0:T(8,128)S(1)} %get-tuple-element.105.near, bf16[4,512,512]{2,1,0:T(8,128)(2,1)S(1)} %collective-permute-done.28.arrived.others, ...), custom_call_target="tpu_custom_call" | custom-call | tf_op jit(solution)/shard_map/last_sums/pallas_call | solution.py:45
  (71 shorter events, 30.5 us)
Async XLA Ops:
  2.7 10.1 %collective-permute-start.1 = (bf16[2,512,512]{2,1,0:T(8,128)(2,1)S(1)}, bf16[2,512,512]{2,1,0:T(8,128)(2,1)S(1)}, u32[]{:S(2)}, u32[]{:S(2)}) collective-permute-start(bf16[2,512,512]{2,1,0:T(8,128)(2,1)S(1)} %get-tuple-element.64.refs_8_), channel_id=1, source_target_pairs={{0,1},{1,0},{2,3},{3,2},{4,5},{5,4},{6,7},{7,6},{8,9},{9,8},{10,11... | collective-permute-start | bytes 3145736 | tf_op jit(solution)/shard_map/ppermute | solution.py:33
  3.3 9.5 %collective-permute-start = (bf16[2,128,512]{2,1,0:T(8,128)(2,1)S(1)}, bf16[2,128,512]{2,1,0:T(8,128)(2,1)S(1)}, u32[]{:S(2)}, u32[]{:S(2)}) collective-permute-start(bf16[2,128,512]{2,1,0:T(8,128)(2,1)S(1)} %get-tuple-element.62), channel_id=1, source_target_pairs={{0,2},{1,3},{2,0},{3,1},{4,6},{5,7},{6,4},{7,5},{8,10},{9,11},{10,... | collective-permute-start | bytes 786440 | tf_op jit(solution)/shard_map/ppermute | solution.py:33
  5.8 10.3 %collective-permute-start.4 = (bf16[128,512]{1,0:T(8,128)(2,1)}, bf16[128,512]{1,0:T(8,128)(2,1)S(1)}, u32[]{:S(2)}, u32[]{:S(2)}) collective-permute-start(bf16[128,512]{1,0:T(8,128)(2,1)} %refs_4_.1), channel_id=1, source_target_pairs={{0,4},{1,5},{2,6},{3,7},{4,8},{5,9},{6,10},{7,11},{8,12},{9,13},{1... | collective-permute-start | bytes 393224 | tf_op jit(solution)/shard_map/ppermute | solution.py:29
  7.4 11.8 %collective-permute-start.5 = (bf16[128,512]{1,0:T(8,128)(2,1)}, bf16[128,512]{1,0:T(8,128)(2,1)S(1)}, u32[]{:S(2)}, u32[]{:S(2)}) collective-permute-start(bf16[128,512]{1,0:T(8,128)(2,1)} %refs_4_.1), channel_id=1, source_target_pairs={{0,8},{1,9},{2,10},{3,11},{4,12},{5,13},{6,14},{7,15},{8,0},{9,1},... | collective-permute-start | bytes 393224 | tf_op jit(solution)/shard_map/ppermute | solution.py:29
  10.0 9.2 %collective-permute-start.6 = (bf16[128,512]{1,0:T(8,128)(2,1)}, bf16[128,512]{1,0:T(8,128)(2,1)S(1)}, u32[]{:S(2)}, u32[]{:S(2)}) collective-permute-start(bf16[128,512]{1,0:T(8,128)(2,1)} %refs_4_.1), channel_id=1, source_target_pairs={{0,12},{1,13},{2,14},{3,15},{4,0},{5,1},{6,2},{7,3},{8,4},{9,5},{1... | collective-permute-start | bytes 393224 | tf_op jit(solution)/shard_map/ppermute | solution.py:29
  20.3 15.5 %collective-permute-start.9 = (bf16[512,512]{1,0:T(8,128)(2,1)S(1)}, bf16[512,512]{1,0:T(8,128)(2,1)S(1)}, u32[]{:S(2)}, u32[]{:S(2)}) collective-permute-start(bf16[512,512]{1,0:T(8,128)(2,1)S(1)} %bitcast.15), channel_id=1, source_target_pairs={{0,2},{1,3},{2,0},{3,1},{4,6},{5,7},{6,4},{7,5},{8,10},{9,11},{10,... | collective-permute-start | bytes 1572872 | tf_op jit(solution)/shard_map/ppermute | solution.py:33
  20.9 9.1 %collective-permute-start.10 = (bf16[144,512]{1,0:T(8,128)(2,1)S(1)}, bf16[144,512]{1,0:T(8,128)(2,1)S(1)}, u32[]{:S(2)}, u32[]{:S(2)}) collective-permute-start(bf16[144,512]{1,0:T(8,128)(2,1)S(1)} %payload.1.refs_7_), channel_id=1, source_target_pairs={{0,4},{1,5},{2,6},{3,7},{4,8},{5,9},{6,10},{7,11},{8,12},{9,13},{1... | collective-permute-start | bytes 442376 | tf_op jit(solution)/shard_map/ppermute | solution.py:29
  24.2 11.7 %collective-permute-start.11 = (bf16[144,512]{1,0:T(8,128)(2,1)S(1)}, bf16[144,512]{1,0:T(8,128)(2,1)S(1)}, u32[]{:S(2)}, u32[]{:S(2)}) collective-permute-start(bf16[144,512]{1,0:T(8,128)(2,1)S(1)} %payload.1.refs_7_), channel_id=1, source_target_pairs={{0,8},{1,9},{2,10},{3,11},{4,12},{5,13},{6,14},{7,15},{8,0},{9,1},... | collective-permute-start | bytes 442376 | tf_op jit(solution)/shard_map/ppermute | solution.py:29
  25.8 10.0 %collective-permute-start.12 = (bf16[144,512]{1,0:T(8,128)(2,1)S(1)}, bf16[144,512]{1,0:T(8,128)(2,1)S(1)}, u32[]{:S(2)}, u32[]{:S(2)}) collective-permute-start(bf16[144,512]{1,0:T(8,128)(2,1)S(1)} %payload.1.refs_7_), channel_id=1, source_target_pairs={{0,12},{1,13},{2,14},{3,15},{4,0},{5,1},{6,2},{7,3},{8,4},{9,5},{1... | collective-permute-start | bytes 442376 | tf_op jit(solution)/shard_map/ppermute | solution.py:29
  27.2 10.3 %collective-permute-start.8 = (bf16[128,512]{1,0:T(8,128)(2,1)S(1)}, bf16[128,512]{1,0:T(8,128)(2,1)S(1)}, u32[]{:S(2)}, u32[]{:S(2)}) collective-permute-start(bf16[128,512]{1,0:T(8,128)(2,1)S(1)} %get-tuple-element.69), channel_id=1, source_target_pairs={{0,2},{1,3},{2,0},{3,1},{4,6},{5,7},{6,4},{7,5},{8,10},{9,11},{10,... | collective-permute-start | bytes 393224 | tf_op jit(solution)/shard_map/ppermute | solution.py:33
  38.0 13.7 %collective-permute-start.16 = (bf16[512,512]{1,0:T(8,128)(2,1)S(1)}, bf16[512,512]{1,0:T(8,128)(2,1)S(1)}, u32[]{:S(2)}, u32[]{:S(2)}) collective-permute-start(bf16[512,512]{1,0:T(8,128)(2,1)S(1)} %bitcast.16), channel_id=1, source_target_pairs={{0,2},{1,3},{2,0},{3,1},{4,6},{5,7},{6,4},{7,5},{8,10},{9,11},{10,... | collective-permute-start | bytes 1572872 | tf_op jit(solution)/shard_map/ppermute | solution.py:33
  38.6 8.8 %collective-permute-start.13 = (bf16[128,512]{1,0:T(8,128)(2,1)S(1)}, bf16[128,512]{1,0:T(8,128)(2,1)S(1)}, u32[]{:S(2)}, u32[]{:S(2)}) collective-permute-start(bf16[128,512]{1,0:T(8,128)(2,1)S(1)} %latent.1.refs_3_), channel_id=1, source_target_pairs={{0,4},{1,5},{2,6},{3,7},{4,8},{5,9},{6,10},{7,11},{8,12},{9,13},{1... | collective-permute-start | bytes 393224 | tf_op jit(solution)/shard_map/ppermute | solution.py:29
  41.9 9.8 %collective-permute-start.14 = (bf16[128,512]{1,0:T(8,128)(2,1)S(1)}, bf16[128,512]{1,0:T(8,128)(2,1)S(1)}, u32[]{:S(2)}, u32[]{:S(2)}) collective-permute-start(bf16[128,512]{1,0:T(8,128)(2,1)S(1)} %latent.1.refs_3_), channel_id=1, source_target_pairs={{0,8},{1,9},{2,10},{3,11},{4,12},{5,13},{6,14},{7,15},{8,0},{9,1},... | collective-permute-start | bytes 393224 | tf_op jit(solution)/shard_map/ppermute | solution.py:29
  43.5 8.2 %collective-permute-start.15 = (bf16[128,512]{1,0:T(8,128)(2,1)S(1)}, bf16[128,512]{1,0:T(8,128)(2,1)S(1)}, u32[]{:S(2)}, u32[]{:S(2)}) collective-permute-start(bf16[128,512]{1,0:T(8,128)(2,1)S(1)} %latent.1.refs_3_), channel_id=1, source_target_pairs={{0,12},{1,13},{2,14},{3,15},{4,0},{5,1},{6,2},{7,3},{8,4},{9,5},{1... | collective-permute-start | bytes 393224 | tf_op jit(solution)/shard_map/ppermute | solution.py:29
  44.3 7.5 %collective-permute-start.17 = (bf16[512,512]{1,0:T(8,128)(2,1)S(1)}, bf16[512,512]{1,0:T(8,128)(2,1)S(1)}, u32[]{:S(2)}, u32[]{:S(2)}) collective-permute-start(bf16[512,512]{1,0:T(8,128)(2,1)S(1)} %collective-permute-done.9.refs_10_), channel_id=1, source_target_pairs={{0,1},{1,0},{2,3},{3,2},{4,5},{5,4},{6,7},{7,6},{8,9},{9,8},{10,11... | collective-permute-start | bytes 1572872 | tf_op jit(solution)/shard_map/ppermute | solution.py:33
  61.7 20.4 %collective-permute-start.24 = (bf16[512,512]{1,0:T(8,128)(2,1)S(1)}, bf16[512,512]{1,0:T(8,128)(2,1)S(1)}, u32[]{:S(2)}, u32[]{:S(2)}) collective-permute-start(bf16[512,512]{1,0:T(8,128)(2,1)S(1)} %get-tuple-element.94.down), channel_id=1, source_target_pairs={{0,2},{1,3},{2,0},{3,1},{4,6},{5,7},{6,4},{7,5},{8,10},{9,11},{10,... | collective-permute-start | bytes 1572872 | tf_op jit(solution)/shard_map/ppermute | solution.py:33
  63.2 8.4 %collective-permute-start.22 = (bf16[128,512]{1,0:T(8,128)(2,1)S(1)}, bf16[128,512]{1,0:T(8,128)(2,1)S(1)}, u32[]{:S(2)}, u32[]{:S(2)}) collective-permute-start(bf16[128,512]{1,0:T(8,128)(2,1)S(1)} %get-tuple-element.89), channel_id=1, source_target_pairs={{0,4},{1,5},{2,6},{3,7},{4,8},{5,9},{6,10},{7,11},{8,12},{9,13},{1... | collective-permute-start | bytes 393224 | tf_op jit(solution)/shard_map/ppermute | solution.py:29
  66.4 10.2 %collective-permute-start.21 = (bf16[128,512]{1,0:T(8,128)(2,1)S(1)}, bf16[128,512]{1,0:T(8,128)(2,1)S(1)}, u32[]{:S(2)}, u32[]{:S(2)}) collective-permute-start(bf16[128,512]{1,0:T(8,128)(2,1)S(1)} %get-tuple-element.87), channel_id=1, source_target_pairs={{0,8},{1,9},{2,10},{3,11},{4,12},{5,13},{6,14},{7,15},{8,0},{9,1},... | collective-permute-start | bytes 393224 | tf_op jit(solution)/shard_map/ppermute | solution.py:29
  67.7 8.9 %collective-permute-start.20 = (bf16[128,512]{1,0:T(8,128)(2,1)S(1)}, bf16[128,512]{1,0:T(8,128)(2,1)S(1)}, u32[]{:S(2)}, u32[]{:S(2)}) collective-permute-start(bf16[128,512]{1,0:T(8,128)(2,1)S(1)} %get-tuple-element.85), channel_id=1, source_target_pairs={{0,12},{1,13},{2,14},{3,15},{4,0},{5,1},{6,2},{7,3},{8,4},{9,5},{1... | collective-permute-start | bytes 393224 | tf_op jit(solution)/shard_map/ppermute | solution.py:29
  69.5 14.0 %collective-permute-start.25 = (bf16[256,512]{1,0:T(8,128)(2,1)S(1)}, bf16[256,512]{1,0:T(8,128)(2,1)S(1)}, u32[]{:S(2)}, u32[]{:S(2)}) collective-permute-start(bf16[256,512]{1,0:T(8,128)(2,1)S(1)} %get-tuple-element.95), channel_id=1, source_target_pairs={{0,2},{1,3},{2,0},{3,1},{4,6},{5,7},{6,4},{7,5},{8,10},{9,11},{10,... | collective-permute-start | bytes 786440 | tf_op jit(solution)/shard_map/ppermute | solution.py:33
  88.2 23.3 %collective-permute-start.29 = (bf16[768,512]{1,0:T(8,128)(2,1)S(1)}, bf16[768,512]{1,0:T(8,128)(2,1)S(1)}, u32[]{:S(2)}, u32[]{:S(2)}) collective-permute-start(bf16[768,512]{1,0:T(8,128)(2,1)S(1)} %get-tuple-element.106), channel_id=1, source_target_pairs={{0,2},{1,3},{2,0},{3,1},{4,6},{5,7},{6,4},{7,5},{8,10},{9,11},{10,... | collective-permute-start | bytes 2359304 | tf_op jit(solution)/shard_map/ppermute | solution.py:33
  89.4 22.2 %collective-permute-start.30 = (bf16[2,128,512]{2,1,0:T(8,128)(2,1)S(1)}, bf16[2,128,512]{2,1,0:T(8,128)(2,1)S(1)}, u32[]{:S(2)}, u32[]{:S(2)}) collective-permute-start(bf16[2,128,512]{2,1,0:T(8,128)(2,1)S(1)} %get-tuple-element.101), channel_id=1, source_target_pairs={{0,12},{1,13},{2,14},{3,15},{4,0},{5,1},{6,2},{7,3},{8,4},{9,5},{1... | collective-permute-start | bytes 786440 | tf_op jit(solution)/shard_map/ppermute | solution.py:29
  93.9 17.7 %collective-permute-start.32 = (bf16[2,128,512]{2,1,0:T(8,128)(2,1)S(1)}, bf16[2,128,512]{2,1,0:T(8,128)(2,1)S(1)}, u32[]{:S(2)}, u32[]{:S(2)}) collective-permute-start(bf16[2,128,512]{2,1,0:T(8,128)(2,1)S(1)} %get-tuple-element.109), channel_id=1, source_target_pairs={{0,4},{1,5},{2,6},{3,7},{4,8},{5,9},{6,10},{7,11},{8,12},{9,13},{1... | collective-permute-start | bytes 786440 | tf_op jit(solution)/shard_map/ppermute | solution.py:29
  93.9 17.7 %collective-permute-start.31 = (bf16[128,512]{1,0:T(8,128)(2,1)S(1)}, bf16[128,512]{1,0:T(8,128)(2,1)S(1)}, u32[]{:S(2)}, u32[]{:S(2)}) collective-permute-start(bf16[128,512]{1,0:T(8,128)(2,1)S(1)} %get-tuple-element.108), channel_id=1, source_target_pairs={{0,8},{1,9},{2,10},{3,11},{4,12},{5,13},{6,14},{7,15},{8,0},{9,1},... | collective-permute-start | bytes 393224 | tf_op jit(solution)/shard_map/ppermute | solution.py:29
  (15 other events, 125.6 us)

commit v19 on v18

--- a/solution.py
+++ b/solution.py
@@ -77,10 +77,6 @@
         copy.start()
     for copy in copies:
         copy.wait()
-
-
-def stack_body(place, first, second, out):
-    out[0], out[1] = first[...], second[...]
 
 
 def add_body(place, *refs):
@@ -217,10 +213,10 @@
 
 
 def down_grad_body(n_line, place, *refs):
-    own, across, core, core_across, *deltas, core_deltas = refs[:7]
-    riders, blocks = refs[7:-n_line], refs[-n_line:]
+    own, across, core, core_across, *deltas = refs[:8]
+    riders, blocks = refs[8:-n_line], refs[-n_line:]
     tokens = jnp.concatenate([own[...], across[0], core[...], core_across[...]], axis=0)
-    delta = jnp.concatenate([d[...] for d in deltas] + [core_deltas[0], core_deltas[1]], axis=0)
+    delta = jnp.concatenate([d[...] for d in deltas], axis=0)
     part = lax.dot_general(tokens, delta, contract_first, preferred_element_type=wide)
     block = blocks[0].shape[0]
     targets = [out if len(out.shape) == 2 else out.at[0] for out in blocks]
@@ -272,9 +268,6 @@
         scratch=[pltpu.SemaphoreType.DMA((4 * n_line + 2,))],
         outside=3,
     )(place, *(pltpu.with_memory_space_constraint(value, pltpu.HBM) for value in (tokens, expert_in, expert_out)))
-    stack = lambda first, second, *earlier: call(
-        stack_body, [shape((2,) + first.shape, narrow)], "stack"
-    )(after(place, *earlier) if earlier else place, first, second)[0]
     (payload,) = call(payload_body, [shape((tok_rows + gate_rows, latent_width), narrow)], "payload")(
         place, routes.T, gate_levels.T, latent_grad
     )
@@ -357,7 +350,8 @@
     (others,) = call(pack_body, [shape((4, latent_width, hidden_width), narrow)], "pack")(
         after(place, delta), near_other, down, side_down
     )
-    core_deltas = swap(stack(delta, side_delta, others, far_first, *(out_lines[back] for back in range(1, n_line) if back not in riding)), n_line, 1, 0)
+    beside = [out_lines[back] for back in range(1, n_line) if back not in riding]
+    core_deltas = [swap(delta, n_line, 1, 0), swap(after(side_delta, others, far_first, *beside), n_line, 1, 0)]
     blocks = call(
         functools.partial(down_grad_body, n_line),
         [
@@ -365,7 +359,7 @@
             for back in range(n_line)
         ],
         "down_grad",
-    )(place, columns[0], across, *core_tokens, delta, side_delta, core_deltas, *(outs_of[back] for back in riding))
+    )(place, columns[0], across, *core_tokens, delta, side_delta, *core_deltas, *(outs_of[back] for back in riding))
     others = [others, swap(after(others, blocks[1]), n_line, 1, 0)]
     (grad_tokens,) = call(
         functools.partial(token_grad_body, n_line, block), [shape((tok_rows, width), narrow)], "token_grad"

time: 114 us -> 113 us (level)
  waiting for transfers between devices: 47.4 us -> 45.8 us
  starting transfers between devices: 40.7 us -> 42 us
    ppermute x16, waiting for transfers between devices: 39.8 us -> 38 us  [turn(): lax.ppermute(value, plane, device_pairs(n_line, lambda z, x, c: ((z + by)...]
    pallas_call x15 -> x14, Pallas kernels: 22.2 us -> 21.6 us  [run(): pl.pallas_call(body, out_shape=outs, in_specs=[pl.BlockSpec(memory_space=...]
    ppermute x17 -> x18, starting transfers between devices: 10.9 us -> 11.3 us  [swap(): lax.ppermute(value, plane, device_pairs(n_line, lambda z, x, c: (z, x ^ s...]
    ppermute x17 -> x18, waiting for transfers between devices: 7.61 us -> 7.77 us  [swap(): lax.ppermute(value, plane, device_pairs(n_line, lambda z, x, c: (z, x ^ s...]
  transfers between devices with their start and end apart: 33 -> 34, of which waited for: 14 -> 13; matrix products, arithmetic and copies ran while one was open for 0% -> 0% of each run, Pallas kernels for 6% -> 6%
where the time goes in v19:
time: 113 us
  waiting for transfers between devices  45.8 us (41%)
  starting transfers between devices  42 us (37%)
  Pallas kernels  21.6 us (19%)
  local copies, waits for them, and re-layouts  2.39 us (2%)
    ppermute x16, waiting for transfers between devices, turn(): lax.ppermute(value, plane, device_pairs(n_line, lambda z, x, c: ((z + by)...  38 us
    ppermute x16, starting transfers between devices, turn(): lax.ppermute(value, plane, device_pairs(n_line, lambda z, x, c: ((z + by)...  30.7 us
    pallas_call x14, Pallas kernels, run(): pl.pallas_call(body, out_shape=outs, in_specs=[pl.BlockSpec(memory_space=...  21.6 us
    ppermute x18, starting transfers between devices, swap(): lax.ppermute(value, plane, device_pairs(n_line, lambda z, x, c: (z, x ^ s...  11.3 us
    ppermute x18, waiting for transfers between devices, swap(): lax.ppermute(value, plane, device_pairs(n_line, lambda z, x, c: (z, x ^ s...  7.77 us
    unnamed x12, local copies, waits for them, and re-layouts  2.29 us
  transfers between devices with their start and end apart: 34, of which 13 were waited for; matrix products, arithmetic and copies ran while one was open for 0% of the time, Pallas kernels for 6%

profile of v19, /device:TPU:0, one launch (start us, length us, event | category | flops | bytes accessed | tf_op | source)
XLA Modules:
  0.0 112.7 jit_solution(6316488332259490219)
XLA Ops:
  0.8 2.0 %columns.1 = (bf16[128,512]{1,0:T(8,128)(2,1)S(1)}, bf16[128,512]{1,0:T(8,128)(2,1)S(1)}, bf16[2,128,512]{2,1,0:T(8,128)(2,1)S(1)}, bf16[2,512,512]{2,1,0:T(8,128)(2,1)S(1)}) custom-call(s32[7]{0:T(128)S(1)} %stack.31.place, bf16[128,2048]{1,0:T(8,128)(2,1)} %tokens.1, bf16[1,512,512]{2,1,0:T(8,128)(2,1)} %expert_in.1, bf16[1,512,512]{2,1,0:T(8,128)(2,1)} %expert_out.1), custom_call_target="tpu_custom_call" | custom-call | tf_op jit(solution)/shard_map/columns/pallas_call | solution.py:45
  3.3 2.6 %collective-permute-start = (bf16[2,128,512]{2,1,0:T(8,128)(2,1)S(1)}, bf16[2,128,512]{2,1,0:T(8,128)(2,1)S(1)}, u32[]{:S(2)}, u32[]{:S(2)}) collective-permute-start(bf16[2,128,512]{2,1,0:T(8,128)(2,1)S(1)} %get-tuple-element.62), channel_id=1, source_target_pairs={{0,2},{1,3},{2,0},{3,1},{4,6},{5,7},{6,4},{7,5},{8,10},{9,11},{10,... | collective-permute-start | bytes 786440 | tf_op jit(solution)/shard_map/ppermute | solution.py:33
  5.8 1.6 %collective-permute-start.4 = (bf16[128,512]{1,0:T(8,128)(2,1)}, bf16[128,512]{1,0:T(8,128)(2,1)S(1)}, u32[]{:S(2)}, u32[]{:S(2)}) collective-permute-start(bf16[128,512]{1,0:T(8,128)(2,1)} %refs_4_.1), channel_id=1, source_target_pairs={{0,4},{1,5},{2,6},{3,7},{4,8},{5,9},{6,10},{7,11},{8,12},{9,13},{1... | collective-permute-start | bytes 393224 | tf_op jit(solution)/shard_map/ppermute | solution.py:29
  7.4 2.6 %collective-permute-start.5 = (bf16[128,512]{1,0:T(8,128)(2,1)}, bf16[128,512]{1,0:T(8,128)(2,1)S(1)}, u32[]{:S(2)}, u32[]{:S(2)}) collective-permute-start(bf16[128,512]{1,0:T(8,128)(2,1)} %refs_4_.1), channel_id=1, source_target_pairs={{0,8},{1,9},{2,10},{3,11},{4,12},{5,13},{6,14},{7,15},{8,0},{9,1},... | collective-permute-start | bytes 393224 | tf_op jit(solution)/shard_map/ppermute | solution.py:29
  16.2 3.0 %collective-permute-done.5.refs_6_ = bf16[128,512]{1,0:T(8,128)(2,1)S(1)} collective-permute-done((bf16[128,512]{1,0:T(8,128)(2,1)}, bf16[128,512]{1,0:T(8,128)(2,1)S(1)}, u32[]{:S(2)}, u32[]{:S(2)}) %collective-permute-start.5) | collective-permute-done | bytes 131104 | tf_op jit(solution)/shard_map/ppermute | solution.py:29
  20.9 3.3 %collective-permute-start.10 = (bf16[144,512]{1,0:T(8,128)(2,1)S(1)}, bf16[144,512]{1,0:T(8,128)(2,1)S(1)}, u32[]{:S(2)}, u32[]{:S(2)}) collective-permute-start(bf16[144,512]{1,0:T(8,128)(2,1)S(1)} %payload.1.refs_7_), channel_id=1, source_target_pairs={{0,4},{1,5},{2,6},{3,7},{4,8},{5,9},{6,10},{7,11},{8,12},{9,13},{1... | collective-permute-start | bytes 442376 | tf_op jit(solution)/shard_map/ppermute | solution.py:29
  24.2 1.6 %collective-permute-start.11 = (bf16[144,512]{1,0:T(8,128)(2,1)S(1)}, bf16[144,512]{1,0:T(8,128)(2,1)S(1)}, u32[]{:S(2)}, u32[]{:S(2)}) collective-permute-start(bf16[144,512]{1,0:T(8,128)(2,1)S(1)} %payload.1.refs_7_), channel_id=1, source_target_pairs={{0,8},{1,9},{2,10},{3,11},{4,12},{5,13},{6,14},{7,15},{8,0},{9,1},... | collective-permute-start | bytes 442376 | tf_op jit(solution)/shard_map/ppermute | solution.py:29
  30.0 5.9 %collective-permute-done.11.refs_5_ = bf16[144,512]{1,0:T(8,128)(2,1)S(1)} collective-permute-done((bf16[144,512]{1,0:T(8,128)(2,1)S(1)}, bf16[144,512]{1,0:T(8,128)(2,1)S(1)}, u32[]{:S(2)}, u32[]{:S(2)}) %collective-permute-start.11) | collective-permute-done | bytes 147488 | tf_op jit(solution)/shard_map/ppermute | solution.py:29
  35.8 1.6 %collective-permute-done.8.refs_1_ = bf16[128,512]{1,0:T(8,128)(2,1)S(1)} collective-permute-done((bf16[128,512]{1,0:T(8,128)(2,1)S(1)}, bf16[128,512]{1,0:T(8,128)(2,1)S(1)}, u32[]{:S(2)}, u32[]{:S(2)}) %collective-permute-start.8) | collective-permute-done | bytes 131104 | tf_op jit(solution)/shard_map/ppermute | solution.py:33
  38.6 3.3 %collective-permute-start.13 = (bf16[128,512]{1,0:T(8,128)(2,1)S(1)}, bf16[128,512]{1,0:T(8,128)(2,1)S(1)}, u32[]{:S(2)}, u32[]{:S(2)}) collective-permute-start(bf16[128,512]{1,0:T(8,128)(2,1)S(1)} %latent.1.refs_3_), channel_id=1, source_target_pairs={{0,4},{1,5},{2,6},{3,7},{4,8},{5,9},{6,10},{7,11},{8,12},{9,13},{1... | collective-permute-start | bytes 393224 | tf_op jit(solution)/shard_map/ppermute | solution.py:29
  41.9 1.6 %collective-permute-start.14 = (bf16[128,512]{1,0:T(8,128)(2,1)S(1)}, bf16[128,512]{1,0:T(8,128)(2,1)S(1)}, u32[]{:S(2)}, u32[]{:S(2)}) collective-permute-start(bf16[128,512]{1,0:T(8,128)(2,1)S(1)} %latent.1.refs_3_), channel_id=1, source_target_pairs={{0,8},{1,9},{2,10},{3,11},{4,12},{5,13},{6,14},{7,15},{8,0},{9,1},... | collective-permute-start | bytes 393224 | tf_op jit(solution)/shard_map/ppermute | solution.py:29
  44.3 3.2 %collective-permute-done.13.refs_0_ = bf16[128,512]{1,0:T(8,128)(2,1)S(1)} collective-permute-done((bf16[128,512]{1,0:T(8,128)(2,1)S(1)}, bf16[128,512]{1,0:T(8,128)(2,1)S(1)}, u32[]{:S(2)}, u32[]{:S(2)}) %collective-permute-start.13) | collective-permute-done | bytes 131104 | tf_op jit(solution)/shard_map/ppermute | solution.py:29
  47.5 4.3 %collective-permute-done.14.refs_1_ = bf16[128,512]{1,0:T(8,128)(2,1)S(1)} collective-permute-done((bf16[128,512]{1,0:T(8,128)(2,1)S(1)}, bf16[128,512]{1,0:T(8,128)(2,1)S(1)}, u32[]{:S(2)}, u32[]{:S(2)}) %collective-permute-start.14) | collective-permute-done | bytes 131104 | tf_op jit(solution)/shard_map/ppermute | solution.py:29
  51.8 1.9 %collective-permute-done.18.refs_13_ = bf16[512,512]{1,0:T(8,128)(2,1)S(1)} collective-permute-done((bf16[512,512]{1,0:T(8,128)(2,1)S(1)}, bf16[512,512]{1,0:T(8,128)(2,1)S(1)}, u32[]{:S(2)}, u32[]{:S(2)}) %collective-permute-start.18) | collective-permute-done | bytes 524320 | tf_op jit(solution)/shard_map/ppermute | solution.py:33
  53.7 5.9 %experts.1 = (bf16[128,512]{1,0:T(8,128)(2,1)S(1)}, bf16[128,512]{1,0:T(8,128)(2,1)S(1)}, bf16[128,512]{1,0:T(8,128)(2,1)S(1)}, bf16[128,512]{1,0:T(8,128)(2,1)S...) custom-call(s32[7]{0:T(128)S(1)} %stack.31.place, ...), custom_call_target="tpu_custom_call" | custom-call | tf_op jit(solution)/shard_map/experts/pallas_call | solution.py:45
  59.6 1.8 %weight_grads.2 = (f32[2,512,512]{2,1,0:T(8,128)S(1)}, bf16[2,512,512]{2,1,0:T(8,128)(2,1)S(1)}) custom-call(s32[7]{0:T(128)S(1)} %stack.31.place, bf16[128,512]{1,0:T(8,128)(2,1)S(1)} %collective-permute-done.13.refs_0_, bf16[128,512]{1,0:T(8,128)(2,1)S(1)} %collective-permute-done.14.refs_1_, bf16[128,512]{1,0:T(8,128)(2,1)S(1)} %collective-permute-done.15.refs_2_, ...), custom_call_target="tpu_custom_call" | custom-call | flops 1073741824 | tf_op jit(solution)/shard_map/weight_grads/pallas_call | solution.py:45
  63.2 3.2 %collective-permute-start.22 = (bf16[128,512]{1,0:T(8,128)(2,1)S(1)}, bf16[128,512]{1,0:T(8,128)(2,1)S(1)}, u32[]{:S(2)}, u32[]{:S(2)}) collective-permute-start(bf16[128,512]{1,0:T(8,128)(2,1)S(1)} %get-tuple-element.89), channel_id=1, source_target_pairs={{0,4},{1,5},{2,6},{3,7},{4,8},{5,9},{6,10},{7,11},{8,12},{9,13},{1... | collective-permute-start | bytes 393224 | tf_op jit(solution)/shard_map/ppermute | solution.py:29
  71.5 5.1 %collective-permute-done.21.refs_2_ = bf16[128,512]{1,0:T(8,128)(2,1)S(1)} collective-permute-done((bf16[128,512]{1,0:T(8,128)(2,1)S(1)}, bf16[128,512]{1,0:T(8,128)(2,1)S(1)}, u32[]{:S(2)}, u32[]{:S(2)}) %collective-permute-start.21) | collective-permute-done | bytes 131104 | tf_op jit(solution)/shard_map/ppermute | solution.py:29
  78.0 2.3 %collective-permute-start.27 = (bf16[128,512]{1,0:T(8,128)(2,1)S(1)}, bf16[128,512]{1,0:T(8,128)(2,1)S(1)}, u32[]{:S(2)}, u32[]{:S(2)}) collective-permute-start(bf16[128,512]{1,0:T(8,128)(2,1)S(1)} %get-tuple-element.97), channel_id=1, source_target_pairs={{0,8},{1,9},{2,10},{3,11},{4,12},{5,13},{6,14},{7,15},{8,0},{9,1},... | collective-permute-start | bytes 393224 | tf_op jit(solution)/shard_map/ppermute | solution.py:29
  80.3 1.8 %weight_grads.3 = (f32[2,512,512]{2,1,0:T(8,128)S(1)}, bf16[2,512,512]{2,1,0:T(8,128)(2,1)S(1)}) custom-call(s32[7]{0:T(128)S(1)} %stack.31.place, bf16[128,512]{1,0:T(8,128)(2,1)S(1)} %collective-permute-done.13.refs_0_, bf16[128,512]{1,0:T(8,128)(2,1)S(1)} %collective-permute-done.14.refs_1_, bf16[128,512]{1,0:T(8,128)(2,1)S(1)} %collective-permute-done.15.refs_2_, ...), custom_call_target="tpu_custom_call" | custom-call | flops 1073741824 | tf_op jit(solution)/shard_map/weight_grads/pallas_call | solution.py:45
  88.6 5.5 %collective-permute-start.31 = (bf16[2,128,512]{2,1,0:T(8,128)(2,1)S(1)}, bf16[2,128,512]{2,1,0:T(8,128)(2,1)S(1)}, u32[]{:S(2)}, u32[]{:S(2)}) collective-permute-start(bf16[2,128,512]{2,1,0:T(8,128)(2,1)S(1)} %get-tuple-element.101), channel_id=1, source_target_pairs={{0,12},{1,13},{2,14},{3,15},{4,0},{5,1},{6,2},{7,3},{8,4},{9,5},{1... | collective-permute-start | bytes 786440 | tf_op jit(solution)/shard_map/ppermute | solution.py:29
  94.7 2.2 %token_grad.1 = bf16[128,2048]{1,0:T(8,128)(2,1)} custom-call(s32[7]{0:T(128)S(1)} %stack.31.place, bf16[128,512]{1,0:T(8,128)(2,1)S(1)} %latent_delta.1.refs_4_.delta, bf16[4,512,512]{2,1,0:T(8,128)(2,1)S(1)} %pack.1.held, bf16[4,512,512]{2,1,0:T(8,128)(2,1)S(1)} %collective-permute-done.29.arrived.others), custom_call_target="tpu_custom_call" | custom-call | tf_op jit(solution)/shard_map/token_grad/pallas_call | solution.py:45
  96.9 13.9 %collective-permute-done.32.refs_2_ = bf16[128,512]{1,0:T(8,128)(2,1)S(1)} collective-permute-done((bf16[128,512]{1,0:T(8,128)(2,1)S(1)}, bf16[128,512]{1,0:T(8,128)(2,1)S(1)}, u32[]{:S(2)}, u32[]{:S(2)}) %collective-permute-start.32) | collective-permute-done | bytes 131104 | tf_op jit(solution)/shard_map/ppermute | solution.py:29
  110.8 1.9 %last_sums.1 = (f32[128,512]{1,0:T(8,128)}, bf16[128,512]{1,0:T(8,128)(2,1)}, bf16[1,512,512]{2,1,0:T(8,128)(2,1)}, bf16[1,512,512]{2,1,0:T(8,128)(2,1)}) custom-call(s32[7]{0:T(128)S(1)} %stack.31.place, f32[2,512,512]{2,1,0:T(8,128)S(1)} %get-tuple-element.105.near, bf16[4,512,512]{2,1,0:T(8,128)(2,1)S(1)} %collective-permute-done.29.arrived.others, ...), custom_call_target="tpu_custom_call" | custom-call | tf_op jit(solution)/shard_map/last_sums/pallas_call | solution.py:45
  (72 shorter events, 29.8 us)
Async XLA Ops:
  2.7 10.1 %collective-permute-start.1 = (bf16[2,512,512]{2,1,0:T(8,128)(2,1)S(1)}, bf16[2,512,512]{2,1,0:T(8,128)(2,1)S(1)}, u32[]{:S(2)}, u32[]{:S(2)}) collective-permute-start(bf16[2,512,512]{2,1,0:T(8,128)(2,1)S(1)} %get-tuple-element.64.refs_8_), channel_id=1, source_target_pairs={{0,1},{1,0},{2,3},{3,2},{4,5},{5,4},{6,7},{7,6},{8,9},{9,8},{10,11... | collective-permute-start | bytes 3145736 | tf_op jit(solution)/shard_map/ppermute | solution.py:33
  3.3 9.5 %collective-permute-start = (bf16[2,128,512]{2,1,0:T(8,128)(2,1)S(1)}, bf16[2,128,512]{2,1,0:T(8,128)(2,1)S(1)}, u32[]{:S(2)}, u32[]{:S(2)}) collective-permute-start(bf16[2,128,512]{2,1,0:T(8,128)(2,1)S(1)} %get-tuple-element.62), channel_id=1, source_target_pairs={{0,2},{1,3},{2,0},{3,1},{4,6},{5,7},{6,4},{7,5},{8,10},{9,11},{10,... | collective-permute-start | bytes 786440 | tf_op jit(solution)/shard_map/ppermute | solution.py:33
  5.8 10.3 %collective-permute-start.4 = (bf16[128,512]{1,0:T(8,128)(2,1)}, bf16[128,512]{1,0:T(8,128)(2,1)S(1)}, u32[]{:S(2)}, u32[]{:S(2)}) collective-permute-start(bf16[128,512]{1,0:T(8,128)(2,1)} %refs_4_.1), channel_id=1, source_target_pairs={{0,4},{1,5},{2,6},{3,7},{4,8},{5,9},{6,10},{7,11},{8,12},{9,13},{1... | collective-permute-start | bytes 393224 | tf_op jit(solution)/shard_map/ppermute | solution.py:29
  7.4 11.8 %collective-permute-start.5 = (bf16[128,512]{1,0:T(8,128)(2,1)}, bf16[128,512]{1,0:T(8,128)(2,1)S(1)}, u32[]{:S(2)}, u32[]{:S(2)}) collective-permute-start(bf16[128,512]{1,0:T(8,128)(2,1)} %refs_4_.1), channel_id=1, source_target_pairs={{0,8},{1,9},{2,10},{3,11},{4,12},{5,13},{6,14},{7,15},{8,0},{9,1},... | collective-permute-start | bytes 393224 | tf_op jit(solution)/shard_map/ppermute | solution.py:29
  10.0 9.2 %collective-permute-start.6 = (bf16[128,512]{1,0:T(8,128)(2,1)}, bf16[128,512]{1,0:T(8,128)(2,1)S(1)}, u32[]{:S(2)}, u32[]{:S(2)}) collective-permute-start(bf16[128,512]{1,0:T(8,128)(2,1)} %refs_4_.1), channel_id=1, source_target_pairs={{0,12},{1,13},{2,14},{3,15},{4,0},{5,1},{6,2},{7,3},{8,4},{9,5},{1... | collective-permute-start | bytes 393224 | tf_op jit(solution)/shard_map/ppermute | solution.py:29
  20.3 15.5 %collective-permute-start.9 = (bf16[512,512]{1,0:T(8,128)(2,1)S(1)}, bf16[512,512]{1,0:T(8,128)(2,1)S(1)}, u32[]{:S(2)}, u32[]{:S(2)}) collective-permute-start(bf16[512,512]{1,0:T(8,128)(2,1)S(1)} %bitcast.15), channel_id=1, source_target_pairs={{0,2},{1,3},{2,0},{3,1},{4,6},{5,7},{6,4},{7,5},{8,10},{9,11},{10,... | collective-permute-start | bytes 1572872 | tf_op jit(solution)/shard_map/ppermute | solution.py:33
  20.9 9.1 %collective-permute-start.10 = (bf16[144,512]{1,0:T(8,128)(2,1)S(1)}, bf16[144,512]{1,0:T(8,128)(2,1)S(1)}, u32[]{:S(2)}, u32[]{:S(2)}) collective-permute-start(bf16[144,512]{1,0:T(8,128)(2,1)S(1)} %payload.1.refs_7_), channel_id=1, source_target_pairs={{0,4},{1,5},{2,6},{3,7},{4,8},{5,9},{6,10},{7,11},{8,12},{9,13},{1... | collective-permute-start | bytes 442376 | tf_op jit(solution)/shard_map/ppermute | solution.py:29
  24.2 11.7 %collective-permute-start.11 = (bf16[144,512]{1,0:T(8,128)(2,1)S(1)}, bf16[144,512]{1,0:T(8,128)(2,1)S(1)}, u32[]{:S(2)}, u32[]{:S(2)}) collective-permute-start(bf16[144,512]{1,0:T(8,128)(2,1)S(1)} %payload.1.refs_7_), channel_id=1, source_target_pairs={{0,8},{1,9},{2,10},{3,11},{4,12},{5,13},{6,14},{7,15},{8,0},{9,1},... | collective-permute-start | bytes 442376 | tf_op jit(solution)/shard_map/ppermute | solution.py:29
  25.8 10.0 %collective-permute-start.12 = (bf16[144,512]{1,0:T(8,128)(2,1)S(1)}, bf16[144,512]{1,0:T(8,128)(2,1)S(1)}, u32[]{:S(2)}, u32[]{:S(2)}) collective-permute-start(bf16[144,512]{1,0:T(8,128)(2,1)S(1)} %payload.1.refs_7_), channel_id=1, source_target_pairs={{0,12},{1,13},{2,14},{3,15},{4,0},{5,1},{6,2},{7,3},{8,4},{9,5},{1... | collective-permute-start | bytes 442376 | tf_op jit(solution)/shard_map/ppermute | solution.py:29
  27.2 10.3 %collective-permute-start.8 = (bf16[128,512]{1,0:T(8,128)(2,1)S(1)}, bf16[128,512]{1,0:T(8,128)(2,1)S(1)}, u32[]{:S(2)}, u32[]{:S(2)}) collective-permute-start(bf16[128,512]{1,0:T(8,128)(2,1)S(1)} %get-tuple-element.69), channel_id=1, source_target_pairs={{0,2},{1,3},{2,0},{3,1},{4,6},{5,7},{6,4},{7,5},{8,10},{9,11},{10,... | collective-permute-start | bytes 393224 | tf_op jit(solution)/shard_map/ppermute | solution.py:33
  38.0 13.7 %collective-permute-start.16 = (bf16[512,512]{1,0:T(8,128)(2,1)S(1)}, bf16[512,512]{1,0:T(8,128)(2,1)S(1)}, u32[]{:S(2)}, u32[]{:S(2)}) collective-permute-start(bf16[512,512]{1,0:T(8,128)(2,1)S(1)} %bitcast.16), channel_id=1, source_target_pairs={{0,2},{1,3},{2,0},{3,1},{4,6},{5,7},{6,4},{7,5},{8,10},{9,11},{10,... | collective-permute-start | bytes 1572872 | tf_op jit(solution)/shard_map/ppermute | solution.py:33
  38.6 8.8 %collective-permute-start.13 = (bf16[128,512]{1,0:T(8,128)(2,1)S(1)}, bf16[128,512]{1,0:T(8,128)(2,1)S(1)}, u32[]{:S(2)}, u32[]{:S(2)}) collective-permute-start(bf16[128,512]{1,0:T(8,128)(2,1)S(1)} %latent.1.refs_3_), channel_id=1, source_target_pairs={{0,4},{1,5},{2,6},{3,7},{4,8},{5,9},{6,10},{7,11},{8,12},{9,13},{1... | collective-permute-start | bytes 393224 | tf_op jit(solution)/shard_map/ppermute | solution.py:29
  41.9 9.8 %collective-permute-start.14 = (bf16[128,512]{1,0:T(8,128)(2,1)S(1)}, bf16[128,512]{1,0:T(8,128)(2,1)S(1)}, u32[]{:S(2)}, u32[]{:S(2)}) collective-permute-start(bf16[128,512]{1,0:T(8,128)(2,1)S(1)} %latent.1.refs_3_), channel_id=1, source_target_pairs={{0,8},{1,9},{2,10},{3,11},{4,12},{5,13},{6,14},{7,15},{8,0},{9,1},... | collective-permute-start | bytes 393224 | tf_op jit(solution)/shard_map/ppermute | solution.py:29
  43.5 8.2 %collective-permute-start.15 = (bf16[128,512]{1,0:T(8,128)(2,1)S(1)}, bf16[128,512]{1,0:T(8,128)(2,1)S(1)}, u32[]{:S(2)}, u32[]{:S(2)}) collective-permute-start(bf16[128,512]{1,0:T(8,128)(2,1)S(1)} %latent.1.refs_3_), channel_id=1, source_target_pairs={{0,12},{1,13},{2,14},{3,15},{4,0},{5,1},{6,2},{7,3},{8,4},{9,5},{1... | collective-permute-start | bytes 393224 | tf_op jit(solution)/shard_map/ppermute | solution.py:29
  61.7 20.4 %collective-permute-start.25 = (bf16[512,512]{1,0:T(8,128)(2,1)S(1)}, bf16[512,512]{1,0:T(8,128)(2,1)S(1)}, u32[]{:S(2)}, u32[]{:S(2)}) collective-permute-start(bf16[512,512]{1,0:T(8,128)(2,1)S(1)} %get-tuple-element.94.down), channel_id=1, source_target_pairs={{0,2},{1,3},{2,0},{3,1},{4,6},{5,7},{6,4},{7,5},{8,10},{9,11},{10,... | collective-permute-start | bytes 1572872 | tf_op jit(solution)/shard_map/ppermute | solution.py:33
  63.2 8.4 %collective-permute-start.22 = (bf16[128,512]{1,0:T(8,128)(2,1)S(1)}, bf16[128,512]{1,0:T(8,128)(2,1)S(1)}, u32[]{:S(2)}, u32[]{:S(2)}) collective-permute-start(bf16[128,512]{1,0:T(8,128)(2,1)S(1)} %get-tuple-element.89), channel_id=1, source_target_pairs={{0,4},{1,5},{2,6},{3,7},{4,8},{5,9},{6,10},{7,11},{8,12},{9,13},{1... | collective-permute-start | bytes 393224 | tf_op jit(solution)/shard_map/ppermute | solution.py:29
  66.4 10.2 %collective-permute-start.21 = (bf16[128,512]{1,0:T(8,128)(2,1)S(1)}, bf16[128,512]{1,0:T(8,128)(2,1)S(1)}, u32[]{:S(2)}, u32[]{:S(2)}) collective-permute-start(bf16[128,512]{1,0:T(8,128)(2,1)S(1)} %get-tuple-element.87), channel_id=1, source_target_pairs={{0,8},{1,9},{2,10},{3,11},{4,12},{5,13},{6,14},{7,15},{8,0},{9,1},... | collective-permute-start | bytes 393224 | tf_op jit(solution)/shard_map/ppermute | solution.py:29
  67.7 8.9 %collective-permute-start.20 = (bf16[128,512]{1,0:T(8,128)(2,1)S(1)}, bf16[128,512]{1,0:T(8,128)(2,1)S(1)}, u32[]{:S(2)}, u32[]{:S(2)}) collective-permute-start(bf16[128,512]{1,0:T(8,128)(2,1)S(1)} %get-tuple-element.85), channel_id=1, source_target_pairs={{0,12},{1,13},{2,14},{3,15},{4,0},{5,1},{6,2},{7,3},{8,4},{9,5},{1... | collective-permute-start | bytes 393224 | tf_op jit(solution)/shard_map/ppermute | solution.py:29
  69.5 14.8 %collective-permute-start.26 = (bf16[256,512]{1,0:T(8,128)(2,1)S(1)}, bf16[256,512]{1,0:T(8,128)(2,1)S(1)}, u32[]{:S(2)}, u32[]{:S(2)}) collective-permute-start(bf16[256,512]{1,0:T(8,128)(2,1)S(1)} %get-tuple-element.95), channel_id=1, source_target_pairs={{0,2},{1,3},{2,0},{3,1},{4,6},{5,7},{6,4},{7,5},{8,10},{9,11},{10,... | collective-permute-start | bytes 786440 | tf_op jit(solution)/shard_map/ppermute | solution.py:33
  86.9 7.8 %collective-permute-start.29 = (bf16[4,512,512]{2,1,0:T(8,128)(2,1)S(1)}, bf16[4,512,512]{2,1,0:T(8,128)(2,1)S(1)}, u32[]{:S(2)}, u32[]{:S(2)}) collective-permute-start(bf16[4,512,512]{2,1,0:T(8,128)(2,1)S(1)} %pack.1.held), channel_id=1, source_target_pairs={{0,1},{1,0},{2,3},{3,2},{4,5},{5,4},{6,7},{7,6},{8,9},{9,8},{10,11... | collective-permute-start | bytes 6291464 | tf_op jit(solution)/shard_map/ppermute | solution.py:33
  87.1 23.7 %collective-permute-start.30 = (bf16[768,512]{1,0:T(8,128)(2,1)S(1)}, bf16[768,512]{1,0:T(8,128)(2,1)S(1)}, u32[]{:S(2)}, u32[]{:S(2)}) collective-permute-start(bf16[768,512]{1,0:T(8,128)(2,1)S(1)} %get-tuple-element.106), channel_id=1, source_target_pairs={{0,2},{1,3},{2,0},{3,1},{4,6},{5,7},{6,4},{7,5},{8,10},{9,11},{10,... | collective-permute-start | bytes 2359304 | tf_op jit(solution)/shard_map/ppermute | solution.py:33
  88.6 22.2 %collective-permute-start.31 = (bf16[2,128,512]{2,1,0:T(8,128)(2,1)S(1)}, bf16[2,128,512]{2,1,0:T(8,128)(2,1)S(1)}, u32[]{:S(2)}, u32[]{:S(2)}) collective-permute-start(bf16[2,128,512]{2,1,0:T(8,128)(2,1)S(1)} %get-tuple-element.101), channel_id=1, source_target_pairs={{0,12},{1,13},{2,14},{3,15},{4,0},{5,1},{6,2},{7,3},{8,4},{9,5},{1... | collective-permute-start | bytes 786440 | tf_op jit(solution)/shard_map/ppermute | solution.py:29
  94.1 16.7 %collective-permute-start.33 = (bf16[2,128,512]{2,1,0:T(8,128)(2,1)S(1)}, bf16[2,128,512]{2,1,0:T(8,128)(2,1)S(1)}, u32[]{:S(2)}, u32[]{:S(2)}) collective-permute-start(bf16[2,128,512]{2,1,0:T(8,128)(2,1)S(1)} %get-tuple-element.109), channel_id=1, source_target_pairs={{0,4},{1,5},{2,6},{3,7},{4,8},{5,9},{6,10},{7,11},{8,12},{9,13},{1... | collective-permute-start | bytes 786440 | tf_op jit(solution)/shard_map/ppermute | solution.py:29
  94.1 16.7 %collective-permute-start.32 = (bf16[128,512]{1,0:T(8,128)(2,1)S(1)}, bf16[128,512]{1,0:T(8,128)(2,1)S(1)}, u32[]{:S(2)}, u32[]{:S(2)}) collective-permute-start(bf16[128,512]{1,0:T(8,128)(2,1)S(1)} %get-tuple-element.108), channel_id=1, source_target_pairs={{0,8},{1,9},{2,10},{3,11},{4,12},{5,13},{6,14},{7,15},{8,0},{9,1},... | collective-permute-start | bytes 393224 | tf_op jit(solution)/shard_map/ppermute | solution.py:29
  (16 other events, 132.4 us)

commit v20 on v19

--- a/solution.py
+++ b/solution.py
@@ -275,7 +275,7 @@
     core_own = swap(own, n_line, 1, 0)
     across = swap(columns[2], n_line, 0, 1)
     core_tokens = [swap(after(columns[1], across, core_own), n_line, 1, 0), swap(across[1], n_line, 1, 0)]
-    side_in = swap(after(expert_in[0], across), n_line, 0, 1)
+    side_in = swap(after(expert_in[0], core_tokens[0]), n_line, 0, 1)
 
     project = call(
         functools.partial(project_body, n_line),
@@ -284,7 +284,7 @@
     )
     keep, send, down = project(after(place, payload), columns[0], across, *core_tokens, *downs)
     half, cross = call(half_body, [rows_of(wide), rows_of(narrow)], "half")(
-        place, keep, swap(send, n_line, 1, 0)
+        after(place, side_in), keep, swap(send, n_line, 1, 0)
     )
     payloads = [payload] + [turn(after(payload, *downs[1:]), n_line, back) for back in range(1, n_line)]
     crossed = swap(cross, n_line, 0, 1)

time: 113 us -> 111 us (0.982)
  waiting for transfers between devices: 45.8 us -> 41.3 us
  starting transfers between devices: 42 us -> 45 us
    ppermute x16, waiting for transfers between devices: 38 us -> 31 us  [turn(): lax.ppermute(value, plane, device_pairs(n_line, lambda z, x, c: ((z + by)...]
    ppermute x18, waiting for transfers between devices: 7.77 us -> 10.3 us  [swap(): lax.ppermute(value, plane, device_pairs(n_line, lambda z, x, c: (z, x ^ s...]
    ppermute x18, starting transfers between devices: 11.3 us -> 13.7 us  [swap(): lax.ppermute(value, plane, device_pairs(n_line, lambda z, x, c: (z, x ^ s...]
  transfers between devices with their start and end apart: 34 -> 34, of which waited for: 13 -> 14; matrix products, arithmetic and copies ran while one was open for 0% -> 0% of each run, Pallas kernels for 6% -> 7%
where the time goes in v20:
time: 111 us
  starting transfers between devices  45 us (41%)
  waiting for transfers between devices  41.3 us (37%)
  Pallas kernels  21.6 us (19%)
  local copies, waits for them, and re-layouts  2.39 us (2%)
    ppermute x16, starting transfers between devices, turn(): lax.ppermute(value, plane, device_pairs(n_line, lambda z, x, c: ((z + by)...  31.3 us
    ppermute x16, waiting for transfers between devices, turn(): lax.ppermute(value, plane, device_pairs(n_line, lambda z, x, c: ((z + by)...  31 us
    pallas_call x14, Pallas kernels, run(): pl.pallas_call(body, out_shape=outs, in_specs=[pl.BlockSpec(memory_space=...  21.6 us
    ppermute x18, starting transfers between devices, swap(): lax.ppermute(value, plane, device_pairs(n_line, lambda z, x, c: (z, x ^ s...  13.7 us
    ppermute x18, waiting for transfers between devices, swap(): lax.ppermute(value, plane, device_pairs(n_line, lambda z, x, c: (z, x ^ s...  10.3 us
    unnamed x12, local copies, waits for them, and re-layouts  2.29 us
  transfers between devices with their start and end apart: 34, of which 14 were waited for; matrix products, arithmetic and copies ran while one was open for 0% of the time, Pallas kernels for 7%

profile of v20, /device:TPU:0, one launch (start us, length us, event | category | flops | bytes accessed | tf_op | source)
XLA Modules:
  0.0 111.2 jit_solution(13700809525431197807)
XLA Ops:
  0.8 2.0 %columns.1 = (bf16[128,512]{1,0:T(8,128)(2,1)S(1)}, bf16[128,512]{1,0:T(8,128)(2,1)S(1)}, bf16[2,128,512]{2,1,0:T(8,128)(2,1)S(1)}, bf16[2,512,512]{2,1,0:T(8,128)(2,1)S(1)}) custom-call(s32[7]{0:T(128)S(1)} %stack.31.place, bf16[128,2048]{1,0:T(8,128)(2,1)} %tokens.1, bf16[1,512,512]{2,1,0:T(8,128)(2,1)} %expert_in.1, bf16[1,512,512]{2,1,0:T(8,128)(2,1)} %expert_out.1), custom_call_target="tpu_custom_call" | custom-call | tf_op jit(solution)/shard_map/columns/pallas_call | solution.py:45
  3.3 2.6 %collective-permute-start = (bf16[2,128,512]{2,1,0:T(8,128)(2,1)S(1)}, bf16[2,128,512]{2,1,0:T(8,128)(2,1)S(1)}, u32[]{:S(2)}, u32[]{:S(2)}) collective-permute-start(bf16[2,128,512]{2,1,0:T(8,128)(2,1)S(1)} %get-tuple-element.62), channel_id=1, source_target_pairs={{0,2},{1,3},{2,0},{3,1},{4,6},{5,7},{6,4},{7,5},{8,10},{9,11},{10,... | collective-permute-start | bytes 786440 | tf_op jit(solution)/shard_map/ppermute | solution.py:33
  7.4 2.6 %collective-permute-start.6 = (bf16[128,512]{1,0:T(8,128)(2,1)}, bf16[128,512]{1,0:T(8,128)(2,1)S(1)}, u32[]{:S(2)}, u32[]{:S(2)}) collective-permute-start(bf16[128,512]{1,0:T(8,128)(2,1)} %refs_4_.1), channel_id=1, source_target_pairs={{0,8},{1,9},{2,10},{3,11},{4,12},{5,13},{6,14},{7,15},{8,0},{9,1},... | collective-permute-start | bytes 393224 | tf_op jit(solution)/shard_map/ppermute | solution.py:29
  16.2 1.8 %collective-permute-start.3 = (bf16[512,512]{1,0:T(8,128)(2,1)S(1)}, bf16[512,512]{1,0:T(8,128)(2,1)S(1)}, u32[]{:S(2)}, u32[]{:S(2)}) collective-permute-start(bf16[512,512]{1,0:T(8,128)(2,1)S(1)} %bitcast.15), channel_id=1, source_target_pairs={{0,2},{1,3},{2,0},{3,1},{4,6},{5,7},{6,4},{7,5},{8,10},{9,11},{10,... | collective-permute-start | bytes 1572872 | tf_op jit(solution)/shard_map/ppermute | solution.py:33
  20.3 3.3 %collective-permute-start.10 = (bf16[144,512]{1,0:T(8,128)(2,1)S(1)}, bf16[144,512]{1,0:T(8,128)(2,1)S(1)}, u32[]{:S(2)}, u32[]{:S(2)}) collective-permute-start(bf16[144,512]{1,0:T(8,128)(2,1)S(1)} %payload.1.refs_7_), channel_id=1, source_target_pairs={{0,4},{1,5},{2,6},{3,7},{4,8},{5,9},{6,10},{7,11},{8,12},{9,13},{1... | collective-permute-start | bytes 442376 | tf_op jit(solution)/shard_map/ppermute | solution.py:29
  26.1 4.0 %collective-permute-done.3.refs_10_ = bf16[512,512]{1,0:T(8,128)(2,1)S(1)} collective-permute-done((bf16[512,512]{1,0:T(8,128)(2,1)S(1)}, bf16[512,512]{1,0:T(8,128)(2,1)S(1)}, u32[]{:S(2)}, u32[]{:S(2)}) %collective-permute-start.3) | collective-permute-done | bytes 524320 | tf_op jit(solution)/shard_map/ppermute | solution.py:33
  30.7 1.8 %collective-permute-start.9 = (bf16[128,512]{1,0:T(8,128)(2,1)S(1)}, bf16[128,512]{1,0:T(8,128)(2,1)S(1)}, u32[]{:S(2)}, u32[]{:S(2)}) collective-permute-start(bf16[128,512]{1,0:T(8,128)(2,1)S(1)} %get-tuple-element.72), channel_id=1, source_target_pairs={{0,2},{1,3},{2,0},{3,1},{4,6},{5,7},{6,4},{7,5},{8,10},{9,11},{10,... | collective-permute-start | bytes 393224 | tf_op jit(solution)/shard_map/ppermute | solution.py:33
  32.5 3.0 %collective-permute-done.11.refs_5_ = bf16[144,512]{1,0:T(8,128)(2,1)S(1)} collective-permute-done((bf16[144,512]{1,0:T(8,128)(2,1)S(1)}, bf16[144,512]{1,0:T(8,128)(2,1)S(1)}, u32[]{:S(2)}, u32[]{:S(2)}) %collective-permute-start.11) | collective-permute-done | bytes 147488 | tf_op jit(solution)/shard_map/ppermute | solution.py:29
  38.1 2.2 %collective-permute-start.13 = (bf16[128,512]{1,0:T(8,128)(2,1)S(1)}, bf16[128,512]{1,0:T(8,128)(2,1)S(1)}, u32[]{:S(2)}, u32[]{:S(2)}) collective-permute-start(bf16[128,512]{1,0:T(8,128)(2,1)S(1)} %latent.1.refs_3_), channel_id=1, source_target_pairs={{0,4},{1,5},{2,6},{3,7},{4,8},{5,9},{6,10},{7,11},{8,12},{9,13},{1... | collective-permute-start | bytes 393224 | tf_op jit(solution)/shard_map/ppermute | solution.py:29
  40.4 1.9 %collective-permute-start.14 = (bf16[128,512]{1,0:T(8,128)(2,1)S(1)}, bf16[128,512]{1,0:T(8,128)(2,1)S(1)}, u32[]{:S(2)}, u32[]{:S(2)}) collective-permute-start(bf16[128,512]{1,0:T(8,128)(2,1)S(1)} %latent.1.refs_3_), channel_id=1, source_target_pairs={{0,8},{1,9},{2,10},{3,11},{4,12},{5,13},{6,14},{7,15},{8,0},{9,1},... | collective-permute-start | bytes 393224 | tf_op jit(solution)/shard_map/ppermute | solution.py:29
  43.7 2.7 %collective-permute-done.13.refs_0_ = bf16[128,512]{1,0:T(8,128)(2,1)S(1)} collective-permute-done((bf16[128,512]{1,0:T(8,128)(2,1)S(1)}, bf16[128,512]{1,0:T(8,128)(2,1)S(1)}, u32[]{:S(2)}, u32[]{:S(2)}) %collective-permute-start.13) | collective-permute-done | bytes 131104 | tf_op jit(solution)/shard_map/ppermute | solution.py:29
  46.3 3.9 %collective-permute-done.14.refs_1_ = bf16[128,512]{1,0:T(8,128)(2,1)S(1)} collective-permute-done((bf16[128,512]{1,0:T(8,128)(2,1)S(1)}, bf16[128,512]{1,0:T(8,128)(2,1)S(1)}, u32[]{:S(2)}, u32[]{:S(2)}) %collective-permute-start.14) | collective-permute-done | bytes 131104 | tf_op jit(solution)/shard_map/ppermute | solution.py:29
  50.3 1.9 %collective-permute-done.18.refs_13_ = bf16[512,512]{1,0:T(8,128)(2,1)S(1)} collective-permute-done((bf16[512,512]{1,0:T(8,128)(2,1)S(1)}, bf16[512,512]{1,0:T(8,128)(2,1)S(1)}, u32[]{:S(2)}, u32[]{:S(2)}) %collective-permute-start.18) | collective-permute-done | bytes 524320 | tf_op jit(solution)/shard_map/ppermute | solution.py:33
  52.2 5.9 %experts.1 = (bf16[128,512]{1,0:T(8,128)(2,1)S(1)}, bf16[128,512]{1,0:T(8,128)(2,1)S(1)}, bf16[128,512]{1,0:T(8,128)(2,1)S(1)}, bf16[128,512]{1,0:T(8,128)(2,1)S...) custom-call(s32[7]{0:T(128)S(1)} %stack.31.place, ...), custom_call_target="tpu_custom_call" | custom-call | tf_op jit(solution)/shard_map/experts/pallas_call | solution.py:45
  58.2 1.8 %weight_grads.2 = (f32[2,512,512]{2,1,0:T(8,128)S(1)}, bf16[2,512,512]{2,1,0:T(8,128)(2,1)S(1)}) custom-call(s32[7]{0:T(128)S(1)} %stack.31.place, bf16[128,512]{1,0:T(8,128)(2,1)S(1)} %collective-permute-done.13.refs_0_, bf16[128,512]{1,0:T(8,128)(2,1)S(1)} %collective-permute-done.14.refs_1_, bf16[128,512]{1,0:T(8,128)(2,1)S(1)} %collective-permute-done.15.refs_2_, ...), custom_call_target="tpu_custom_call" | custom-call | flops 1073741824 | tf_op jit(solution)/shard_map/weight_grads/pallas_call | solution.py:45
  61.5 3.3 %collective-permute-start.22 = (bf16[128,512]{1,0:T(8,128)(2,1)S(1)}, bf16[128,512]{1,0:T(8,128)(2,1)S(1)}, u32[]{:S(2)}, u32[]{:S(2)}) collective-permute-start(bf16[128,512]{1,0:T(8,128)(2,1)S(1)} %get-tuple-element.91), channel_id=1, source_target_pairs={{0,4},{1,5},{2,6},{3,7},{4,8},{5,9},{6,10},{7,11},{8,12},{9,13},{1... | collective-permute-start | bytes 393224 | tf_op jit(solution)/shard_map/ppermute | solution.py:29
  64.8 1.8 %collective-permute-start.21 = (bf16[128,512]{1,0:T(8,128)(2,1)S(1)}, bf16[128,512]{1,0:T(8,128)(2,1)S(1)}, u32[]{:S(2)}, u32[]{:S(2)}) collective-permute-start(bf16[128,512]{1,0:T(8,128)(2,1)S(1)} %get-tuple-element.89), channel_id=1, source_target_pairs={{0,8},{1,9},{2,10},{3,11},{4,12},{5,13},{6,14},{7,15},{8,0},{9,1},... | collective-permute-start | bytes 393224 | tf_op jit(solution)/shard_map/ppermute | solution.py:29
  70.4 5.1 %collective-permute-done.21.refs_2_ = bf16[128,512]{1,0:T(8,128)(2,1)S(1)} collective-permute-done((bf16[128,512]{1,0:T(8,128)(2,1)S(1)}, bf16[128,512]{1,0:T(8,128)(2,1)S(1)}, u32[]{:S(2)}, u32[]{:S(2)}) %collective-permute-start.21) | collective-permute-done | bytes 131104 | tf_op jit(solution)/shard_map/ppermute | solution.py:29
  76.7 2.3 %collective-permute-start.27 = (bf16[128,512]{1,0:T(8,128)(2,1)S(1)}, bf16[128,512]{1,0:T(8,128)(2,1)S(1)}, u32[]{:S(2)}, u32[]{:S(2)}) collective-permute-start(bf16[128,512]{1,0:T(8,128)(2,1)S(1)} %get-tuple-element.99), channel_id=1, source_target_pairs={{0,8},{1,9},{2,10},{3,11},{4,12},{5,13},{6,14},{7,15},{8,0},{9,1},... | collective-permute-start | bytes 393224 | tf_op jit(solution)/shard_map/ppermute | solution.py:29
  78.9 1.8 %weight_grads.3 = (f32[2,512,512]{2,1,0:T(8,128)S(1)}, bf16[2,512,512]{2,1,0:T(8,128)(2,1)S(1)}) custom-call(s32[7]{0:T(128)S(1)} %stack.31.place, bf16[128,512]{1,0:T(8,128)(2,1)S(1)} %collective-permute-done.13.refs_0_, bf16[128,512]{1,0:T(8,128)(2,1)S(1)} %collective-permute-done.14.refs_1_, bf16[128,512]{1,0:T(8,128)(2,1)S(1)} %collective-permute-done.15.refs_2_, ...), custom_call_target="tpu_custom_call" | custom-call | flops 1073741824 | tf_op jit(solution)/shard_map/weight_grads/pallas_call | solution.py:45
  86.9 6.1 %collective-permute-start.31 = (bf16[2,128,512]{2,1,0:T(8,128)(2,1)S(1)}, bf16[2,128,512]{2,1,0:T(8,128)(2,1)S(1)}, u32[]{:S(2)}, u32[]{:S(2)}) collective-permute-start(bf16[2,128,512]{2,1,0:T(8,128)(2,1)S(1)} %get-tuple-element.103), channel_id=1, source_target_pairs={{0,12},{1,13},{2,14},{3,15},{4,0},{5,1},{6,2},{7,3},{8,4},{9,5},{1... | collective-permute-start | bytes 786440 | tf_op jit(solution)/shard_map/ppermute | solution.py:29
  93.5 2.2 %token_grad.1 = bf16[128,2048]{1,0:T(8,128)(2,1)} custom-call(s32[7]{0:T(128)S(1)} %stack.31.place, bf16[128,512]{1,0:T(8,128)(2,1)S(1)} %latent_delta.1.refs_4_.delta, bf16[4,512,512]{2,1,0:T(8,128)(2,1)S(1)} %pack.1.held, bf16[4,512,512]{2,1,0:T(8,128)(2,1)S(1)} %collective-permute-done.29.arrived.others), custom_call_target="tpu_custom_call" | custom-call | tf_op jit(solution)/shard_map/token_grad/pallas_call | solution.py:45
  95.7 13.5 %collective-permute-done.32.refs_2_ = bf16[128,512]{1,0:T(8,128)(2,1)S(1)} collective-permute-done((bf16[128,512]{1,0:T(8,128)(2,1)S(1)}, bf16[128,512]{1,0:T(8,128)(2,1)S(1)}, u32[]{:S(2)}, u32[]{:S(2)}) %collective-permute-start.32) | collective-permute-done | bytes 131104 | tf_op jit(solution)/shard_map/ppermute | solution.py:29
  109.2 1.9 %last_sums.1 = (f32[128,512]{1,0:T(8,128)}, bf16[128,512]{1,0:T(8,128)(2,1)}, bf16[1,512,512]{2,1,0:T(8,128)(2,1)}, bf16[1,512,512]{2,1,0:T(8,128)(2,1)}) custom-call(s32[7]{0:T(128)S(1)} %stack.31.place, f32[2,512,512]{2,1,0:T(8,128)S(1)} %get-tuple-element.107.near, bf16[4,512,512]{2,1,0:T(8,128)(2,1)S(1)} %collective-permute-done.29.arrived.others, ...), custom_call_target="tpu_custom_call" | custom-call | tf_op jit(solution)/shard_map/last_sums/pallas_call | solution.py:45
  (72 shorter events, 30.9 us)
Async XLA Ops:
  2.7 10.0 %collective-permute-start.1 = (bf16[2,512,512]{2,1,0:T(8,128)(2,1)S(1)}, bf16[2,512,512]{2,1,0:T(8,128)(2,1)S(1)}, u32[]{:S(2)}, u32[]{:S(2)}) collective-permute-start(bf16[2,512,512]{2,1,0:T(8,128)(2,1)S(1)} %get-tuple-element.63.refs_8_), channel_id=1, source_target_pairs={{0,1},{1,0},{2,3},{3,2},{4,5},{5,4},{6,7},{7,6},{8,9},{9,8},{10,11... | collective-permute-start | bytes 3145736 | tf_op jit(solution)/shard_map/ppermute | solution.py:33
  3.3 9.5 %collective-permute-start = (bf16[2,128,512]{2,1,0:T(8,128)(2,1)S(1)}, bf16[2,128,512]{2,1,0:T(8,128)(2,1)S(1)}, u32[]{:S(2)}, u32[]{:S(2)}) collective-permute-start(bf16[2,128,512]{2,1,0:T(8,128)(2,1)S(1)} %get-tuple-element.62), channel_id=1, source_target_pairs={{0,2},{1,3},{2,0},{3,1},{4,6},{5,7},{6,4},{7,5},{8,10},{9,11},{10,... | collective-permute-start | bytes 786440 | tf_op jit(solution)/shard_map/ppermute | solution.py:33
  5.8 12.2 %collective-permute-start.5 = (bf16[128,512]{1,0:T(8,128)(2,1)}, bf16[128,512]{1,0:T(8,128)(2,1)S(1)}, u32[]{:S(2)}, u32[]{:S(2)}) collective-permute-start(bf16[128,512]{1,0:T(8,128)(2,1)} %refs_4_.1), channel_id=1, source_target_pairs={{0,4},{1,5},{2,6},{3,7},{4,8},{5,9},{6,10},{7,11},{8,12},{9,13},{1... | collective-permute-start | bytes 393224 | tf_op jit(solution)/shard_map/ppermute | solution.py:29
  7.4 11.8 %collective-permute-start.6 = (bf16[128,512]{1,0:T(8,128)(2,1)}, bf16[128,512]{1,0:T(8,128)(2,1)S(1)}, u32[]{:S(2)}, u32[]{:S(2)}) collective-permute-start(bf16[128,512]{1,0:T(8,128)(2,1)} %refs_4_.1), channel_id=1, source_target_pairs={{0,8},{1,9},{2,10},{3,11},{4,12},{5,13},{6,14},{7,15},{8,0},{9,1},... | collective-permute-start | bytes 393224 | tf_op jit(solution)/shard_map/ppermute | solution.py:29
  10.0 9.2 %collective-permute-start.7 = (bf16[128,512]{1,0:T(8,128)(2,1)}, bf16[128,512]{1,0:T(8,128)(2,1)S(1)}, u32[]{:S(2)}, u32[]{:S(2)}) collective-permute-start(bf16[128,512]{1,0:T(8,128)(2,1)} %refs_4_.1), channel_id=1, source_target_pairs={{0,12},{1,13},{2,14},{3,15},{4,0},{5,1},{6,2},{7,3},{8,4},{9,5},{1... | collective-permute-start | bytes 393224 | tf_op jit(solution)/shard_map/ppermute | solution.py:29
  16.2 13.9 %collective-permute-start.3 = (bf16[512,512]{1,0:T(8,128)(2,1)S(1)}, bf16[512,512]{1,0:T(8,128)(2,1)S(1)}, u32[]{:S(2)}, u32[]{:S(2)}) collective-permute-start(bf16[512,512]{1,0:T(8,128)(2,1)S(1)} %bitcast.15), channel_id=1, source_target_pairs={{0,2},{1,3},{2,0},{3,1},{4,6},{5,7},{6,4},{7,5},{8,10},{9,11},{10,... | collective-permute-start | bytes 1572872 | tf_op jit(solution)/shard_map/ppermute | solution.py:33
  20.2 9.9 %collective-permute-start.8 = (f32[2,128,512]{2,1,0:T(8,128)S(1)}, f32[2,128,512]{2,1,0:T(8,128)S(1)}, u32[]{:S(2)}, u32[]{:S(2)}) collective-permute-start(f32[2,128,512]{2,1,0:T(8,128)S(1)} %get-tuple-element.70), channel_id=1, source_target_pairs={{0,1},{1,0},{2,3},{3,2},{4,5},{5,4},{6,7},{7,6},{8,9},{9,8},{10,11... | collective-permute-start | bytes 1572872 | tf_op jit(solution)/shard_map/ppermute | solution.py:33
  20.3 12.2 %collective-permute-start.10 = (bf16[144,512]{1,0:T(8,128)(2,1)S(1)}, bf16[144,512]{1,0:T(8,128)(2,1)S(1)}, u32[]{:S(2)}, u32[]{:S(2)}) collective-permute-start(bf16[144,512]{1,0:T(8,128)(2,1)S(1)} %payload.1.refs_7_), channel_id=1, source_target_pairs={{0,4},{1,5},{2,6},{3,7},{4,8},{5,9},{6,10},{7,11},{8,12},{9,13},{1... | collective-permute-start | bytes 442376 | tf_op jit(solution)/shard_map/ppermute | solution.py:29
  23.6 11.9 %collective-permute-start.11 = (bf16[144,512]{1,0:T(8,128)(2,1)S(1)}, bf16[144,512]{1,0:T(8,128)(2,1)S(1)}, u32[]{:S(2)}, u32[]{:S(2)}) collective-permute-start(bf16[144,512]{1,0:T(8,128)(2,1)S(1)} %payload.1.refs_7_), channel_id=1, source_target_pairs={{0,8},{1,9},{2,10},{3,11},{4,12},{5,13},{6,14},{7,15},{8,0},{9,1},... | collective-permute-start | bytes 442376 | tf_op jit(solution)/shard_map/ppermute | solution.py:29
  25.3 10.3 %collective-permute-start.12 = (bf16[144,512]{1,0:T(8,128)(2,1)S(1)}, bf16[144,512]{1,0:T(8,128)(2,1)S(1)}, u32[]{:S(2)}, u32[]{:S(2)}) collective-permute-start(bf16[144,512]{1,0:T(8,128)(2,1)S(1)} %payload.1.refs_7_), channel_id=1, source_target_pairs={{0,12},{1,13},{2,14},{3,15},{4,0},{5,1},{6,2},{7,3},{8,4},{9,5},{1... | collective-permute-start | bytes 442376 | tf_op jit(solution)/shard_map/ppermute | solution.py:29
  36.3 14.0 %collective-permute-start.16 = (bf16[512,512]{1,0:T(8,128)(2,1)S(1)}, bf16[512,512]{1,0:T(8,128)(2,1)S(1)}, u32[]{:S(2)}, u32[]{:S(2)}) collective-permute-start(bf16[512,512]{1,0:T(8,128)(2,1)S(1)} %bitcast.16), channel_id=1, source_target_pairs={{0,2},{1,3},{2,0},{3,1},{4,6},{5,7},{6,4},{7,5},{8,10},{9,11},{10,... | collective-permute-start | bytes 1572872 | tf_op jit(solution)/shard_map/ppermute | solution.py:33
  38.1 8.2 %collective-permute-start.13 = (bf16[128,512]{1,0:T(8,128)(2,1)S(1)}, bf16[128,512]{1,0:T(8,128)(2,1)S(1)}, u32[]{:S(2)}, u32[]{:S(2)}) collective-permute-start(bf16[128,512]{1,0:T(8,128)(2,1)S(1)} %latent.1.refs_3_), channel_id=1, source_target_pairs={{0,4},{1,5},{2,6},{3,7},{4,8},{5,9},{6,10},{7,11},{8,12},{9,13},{1... | collective-permute-start | bytes 393224 | tf_op jit(solution)/shard_map/ppermute | solution.py:29
  40.4 9.8 %collective-permute-start.14 = (bf16[128,512]{1,0:T(8,128)(2,1)S(1)}, bf16[128,512]{1,0:T(8,128)(2,1)S(1)}, u32[]{:S(2)}, u32[]{:S(2)}) collective-permute-start(bf16[128,512]{1,0:T(8,128)(2,1)S(1)} %latent.1.refs_3_), channel_id=1, source_target_pairs={{0,8},{1,9},{2,10},{3,11},{4,12},{5,13},{6,14},{7,15},{8,0},{9,1},... | collective-permute-start | bytes 393224 | tf_op jit(solution)/shard_map/ppermute | solution.py:29
  42.3 8.0 %collective-permute-start.15 = (bf16[128,512]{1,0:T(8,128)(2,1)S(1)}, bf16[128,512]{1,0:T(8,128)(2,1)S(1)}, u32[]{:S(2)}, u32[]{:S(2)}) collective-permute-start(bf16[128,512]{1,0:T(8,128)(2,1)S(1)} %latent.1.refs_3_), channel_id=1, source_target_pairs={{0,12},{1,13},{2,14},{3,15},{4,0},{5,1},{6,2},{7,3},{8,4},{9,5},{1... | collective-permute-start | bytes 393224 | tf_op jit(solution)/shard_map/ppermute | solution.py:29
  60.2 20.5 %collective-permute-start.25 = (bf16[512,512]{1,0:T(8,128)(2,1)S(1)}, bf16[512,512]{1,0:T(8,128)(2,1)S(1)}, u32[]{:S(2)}, u32[]{:S(2)}) collective-permute-start(bf16[512,512]{1,0:T(8,128)(2,1)S(1)} %get-tuple-element.96.down), channel_id=1, source_target_pairs={{0,2},{1,3},{2,0},{3,1},{4,6},{5,7},{6,4},{7,5},{8,10},{9,11},{10,... | collective-permute-start | bytes 1572872 | tf_op jit(solution)/shard_map/ppermute | solution.py:33
  61.5 8.9 %collective-permute-start.22 = (bf16[128,512]{1,0:T(8,128)(2,1)S(1)}, bf16[128,512]{1,0:T(8,128)(2,1)S(1)}, u32[]{:S(2)}, u32[]{:S(2)}) collective-permute-start(bf16[128,512]{1,0:T(8,128)(2,1)S(1)} %get-tuple-element.91), channel_id=1, source_target_pairs={{0,4},{1,5},{2,6},{3,7},{4,8},{5,9},{6,10},{7,11},{8,12},{9,13},{1... | collective-permute-start | bytes 393224 | tf_op jit(solution)/shard_map/ppermute | solution.py:29
  64.8 10.7 %collective-permute-start.21 = (bf16[128,512]{1,0:T(8,128)(2,1)S(1)}, bf16[128,512]{1,0:T(8,128)(2,1)S(1)}, u32[]{:S(2)}, u32[]{:S(2)}) collective-permute-start(bf16[128,512]{1,0:T(8,128)(2,1)S(1)} %get-tuple-element.89), channel_id=1, source_target_pairs={{0,8},{1,9},{2,10},{3,11},{4,12},{5,13},{6,14},{7,15},{8,0},{9,1},... | collective-permute-start | bytes 393224 | tf_op jit(solution)/shard_map/ppermute | solution.py:29
  66.6 8.9 %collective-permute-start.20 = (bf16[128,512]{1,0:T(8,128)(2,1)S(1)}, bf16[128,512]{1,0:T(8,128)(2,1)S(1)}, u32[]{:S(2)}, u32[]{:S(2)}) collective-permute-start(bf16[128,512]{1,0:T(8,128)(2,1)S(1)} %get-tuple-element.87), channel_id=1, source_target_pairs={{0,12},{1,13},{2,14},{3,15},{4,0},{5,1},{6,2},{7,3},{8,4},{9,5},{1... | collective-permute-start | bytes 393224 | tf_op jit(solution)/shard_map/ppermute | solution.py:29
  67.8 15.0 %collective-permute-start.26 = (bf16[256,512]{1,0:T(8,128)(2,1)S(1)}, bf16[256,512]{1,0:T(8,128)(2,1)S(1)}, u32[]{:S(2)}, u32[]{:S(2)}) collective-permute-start(bf16[256,512]{1,0:T(8,128)(2,1)S(1)} %get-tuple-element.97), channel_id=1, source_target_pairs={{0,2},{1,3},{2,0},{3,1},{4,6},{5,7},{6,4},{7,5},{8,10},{9,11},{10,... | collective-permute-start | bytes 786440 | tf_op jit(solution)/shard_map/ppermute | solution.py:33
  85.4 8.1 %collective-permute-start.29 = (bf16[4,512,512]{2,1,0:T(8,128)(2,1)S(1)}, bf16[4,512,512]{2,1,0:T(8,128)(2,1)S(1)}, u32[]{:S(2)}, u32[]{:S(2)}) collective-permute-start(bf16[4,512,512]{2,1,0:T(8,128)(2,1)S(1)} %pack.1.held), channel_id=1, source_target_pairs={{0,1},{1,0},{2,3},{3,2},{4,5},{5,4},{6,7},{7,6},{8,9},{9,8},{10,11... | collective-permute-start | bytes 6291464 | tf_op jit(solution)/shard_map/ppermute | solution.py:33
  85.6 23.6 %collective-permute-start.30 = (bf16[768,512]{1,0:T(8,128)(2,1)S(1)}, bf16[768,512]{1,0:T(8,128)(2,1)S(1)}, u32[]{:S(2)}, u32[]{:S(2)}) collective-permute-start(bf16[768,512]{1,0:T(8,128)(2,1)S(1)} %get-tuple-element.108), channel_id=1, source_target_pairs={{0,2},{1,3},{2,0},{3,1},{4,6},{5,7},{6,4},{7,5},{8,10},{9,11},{10,... | collective-permute-start | bytes 2359304 | tf_op jit(solution)/shard_map/ppermute | solution.py:33
  86.9 22.3 %collective-permute-start.31 = (bf16[2,128,512]{2,1,0:T(8,128)(2,1)S(1)}, bf16[2,128,512]{2,1,0:T(8,128)(2,1)S(1)}, u32[]{:S(2)}, u32[]{:S(2)}) collective-permute-start(bf16[2,128,512]{2,1,0:T(8,128)(2,1)S(1)} %get-tuple-element.103), channel_id=1, source_target_pairs={{0,12},{1,13},{2,14},{3,15},{4,0},{5,1},{6,2},{7,3},{8,4},{9,5},{1... | collective-permute-start | bytes 786440 | tf_op jit(solution)/shard_map/ppermute | solution.py:29
  93.0 16.3 %collective-permute-start.33 = (bf16[2,128,512]{2,1,0:T(8,128)(2,1)S(1)}, bf16[2,128,512]{2,1,0:T(8,128)(2,1)S(1)}, u32[]{:S(2)}, u32[]{:S(2)}) collective-permute-start(bf16[2,128,512]{2,1,0:T(8,128)(2,1)S(1)} %get-tuple-element.111), channel_id=1, source_target_pairs={{0,4},{1,5},{2,6},{3,7},{4,8},{5,9},{6,10},{7,11},{8,12},{9,13},{1... | collective-permute-start | bytes 786440 | tf_op jit(solution)/shard_map/ppermute | solution.py:29
  93.0 16.3 %collective-permute-start.32 = (bf16[128,512]{1,0:T(8,128)(2,1)S(1)}, bf16[128,512]{1,0:T(8,128)(2,1)S(1)}, u32[]{:S(2)}, u32[]{:S(2)}) collective-permute-start(bf16[128,512]{1,0:T(8,128)(2,1)S(1)} %get-tuple-element.110), channel_id=1, source_target_pairs={{0,8},{1,9},{2,10},{3,11},{4,12},{5,13},{6,14},{7,15},{8,0},{9,1},... | collective-permute-start | bytes 393224 | tf_op jit(solution)/shard_map/ppermute | solution.py:29
  (16 other events, 120.8 us)
